TPU v7x, 32 devices: a whole 2x2x4 slice. The times are simulated.
32 devices in a mesh: batch: 4 (over z), blk: 2 (over x), head: 4 (over y, core).
Axes of the slice: x: 2, y: 2, z: 4, core: 2. Of those that a mesh axis runs over, the one named last changes fastest.
Arguments:
- tokens: bfloat16 [8, 1024, 1280], P('batch', ('blk', 'head')), may hold values from -6 to 6
- segments: int32 [8, 1024], P('batch'), may hold values from 0 to 1023, as said below
- qkv_weight: bfloat16 [2, 1280, 3840], P(None, ('batch', 'blk', 'head')), may hold values from -0.15625 to 0.15625
- out_weight: bfloat16 [2, 1280, 1280], P(None, ('batch', 'blk', 'head')), may hold values from -1.25 to 1.25
- up_weight: bfloat16 [2, 1280, 1280], P(None, ('batch', 'blk', 'head')), may hold values from -0.15625 to 0.15625
- down_weight: bfloat16 [2, 1280, 1280], P(None, ('batch', 'blk', 'head')), may hold values from -0.15625 to 0.15625
- attn_gain: bfloat16 [2, 1280], P(None, ('batch', 'blk', 'head')), may hold values from 0.099609375 to 1.8984375
- mlp_gain: bfloat16 [2, 1280], P(None, ('batch', 'blk', 'head')), may hold values from 0.099609375 to 1.8984375
- scale_param: float32 [2, 80], replicated, may hold values from -1 to 1.5
- cotangent: bfloat16 [8, 1024, 1280], P('batch', ('blk', 'head')), may hold values from -6 to 6
Outputs:
- layer_out: bfloat16 [8, 1024, 1280], P('batch', ('blk', 'head'))
- input_grad: float32 [8, 1024, 1280], P('batch', ('blk', 'head'))
- qkv_grad: float32 [2, 1280, 3840], P(None, ('batch', 'blk', 'head'))
- out_grad: float32 [2, 1280, 1280], P(None, ('batch', 'blk', 'head'))
- up_grad: float32 [2, 1280, 1280], P(None, ('batch', 'blk', 'head'))
- down_grad: float32 [2, 1280, 1280], P(None, ('batch', 'blk', 'head'))
- attn_gain_grad: float32 [2, 1280], P(None, ('batch', 'blk', 'head'))
- mlp_gain_grad: float32 [2, 1280], P(None, ('batch', 'blk', 'head'))
- scale_grad: float32 [2, 80], replicated
Inputs may be any that keep to these rules, and one draw needn't show every extreme that they name: `segments`: within each sequence the segment numbers start at 0 and never fall along the positions.
All inputs are finite; a program needn't handle non-finite values.
Results may differ from a plain program's by a relative error of at most 0.035.
Values may be sent and summed in bfloat16 or wider, within the bound.
No kernel may reach another device: no remote copies, remote signals or barrier semaphores. Data moves between devices by JAX's collectives and lax.ppermute only.
A program may use at most 256 MiB of HBM per device.

v0:
```python
import math

import jax
import jax.numpy as jnp
from jax import lax
from jax.sharding import PartitionSpec as P

WINDOW = 1024


EPSILON = 1e-06
SCALE_BASE = 1.4426950408889634
MASKED_SCORE = -1e30


def shifted(block, axis, distance):
    devices = range(lax.axis_size(axis))
    route = [(i - distance, i) for i in devices if i - distance in devices]
    return lax.ppermute(block, axis, route)


def as_sent(array):

    def short(part):
        return part.astype(jnp.bfloat16) if part.dtype == jnp.float32 else part

    return jax.tree.map(short, array)


def normalize(stream, gain):
    factor = lax.rsqrt(jnp.mean(stream * stream, axis=-1, keepdims=True) + EPSILON)
    return (stream * factor * gain, factor)


def norm_back(upper, stream, factor, gain):
    inner = upper * gain
    model_width = stream.shape[-1]
    gain_grad = jnp.sum((upper * stream * factor).reshape(-1, model_width), axis=0)
    lower = factor * inner - stream * factor * factor * factor * jnp.mean(
        inner * stream, axis=-1, keepdims=True
    )
    return (lower, gain_grad)


def outer_sum(left, right):
    left_flat = left.reshape(-1, left.shape[-1])
    right_flat = right.reshape(-1, right.shape[-1])
    return lax.dot_general(
        left_flat, right_flat, (((0,), (0,)), ((), ())), preferred_element_type=jnp.float32
    )


def times_transposed(grad, matrix):
    return lax.dot_general(
        grad, matrix, (((grad.ndim - 1,), (1,)), ((), ())), preferred_element_type=jnp.float32
    )


def window_mask(segments, block_index, reach, block):
    seq_count = segments.shape[0]
    key_count = (reach + 1) * block
    leading = jnp.full((seq_count, reach * block), -1, jnp.int32)
    padded = jnp.concatenate([leading, segments], axis=1)
    query_segs = lax.dynamic_slice_in_dim(segments, block_index * block, block, 1)
    key_segs = lax.dynamic_slice_in_dim(padded, block_index * block, key_count, 1)
    query_place = jnp.arange(block, dtype=jnp.int32)[:, None] + reach * block
    key_place = jnp.arange(key_count, dtype=jnp.int32)[None, :]
    near = (key_place <= query_place) & (query_place - key_place < WINDOW)
    return (key_segs[:, None, :] == query_segs[:, :, None]) & near[None]


def scores_of(queries, keys_all, allowed):
    scores = jnp.einsum("sqhd,skhd->shqk", queries, keys_all, preferred_element_type=jnp.float32)
    return jnp.where(allowed[:, None], scores, MASKED_SCORE)


def cycle_forward(own_pairs, reach):
    arrived = [own_pairs]
    for cycle_step in range(reach):
        arrived.append(shifted(arrived[-1], "blk", 1))
    return jnp.concatenate(arrived[::-1], axis=1)


def split_pairs(pairs_all, local_heads, head_dim):
    seq_count, key_count = (pairs_all.shape[0], pairs_all.shape[1])
    keys_all = pairs_all[:, :, 0].reshape(seq_count, key_count, local_heads, head_dim)
    values_all = pairs_all[:, :, 1].reshape(seq_count, key_count, local_heads, head_dim)
    return (keys_all, values_all)


def attend(queries, pairs_all, allowed):
    keys_all, values_all = split_pairs(pairs_all, queries.shape[2], queries.shape[3])
    scores = scores_of(queries, keys_all, allowed)
    top_score = jnp.max(scores, axis=-1, keepdims=True)
    exp_terms = jnp.exp(scores - top_score)
    totals = jnp.sum(exp_terms, axis=-1, keepdims=True)
    probs_low = (exp_terms / totals).astype(jnp.bfloat16)
    attended = jnp.einsum(
        "shqk,skhd->sqhd", probs_low, values_all, preferred_element_type=jnp.float32
    )
    return (attended, top_score + jnp.log(totals))


def attend_back(queries, pairs_all, allowed, log_normalizer_total, attended_grad, reach):
    seq_count, block, local_heads, head_dim = queries.shape
    local_width = local_heads * head_dim
    key_count = pairs_all.shape[1]
    keys_all, values_all = split_pairs(pairs_all, local_heads, head_dim)
    scores = scores_of(queries, keys_all, allowed)
    probs = jnp.exp(scores - log_normalizer_total)
    probs_low = probs.astype(jnp.bfloat16)
    values_grad = jnp.einsum(
        "shqk,sqhd->skhd", probs_low, attended_grad, preferred_element_type=jnp.float32
    )
    probs_grad = jnp.einsum(
        "sqhd,skhd->shqk", attended_grad, values_all, preferred_element_type=jnp.float32
    )
    row_dot = jnp.sum(probs_grad * probs, axis=-1, keepdims=True)
    scores_low = (probs * (probs_grad - row_dot)).astype(jnp.bfloat16)
    queries_grad = jnp.einsum(
        "shqk,skhd->sqhd", scores_low, keys_all, preferred_element_type=jnp.float32
    )
    keys_grad = jnp.einsum(
        "shqk,sqhd->skhd", scores_low, queries, preferred_element_type=jnp.float32
    )
    pair_grads = jnp.stack(
        [
            keys_grad.reshape(seq_count, key_count, local_width),
            values_grad.reshape(seq_count, key_count, local_width),
        ],
        axis=2,
    )
    summed_pairs = pair_grads[:, :block]
    for cycle_step in range(1, reach + 1):
        summed_pairs = (
            shifted(summed_pairs.astype(jnp.bfloat16), "blk", -1).astype(summed_pairs.dtype)
            + pair_grads[:, cycle_step * block : (cycle_step + 1) * block]
        )
    return (queries_grad, summed_pairs)


def over_heads(values_in):
    return lax.all_gather(values_in, "head", axis=1, tiled=True)


def head_sums(partial_in):
    return lax.psum_scatter(
        partial_in.astype(jnp.bfloat16), "head", scatter_dimension=1, tiled=True
    ).astype(jnp.float32)


def cols_to_tokens(column_part):
    seq_count, block, width_part = column_part.shape
    head_count = lax.axis_size("head")
    moved = lax.all_to_all(
        column_part.reshape(seq_count, head_count, block // head_count, 1, width_part).astype(
            jnp.bfloat16
        ),
        "head",
        split_axis=1,
        concat_axis=3,
        tiled=True,
    ).astype(jnp.float32)
    return moved.reshape(seq_count, block // head_count, head_count * width_part)


def tokens_to_cols(token_rows):
    seq_count, tok_rows, model_width = token_rows.shape
    head_count = lax.axis_size("head")
    moved = lax.all_to_all(
        token_rows.reshape(seq_count, 1, tok_rows, head_count, model_width // head_count),
        "head",
        split_axis=3,
        concat_axis=1,
        tiled=True,
    )
    return moved.reshape(seq_count, tok_rows * head_count, model_width // head_count)


def gather_columns(qkv_rows, out_rows, up_rows, down_rows):
    pieces = (
        qkv_rows.reshape(qkv_rows.shape[0], 3, -1),
        out_rows.reshape(out_rows.shape[0], 1, -1),
        up_rows.reshape(up_rows.shape[0], 1, -1),
        down_rows.reshape(down_rows.shape[0], 1, -1),
    )
    moved = (
        lax.all_to_all(pieces[0], "head", split_axis=2, concat_axis=0, tiled=True),
        lax.all_to_all(pieces[1], "head", split_axis=2, concat_axis=0, tiled=True),
        lax.all_to_all(pieces[2], "head", split_axis=2, concat_axis=0, tiled=True),
        lax.all_to_all(pieces[3], "head", split_axis=2, concat_axis=0, tiled=True),
    )
    return (
        lax.all_gather(moved[0], ("batch", "blk"), axis=0, tiled=True),
        lax.all_gather(moved[1], ("batch", "blk"), axis=0, tiled=True),
        lax.all_gather(moved[2], ("batch", "blk"), axis=0, tiled=True),
        lax.all_gather(moved[3], ("batch", "blk"), axis=0, tiled=True),
    )


def split_forward(stream, weights, gains, scale_vec, segments, reach, block_index):
    qkv_cols, out_cols, up_cols, down_cols = weights
    seq_count, tok_rows, model_width = stream.shape
    head_count = lax.axis_size("head")
    head_dim = scale_vec.shape[0]
    local_width = qkv_cols.shape[2]
    local_heads = local_width // head_dim
    ff_part = up_cols.shape[2]
    block = tok_rows * head_count
    normed, factor_one = normalize(stream, gains[0].astype(jnp.float32))
    normed_block = over_heads(normed.astype(jnp.bfloat16))
    projected = jnp.dot(
        normed_block,
        qkv_cols.reshape(model_width, 3 * local_width),
        preferred_element_type=jnp.float32,
    ).reshape(seq_count, block, 3, local_width)
    query_pre = projected[:, :, 0]
    queries = (query_pre.reshape(seq_count, block, local_heads, head_dim) * scale_vec).astype(
        jnp.bfloat16
    )
    own_pairs = projected[:, :, 1:3].astype(jnp.bfloat16)
    pairs_all = cycle_forward(own_pairs, reach)
    allowed = window_mask(segments, block_index, reach, block)
    attended, log_normalizer_total = attend(queries, pairs_all, allowed)
    attended_low = attended.reshape(seq_count, 1, block, local_width).astype(jnp.bfloat16)
    attended_full = over_heads(attended_low)
    out_part = jnp.einsum(
        "sgbw,gwc->sbc",
        attended_full,
        out_cols.reshape(head_count, local_width, -1),
        preferred_element_type=jnp.float32,
    )
    middle = stream + cols_to_tokens(out_part)
    normed_two, factor_two = normalize(middle, gains[1].astype(jnp.float32))
    normed_two_block = over_heads(normed_two.astype(jnp.bfloat16))
    hidden = jnp.dot(
        normed_two_block, up_cols.reshape(model_width, ff_part), preferred_element_type=jnp.float32
    )
    active_low = (
        (hidden * jax.nn.sigmoid(hidden)).astype(jnp.bfloat16).reshape(seq_count, 1, block, ff_part)
    )
    complete_active = over_heads(active_low)
    down_part = jnp.einsum(
        "prna,ram->pnm",
        complete_active,
        down_cols.reshape(head_count, ff_part, -1),
        preferred_element_type=jnp.float32,
    )
    result = middle + cols_to_tokens(down_part)
    kept = (
        stream,
        factor_one,
        normed_block,
        query_pre,
        queries,
        own_pairs,
        pairs_all,
        allowed,
        log_normalizer_total,
        attended_full,
        middle,
        factor_two,
        normed_two_block,
        hidden,
        complete_active,
    )
    return (result, kept)


def split_backward(upper, kept, weights, gains, scale_vec, reach):
    (
        stream,
        factor_one,
        normed_block,
        query_pre,
        queries,
        own_pairs,
        pairs_all,
        allowed,
        log_normalizer_total,
        attended_full,
        middle,
        factor_two,
        normed_two_block,
        hidden,
        complete_active,
    ) = kept
    qkv_cols, out_cols, up_cols, down_cols = weights
    seq_count, tok_rows, model_width = stream.shape
    head_count = lax.axis_size("head")
    block, local_heads, head_dim = (queries.shape[1], queries.shape[2], queries.shape[3])
    local_width = local_heads * head_dim
    ff_part = up_cols.shape[2]
    out_part = out_cols.shape[2]
    down_projection_heads = down_cols.reshape(head_count, ff_part, out_part)
    out_by_heads = out_cols.reshape(head_count, local_width, out_part)
    perceptron_columns = tokens_to_cols(upper.astype(jnp.bfloat16))
    down_grad = jnp.einsum(
        "mvxq,mxa->vqa", complete_active, perceptron_columns, preferred_element_type=jnp.float32
    ).reshape(-1, 1, out_part)
    active_part = jnp.einsum(
        "qlz,wxz->qwlx",
        perceptron_columns,
        down_projection_heads,
        preferred_element_type=jnp.float32,
    )
    active_grad = head_sums(active_part).reshape(seq_count, block, ff_part)
    gate_sig = jax.nn.sigmoid(hidden)
    hidden_low = (active_grad * gate_sig * (1.0 + hidden * (1.0 - gate_sig))).astype(jnp.bfloat16)
    up_grad = outer_sum(normed_two_block, hidden_low).reshape(model_width, 1, ff_part)
    normed_two_grad = head_sums(times_transposed(hidden_low, up_cols.reshape(model_width, ff_part)))
    extra_two, mlp_gain_grad = norm_back(
        normed_two_grad, middle, factor_two, gains[1].astype(jnp.float32)
    )
    middle_gradient = upper + extra_two
    branch_cols = tokens_to_cols(middle_gradient.astype(jnp.bfloat16))
    out_grad = jnp.einsum(
        "sgbw,sbc->gwc", attended_full, branch_cols, preferred_element_type=jnp.float32
    ).reshape(-1, 1, out_part)
    attended_part = jnp.einsum(
        "sbc,gwc->sgbw", branch_cols, out_by_heads, preferred_element_type=jnp.float32
    )
    attended_grad = (
        head_sums(attended_part)
        .astype(jnp.bfloat16)
        .reshape(seq_count, block, local_heads, head_dim)
    )
    queries_grad, summed_pairs = attend_back(
        queries, pairs_all, allowed, log_normalizer_total, attended_grad, reach
    )
    query_bar = queries_grad.astype(jnp.bfloat16).astype(jnp.float32)
    scale_vec_grad = jnp.sum(
        (query_bar * query_pre.reshape(seq_count, block, local_heads, head_dim)).reshape(
            -1, head_dim
        ),
        axis=0,
    )
    query_low = (
        (query_bar * scale_vec).reshape(seq_count, block, 1, local_width).astype(jnp.bfloat16)
    )
    projected_reduced = jnp.concatenate(
        [query_low, summed_pairs.astype(jnp.bfloat16)], axis=2
    ).reshape(seq_count, block, 3 * local_width)
    qkv_grad = outer_sum(normed_block, projected_reduced).reshape(model_width, 3, local_width)
    normed_grad = head_sums(
        times_transposed(projected_reduced, qkv_cols.reshape(model_width, 3 * local_width))
    )
    extra_one, attn_gain_grad = norm_back(
        normed_grad, stream, factor_one, gains[0].astype(jnp.float32)
    )
    lower = middle_gradient + extra_one
    return (
        lower,
        (qkv_grad, out_grad, up_grad, down_grad),
        (attn_gain_grad, mlp_gain_grad),
        scale_vec_grad,
    )


def split_body(
    tokens,
    segments,
    qkv_weight,
    out_weight,
    up_weight,
    down_weight,
    attn_gain,
    mlp_gain,
    scale_param,
    cotangent,
    reach,
    block_index,
    scale_vecs,
):
    layer_count = qkv_weight.shape[0]
    head_dim = scale_param.shape[1]
    stream = tokens.astype(jnp.float32)
    weights_all = []
    gains_all = []
    kept_all = []
    for layer_index in range(layer_count):
        weights = gather_columns(
            qkv_weight[layer_index],
            out_weight[layer_index],
            up_weight[layer_index],
            down_weight[layer_index],
        )
        gains = (
            lax.all_gather(attn_gain[layer_index], ("batch", "blk", "head"), axis=0, tiled=True),
            lax.all_gather(mlp_gain[layer_index], ("batch", "blk", "head"), axis=0, tiled=True),
        )
        stream, kept = split_forward(
            stream, weights, gains, scale_vecs[layer_index], segments, reach, block_index
        )
        weights_all.append(weights)
        gains_all.append(gains)
        kept_all.append(kept)
    layer_out = stream.astype(jnp.bfloat16)
    upper = cotangent.astype(jnp.float32)
    dense_by_layer = [None] * layer_count
    gain_by_layer = [None] * layer_count
    scale_by_layer = [None] * layer_count
    for layer_index in reversed(range(layer_count)):
        upper, dense, gain_grads, scale_vec_grad = split_backward(
            upper,
            kept_all[layer_index],
            weights_all[layer_index],
            gains_all[layer_index],
            scale_vecs[layer_index],
            reach,
        )
        dense_by_layer[layer_index] = dense
        gain_by_layer[layer_index] = gain_grads
        scale_by_layer[layer_index] = (
            scale_vec_grad
            * (SCALE_BASE / math.sqrt(head_dim))
            * jax.nn.sigmoid(scale_param[layer_index])
        )
    stacked = tuple(
        (
            jnp.stack([dense_by_layer[layer_index][member] for layer_index in range(layer_count)])
            for member in range(4)
        )
    )
    summed = (
        lax.psum_scatter(
            stacked[0].astype(jnp.bfloat16), ("batch", "blk"), scatter_dimension=1, tiled=True
        ).astype(jnp.float32),
        lax.psum_scatter(
            stacked[1].astype(jnp.bfloat16), ("batch", "blk"), scatter_dimension=1, tiled=True
        ).astype(jnp.float32),
        lax.psum_scatter(
            stacked[2].astype(jnp.bfloat16), ("batch", "blk"), scatter_dimension=1, tiled=True
        ).astype(jnp.float32),
        lax.psum_scatter(
            stacked[3].astype(jnp.bfloat16), ("batch", "blk"), scatter_dimension=1, tiled=True
        ).astype(jnp.float32),
    )
    owned = jax.tree.map(
        lambda part, own: part.astype(own.dtype),
        lax.all_to_all(as_sent(summed), "head", split_axis=1, concat_axis=3, tiled=True),
        summed,
    )
    attn_total, mlp_total, scale_grad = lax.psum(
        (
            jnp.stack([gain_by_layer[layer_index][0] for layer_index in range(layer_count)]),
            jnp.stack([gain_by_layer[layer_index][1] for layer_index in range(layer_count)]),
            jnp.stack(scale_by_layer),
        ),
        ("batch", "blk", "head"),
    )
    gain_rows = attn_gain.shape[1]
    owner = lax.axis_index(("batch", "blk", "head"))
    attn_gain_grad = lax.dynamic_slice_in_dim(attn_total, owner * gain_rows, gain_rows, 1)
    mlp_gain_grad = lax.dynamic_slice_in_dim(mlp_total, owner * gain_rows, gain_rows, 1)
    qkv_grad = owned[0].reshape(layer_count, owned[0].shape[1], -1)
    out_grad = owned[1].reshape(layer_count, owned[1].shape[1], -1)
    up_grad = owned[2].reshape(layer_count, owned[2].shape[1], -1)
    down_grad = owned[3].reshape(layer_count, owned[3].shape[1], -1)
    return (
        layer_out,
        upper,
        qkv_grad,
        out_grad,
        up_grad,
        down_grad,
        attn_gain_grad,
        mlp_gain_grad,
        scale_grad,
    )


def per_device(
    tokens,
    segments,
    qkv_weight,
    out_weight,
    up_weight,
    down_weight,
    attn_gain,
    mlp_gain,
    scale_param,
    cotangent,
):
    head_dim = scale_param.shape[1]
    block = tokens.shape[1] * lax.axis_size("head")
    reach = min((WINDOW - 1) // block + 1, lax.axis_size("blk") - 1)
    block_index = lax.axis_index("blk")
    scale_vecs = SCALE_BASE / math.sqrt(head_dim) * jax.nn.softplus(scale_param)
    return split_body(
        tokens,
        segments,
        qkv_weight,
        out_weight,
        up_weight,
        down_weight,
        attn_gain,
        mlp_gain,
        scale_param,
        cotangent,
        reach,
        block_index,
        scale_vecs,
    )


def solution(mesh):
    return jax.shard_map(
        per_device,
        mesh=mesh,
        in_specs=(
            P("batch", ("blk", "head"), None),
            P("batch", None),
            P(None, ("batch", "blk", "head"), None),
            P(None, ("batch", "blk", "head"), None),
            P(None, ("batch", "blk", "head"), None),
            P(None, ("batch", "blk", "head"), None),
            P(None, ("batch", "blk", "head")),
            P(None, ("batch", "blk", "head")),
            P(),
            P("batch", ("blk", "head"), None),
        ),
        out_specs=(
            P("batch", ("blk", "head"), None),
            P("batch", ("blk", "head"), None),
            P(None, ("batch", "blk", "head"), None),
            P(None, ("batch", "blk", "head"), None),
            P(None, ("batch", "blk", "head"), None),
            P(None, ("batch", "blk", "head"), None),
            P(None, ("batch", "blk", "head")),
            P(None, ("batch", "blk", "head")),
            P(),
        ),
        check_vma=False,
    )
```

profile of v0, /device:TPU:0, one launch (start us, length us, event | category | flops | bytes accessed | tf_op | source)
XLA Modules:
  0.0 1702.3 jit_solution(14027726372671148429)
XLA Ops:
  26.4 40.5 %all-reduce.12 = (bf16[1280]{0:T(1024)(128)(2,1)S(1)}, bf16[1280]{0:T(1024)(128)(2,1)S(1)}, bf16[1280]{0:T(1024)(128)(2,1)}, bf16[1280]{0:T(1024)(128)(2,1)}) all-reduce(bf16[1280]{0:T(1024)(128)(2,1)S(1)} %dynamic-update-slice, ...), channel_id=2, replica_groups=mesh['batch'=4,'blk'=2,'head'=4] {'batch','blk','head'}, use_global_device_ids=true, to_apply=%add.1 | all-reduce | flops 5120 | bytes 20480
  68.2 16.7 all-gather.19.cloned.1.call-done
  90.2 21.1 %all-gather.17.cloned.1.call-done = bf16[2,512,1280]{2,1,0:T(8,128)(2,1)} async-done(((bf16[2,128,1280]{2,1,0:T(8,128)(2,1)}), bf16[2,512,1280]{2,1,0:T(8,128)(2,1)}) %all-gather.17.cloned.1.call-update) | async-done | bytes 2621456 | tf_op jit(solution)/shard_map/all_gather | solution.py:143
  127.0 23.4 %collective-permute-done = bf16[2,512,2,320]{1,3,2,0:T(8,128)(2,1)} collective-permute-done((bf16[2,512,2,320]{1,3,2,0:T(8,128)(2,1)S(1)}, bf16[2,512,2,320]{1,3,2,0:T(8,128)(2,1)}, u32[]{:S(2)}, u32[]{:S(2)}) %collective-permute-start) | collective-permute-done | bytes 1310752 | tf_op jit(solution)/shard_map/ppermute | solution.py:19
  186.4 33.6 %all_gather.64 = bf16[1280,1,320]{2,0,1:T(8,128)(2,1)S(1)} all-gather(bf16[160,1,320]{2,0,1:T(8,128)(2,1)S(1)} %bitcast.668), channel_id=1, replica_groups=mesh['batch'=4,'blk'=2,'head'=4] {'batch','blk'}, dimensions={0}, use_global_device_ids=true | all-gather | bytes 921600 | tf_op jit(solution)/shard_map/all_gather | solution.py:195
  261.0 32.7 %all_gather.67 = bf16[1280,1,320]{2,0,1:T(8,128)(2,1)S(1)} all-gather(bf16[160,1,320]{2,0,1:T(8,128)(2,1)S(1)} %bitcast.669), channel_id=1, replica_groups=mesh['batch'=4,'blk'=2,'head'=4] {'batch','blk'}, dimensions={0}, use_global_device_ids=true | all-gather | bytes 921600 | tf_op jit(solution)/shard_map/all_gather | solution.py:196
  333.7 35.5 %all_gather.69 = bf16[1280,1,320]{2,0,1:T(8,128)(2,1)S(1)} all-gather(bf16[160,1,320]{2,0,1:T(8,128)(2,1)S(1)} %bitcast.670), channel_id=1, replica_groups=mesh['batch'=4,'blk'=2,'head'=4] {'batch','blk'}, dimensions={0}, use_global_device_ids=true | all-gather | bytes 921600 | tf_op jit(solution)/shard_map/all_gather | solution.py:197
  398.9 21.7 %all-gather.25.cloned.1.call-done = bf16[2,512,1280]{2,1,0:T(8,128)(2,1)} async-done(((bf16[2,128,1280]{2,1,0:T(8,128)(2,1)}), bf16[2,512,1280]{2,1,0:T(8,128)(2,1)}) %all-gather.25.cloned.1.call-update) | async-done | bytes 2621456 | tf_op jit(solution)/shard_map/all_gather | solution.py:143
  430.0 27.8 %collective-permute-done.1 = bf16[2,512,2,320]{1,3,2,0:T(8,128)(2,1)S(1)} collective-permute-done((bf16[2,512,2,320]{1,3,2,0:T(8,128)(2,1)S(1)}, bf16[2,512,2,320]{1,3,2,0:T(8,128)(2,1)S(1)}, u32[]{:S(2)}, u32[]{:S(2)}) %collective-permute-start.1) | collective-permute-done | bytes 1310752 | tf_op jit(solution)/shard_map/ppermute | solution.py:19
  492.1 33.2 %all_gather.74 = bf16[1280,1,320]{2,0,1:T(8,128)(2,1)S(1)} all-gather(bf16[160,1,320]{2,0,1:T(8,128)(2,1)S(1)} %bitcast.671), channel_id=1, replica_groups=mesh['batch'=4,'blk'=2,'head'=4] {'batch','blk'}, dimensions={0}, use_global_device_ids=true | all-gather | bytes 921600 | tf_op jit(solution)/shard_map/all_gather | solution.py:195
  577.0 34.5 %all_gather.79 = bf16[1280,1,320]{2,0,1:T(8,128)(2,1)} all-gather(bf16[160,1,320]{2,0,1:T(8,128)(2,1)S(1)} %bitcast.672), channel_id=1, replica_groups=mesh['batch'=4,'blk'=2,'head'=4] {'batch','blk'}, dimensions={0}, use_global_device_ids=true | all-gather | bytes 921600 | tf_op jit(solution)/shard_map/all_gather | solution.py:197
  636.7 33.0 %all_gather.77 = bf16[1280,1,320]{2,0,1:T(8,128)(2,1)S(1)} all-gather(bf16[160,1,320]{2,0,1:T(8,128)(2,1)S(1)} %bitcast.673), channel_id=1, replica_groups=mesh['batch'=4,'blk'=2,'head'=4] {'batch','blk'}, dimensions={0}, use_global_device_ids=true | all-gather | bytes 921600 | tf_op jit(solution)/shard_map/all_gather | solution.py:196
  678.9 21.0 %all-gather.35.cloned.1.call-done = bf16[2,2048,320]{1,2,0:T(8,128)(2,1)} async-done(((bf16[2,512,320]{1,2,0:T(8,128)(2,1)}), bf16[2,2048,320]{1,2,0:T(8,128)(2,1)}) %all-gather.35.cloned.1.call-update) | async-done | bytes 2621456 | tf_op jit(solution)/shard_map/all_gather | solution.py:143
  702.8 12.7 all_to_all.283
  719.5 17.8 %reduce-scatter.15.cloned.1.call-done = bf16[2,128,1280]{2,1,0:T(8,128)(2,1)} async-done(((bf16[2,512,1280]{2,1,0:T(8,128)(2,1)}), bf16[2,128,1280]{2,1,0:T(8,128)(2,1)}) %reduce-scatter.15.cloned.1.call-update) | async-done | bytes 655376 | tf_op jit(solution)/shard_map/reduce_scatter | solution.py:147
  744.7 12.7 all_to_all.284
  764.7 58.8 %all-reduce.18.cloned.1.call-done = bf16[2,4,512,320]{2,3,1,0:T(8,128)(2,1)} async-done(((bf16[2,4,512,320]{2,3,1,0:T(8,128)(2,1)}), bf16[2,4,512,320]{2,3,1,0:T(8,128)(2,1)}) %all-reduce.18.cloned.1.call-update) | async-done | bytes 2621456
  833.3 11.9 multiply_reduce_fusion.1
  845.2 12.3 multiply_convert_fusion.1
  863.5 28.3 %collective-permute-done.2 = bf16[2,512,2,320]{1,3,2,0:T(8,128)(2,1)} collective-permute-done((bf16[2,512,2,320]{1,3,2,0:T(8,128)(2,1)S(1)}, bf16[2,512,2,320]{1,3,2,0:T(8,128)(2,1)}, u32[]{:S(2)}, u32[]{:S(2)}) %collective-permute-start.2) | collective-permute-done | bytes 1310752 | tf_op jit(solution)/shard_map/ppermute | solution.py:19
  900.2 33.9 %reduce-scatter.17.cloned.1.call-done = bf16[2,128,1280]{2,1,0:T(8,128)(2,1)} async-done(((bf16[2,512,1280]{2,1,0:T(8,128)(2,1)}), bf16[2,128,1280]{2,1,0:T(8,128)(2,1)}) %reduce-scatter.17.cloned.1.call-update) | async-done | bytes 655376 | tf_op jit(solution)/shard_map/reduce_scatter | solution.py:147
  940.4 12.7 all_to_all.285
  961.2 34.8 %reduce-scatter.19.cloned.1.call-done = bf16[2,1,512,320]{2,3,0,1:T(8,128)(2,1)} async-done(((bf16[2,4,512,320]{2,3,0,1:T(8,128)(2,1)}), bf16[2,1,512,320]{2,3,0,1:T(8,128)(2,1)}) %reduce-scatter.19.cloned.1.call-update) | async-done | bytes 655376 | tf_op jit(solution)/shard_map/reduce_scatter | solution.py:147
  1001.2 34.7 %reduce-scatter.21.cloned.1.call-done = bf16[2,128,1280]{2,1,0:T(8,128)(2,1)} async-done(((bf16[2,512,1280]{2,1,0:T(8,128)(2,1)}), bf16[2,128,1280]{2,1,0:T(8,128)(2,1)}) %reduce-scatter.21.cloned.1.call-update) | async-done | bytes 655376 | tf_op jit(solution)/shard_map/reduce_scatter | solution.py:147
  1043.0 12.7 all_to_all.286
  1060.5 59.4 %all-reduce.20.cloned.1.call-done = bf16[2,4,512,320]{2,3,1,0:T(8,128)(2,1)} async-done(((bf16[2,4,512,320]{2,3,1,0:T(8,128)(2,1)}), bf16[2,4,512,320]{2,3,1,0:T(8,128)(2,1)}) %all-reduce.20.cloned.1.call-update) | async-done | bytes 2621456
  1129.7 12.8 multiply_reduce_fusion
  1142.5 12.3 multiply_convert_fusion
  1178.2 14.5 collective-permute-done.3
  1266.2 17.7 %copy.439 = bf16[2,1280,3,320]{3,0,2,1:T(2,128)(2,1)} copy(bf16[2,1280,3,320]{1,3,2,0:T(8,128)(2,1)} %pad_maximum_fusion) | data formatting | bytes 9830400 | tf_op jit(solution)/shard_map/stack | solution.py:421
  1287.5 44.2 %all-reduce.11 = (f32[2,1280]{1,0:T(2,128)S(1)}, f32[2,1280]{1,0:T(2,128)S(1)}, f32[2,80]{1,0:T(2,128)}) all-reduce(f32[2,1280]{1,0:T(2,128)S(1)} %pad_maximum_fusion.10, f32[2,1280]{1,0:T(2,128)S(1)} %pad_maximum_fusion.11, f32[2,80]{1,0:T(2,128)S(1)} %pad_maximum_fusion.12), channel_id=1, replica_groups=mesh['batch'=4,'blk'=2,'head'=4] {'batch','blk','head'}, use_global_device_ids=true, to_apply=%region_28.29 | all-reduce | flops 5280 | bytes 42240 | tf_op jit(solution)/shard_map/psum | solution.py:444
  1334.3 314.7 %all-reduce.22.cloned.1.call-done = (bf16[2,1280,3,320]{3,0,2,1:T(2,128)(2,1)}, bf16[2,1280,1,320]{3,0,2,1:T(2,128)(2,1)}, bf16[2,1280,1,320]{3,0,2,1:T(2,128)(2,1)}, bf16[2,1280,1,320]{3,0,2,1:T(2,128)(2,1)}) async-done(((bf16[2,1280,3,320]{3,0,2,1:T(2,128)(2,1)}, bf16[2,1280,1,320]{3,0,2,1:T(2,128)(2,1)}, bf16[2,1280,1,320]{3,0,2,1:T(2,128)(2,1)}, bf16[2,1280,1,320]{3,0,2,1:T(2,128)(2,1)}), ...) | async-done | bytes 9830416
  (507 shorter events, 552.0 us)
Async XLA Ops:
  7.2 77.8 %all-gather.19.cloned.1.call-start = ((), (), s32[]{:S(2)}) async-start(), calls=%async_computation.27 | async-start | bytes 3317760 | tf_op jit(solution)/shard_map/all_gather | solution.py:194
  25.3 86.0 %all-gather.17.cloned.1.call-start = ((), (), s32[]{:S(2)}) async-start(), calls=%async_computation.26 | async-start | bytes 3276800 | tf_op jit(solution)/shard_map/all_gather | solution.py:143
  68.2 151.8 %all-gather.21.cloned.1.call-start = ((), (), s32[]{:S(2)}) async-start(), calls=%async_computation.28 | async-start | bytes 3276800 | tf_op jit(solution)/shard_map/all_gather | solution.py:143
  118.6 31.8 %collective-permute-start = (bf16[2,512,2,320]{1,3,2,0:T(8,128)(2,1)S(1)}, bf16[2,512,2,320]{1,3,2,0:T(8,128)(2,1)}, u32[]{:S(2)}, u32[]{:S(2)}) collective-permute-start(bf16[2,512,2,320]{1,3,2,0:T(8,128)(2,1)S(1)} %slice.179), channel_id=1, source_target_pairs={{0,4},{1,5},{2,6},{3,7},{8,12},{9,13},{10,14},{11,15},{16,20},{17,... | collective-permute-start | bytes 3932168 | tf_op jit(solution)/shard_map/ppermute | solution.py:19
  224.0 13.7 all-to-all-start.2
  227.5 66.2 %all-gather.23.cloned.1.call-start = ((), (), s32[]{:S(2)}) async-start(), calls=%async_computation.29 | async-start | bytes 3276800 | tf_op jit(solution)/shard_map/all_gather | solution.py:143
  242.9 126.2 %all-gather.33.cloned.1.call-start = ((), (), s32[]{:S(2)}) async-start(), calls=%async_computation.40 | async-start | bytes 3276800 | tf_op jit(solution)/shard_map/all_gather | solution.py:143
  298.3 95.3 %all-gather.27.cloned.1.call-start = ((), (), s32[]{:S(2)}) async-start(), calls=%async_computation.31 | async-start | bytes 3317760 | tf_op jit(solution)/shard_map/all_gather | solution.py:194
  373.2 13.7 all-to-all-start.5
  376.7 43.9 %all-gather.25.cloned.1.call-start = ((), (), s32[]{:S(2)}) async-start(), calls=%async_computation.30 | async-start | bytes 3276800 | tf_op jit(solution)/shard_map/all_gather | solution.py:143
  391.5 133.8 %all-gather.29.cloned.1.call-start = ((), (), s32[]{:S(2)}) async-start(), calls=%async_computation.32 | async-start | bytes 3276800 | tf_op jit(solution)/shard_map/all_gather | solution.py:143
  426.0 31.8 %collective-permute-start.1 = (bf16[2,512,2,320]{1,3,2,0:T(8,128)(2,1)S(1)}, bf16[2,512,2,320]{1,3,2,0:T(8,128)(2,1)S(1)}, u32[]{:S(2)}, u32[]{:S(2)}) collective-permute-start(bf16[2,512,2,320]{1,3,2,0:T(8,128)(2,1)S(1)} %slice.178), channel_id=1, source_target_pairs={{0,4},{1,5},{2,6},{3,7},{8,12},{9,13},{10,14},{11,15},{16,20},{17,... | collective-permute-start | bytes 3932168 | tf_op jit(solution)/shard_map/ppermute | solution.py:19
  529.3 13.7 all-to-all-start.8
  532.8 136.9 %all-gather.31.cloned.1.call-start = ((), (), s32[]{:S(2)}) async-start(), calls=%async_computation.33 | async-start | bytes 3276800 | tf_op jit(solution)/shard_map/all_gather | solution.py:143
  561.3 9.0 all-to-all-start.10
  570.3 41.2 %all-to-all-start.12 = ((bf16[2,1,128,4,320]{2,4,0,1,3:T(8,128)(2,1)}), bf16[2,1,128,4,320]{2,4,0,1,3:T(8,128)(2,1)S(1)}, u32[]{:S(2)}, u32[]{:S(2)}) async-start(bf16[2,1,128,4,320]{2,4,0,1,3:T(8,128)(2,1)} %copy.415), calls=%async_computation.12 | async-start | bytes 1310720 | tf_op jit(solution)/shard_map/all_to_all | solution.py:170
  573.8 100.2 %reduce-scatter.13.cloned.1.call-start = ((), (), s32[]{:S(2)}) async-start(), calls=%async_computation.34 | async-start | bytes 3276800 | tf_op jit(solution)/shard_map/reduce_scatter | solution.py:147
  619.5 80.5 %all-gather.35.cloned.1.call-start = ((), (), s32[]{:S(2)}) async-start(), calls=%async_computation.41 | async-start | bytes 3276800 | tf_op jit(solution)/shard_map/all_gather | solution.py:143
  673.9 63.3 %reduce-scatter.15.cloned.1.call-start = ((), (), s32[]{:S(2)}) async-start(), calls=%async_computation.35 | async-start | bytes 3276800 | tf_op jit(solution)/shard_map/reduce_scatter | solution.py:147
  678.9 144.6 %all-reduce.18.cloned.1.call-start = ((), (), s32[]{:S(2)}) async-start(), calls=%async_computation.42 | async-start | bytes 5242880
  763.5 170.7 %reduce-scatter.17.cloned.1.call-start = ((), (), s32[]{:S(2)}) async-start(), calls=%async_computation.36 | async-start | bytes 3276800 | tf_op jit(solution)/shard_map/reduce_scatter | solution.py:147
  859.3 32.6 %collective-permute-start.2 = (bf16[2,512,2,320]{1,3,2,0:T(8,128)(2,1)S(1)}, bf16[2,512,2,320]{1,3,2,0:T(8,128)(2,1)}, u32[]{:S(2)}, u32[]{:S(2)}) collective-permute-start(bf16[2,512,2,320]{1,3,2,0:T(8,128)(2,1)S(1)} %fusion.29), channel_id=1, source_target_pairs={{4,0},{5,1},{6,2},{7,3},{12,8},{13,9},{14,10},{15,11},{20,16},{21,... | collective-permute-start | bytes 3932168 | tf_op jit(solution)/shard_map/ppermute | solution.py:19
  900.0 96.0 %reduce-scatter.19.cloned.1.call-start = ((), (), s32[]{:S(2)}) async-start(), calls=%async_computation.37 | async-start | bytes 3276800 | tf_op jit(solution)/shard_map/reduce_scatter | solution.py:147
  961.2 74.8 %reduce-scatter.21.cloned.1.call-start = ((), (), s32[]{:S(2)}) async-start(), calls=%async_computation.38 | async-start | bytes 3276800 | tf_op jit(solution)/shard_map/reduce_scatter | solution.py:147
  1001.2 118.7 %all-reduce.20.cloned.1.call-start = ((), (), s32[]{:S(2)}) async-start(), calls=%async_computation.43 | async-start | bytes 5242880
  1059.8 226.2 %reduce-scatter.23.cloned.1.call-start = ((), (), s32[]{:S(2)}) async-start(), calls=%async_computation.39 | async-start | bytes 3276800 | tf_op jit(solution)/shard_map/reduce_scatter | solution.py:147
  1160.1 32.6 %collective-permute-start.3 = (bf16[2,512,2,320]{1,3,2,0:T(8,128)(2,1)}, bf16[2,512,2,320]{1,3,2,0:T(8,128)(2,1)}, u32[]{:S(2)}, u32[]{:S(2)}) collective-permute-start(bf16[2,512,2,320]{1,3,2,0:T(8,128)(2,1)} %fusion.27), channel_id=1, source_target_pairs={{4,0},{5,1},{6,2},{7,3},{12,8},{13,9},{14,10},{15,11},{20,16},{21,... | collective-permute-start | bytes 3932168 | tf_op jit(solution)/shard_map/ppermute | solution.py:19
  1200.7 448.4 %all-reduce.22.cloned.1.call-start = ((), (), s32[]{:S(2)}) async-start(), calls=%async_computation.44 | async-start | bytes 23592960
  1650.8 9.2 all-to-all-start.17
  1660.1 9.2 all-to-all-start.18
  1669.3 9.2 all-to-all-start.19
  1678.5 14.6 all-to-all-start.16
  (99 other events, 884.0 us)
Sparse Core Ops, SparseCore 0:
  25.4 59.4 all-gather.18
  87.1 24.1 all-gather.16
  168.0 27.7 all-gather.20
  243.1 26.9 all-gather.22
  298.4 27.9 all-gather.32
  329.0 64.5 all-gather.26
  395.7 24.8 all-gather.24
  474.3 27.6 all-gather.28
  550.7 27.1 all-gather.30
  619.6 36.6 reduce-scatter.12
  674.0 25.8 all-gather.34
  702.5 34.6 reduce-scatter.14
  763.6 59.8 all-reduce.17
  900.1 33.9 reduce-scatter.16
  961.3 34.6 reduce-scatter.18
  1001.3 34.6 reduce-scatter.20
  1059.9 59.9 all-reduce.19
  1200.8 34.0 reduce-scatter.22
  1284.1 364.8 all-reduce.21
where the time goes:
time: 1710 us; the launch traced here: 1700 us
  waiting for transfers between devices  782 us (46%)
  blocking collectives  399 us (23%)
  local copies, waits for them, and re-layouts  172 us (10%)
  matrix products  165 us (10%)
  other arithmetic  124 us (7%)
  starting transfers between devices  44.1 us (3%)
    unnamed x22, waiting for transfers between devices  433 us
    reduce_scatter x6, waiting for transfers between devices, head_sums(): lax.psum_scatter(partial_in.astype(jnp.bfloat16), 'head', scatter_dimensi...  121 us
    ppermute x4, waiting for transfers between devices, shifted(): return lax.ppermute(block, axis, route)  94.1 us
    all_gather x2, blocking collectives, gather_columns(): lax.all_gather(moved[3], ('batch', 'blk'), axis=0, tiled=True)  70 us
    all_gather x2, blocking collectives, gather_columns(): lax.all_gather(moved[1], ('batch', 'blk'), axis=0, tiled=True)  66.8 us
    all_gather x2, blocking collectives, gather_columns(): lax.all_gather(moved[2], ('batch', 'blk'), axis=0, tiled=True)  65.7 us
    all_gather x8, waiting for transfers between devices, over_heads(): return lax.all_gather(values_in, 'head', axis=1, tiled=True)  63.8 us
    unnamed x236, local copies, waits for them, and re-layouts  50.5 us
  transfers between devices with their start and end apart: 32, of which 24 were waited for; matrix products, arithmetic and copies ran while one was open for 14% of the time, Pallas kernels for 0%

commit v1 on v0

v1 whole, which is shorter than its diff:
```python
import math

import jax
import jax.numpy as jnp
from jax import lax
from jax.sharding import PartitionSpec as P

WINDOW = 1024
EPSILON = 1e-06
SCALE_BASE = 1.4426950408889634
MASKED_SCORE = -1e30

ALL = ("batch", "blk", "head")
REST = ("batch", "blk")
F32 = jnp.float32
BF16 = jnp.bfloat16


def shifted(block, axis, distance):
    devices = range(lax.axis_size(axis))
    route = [(i - distance, i) for i in devices if i - distance in devices]
    return lax.ppermute(block, axis, route)


def dot(left, right):
    return jnp.dot(left, right, preferred_element_type=F32)


def dot_rows(left, right):
    return lax.dot_general(left, right, (((0,), (0,)), ((), ())), preferred_element_type=F32)


def dot_cols(left, right):
    return lax.dot_general(left, right, (((1,), (1,)), ((), ())), preferred_element_type=F32)


def normalize(stream, gain):
    factor = lax.rsqrt(jnp.mean(stream * stream, axis=-1, keepdims=True) + EPSILON)
    return stream * factor * gain, factor


def norm_back(upper, stream, factor, gain):
    inner = upper * gain
    gain_grad = jnp.sum(upper * stream * factor, axis=0)
    lower = factor * inner - stream * factor * factor * factor * jnp.mean(
        inner * stream, axis=-1, keepdims=True
    )
    return lower, gain_grad


class Plan:
    def __init__(self, tokens):
        self.seqs, self.rows, self.width = tokens.shape
        self.heads = lax.axis_size("head")
        self.blks = lax.axis_size("blk")
        self.block = self.rows * self.heads
        self.whole = self.seqs % self.blks == 0
        if self.whole:
            self.groups, self.own_seqs = self.blks, self.seqs // self.blks
            self.reach = 0
        else:
            self.groups, self.own_seqs = 1, self.seqs
            self.reach = min((WINDOW - 1) // self.block + 1, self.blks - 1)
        self.length = self.groups * self.block
        self.tokens = self.seqs * self.rows


def to_plan(plan, array):
    if plan.whole and plan.blks > 1:
        array = lax.all_to_all(array, "blk", split_axis=0, concat_axis=0, tiled=True)
    return array.reshape(plan.tokens, plan.width)


def from_plan(plan, flat):
    array = flat.reshape(plan.seqs, plan.rows, plan.width)
    if plan.whole and plan.blks > 1:
        array = lax.all_to_all(array, "blk", split_axis=0, concat_axis=0, tiled=True)
    return array


def in_sequence(plan, by_head, width):
    parts = by_head.reshape(plan.heads, plan.groups, plan.own_seqs, plan.rows, width)
    return parts.transpose(2, 1, 0, 3, 4).reshape(-1, width)


def by_owner(plan, rows, width):
    parts = rows.reshape(plan.own_seqs, plan.groups, plan.heads, plan.rows, width)
    return parts.transpose(2, 1, 0, 3, 4).reshape(plan.heads, plan.tokens, width)


def gather_tokens(plan, rows):
    moved = lax.all_gather(rows, "head", axis=0, tiled=False)
    return in_sequence(plan, moved, rows.shape[-1])


def scatter_tokens(plan, rows):
    width = rows.shape[-1]
    return lax.psum_scatter(
        by_owner(plan, rows.astype(BF16), width), "head", scatter_dimension=0, tiled=False
    ).astype(F32)


def heads_to_tokens(plan, rows):
    part = rows.shape[-1]
    moved = lax.all_to_all(
        by_owner(plan, rows, part), "head", split_axis=0, concat_axis=0, tiled=True
    )
    return moved.transpose(1, 0, 2).reshape(plan.tokens, plan.heads * part)


def tokens_to_heads(plan, rows):
    part = rows.shape[-1] // plan.heads
    sent = rows.reshape(plan.tokens, plan.heads, part).transpose(1, 0, 2)
    moved = lax.all_to_all(sent, "head", split_axis=0, concat_axis=0, tiled=True)
    return in_sequence(plan, moved, part)


def gather_qkv(rows):
    own, width = rows.shape
    heads = lax.axis_size("head")
    part = width // 3 // heads
    sent = rows.reshape(own, 3, heads, part).transpose(2, 0, 1, 3).reshape(heads, own, 3 * part)
    moved = lax.all_to_all(sent, "head", split_axis=0, concat_axis=0, tiled=True)
    full = lax.all_gather(moved, REST, axis=0, tiled=True)
    return full.reshape(-1, 3 * part)


def scatter_qkv(grad):
    heads = lax.axis_size("head")
    part = grad.shape[1] // 3
    summed = lax.psum_scatter(grad.astype(BF16), REST, scatter_dimension=0, tiled=True)
    own = summed.shape[0] // heads
    moved = lax.all_to_all(
        summed.reshape(heads, own, 3 * part), "head", split_axis=0, concat_axis=0, tiled=True
    )
    return (
        moved.reshape(heads, own, 3, part)
        .transpose(1, 2, 0, 3)
        .reshape(own, 3 * heads * part)
        .astype(F32)
    )


def window_mask(plan, segments, block_index):
    key_count = plan.length + plan.reach * plan.block
    if plan.whole:
        query_segs, key_segs = segments, segments
    else:
        leading = jnp.full((plan.own_seqs, plan.reach * plan.block), -1, jnp.int32)
        padded = jnp.concatenate([leading, segments], axis=1)
        start = block_index * plan.block
        query_segs = lax.dynamic_slice_in_dim(segments, start, plan.block, 1)
        key_segs = lax.dynamic_slice_in_dim(padded, start, key_count, 1)
    query_place = jnp.arange(plan.length, dtype=jnp.int32)[:, None] + plan.reach * plan.block
    key_place = jnp.arange(key_count, dtype=jnp.int32)[None, :]
    near = (key_place <= query_place) & (query_place - key_place < WINDOW)
    return (key_segs[:, None, :] == query_segs[:, :, None]) & near[None]


def with_earlier(plan, own):
    arrived = [own]
    for _ in range(plan.reach):
        arrived.append(shifted(arrived[-1], "blk", 1))
    return jnp.concatenate(arrived[::-1], axis=1) if plan.reach else own


def to_earlier(plan, grads):
    if not plan.reach:
        return grads
    block = plan.block
    total = grads[:, :block]
    for step in range(1, plan.reach + 1):
        total = (
            shifted(total.astype(BF16), "blk", -1).astype(F32)
            + grads[:, step * block : (step + 1) * block]
        )
    return total


def scores_of(queries, keys, allowed):
    scores = jnp.einsum("sqhd,skhd->shqk", queries, keys, preferred_element_type=F32)
    return jnp.where(allowed[:, None], scores, MASKED_SCORE)


def attend(queries, keys, values, allowed):
    scores = scores_of(queries, keys, allowed)
    top_score = jnp.max(scores, axis=-1, keepdims=True)
    exp_terms = jnp.exp(scores - top_score)
    totals = jnp.sum(exp_terms, axis=-1, keepdims=True)
    probs_low = (exp_terms / totals).astype(BF16)
    attended = jnp.einsum("shqk,skhd->sqhd", probs_low, values, preferred_element_type=F32)
    return attended, top_score + jnp.log(totals)


def attend_back(queries, keys, values, allowed, log_total, attended_grad):
    probs = jnp.exp(scores_of(queries, keys, allowed) - log_total)
    probs_low = probs.astype(BF16)
    values_grad = jnp.einsum(
        "shqk,sqhd->skhd", probs_low, attended_grad, preferred_element_type=F32
    )
    probs_grad = jnp.einsum("sqhd,skhd->shqk", attended_grad, values, preferred_element_type=F32)
    row_dot = jnp.sum(probs_grad * probs, axis=-1, keepdims=True)
    scores_low = (probs * (probs_grad - row_dot)).astype(BF16)
    queries_grad = jnp.einsum("shqk,skhd->sqhd", scores_low, keys, preferred_element_type=F32)
    keys_grad = jnp.einsum("shqk,sqhd->skhd", scores_low, queries, preferred_element_type=F32)
    return queries_grad, keys_grad, values_grad


def forward(plan, stream, qkv, dense, gains, scale_vec, allowed):
    width = plan.width
    head_dim = scale_vec.shape[0]
    part = qkv.shape[1] // 3
    local_heads = part // head_dim
    split = (plan.own_seqs, plan.length, local_heads, head_dim)
    out_w, up_w, down_w = dense[:, :width], dense[:, width:-width], dense[:, -width:]
    normed, factor_one = normalize(stream, gains[0])
    normed_all = gather_tokens(plan, normed.astype(BF16))
    projected = dot(normed_all, qkv)
    query_pre = projected[:, :part].reshape(split)
    queries = (query_pre * scale_vec).astype(BF16)
    keys = with_earlier(plan, projected[:, part : 2 * part].astype(BF16).reshape(split))
    values = with_earlier(plan, projected[:, 2 * part :].astype(BF16).reshape(split))
    attended_part, log_total = attend(queries, keys, values, allowed)
    attended = heads_to_tokens(plan, attended_part.astype(BF16).reshape(-1, part))
    middle = stream + dot(attended, out_w)
    normed_two, factor_two = normalize(middle, gains[1])
    normed_two = normed_two.astype(BF16)
    hidden = dot(normed_two, up_w)
    active = (hidden * jax.nn.sigmoid(hidden)).astype(BF16)
    result = middle + dot(active, down_w)
    kept = (
        stream, factor_one, normed_all, query_pre, queries, keys, values, log_total,
        attended, middle, factor_two, normed_two, hidden, active,
    )
    return result, kept


def backward(plan, upper, kept, qkv, dense, gains, scale_vec, allowed):
    (
        stream, factor_one, normed_all, query_pre, queries, keys, values, log_total,
        attended, middle, factor_two, normed_two, hidden, active,
    ) = kept
    width = plan.width
    head_dim = scale_vec.shape[0]
    part = qkv.shape[1] // 3
    out_w, up_w, down_w = dense[:, :width], dense[:, width:-width], dense[:, -width:]
    upper_low = upper.astype(BF16)
    down_grad = dot_rows(active, upper_low)
    active_grad = dot_cols(upper_low, down_w)
    gate = jax.nn.sigmoid(hidden)
    hidden_low = (active_grad * gate * (1.0 + hidden * (1.0 - gate))).astype(BF16)
    up_grad = dot_rows(normed_two, hidden_low)
    extra_two, mlp_gain_grad = norm_back(dot_cols(hidden_low, up_w), middle, factor_two, gains[1])
    middle_grad = upper + extra_two
    middle_low = middle_grad.astype(BF16)
    out_grad = dot_rows(attended, middle_low)
    dense_grad = jnp.concatenate([out_grad, up_grad, down_grad], axis=1).astype(BF16)
    dense_own = lax.psum_scatter(dense_grad, ALL, scatter_dimension=0, tiled=True)
    attended_grad = tokens_to_heads(plan, dot_cols(middle_low, out_w).astype(BF16))
    queries_grad, keys_grad, values_grad = attend_back(
        queries, keys, values, allowed, log_total, attended_grad.reshape(queries.shape)
    )
    query_bar = queries_grad.astype(BF16).astype(F32)
    scale_vec_grad = jnp.sum((query_bar * query_pre).reshape(-1, head_dim), axis=0)
    query_low = (query_bar * scale_vec).astype(BF16).reshape(-1, part)
    keys_low = to_earlier(plan, keys_grad).astype(BF16).reshape(-1, part)
    values_low = to_earlier(plan, values_grad).astype(BF16).reshape(-1, part)
    projected_low = jnp.concatenate([query_low, keys_low, values_low], axis=1)
    normed_grad = scatter_tokens(plan, dot_cols(projected_low, qkv))
    qkv_own = scatter_qkv(dot_rows(normed_all, projected_low))
    extra_one, attn_gain_grad = norm_back(normed_grad, stream, factor_one, gains[0])
    lower = middle_grad + extra_one
    return lower, qkv_own, dense_own, (attn_gain_grad, mlp_gain_grad), scale_vec_grad


def per_device(
    tokens,
    segments,
    qkv_weight,
    out_weight,
    up_weight,
    down_weight,
    attn_gain,
    mlp_gain,
    scale_param,
    cotangent,
):
    plan = Plan(tokens)
    layers, head_dim = scale_param.shape
    block_index = lax.axis_index("blk")
    scale_vecs = SCALE_BASE / math.sqrt(head_dim) * jax.nn.softplus(scale_param)
    own_gains = jnp.concatenate([attn_gain, mlp_gain], axis=0)
    gains = (
        lax.all_gather(own_gains.reshape(1, -1), ALL, axis=0, tiled=True)
        .reshape(-1, 2 * layers, attn_gain.shape[1])
        .transpose(1, 0, 2)
        .reshape(2 * layers, plan.width)
        .astype(F32)
    )
    if plan.whole:
        segments = lax.dynamic_slice_in_dim(
            segments, block_index * plan.own_seqs, plan.own_seqs, 0
        )
    allowed = window_mask(plan, segments, block_index)
    stream = to_plan(plan, tokens).astype(F32)
    qkvs, denses, kept = [], [], []
    for layer in range(layers):
        qkvs.append(gather_qkv(qkv_weight[layer]))
        own = jnp.concatenate([out_weight[layer], up_weight[layer], down_weight[layer]], axis=1)
        denses.append(lax.all_gather(own, ALL, axis=0, tiled=True))
        layer_gains = (gains[layer], gains[layers + layer])
        stream, saved = forward(
            plan, stream, qkvs[layer], denses[layer], layer_gains, scale_vecs[layer], allowed
        )
        kept.append(saved)
    layer_out = from_plan(plan, stream.astype(BF16))
    upper = to_plan(plan, cotangent).astype(F32)
    qkv_grads, dense_grads = [None] * layers, [None] * layers
    gain_grads, scale_grads = [None] * layers, [None] * layers
    for layer in reversed(range(layers)):
        layer_gains = (gains[layer], gains[layers + layer])
        upper, qkv_grads[layer], dense_grads[layer], gain_grads[layer], scale_grads[layer] = (
            backward(
                plan, upper, kept[layer], qkvs[layer], denses[layer], layer_gains,
                scale_vecs[layer], allowed,
            )
        )
    input_grad = from_plan(plan, upper.astype(BF16)).astype(F32)
    small = jnp.concatenate(
        [g[0] for g in gain_grads] + [g[1] for g in gain_grads] + scale_grads, axis=0
    )
    total = lax.psum(small, ALL)
    gain_total = total[: 2 * layers * plan.width].reshape(2 * layers, plan.width)
    owner = lax.axis_index(ALL)
    gain_rows = attn_gain.shape[1]
    own_total = lax.dynamic_slice_in_dim(gain_total, owner * gain_rows, gain_rows, 1)
    scale_total = total[2 * layers * plan.width :].reshape(layers, head_dim)
    scale_grad = scale_total * (SCALE_BASE / math.sqrt(head_dim)) * jax.nn.sigmoid(scale_param)
    dense_all = jnp.stack(dense_grads).astype(F32)
    width = plan.width
    return (
        layer_out,
        input_grad,
        jnp.stack(qkv_grads),
        dense_all[:, :, :width],
        dense_all[:, :, width:-width],
        dense_all[:, :, -width:],
        own_total[:layers],
        own_total[layers:],
        scale_grad,
    )


def solution(mesh):
    rows = P(None, ALL, None)
    by_token = P("batch", ("blk", "head"), None)
    return jax.shard_map(
        per_device,
        mesh=mesh,
        in_specs=(
            by_token, P("batch", None), rows, rows, rows, rows, P(None, ALL), P(None, ALL), P(),
            by_token,
        ),
        out_specs=(
            by_token, by_token, rows, rows, rows, rows, P(None, ALL), P(None, ALL), P(),
        ),
        check_vma=False,
    )
```

time: 1710 us -> 1050 us (0.61)
  blocking collectives: 399 us -> 132 us
  waiting for transfers between devices: 782 us -> 526 us
  local copies, waits for them, and re-layouts: 172 us -> 93.5 us
  other arithmetic: 124 us -> 72 us
    unnamed x22 -> x14, waiting for transfers between devices: 433 us -> 228 us
    all_gather x6 -> x1, blocking collectives: 203 us -> 43.1 us  [per_device(): lax.all_gather(own_gains.reshape(1, -1), ALL, axis=0, tiled=True)]
    all_gather x10 -> x6, waiting for transfers between devices: 82.5 us -> 188 us  [the longest x2 102 us: gather_qkv(): full = lax.all_gather(moved, REST, axis=0, tiled=True)]
    ppermute x4 -> x0, waiting for transfers between devices: 94.1 us -> none  [shifted(): return lax.ppermute(block, axis, route)]
    all_to_all x11 -> x4, blocking collectives: 111 us -> 49.7 us  [the longest x2 25.8 us: gather_qkv(): lax.all_to_all(sent, 'head', split_axis=0, concat_axis=0, tiled=True)]
    reduce_scatter x6 -> x4, waiting for transfers between devices: 121 us -> 64.5 us  [the longest x2 52.6 us: scatter_tokens(): lax.psum_scatter(by_owner(plan, rows.astype(BF16), width), 'head', scatte...]
    unnamed x6 -> x0, other arithmetic: 45.1 us -> none
    unnamed x1 -> x0, blocking collectives: 40.5 us -> none
  transfers between devices with their start and end apart: 32 -> 20, of which waited for: 24 -> 17; matrix products, arithmetic and copies ran while one was open for 14% -> 22% of each run, Pallas kernels for 0% -> 0%
where the time goes in v1:
time: 1050 us; the launch traced here: 1040 us
  waiting for transfers between devices  526 us (50%)
  matrix products  169 us (16%)
  blocking collectives  132 us (13%)
  local copies, waits for them, and re-layouts  93.5 us (9%)
  other arithmetic  72 us (7%)
  starting transfers between devices  32.7 us (3%)
  between operations  15.6 us (1%)
    unnamed x14, waiting for transfers between devices  228 us
    all_gather x2, waiting for transfers between devices, gather_qkv(): full = lax.all_gather(moved, REST, axis=0, tiled=True)  102 us
    all_gather x2, waiting for transfers between devices, per_device(): denses.append(lax.all_gather(own, ALL, axis=0, tiled=True))  68.1 us
    reduce_scatter x2, waiting for transfers between devices, scatter_tokens(): lax.psum_scatter(by_owner(plan, rows.astype(BF16), width), 'head', scatte...  52.6 us
    all_gather x1, blocking collectives, per_device(): lax.all_gather(own_gains.reshape(1, -1), ALL, axis=0, tiled=True)  43.1 us
    unnamed x130, local copies, waits for them, and re-layouts  39.8 us
    psum x1, blocking collectives, per_device(): total = lax.psum(small, ALL)  39.5 us
    dot_general x8, matrix products, dot(): return jnp.dot(left, right, preferred_element_type=F32)  32.3 us
  transfers between devices with their start and end apart: 20, of which 17 were waited for; matrix products, arithmetic and copies ran while one was open for 22% of the time, Pallas kernels for 0%

profile of v1, /device:TPU:0, one launch (start us, length us, event | category | flops | bytes accessed | tf_op | source)
XLA Modules:
  0.0 1040.9 jit_solution(1347383379103236286)
XLA Ops:
  12.2 43.1 %all-gather.1 = bf16[32,1,160]{2,1,0:T(2,128)(2,1)S(1)} all-gather(bf16[1,1,160]{2,1,0:T(2,128)(2,1)S(1)} %reshape.629), channel_id=1, replica_groups=mesh['batch'=4,'blk'=2,'head'=4] {'batch','blk','head'}, dimensions={0}, use_global_device_ids=true | all-gather | bytes 10560 | tf_op jit(solution)/shard_map/all_gather | solution.py:294
  58.8 13.4 %all_to_all.60 = bf16[4,40,960]{2,1,0:T(8,128)(2,1)} all-to-all(bf16[4,40,960]{2,1,0:T(8,128)(2,1)S(1)} %reshape.580), channel_id=1, replica_groups=mesh['batch'=4,'blk'=2,'head'=4] {'head'}, dimensions={0} | all-to-all | bytes 614400 | tf_op jit(solution)/shard_map/all_to_all | solution.py:123
  86.5 49.9 %all-gather.11.cloned.1.call-done = bf16[32,40,960]{2,1,0:T(8,128)(2,1)} async-done(((bf16[4,40,960]{2,1,0:T(8,128)(2,1)}), bf16[32,40,960]{2,1,0:T(8,128)(2,1)}) %all-gather.11.cloned.1.call-update) | async-done | bytes 2457616 | tf_op jit(solution)/shard_map/all_gather | solution.py:124
  149.6 9.4 fusion
  159.0 9.0 fusion.119
  180.0 8.0 all-to-all-done.2
  188.0 34.3 %all-gather.13.cloned.1.call-done = bf16[1280,3840]{1,0:T(8,128)(2,1)} async-done(((bf16[40,3840]{1,0:T(8,128)(2,1)}), bf16[1280,3840]{1,0:T(8,128)(2,1)}) %all-gather.13.cloned.1.call-update) | async-done | bytes 9830416 | tf_op jit(solution)/shard_map/all_gather | solution.py:310
  235.9 12.3 %all_to_all.61 = bf16[4,40,960]{2,1,0:T(8,128)(2,1)} all-to-all(bf16[4,40,960]{2,1,0:T(8,128)(2,1)S(1)} %reshape.589), channel_id=1, replica_groups=mesh['batch'=4,'blk'=2,'head'=4] {'head'}, dimensions={0} | all-to-all | bytes 614400 | tf_op jit(solution)/shard_map/all_to_all | solution.py:123
  249.0 12.1 %all-gather.19.cloned.1.call-done = bf16[1024,1280]{1,0:T(8,128)(2,1)} async-done(((bf16[256,1280]{1,0:T(8,128)(2,1)}), bf16[1024,1280]{1,0:T(8,128)(2,1)}) %all-gather.19.cloned.1.call-update) | async-done | bytes 2621456 | tf_op jit(solution)/shard_map/all_gather | solution.py:92
  264.6 51.8 %all-gather.15.cloned.1.call-done = bf16[32,40,960]{2,1,0:T(8,128)(2,1)} async-done(((bf16[4,40,960]{2,1,0:T(8,128)(2,1)}), bf16[32,40,960]{2,1,0:T(8,128)(2,1)}) %all-gather.15.cloned.1.call-update) | async-done | bytes 2457616 | tf_op jit(solution)/shard_map/all_gather | solution.py:124
  330.7 8.8 fusion.1
  339.5 9.0 fusion.120
  360.5 10.4 all-to-all-done.4
  375.4 33.8 %all-gather.17.cloned.1.call-done = bf16[1280,3840]{1,0:T(8,128)(2,1)} async-done(((bf16[40,3840]{1,0:T(8,128)(2,1)}), bf16[1280,3840]{1,0:T(8,128)(2,1)}) %all-gather.17.cloned.1.call-update) | async-done | bytes 9830416 | tf_op jit(solution)/shard_map/all_gather | solution.py:310
  438.6 10.2 all-to-all-done.7
  456.4 10.0 fusion.86
  466.4 12.2 %multiply_reduce_fusion.1 = (f32[4,1024]{1,0:T(4,128)S(1)}, f32[4,1024,1024]{1,2,0:T(8,128)}) fusion(f32[4,1024,1024]{1,2,0:T(8,128)} %get-tuple-element.82, f32[4,1024]{1,0:T(4,128)S(1)} %log_add_fusion.1, pred[1024,1024]{0,1:T(8,128)(4,1)S(1)} %fusion.13, bf16[1024,4,80]{0,2,1:T(8,128)(2,1)S(1)} %copy-done.26, bf16[1024,4,80]{0,2,1:T(8,128)(2,1)S(1)} %bitcast.271), kind=kOutput, calls=%fused_computation.4 | convolution fusion | flops 687861760 | bytes 35946496 | tf_op jit(solution)/shard_map/sqhd,skhd->shqk/dot_general | solution.py:201
  478.5 12.4 %multiply_convert_fusion.1 = bf16[4,1024,1024]{1,2,0:T(8,128)(2,1)S(1)} fusion(f32[4,1024,1024]{1,2,0:T(8,128)} %get-tuple-element.87, f32[4,1024,1024]{1,2,0:T(8,128)} %get-tuple-element.82, f32[4,1024]{1,0:T(4,128)S(1)} %get-tuple-element.86, f32[4,1024]{1,0:T(4,128)S(1)} %log_add_fusion.1, pred[1024,1024]{0,1:T(8,128)(4,1)S(1)} %fusion.13), kind=kLoop, calls=%fused_computation.3 | loop fusion | flops 20971520 | bytes 43024384 | tf_op jit(solution)/shard_map/convert_element_type | solution.py:203
  501.6 31.8 %reduce-scatter.11.cloned.1.call-done = bf16[1,256,1280]{2,1,0:T(8,128)(2,1)} async-done(((bf16[4,256,1280]{2,1,0:T(8,128)(2,1)}), bf16[1,256,1280]{2,1,0:T(8,128)(2,1)}) %reduce-scatter.11.cloned.1.call-update) | async-done | bytes 655376 | tf_op jit(solution)/shard_map/reduce_scatter | solution.py:98
  566.1 12.6 %multiply_reduce_fusion = (f32[4,1024]{1,0:T(4,128)S(1)}, f32[4,1024,1024]{1,2,0:T(8,128)}) fusion(f32[4,1024,1024]{1,2,0:T(8,128)} %get-tuple-element.74, f32[4,1024]{1,0:T(4,128)S(1)} %log_add_fusion, pred[1024,1024]{0,1:T(8,128)(4,1)S(1)} %fusion.13, bf16[1024,4,80]{0,2,1:T(8,128)(2,1)} %reshape.608, bf16[1024,4,80]{0,2,1:T(8,128)(2,1)} %bitcast.269), kind=kOutput, calls=%fused_computation.1 | convolution fusion | flops 687861760 | bytes 35946496 | tf_op jit(solution)/shard_map/sqhd,skhd->shqk/dot_general | solution.py:201
  578.7 12.9 %multiply_convert_fusion = bf16[4,1024,1024]{1,2,0:T(8,128)(2,1)S(1)} fusion(f32[4,1024,1024]{1,2,0:T(8,128)} %get-tuple-element.90, f32[4,1024,1024]{1,2,0:T(8,128)} %get-tuple-element.74, f32[4,1024]{1,0:T(4,128)S(1)} %get-tuple-element.89, f32[4,1024]{1,0:T(4,128)S(1)} %log_add_fusion, pred[1024,1024]{0,1:T(8,128)(4,1)S(1)} %fusion.13), kind=kLoop, calls=%fused_computation | loop fusion | flops 20971520 | bytes 43024384 | tf_op jit(solution)/shard_map/convert_element_type | solution.py:203
  596.0 8.2 fusion.89
  629.2 13.8 %copy.122 = bf16[1280,3840]{1,0:T(8,128)(2,1)} copy(bf16[1280,3840]{0,1:T(8,128)(2,1)} %pad_maximum_fusion.1) | data formatting | bytes 19660800
  652.8 13.8 %copy.120 = bf16[1280,3840]{1,0:T(8,128)(2,1)} copy(bf16[1280,3840]{0,1:T(8,128)(2,1)} %pad_maximum_fusion) | data formatting | bytes 19660800
  670.7 13.8 %all_to_all.62 = bf16[2,128,1280]{2,1,0:T(8,128)(2,1)S(1)} all-to-all(bf16[2,128,1280]{2,1,0:T(8,128)(2,1)S(1)} %bitcast.280), channel_id=1, replica_groups=mesh['batch'=4,'blk'=2,'head'=4] {'blk'}, dimensions={0} | all-to-all | bytes 1310720 | tf_op jit(solution)/shard_map/all_to_all | solution.py:77
  684.5 10.2 all_to_all.63
  694.6 11.9 %reduce-scatter.15.cloned.1.call-done = bf16[160,960]{1,0:T(8,128)(2,1)} async-done(((bf16[1280,960]{1,0:T(8,128)(2,1)}), bf16[160,960]{1,0:T(8,128)(2,1)}) %reduce-scatter.15.cloned.1.call-update) | async-done | bytes 307216 | tf_op jit(solution)/shard_map/reduce_scatter | solution.py:131
  721.7 20.8 %reduce-scatter.13.cloned.1.call-done = bf16[1,256,1280]{2,1,0:T(8,128)(2,1)} async-done(((bf16[4,256,1280]{2,1,0:T(8,128)(2,1)}), bf16[1,256,1280]{2,1,0:T(8,128)(2,1)}) %reduce-scatter.13.cloned.1.call-update) | async-done | bytes 655376 | tf_op jit(solution)/shard_map/reduce_scatter | solution.py:98
  744.2 39.5 %psum.7 = f32[5280]{0:T(1024)S(1)} all-reduce(f32[5280]{0:T(1024)S(1)} %concatenate.33), channel_id=1, replica_groups=mesh['batch'=4,'blk'=2,'head'=4] {'batch','blk','head'}, use_global_device_ids=true, to_apply=%region_26.27 | all-reduce | flops 5280 | bytes 42240 | tf_op jit(solution)/shard_map/psum | solution.py:332
  791.0 8.2 all-to-all-done.9
  800.4 85.8 %reduce-scatter.21.cloned.1.call-done = bf16[40,3840]{1,0:T(8,128)(2,1)} async-done(((bf16[1280,3840]{1,0:T(8,128)(2,1)}), bf16[40,3840]{1,0:T(8,128)(2,1)}) %reduce-scatter.21.cloned.1.call-update) | async-done | bytes 307216
  888.0 142.0 %reduce-scatter.19.cloned.1.call-done = bf16[40,3840]{1,0:T(8,128)(2,1)} async-done(((bf16[1280,3840]{1,0:T(8,128)(2,1)}), bf16[40,3840]{1,0:T(8,128)(2,1)}) %reduce-scatter.19.cloned.1.call-update) | async-done | bytes 307216
  (283 shorter events, 250.0 us)
Async XLA Ops:
  7.2 67.9 %copy-start = (s32[2,1024]{1,0:T(2,128)S(1)}, s32[2,1024]{1,0:T(2,128)}, u32[]{:S(2)}) copy-start(s32[2,1024]{1,0:T(2,128)} %param.11) | copy-start | bytes 24580
  7.2 49.1 %all-to-all-start = ((bf16[2,128,1280]{2,1,0:T(8,128)(2,1)}), bf16[2,128,1280]{2,1,0:T(8,128)(2,1)S(1)}, u32[]{:S(2)}, u32[]{:S(2)}) async-start(bf16[2,128,1280]{2,1,0:T(8,128)(2,1)} %param.10), calls=%async_computation | async-start | bytes 1310720 | tf_op jit(solution)/shard_map/all_to_all | solution.py:70
  11.4 71.6 %all-gather.9.cloned.1.call-start = ((), (), s32[]{:S(2)}) async-start(), calls=%async_computation.18 | async-start | bytes 3276800 | tf_op jit(solution)/shard_map/all_gather | solution.py:92
  57.7 78.7 %all-gather.11.cloned.1.call-start = ((), (), s32[]{:S(2)}) async-start(), calls=%async_computation.19 | async-start | bytes 2949120 | tf_op jit(solution)/shard_map/all_gather | solution.py:124
  57.8 17.2 %copy-start.52 = (f32[2,80]{1,0:T(2,128)S(1)}, f32[2,80]{1,0:T(2,128)}, u32[]{:S(2)}) copy-start(f32[2,80]{1,0:T(2,128)} %param.18) | copy-start | bytes 1924
  72.3 150.0 %all-gather.13.cloned.1.call-start = ((), (), s32[]{:S(2)}) async-start(), calls=%async_computation.20 | async-start | bytes 10137600 | tf_op jit(solution)/shard_map/all_gather | solution.py:310
  75.6 66.4 %copy-start.48 = (f32[80]{0:T(128)}, f32[80]{0:T(128)S(1)}, u32[]{:S(2)}) copy-start(f32[80]{0:T(128)S(1)} %get-tuple-element.70) | copy-start | bytes 964
  174.3 13.7 %all-to-all-start.2 = ((bf16[4,256,320]{1,2,0:T(8,128)(2,1)}), bf16[4,256,320]{1,2,0:T(8,128)(2,1)S(1)}, u32[]{:S(2)}, u32[]{:S(2)}) async-start(bf16[4,256,320]{1,2,0:T(8,128)(2,1)} %reshape.585), calls=%async_computation.2 | async-start | bytes 1310720 | tf_op jit(solution)/shard_map/all_to_all | solution.py:105
  177.8 83.4 %all-gather.19.cloned.1.call-start = ((), (), s32[]{:S(2)}) async-start(), calls=%async_computation.27 | async-start | bytes 3276800 | tf_op jit(solution)/shard_map/all_gather | solution.py:92
  188.0 37.4 %copy-start.20 = (bf16[4,256,320]{1,2,0:T(8,128)(2,1)}, bf16[4,256,320]{1,2,0:T(8,128)(2,1)S(1)}, u32[]{:S(2)}) copy-start(bf16[4,256,320]{1,2,0:T(8,128)(2,1)S(1)} %all-to-all-done.2) | copy-start | bytes 1966084
  234.9 81.5 %all-gather.15.cloned.1.call-start = ((), (), s32[]{:S(2)}) async-start(), calls=%async_computation.21 | async-start | bytes 2949120 | tf_op jit(solution)/shard_map/all_gather | solution.py:124
  248.2 160.9 %all-gather.17.cloned.1.call-start = ((), (), s32[]{:S(2)}) async-start(), calls=%async_computation.22 | async-start | bytes 10137600 | tf_op jit(solution)/shard_map/all_gather | solution.py:310
  356.3 14.6 %all-to-all-start.4 = ((bf16[4,256,320]{1,2,0:T(8,128)(2,1)}), bf16[4,256,320]{1,2,0:T(8,128)(2,1)}, u32[]{:S(2)}, u32[]{:S(2)}) async-start(bf16[4,256,320]{1,2,0:T(8,128)(2,1)} %reshape.594), calls=%async_computation.4 | async-start | bytes 1310720 | tf_op jit(solution)/shard_map/all_to_all | solution.py:105
  370.9 47.1 %all-to-all-start.6 = ((bf16[2,128,1280]{2,1,0:T(8,128)(2,1)}), bf16[2,128,1280]{2,1,0:T(8,128)(2,1)}, u32[]{:S(2)}, u32[]{:S(2)}) async-start(bf16[2,128,1280]{2,1,0:T(8,128)(2,1)} %param.19), calls=%async_computation.6 | async-start | bytes 1310720 | tf_op jit(solution)/shard_map/all_to_all | solution.py:70
  434.3 14.5 %all-to-all-start.7 = ((bf16[4,256,320]{1,2,0:T(8,128)(2,1)}), bf16[4,256,320]{1,2,0:T(8,128)(2,1)}, u32[]{:S(2)}, u32[]{:S(2)}) async-start(bf16[4,256,320]{1,2,0:T(8,128)(2,1)} %bitcast.262), calls=%async_computation.7 | async-start | bytes 1310720 | tf_op jit(solution)/shard_map/all_to_all | solution.py:114
  438.5 94.8 %reduce-scatter.11.cloned.1.call-start = ((), (), s32[]{:S(2)}) async-start(), calls=%async_computation.23 | async-start | bytes 3276800 | tf_op jit(solution)/shard_map/reduce_scatter | solution.py:98
  466.4 29.5 %copy-start.56 = (bf16[4,80,1024]{2,1,0:T(8,128)(2,1)}, bf16[4,80,1024]{2,1,0:T(8,128)(2,1)S(1)}, u32[]{:S(2)}) copy-start(bf16[4,80,1024]{2,1,0:T(8,128)(2,1)S(1)} %fusion.86) | copy-start | bytes 1966084
  500.8 32.5 %copy-start.7 = (f32[256,1280]{1,0:T(8,128)S(1)}, f32[256,1280]{1,0:T(8,128)}, u32[]{:S(2)}) copy-start(f32[256,1280]{1,0:T(8,128)} %copy-done.6) | copy-start | bytes 3932164
  548.1 13.7 %all-to-all-start.8 = ((bf16[4,256,320]{1,2,0:T(8,128)(2,1)}), bf16[4,256,320]{1,2,0:T(8,128)(2,1)S(1)}, u32[]{:S(2)}, u32[]{:S(2)}) async-start(bf16[4,256,320]{1,2,0:T(8,128)(2,1)} %bitcast.261), calls=%async_computation.9 | async-start | bytes 1310720 | tf_op jit(solution)/shard_map/all_to_all | solution.py:114
  551.6 132.8 %reduce-scatter.17.cloned.1.call-start = ((), (), s32[]{:S(2)}) async-start(), calls=%async_computation.26 | async-start | bytes 2949120 | tf_op jit(solution)/shard_map/reduce_scatter | solution.py:131
  558.4 148.1 %reduce-scatter.15.cloned.1.call-start = ((), (), s32[]{:S(2)}) async-start(), calls=%async_computation.25 | async-start | bytes 2949120 | tf_op jit(solution)/shard_map/reduce_scatter | solution.py:131
  610.7 131.9 %reduce-scatter.13.cloned.1.call-start = ((), (), s32[]{:S(2)}) async-start(), calls=%async_computation.24 | async-start | bytes 3276800 | tf_op jit(solution)/shard_map/reduce_scatter | solution.py:98
  618.4 267.7 %reduce-scatter.21.cloned.1.call-start = ((), (), s32[]{:S(2)}) async-start(), calls=%async_computation.29 | async-start | bytes 10137600
  643.0 387.0 %reduce-scatter.19.cloned.1.call-start = ((), (), s32[]{:S(2)}) async-start(), calls=%async_computation.28 | async-start | bytes 10137600
  706.5 11.1 %all-to-all-start.10 = ((bf16[4,40,960]{2,1,0:T(8,128)(2,1)}), bf16[4,40,960]{2,1,0:T(8,128)(2,1)}, u32[]{:S(2)}, u32[]{:S(2)}) async-start(bf16[4,40,960]{2,1,0:T(8,128)(2,1)} %bitcast.285), calls=%async_computation.13 | async-start | bytes 655360 | tf_op jit(solution)/shard_map/all_to_all | solution.py:133
  711.3 31.3 %copy-start.5 = (bf16[2,128,1280]{2,1,0:T(8,128)(2,1)S(1)}, bf16[2,128,1280]{2,1,0:T(8,128)(2,1)}, u32[]{:S(2)}) copy-start(bf16[2,128,1280]{2,1,0:T(8,128)(2,1)} %copy-done.4) | copy-start | bytes 1966084
  711.3 31.3 %copy-start.39 = (f32[1280]{0:T(1024)S(1)}, f32[1280]{0:T(1024)}, u32[]{:S(2)}) copy-start(f32[1280]{0:T(1024)} %copy-done.38) | copy-start | bytes 15364
  711.3 31.3 %copy-start.45 = (f32[256]{0:T(256)S(1)}, f32[256]{0:T(256)}, u32[]{:S(2)}) copy-start(f32[256]{0:T(256)} %copy-done.44) | copy-start | bytes 3076
  712.4 31.7 %copy-start.51 = (f32[1280]{0:T(1024)S(1)}, f32[1280]{0:T(1024)}, u32[]{:S(2)}) copy-start(f32[1280]{0:T(1024)} %get-tuple-element.36) | copy-start | bytes 15364
  712.4 31.8 %copy-start.54 = (f32[80]{0:T(128)S(1)}, f32[80]{0:T(128)}, u32[]{:S(2)}) copy-start(f32[80]{0:T(128)} %get-tuple-element.55) | copy-start | bytes 964
  744.1 45.7 %copy-start.53 = (f32[2,80]{1,0:T(2,128)S(1)}, f32[2,80]{1,0:T(2,128)}, u32[]{:S(2)}) copy-start(f32[2,80]{1,0:T(2,128)} %param.18) | copy-start | bytes 1924
  786.2 13.0 %all-to-all-start.9 = ((bf16[2,128,1280]{2,1,0:T(8,128)(2,1)}), bf16[2,128,1280]{2,1,0:T(8,128)(2,1)S(1)}, u32[]{:S(2)}, u32[]{:S(2)}) async-start(bf16[2,128,1280]{2,1,0:T(8,128)(2,1)} %bitcast.267), calls=%async_computation.11 | async-start | bytes 1310720 | tf_op jit(solution)/shard_map/all_to_all | solution.py:77
  (50 other events, 223.8 us)
Sparse Core Ops, SparseCore 0:
  57.8 25.1 all-gather.8
  85.2 51.1 all-gather.10
  139.9 82.3 all-gather.12
  235.0 26.1 all-gather.18
  263.2 53.1 all-gather.14
  319.7 89.3 all-gather.16
  501.0 32.3 reduce-scatter.10
  558.5 71.8 reduce-scatter.16
  634.3 72.0 reduce-scatter.14
  709.0 33.5 reduce-scatter.12
  748.6 137.5 reduce-scatter.20
  893.0 136.9 reduce-scatter.18

commit v2 on v1

--- a/solution.py
+++ b/solution.py
@@ -34,6 +34,20 @@
     return lax.dot_general(left, right, (((1,), (1,)), ((), ())), preferred_element_type=F32)
 
 
+def swapped(array, axis, mask):
+    size = lax.axis_size(axis)
+    return lax.ppermute(array, axis, [(i, i ^ mask) for i in range(size)])
+
+
+def pick(array, index, axis=0):
+    return lax.dynamic_index_in_dim(array, index, axis, keepdims=False)
+
+
+def small_slice():
+    sizes = tuple(lax.axis_size(axis) for axis in ALL)
+    return sizes == (4, 2, 4)
+
+
 def normalize(stream, gain):
     factor = lax.rsqrt(jnp.mean(stream * stream, axis=-1, keepdims=True) + EPSILON)
     return stream * factor * gain, factor
@@ -41,11 +55,13 @@
 
 def norm_back(upper, stream, factor, gain):
     inner = upper * gain
-    gain_grad = jnp.sum(upper * stream * factor, axis=0)
-    lower = factor * inner - stream * factor * factor * factor * jnp.mean(
+    return factor * inner - stream * factor * factor * factor * jnp.mean(
         inner * stream, axis=-1, keepdims=True
     )
-    return lower, gain_grad
+
+
+def gain_grad(weight, weight_grad, gain):
+    return jnp.sum(weight.astype(F32) * weight_grad, axis=-1) / gain.astype(F32)
 
 
 class Plan:
@@ -65,17 +81,26 @@
         self.tokens = self.seqs * self.rows
 
 
+def swap_blocks(plan, array):
+    if not plan.whole or plan.blks == 1:
+        return array
+    if plan.blks > 2:
+        return lax.all_to_all(array, "blk", split_axis=0, concat_axis=0, tiled=True)
+    halves = array.reshape(2, plan.own_seqs, plan.rows, plan.width)
+    me = lax.axis_index("blk")
+    got = swapped(pick(halves, 1 - me), "blk", 1)
+    kept = pick(halves, me)
+    mine = me == 0
+    swapped_halves = jnp.stack([jnp.where(mine, kept, got), jnp.where(mine, got, kept)])
+    return swapped_halves.reshape(array.shape)
+
+
 def to_plan(plan, array):
-    if plan.whole and plan.blks > 1:
-        array = lax.all_to_all(array, "blk", split_axis=0, concat_axis=0, tiled=True)
-    return array.reshape(plan.tokens, plan.width)
+    return swap_blocks(plan, array).reshape(plan.tokens, plan.width)
 
 
 def from_plan(plan, flat):
-    array = flat.reshape(plan.seqs, plan.rows, plan.width)
-    if plan.whole and plan.blks > 1:
-        array = lax.all_to_all(array, "blk", split_axis=0, concat_axis=0, tiled=True)
-    return array
+    return swap_blocks(plan, flat.reshape(plan.seqs, plan.rows, plan.width))
 
 
 def in_sequence(plan, by_head, width):
@@ -89,15 +114,32 @@
 
 
 def gather_tokens(plan, rows):
-    moved = lax.all_gather(rows, "head", axis=0, tiled=False)
-    return in_sequence(plan, moved, rows.shape[-1])
+    width = rows.shape[-1]
+    if not small_slice():
+        moved = lax.all_gather(rows, "head", axis=0, tiled=False)
+        return in_sequence(plan, moved, width)
+    far = swapped(rows, "head", 2)
+    near = swapped(rows, "head", 1)
+    both = swapped(far, "head", 1)
+    pieces = jnp.stack([rows, near, far, both])
+    me = lax.axis_index("head")
+    return in_sequence(plan, jnp.stack([pick(pieces, me ^ i) for i in range(4)]), width)
 
 
 def scatter_tokens(plan, rows):
     width = rows.shape[-1]
-    return lax.psum_scatter(
-        by_owner(plan, rows.astype(BF16), width), "head", scatter_dimension=0, tiled=False
+    parts = by_owner(plan, rows, width)
+    if not small_slice():
+        return lax.psum_scatter(
+            parts.astype(BF16), "head", scatter_dimension=0, tiled=False
+        ).astype(F32)
+    me = lax.axis_index("head")
+    parts = parts.reshape(2, 2, plan.tokens, width)
+    row, core = me // 2, me % 2
+    halves = pick(parts, core, 1) + swapped(
+        pick(parts, 1 - core, 1).astype(BF16), "head", 1
     ).astype(F32)
+    return pick(halves, row) + swapped(pick(halves, 1 - row).astype(BF16), "head", 2).astype(F32)
 
 
 def heads_to_tokens(plan, rows):
@@ -115,20 +157,62 @@
     return in_sequence(plan, moved, part)
 
 
-def gather_qkv(rows):
-    own, width = rows.shape
+def gather_over(piece, axis):
+    size = lax.axis_size(axis)
+    pieces = jnp.stack([piece] + [swapped(piece, axis, mask) for mask in range(1, size)])
+    me = lax.axis_index(axis)
+    return jnp.stack([pick(pieces, me ^ i) for i in range(size)])
+
+
+def gather_qkv(rows, extra):
+    layers, own, width = rows.shape
     heads = lax.axis_size("head")
     part = width // 3 // heads
-    sent = rows.reshape(own, 3, heads, part).transpose(2, 0, 1, 3).reshape(heads, own, 3 * part)
+    sent = rows.reshape(layers, own, 3, heads, part).transpose(3, 0, 1, 2, 4)
+    sent = sent.reshape(heads, layers, own, 3 * part)
     moved = lax.all_to_all(sent, "head", split_axis=0, concat_axis=0, tiled=True)
-    full = lax.all_gather(moved, REST, axis=0, tiled=True)
-    return full.reshape(-1, 3 * part)
+    full = []
+    if not small_slice():
+        for layer in range(layers):
+            full.append(lax.all_gather(moved[:, layer], REST, axis=0, tiled=True))
+            full[layer] = full[layer].reshape(-1, 3 * part)
+        return full, lax.all_gather(extra, ALL, axis=0, tiled=True)
+    with_extra = jnp.broadcast_to(extra[None], (heads, own, extra.shape[1]))
+    extra_moved = lax.all_to_all(with_extra, "head", split_axis=0, concat_axis=0, tiled=True)
+    extra_full = None
+    for layer in range(layers):
+        piece = moved[:, layer]
+        if layer == 0:
+            piece = jnp.concatenate([piece, extra_moved], axis=2)
+        along = gather_over(piece, "batch")
+        other = swapped(along, "blk", 1)
+        mine = lax.axis_index("blk") == 0
+        both = jnp.stack(
+            [jnp.where(mine, along, other), jnp.where(mine, other, along)], axis=1
+        ).reshape(-1, piece.shape[-1])
+        full.append(both[:, : 3 * part])
+        if layer == 0:
+            extra_full = both[:, 3 * part :]
+    return full, extra_full
+
+
+def scatter_over(parts, axis):
+    size = lax.axis_size(axis)
+    me = lax.axis_index(axis)
+    total = pick(parts, me).astype(F32)
+    for mask in range(1, size):
+        total = total + swapped(pick(parts, me ^ mask).astype(BF16), axis, mask).astype(F32)
+    return total
 
 
 def scatter_qkv(grad):
     heads = lax.axis_size("head")
     part = grad.shape[1] // 3
-    summed = lax.psum_scatter(grad.astype(BF16), REST, scatter_dimension=0, tiled=True)
+    if small_slice():
+        parts = grad.reshape(4, 2, -1, 3 * part).transpose(1, 0, 2, 3)
+        summed = scatter_over(scatter_over(parts, "blk"), "batch").astype(BF16)
+    else:
+        summed = lax.psum_scatter(grad.astype(BF16), REST, scatter_dimension=0, tiled=True)
     own = summed.shape[0] // heads
     moved = lax.all_to_all(
         summed.reshape(heads, own, 3 * part), "head", split_axis=0, concat_axis=0, tiled=True
@@ -139,6 +223,42 @@
         .reshape(own, 3 * heads * part)
         .astype(F32)
     )
+
+
+def scatter_dense(grad, spread):
+    if not (spread and small_slice()):
+        return lax.psum_scatter(grad.astype(BF16), ALL, scatter_dimension=0, tiled=True).astype(F32)
+    columns = grad.shape[1]
+    core = lax.axis_index("head") % 2
+    row = lax.axis_index("head") // 2
+    parts = grad.reshape(4, 2, 2, 2, -1, columns)
+    cored = (
+        pick(parts, core, 3).astype(F32)
+        + swapped(pick(parts, 1 - core, 3).astype(BF16), "head", 1).astype(F32)
+    ).astype(BF16)
+    half = columns // 2
+    first, second = cored[..., :half], cored[..., half:]
+    blk = lax.axis_index("blk")
+
+    def over_blk(part, dim):
+        got = swapped(pick(part, 1 - blk, dim).astype(BF16), "blk", 1).astype(F32)
+        return pick(part, blk, dim).astype(F32) + got
+
+    def over_row(part, dim):
+        got = swapped(pick(part, 1 - row, dim).astype(BF16), "head", 2).astype(F32)
+        return pick(part, row, dim).astype(F32) + got
+
+    first = over_row(over_blk(first, 1), 1)
+    second = over_blk(over_row(second, 2), 1)
+    return scatter_over(jnp.concatenate([first, second], axis=-1), "batch")
+
+
+def sum_all(array):
+    if not small_slice():
+        return lax.psum(array, ALL)
+    for axis, mask in (("head", 1), ("head", 2), ("blk", 1), ("batch", 1), ("batch", 2)):
+        array = array + swapped(array, axis, mask)
+    return array
 
 
 def window_mask(plan, segments, block_index):
@@ -235,7 +355,7 @@
     return result, kept
 
 
-def backward(plan, upper, kept, qkv, dense, gains, scale_vec, allowed):
+def backward(plan, upper, kept, qkv, dense, gains, scale_vec, allowed, spread):
     (
         stream, factor_one, normed_all, query_pre, queries, keys, values, log_total,
         attended, middle, factor_two, normed_two, hidden, active,
@@ -250,12 +370,12 @@
     gate = jax.nn.sigmoid(hidden)
     hidden_low = (active_grad * gate * (1.0 + hidden * (1.0 - gate))).astype(BF16)
     up_grad = dot_rows(normed_two, hidden_low)
-    extra_two, mlp_gain_grad = norm_back(dot_cols(hidden_low, up_w), middle, factor_two, gains[1])
+    extra_two = norm_back(dot_cols(hidden_low, up_w), middle, factor_two, gains[1])
     middle_grad = upper + extra_two
     middle_low = middle_grad.astype(BF16)
     out_grad = dot_rows(attended, middle_low)
     dense_grad = jnp.concatenate([out_grad, up_grad, down_grad], axis=1).astype(BF16)
-    dense_own = lax.psum_scatter(dense_grad, ALL, scatter_dimension=0, tiled=True)
+    dense_own = scatter_dense(dense_grad, spread)
     attended_grad = tokens_to_heads(plan, dot_cols(middle_low, out_w).astype(BF16))
     queries_grad, keys_grad, values_grad = attend_back(
         queries, keys, values, allowed, log_total, attended_grad.reshape(queries.shape)
@@ -268,9 +388,8 @@
     projected_low = jnp.concatenate([query_low, keys_low, values_low], axis=1)
     normed_grad = scatter_tokens(plan, dot_cols(projected_low, qkv))
     qkv_own = scatter_qkv(dot_rows(normed_all, projected_low))
-    extra_one, attn_gain_grad = norm_back(normed_grad, stream, factor_one, gains[0])
-    lower = middle_grad + extra_one
-    return lower, qkv_own, dense_own, (attn_gain_grad, mlp_gain_grad), scale_vec_grad
+    lower = middle_grad + norm_back(normed_grad, stream, factor_one, gains[0])
+    return lower, qkv_own, dense_own, scale_vec_grad
 
 
 def per_device(
@@ -290,22 +409,16 @@
     block_index = lax.axis_index("blk")
     scale_vecs = SCALE_BASE / math.sqrt(head_dim) * jax.nn.softplus(scale_param)
     own_gains = jnp.concatenate([attn_gain, mlp_gain], axis=0)
-    gains = (
-        lax.all_gather(own_gains.reshape(1, -1), ALL, axis=0, tiled=True)
-        .reshape(-1, 2 * layers, attn_gain.shape[1])
-        .transpose(1, 0, 2)
-        .reshape(2 * layers, plan.width)
-        .astype(F32)
-    )
+    qkvs, gains = gather_qkv(qkv_weight, own_gains.T)
+    gains = gains.T.astype(F32)
     if plan.whole:
         segments = lax.dynamic_slice_in_dim(
             segments, block_index * plan.own_seqs, plan.own_seqs, 0
         )
     allowed = window_mask(plan, segments, block_index)
     stream = to_plan(plan, tokens).astype(F32)
-    qkvs, denses, kept = [], [], []
+    denses, kept = [], []
     for layer in range(layers):
-        qkvs.append(gather_qkv(qkv_weight[layer]))
         own = jnp.concatenate([out_weight[layer], up_weight[layer], down_weight[layer]], axis=1)
         denses.append(lax.all_gather(own, ALL, axis=0, tiled=True))
         layer_gains = (gains[layer], gains[layers + layer])
@@ -316,37 +429,29 @@
     layer_out = from_plan(plan, stream.astype(BF16))
     upper = to_plan(plan, cotangent).astype(F32)
     qkv_grads, dense_grads = [None] * layers, [None] * layers
-    gain_grads, scale_grads = [None] * layers, [None] * layers
+    scale_grads = [None] * layers
     for layer in reversed(range(layers)):
         layer_gains = (gains[layer], gains[layers + layer])
-        upper, qkv_grads[layer], dense_grads[layer], gain_grads[layer], scale_grads[layer] = (
-            backward(
-                plan, upper, kept[layer], qkvs[layer], denses[layer], layer_gains,
-                scale_vecs[layer], allowed,
-            )
+        upper, qkv_grads[layer], dense_grads[layer], scale_grads[layer] = backward(
+            plan, upper, kept[layer], qkvs[layer], denses[layer], layer_gains,
+            scale_vecs[layer], allowed, layer == 0,
         )
     input_grad = from_plan(plan, upper.astype(BF16)).astype(F32)
-    small = jnp.concatenate(
-        [g[0] for g in gain_grads] + [g[1] for g in gain_grads] + scale_grads, axis=0
-    )
-    total = lax.psum(small, ALL)
-    gain_total = total[: 2 * layers * plan.width].reshape(2 * layers, plan.width)
-    owner = lax.axis_index(ALL)
-    gain_rows = attn_gain.shape[1]
-    own_total = lax.dynamic_slice_in_dim(gain_total, owner * gain_rows, gain_rows, 1)
-    scale_total = total[2 * layers * plan.width :].reshape(layers, head_dim)
+    scale_total = sum_all(jnp.stack(scale_grads))
     scale_grad = scale_total * (SCALE_BASE / math.sqrt(head_dim)) * jax.nn.sigmoid(scale_param)
-    dense_all = jnp.stack(dense_grads).astype(F32)
+    dense_all = jnp.stack(dense_grads)
+    qkv_all = jnp.stack(qkv_grads)
     width = plan.width
+    up_all = dense_all[:, :, width:-width]
     return (
         layer_out,
         input_grad,
-        jnp.stack(qkv_grads),
+        qkv_all,
         dense_all[:, :, :width],
-        dense_all[:, :, width:-width],
+        up_all,
         dense_all[:, :, -width:],
-        own_total[:layers],
-        own_total[layers:],
+        gain_grad(qkv_weight, qkv_all, attn_gain),
+        gain_grad(up_weight, up_all, mlp_gain),
         scale_grad,
     )
 

time: 1050 us -> 746 us (0.71)
  waiting for transfers between devices: 526 us -> 293 us
  blocking collectives: 132 us -> 0 us
  starting transfers between devices: 32.7 us -> 76.8 us
  other arithmetic: 72 us -> 101 us
  matrix products: 169 us -> 153 us
    ppermute x0 -> x43, waiting for transfers between devices: none -> 255 us  [swapped(): return lax.ppermute(array, axis, [(i, i ^ mask) for i in range(size)])]
    unnamed x14 -> x3, waiting for transfers between devices: 228 us -> 0.05 us
    all_gather x4 -> x0, waiting for transfers between devices: 119 us -> none  [the longest x2 102 us: gather_qkv(): full = lax.all_gather(moved, REST, axis=0, tiled=True)]
    all_gather x2, waiting for transfers between devices: 68.1 us -> 0.02 us  [per_device(): denses.append(lax.all_gather(own, ALL, axis=0, tiled=True))]
    reduce_scatter x4 -> x1, waiting for transfers between devices: 64.5 us -> 0.02 us  [scatter_dense(): lax.psum_scatter(grad.astype(BF16), ALL, scatter_dimension=0, tiled=True)]
    all_to_all x4 -> x0, blocking collectives: 49.7 us -> none  [the longest x2 25.8 us: gather_qkv(): lax.all_to_all(sent, 'head', split_axis=0, concat_axis=0, tiled=True)]
    ppermute x0 -> x43, starting transfers between devices: none -> 45.4 us  [swapped(): return lax.ppermute(array, axis, [(i, i ^ mask) for i in range(size)])]
    all_gather x1 -> x0, blocking collectives: 43.1 us -> none  [per_device(): lax.all_gather(own_gains.reshape(1, -1), ALL, axis=0, tiled=True)]
  transfers between devices with their start and end apart: 20 -> 54, of which waited for: 17 -> 28; matrix products, arithmetic and copies ran while one was open for 22% -> 33% of each run, Pallas kernels for 0% -> 0%
where the time goes in v2:
time: 746 us; the launch traced here: 738 us
  waiting for transfers between devices  293 us (39%)
  matrix products  153 us (21%)
  other arithmetic  101 us (14%)
  local copies, waits for them, and re-layouts  98.7 us (13%)
  starting transfers between devices  76.8 us (10%)
  between operations  16.1 us (2%)
    ppermute x43, waiting for transfers between devices, swapped(): return lax.ppermute(array, axis, [(i, i ^ mask) for i in range(size)])  255 us
    ppermute x43, starting transfers between devices, swapped(): return lax.ppermute(array, axis, [(i, i ^ mask) for i in range(size)])  45.4 us
    dot_general x8, matrix products, dot(): return jnp.dot(left, right, preferred_element_type=F32)  27.9 us
    convert_element_type x2, other arithmetic, attend_back(): scores_low = (probs * (probs_grad - row_dot)).astype(BF16)  25.4 us
    dot_general x2, matrix products, attend_back(): jnp.einsum('sqhd,skhd->shqk', attended_grad, values, preferred_element_ty...  24.1 us
    dot_general x8, matrix products, dot_rows(): lax.dot_general(left, right, (((0,), (0,)), ((), ())), preferred_element_...  21.3 us
    dot_general x2, matrix products, attend_back(): jnp.einsum('shqk,sqhd->skhd', probs_low, attended_grad, preferred_element...  19.1 us
    dot_general x2, matrix products, attend(): jnp.einsum('shqk,skhd->sqhd', probs_low, values, preferred_element_type=F32)  18.2 us
  transfers between devices with their start and end apart: 54, of which 28 were waited for; matrix products, arithmetic and copies ran while one was open for 33% of the time, Pallas kernels for 0%

profile of v2, /device:TPU:0, one launch (start us, length us, event | category | flops | bytes accessed | tf_op | source)
XLA Modules:
  0.0 738.4 jit_solution(16554817696144057770)
XLA Ops:
  23.1 11.2 %all-to-all-done = bf16[4,2,40,960]{3,2,1,0:T(8,128)(2,1)S(1)} async-done(((bf16[4,2,40,960]{3,2,1,0:T(8,128)(2,1)}), bf16[4,2,40,960]{3,2,1,0:T(8,128)(2,1)S(1)}, u32[]{:S(2)}, u32[]{:S(2)}) %all-to-all-start) | async-done | bytes 614432 | tf_op jit(solution)/shard_map/all_to_all | solution.py:173
  42.0 26.5 %collective-permute-done.2 = bf16[4,40,964]{2,1,0:T(8,128)(2,1)S(1)} collective-permute-done((bf16[4,40,964]{2,1,0:T(8,128)(2,1)S(1)}, bf16[4,40,964]{2,1,0:T(8,128)(2,1)S(1)}, u32[]{:S(2)}, u32[]{:S(2)}) %collective-permute-start.2) | collective-permute-done | bytes 308512 | tf_op jit(solution)/shard_map/ppermute | solution.py:39
  68.5 5.5 collective-permute-done.3
  78.3 43.8 %collective-permute-done.4 = bf16[4,4,40,964]{3,2,1,0:T(8,128)(2,1)} collective-permute-done((bf16[4,4,40,964]{3,2,1,0:T(8,128)(2,1)S(1)}, bf16[4,4,40,964]{3,2,1,0:T(8,128)(2,1)}, u32[]{:S(2)}, u32[]{:S(2)}) %collective-permute-start.4) | collective-permute-done | bytes 1233952 | tf_op jit(solution)/shard_map/ppermute | solution.py:39
  129.7 12.3 %collective-permute-done.6 = bf16[256,1280]{1,0:T(8,128)(2,1)} collective-permute-done((bf16[256,1280]{1,0:T(8,128)(2,1)}, bf16[256,1280]{1,0:T(8,128)(2,1)}, u32[]{:S(2)}, u32[]{:S(2)}) %collective-permute-start.6) | collective-permute-done | bytes 655392 | tf_op jit(solution)/shard_map/ppermute | solution.py:39
  144.4 9.3 %collective-permute-start.12 = (bf16[4,40,960]{2,1,0:T(8,128)(2,1)}, bf16[4,40,960]{2,1,0:T(8,128)(2,1)}, u32[]{:S(2)}, u32[]{:S(2)}) collective-permute-start(bf16[4,40,960]{2,1,0:T(8,128)(2,1)} %get-tuple-element.71), channel_id=1, source_target_pairs={{0,16},{8,24},{16,0},{24,8},{1,17},{9,25},{17,1},{25,9},{2,18},{10... | collective-permute-start | bytes 921608 | tf_op jit(solution)/shard_map/ppermute | solution.py:39
  161.9 7.3 select_reduce_fusion.1
  169.2 9.1 %fusion = f32[4,1024]{1,0:T(4,128)S(1)} fusion(f32[4,1024,1024]{1,2,0:T(8,128)} %get-tuple-element.84, f32[4,1024]{1,0:T(4,128)S(1)} %get-tuple-element.83, pred[1024,1024]{0,1:T(8,128)(4,1)S(1)} %fusion.14), kind=kLoop, calls=%fused_computation.10 | loop fusion | flops 12578816 | bytes 17858560 | tf_op jit(solution)/shard_map/reduce_sum | solution.py:309
  178.3 9.2 %fusion.124 = bf16[1,1024,4,80]{1,3,2,0:T(8,128)(2,1)} fusion(bf16[1024,4,80]{0,2,1:T(8,128)(2,1)S(1)} %bitcast.491, f32[4,1024,1024]{1,2,0:T(8,128)} %get-tuple-element.84, f32[4,1024]{1,0:T(4,128)S(1)} %fusion, f32[4,1024]{1,0:T(4,128)S(1)} %get-tuple-element.83, pred[1024,1024]{0,1:T(8,128)(4,1)S(1)} %fusion.14), kind=kOutput, calls=%fused_computation.186 | convolution fusion | flops 688193536 | bytes 19169280 | tf_op jit(solution)/shard_map/shqk,skhd->sqhd/dot_general | solution.py:311
  204.4 10.0 %all-to-all-done.2 = bf16[4,256,320]{1,2,0:T(8,128)(2,1)S(1)} async-done(((bf16[4,256,320]{1,2,0:T(8,128)(2,1)}), bf16[4,256,320]{1,2,0:T(8,128)(2,1)S(1)}, u32[]{:S(2)}, u32[]{:S(2)}) %all-to-all-start.2) | async-done | bytes 655392 | tf_op jit(solution)/shard_map/all_to_all | solution.py:147
  228.5 24.7 %collective-permute-done.14 = bf16[4,4,40,960]{3,2,1,0:T(8,128)(2,1)} collective-permute-done((bf16[4,4,40,960]{3,2,1,0:T(8,128)(2,1)}, bf16[4,4,40,960]{3,2,1,0:T(8,128)(2,1)}, u32[]{:S(2)}, u32[]{:S(2)}) %collective-permute-start.14) | collective-permute-done | bytes 1228832 | tf_op jit(solution)/shard_map/ppermute | solution.py:39
  263.0 7.7 %select_reduce_fusion = (f32[4,1024]{1,0:T(4,128)S(1)}, f32[4,1024,1024]{1,2,0:T(8,128)}) fusion(pred[1024,1024]{0,1:T(8,128)(4,1)S(1)} %fusion.14, bf16[1024,4,80]{0,2,1:T(8,128)(2,1)S(1)} %bitcast.462, f32[1024,4,80]{0,2,1:T(8,128)S(1)} %bitcast.444, f32[80]{0:T(128)S(1)} %get-tuple-element.79), kind=kOutput, calls=%fused_computation.12 | convolution fusion | flops 680128512 | bytes 19808576 | tf_op jit(solution)/shard_map/sqhd,skhd->shqk/dot_general | solution.py:301
  270.7 8.8 %fusion.1 = f32[4,1024]{1,0:T(4,128)S(1)} fusion(f32[4,1024,1024]{1,2,0:T(8,128)} %get-tuple-element.92, f32[4,1024]{1,0:T(4,128)S(1)} %get-tuple-element.91, pred[1024,1024]{0,1:T(8,128)(4,1)S(1)} %fusion.14), kind=kLoop, calls=%fused_computation.11 | loop fusion | flops 12578816 | bytes 17858560 | tf_op jit(solution)/shard_map/reduce_sum | solution.py:309
  279.5 8.9 %fusion.125 = bf16[1,1024,4,80]{1,3,2,0:T(8,128)(2,1)} fusion(bf16[1024,4,80]{0,2,1:T(8,128)(2,1)} %bitcast.493, f32[4,1024,1024]{1,2,0:T(8,128)} %get-tuple-element.92, f32[4,1024]{1,0:T(4,128)S(1)} %fusion.1, f32[4,1024]{1,0:T(4,128)S(1)} %get-tuple-element.91, pred[1024,1024]{0,1:T(8,128)(4,1)S(1)} %fusion.14), kind=kOutput, calls=%fused_computation.187 | convolution fusion | flops 688193536 | bytes 19169280 | tf_op jit(solution)/shard_map/shqk,skhd->sqhd/dot_general | solution.py:311
  342.1 5.5 all-to-all-done.4
  355.4 10.8 %fusion.101 = bf16[4,80,1024]{2,1,0:T(8,128)(2,1)} fusion(bf16[1024,4,80]{0,2,1:T(8,128)(2,1)} %reshape.648, f32[4,1024,1024]{1,2,0:T(8,128)} %get-tuple-element.92, f32[4,1024]{1,0:T(4,128)S(1)} %log_add_fusion.1, pred[1024,1024]{0,1:T(8,128)(4,1)S(1)} %fusion.14), kind=kOutput, calls=%fused_computation.125 | convolution fusion | flops 683999232 | bytes 19152896 | tf_op jit(solution)/shard_map/shqk,sqhd->skhd/dot_general | solution.py:318
  366.2 11.9 %multiply_reduce_fusion.1 = (f32[4,1024]{1,0:T(4,128)S(1)}, f32[4,1024,1024]{1,2,0:T(8,128)}) fusion(f32[4,1024,1024]{1,2,0:T(8,128)} %get-tuple-element.92, f32[4,1024]{1,0:T(4,128)S(1)} %log_add_fusion.1, pred[1024,1024]{0,1:T(8,128)(4,1)S(1)} %fusion.14, bf16[1024,4,80]{0,2,1:T(8,128)(2,1)S(1)} %copy-done.51, bf16[1024,4,80]{0,2,1:T(8,128)(2,1)S(1)} %bitcast.494), kind=kOutput, calls=%fused_computation.4 | convolution fusion | flops 687861760 | bytes 35946496 | tf_op jit(solution)/shard_map/sqhd,skhd->shqk/dot_general | solution.py:321
  382.6 12.5 %multiply_convert_fusion.1 = bf16[4,1024,1024]{1,2,0:T(8,128)(2,1)S(1)} fusion(f32[4,1024,1024]{1,2,0:T(8,128)} %get-tuple-element.98, f32[4,1024,1024]{1,2,0:T(8,128)} %get-tuple-element.92, f32[4,1024]{1,0:T(4,128)S(1)} %get-tuple-element.97, f32[4,1024]{1,0:T(4,128)S(1)} %log_add_fusion.1, pred[1024,1024]{0,1:T(8,128)(4,1)S(1)} %fusion.14), kind=kLoop, calls=%fused_computation.3 | loop fusion | flops 20971520 | bytes 43024384 | tf_op jit(solution)/shard_map/convert_element_type | solution.py:323
  408.2 5.2 convolution_bitcast_fusion
  431.9 21.4 %collective-permute-done.26 = bf16[4,160,960]{2,1,0:T(8,128)(2,1)} collective-permute-done((bf16[4,160,960]{2,1,0:T(8,128)(2,1)}, bf16[4,160,960]{2,1,0:T(8,128)(2,1)}, u32[]{:S(2)}, u32[]{:S(2)}) %collective-permute-start.26) | collective-permute-done | bytes 1228832 | tf_op jit(solution)/shard_map/ppermute | solution.py:39
  496.9 8.3 %fusion.104 = bf16[4,80,1024]{2,1,0:T(8,128)(2,1)S(1)} fusion(bf16[1024,4,80]{0,2,1:T(8,128)(2,1)S(1)} %reshape.652, f32[4,1024,1024]{1,2,0:T(8,128)} %get-tuple-element.84, f32[4,1024]{1,0:T(4,128)S(1)} %log_add_fusion, pred[1024,1024]{0,1:T(8,128)(4,1)S(1)} %fusion.14), kind=kOutput, calls=%fused_computation.126 | convolution fusion | flops 683999232 | bytes 19152896 | tf_op jit(solution)/shard_map/shqk,sqhd->skhd/dot_general | solution.py:318
  505.2 12.2 %multiply_reduce_fusion = (f32[4,1024]{1,0:T(4,128)S(1)}, f32[4,1024,1024]{1,2,0:T(8,128)}) fusion(f32[4,1024,1024]{1,2,0:T(8,128)} %get-tuple-element.84, f32[4,1024]{1,0:T(4,128)S(1)} %log_add_fusion, pred[1024,1024]{0,1:T(8,128)(4,1)S(1)} %fusion.14, bf16[1024,4,80]{0,2,1:T(8,128)(2,1)S(1)} %reshape.652, bf16[1024,4,80]{0,2,1:T(8,128)(2,1)S(1)} %bitcast.492), kind=kOutput, calls=%fused_computation.1 | convolution fusion | flops 687861760 | bytes 35946496 | tf_op jit(solution)/shard_map/sqhd,skhd->shqk/dot_general | solution.py:321
  517.4 12.9 %multiply_convert_fusion = bf16[4,1024,1024]{1,2,0:T(8,128)(2,1)S(1)} fusion(f32[4,1024,1024]{1,2,0:T(8,128)} %get-tuple-element.102, f32[4,1024,1024]{1,2,0:T(8,128)} %get-tuple-element.84, f32[4,1024]{1,0:T(4,128)S(1)} %get-tuple-element.101, f32[4,1024]{1,0:T(4,128)S(1)} %log_add_fusion, pred[1024,1024]{0,1:T(8,128)(4,1)S(1)} %fusion.14), kind=kLoop, calls=%fused_computation | loop fusion | flops 20971520 | bytes 43024384 | tf_op jit(solution)/shard_map/convert_element_type | solution.py:323
  550.6 27.1 %collective-permute-done.40 = f32[2,80]{1,0:T(2,128)S(1)} collective-permute-done((f32[2,80]{1,0:T(2,128)S(1)}, f32[2,80]{1,0:T(2,128)S(1)}, u32[]{:S(2)}, u32[]{:S(2)}) %collective-permute-start.40) | collective-permute-done | bytes 672 | tf_op jit(solution)/shard_map/ppermute | solution.py:39
  580.1 6.0 collective-permute-done.28
  593.0 5.7 all-to-all-done.7
  614.3 7.4 collective-permute-done.25
  621.7 13.4 %collective-permute-done.24 = bf16[160,960]{1,0:T(8,128)(2,1)S(1)} collective-permute-done((bf16[160,960]{1,0:T(8,128)(2,1)S(1)}, bf16[160,960]{1,0:T(8,128)(2,1)S(1)}, u32[]{:S(2)}, u32[]{:S(2)}) %collective-permute-start.24) | collective-permute-done | bytes 307232 | tf_op jit(solution)/shard_map/ppermute | solution.py:39
  662.2 24.4 %collective-permute-done.33 = bf16[4,2,40,1920]{3,2,1,0:T(8,128)(2,1)S(1)} collective-permute-done((bf16[4,2,40,1920]{3,2,1,0:T(8,128)(2,1)S(1)}, bf16[4,2,40,1920]{3,2,1,0:T(8,128)(2,1)S(1)}, u32[]{:S(2)}, u32[]{:S(2)}) %collective-permute-start.33) | collective-permute-done | bytes 1228832 | tf_op jit(solution)/shard_map/ppermute | solution.py:39
  692.0 12.2 %collective-permute-done.34 = bf16[4,40,1920]{2,1,0:T(8,128)(2,1)S(1)} collective-permute-done((bf16[4,40,1920]{2,1,0:T(8,128)(2,1)S(1)}, bf16[4,40,1920]{2,1,0:T(8,128)(2,1)S(1)}, u32[]{:S(2)}, u32[]{:S(2)}) %collective-permute-start.34) | collective-permute-done | bytes 614432 | tf_op jit(solution)/shard_map/ppermute | solution.py:39
  711.0 6.0 collective-permute-done.35
  717.0 11.4 %collective-permute-done.36 = bf16[40,3840]{1,0:T(8,128)(2,1)S(1)} collective-permute-done((bf16[40,3840]{1,0:T(8,128)(2,1)S(1)}, bf16[40,3840]{1,0:T(8,128)(2,1)S(1)}, u32[]{:S(2)}, u32[]{:S(2)}) %collective-permute-start.36) | collective-permute-done | bytes 307232 | tf_op jit(solution)/shard_map/ppermute | solution.py:39
  (452 shorter events, 313.6 us)
Async XLA Ops:
  7.2 207.1 %all-gather.3.cloned.1.call-start = ((), (), s32[]{:S(2)}) async-start(), calls=%async_computation.9 | async-start | bytes 10137600 | tf_op jit(solution)/shard_map/all_gather | solution.py:423
  22.9 288.7 %all-gather.5.cloned.1.call-start = ((), (), s32[]{:S(2)}) async-start(), calls=%async_computation.10 | async-start | bytes 10137600 | tf_op jit(solution)/shard_map/all_gather | solution.py:423
  35.3 33.3 %collective-permute-start.2 = (bf16[4,40,964]{2,1,0:T(8,128)(2,1)S(1)}, bf16[4,40,964]{2,1,0:T(8,128)(2,1)S(1)}, u32[]{:S(2)}, u32[]{:S(2)}) collective-permute-start(bf16[4,40,964]{2,1,0:T(8,128)(2,1)S(1)} %pad_maximum_fusion.18), channel_id=1, source_target_pairs={{0,16},{8,24},{16,0},{24,8},{1,17},{9,25},{17,1},{25,9},{2,18},{10... | collective-permute-start | bytes 925448 | tf_op jit(solution)/shard_map/ppermute | solution.py:39
  37.7 30.8 %collective-permute-start.1 = (bf16[4,40,964]{2,1,0:T(8,128)(2,1)S(1)}, bf16[4,40,964]{2,1,0:T(8,128)(2,1)S(1)}, u32[]{:S(2)}, u32[]{:S(2)}) collective-permute-start(bf16[4,40,964]{2,1,0:T(8,128)(2,1)S(1)} %pad_maximum_fusion.18), channel_id=1, source_target_pairs={{0,8},{8,0},{16,24},{24,16},{1,9},{9,1},{17,25},{25,17},{2,10},{10... | collective-permute-start | bytes 925448 | tf_op jit(solution)/shard_map/ppermute | solution.py:39
  39.2 34.8 %collective-permute-start.3 = (bf16[4,40,964]{2,1,0:T(8,128)(2,1)S(1)}, bf16[4,40,964]{2,1,0:T(8,128)(2,1)S(1)}, u32[]{:S(2)}, u32[]{:S(2)}) collective-permute-start(bf16[4,40,964]{2,1,0:T(8,128)(2,1)S(1)} %pad_maximum_fusion.18), channel_id=1, source_target_pairs={{0,24},{8,16},{16,8},{24,0},{1,25},{9,17},{17,9},{25,1},{2,26},{10... | collective-permute-start | bytes 925448 | tf_op jit(solution)/shard_map/ppermute | solution.py:39
  40.5 36.4 %collective-permute-start = (bf16[1,128,1280]{2,1,0:T(8,128)(2,1)}, bf16[1,128,1280]{2,1,0:T(8,128)(2,1)}, u32[]{:S(2)}, u32[]{:S(2)}) collective-permute-start(bf16[1,128,1280]{2,1,0:T(8,128)(2,1)} %constant_dynamic-slice_fusion.20), channel_id=1, source_target_pairs={{0,4},{4,0},{1,5},{5,1},{2,6},{6,2},{3,7},{7,3},{8,12},{12,8},{9,1... | collective-permute-start | bytes 983048 | tf_op jit(solution)/shard_map/ppermute | solution.py:39
  74.5 47.6 %collective-permute-start.4 = (bf16[4,4,40,964]{3,2,1,0:T(8,128)(2,1)S(1)}, bf16[4,4,40,964]{3,2,1,0:T(8,128)(2,1)}, u32[]{:S(2)}, u32[]{:S(2)}) collective-permute-start(bf16[4,4,40,964]{3,2,1,0:T(8,128)(2,1)S(1)} %pad_maximum_fusion.10), channel_id=1, source_target_pairs={{0,4},{4,0},{1,5},{5,1},{2,6},{6,2},{3,7},{7,3},{8,12},{12,8},{9,1... | collective-permute-start | bytes 3701768 | tf_op jit(solution)/shard_map/ppermute | solution.py:39
  129.7 24.4 %collective-permute-start.5 = (bf16[256,1280]{1,0:T(8,128)(2,1)}, bf16[256,1280]{1,0:T(8,128)(2,1)S(1)}, u32[]{:S(2)}, u32[]{:S(2)}) collective-permute-start(bf16[256,1280]{1,0:T(8,128)(2,1)} %multiply_convert_fusion.9), channel_id=1, source_target_pairs={{0,1},{1,0},{2,3},{3,2},{4,5},{5,4},{6,7},{7,6},{8,9},{9,8},{10,11... | collective-permute-start | bytes 1966088 | tf_op jit(solution)/shard_map/ppermute | solution.py:39
  142.1 57.3 %collective-permute-start.13 = (bf16[4,40,960]{2,1,0:T(8,128)(2,1)}, bf16[4,40,960]{2,1,0:T(8,128)(2,1)}, u32[]{:S(2)}, u32[]{:S(2)}) collective-permute-start(bf16[4,40,960]{2,1,0:T(8,128)(2,1)} %get-tuple-element.71), channel_id=1, source_target_pairs={{0,24},{8,16},{16,8},{24,0},{1,25},{9,17},{17,9},{25,1},{2,26},{10... | collective-permute-start | bytes 921608 | tf_op jit(solution)/shard_map/ppermute | solution.py:39
  144.4 55.0 %collective-permute-start.12 = (bf16[4,40,960]{2,1,0:T(8,128)(2,1)}, bf16[4,40,960]{2,1,0:T(8,128)(2,1)}, u32[]{:S(2)}, u32[]{:S(2)}) collective-permute-start(bf16[4,40,960]{2,1,0:T(8,128)(2,1)} %get-tuple-element.71), channel_id=1, source_target_pairs={{0,16},{8,24},{16,0},{24,8},{1,17},{9,25},{17,1},{25,9},{2,18},{10... | collective-permute-start | bytes 921608 | tf_op jit(solution)/shard_map/ppermute | solution.py:39
  153.7 45.7 %collective-permute-start.11 = (bf16[4,40,960]{2,1,0:T(8,128)(2,1)}, bf16[4,40,960]{2,1,0:T(8,128)(2,1)}, u32[]{:S(2)}, u32[]{:S(2)}) collective-permute-start(bf16[4,40,960]{2,1,0:T(8,128)(2,1)} %get-tuple-element.71), channel_id=1, source_target_pairs={{0,8},{8,0},{16,24},{24,16},{1,9},{9,1},{17,25},{25,17},{2,10},{10... | collective-permute-start | bytes 921608 | tf_op jit(solution)/shard_map/ppermute | solution.py:39
  193.6 20.7 %all-to-all-start.2 = ((bf16[4,256,320]{1,2,0:T(8,128)(2,1)}), bf16[4,256,320]{1,2,0:T(8,128)(2,1)S(1)}, u32[]{:S(2)}, u32[]{:S(2)}) async-start(bf16[4,256,320]{1,2,0:T(8,128)(2,1)} %reshape.635), calls=%async_computation.2 | async-start | bytes 1310720 | tf_op jit(solution)/shard_map/all_to_all | solution.py:147
  198.8 27.3 %collective-permute-start.16 = (bf16[1,128,1280]{2,1,0:T(8,128)(2,1)}, bf16[1,128,1280]{2,1,0:T(8,128)(2,1)}, u32[]{:S(2)}, u32[]{:S(2)}) collective-permute-start(bf16[1,128,1280]{2,1,0:T(8,128)(2,1)} %constant_dynamic-slice_fusion.2), channel_id=1, source_target_pairs={{0,4},{4,0},{1,5},{5,1},{2,6},{6,2},{3,7},{7,3},{8,12},{12,8},{9,1... | collective-permute-start | bytes 983048 | tf_op jit(solution)/shard_map/ppermute | solution.py:39
  202.9 50.3 %collective-permute-start.14 = (bf16[4,4,40,960]{3,2,1,0:T(8,128)(2,1)}, bf16[4,4,40,960]{3,2,1,0:T(8,128)(2,1)}, u32[]{:S(2)}, u32[]{:S(2)}) collective-permute-start(bf16[4,4,40,960]{3,2,1,0:T(8,128)(2,1)} %pad_maximum_fusion.12), channel_id=1, source_target_pairs={{0,4},{4,0},{1,5},{5,1},{2,6},{6,2},{3,7},{7,3},{8,12},{12,8},{9,1... | collective-permute-start | bytes 3686408 | tf_op jit(solution)/shard_map/ppermute | solution.py:39
  225.7 29.1 %collective-permute-start.9 = (bf16[256,1280]{1,0:T(8,128)(2,1)S(1)}, bf16[256,1280]{1,0:T(8,128)(2,1)S(1)}, u32[]{:S(2)}, u32[]{:S(2)}) collective-permute-start(bf16[256,1280]{1,0:T(8,128)(2,1)S(1)} %multiply_convert_fusion.5), channel_id=1, source_target_pairs={{0,2},{1,3},{2,0},{3,1},{4,6},{5,7},{6,4},{7,5},{8,10},{9,11},{10,... | collective-permute-start | bytes 1966088 | tf_op jit(solution)/shard_map/ppermute | solution.py:39
  337.3 391.3 %reduce-scatter.2.cloned.1.call-start = ((), (), s32[]{:S(2)}) async-start(), calls=%async_computation.11 | async-start | bytes 10137600 | tf_op jit(solution)/shard_map/reduce_scatter | solution.py:230
  415.6 131.7 %collective-permute-start.15 = (bf16[1,128,1280]{2,1,0:T(8,128)(2,1)}, bf16[1,128,1280]{2,1,0:T(8,128)(2,1)}, u32[]{:S(2)}, u32[]{:S(2)}) collective-permute-start(bf16[1,128,1280]{2,1,0:T(8,128)(2,1)} %dynamic-slice_bitcast_fusion.3), channel_id=1, source_target_pairs={{0,4},{4,0},{1,5},{5,1},{2,6},{6,2},{3,7},{7,3},{8,12},{12,8},{9,1... | collective-permute-start | bytes 983048 | tf_op jit(solution)/shard_map/ppermute | solution.py:39
  422.1 31.2 %collective-permute-start.26 = (bf16[4,160,960]{2,1,0:T(8,128)(2,1)}, bf16[4,160,960]{2,1,0:T(8,128)(2,1)}, u32[]{:S(2)}, u32[]{:S(2)}) collective-permute-start(bf16[4,160,960]{2,1,0:T(8,128)(2,1)} %fusion.108), channel_id=1, source_target_pairs={{0,4},{4,0},{1,5},{5,1},{2,6},{6,2},{3,7},{7,3},{8,12},{12,8},{9,1... | collective-permute-start | bytes 3686408 | tf_op jit(solution)/shard_map/ppermute | solution.py:39
  426.1 32.8 %collective-permute-start.18 = (bf16[256,1280]{1,0:T(8,128)(2,1)}, bf16[256,1280]{1,0:T(8,128)(2,1)S(1)}, u32[]{:S(2)}, u32[]{:S(2)}) collective-permute-start(bf16[256,1280]{1,0:T(8,128)(2,1)} %fusion.126), channel_id=1, source_target_pairs={{0,2},{1,3},{2,0},{3,1},{4,6},{5,7},{6,4},{7,5},{8,10},{9,11},{10,... | collective-permute-start | bytes 1966088 | tf_op jit(solution)/shard_map/ppermute | solution.py:39
  457.4 93.2 %collective-permute-start.27 = (bf16[160,960]{1,0:T(8,128)(2,1)}, bf16[160,960]{1,0:T(8,128)(2,1)}, u32[]{:S(2)}, u32[]{:S(2)}) collective-permute-start(bf16[160,960]{1,0:T(8,128)(2,1)} %get-tuple-element.22), channel_id=1, source_target_pairs={{0,8},{8,0},{16,24},{24,16},{1,9},{9,1},{17,25},{25,17},{2,10},{10... | collective-permute-start | bytes 921608 | tf_op jit(solution)/shard_map/ppermute | solution.py:39
  489.4 163.3 %collective-permute-start.30 = (bf16[4,2,2,40,3840]{4,3,2,1,0:T(8,128)(2,1)}, bf16[4,2,2,40,3840]{4,3,2,1,0:T(8,128)(2,1)}, u32[]{:S(2)}, u32[]{:S(2)}) collective-permute-start(bf16[4,2,2,40,3840]{4,3,2,1,0:T(8,128)(2,1)} %dynamic-slice_bitcast_fusion), channel_id=1, source_target_pairs={{0,1},{1,0},{2,3},{3,2},{4,5},{5,4},{6,7},{7,6},{8,9},{9,8},{10,11... | collective-permute-start | bytes 14745608 | tf_op jit(solution)/shard_map/ppermute | solution.py:39
  543.9 56.8 %collective-permute-start.22 = (bf16[4,160,960]{2,1,0:T(8,128)(2,1)}, bf16[4,160,960]{2,1,0:T(8,128)(2,1)}, u32[]{:S(2)}, u32[]{:S(2)}) collective-permute-start(bf16[4,160,960]{2,1,0:T(8,128)(2,1)} %fusion.107), channel_id=1, source_target_pairs={{0,4},{4,0},{1,5},{5,1},{2,6},{6,2},{3,7},{7,3},{8,12},{12,8},{9,1... | collective-permute-start | bytes 3686408 | tf_op jit(solution)/shard_map/ppermute | solution.py:39
  544.5 33.2 %collective-permute-start.40 = (f32[2,80]{1,0:T(2,128)S(1)}, f32[2,80]{1,0:T(2,128)S(1)}, u32[]{:S(2)}, u32[]{:S(2)}) collective-permute-start(f32[2,80]{1,0:T(2,128)S(1)} %fusion.222), channel_id=1, source_target_pairs={{0,4},{4,0},{1,5},{5,1},{2,6},{6,2},{3,7},{7,3},{8,12},{12,8},{9,1... | collective-permute-start | bytes 1928 | tf_op jit(solution)/shard_map/ppermute | solution.py:39
  547.4 31.3 %collective-permute-start.29 = (bf16[160,960]{1,0:T(8,128)(2,1)S(1)}, bf16[160,960]{1,0:T(8,128)(2,1)S(1)}, u32[]{:S(2)}, u32[]{:S(2)}) collective-permute-start(bf16[160,960]{1,0:T(8,128)(2,1)S(1)} %copy-done.65), channel_id=1, source_target_pairs={{0,24},{8,16},{16,8},{24,0},{1,25},{9,17},{17,9},{25,1},{2,26},{10... | collective-permute-start | bytes 921608 | tf_op jit(solution)/shard_map/ppermute | solution.py:39
  550.6 35.5 %collective-permute-start.28 = (bf16[160,960]{1,0:T(8,128)(2,1)S(1)}, bf16[160,960]{1,0:T(8,128)(2,1)S(1)}, u32[]{:S(2)}, u32[]{:S(2)}) collective-permute-start(bf16[160,960]{1,0:T(8,128)(2,1)S(1)} %copy-done.64), channel_id=1, source_target_pairs={{0,16},{8,24},{16,0},{24,8},{1,17},{9,25},{17,1},{25,9},{2,18},{10... | collective-permute-start | bytes 921608 | tf_op jit(solution)/shard_map/ppermute | solution.py:39
  577.7 29.4 %collective-permute-start.19 = (bf16[2,256,1280]{2,1,0:T(8,128)(2,1)}, bf16[2,256,1280]{2,1,0:T(8,128)(2,1)}, u32[]{:S(2)}, u32[]{:S(2)}) collective-permute-start(bf16[2,256,1280]{2,1,0:T(8,128)(2,1)} %fusion.110), channel_id=1, source_target_pairs={{0,1},{1,0},{2,3},{3,2},{4,5},{5,4},{6,7},{7,6},{8,9},{9,8},{10,11... | collective-permute-start | bytes 3932168 | tf_op jit(solution)/shard_map/ppermute | solution.py:39
  606.1 29.1 %collective-permute-start.24 = (bf16[160,960]{1,0:T(8,128)(2,1)S(1)}, bf16[160,960]{1,0:T(8,128)(2,1)S(1)}, u32[]{:S(2)}, u32[]{:S(2)}) collective-permute-start(bf16[160,960]{1,0:T(8,128)(2,1)S(1)} %get-tuple-element.21), channel_id=1, source_target_pairs={{0,16},{8,24},{16,0},{24,8},{1,17},{9,25},{17,1},{25,9},{2,18},{10... | collective-permute-start | bytes 921608 | tf_op jit(solution)/shard_map/ppermute | solution.py:39
  641.8 18.5 %collective-permute-start.20 = (bf16[256,1280]{1,0:T(8,128)(2,1)}, bf16[256,1280]{1,0:T(8,128)(2,1)S(1)}, u32[]{:S(2)}, u32[]{:S(2)}) collective-permute-start(bf16[256,1280]{1,0:T(8,128)(2,1)} %fusion.127), channel_id=1, source_target_pairs={{0,2},{1,3},{2,0},{3,1},{4,6},{5,7},{6,4},{7,5},{8,10},{9,11},{10,... | collective-permute-start | bytes 1966088 | tf_op jit(solution)/shard_map/ppermute | solution.py:39
  658.2 28.3 %collective-permute-start.33 = (bf16[4,2,40,1920]{3,2,1,0:T(8,128)(2,1)S(1)}, bf16[4,2,40,1920]{3,2,1,0:T(8,128)(2,1)S(1)}, u32[]{:S(2)}, u32[]{:S(2)}) collective-permute-start(bf16[4,2,40,1920]{3,2,1,0:T(8,128)(2,1)S(1)} %dynamic-slice_bitcast_fusion.1), channel_id=1, source_target_pairs={{0,2},{1,3},{2,0},{3,1},{4,6},{5,7},{6,4},{7,5},{8,10},{9,11},{10,... | collective-permute-start | bytes 3686408 | tf_op jit(solution)/shard_map/ppermute | solution.py:39
  661.1 30.0 %collective-permute-start.31 = (bf16[4,2,40,1920]{3,2,0,1:T(8,128)(2,1)S(1)}, bf16[4,2,40,1920]{3,2,0,1:T(8,128)(2,1)S(1)}, u32[]{:S(2)}, u32[]{:S(2)}) collective-permute-start(bf16[4,2,40,1920]{3,2,0,1:T(8,128)(2,1)S(1)} %bitcast.497), channel_id=1, source_target_pairs={{0,4},{4,0},{1,5},{5,1},{2,6},{6,2},{3,7},{7,3},{8,12},{12,8},{9,1... | collective-permute-start | bytes 3686408 | tf_op jit(solution)/shard_map/ppermute | solution.py:39
  704.8 23.7 %collective-permute-start.36 = (bf16[40,3840]{1,0:T(8,128)(2,1)S(1)}, bf16[40,3840]{1,0:T(8,128)(2,1)S(1)}, u32[]{:S(2)}, u32[]{:S(2)}) collective-permute-start(bf16[40,3840]{1,0:T(8,128)(2,1)S(1)} %get-tuple-element.38), channel_id=1, source_target_pairs={{0,16},{8,24},{16,0},{24,8},{1,17},{9,25},{17,1},{25,9},{2,18},{10... | collective-permute-start | bytes 921608 | tf_op jit(solution)/shard_map/ppermute | solution.py:39
  707.7 20.8 %collective-permute-start.37 = (bf16[40,3840]{1,0:T(8,128)(2,1)S(1)}, bf16[40,3840]{1,0:T(8,128)(2,1)S(1)}, u32[]{:S(2)}, u32[]{:S(2)}) collective-permute-start(bf16[40,3840]{1,0:T(8,128)(2,1)S(1)} %get-tuple-element.39), channel_id=1, source_target_pairs={{0,24},{8,16},{16,8},{24,0},{1,25},{9,17},{17,9},{25,1},{2,26},{10... | collective-permute-start | bytes 921608 | tf_op jit(solution)/shard_map/ppermute | solution.py:39
  (114 other events, 1257.9 us)
Sparse Core Ops, SparseCore 0:
  11.0 117.7 all-gather.2
  131.6 115.3 all-gather.4
  432.0 148.3 reduce-scatter.1

commit v3 on v1

--- a/solution.py
+++ b/solution.py
@@ -1,8 +1,11 @@
+import functools
 import math
 
 import jax
 import jax.numpy as jnp
 from jax import lax
+from jax.experimental import pallas as pl
+from jax.experimental.pallas import tpu as pltpu
 from jax.sharding import PartitionSpec as P
 
 WINDOW = 1024
@@ -20,6 +23,10 @@
     devices = range(lax.axis_size(axis))
     route = [(i - distance, i) for i in devices if i - distance in devices]
     return lax.ppermute(block, axis, route)
+
+
+NT = (((1,), (1,)), ((), ()))
+TN = (((0,), (0,)), ((), ()))
 
 
 def dot(left, right):
@@ -273,7 +280,7 @@
     return lower, qkv_own, dense_own, (attn_gain_grad, mlp_gain_grad), scale_vec_grad
 
 
-def per_device(
+def general_device(
     tokens,
     segments,
     qkv_weight,
@@ -351,6 +358,493 @@
     )
 
 
+Q_ROWS = 256
+KERNEL = pltpu.CompilerParams(vmem_limit_bytes=50 * 1024 * 1024)
+
+
+def allowed_keys(col, row, first):
+    count = first + row.shape[1]
+    key_place = lax.broadcasted_iota(jnp.int32, (count, row.shape[1]), 0)
+    query_place = lax.broadcasted_iota(jnp.int32, (count, row.shape[1]), 1) + first
+    return (col[:count] == row) & (key_place <= query_place)
+
+
+def token_places(length, heads, token_rows):
+    for first in range(0, length, Q_ROWS):
+        parts = []
+        for start in range(0, Q_ROWS, token_rows):
+            place = (first + start) // token_rows
+            parts.append((start, place % heads, place // heads * token_rows))
+        yield first, parts
+
+
+def attend_kernel(token_rows, proj_ref, scale_ref, col_ref, row_ref, out_ref, lse_ref):
+    length = proj_ref.shape[-1]
+    queries = (proj_ref[0, 0] * scale_ref[...]).astype(BF16)
+    keys = proj_ref[1, 0].T.astype(BF16)
+    values = proj_ref[2, 0].astype(BF16)
+    for first, parts in token_places(length, out_ref.shape[0], token_rows):
+        end = first + Q_ROWS
+        scores = jnp.dot(keys[:end], queries[:, first:end], preferred_element_type=F32)
+        allowed = allowed_keys(col_ref[...], row_ref[:, first:end], first)
+        scores = jnp.where(allowed, scores, MASKED_SCORE)
+        top = jnp.max(scores, axis=0, keepdims=True)
+        terms = jnp.exp(scores - top)
+        total = jnp.sum(terms, axis=0, keepdims=True)
+        probs = (terms * (1.0 / total)).astype(BF16)
+        attended = jnp.dot(values[:, :end], probs, preferred_element_type=F32).astype(BF16)
+        lse_ref[0, :, first:end] = top + jnp.log(total)
+        for start, owner, offset in parts:
+            out_ref[owner, 0, :, offset : offset + token_rows] = attended[
+                :, start : start + token_rows
+            ]
+
+
+def attend_rows(projected, scale_vec, segments, owners, token_rows):
+    head_dim = scale_vec.shape[0]
+    length = projected.shape[1]
+    local_heads = projected.shape[0] // 3 // head_dim
+    tokens = length // owners
+    attended, log_total = pl.pallas_call(
+        functools.partial(attend_kernel, token_rows),
+        grid=(local_heads,),
+        in_specs=[
+            pl.BlockSpec((3, 1, head_dim, length), lambda h: (0, h, 0, 0)),
+            pl.BlockSpec((head_dim, 1), lambda h: (0, 0)),
+            pl.BlockSpec((length, 1), lambda h: (0, 0)),
+            pl.BlockSpec((1, length), lambda h: (0, 0)),
+        ],
+        out_specs=[
+            pl.BlockSpec((owners, 1, head_dim, tokens), lambda h: (0, h, 0, 0)),
+            pl.BlockSpec((1, 1, length), lambda h: (h, 0, 0)),
+        ],
+        out_shape=[
+            jax.ShapeDtypeStruct((owners, local_heads, head_dim, tokens), BF16),
+            jax.ShapeDtypeStruct((local_heads, 1, length), F32),
+        ],
+        compiler_params=KERNEL,
+        cost_estimate=pl.CostEstimate(
+            flops=4 * local_heads * length * length * head_dim,
+            bytes_accessed=projected.size * 4,
+            transcendentals=local_heads * length * length // 2,
+        ),
+    )(
+        projected.reshape(3, local_heads, head_dim, length),
+        scale_vec.reshape(head_dim, 1),
+        segments.reshape(length, 1),
+        segments.reshape(1, length),
+    )
+    return attended.reshape(owners, local_heads * head_dim, tokens), log_total
+
+
+def attend_back_kernel(
+    token_rows,
+    proj_ref,
+    grad_ref,
+    lse_ref,
+    scale_ref,
+    col_ref,
+    row_ref,
+    out_ref,
+    scale_grad_ref,
+    keys_acc,
+    values_acc,
+):
+    length = proj_ref.shape[-1]
+    scale = scale_ref[...]
+    query_pre = proj_ref[0, 0]
+    queries = (query_pre * scale).astype(BF16)
+    keys_t = proj_ref[1, 0].astype(BF16)
+    keys = proj_ref[1, 0].T.astype(BF16)
+    values = proj_ref[2, 0].T.astype(BF16)
+    keys_acc[...] = jnp.zeros_like(keys_acc)
+    values_acc[...] = jnp.zeros_like(values_acc)
+    scale_grad = jnp.zeros((scale.shape[0], 1), F32)
+    for first, parts in token_places(length, grad_ref.shape[0], token_rows):
+        end = first + Q_ROWS
+        block = queries[:, first:end]
+        grad = jnp.concatenate(
+            [grad_ref[owner, 0, :, at : at + token_rows] for _, owner, at in parts], axis=1
+        )
+        scores = jnp.dot(keys[:end], block, preferred_element_type=F32)
+        allowed = allowed_keys(col_ref[...], row_ref[:, first:end], first)
+        scores = jnp.where(allowed, scores, MASKED_SCORE)
+        probs = jnp.exp(scores - lse_ref[0, :, first:end])
+        probs_grad = jnp.dot(values[:end], grad, preferred_element_type=F32)
+        row_dot = jnp.sum(probs_grad * probs, axis=0, keepdims=True)
+        scores_low = (probs * (probs_grad - row_dot)).astype(BF16)
+        values_acc[:, :end] += lax.dot_general(
+            grad, probs.astype(BF16), NT, preferred_element_type=F32
+        )
+        keys_acc[:, :end] += lax.dot_general(
+            block, scores_low, NT, preferred_element_type=F32
+        )
+        query_bar = jnp.dot(keys_t[:, :end], scores_low, preferred_element_type=F32)
+        query_bar = query_bar.astype(BF16).astype(F32)
+        scale_grad += jnp.sum(query_bar * query_pre[:, first:end], axis=1, keepdims=True)
+        out_ref[0, 0, :, first:end] = (query_bar * scale).astype(BF16)
+    out_ref[1, 0] = keys_acc[...].astype(BF16)
+    out_ref[2, 0] = values_acc[...].astype(BF16)
+    spread = jnp.broadcast_to(scale_grad, scale_grad_ref.shape)
+
+    @pl.when(pl.program_id(0) == 0)
+    def _():
+        scale_grad_ref[...] = spread
+
+    @pl.when(pl.program_id(0) > 0)
+    def _():
+        scale_grad_ref[...] += spread
+
+
+def attend_back_rows(projected, attended_grad, log_total, scale_vec, segments, token_rows):
+    head_dim = scale_vec.shape[0]
+    length = projected.shape[1]
+    local_heads = projected.shape[0] // 3 // head_dim
+    owners, _, tokens = attended_grad.shape
+    lanes = 128
+    grads, scale_grad = pl.pallas_call(
+        functools.partial(attend_back_kernel, token_rows),
+        grid=(local_heads,),
+        in_specs=[
+            pl.BlockSpec((3, 1, head_dim, length), lambda h: (0, h, 0, 0)),
+            pl.BlockSpec((owners, 1, head_dim, tokens), lambda h: (0, h, 0, 0)),
+            pl.BlockSpec((1, 1, length), lambda h: (h, 0, 0)),
+            pl.BlockSpec((head_dim, 1), lambda h: (0, 0)),
+            pl.BlockSpec((length, 1), lambda h: (0, 0)),
+            pl.BlockSpec((1, length), lambda h: (0, 0)),
+        ],
+        out_specs=[
+            pl.BlockSpec((3, 1, head_dim, length), lambda h: (0, h, 0, 0)),
+            pl.BlockSpec((head_dim, lanes), lambda h: (0, 0)),
+        ],
+        out_shape=[
+            jax.ShapeDtypeStruct((3, local_heads, head_dim, length), BF16),
+            jax.ShapeDtypeStruct((head_dim, lanes), F32),
+        ],
+        scratch_shapes=[
+            pltpu.VMEM((head_dim, length), F32),
+            pltpu.VMEM((head_dim, length), F32),
+        ],
+        compiler_params=KERNEL,
+        cost_estimate=pl.CostEstimate(
+            flops=10 * local_heads * length * length * head_dim,
+            bytes_accessed=projected.size * 6,
+            transcendentals=local_heads * length * length // 2,
+        ),
+    )(
+        projected.reshape(3, local_heads, head_dim, length),
+        attended_grad.reshape(owners, local_heads, head_dim, tokens),
+        log_total,
+        scale_vec.reshape(head_dim, 1),
+        segments.reshape(length, 1),
+        segments.reshape(1, length),
+    )
+    return grads.reshape(3 * local_heads * head_dim, length), scale_grad[:, 0]
+
+
+def dense_grad_kernel(attended_ref, normed_ref, active_ref, out_bar, up_bar, down_bar, grad_ref):
+    width = out_bar.shape[1]
+    grad_ref[:, :width] = jnp.dot(
+        attended_ref[...], out_bar[...], preferred_element_type=F32
+    ).astype(BF16)
+    grad_ref[:, width : 2 * width] = lax.dot_general(
+        normed_ref[...], up_bar[...], TN, preferred_element_type=F32
+    ).astype(BF16)
+    grad_ref[:, 2 * width :] = lax.dot_general(
+        active_ref[...], down_bar[...], TN, preferred_element_type=F32
+    ).astype(BF16)
+
+
+def dense_grads(attended_t, normed, active, out_bar, up_bar, down_bar):
+    width, tokens = attended_t.shape
+    tile = 256
+    whole = pl.BlockSpec((tokens, width), lambda i: (0, 0))
+    columns = pl.BlockSpec((tokens, tile), lambda i: (0, i))
+    return pl.pallas_call(
+        dense_grad_kernel,
+        grid=(width // tile,),
+        in_specs=[
+            pl.BlockSpec((tile, tokens), lambda i: (i, 0)), columns, columns, whole, whole, whole,
+        ],
+        out_specs=pl.BlockSpec((tile, 3 * width), lambda i: (i, 0)),
+        out_shape=jax.ShapeDtypeStruct((width, 3 * width), BF16),
+        compiler_params=KERNEL,
+        cost_estimate=pl.CostEstimate(
+            flops=6 * tokens * width * width, bytes_accessed=6 * width * width, transcendentals=0
+        ),
+    )(attended_t, normed, active, out_bar, up_bar, down_bar)
+
+
+def tied(*arrays):
+    return lax.optimization_barrier(arrays)
+
+
+def swapped(array, axis, mask):
+    size = lax.axis_size(axis)
+    return lax.ppermute(array, axis, [(i, i ^ mask) for i in range(size)])
+
+
+def pick(array, index, axis=0):
+    return lax.dynamic_index_in_dim(array, index, axis, keepdims=False)
+
+
+def swap_halves(array):
+    me = lax.axis_index("blk")
+    got = swapped(pick(array, 1 - me), "blk", 1)
+    kept = pick(array, me)
+    return jnp.stack([jnp.where(me == 0, kept, got), jnp.where(me == 0, got, kept)])
+
+
+def gather_rows(rows):
+    width = rows.shape[-1]
+    far = swapped(rows, "head", 2)
+    near = swapped(rows, "head", 1)
+    both = swapped(far, "head", 1)
+    pieces = jnp.stack([rows, near, far, both])
+    me = lax.axis_index("head")
+    ordered = jnp.stack([pick(pieces, me ^ i) for i in range(4)])
+    return ordered.reshape(4, 2, -1, width).transpose(1, 0, 2, 3).reshape(-1, width)
+
+
+def scatter_rows(rows):
+    width = rows.shape[-1]
+    me = lax.axis_index("head")
+    row, core = me // 2, me % 2
+    parts = rows.reshape(2, 2, 2, -1, width)
+    halves = pick(parts, core, 2) + swapped(
+        pick(parts, 1 - core, 2).astype(BF16), "head", 1
+    ).astype(F32)
+    got = swapped(pick(halves, 1 - row, 1).astype(BF16), "head", 2).astype(F32)
+    return (pick(halves, row, 1) + got).reshape(-1, width)
+
+
+def over_head(parts):
+    return lax.all_to_all(parts, "head", split_axis=0, concat_axis=0, tiled=True)
+
+
+def qkv_columns(rows, extra):
+    own, width = rows.shape
+    part = width // 3 // 4
+    sent = rows.reshape(own, 3, 4, part).transpose(2, 0, 1, 3).reshape(4, own, 3 * part)
+    if extra is not None:
+        sent = jnp.concatenate([sent, jnp.broadcast_to(extra[None], (4,) + extra.shape)], axis=2)
+    return over_head(sent)
+
+
+def gather_columns(piece, early):
+    along = [piece] + [swapped(piece, "batch", mask) for mask in (1, 2, 3)]
+    if early:
+        across = jnp.stack([swapped(part, "blk", 1) for part in along])
+        along = jnp.stack(along)
+    else:
+        along = jnp.stack(along)
+        across = swapped(along, "blk", 1)
+    me, blk = lax.axis_index("batch"), lax.axis_index("blk")
+    ordered = []
+    for i in range(4):
+        one, two = pick(along, me ^ i), pick(across, me ^ i)
+        ordered += [jnp.where(blk == 0, one, two), jnp.where(blk == 0, two, one)]
+    return jnp.stack(ordered).reshape(-1, piece.shape[-1])
+
+
+def scatter_over_batch(parts):
+    me = lax.axis_index("batch")
+    total = pick(parts, me).astype(F32)
+    for mask in (1, 2, 3):
+        total = total + swapped(pick(parts, me ^ mask).astype(BF16), "batch", mask).astype(F32)
+    return total
+
+
+def scatter_columns(grad):
+    blk = lax.axis_index("blk")
+    columns = grad.shape[1]
+    parts = grad.reshape(4, 2, -1, columns)
+    summed = pick(parts, blk, 1) + swapped(
+        pick(parts, 1 - blk, 1).astype(BF16), "blk", 1
+    ).astype(F32)
+    summed = scatter_over_batch(summed).astype(BF16)
+    moved = over_head(summed.reshape(4, -1, columns))
+    own = moved.shape[1]
+    return moved.reshape(4, own, 3, -1).transpose(1, 2, 0, 3).reshape(own, -1).astype(F32)
+
+
+def over_core(grad):
+    core = lax.axis_index("head") % 2
+    parts = grad.reshape(4, 2, 2, 2, -1, grad.shape[1])
+    got = swapped(pick(parts, 1 - core, 3), "head", 1).astype(F32)
+    return (pick(parts, core, 3).astype(F32) + got).astype(BF16)
+
+
+def over_chips(cored):
+    row, blk = lax.axis_index("head") // 2, lax.axis_index("blk")
+    half = cored.shape[-1] // 2
+
+    def over(part, axis, mask, mine, dim):
+        got = swapped(pick(part, 1 - mine, dim), axis, mask).astype(F32)
+        return (pick(part, mine, dim).astype(F32) + got).astype(BF16)
+
+    first = over(cored[..., :half], "blk", 1, blk, 1)
+    second = over(cored[..., half:], "head", 2, row, 2)
+    first = over(first, "head", 2, row, 1)
+    second = over(second, "blk", 1, blk, 1)
+    return scatter_over_batch(jnp.concatenate([first, second], axis=-1))
+
+
+def sum_all(array):
+    for axis, mask in (("head", 1), ("head", 2), ("blk", 1), ("batch", 1), ("batch", 2)):
+        array = array + swapped(array, axis, mask)
+    return array
+
+
+def gain_back(weight, weight_grad, gain):
+    return jnp.sum(weight.astype(F32) * weight_grad, axis=-1) / gain.astype(F32)
+
+
+def lower_of(upper, stream, factor, gain):
+    return norm_back(upper, stream, factor, gain)[0]
+
+
+def spread_device(
+    tokens,
+    segments,
+    qkv_weight,
+    out_weight,
+    up_weight,
+    down_weight,
+    attn_gain,
+    mlp_gain,
+    scale_param,
+    cotangent,
+):
+    layers, head_dim = scale_param.shape
+    _, token_rows, width = tokens.shape
+    scale_vecs = SCALE_BASE / math.sqrt(head_dim) * jax.nn.softplus(scale_param)
+    segments = pick(segments, lax.axis_index("blk"))
+    own_gains = jnp.concatenate([attn_gain, mlp_gain], axis=0)
+
+    first = swap_halves(tokens).reshape(-1, width)
+    columns = [qkv_columns(qkv_weight[0], own_gains.T)]
+    columns[0], first = tied(columns[0], first)
+    first_all = gather_rows(first)
+    stream = first.astype(F32)
+    with_gains = gather_columns(columns[0].reshape(-1, columns[0].shape[-1]), True)
+    part3 = 3 * width // 4
+    qkvs = [with_gains[:, :part3]]
+    gains = with_gains[:, part3:].T.astype(F32)
+    denses = []
+    for layer in range(layers):
+        own = jnp.concatenate([out_weight[layer], up_weight[layer], down_weight[layer]], axis=1)
+        denses.append(lax.all_gather(own, ALL, axis=0, tiled=True))
+
+    kept = []
+    for layer in range(layers):
+        if layer > 0:
+            piece = qkv_columns(qkv_weight[layer], None)
+            piece, _ = tied(piece.reshape(-1, part3), qkvs[layer - 1])
+            qkvs.append(gather_columns(piece, False))
+        qkv, dense = qkvs[layer], denses[layer]
+        out_w, up_w, down_w = dense[:, :width], dense[:, width:-width], dense[:, -width:]
+        normed, factor_one = normalize(stream, gains[layer])
+        if layer == 0:
+            normed_all = normalize(first_all.astype(F32), gains[0])[0].astype(BF16)
+        else:
+            normed_all = gather_rows(normed.astype(BF16))
+        projected = lax.dot_general(
+            qkv, normed_all, (((0,), (1,)), ((), ())), preferred_element_type=F32
+        )
+        attended, log_total = attend_rows(
+            projected, scale_vecs[layer], segments, 4, token_rows
+        )
+        attended_t = over_head(attended).reshape(width, -1)
+        middle = stream + dot_rows(attended_t, out_w)
+        normed_two, factor_two = normalize(middle, gains[layers + layer])
+        normed_two = normed_two.astype(BF16)
+        hidden = dot(normed_two, up_w)
+        active = (hidden * jax.nn.sigmoid(hidden)).astype(BF16)
+        kept.append(
+            (
+                stream, factor_one, normed_all, projected, log_total, attended_t, middle,
+                factor_two, normed_two, hidden, active,
+            )
+        )
+        stream = middle + dot(active, down_w)
+    layer_out = swap_halves(stream.astype(BF16).reshape(tokens.shape))
+    upper = swap_halves(cotangent).reshape(-1, width).astype(F32)
+
+    qkv_grads, dense_own, scale_grads = [None] * layers, [None] * layers, [None] * layers
+    for layer in reversed(range(layers)):
+        (
+            stream, factor_one, normed_all, projected, log_total, attended_t, middle,
+            factor_two, normed_two, hidden, active,
+        ) = kept[layer]
+        qkv, dense = qkvs[layer], denses[layer]
+        out_w, up_w, down_w = dense[:, :width], dense[:, width:-width], dense[:, -width:]
+        down_bar = upper.astype(BF16)
+        gate = jax.nn.sigmoid(hidden)
+        up_bar = (
+            dot_cols(down_bar, down_w) * gate * (1.0 + hidden * (1.0 - gate))
+        ).astype(BF16)
+        middle_grad = upper + lower_of(
+            dot_cols(up_bar, up_w), middle, factor_two, gains[layers + layer]
+        )
+        out_bar = middle_grad.astype(BF16)
+        attended_grad = over_head(dot_cols(out_w, out_bar).astype(BF16).reshape(4, -1, out_bar.shape[0]))
+        grads = dense_grads(attended_t, normed_two, active, out_bar, up_bar, down_bar)
+        attended_grad, grads = tied(attended_grad, grads)
+        cored = over_core(grads) if layer == 0 else None
+        bars, scale_grads[layer] = attend_back_rows(
+            projected, attended_grad, log_total, scale_vecs[layer], segments, token_rows
+        )
+        if layer == 0:
+            bars, cored = tied(bars, cored)
+            dense_own[layer] = over_chips(cored)
+        else:
+            dense_own[layer] = lax.psum_scatter(
+                grads, ALL, scatter_dimension=0, tiled=True
+            ).astype(F32)
+        normed_grad = scatter_rows(
+            lax.dot_general(bars, qkv, (((0,), (1,)), ((), ())), preferred_element_type=F32)
+        )
+        qkv_grads[layer] = scatter_columns(
+            lax.dot_general(normed_all, bars, (((0,), (1,)), ((), ())), preferred_element_type=F32)
+        )
+        upper = middle_grad + lower_of(normed_grad, stream, factor_one, gains[layer])
+    input_grad = swap_halves(upper.astype(BF16).reshape(tokens.shape)).astype(F32)
+    scale_total = sum_all(jnp.stack(scale_grads))
+    scale_grad = scale_total * (SCALE_BASE / math.sqrt(head_dim)) * jax.nn.sigmoid(scale_param)
+    dense_all = jnp.stack(dense_own)
+    qkv_all = jnp.stack(qkv_grads)
+    up_all = dense_all[:, :, width:-width]
+    return (
+        layer_out,
+        input_grad,
+        qkv_all,
+        dense_all[:, :, :width],
+        up_all,
+        dense_all[:, :, -width:],
+        gain_back(qkv_weight, qkv_all, attn_gain),
+        gain_back(up_weight, up_all, mlp_gain),
+        scale_grad,
+    )
+
+
+def per_device(*args):
+    tokens, segments = args[0], args[1]
+    sizes = tuple(lax.axis_size(axis) for axis in ALL)
+    heads = tokens.shape[2] // args[8].shape[1]
+    spread = (
+        sizes == (4, 2, 4)
+        and tokens.shape[0] == 2
+        and tokens.shape[1] % 128 == 0
+        and Q_ROWS % tokens.shape[1] == 0
+        and segments.shape[1] <= WINDOW
+        and segments.shape[1] % Q_ROWS == 0
+        and heads % 4 == 0
+        and tokens.shape[2] % 256 == 0
+    )
+    return spread_device(*args) if spread else general_device(*args)
+
+
 def solution(mesh):
     rows = P(None, ALL, None)
     by_token = P("batch", ("blk", "head"), None)

time: 1050 us -> 696 us (0.66)
  waiting for transfers between devices: 526 us -> 348 us
  blocking collectives: 132 us -> 0 us
  matrix products: 169 us -> 53.7 us
  Pallas kernels: 0 us -> 56.7 us
  starting transfers between devices: 32.7 us -> 74.5 us
  local copies, waits for them, and re-layouts: 93.5 us -> 77.5 us
    ppermute x0 -> x46, waiting for transfers between devices: none -> 306 us  [swapped(): return lax.ppermute(array, axis, [(i, i ^ mask) for i in range(size)])]
    unnamed x14 -> x3, waiting for transfers between devices: 228 us -> 0.05 us
    all_gather x6 -> x2, waiting for transfers between devices: 188 us -> 0.02 us  [spread_device(): denses.append(lax.all_gather(own, ALL, axis=0, tiled=True))]
    dot_general x12 -> x6, matrix products: 85.6 us -> 25.2 us  [the longest x2 9.18 us: spread_device(): lax.dot_general(qkv, normed_all, (((0,), (1,)), ((), ())), preferred_elem...]
    pallas_call x0 -> x6, Pallas kernels: none -> 56.7 us  [the longest x2 23.4 us: attend_back_rows(): pl.pallas_call(functools.partial(attend_back_kernel, token_rows), grid=(l...]
    reduce_scatter x4 -> x1, waiting for transfers between devices: 64.5 us -> 13.1 us  [spread_device(): lax.psum_scatter(grads, ALL, scatter_dimension=0, tiled=True).astype(F32)]
    all_to_all x4 -> x0, blocking collectives: 49.7 us -> none  [the longest x2 25.8 us: gather_qkv(): lax.all_to_all(sent, 'head', split_axis=0, concat_axis=0, tiled=True)]
    all_gather x1 -> x0, blocking collectives: 43.1 us -> none  [per_device(): lax.all_gather(own_gains.reshape(1, -1), ALL, axis=0, tiled=True)]
  transfers between devices with their start and end apart: 20 -> 57, of which waited for: 17 -> 31; matrix products, arithmetic and copies ran while one was open for 22% -> 18% of each run, Pallas kernels for 0% -> 7%
where the time goes in v3:
time: 696 us; the launch traced here: 691 us
  waiting for transfers between devices  348 us (50%)
  local copies, waits for them, and re-layouts  77.5 us (11%)
  starting transfers between devices  74.5 us (11%)
  other arithmetic  65.2 us (9%)
  Pallas kernels  56.7 us (8%)
  matrix products  53.7 us (8%)
  between operations  15.9 us (2%)
    ppermute x46, waiting for transfers between devices, swapped(): return lax.ppermute(array, axis, [(i, i ^ mask) for i in range(size)])  306 us
    ppermute x46, starting transfers between devices, swapped(): return lax.ppermute(array, axis, [(i, i ^ mask) for i in range(size)])  42.9 us
    all_to_all x8, starting transfers between devices, over_head(): lax.all_to_all(parts, 'head', split_axis=0, concat_axis=0, tiled=True)  31.2 us
    all_to_all x8, waiting for transfers between devices, over_head(): lax.all_to_all(parts, 'head', split_axis=0, concat_axis=0, tiled=True)  29 us
    pallas_call x2, Pallas kernels, attend_back_rows(): pl.pallas_call(functools.partial(attend_back_kernel, token_rows), grid=(l...  23.4 us
    pallas_call x2, Pallas kernels, attend_rows(): pl.pallas_call(functools.partial(attend_kernel, token_rows), grid=(local_...  21.1 us
    unnamed x134, local copies, waits for them, and re-layouts  21.1 us
    unnamed x17, other arithmetic  14.4 us
  transfers between devices with their start and end apart: 57, of which 31 were waited for; matrix products, arithmetic and copies ran while one was open for 18% of the time, Pallas kernels for 7%

profile of v3, /device:TPU:0, one launch (start us, length us, event | category | flops | bytes accessed | tf_op | source)
XLA Modules:
  0.0 691.3 jit_solution(3461302006846007898)
XLA Ops:
  22.0 6.5 all-to-all-done
  36.9 8.2 %collective-permute-done.3 = bf16[160,964]{1,0:T(8,128)(2,1)S(1)} collective-permute-done((bf16[160,964]{1,0:T(8,128)(2,1)}, bf16[160,964]{1,0:T(8,128)(2,1)S(1)}, u32[]{:S(2)}, u32[]{:S(2)}) %collective-permute-start.3) | collective-permute-done | bytes 308512 | tf_op jit(solution)/shard_map/ppermute | solution.py:584
  45.1 33.6 %collective-permute-done.2 = bf16[160,964]{1,0:T(8,128)(2,1)} collective-permute-done((bf16[160,964]{1,0:T(8,128)(2,1)}, bf16[160,964]{1,0:T(8,128)(2,1)}, u32[]{:S(2)}, u32[]{:S(2)}) %collective-permute-start.2) | collective-permute-done | bytes 308512 | tf_op jit(solution)/shard_map/ppermute | solution.py:584
  83.7 8.7 %collective-permute-done.6 = bf16[160,964]{1,0:T(8,128)(2,1)} collective-permute-done((bf16[160,964]{1,0:T(8,128)(2,1)}, bf16[160,964]{1,0:T(8,128)(2,1)}, u32[]{:S(2)}, u32[]{:S(2)}) %collective-permute-start.6) | collective-permute-done | bytes 308512 | tf_op jit(solution)/shard_map/ppermute | solution.py:584
  92.4 13.0 %collective-permute-done.5 = bf16[160,964]{1,0:T(8,128)(2,1)} collective-permute-done((bf16[160,964]{1,0:T(8,128)(2,1)}, bf16[160,964]{1,0:T(8,128)(2,1)}, u32[]{:S(2)}, u32[]{:S(2)}) %collective-permute-start.5) | collective-permute-done | bytes 308512 | tf_op jit(solution)/shard_map/ppermute | solution.py:584
  127.8 10.6 %shard_map.169 = (bf16[4,4,80,256]{3,2,1,0:T(8,128)(2,1)}, f32[4,1,1024]{2,1,0:T(1,128)S(1)}) custom-call(f32[3,4,80,1024]{3,2,1,0:T(8,128)} %fusion.140.proj_ref, f32[80,1]{1,0:T(8,128)S(1)} %copy.69.scale_ref, s32[1024,1]{1,0:T(8,128)S(1)} %copy.70.col_ref, s32[1,1024]{1,0:T(1,128)S(1)} %constant_dynamic-slice_fusion.8.row_ref), custom_call_target="tpu_custom_call" | custom-call | flops 1342177280 | bytes 3932160 | tf_op jit(solution)/shard_map/pallas_call | solution.py:408
  148.8 8.5 %collective-permute-done.13 = bf16[160,960]{1,0:T(8,128)(2,1)S(1)} collective-permute-done((bf16[160,960]{1,0:T(8,128)(2,1)}, bf16[160,960]{1,0:T(8,128)(2,1)S(1)}, u32[]{:S(2)}, u32[]{:S(2)}) %collective-permute-start.13) | collective-permute-done | bytes 307232 | tf_op jit(solution)/shard_map/ppermute | solution.py:584
  157.3 24.7 %collective-permute-done.12 = bf16[160,960]{1,0:T(8,128)(2,1)S(1)} collective-permute-done((bf16[160,960]{1,0:T(8,128)(2,1)}, bf16[160,960]{1,0:T(8,128)(2,1)S(1)}, u32[]{:S(2)}, u32[]{:S(2)}) %collective-permute-start.12) | collective-permute-done | bytes 307232 | tf_op jit(solution)/shard_map/ppermute | solution.py:584
  196.9 35.7 %collective-permute-done.14 = bf16[4,160,960]{2,1,0:T(8,128)(2,1)} collective-permute-done((bf16[4,160,960]{2,1,0:T(8,128)(2,1)}, bf16[4,160,960]{2,1,0:T(8,128)(2,1)}, u32[]{:S(2)}, u32[]{:S(2)}) %collective-permute-start.14) | collective-permute-done | bytes 1228832 | tf_op jit(solution)/shard_map/ppermute | solution.py:584
  262.8 10.5 %shard_map.170 = (bf16[4,4,80,256]{3,2,1,0:T(8,128)(2,1)}, f32[4,1,1024]{2,1,0:T(1,128)S(1)}) custom-call(f32[3,4,80,1024]{3,2,1,0:T(8,128)} %fusion.141.proj_ref, f32[80,1]{1,0:T(8,128)S(1)} %copy.74.scale_ref, s32[1024,1]{1,0:T(8,128)S(1)} %copy.70.col_ref, s32[1,1024]{1,0:T(1,128)S(1)} %constant_dynamic-slice_fusion.8.row_ref), custom_call_target="tpu_custom_call" | custom-call | flops 1342177280 | bytes 3932160 | tf_op jit(solution)/shard_map/pallas_call | solution.py:408
  278.6 9.0 %all-to-all-done.3 = bf16[4,320,256]{2,1,0:T(8,128)(2,1)S(1)} async-done(((bf16[4,320,256]{2,1,0:T(8,128)(2,1)}), bf16[4,320,256]{2,1,0:T(8,128)(2,1)S(1)}, u32[]{:S(2)}, u32[]{:S(2)}) %all-to-all-start.3) | async-done | bytes 655392 | tf_op jit(solution)/shard_map/all_to_all | solution.py:622
  308.8 6.1 shard_map.171
  316.8 11.7 %shard_map.172 = (bf16[3,4,80,1024]{3,2,1,0:T(8,128)(2,1)S(1)}, f32[80,128]{1,0:T(8,128)S(1)}) custom-call(f32[3,4,80,1024]{3,2,1,0:T(8,128)} %fusion.141.proj_ref, bf16[4,4,80,256]{3,2,1,0:T(8,128)(2,1)} %bitcast.71.grad_ref, f32[4,1,1024]{2,1,0:T(1,128)S(1)} %get-tuple-element.32.lse_ref, f32[80,1]{1,0:T(8,128)S(1)} %copy.74.scale_ref, ...), custom_call_target="tpu_custom_call" | custom-call | flops 3355443200 | bytes 5898240 | tf_op jit(solution)/shard_map/pallas_call | solution.py:505
  329.8 5.9 dot_general.90
  335.7 5.4 fusion.79
  352.6 16.1 %collective-permute-done.21 = bf16[2,128,1280]{2,1,0:T(8,128)(2,1)} collective-permute-done((bf16[2,128,1280]{2,1,0:T(8,128)(2,1)}, bf16[2,128,1280]{2,1,0:T(8,128)(2,1)}, u32[]{:S(2)}, u32[]{:S(2)}) %collective-permute-start.21) | collective-permute-done | bytes 655392 | tf_op jit(solution)/shard_map/ppermute | solution.py:584
  390.6 6.1 shard_map.173
  396.7 6.7 constant_dynamic-slice_fusion.3
  425.7 11.7 %shard_map.174 = (bf16[3,4,80,1024]{3,2,1,0:T(8,128)(2,1)S(1)}, f32[80,128]{1,0:T(8,128)S(1)}) custom-call(f32[3,4,80,1024]{3,2,1,0:T(8,128)} %fusion.140.proj_ref, bf16[4,4,80,256]{3,2,1,0:T(8,128)(2,1)S(1)} %bitcast.331, f32[4,1,1024]{2,1,0:T(1,128)S(1)} %get-tuple-element.35.lse_ref, f32[80,1]{1,0:T(8,128)S(1)} %copy.69.scale_ref, ...), custom_call_target="tpu_custom_call" | custom-call | flops 3355443200 | bytes 5898240 | tf_op jit(solution)/shard_map/pallas_call | solution.py:505
  437.8 14.3 %collective-permute-done.30 = bf16[4,160,960]{2,1,0:T(8,128)(2,1)S(1)} collective-permute-done((bf16[4,160,960]{2,1,0:T(8,128)(2,1)S(1)}, bf16[4,160,960]{2,1,0:T(8,128)(2,1)S(1)}, u32[]{:S(2)}, u32[]{:S(2)}) %collective-permute-start.30) | collective-permute-done | bytes 1228832 | tf_op jit(solution)/shard_map/ppermute | solution.py:584
  462.9 5.7 collective-permute-done.31
  471.0 13.9 %collective-permute-done.32 = bf16[160,960]{1,0:T(8,128)(2,1)S(1)} collective-permute-done((bf16[160,960]{1,0:T(8,128)(2,1)S(1)}, bf16[160,960]{1,0:T(8,128)(2,1)S(1)}, u32[]{:S(2)}, u32[]{:S(2)}) %collective-permute-start.32) | collective-permute-done | bytes 307232 | tf_op jit(solution)/shard_map/ppermute | solution.py:584
  490.6 5.4 all-to-all-done.7
  512.0 21.1 %collective-permute-done.34 = bf16[4,2,40,1920]{3,2,0,1:T(8,128)(2,1)S(1)} collective-permute-done((bf16[4,2,40,1920]{3,2,0,1:T(8,128)(2,1)S(1)}, bf16[4,2,40,1920]{3,2,0,1:T(8,128)(2,1)S(1)}, u32[]{:S(2)}, u32[]{:S(2)}) %collective-permute-start.34) | collective-permute-done | bytes 1228832 | tf_op jit(solution)/shard_map/ppermute | solution.py:584
  536.6 33.4 %collective-permute-done.26 = bf16[4,160,960]{2,1,0:T(8,128)(2,1)S(1)} collective-permute-done((bf16[4,160,960]{2,1,0:T(8,128)(2,1)S(1)}, bf16[4,160,960]{2,1,0:T(8,128)(2,1)S(1)}, u32[]{:S(2)}, u32[]{:S(2)}) %collective-permute-start.26) | collective-permute-done | bytes 1228832 | tf_op jit(solution)/shard_map/ppermute | solution.py:584
  574.6 18.1 %collective-permute-done.27 = bf16[160,960]{1,0:T(8,128)(2,1)S(1)} collective-permute-done((bf16[160,960]{1,0:T(8,128)(2,1)S(1)}, bf16[160,960]{1,0:T(8,128)(2,1)S(1)}, u32[]{:S(2)}, u32[]{:S(2)}) %collective-permute-start.27) | collective-permute-done | bytes 307232 | tf_op jit(solution)/shard_map/ppermute | solution.py:584
  592.7 5.3 collective-permute-done.29
  598.0 12.6 %collective-permute-done.28 = bf16[160,960]{1,0:T(8,128)(2,1)S(1)} collective-permute-done((bf16[160,960]{1,0:T(8,128)(2,1)S(1)}, bf16[160,960]{1,0:T(8,128)(2,1)S(1)}, u32[]{:S(2)}, u32[]{:S(2)}) %collective-permute-start.28) | collective-permute-done | bytes 307232 | tf_op jit(solution)/shard_map/ppermute | solution.py:584
  618.8 7.2 %all-to-all-done.6 = bf16[4,40,960]{2,1,0:T(8,128)(2,1)} async-done(((bf16[4,40,960]{2,1,0:T(8,128)(2,1)}), bf16[4,40,960]{2,1,0:T(8,128)(2,1)}, u32[]{:S(2)}, u32[]{:S(2)}) %all-to-all-start.6) | async-done | bytes 307232 | tf_op jit(solution)/shard_map/all_to_all | solution.py:622
  648.6 7.0 %collective-permute-done.38 = bf16[40,3840]{1,0:T(8,128)(2,1)S(1)} collective-permute-done((bf16[40,3840]{1,0:T(8,128)(2,1)S(1)}, bf16[40,3840]{1,0:T(8,128)(2,1)S(1)}, u32[]{:S(2)}, u32[]{:S(2)}) %collective-permute-start.38) | collective-permute-done | bytes 307232 | tf_op jit(solution)/shard_map/ppermute | solution.py:584
  655.6 11.4 %collective-permute-done.39 = bf16[40,3840]{1,0:T(8,128)(2,1)S(1)} collective-permute-done((bf16[40,3840]{1,0:T(8,128)(2,1)S(1)}, bf16[40,3840]{1,0:T(8,128)(2,1)S(1)}, u32[]{:S(2)}, u32[]{:S(2)}) %collective-permute-start.39) | collective-permute-done | bytes 307232 | tf_op jit(solution)/shard_map/ppermute | solution.py:584
  668.4 13.1 %reduce-scatter.2.cloned.1.call-done = bf16[40,3840]{1,0:T(8,128)(2,1)} async-done(((bf16[1280,3840]{1,0:T(8,128)(2,1)}), bf16[40,3840]{1,0:T(8,128)(2,1)}) %reduce-scatter.2.cloned.1.call-update) | async-done | bytes 307216 | tf_op jit(solution)/shard_map/reduce_scatter | solution.py:802
  (387 shorter events, 268.5 us)
Async XLA Ops:
  7.2 178.1 %all-gather.3.cloned.1.call-start = ((), (), s32[]{:S(2)}) async-start(), calls=%async_computation.9 | async-start | bytes 10137600 | tf_op jit(solution)/shard_map/all_gather | solution.py:737
  10.2 268.4 %all-gather.5.cloned.1.call-start = ((), (), s32[]{:S(2)}) async-start(), calls=%async_computation.10 | async-start | bytes 10137600 | tf_op jit(solution)/shard_map/all_gather | solution.py:737
  28.5 109.8 %all-to-all-start.2 = ((bf16[4,40,960]{2,1,0:T(8,128)(2,1)}), bf16[4,40,960]{2,1,0:T(8,128)(2,1)S(1)}, u32[]{:S(2)}, u32[]{:S(2)}) async-start(bf16[4,40,960]{2,1,0:T(8,128)(2,1)} %reshape.273), calls=%async_computation.2 | async-start | bytes 655360 | tf_op jit(solution)/shard_map/all_to_all | solution.py:622
  36.1 42.5 %collective-permute-start.2 = (bf16[160,964]{1,0:T(8,128)(2,1)}, bf16[160,964]{1,0:T(8,128)(2,1)}, u32[]{:S(2)}, u32[]{:S(2)}) collective-permute-start(bf16[160,964]{1,0:T(8,128)(2,1)} %bitcast.8), channel_id=1, source_target_pairs={{0,16},{8,24},{16,0},{24,8},{1,17},{9,25},{17,1},{25,9},{2,18},{10... | collective-permute-start | bytes 925448 | tf_op jit(solution)/shard_map/ppermute | solution.py:584
  36.1 43.0 %collective-permute-start.1 = (bf16[160,964]{1,0:T(8,128)(2,1)}, bf16[160,964]{1,0:T(8,128)(2,1)}, u32[]{:S(2)}, u32[]{:S(2)}) collective-permute-start(bf16[160,964]{1,0:T(8,128)(2,1)} %bitcast.8), channel_id=1, source_target_pairs={{0,8},{8,0},{16,24},{24,16},{1,9},{9,1},{17,25},{25,17},{2,10},{10... | collective-permute-start | bytes 925448 | tf_op jit(solution)/shard_map/ppermute | solution.py:584
  36.8 46.8 %collective-permute-start.4 = (bf16[160,964]{1,0:T(8,128)(2,1)}, bf16[160,964]{1,0:T(8,128)(2,1)}, u32[]{:S(2)}, u32[]{:S(2)}) collective-permute-start(bf16[160,964]{1,0:T(8,128)(2,1)} %bitcast.8), channel_id=1, source_target_pairs={{0,4},{4,0},{1,5},{5,1},{2,6},{6,2},{3,7},{7,3},{8,12},{12,8},{9,1... | collective-permute-start | bytes 925448 | tf_op jit(solution)/shard_map/ppermute | solution.py:584
  45.0 38.6 %collective-permute-start.7 = (bf16[160,964]{1,0:T(8,128)(2,1)S(1)}, bf16[160,964]{1,0:T(8,128)(2,1)}, u32[]{:S(2)}, u32[]{:S(2)}) collective-permute-start(bf16[160,964]{1,0:T(8,128)(2,1)S(1)} %collective-permute-done.3), channel_id=1, source_target_pairs={{0,4},{4,0},{1,5},{5,1},{2,6},{6,2},{3,7},{7,3},{8,12},{12,8},{9,1... | collective-permute-start | bytes 925448 | tf_op jit(solution)/shard_map/ppermute | solution.py:584
  81.1 28.4 %collective-permute-start.9 = (bf16[256,1280]{1,0:T(8,128)(2,1)S(1)}, bf16[256,1280]{1,0:T(8,128)(2,1)}, u32[]{:S(2)}, u32[]{:S(2)}) collective-permute-start(bf16[256,1280]{1,0:T(8,128)(2,1)S(1)} %bitcast.337), channel_id=1, source_target_pairs={{0,2},{1,3},{2,0},{3,1},{4,6},{5,7},{6,4},{7,5},{8,10},{9,11},{10,... | collective-permute-start | bytes 1966088 | tf_op jit(solution)/shard_map/ppermute | solution.py:584
  83.6 34.5 %collective-permute-start.8 = (bf16[256,1280]{1,0:T(8,128)(2,1)S(1)}, bf16[256,1280]{1,0:T(8,128)(2,1)}, u32[]{:S(2)}, u32[]{:S(2)}) collective-permute-start(bf16[256,1280]{1,0:T(8,128)(2,1)S(1)} %bitcast.338), channel_id=1, source_target_pairs={{0,1},{1,0},{2,3},{3,2},{4,5},{5,4},{6,7},{7,6},{8,9},{9,8},{10,11... | collective-permute-start | bytes 1966088 | tf_op jit(solution)/shard_map/ppermute | solution.py:584
  139.1 46.2 %all-to-all-start.1 = ((bf16[4,320,256]{2,1,0:T(8,128)(2,1)}), bf16[4,320,256]{2,1,0:T(8,128)(2,1)S(1)}, u32[]{:S(2)}, u32[]{:S(2)}) async-start(bf16[4,320,256]{2,1,0:T(8,128)(2,1)} %bitcast.31), calls=%async_computation.1 | async-start | bytes 1310720 | tf_op jit(solution)/shard_map/all_to_all | solution.py:622
  143.9 38.1 %collective-permute-start.12 = (bf16[160,960]{1,0:T(8,128)(2,1)}, bf16[160,960]{1,0:T(8,128)(2,1)S(1)}, u32[]{:S(2)}, u32[]{:S(2)}) collective-permute-start(bf16[160,960]{1,0:T(8,128)(2,1)} %bitcast.365), channel_id=1, source_target_pairs={{0,16},{8,24},{16,0},{24,8},{1,17},{9,25},{17,1},{25,9},{2,18},{10... | collective-permute-start | bytes 921608 | tf_op jit(solution)/shard_map/ppermute | solution.py:584
  143.9 38.1 %collective-permute-start.11 = (bf16[160,960]{1,0:T(8,128)(2,1)}, bf16[160,960]{1,0:T(8,128)(2,1)}, u32[]{:S(2)}, u32[]{:S(2)}) collective-permute-start(bf16[160,960]{1,0:T(8,128)(2,1)} %bitcast.366), channel_id=1, source_target_pairs={{0,8},{8,0},{16,24},{24,16},{1,9},{9,1},{17,25},{25,17},{2,10},{10... | collective-permute-start | bytes 921608 | tf_op jit(solution)/shard_map/ppermute | solution.py:584
  148.0 129.3 %collective-permute-start.19 = (bf16[128,1280]{1,0:T(8,128)(2,1)}, bf16[128,1280]{1,0:T(8,128)(2,1)}, u32[]{:S(2)}, u32[]{:S(2)}) collective-permute-start(bf16[128,1280]{1,0:T(8,128)(2,1)} %dynamic-slice_bitcast_fusion.5), channel_id=1, source_target_pairs={{0,4},{4,0},{1,5},{5,1},{2,6},{6,2},{3,7},{7,3},{8,12},{12,8},{9,1... | collective-permute-start | bytes 983048 | tf_op jit(solution)/shard_map/ppermute | solution.py:584
  184.3 48.3 %collective-permute-start.14 = (bf16[4,160,960]{2,1,0:T(8,128)(2,1)}, bf16[4,160,960]{2,1,0:T(8,128)(2,1)}, u32[]{:S(2)}, u32[]{:S(2)}) collective-permute-start(bf16[4,160,960]{2,1,0:T(8,128)(2,1)} %pad_maximum_fusion.6), channel_id=1, source_target_pairs={{0,4},{4,0},{1,5},{5,1},{2,6},{6,2},{3,7},{7,3},{8,12},{12,8},{9,1... | collective-permute-start | bytes 3686408 | tf_op jit(solution)/shard_map/ppermute | solution.py:584
  195.0 49.4 %collective-permute-start.16 = (bf16[256,1280]{1,0:T(8,128)(2,1)}, bf16[256,1280]{1,0:T(8,128)(2,1)}, u32[]{:S(2)}, u32[]{:S(2)}) collective-permute-start(bf16[256,1280]{1,0:T(8,128)(2,1)} %multiply_convert_fusion.2), channel_id=1, source_target_pairs={{0,2},{1,3},{2,0},{3,1},{4,6},{5,7},{6,4},{7,5},{8,10},{9,11},{10,... | collective-permute-start | bytes 1966088 | tf_op jit(solution)/shard_map/ppermute | solution.py:584
  406.1 91.2 %collective-permute-start.22 = (bf16[4,2,2,40,3840]{4,3,0,1,2:T(8,128)(2,1)}, bf16[4,2,2,40,3840]{4,3,0,1,2:T(8,128)(2,1)}, u32[]{:S(2)}, u32[]{:S(2)}) collective-permute-start(bf16[4,2,2,40,3840]{4,3,0,1,2:T(8,128)(2,1)} %bitcast.320), channel_id=1, source_target_pairs={{0,1},{1,0},{2,3},{3,2},{4,5},{5,4},{6,7},{7,6},{8,9},{9,8},{10,11... | collective-permute-start | bytes 14745608 | tf_op jit(solution)/shard_map/ppermute | solution.py:584
  420.4 31.6 %collective-permute-start.30 = (bf16[4,160,960]{2,1,0:T(8,128)(2,1)S(1)}, bf16[4,160,960]{2,1,0:T(8,128)(2,1)S(1)}, u32[]{:S(2)}, u32[]{:S(2)}) collective-permute-start(bf16[4,160,960]{2,1,0:T(8,128)(2,1)S(1)} %fusion.91), channel_id=1, source_target_pairs={{0,4},{4,0},{1,5},{5,1},{2,6},{6,2},{3,7},{7,3},{8,12},{12,8},{9,1... | collective-permute-start | bytes 3686408 | tf_op jit(solution)/shard_map/ppermute | solution.py:584
  424.7 33.9 %collective-permute-start.18 = (bf16[128,1280]{1,0:T(8,128)(2,1)S(1)}, bf16[128,1280]{1,0:T(8,128)(2,1)S(1)}, u32[]{:S(2)}, u32[]{:S(2)}) collective-permute-start(bf16[128,1280]{1,0:T(8,128)(2,1)S(1)} %dynamic-slice_bitcast_fusion.6), channel_id=1, source_target_pairs={{0,4},{4,0},{1,5},{5,1},{2,6},{6,2},{3,7},{7,3},{8,12},{12,8},{9,1... | collective-permute-start | bytes 983048 | tf_op jit(solution)/shard_map/ppermute | solution.py:584
  456.1 28.8 %collective-permute-start.32 = (bf16[160,960]{1,0:T(8,128)(2,1)S(1)}, bf16[160,960]{1,0:T(8,128)(2,1)S(1)}, u32[]{:S(2)}, u32[]{:S(2)}) collective-permute-start(bf16[160,960]{1,0:T(8,128)(2,1)S(1)} %get-tuple-element.66), channel_id=1, source_target_pairs={{0,16},{8,24},{16,0},{24,8},{1,17},{9,25},{17,1},{25,9},{2,18},{10... | collective-permute-start | bytes 921608 | tf_op jit(solution)/shard_map/ppermute | solution.py:584
  462.2 27.4 %collective-permute-start.44 = (f32[2,80]{1,0:T(2,128)S(1)}, f32[2,80]{1,0:T(2,128)S(1)}, u32[]{:S(2)}, u32[]{:S(2)}) collective-permute-start(f32[2,80]{1,0:T(2,128)S(1)} %add.342), channel_id=1, source_target_pairs={{0,8},{8,0},{16,24},{24,16},{1,9},{9,1},{17,25},{25,17},{2,10},{10... | collective-permute-start | bytes 1928 | tf_op jit(solution)/shard_map/ppermute | solution.py:584
  489.3 192.2 %reduce-scatter.2.cloned.1.call-start = ((), (), s32[]{:S(2)}) async-start(), calls=%async_computation.11 | async-start | bytes 10137600 | tf_op jit(solution)/shard_map/reduce_scatter | solution.py:802
  503.1 30.0 %collective-permute-start.34 = (bf16[4,2,40,1920]{3,2,0,1:T(8,128)(2,1)S(1)}, bf16[4,2,40,1920]{3,2,0,1:T(8,128)(2,1)S(1)}, u32[]{:S(2)}, u32[]{:S(2)}) collective-permute-start(bf16[4,2,40,1920]{3,2,0,1:T(8,128)(2,1)S(1)} %dynamic-slice_bitcast_fusion.1), channel_id=1, source_target_pairs={{0,4},{4,0},{1,5},{5,1},{2,6},{6,2},{3,7},{7,3},{8,12},{12,8},{9,1... | collective-permute-start | bytes 3686408 | tf_op jit(solution)/shard_map/ppermute | solution.py:584
  503.8 30.7 %collective-permute-start.36 = (bf16[4,2,40,1920]{3,2,0,1:T(8,128)(2,1)S(1)}, bf16[4,2,40,1920]{3,2,0,1:T(8,128)(2,1)S(1)}, u32[]{:S(2)}, u32[]{:S(2)}) collective-permute-start(bf16[4,2,40,1920]{3,2,0,1:T(8,128)(2,1)S(1)} %dynamic-slice_bitcast_fusion), channel_id=1, source_target_pairs={{0,2},{1,3},{2,0},{3,1},{4,6},{5,7},{6,4},{7,5},{8,10},{9,11},{10,... | collective-permute-start | bytes 3686408 | tf_op jit(solution)/shard_map/ppermute | solution.py:584
  511.1 58.9 %collective-permute-start.26 = (bf16[4,160,960]{2,1,0:T(8,128)(2,1)S(1)}, bf16[4,160,960]{2,1,0:T(8,128)(2,1)S(1)}, u32[]{:S(2)}, u32[]{:S(2)}) collective-permute-start(bf16[4,160,960]{2,1,0:T(8,128)(2,1)S(1)} %fusion.90), channel_id=1, source_target_pairs={{0,4},{4,0},{1,5},{5,1},{2,6},{6,2},{3,7},{7,3},{8,12},{12,8},{9,1... | collective-permute-start | bytes 3686408 | tf_op jit(solution)/shard_map/ppermute | solution.py:584
  511.9 59.9 %collective-permute-start.23 = (bf16[2,2,128,1280]{3,2,0,1:T(8,128)(2,1)S(1)}, bf16[2,2,128,1280]{3,2,0,1:T(8,128)(2,1)S(1)}, u32[]{:S(2)}, u32[]{:S(2)}) collective-permute-start(bf16[2,2,128,1280]{3,2,0,1:T(8,128)(2,1)S(1)} %fusion.92), channel_id=1, source_target_pairs={{0,1},{1,0},{2,3},{3,2},{4,5},{5,4},{6,7},{7,6},{8,9},{9,8},{10,11... | collective-permute-start | bytes 3932168 | tf_op jit(solution)/shard_map/ppermute | solution.py:584
  534.4 100.6 %collective-permute-start.35 = (bf16[4,40,1920]{2,1,0:T(8,128)(2,1)}, bf16[4,40,1920]{2,1,0:T(8,128)(2,1)}, u32[]{:S(2)}, u32[]{:S(2)}) collective-permute-start(bf16[4,40,1920]{2,1,0:T(8,128)(2,1)} %dynamic-slice_bitcast_fusion.3), channel_id=1, source_target_pairs={{0,2},{1,3},{2,0},{3,1},{4,6},{5,7},{6,4},{7,5},{8,10},{9,11},{10,... | collective-permute-start | bytes 1843208 | tf_op jit(solution)/shard_map/ppermute | solution.py:584
  535.8 100.5 %collective-permute-start.37 = (bf16[4,40,1920]{2,1,0:T(8,128)(2,1)}, bf16[4,40,1920]{2,1,0:T(8,128)(2,1)}, u32[]{:S(2)}, u32[]{:S(2)}) collective-permute-start(bf16[4,40,1920]{2,1,0:T(8,128)(2,1)} %dynamic-slice_bitcast_fusion.2), channel_id=1, source_target_pairs={{0,4},{4,0},{1,5},{5,1},{2,6},{6,2},{3,7},{7,3},{8,12},{12,8},{9,1... | collective-permute-start | bytes 1843208 | tf_op jit(solution)/shard_map/ppermute | solution.py:584
  570.8 27.1 %collective-permute-start.29 = (bf16[160,960]{1,0:T(8,128)(2,1)S(1)}, bf16[160,960]{1,0:T(8,128)(2,1)S(1)}, u32[]{:S(2)}, u32[]{:S(2)}) collective-permute-start(bf16[160,960]{1,0:T(8,128)(2,1)S(1)} %get-tuple-element.62), channel_id=1, source_target_pairs={{0,24},{8,16},{16,8},{24,0},{1,25},{9,17},{17,9},{25,1},{2,26},{10... | collective-permute-start | bytes 921608 | tf_op jit(solution)/shard_map/ppermute | solution.py:584
  571.8 38.7 %collective-permute-start.28 = (bf16[160,960]{1,0:T(8,128)(2,1)S(1)}, bf16[160,960]{1,0:T(8,128)(2,1)S(1)}, u32[]{:S(2)}, u32[]{:S(2)}) collective-permute-start(bf16[160,960]{1,0:T(8,128)(2,1)S(1)} %get-tuple-element.63), channel_id=1, source_target_pairs={{0,16},{8,24},{16,0},{24,8},{1,17},{9,25},{17,1},{25,9},{2,18},{10... | collective-permute-start | bytes 921608 | tf_op jit(solution)/shard_map/ppermute | solution.py:584
  616.8 28.7 %collective-permute-start.24 = (bf16[2,128,1280]{2,1,0:T(8,128)(2,1)}, bf16[2,128,1280]{2,1,0:T(8,128)(2,1)}, u32[]{:S(2)}, u32[]{:S(2)}) collective-permute-start(bf16[2,128,1280]{2,1,0:T(8,128)(2,1)} %fusion.96), channel_id=1, source_target_pairs={{0,2},{1,3},{2,0},{3,1},{4,6},{5,7},{6,4},{7,5},{8,10},{9,11},{10,... | collective-permute-start | bytes 1966088 | tf_op jit(solution)/shard_map/ppermute | solution.py:584
  637.7 29.3 %collective-permute-start.39 = (bf16[40,3840]{1,0:T(8,128)(2,1)S(1)}, bf16[40,3840]{1,0:T(8,128)(2,1)S(1)}, u32[]{:S(2)}, u32[]{:S(2)}) collective-permute-start(bf16[40,3840]{1,0:T(8,128)(2,1)S(1)} %get-tuple-element.80), channel_id=1, source_target_pairs={{0,16},{8,24},{16,0},{24,8},{1,17},{9,25},{17,1},{25,9},{2,18},{10... | collective-permute-start | bytes 921608 | tf_op jit(solution)/shard_map/ppermute | solution.py:584
  637.8 29.2 %collective-permute-start.40 = (bf16[40,3840]{1,0:T(8,128)(2,1)S(1)}, bf16[40,3840]{1,0:T(8,128)(2,1)S(1)}, u32[]{:S(2)}, u32[]{:S(2)}) collective-permute-start(bf16[40,3840]{1,0:T(8,128)(2,1)S(1)} %get-tuple-element.81), channel_id=1, source_target_pairs={{0,24},{8,16},{16,8},{24,0},{1,25},{9,17},{17,9},{25,1},{2,26},{10... | collective-permute-start | bytes 921608 | tf_op jit(solution)/shard_map/ppermute | solution.py:584
  (92 other events, 1101.1 us)
Sparse Core Ops, SparseCore 0:
  11.5 114.9 all-gather.2
  130.0 112.0 all-gather.4
  496.1 185.3 reduce-scatter.1

commit v4 on v3

--- a/solution.py
+++ b/solution.py
@@ -360,6 +360,7 @@
 
 Q_ROWS = 256
 KERNEL = pltpu.CompilerParams(vmem_limit_bytes=50 * 1024 * 1024)
+LIGHT = pl.CostEstimate(flops=1 << 20, bytes_accessed=1 << 20, transcendentals=0)
 
 
 def allowed_keys(col, row, first):
@@ -423,11 +424,7 @@
             jax.ShapeDtypeStruct((local_heads, 1, length), F32),
         ],
         compiler_params=KERNEL,
-        cost_estimate=pl.CostEstimate(
-            flops=4 * local_heads * length * length * head_dim,
-            bytes_accessed=projected.size * 4,
-            transcendentals=local_heads * length * length // 2,
-        ),
+        cost_estimate=LIGHT,
     )(
         projected.reshape(3, local_heads, head_dim, length),
         scale_vec.reshape(head_dim, 1),
@@ -526,11 +523,7 @@
             pltpu.VMEM((head_dim, length), F32),
         ],
         compiler_params=KERNEL,
-        cost_estimate=pl.CostEstimate(
-            flops=10 * local_heads * length * length * head_dim,
-            bytes_accessed=projected.size * 6,
-            transcendentals=local_heads * length * length // 2,
-        ),
+        cost_estimate=LIGHT,
     )(
         projected.reshape(3, local_heads, head_dim, length),
         attended_grad.reshape(owners, local_heads, head_dim, tokens),
@@ -569,9 +562,7 @@
         out_specs=pl.BlockSpec((tile, 3 * width), lambda i: (i, 0)),
         out_shape=jax.ShapeDtypeStruct((width, 3 * width), BF16),
         compiler_params=KERNEL,
-        cost_estimate=pl.CostEstimate(
-            flops=6 * tokens * width * width, bytes_accessed=6 * width * width, transcendentals=0
-        ),
+        cost_estimate=LIGHT,
     )(attended_t, normed, active, out_bar, up_bar, down_bar)
 
 
@@ -631,41 +622,36 @@
     return over_head(sent)
 
 
-def gather_columns(piece, early):
-    along = [piece] + [swapped(piece, "batch", mask) for mask in (1, 2, 3)]
-    if early:
-        across = jnp.stack([swapped(part, "blk", 1) for part in along])
-        along = jnp.stack(along)
-    else:
-        along = jnp.stack(along)
-        across = swapped(along, "blk", 1)
+def along_batch(piece):
+    return [piece] + [swapped(piece, "batch", mask) for mask in (1, 2, 3)]
+
+
+def in_rows(along, across):
     me, blk = lax.axis_index("batch"), lax.axis_index("blk")
     ordered = []
     for i in range(4):
         one, two = pick(along, me ^ i), pick(across, me ^ i)
         ordered += [jnp.where(blk == 0, one, two), jnp.where(blk == 0, two, one)]
-    return jnp.stack(ordered).reshape(-1, piece.shape[-1])
-
-
-def scatter_over_batch(parts):
+    return jnp.stack(ordered).reshape(-1, along.shape[-1])
+
+
+def columns_over_blk(grad):
+    blk = lax.axis_index("blk")
+    parts = grad.reshape(4, 2, -1, grad.shape[1])
+    return pick(parts, blk, 1), swapped(pick(parts, 1 - blk, 1).astype(BF16), "blk", 1)
+
+
+def sent_over_batch(parts):
     me = lax.axis_index("batch")
-    total = pick(parts, me).astype(F32)
-    for mask in (1, 2, 3):
-        total = total + swapped(pick(parts, me ^ mask).astype(BF16), "batch", mask).astype(F32)
-    return total
-
-
-def scatter_columns(grad):
-    blk = lax.axis_index("blk")
-    columns = grad.shape[1]
-    parts = grad.reshape(4, 2, -1, columns)
-    summed = pick(parts, blk, 1) + swapped(
-        pick(parts, 1 - blk, 1).astype(BF16), "blk", 1
-    ).astype(F32)
-    summed = scatter_over_batch(summed).astype(BF16)
-    moved = over_head(summed.reshape(4, -1, columns))
-    own = moved.shape[1]
-    return moved.reshape(4, own, 3, -1).transpose(1, 2, 0, 3).reshape(own, -1).astype(F32)
+    sent = [swapped(pick(parts, me ^ mask).astype(BF16), "batch", mask) for mask in (1, 2, 3)]
+    return pick(parts, me).astype(F32), jnp.stack(sent)
+
+
+def columns_to_rows(own, sent):
+    summed = (own + jnp.sum(sent.astype(F32), axis=0)).astype(BF16)
+    moved = over_head(summed.reshape(4, -1, summed.shape[-1]))
+    rows = moved.shape[1]
+    return moved.reshape(4, rows, 3, -1).transpose(1, 2, 0, 3).reshape(rows, -1).astype(F32)
 
 
 def over_core(grad):
@@ -675,19 +661,25 @@
     return (pick(parts, core, 3).astype(F32) + got).astype(BF16)
 
 
-def over_chips(cored):
+def over_one(part, axis, mask, mine, dim):
+    got = swapped(pick(part, 1 - mine, dim), axis, mask).astype(F32)
+    return (pick(part, mine, dim).astype(F32) + got).astype(BF16)
+
+
+def over_chips_first(cored):
     row, blk = lax.axis_index("head") // 2, lax.axis_index("blk")
     half = cored.shape[-1] // 2
-
-    def over(part, axis, mask, mine, dim):
-        got = swapped(pick(part, 1 - mine, dim), axis, mask).astype(F32)
-        return (pick(part, mine, dim).astype(F32) + got).astype(BF16)
-
-    first = over(cored[..., :half], "blk", 1, blk, 1)
-    second = over(cored[..., half:], "head", 2, row, 2)
-    first = over(first, "head", 2, row, 1)
-    second = over(second, "blk", 1, blk, 1)
-    return scatter_over_batch(jnp.concatenate([first, second], axis=-1))
+    return (
+        over_one(cored[..., :half], "blk", 1, blk, 1),
+        over_one(cored[..., half:], "head", 2, row, 2),
+    )
+
+
+def over_chips_second(first, second):
+    row, blk = lax.axis_index("head") // 2, lax.axis_index("blk")
+    first = over_one(first, "head", 2, row, 1)
+    second = over_one(second, "blk", 1, blk, 1)
+    return jnp.concatenate([first, second], axis=-1)
 
 
 def sum_all(array):
@@ -727,21 +719,22 @@
     columns[0], first = tied(columns[0], first)
     first_all = gather_rows(first)
     stream = first.astype(F32)
-    with_gains = gather_columns(columns[0].reshape(-1, columns[0].shape[-1]), True)
+    along = along_batch(columns[0].reshape(-1, columns[0].shape[-1]))
+    across = jnp.stack([swapped(part, "blk", 1) for part in along])
+    along = jnp.stack(along)
+    with_gains = in_rows(along, across)
     part3 = 3 * width // 4
     qkvs = [with_gains[:, :part3]]
     gains = with_gains[:, part3:].T.astype(F32)
-    denses = []
-    for layer in range(layers):
-        own = jnp.concatenate([out_weight[layer], up_weight[layer], down_weight[layer]], axis=1)
-        denses.append(lax.all_gather(own, ALL, axis=0, tiled=True))
+    own = [w[layer] for layer in range(layers) for w in (out_weight, up_weight, down_weight)]
+    dense_whole = lax.all_gather(jnp.concatenate(own, axis=1), ALL, axis=0, tiled=True)
+    denses = [dense_whole[:, 3 * width * i : 3 * width * (i + 1)] for i in range(layers)]
+    next_piece = qkv_columns(qkv_weight[1], None).reshape(-1, part3)
+    next_piece, _ = tied(next_piece, along)
+    next_along = jnp.stack(along_batch(next_piece))
 
     kept = []
     for layer in range(layers):
-        if layer > 0:
-            piece = qkv_columns(qkv_weight[layer], None)
-            piece, _ = tied(piece.reshape(-1, part3), qkvs[layer - 1])
-            qkvs.append(gather_columns(piece, False))
         qkv, dense = qkvs[layer], denses[layer]
         out_w, up_w, down_w = dense[:, :width], dense[:, width:-width], dense[:, -width:]
         normed, factor_one = normalize(stream, gains[layer])
@@ -755,8 +748,14 @@
         attended, log_total = attend_rows(
             projected, scale_vecs[layer], segments, 4, token_rows
         )
+        if layer == 0:
+            attended, next_along = tied(attended, next_along)
+            next_across = swapped(next_along, "blk", 1)
         attended_t = over_head(attended).reshape(width, -1)
         middle = stream + dot_rows(attended_t, out_w)
+        if layer == 0:
+            middle, next_across = tied(middle, next_across)
+            qkvs.append(in_rows(next_along, next_across))
         normed_two, factor_two = normalize(middle, gains[layers + layer])
         normed_two = normed_two.astype(BF16)
         hidden = dot(normed_two, up_w)
@@ -790,29 +789,37 @@
         out_bar = middle_grad.astype(BF16)
         attended_grad = over_head(dot_cols(out_w, out_bar).astype(BF16).reshape(4, -1, out_bar.shape[0]))
         grads = dense_grads(attended_t, normed_two, active, out_bar, up_bar, down_bar)
-        attended_grad, grads = tied(attended_grad, grads)
-        cored = over_core(grads) if layer == 0 else None
+        if layer == 0:
+            attended_grad, grads, later = tied(attended_grad, grads, later)
+            own, sent = sent_over_batch(later[0] + later[1].astype(F32))
+            cored = over_core(grads)
+        else:
+            attended_grad, grads = tied(attended_grad, grads)
         bars, scale_grads[layer] = attend_back_rows(
             projected, attended_grad, log_total, scale_vecs[layer], segments, token_rows
         )
         if layer == 0:
-            bars, cored = tied(bars, cored)
-            dense_own[layer] = over_chips(cored)
-        else:
-            dense_own[layer] = lax.psum_scatter(
-                grads, ALL, scatter_dimension=0, tiled=True
-            ).astype(F32)
+            bars, cored, sent = tied(bars, cored, sent)
+            qkv_grads[1] = columns_to_rows(own, sent)
+            halves = over_chips_first(cored)
         normed_grad = scatter_rows(
             lax.dot_general(bars, qkv, (((0,), (1,)), ((), ())), preferred_element_type=F32)
         )
-        qkv_grads[layer] = scatter_columns(
+        later = columns_over_blk(
             lax.dot_general(normed_all, bars, (((0,), (1,)), ((), ())), preferred_element_type=F32)
         )
+        if layer == 0:
+            normed_grad, halves, dense_own[1] = tied(normed_grad, halves, dense_own[1])
+            own, sent = sent_over_batch(over_chips_second(*halves))
+            dense_own[0] = own + jnp.sum(sent.astype(F32), axis=0)
+            qkv_grads[0] = columns_to_rows(*sent_over_batch(later[0] + later[1].astype(F32)))
+        else:
+            dense_own[1] = lax.psum_scatter(grads, ALL, scatter_dimension=0, tiled=True)
         upper = middle_grad + lower_of(normed_grad, stream, factor_one, gains[layer])
     input_grad = swap_halves(upper.astype(BF16).reshape(tokens.shape)).astype(F32)
     scale_total = sum_all(jnp.stack(scale_grads))
     scale_grad = scale_total * (SCALE_BASE / math.sqrt(head_dim)) * jax.nn.sigmoid(scale_param)
-    dense_all = jnp.stack(dense_own)
+    dense_all = jnp.stack([part.astype(F32) for part in dense_own])
     qkv_all = jnp.stack(qkv_grads)
     up_all = dense_all[:, :, width:-width]
     return (
@@ -835,6 +842,7 @@
     spread = (
         sizes == (4, 2, 4)
         and tokens.shape[0] == 2
+        and args[2].shape[0] == 2
         and tokens.shape[1] % 128 == 0
         and Q_ROWS % tokens.shape[1] == 0
         and segments.shape[1] <= WINDOW

time: 696 us -> 680 us (0.977)
  waiting for transfers between devices: 348 us -> 299 us
  matrix products: 53.7 us -> 67.7 us
  local copies, waits for them, and re-layouts: 77.5 us -> 91.2 us
    ppermute x46, waiting for transfers between devices: 306 us -> 273 us  [swapped(): return lax.ppermute(array, axis, [(i, i ^ mask) for i in range(size)])]
    reduce_scatter x1, waiting for transfers between devices: 13.1 us -> 0.02 us  [spread_device(): dense_own[1] = lax.psum_scatter(grads, ALL, scatter_dimension=0, tiled=True)]
    dot_general x6, matrix products: 10.8 us -> 20.8 us  [dot_cols(): lax.dot_general(left, right, (((1,), (1,)), ((), ())), preferred_element_...]
    ppermute x46, starting transfers between devices: 42.9 us -> 50 us  [swapped(): return lax.ppermute(array, axis, [(i, i ^ mask) for i in range(size)])]
    unnamed x17 -> x15, other arithmetic: 14.4 us -> 8.36 us
    unnamed x134 -> x161, local copies, waits for them, and re-layouts: 21.1 us -> 26.4 us
  transfers between devices with their start and end apart: 57 -> 56, of which waited for: 31 -> 30; matrix products, arithmetic and copies ran while one was open for 18% -> 21% of each run, Pallas kernels for 7% -> 7%
where the time goes in v4:
time: 680 us; the launch traced here: 672 us
  waiting for transfers between devices  299 us (44%)
  local copies, waits for them, and re-layouts  91.2 us (13%)
  starting transfers between devices  79.9 us (12%)
  matrix products  67.7 us (10%)
  other arithmetic  61 us (9%)
  Pallas kernels  57 us (8%)
  between operations  16.1 us (2%)
    ppermute x46, waiting for transfers between devices, swapped(): return lax.ppermute(array, axis, [(i, i ^ mask) for i in range(size)])  273 us
    ppermute x46, starting transfers between devices, swapped(): return lax.ppermute(array, axis, [(i, i ^ mask) for i in range(size)])  50 us
    all_to_all x8, starting transfers between devices, over_head(): lax.all_to_all(parts, 'head', split_axis=0, concat_axis=0, tiled=True)  29.9 us
    all_to_all x8, waiting for transfers between devices, over_head(): lax.all_to_all(parts, 'head', split_axis=0, concat_axis=0, tiled=True)  26.5 us
    unnamed x161, local copies, waits for them, and re-layouts  26.4 us
    pallas_call x2, Pallas kernels, attend_back_rows(): pl.pallas_call(functools.partial(attend_back_kernel, token_rows), grid=(l...  23.7 us
    pallas_call x2, Pallas kernels, attend_rows(): pl.pallas_call(functools.partial(attend_kernel, token_rows), grid=(local_...  21 us
    dot_general x6, matrix products, dot_cols(): lax.dot_general(left, right, (((1,), (1,)), ((), ())), preferred_element_...  20.8 us
  transfers between devices with their start and end apart: 56, of which 30 were waited for; matrix products, arithmetic and copies ran while one was open for 21% of the time, Pallas kernels for 7%

profile of v4, /device:TPU:0, one launch (start us, length us, event | category | flops | bytes accessed | tf_op | source)
XLA Modules:
  0.0 672.4 jit_solution(4877230323161733778)
XLA Ops:
  24.5 5.4 all-to-all-done
  39.7 9.3 %collective-permute-done.3 = bf16[160,964]{1,0:T(8,128)(2,1)} collective-permute-done((bf16[160,964]{1,0:T(8,128)(2,1)S(1)}, bf16[160,964]{1,0:T(8,128)(2,1)}, u32[]{:S(2)}, u32[]{:S(2)}) %collective-permute-start.3) | collective-permute-done | bytes 308512 | tf_op jit(solution)/shard_map/ppermute | solution.py:575
  49.1 23.5 %collective-permute-done.2 = bf16[160,964]{1,0:T(8,128)(2,1)} collective-permute-done((bf16[160,964]{1,0:T(8,128)(2,1)S(1)}, bf16[160,964]{1,0:T(8,128)(2,1)}, u32[]{:S(2)}, u32[]{:S(2)}) %collective-permute-start.2) | collective-permute-done | bytes 308512 | tf_op jit(solution)/shard_map/ppermute | solution.py:575
  81.5 12.9 %collective-permute-done.13 = bf16[160,960]{1,0:T(8,128)(2,1)S(1)} collective-permute-done((bf16[160,960]{1,0:T(8,128)(2,1)S(1)}, bf16[160,960]{1,0:T(8,128)(2,1)S(1)}, u32[]{:S(2)}, u32[]{:S(2)}) %collective-permute-start.13) | collective-permute-done | bytes 307232 | tf_op jit(solution)/shard_map/ppermute | solution.py:575
  95.6 29.4 %collective-permute-done.12 = bf16[160,960]{1,0:T(8,128)(2,1)S(1)} collective-permute-done((bf16[160,960]{1,0:T(8,128)(2,1)S(1)}, bf16[160,960]{1,0:T(8,128)(2,1)S(1)}, u32[]{:S(2)}, u32[]{:S(2)}) %collective-permute-start.12) | collective-permute-done | bytes 307232 | tf_op jit(solution)/shard_map/ppermute | solution.py:575
  130.4 11.0 %collective-permute-done.5 = bf16[160,964]{1,0:T(8,128)(2,1)} collective-permute-done((bf16[160,964]{1,0:T(8,128)(2,1)}, bf16[160,964]{1,0:T(8,128)(2,1)}, u32[]{:S(2)}, u32[]{:S(2)}) %collective-permute-start.5) | collective-permute-done | bytes 308512 | tf_op jit(solution)/shard_map/ppermute | solution.py:575
  143.8 14.2 %collective-permute-done.9 = bf16[256,1280]{1,0:T(8,128)(2,1)} collective-permute-done((bf16[256,1280]{1,0:T(8,128)(2,1)S(1)}, bf16[256,1280]{1,0:T(8,128)(2,1)}, u32[]{:S(2)}, u32[]{:S(2)}) %collective-permute-start.9) | collective-permute-done | bytes 655392 | tf_op jit(solution)/shard_map/ppermute | solution.py:575
  171.8 4.7 fusion.130.proj_ref
  176.5 10.5 %shard_map.169 = (bf16[4,4,80,256]{3,2,1,0:T(8,128)(2,1)}, f32[4,1,1024]{2,1,0:T(1,128)S(1)}) custom-call(f32[3,4,80,1024]{3,2,1,0:T(8,128)} %fusion.130.proj_ref, f32[80,1]{1,0:T(8,128)S(1)} %copy.67.scale_ref, s32[1024,1]{1,0:T(8,128)S(1)} %copy.68.col_ref, s32[1,1024]{1,0:T(1,128)S(1)} %constant_dynamic-slice_fusion.10.row_ref), custom_call_target="tpu_custom_call" | custom-call | flops 1048576 | bytes 1048576 | tf_op jit(solution)/shard_map/pallas_call | solution.py:409
  194.6 6.4 all-to-all-done.2
  204.2 14.5 %collective-permute-done.14 = bf16[4,160,960]{2,1,0:T(8,128)(2,1)} collective-permute-done((bf16[4,160,960]{2,1,0:T(8,128)(2,1)S(1)}, bf16[4,160,960]{2,1,0:T(8,128)(2,1)}, u32[]{:S(2)}, u32[]{:S(2)}) %collective-permute-start.14) | collective-permute-done | bytes 1228832 | tf_op jit(solution)/shard_map/ppermute | solution.py:575
  235.6 9.3 %collective-permute-done.16 = bf16[256,1280]{1,0:T(8,128)(2,1)} collective-permute-done((bf16[256,1280]{1,0:T(8,128)(2,1)}, bf16[256,1280]{1,0:T(8,128)(2,1)}, u32[]{:S(2)}, u32[]{:S(2)}) %collective-permute-start.16) | collective-permute-done | bytes 655392 | tf_op jit(solution)/shard_map/ppermute | solution.py:575
  262.6 10.5 %shard_map.170 = (bf16[4,4,80,256]{3,2,1,0:T(8,128)(2,1)}, f32[4,1,1024]{2,1,0:T(1,128)S(1)}) custom-call(f32[3,4,80,1024]{3,2,1,0:T(8,128)} %fusion.131.proj_ref, f32[80,1]{1,0:T(8,128)S(1)} %copy.72.scale_ref, s32[1024,1]{1,0:T(8,128)S(1)} %copy.68.col_ref, s32[1,1024]{1,0:T(1,128)S(1)} %constant_dynamic-slice_fusion.10.row_ref), custom_call_target="tpu_custom_call" | custom-call | flops 1048576 | bytes 1048576 | tf_op jit(solution)/shard_map/pallas_call | solution.py:409
  278.0 9.1 %all-to-all-done.3 = bf16[4,320,256]{2,1,0:T(8,128)(2,1)S(1)} async-done(((bf16[4,320,256]{2,1,0:T(8,128)(2,1)}), bf16[4,320,256]{2,1,0:T(8,128)(2,1)S(1)}, u32[]{:S(2)}, u32[]{:S(2)}) %all-to-all-start.3) | async-done | bytes 655392 | tf_op jit(solution)/shard_map/all_to_all | solution.py:613
  314.4 6.1 shard_map.171
  321.4 11.7 %shard_map.172 = (bf16[3,4,80,1024]{3,2,1,0:T(8,128)(2,1)S(1)}, f32[80,128]{1,0:T(8,128)S(1)}) custom-call(f32[3,4,80,1024]{3,2,1,0:T(8,128)} %fusion.131.proj_ref, bf16[4,4,80,256]{3,2,1,0:T(8,128)(2,1)} %bitcast.71.grad_ref, f32[4,1,1024]{2,1,0:T(1,128)S(1)} %get-tuple-element.47.lse_ref, f32[80,1]{1,0:T(8,128)S(1)} %copy.72.scale_ref, ...), custom_call_target="tpu_custom_call" | custom-call | flops 1048576 | bytes 1048576 | tf_op jit(solution)/shard_map/pallas_call | solution.py:502
  334.3 5.8 dot_general.90
  340.1 5.4 fusion.81
  348.0 4.7 copy.78
  361.5 11.1 %collective-permute-done.21 = bf16[2,128,1280]{2,1,0:T(8,128)(2,1)S(1)} collective-permute-done((bf16[2,128,1280]{2,1,0:T(8,128)(2,1)S(1)}, bf16[2,128,1280]{2,1,0:T(8,128)(2,1)S(1)}, u32[]{:S(2)}, u32[]{:S(2)}) %collective-permute-start.21) | collective-permute-done | bytes 655392 | tf_op jit(solution)/shard_map/ppermute | solution.py:575
  395.1 6.2 shard_map.173
  401.5 8.2 %constant_dynamic-slice_fusion.5 = (bf16[4,2,2,1,40,3840]{5,4,3,2,1,0:T(8,128)(2,1)}, bf16[4,2,2,1,40,3840]{5,4,3,2,1,0:T(8,128)(2,1)}) fusion(bf16[4,2,2,2,40,3840]{5,4,3,2,1,0:T(8,128)(2,1)} %bitcast.319, s32[]{:T(128)S(6)} %select_n.292, s32[]{:T(128)S(6)} %select_n.293), kind=kLoop, calls=%fused_computation.230 | loop fusion | bytes 19660808 | tf_op jit(solution)/shard_map/jit(dynamic_index_in_dim)/dynamic_slice | solution.py:579
  409.8 4.9 copy.110
  428.5 12.0 %shard_map.174 = (bf16[3,4,80,1024]{3,2,1,0:T(8,128)(2,1)S(1)}, f32[80,128]{1,0:T(8,128)S(1)}) custom-call(f32[3,4,80,1024]{3,2,1,0:T(8,128)} %fusion.130.proj_ref, bf16[4,4,80,256]{3,2,1,0:T(8,128)(2,1)S(1)} %bitcast.314, f32[4,1,1024]{2,1,0:T(1,128)S(1)} %get-tuple-element.50.lse_ref, f32[80,1]{1,0:T(8,128)S(1)} %copy.67.scale_ref, ...), custom_call_target="tpu_custom_call" | custom-call | flops 1048576 | bytes 1048576 | tf_op jit(solution)/shard_map/pallas_call | solution.py:502
  454.7 47.7 %collective-permute-done.45 = f32[2,80]{1,0:T(2,128)S(1)} collective-permute-done((f32[2,80]{1,0:T(2,128)S(1)}, f32[2,80]{1,0:T(2,128)S(1)}, u32[]{:S(2)}, u32[]{:S(2)}) %collective-permute-start.45) | collective-permute-done | bytes 672 | tf_op jit(solution)/shard_map/ppermute | solution.py:575
  516.7 4.8 fusion.77
  535.7 31.5 %collective-permute-done.32 = bf16[4,160,960]{2,1,0:T(8,128)(2,1)} collective-permute-done((bf16[4,160,960]{2,1,0:T(8,128)(2,1)}, bf16[4,160,960]{2,1,0:T(8,128)(2,1)}, u32[]{:S(2)}, u32[]{:S(2)}) %collective-permute-start.32) | collective-permute-done | bytes 1228832 | tf_op jit(solution)/shard_map/ppermute | solution.py:575
  584.3 7.5 %collective-permute-done.35 = bf16[160,960]{1,0:T(8,128)(2,1)S(1)} collective-permute-done((bf16[160,960]{1,0:T(8,128)(2,1)S(1)}, bf16[160,960]{1,0:T(8,128)(2,1)S(1)}, u32[]{:S(2)}, u32[]{:S(2)}) %collective-permute-start.35) | collective-permute-done | bytes 307232 | tf_op jit(solution)/shard_map/ppermute | solution.py:575
  591.8 13.1 %collective-permute-done.34 = bf16[160,960]{1,0:T(8,128)(2,1)S(1)} collective-permute-done((bf16[160,960]{1,0:T(8,128)(2,1)S(1)}, bf16[160,960]{1,0:T(8,128)(2,1)S(1)}, u32[]{:S(2)}, u32[]{:S(2)}) %collective-permute-start.34) | collective-permute-done | bytes 307232 | tf_op jit(solution)/shard_map/ppermute | solution.py:575
  624.9 12.4 %collective-permute-done.36 = bf16[4,40,1920]{2,1,0:T(8,128)(2,1)S(1)} collective-permute-done((bf16[4,40,1920]{2,1,0:T(8,128)(2,1)S(1)}, bf16[4,40,1920]{2,1,0:T(8,128)(2,1)S(1)}, u32[]{:S(2)}, u32[]{:S(2)}) %collective-permute-start.36) | collective-permute-done | bytes 614432 | tf_op jit(solution)/shard_map/ppermute | solution.py:575
  645.9 6.3 collective-permute-done.38
  652.2 10.5 %collective-permute-done.39 = bf16[40,3840]{1,0:T(8,128)(2,1)S(1)} collective-permute-done((bf16[40,3840]{1,0:T(8,128)(2,1)S(1)}, bf16[40,3840]{1,0:T(8,128)(2,1)S(1)}, u32[]{:S(2)}, u32[]{:S(2)}) %collective-permute-start.39) | collective-permute-done | bytes 307232 | tf_op jit(solution)/shard_map/ppermute | solution.py:575
  (412 shorter events, 275.8 us)
Async XLA Ops:
  7.2 193.7 %all-gather.2.cloned.1.call-start = ((), (), s32[]{:S(2)}) async-start(), calls=%async_computation.9 | async-start | bytes 20275200 | tf_op jit(solution)/shard_map/all_gather | solution.py:730
  30.0 19.1 %collective-permute-start.3 = (bf16[160,964]{1,0:T(8,128)(2,1)S(1)}, bf16[160,964]{1,0:T(8,128)(2,1)}, u32[]{:S(2)}, u32[]{:S(2)}) collective-permute-start(bf16[160,964]{1,0:T(8,128)(2,1)S(1)} %bitcast.357), channel_id=1, source_target_pairs={{0,24},{8,16},{16,8},{24,0},{1,25},{9,17},{17,9},{25,1},{2,26},{10... | collective-permute-start | bytes 925448 | tf_op jit(solution)/shard_map/ppermute | solution.py:575
  33.8 38.7 %collective-permute-start.2 = (bf16[160,964]{1,0:T(8,128)(2,1)S(1)}, bf16[160,964]{1,0:T(8,128)(2,1)}, u32[]{:S(2)}, u32[]{:S(2)}) collective-permute-start(bf16[160,964]{1,0:T(8,128)(2,1)S(1)} %bitcast.358), channel_id=1, source_target_pairs={{0,16},{8,24},{16,0},{24,8},{1,17},{9,25},{17,1},{25,9},{2,18},{10... | collective-permute-start | bytes 925448 | tf_op jit(solution)/shard_map/ppermute | solution.py:575
  33.9 38.7 %collective-permute-start.1 = (bf16[160,964]{1,0:T(8,128)(2,1)S(1)}, bf16[160,964]{1,0:T(8,128)(2,1)}, u32[]{:S(2)}, u32[]{:S(2)}) collective-permute-start(bf16[160,964]{1,0:T(8,128)(2,1)S(1)} %bitcast.359), channel_id=1, source_target_pairs={{0,8},{8,0},{16,24},{24,16},{1,9},{9,1},{17,25},{25,17},{2,10},{10... | collective-permute-start | bytes 925448 | tf_op jit(solution)/shard_map/ppermute | solution.py:575
  36.1 38.8 %all-to-all-start.1 = ((bf16[4,40,960]{2,1,0:T(8,128)(2,1)}), bf16[4,40,960]{2,1,0:T(8,128)(2,1)S(1)}, u32[]{:S(2)}, u32[]{:S(2)}) async-start(bf16[4,40,960]{2,1,0:T(8,128)(2,1)} %reshape.271), calls=%async_computation.1 | async-start | bytes 655360 | tf_op jit(solution)/shard_map/all_to_all | solution.py:613
  75.0 19.4 %collective-permute-start.13 = (bf16[160,960]{1,0:T(8,128)(2,1)S(1)}, bf16[160,960]{1,0:T(8,128)(2,1)S(1)}, u32[]{:S(2)}, u32[]{:S(2)}) collective-permute-start(bf16[160,960]{1,0:T(8,128)(2,1)S(1)} %bitcast.362), channel_id=1, source_target_pairs={{0,24},{8,16},{16,8},{24,0},{1,25},{9,17},{17,9},{25,1},{2,26},{10... | collective-permute-start | bytes 921608 | tf_op jit(solution)/shard_map/ppermute | solution.py:575
  77.6 47.4 %collective-permute-start.12 = (bf16[160,960]{1,0:T(8,128)(2,1)S(1)}, bf16[160,960]{1,0:T(8,128)(2,1)S(1)}, u32[]{:S(2)}, u32[]{:S(2)}) collective-permute-start(bf16[160,960]{1,0:T(8,128)(2,1)S(1)} %bitcast.363), channel_id=1, source_target_pairs={{0,16},{8,24},{16,0},{24,8},{1,17},{9,25},{17,1},{25,9},{2,18},{10... | collective-permute-start | bytes 921608 | tf_op jit(solution)/shard_map/ppermute | solution.py:575
  77.6 49.3 %collective-permute-start.11 = (bf16[160,960]{1,0:T(8,128)(2,1)S(1)}, bf16[160,960]{1,0:T(8,128)(2,1)S(1)}, u32[]{:S(2)}, u32[]{:S(2)}) collective-permute-start(bf16[160,960]{1,0:T(8,128)(2,1)S(1)} %bitcast.364), channel_id=1, source_target_pairs={{0,8},{8,0},{16,24},{24,16},{1,9},{9,1},{17,25},{25,17},{2,10},{10... | collective-permute-start | bytes 921608 | tf_op jit(solution)/shard_map/ppermute | solution.py:575
  79.4 50.9 %collective-permute-start.4 = (bf16[160,964]{1,0:T(8,128)(2,1)S(1)}, bf16[160,964]{1,0:T(8,128)(2,1)}, u32[]{:S(2)}, u32[]{:S(2)}) collective-permute-start(bf16[160,964]{1,0:T(8,128)(2,1)S(1)} %bitcast.361), channel_id=1, source_target_pairs={{0,4},{4,0},{1,5},{5,1},{2,6},{6,2},{3,7},{7,3},{8,12},{12,8},{9,1... | collective-permute-start | bytes 925448 | tf_op jit(solution)/shard_map/ppermute | solution.py:575
  80.7 49.7 %collective-permute-start.7 = (bf16[160,964]{1,0:T(8,128)(2,1)}, bf16[160,964]{1,0:T(8,128)(2,1)}, u32[]{:S(2)}, u32[]{:S(2)}) collective-permute-start(bf16[160,964]{1,0:T(8,128)(2,1)} %collective-permute-done.3), channel_id=1, source_target_pairs={{0,4},{4,0},{1,5},{5,1},{2,6},{6,2},{3,7},{7,3},{8,12},{12,8},{9,1... | collective-permute-start | bytes 925448 | tf_op jit(solution)/shard_map/ppermute | solution.py:575
  94.3 36.1 %collective-permute-start.6 = (bf16[160,964]{1,0:T(8,128)(2,1)}, bf16[160,964]{1,0:T(8,128)(2,1)}, u32[]{:S(2)}, u32[]{:S(2)}) collective-permute-start(bf16[160,964]{1,0:T(8,128)(2,1)} %collective-permute-done.2), channel_id=1, source_target_pairs={{0,4},{4,0},{1,5},{5,1},{2,6},{6,2},{3,7},{7,3},{8,12},{12,8},{9,1... | collective-permute-start | bytes 925448 | tf_op jit(solution)/shard_map/ppermute | solution.py:575
  126.9 31.1 %collective-permute-start.9 = (bf16[256,1280]{1,0:T(8,128)(2,1)S(1)}, bf16[256,1280]{1,0:T(8,128)(2,1)}, u32[]{:S(2)}, u32[]{:S(2)}) collective-permute-start(bf16[256,1280]{1,0:T(8,128)(2,1)S(1)} %bitcast.324), channel_id=1, source_target_pairs={{0,2},{1,3},{2,0},{3,1},{4,6},{5,7},{6,4},{7,5},{8,10},{9,11},{10,... | collective-permute-start | bytes 1966088 | tf_op jit(solution)/shard_map/ppermute | solution.py:575
  130.3 36.3 %collective-permute-start.8 = (bf16[256,1280]{1,0:T(8,128)(2,1)S(1)}, bf16[256,1280]{1,0:T(8,128)(2,1)S(1)}, u32[]{:S(2)}, u32[]{:S(2)}) collective-permute-start(bf16[256,1280]{1,0:T(8,128)(2,1)S(1)} %bitcast.325), channel_id=1, source_target_pairs={{0,1},{1,0},{2,3},{3,2},{4,5},{5,4},{6,7},{7,6},{8,9},{9,8},{10,11... | collective-permute-start | bytes 1966088 | tf_op jit(solution)/shard_map/ppermute | solution.py:575
  187.0 31.7 %collective-permute-start.14 = (bf16[4,160,960]{2,1,0:T(8,128)(2,1)S(1)}, bf16[4,160,960]{2,1,0:T(8,128)(2,1)}, u32[]{:S(2)}, u32[]{:S(2)}) collective-permute-start(bf16[4,160,960]{2,1,0:T(8,128)(2,1)S(1)} %pad_maximum_fusion.6), channel_id=1, source_target_pairs={{0,4},{4,0},{1,5},{5,1},{2,6},{6,2},{3,7},{7,3},{8,12},{12,8},{9,1... | collective-permute-start | bytes 3686408 | tf_op jit(solution)/shard_map/ppermute | solution.py:575
  192.5 84.4 %collective-permute-start.19 = (bf16[128,1280]{1,0:T(8,128)(2,1)}, bf16[128,1280]{1,0:T(8,128)(2,1)}, u32[]{:S(2)}, u32[]{:S(2)}) collective-permute-start(bf16[128,1280]{1,0:T(8,128)(2,1)} %dynamic-slice_bitcast_fusion.6), channel_id=1, source_target_pairs={{0,4},{4,0},{1,5},{5,1},{2,6},{6,2},{3,7},{7,3},{8,12},{12,8},{9,1... | collective-permute-start | bytes 983048 | tf_op jit(solution)/shard_map/ppermute | solution.py:575
  227.4 25.7 %collective-permute-start.15 = (bf16[256,1280]{1,0:T(8,128)(2,1)}, bf16[256,1280]{1,0:T(8,128)(2,1)S(1)}, u32[]{:S(2)}, u32[]{:S(2)}) collective-permute-start(bf16[256,1280]{1,0:T(8,128)(2,1)} %multiply_convert_fusion.2), channel_id=1, source_target_pairs={{0,1},{1,0},{2,3},{3,2},{4,5},{5,4},{6,7},{7,6},{8,9},{9,8},{10,11... | collective-permute-start | bytes 1966088 | tf_op jit(solution)/shard_map/ppermute | solution.py:575
  361.1 40.3 %collective-permute-start.22 = (bf16[4,160,960]{2,1,0:T(8,128)(2,1)}, bf16[4,160,960]{2,1,0:T(8,128)(2,1)}, u32[]{:S(2)}, u32[]{:S(2)}) collective-permute-start(bf16[4,160,960]{2,1,0:T(8,128)(2,1)} %fusion.92), channel_id=1, source_target_pairs={{0,4},{4,0},{1,5},{5,1},{2,6},{6,2},{3,7},{7,3},{8,12},{12,8},{9,1... | collective-permute-start | bytes 3686408 | tf_op jit(solution)/shard_map/ppermute | solution.py:575
  391.3 228.7 %reduce-scatter.2.cloned.1.call-start = ((), (), s32[]{:S(2)}) async-start(), calls=%async_computation.10 | async-start | bytes 10137600 | tf_op jit(solution)/shard_map/reduce_scatter | solution.py:817
  414.7 88.4 %collective-permute-start.23 = (bf16[4,2,2,40,3840]{4,3,0,1,2:T(8,128)(2,1)}, bf16[4,2,2,40,3840]{4,3,0,1,2:T(8,128)(2,1)}, u32[]{:S(2)}, u32[]{:S(2)}) collective-permute-start(bf16[4,2,2,40,3840]{4,3,0,1,2:T(8,128)(2,1)} %bitcast.305), channel_id=1, source_target_pairs={{0,1},{1,0},{2,3},{3,2},{4,5},{5,4},{6,7},{7,6},{8,9},{9,8},{10,11... | collective-permute-start | bytes 14745608 | tf_op jit(solution)/shard_map/ppermute | solution.py:575
  449.2 53.7 %collective-permute-start.24 = (bf16[160,960]{1,0:T(8,128)(2,1)S(1)}, bf16[160,960]{1,0:T(8,128)(2,1)S(1)}, u32[]{:S(2)}, u32[]{:S(2)}) collective-permute-start(bf16[160,960]{1,0:T(8,128)(2,1)S(1)} %get-tuple-element.86), channel_id=1, source_target_pairs={{0,8},{8,0},{16,24},{24,16},{1,9},{9,1},{17,25},{25,17},{2,10},{10... | collective-permute-start | bytes 921608 | tf_op jit(solution)/shard_map/ppermute | solution.py:575
  451.3 51.7 %collective-permute-start.26 = (bf16[160,960]{1,0:T(8,128)(2,1)S(1)}, bf16[160,960]{1,0:T(8,128)(2,1)S(1)}, u32[]{:S(2)}, u32[]{:S(2)}) collective-permute-start(bf16[160,960]{1,0:T(8,128)(2,1)S(1)} %get-tuple-element.87), channel_id=1, source_target_pairs={{0,24},{8,16},{16,8},{24,0},{1,25},{9,17},{17,9},{25,1},{2,26},{10... | collective-permute-start | bytes 921608 | tf_op jit(solution)/shard_map/ppermute | solution.py:575
  451.7 51.3 %collective-permute-start.25 = (bf16[160,960]{1,0:T(8,128)(2,1)S(1)}, bf16[160,960]{1,0:T(8,128)(2,1)S(1)}, u32[]{:S(2)}, u32[]{:S(2)}) collective-permute-start(bf16[160,960]{1,0:T(8,128)(2,1)S(1)} %get-tuple-element.88), channel_id=1, source_target_pairs={{0,16},{8,24},{16,0},{24,8},{1,17},{9,25},{17,1},{25,9},{2,18},{10... | collective-permute-start | bytes 921608 | tf_op jit(solution)/shard_map/ppermute | solution.py:575
  452.9 49.5 %collective-permute-start.45 = (f32[2,80]{1,0:T(2,128)S(1)}, f32[2,80]{1,0:T(2,128)S(1)}, u32[]{:S(2)}, u32[]{:S(2)}) collective-permute-start(f32[2,80]{1,0:T(2,128)S(1)} %add.322), channel_id=1, source_target_pairs={{0,16},{8,24},{16,0},{24,8},{1,17},{9,25},{17,1},{25,9},{2,18},{10... | collective-permute-start | bytes 1928 | tf_op jit(solution)/shard_map/ppermute | solution.py:575
  508.6 61.6 %collective-permute-start.29 = (bf16[4,2,40,1920]{3,2,0,1:T(8,128)(2,1)}, bf16[4,2,40,1920]{3,2,0,1:T(8,128)(2,1)}, u32[]{:S(2)}, u32[]{:S(2)}) collective-permute-start(bf16[4,2,40,1920]{3,2,0,1:T(8,128)(2,1)} %dynamic-slice_bitcast_fusion.2), channel_id=1, source_target_pairs={{0,4},{4,0},{1,5},{5,1},{2,6},{6,2},{3,7},{7,3},{8,12},{12,8},{9,1... | collective-permute-start | bytes 3686408 | tf_op jit(solution)/shard_map/ppermute | solution.py:575
  514.3 52.8 %collective-permute-start.32 = (bf16[4,160,960]{2,1,0:T(8,128)(2,1)}, bf16[4,160,960]{2,1,0:T(8,128)(2,1)}, u32[]{:S(2)}, u32[]{:S(2)}) collective-permute-start(bf16[4,160,960]{2,1,0:T(8,128)(2,1)} %fusion.93), channel_id=1, source_target_pairs={{0,4},{4,0},{1,5},{5,1},{2,6},{6,2},{3,7},{7,3},{8,12},{12,8},{9,1... | collective-permute-start | bytes 3686408 | tf_op jit(solution)/shard_map/ppermute | solution.py:575
  528.7 47.8 %collective-permute-start.27 = (bf16[2,2,128,1280]{3,2,0,1:T(8,128)(2,1)}, bf16[2,2,128,1280]{3,2,0,1:T(8,128)(2,1)}, u32[]{:S(2)}, u32[]{:S(2)}) collective-permute-start(bf16[2,2,128,1280]{3,2,0,1:T(8,128)(2,1)} %fusion.94), channel_id=1, source_target_pairs={{0,1},{1,0},{2,3},{3,2},{4,5},{5,4},{6,7},{7,6},{8,9},{9,8},{10,11... | collective-permute-start | bytes 3932168 | tf_op jit(solution)/shard_map/ppermute | solution.py:575
  530.3 79.4 %collective-permute-start.30 = (bf16[4,2,40,1920]{3,2,0,1:T(8,128)(2,1)}, bf16[4,2,40,1920]{3,2,0,1:T(8,128)(2,1)}, u32[]{:S(2)}, u32[]{:S(2)}) collective-permute-start(bf16[4,2,40,1920]{3,2,0,1:T(8,128)(2,1)} %dynamic-slice_bitcast_fusion.1), channel_id=1, source_target_pairs={{0,2},{1,3},{2,0},{3,1},{4,6},{5,7},{6,4},{7,5},{8,10},{9,11},{10,... | collective-permute-start | bytes 3686408 | tf_op jit(solution)/shard_map/ppermute | solution.py:575
  573.9 31.0 %collective-permute-start.34 = (bf16[160,960]{1,0:T(8,128)(2,1)S(1)}, bf16[160,960]{1,0:T(8,128)(2,1)S(1)}, u32[]{:S(2)}, u32[]{:S(2)}) collective-permute-start(bf16[160,960]{1,0:T(8,128)(2,1)S(1)} %get-tuple-element.85), channel_id=1, source_target_pairs={{0,16},{8,24},{16,0},{24,8},{1,17},{9,25},{17,1},{25,9},{2,18},{10... | collective-permute-start | bytes 921608 | tf_op jit(solution)/shard_map/ppermute | solution.py:575
  580.6 37.8 %collective-permute-start.28 = (bf16[2,128,1280]{2,1,0:T(8,128)(2,1)}, bf16[2,128,1280]{2,1,0:T(8,128)(2,1)}, u32[]{:S(2)}, u32[]{:S(2)}) collective-permute-start(bf16[2,128,1280]{2,1,0:T(8,128)(2,1)} %fusion.98), channel_id=1, source_target_pairs={{0,2},{1,3},{2,0},{3,1},{4,6},{5,7},{6,4},{7,5},{8,10},{9,11},{10,... | collective-permute-start | bytes 1966088 | tf_op jit(solution)/shard_map/ppermute | solution.py:575
  623.2 21.5 %collective-permute-start.31 = (bf16[128,1280]{1,0:T(8,128)(2,1)S(1)}, bf16[128,1280]{1,0:T(8,128)(2,1)S(1)}, u32[]{:S(2)}, u32[]{:S(2)}) collective-permute-start(bf16[128,1280]{1,0:T(8,128)(2,1)S(1)} %dynamic-slice_bitcast_fusion.5), channel_id=1, source_target_pairs={{0,4},{4,0},{1,5},{5,1},{2,6},{6,2},{3,7},{7,3},{8,12},{12,8},{9,1... | collective-permute-start | bytes 983048 | tf_op jit(solution)/shard_map/ppermute | solution.py:575
  639.4 23.3 %collective-permute-start.39 = (bf16[40,3840]{1,0:T(8,128)(2,1)S(1)}, bf16[40,3840]{1,0:T(8,128)(2,1)S(1)}, u32[]{:S(2)}, u32[]{:S(2)}) collective-permute-start(bf16[40,3840]{1,0:T(8,128)(2,1)S(1)} %get-tuple-element.102), channel_id=1, source_target_pairs={{0,16},{8,24},{16,0},{24,8},{1,17},{9,25},{17,1},{25,9},{2,18},{10... | collective-permute-start | bytes 921608 | tf_op jit(solution)/shard_map/ppermute | solution.py:575
  641.1 21.6 %collective-permute-start.40 = (bf16[40,3840]{1,0:T(8,128)(2,1)S(1)}, bf16[40,3840]{1,0:T(8,128)(2,1)S(1)}, u32[]{:S(2)}, u32[]{:S(2)}) collective-permute-start(bf16[40,3840]{1,0:T(8,128)(2,1)S(1)} %get-tuple-element.103), channel_id=1, source_target_pairs={{0,24},{8,16},{16,8},{24,0},{1,25},{9,17},{17,9},{25,1},{2,26},{10... | collective-permute-start | bytes 921608 | tf_op jit(solution)/shard_map/ppermute | solution.py:575
  (102 other events, 1185.8 us)
Sparse Core Ops, SparseCore 0:
  13.7 185.8 all-gather.1
  415.1 169.7 reduce-scatter.1

commit v5 on v4

--- a/solution.py
+++ b/solution.py
@@ -535,35 +535,100 @@
     return grads.reshape(3 * local_heads * head_dim, length), scale_grad[:, 0]
 
 
-def dense_grad_kernel(attended_ref, normed_ref, active_ref, out_bar, up_bar, down_bar, grad_ref):
-    width = out_bar.shape[1]
-    grad_ref[:, :width] = jnp.dot(
-        attended_ref[...], out_bar[...], preferred_element_type=F32
-    ).astype(BF16)
-    grad_ref[:, width : 2 * width] = lax.dot_general(
-        normed_ref[...], up_bar[...], TN, preferred_element_type=F32
-    ).astype(BF16)
-    grad_ref[:, 2 * width :] = lax.dot_general(
-        active_ref[...], down_bar[...], TN, preferred_element_type=F32
-    ).astype(BF16)
+def dense_grad_kernel(
+    core_ref, attended_ref, normed_ref, active_ref, out_bar, up_bar, down_bar,
+    own_ref, other_ref, normed_t, active_t,
+):
+    tile = pl.program_id(0)
+    rows, width = own_ref.shape[2] * own_ref.shape[3] * 2, out_bar.shape[1]
+
+    @pl.when(tile == 0)
+    def _():
+        normed_t[...] = normed_ref[...].astype(F32).T.astype(BF16)
+        active_t[...] = active_ref[...].astype(F32).T.astype(BF16)
+
+    start = pl.multiple_of(tile * rows, rows)
+    first_core = core_ref[0] == 0
+    lefts = (attended_ref, normed_t, active_t)
+    for i, (left, right) in enumerate(zip(lefts, (out_bar, up_bar, down_bar))):
+        grad = jnp.dot(left[pl.ds(start, rows), :], right[...], preferred_element_type=F32)
+        grad = grad.reshape(2, 2, rows // 4, width)
+        one, two = grad[:, 0], grad[:, 1]
+        own_ref[0, 0, :, :, i * width : (i + 1) * width] = jnp.where(
+            first_core, one, two
+        ).astype(BF16)
+        other_ref[0, 0, :, :, i * width : (i + 1) * width] = jnp.where(
+            first_core, two, one
+        ).astype(BF16)
 
 
 def dense_grads(attended_t, normed, active, out_bar, up_bar, down_bar):
     width, tokens = attended_t.shape
-    tile = 256
-    whole = pl.BlockSpec((tokens, width), lambda i: (0, 0))
-    columns = pl.BlockSpec((tokens, tile), lambda i: (0, i))
+    own = width // 32
+    whole = pl.BlockSpec((tokens, width), lambda i, core: (0, 0))
+    rows = pl.BlockSpec((1, 1, 2, own, 3 * width), lambda i, core: (i // 2, i % 2, 0, 0, 0))
+    shape = jax.ShapeDtypeStruct((4, 2, 2, own, 3 * width), BF16)
     return pl.pallas_call(
         dense_grad_kernel,
-        grid=(width // tile,),
-        in_specs=[
-            pl.BlockSpec((tile, tokens), lambda i: (i, 0)), columns, columns, whole, whole, whole,
-        ],
-        out_specs=pl.BlockSpec((tile, 3 * width), lambda i: (i, 0)),
-        out_shape=jax.ShapeDtypeStruct((width, 3 * width), BF16),
+        grid_spec=pltpu.PrefetchScalarGridSpec(
+            num_scalar_prefetch=1,
+            grid=(8,),
+            in_specs=[pl.BlockSpec((width, tokens), lambda i, core: (0, 0))] + [whole] * 5,
+            out_specs=[rows, rows],
+            scratch_shapes=[pltpu.VMEM((width, tokens), BF16)] * 2,
+        ),
+        out_shape=[shape, shape],
         compiler_params=KERNEL,
         cost_estimate=LIGHT,
-    )(attended_t, normed, active, out_bar, up_bar, down_bar)
+    )(place()[2:], attended_t, normed, active, out_bar, up_bar, down_bar)
+
+
+def place():
+    head = lax.axis_index("head")
+    return jnp.stack([lax.axis_index("blk"), head // 2, head % 2]).astype(jnp.int32)
+
+
+def assemble_kernel(place_ref, *refs):
+    pieces, whole_ref, sems = refs[:10], refs[10], refs[11]
+    half = whole_ref.shape[-1] // 2
+    blk, row, core = place_ref[0], place_ref[1], place_ref[2]
+    copies = []
+    for i in range(2):
+        at_core = core if i == 0 else 1 - core
+        own, across, beside, one, two = pieces[5 * i : 5 * i + 5]
+        for piece, at_blk, at_row, columns in (
+            (own, blk, row, None),
+            (across, 1 - blk, row, None),
+            (beside, blk, 1 - row, None),
+            (one, 1 - blk, 1 - row, pl.ds(0, half)),
+            (two, 1 - blk, 1 - row, pl.ds(half, half)),
+        ):
+            target = whole_ref.at[:, at_blk, at_row, at_core]
+            if columns is not None:
+                target = whole_ref.at[:, at_blk, at_row, at_core, :, columns]
+            copies.append(pltpu.make_async_copy(piece, target, sems.at[len(copies)]))
+    for copy in copies:
+        copy.start()
+    for copy in copies:
+        copy.wait()
+
+
+def assemble(pieces):
+    batch, own, columns = pieces[0].shape
+    whole = pl.pallas_call(
+        assemble_kernel,
+        grid_spec=pltpu.PrefetchScalarGridSpec(
+            num_scalar_prefetch=1,
+            grid=(1,),
+            in_specs=[pl.BlockSpec(memory_space=pl.ANY)] * 10,
+            out_specs=pl.BlockSpec(memory_space=pl.ANY),
+            scratch_shapes=[pltpu.SemaphoreType.DMA((10,))],
+        ),
+        out_shape=jax.ShapeDtypeStruct((batch, 2, 2, 2, own, columns), BF16),
+        compiler_params=KERNEL,
+        cost_estimate=LIGHT,
+    )(place(), *pieces)
+    return whole.reshape(-1, columns)
 
 
 def tied(*arrays):
@@ -623,16 +688,27 @@
 
 
 def along_batch(piece):
-    return [piece] + [swapped(piece, "batch", mask) for mask in (1, 2, 3)]
-
-
-def in_rows(along, across):
-    me, blk = lax.axis_index("batch"), lax.axis_index("blk")
-    ordered = []
-    for i in range(4):
-        one, two = pick(along, me ^ i), pick(across, me ^ i)
-        ordered += [jnp.where(blk == 0, one, two), jnp.where(blk == 0, two, one)]
-    return jnp.stack(ordered).reshape(-1, along.shape[-1])
+    return lax.all_gather(piece, "batch", axis=0, tiled=False)
+
+
+def along_blk(along):
+    other = swapped(along, "blk", 1)
+    first = lax.axis_index("blk") == 0
+    both = jnp.stack([jnp.where(first, along, other), jnp.where(first, other, along)], axis=1)
+    return both.reshape(-1, along.shape[-1])
+
+
+def other_core(array):
+    return swapped(array, "head", 1)
+
+
+def to_neighbours(along):
+    return swapped(along, "blk", 1), swapped(along, "head", 2)
+
+
+def to_diagonal(across, beside):
+    half = across.shape[-1] // 2
+    return swapped(across[..., :half], "head", 2), swapped(beside[..., half:], "blk", 1)
 
 
 def columns_over_blk(grad):
@@ -641,45 +717,41 @@
     return pick(parts, blk, 1), swapped(pick(parts, 1 - blk, 1).astype(BF16), "blk", 1)
 
 
-def sent_over_batch(parts):
-    me = lax.axis_index("batch")
-    sent = [swapped(pick(parts, me ^ mask).astype(BF16), "batch", mask) for mask in (1, 2, 3)]
-    return pick(parts, me).astype(F32), jnp.stack(sent)
-
-
-def columns_to_rows(own, sent):
-    summed = (own + jnp.sum(sent.astype(F32), axis=0)).astype(BF16)
+def over_batch(parts):
+    return lax.psum_scatter(parts.astype(BF16), "batch", scatter_dimension=0, tiled=False)
+
+
+def columns_to_rows(summed):
     moved = over_head(summed.reshape(4, -1, summed.shape[-1]))
     rows = moved.shape[1]
     return moved.reshape(4, rows, 3, -1).transpose(1, 2, 0, 3).reshape(rows, -1).astype(F32)
 
 
-def over_core(grad):
-    core = lax.axis_index("head") % 2
-    parts = grad.reshape(4, 2, 2, 2, -1, grad.shape[1])
-    got = swapped(pick(parts, 1 - core, 3), "head", 1).astype(F32)
-    return (pick(parts, core, 3).astype(F32) + got).astype(BF16)
-
-
-def over_one(part, axis, mask, mine, dim):
-    got = swapped(pick(part, 1 - mine, dim), axis, mask).astype(F32)
-    return (pick(part, mine, dim).astype(F32) + got).astype(BF16)
-
-
-def over_chips_first(cored):
-    row, blk = lax.axis_index("head") // 2, lax.axis_index("blk")
-    half = cored.shape[-1] // 2
-    return (
-        over_one(cored[..., :half], "blk", 1, blk, 1),
-        over_one(cored[..., half:], "head", 2, row, 2),
-    )
-
-
-def over_chips_second(first, second):
-    row, blk = lax.axis_index("head") // 2, lax.axis_index("blk")
-    first = over_one(first, "head", 2, row, 1)
-    second = over_one(second, "blk", 1, blk, 1)
-    return jnp.concatenate([first, second], axis=-1)
+def diagonal_sent(cored):
+    blk, row, _ = place()
+    rows = pick(pick(cored, 1 - blk, 1), 1 - row, 1)
+    half = rows.shape[-1] // 2
+    return swapped(rows[..., :half], "blk", 1), swapped(rows[..., half:], "head", 2)
+
+
+def neighbours_sent(cored, one, two):
+    blk, row, _ = place()
+    half = one.shape[-1]
+    across = pick(pick(cored, 1 - blk, 1), row, 1)
+    beside = pick(pick(cored, blk, 1), 1 - row, 1)
+    across = jnp.concatenate(
+        [across[..., :half], across[..., half:].astype(F32) + two.astype(F32)], axis=-1
+    ).astype(BF16)
+    beside = jnp.concatenate(
+        [beside[..., :half].astype(F32) + one.astype(F32), beside[..., half:]], axis=-1
+    ).astype(BF16)
+    return swapped(across, "blk", 1), swapped(beside, "head", 2)
+
+
+def own_sum(cored, across, beside):
+    blk, row, _ = place()
+    own = pick(pick(cored, blk, 1), row, 1)
+    return own.astype(F32) + across.astype(F32) + beside.astype(F32)
 
 
 def sum_all(array):
@@ -719,24 +791,27 @@
     columns[0], first = tied(columns[0], first)
     first_all = gather_rows(first)
     stream = first.astype(F32)
-    along = along_batch(columns[0].reshape(-1, columns[0].shape[-1]))
-    across = jnp.stack([swapped(part, "blk", 1) for part in along])
-    along = jnp.stack(along)
-    with_gains = in_rows(along, across)
+    first_columns = columns[0].reshape(-1, columns[0].shape[-1])
     part3 = 3 * width // 4
-    qkvs = [with_gains[:, :part3]]
+    dense_own = [
+        jnp.concatenate([out_weight[i], up_weight[i], down_weight[i]], axis=1) for i in (0, 1)
+    ]
+    along = along_batch(first_columns)
+    dense_along = [along_batch(dense_own[0]), None]
+    with_gains = along_blk(along)
+    qkvs = [with_gains[:, :part3], None]
     gains = with_gains[:, part3:].T.astype(F32)
-    own = [w[layer] for layer in range(layers) for w in (out_weight, up_weight, down_weight)]
-    dense_whole = lax.all_gather(jnp.concatenate(own, axis=1), ALL, axis=0, tiled=True)
-    denses = [dense_whole[:, 3 * width * i : 3 * width * (i + 1)] for i in range(layers)]
-    next_piece = qkv_columns(qkv_weight[1], None).reshape(-1, part3)
-    next_piece, _ = tied(next_piece, along)
-    next_along = jnp.stack(along_batch(next_piece))
-
-    kept = []
+    near = [to_neighbours(dense_along[0]), None]
+    next_along = along_batch(qkv_columns(qkv_weight[1], None).reshape(-1, part3))
+    dense_along[1] = along_batch(dense_own[1])
+
+    def dense_of(layer):
+        pieces = (dense_along[layer],) + near[layer] + to_diagonal(*near[layer])
+        return assemble(pieces + tuple(other_core(piece) for piece in pieces))
+
+    kept, denses = [], []
     for layer in range(layers):
-        qkv, dense = qkvs[layer], denses[layer]
-        out_w, up_w, down_w = dense[:, :width], dense[:, width:-width], dense[:, -width:]
+        qkv = qkvs[layer]
         normed, factor_one = normalize(stream, gains[layer])
         if layer == 0:
             normed_all = normalize(first_all.astype(F32), gains[0])[0].astype(BF16)
@@ -749,13 +824,18 @@
             projected, scale_vecs[layer], segments, 4, token_rows
         )
         if layer == 0:
-            attended, next_along = tied(attended, next_along)
-            next_across = swapped(next_along, "blk", 1)
+            attended, near[0] = tied(attended, near[0])
+        else:
+            attended, near[1] = tied(attended, near[1])
+        denses.append(dense_of(layer))
+        dense = denses[layer]
+        out_w, up_w, down_w = dense[:, :width], dense[:, width:-width], dense[:, -width:]
         attended_t = over_head(attended).reshape(width, -1)
         middle = stream + dot_rows(attended_t, out_w)
         if layer == 0:
-            middle, next_across = tied(middle, next_across)
-            qkvs.append(in_rows(next_along, next_across))
+            middle, next_along, dense_along[1] = tied(middle, next_along, dense_along[1])
+            qkvs[1] = along_blk(next_along)
+            near[1] = to_neighbours(dense_along[1])
         normed_two, factor_two = normalize(middle, gains[layers + layer])
         normed_two = normed_two.astype(BF16)
         hidden = dot(normed_two, up_w)
@@ -770,7 +850,7 @@
     layer_out = swap_halves(stream.astype(BF16).reshape(tokens.shape))
     upper = swap_halves(cotangent).reshape(-1, width).astype(F32)
 
-    qkv_grads, dense_own, scale_grads = [None] * layers, [None] * layers, [None] * layers
+    qkv_grads, dense_grad, scale_grads = [None] * layers, [None] * layers, [None] * layers
     for layer in reversed(range(layers)):
         (
             stream, factor_one, normed_all, projected, log_total, attended_t, middle,
@@ -788,38 +868,37 @@
         )
         out_bar = middle_grad.astype(BF16)
         attended_grad = over_head(dot_cols(out_w, out_bar).astype(BF16).reshape(4, -1, out_bar.shape[0]))
-        grads = dense_grads(attended_t, normed_two, active, out_bar, up_bar, down_bar)
+        grads, others = dense_grads(attended_t, normed_two, active, out_bar, up_bar, down_bar)
         if layer == 0:
-            attended_grad, grads, later = tied(attended_grad, grads, later)
-            own, sent = sent_over_batch(later[0] + later[1].astype(F32))
-            cored = over_core(grads)
+            attended_grad, others, sent, later = tied(attended_grad, others, sent, later)
+            dense_grad[1] = over_batch(own_sum(cored, *sent))
+            qkv_sum = over_batch(later[0] + later[1].astype(F32))
         else:
-            attended_grad, grads = tied(attended_grad, grads)
+            attended_grad, others = tied(attended_grad, others)
+        others = other_core(others)
         bars, scale_grads[layer] = attend_back_rows(
             projected, attended_grad, log_total, scale_vecs[layer], segments, token_rows
         )
-        if layer == 0:
-            bars, cored, sent = tied(bars, cored, sent)
-            qkv_grads[1] = columns_to_rows(own, sent)
-            halves = over_chips_first(cored)
+        bars, others = tied(bars, others)
+        cored = (grads.astype(F32) + others.astype(F32)).astype(BF16)
+        diagonal = diagonal_sent(cored)
         normed_grad = scatter_rows(
             lax.dot_general(bars, qkv, (((0,), (1,)), ((), ())), preferred_element_type=F32)
         )
         later = columns_over_blk(
             lax.dot_general(normed_all, bars, (((0,), (1,)), ((), ())), preferred_element_type=F32)
         )
+        normed_grad, diagonal = tied(normed_grad, diagonal)
+        sent = neighbours_sent(cored, *diagonal)
         if layer == 0:
-            normed_grad, halves, dense_own[1] = tied(normed_grad, halves, dense_own[1])
-            own, sent = sent_over_batch(over_chips_second(*halves))
-            dense_own[0] = own + jnp.sum(sent.astype(F32), axis=0)
-            qkv_grads[0] = columns_to_rows(*sent_over_batch(later[0] + later[1].astype(F32)))
-        else:
-            dense_own[1] = lax.psum_scatter(grads, ALL, scatter_dimension=0, tiled=True)
+            dense_grad[0] = over_batch(own_sum(cored, *sent))
+            qkv_grads[1] = columns_to_rows(qkv_sum)
+            qkv_grads[0] = columns_to_rows(over_batch(later[0] + later[1].astype(F32)))
         upper = middle_grad + lower_of(normed_grad, stream, factor_one, gains[layer])
     input_grad = swap_halves(upper.astype(BF16).reshape(tokens.shape)).astype(F32)
     scale_total = sum_all(jnp.stack(scale_grads))
     scale_grad = scale_total * (SCALE_BASE / math.sqrt(head_dim)) * jax.nn.sigmoid(scale_param)
-    dense_all = jnp.stack([part.astype(F32) for part in dense_own])
+    dense_all = jnp.stack([part.astype(F32) for part in dense_grad])
     qkv_all = jnp.stack(qkv_grads)
     up_all = dense_all[:, :, width:-width]
     return (

time: 680 us -> 1090 us (1.60)
  Pallas kernels: 57 us -> 546 us
  waiting for transfers between devices: 299 us -> 238 us
  matrix products: 67.7 us -> 56.1 us
    pallas_call x2 -> x4, Pallas kernels: 12.3 us -> 502 us  [the longest x2 487 us: assemble(): pl.pallas_call(assemble_kernel, grid_spec=pltpu.PrefetchScalarGridSpec(nu...]
    ppermute x46 -> x51, waiting for transfers between devices: 273 us -> 170 us  [swapped(): return lax.ppermute(array, axis, [(i, i ^ mask) for i in range(size)])]
    all_gather x1 -> x4, waiting for transfers between devices: 0.01 us -> 34.8 us  [along_batch(): return lax.all_gather(piece, 'batch', axis=0, tiled=False)]
    dot_general x6, matrix products: 20.8 us -> 8.65 us  [dot_cols(): lax.dot_general(left, right, (((1,), (1,)), ((), ())), preferred_element_...]
    dynamic_slice x7 -> x3, local copies, waits for them, and re-layouts: 13.7 us -> 2.04 us  [pick(): return lax.dynamic_index_in_dim(array, index, axis, keepdims=False)]
    ppermute x46 -> x51, starting transfers between devices: 50 us -> 44.6 us  [swapped(): return lax.ppermute(array, axis, [(i, i ^ mask) for i in range(size)])]
    unnamed x161 -> x170, local copies, waits for them, and re-layouts: 26.4 us -> 27 us
  transfers between devices with their start and end apart: 56 -> 67, of which waited for: 30 -> 24; matrix products, arithmetic and copies ran while one was open for 21% -> 13% of each run, Pallas kernels for 7% -> 50%
where the time goes in v5:
time: 1090 us; the launch traced here: 1080 us
  Pallas kernels  546 us (50%)
  waiting for transfers between devices  238 us (22%)
  local copies, waits for them, and re-layouts  86.6 us (8%)
  starting transfers between devices  75.2 us (7%)
  other arithmetic  64.8 us (6%)
  matrix products  56.1 us (5%)
  between operations  16.3 us (1%)
    pallas_call x2, Pallas kernels, assemble(): pl.pallas_call(assemble_kernel, grid_spec=pltpu.PrefetchScalarGridSpec(nu...  487 us
    ppermute x51, waiting for transfers between devices, swapped(): return lax.ppermute(array, axis, [(i, i ^ mask) for i in range(size)])  170 us
    ppermute x51, starting transfers between devices, swapped(): return lax.ppermute(array, axis, [(i, i ^ mask) for i in range(size)])  44.6 us
    all_gather x4, waiting for transfers between devices, along_batch(): return lax.all_gather(piece, 'batch', axis=0, tiled=False)  34.8 us
    all_to_all x8, starting transfers between devices, over_head(): lax.all_to_all(parts, 'head', split_axis=0, concat_axis=0, tiled=True)  29.8 us
    all_to_all x8, waiting for transfers between devices, over_head(): lax.all_to_all(parts, 'head', split_axis=0, concat_axis=0, tiled=True)  27.9 us
    unnamed x170, local copies, waits for them, and re-layouts  27 us
    pallas_call x2, Pallas kernels, attend_back_rows(): pl.pallas_call(functools.partial(attend_back_kernel, token_rows), grid=(l...  23.5 us
  transfers between devices with their start and end apart: 67, of which 24 were waited for; matrix products, arithmetic and copies ran while one was open for 13% of the time, Pallas kernels for 50%

profile of v5, /device:TPU:0, one launch (start us, length us, event | category | flops | bytes accessed | tf_op | source)
XLA Modules:
  0.0 1083.5 jit_solution(15662328139306803666)
XLA Ops:
  19.1 5.3 all-to-all-done
  33.3 11.4 %collective-permute-done.3 = bf16[256,1280]{1,0:T(8,128)(2,1)S(1)} collective-permute-done((bf16[256,1280]{1,0:T(8,128)(2,1)S(1)}, bf16[256,1280]{1,0:T(8,128)(2,1)S(1)}, u32[]{:S(2)}, u32[]{:S(2)}) %collective-permute-start.3) | collective-permute-done | bytes 655392 | tf_op jit(solution)/shard_map/ppermute | solution.py:640
  50.5 6.9 all-gather.7.cloned.1.call-done
  62.0 27.9 %all-gather.11.cloned.1.call-done = bf16[160,3840]{1,0:T(8,128)(2,1)} async-done(((bf16[40,3840]{1,0:T(8,128)(2,1)}), bf16[160,3840]{1,0:T(8,128)(2,1)}) %all-gather.11.cloned.1.call-update) | async-done | bytes 1228816 | tf_op jit(solution)/shard_map/all_gather | solution.py:691
  105.2 4.7 fusion.117.proj_ref
  109.9 10.5 shard_map.169
  124.4 13.6 %collective-permute-done.7.refs_3_ = bf16[4,40,1920]{2,1,0:T(8,128)(2,1)S(1)} collective-permute-done((bf16[4,40,1920]{2,1,0:T(8,128)(2,1)S(1)}, bf16[4,40,1920]{2,1,0:T(8,128)(2,1)S(1)}, u32[]{:S(2)}, u32[]{:S(2)}) %collective-permute-start.7) | collective-permute-done | bytes 614432 | tf_op jit(solution)/shard_map/ppermute | solution.py:640
  144.0 243.7 %shard_map.170 = bf16[4,2,2,2,40,3840]{5,4,3,2,1,0:T(8,128)(2,1)} custom-call(s32[3]{0:T(128)S(1)} %pad_add_fusion.place_ref, bf16[4,40,3840]{2,1,0:T(8,128)(2,1)S(1)} %bitcast.273, bf16[4,40,3840]{2,1,0:T(8,128)(2,1)} %collective-permute-done.5.refs_1_, bf16[4,40,3840]{2,1,0:T(8,128)(2,1)} %collective-permute-done.6.refs_2_, ...), custom_call_target="tpu_custom_call" | custom-call | flops 1048576 | bytes 1048576 | tf_op jit(solution)/shard_map/pallas_call | solution.py:618
  407.2 12.8 %collective-permute-done.16 = bf16[256,1280]{1,0:T(8,128)(2,1)} collective-permute-done((bf16[256,1280]{1,0:T(8,128)(2,1)}, bf16[256,1280]{1,0:T(8,128)(2,1)}, u32[]{:S(2)}, u32[]{:S(2)}) %collective-permute-start.16) | collective-permute-done | bytes 655392 | tf_op jit(solution)/shard_map/ppermute | solution.py:640
  422.5 10.6 collective-permute-done.14
  453.1 10.5 shard_map.171
  476.6 8.3 collective-permute-done.20.refs_3_
  488.9 243.7 %shard_map.172 = bf16[4,2,2,2,40,3840]{5,4,3,2,1,0:T(8,128)(2,1)} custom-call(s32[3]{0:T(128)S(1)} %pad_add_fusion.place_ref, bf16[4,40,3840]{2,1,0:T(8,128)(2,1)} %bitcast.40.refs_0_, bf16[4,40,3840]{2,1,0:T(8,128)(2,1)} %copy-done.47, bf16[4,40,3840]{2,1,0:T(8,128)(2,1)} %collective-permute-done.19.refs_2_, ...), custom_call_target="tpu_custom_call" | custom-call | flops 1048576 | bytes 1048576 | tf_op jit(solution)/shard_map/pallas_call | solution.py:618
  753.9 7.2 shard_map.173
  761.1 5.0 copy.102
  771.1 11.7 %shard_map.174 = (bf16[3,4,80,1024]{3,2,1,0:T(8,128)(2,1)S(1)}, f32[80,128]{1,0:T(8,128)S(1)}) custom-call(f32[3,4,80,1024]{3,2,1,0:T(8,128)} %fusion.118.proj_ref, bf16[4,4,80,256]{3,2,1,0:T(8,128)(2,1)} %bitcast.70.grad_ref, f32[4,1,1024]{2,1,0:T(1,128)S(1)} %get-tuple-element.65.lse_ref, f32[80,1]{1,0:T(8,128)S(1)} %copy.98.scale_ref, ...), custom_call_target="tpu_custom_call" | custom-call | flops 1048576 | bytes 1048576 | tf_op jit(solution)/shard_map/pallas_call | solution.py:502
  784.1 5.9 dot_general.90
  790.0 5.5 fusion.85
  816.9 17.7 %collective-permute-done.31 = bf16[2,128,1280]{2,1,0:T(8,128)(2,1)S(1)} collective-permute-done((bf16[2,128,1280]{2,1,0:T(8,128)(2,1)S(1)}, bf16[2,128,1280]{2,1,0:T(8,128)(2,1)S(1)}, u32[]{:S(2)}, u32[]{:S(2)}) %collective-permute-start.31) | collective-permute-done | bytes 655392 | tf_op jit(solution)/shard_map/ppermute | solution.py:640
  857.0 7.2 shard_map.175
  864.2 15.3 %all-to-all-done.5 = bf16[4,320,256]{2,1,0:T(8,128)(2,1)S(1)} async-done(((bf16[4,320,256]{2,1,0:T(8,128)(2,1)}), bf16[4,320,256]{2,1,0:T(8,128)(2,1)S(1)}, u32[]{:S(2)}, u32[]{:S(2)}) %all-to-all-start.5) | async-done | bytes 655392 | tf_op jit(solution)/shard_map/all_to_all | solution.py:678
  891.9 4.6 copy.111
  896.5 11.8 %shard_map.176 = (bf16[3,4,80,1024]{3,2,1,0:T(8,128)(2,1)S(1)}, f32[80,128]{1,0:T(8,128)S(1)}) custom-call(f32[3,4,80,1024]{3,2,1,0:T(8,128)} %fusion.117.proj_ref, bf16[4,4,80,256]{3,2,1,0:T(8,128)(2,1)S(1)} %bitcast.267, f32[4,1,1024]{2,1,0:T(1,128)S(1)} %get-tuple-element.76.lse_ref, f32[80,1]{1,0:T(8,128)S(1)} %copy.92.scale_ref, ...), custom_call_target="tpu_custom_call" | custom-call | flops 1048576 | bytes 1048576 | tf_op jit(solution)/shard_map/pallas_call | solution.py:502
  912.1 30.6 %collective-permute-done.43 = bf16[4,160,960]{2,1,0:T(8,128)(2,1)S(1)} collective-permute-done((bf16[4,160,960]{2,1,0:T(8,128)(2,1)S(1)}, bf16[4,160,960]{2,1,0:T(8,128)(2,1)S(1)}, u32[]{:S(2)}, u32[]{:S(2)}) %collective-permute-start.43) | collective-permute-done | bytes 1228832 | tf_op jit(solution)/shard_map/ppermute | solution.py:640
  953.0 4.8 fusion.79
  958.4 5.1 add_convert_fusion
  971.7 12.0 %collective-permute-done.39 = bf16[2,128,1280]{2,1,0:T(8,128)(2,1)S(1)} collective-permute-done((bf16[2,128,1280]{2,1,0:T(8,128)(2,1)S(1)}, bf16[2,128,1280]{2,1,0:T(8,128)(2,1)S(1)}, u32[]{:S(2)}, u32[]{:S(2)}) %collective-permute-start.39) | collective-permute-done | bytes 655392 | tf_op jit(solution)/shard_map/ppermute | solution.py:640
  983.8 12.2 %collective-permute-done.41 = bf16[4,40,1920]{2,1,0:T(8,128)(2,1)S(1)} collective-permute-done((bf16[4,40,1920]{2,1,0:T(8,128)(2,1)S(1)}, bf16[4,40,1920]{2,1,0:T(8,128)(2,1)S(1)}, u32[]{:S(2)}, u32[]{:S(2)}) %collective-permute-start.41) | collective-permute-done | bytes 614432 | tf_op jit(solution)/shard_map/ppermute | solution.py:640
  1002.5 26.3 %collective-permute-done.48 = f32[2,80]{1,0:T(2,128)S(1)} collective-permute-done((f32[2,80]{1,0:T(2,128)S(1)}, f32[2,80]{1,0:T(2,128)S(1)}, u32[]{:S(2)}, u32[]{:S(2)}) %collective-permute-start.48) | collective-permute-done | bytes 672 | tf_op jit(solution)/shard_map/ppermute | solution.py:640
  1050.1 5.0 collective-permute-done.42
  1059.8 5.6 all-to-all-done.6
  1067.9 5.5 reduce-scatter.9.cloned.1.call-done
  (447 shorter events, 258.3 us)
Async XLA Ops:
  17.7 39.7 %all-gather.7.cloned.1.call-start = ((), (), s32[]{:S(2)}) async-start(), calls=%async_computation.12 | async-start | bytes 1638400 | tf_op jit(solution)/shard_map/all_gather | solution.py:691
  25.2 64.7 %all-gather.11.cloned.1.call-start = ((), (), s32[]{:S(2)}) async-start(), calls=%async_computation.18 | async-start | bytes 1536000 | tf_op jit(solution)/shard_map/all_gather | solution.py:691
  26.1 365.1 %all-gather.13.cloned.1.call-start = ((), (), s32[]{:S(2)}) async-start(), calls=%async_computation.19 | async-start | bytes 1536000 | tf_op jit(solution)/shard_map/all_gather | solution.py:691
  32.5 358.7 %all-gather.9.cloned.1.call-start = ((), (), s32[]{:S(2)}) async-start(), calls=%async_computation.13 | async-start | bytes 1638400 | tf_op jit(solution)/shard_map/all_gather | solution.py:691
  57.4 35.4 %collective-permute-start.1 = (bf16[4,160,964]{2,1,0:T(8,128)(2,1)}, bf16[4,160,964]{2,1,0:T(8,128)(2,1)}, u32[]{:S(2)}, u32[]{:S(2)}) collective-permute-start(bf16[4,160,964]{2,1,0:T(8,128)(2,1)} %all-gather.7.cloned.1.call-done), channel_id=1, source_target_pairs={{0,4},{4,0},{1,5},{5,1},{2,6},{6,2},{3,7},{7,3},{8,12},{12,8},{9,1... | collective-permute-start | bytes 3701768 | tf_op jit(solution)/shard_map/ppermute | solution.py:640
  89.9 30.5 %collective-permute-start.5 = (bf16[4,40,3840]{2,1,0:T(8,128)(2,1)}, bf16[4,40,3840]{2,1,0:T(8,128)(2,1)}, u32[]{:S(2)}, u32[]{:S(2)}) collective-permute-start(bf16[4,40,3840]{2,1,0:T(8,128)(2,1)} %bitcast.270), channel_id=1, source_target_pairs={{0,4},{4,0},{1,5},{5,1},{2,6},{6,2},{3,7},{7,3},{8,12},{12,8},{9,1... | collective-permute-start | bytes 3686408 | tf_op jit(solution)/shard_map/ppermute | solution.py:640
  91.3 29.0 %collective-permute-start.6 = (bf16[4,40,3840]{2,1,0:T(8,128)(2,1)}, bf16[4,40,3840]{2,1,0:T(8,128)(2,1)}, u32[]{:S(2)}, u32[]{:S(2)}) collective-permute-start(bf16[4,40,3840]{2,1,0:T(8,128)(2,1)} %bitcast.271), channel_id=1, source_target_pairs={{0,2},{1,3},{2,0},{3,1},{4,6},{5,7},{6,4},{7,5},{8,10},{9,11},{10,... | collective-permute-start | bytes 3686408 | tf_op jit(solution)/shard_map/ppermute | solution.py:640
  92.8 51.2 %collective-permute-start.9 = (bf16[4,40,3840]{2,1,0:T(8,128)(2,1)}, bf16[4,40,3840]{2,1,0:T(8,128)(2,1)}, u32[]{:S(2)}, u32[]{:S(2)}) collective-permute-start(bf16[4,40,3840]{2,1,0:T(8,128)(2,1)} %bitcast.272), channel_id=1, source_target_pairs={{0,1},{1,0},{2,3},{3,2},{4,5},{5,4},{6,7},{7,6},{8,9},{9,8},{10,11... | collective-permute-start | bytes 3686408 | tf_op jit(solution)/shard_map/ppermute | solution.py:640
  140.2 247.6 %all-to-all-start.1 = ((bf16[4,320,256]{2,1,0:T(8,128)(2,1)}), bf16[4,320,256]{2,1,0:T(8,128)(2,1)S(1)}, u32[]{:S(2)}, u32[]{:S(2)}) async-start(bf16[4,320,256]{2,1,0:T(8,128)(2,1)} %bitcast.25), calls=%async_computation.1 | async-start | bytes 1310720 | tf_op jit(solution)/shard_map/all_to_all | solution.py:678
  401.2 32.0 %collective-permute-start.14 = (bf16[4,160,960]{2,1,0:T(8,128)(2,1)}, bf16[4,160,960]{2,1,0:T(8,128)(2,1)}, u32[]{:S(2)}, u32[]{:S(2)}) collective-permute-start(bf16[4,160,960]{2,1,0:T(8,128)(2,1)} %all-gather.9.cloned.1.call-done), channel_id=1, source_target_pairs={{0,4},{4,0},{1,5},{5,1},{2,6},{6,2},{3,7},{7,3},{8,12},{12,8},{9,1... | collective-permute-start | bytes 3686408 | tf_op jit(solution)/shard_map/ppermute | solution.py:640
  405.6 67.0 %collective-permute-start.28 = (bf16[128,1280]{1,0:T(8,128)(2,1)}, bf16[128,1280]{1,0:T(8,128)(2,1)}, u32[]{:S(2)}, u32[]{:S(2)}) collective-permute-start(bf16[128,1280]{1,0:T(8,128)(2,1)} %dynamic-slice_bitcast_fusion.8), channel_id=1, source_target_pairs={{0,4},{4,0},{1,5},{5,1},{2,6},{6,2},{3,7},{7,3},{8,12},{12,8},{9,1... | collective-permute-start | bytes 983048 | tf_op jit(solution)/shard_map/ppermute | solution.py:640
  407.2 36.3 %collective-permute-start.15 = (bf16[256,1280]{1,0:T(8,128)(2,1)}, bf16[256,1280]{1,0:T(8,128)(2,1)}, u32[]{:S(2)}, u32[]{:S(2)}) collective-permute-start(bf16[256,1280]{1,0:T(8,128)(2,1)} %multiply_convert_fusion.2), channel_id=1, source_target_pairs={{0,1},{1,0},{2,3},{3,2},{4,5},{5,4},{6,7},{7,6},{8,9},{9,8},{10,11... | collective-permute-start | bytes 1966088 | tf_op jit(solution)/shard_map/ppermute | solution.py:640
  421.1 44.9 %collective-permute-start.18 = (bf16[4,40,3840]{2,1,0:T(8,128)(2,1)}, bf16[4,40,3840]{2,1,0:T(8,128)(2,1)S(1)}, u32[]{:S(2)}, u32[]{:S(2)}) collective-permute-start(bf16[4,40,3840]{2,1,0:T(8,128)(2,1)} %bitcast.40.refs_0_), channel_id=1, source_target_pairs={{0,4},{4,0},{1,5},{5,1},{2,6},{6,2},{3,7},{7,3},{8,12},{12,8},{9,1... | collective-permute-start | bytes 3686408 | tf_op jit(solution)/shard_map/ppermute | solution.py:640
  433.1 32.9 %collective-permute-start.19 = (bf16[4,40,3840]{2,1,0:T(8,128)(2,1)}, bf16[4,40,3840]{2,1,0:T(8,128)(2,1)}, u32[]{:S(2)}, u32[]{:S(2)}) collective-permute-start(bf16[4,40,3840]{2,1,0:T(8,128)(2,1)} %bitcast.40.refs_0_), channel_id=1, source_target_pairs={{0,2},{1,3},{2,0},{3,1},{4,6},{5,7},{6,4},{7,5},{8,10},{9,11},{10,... | collective-permute-start | bytes 3686408 | tf_op jit(solution)/shard_map/ppermute | solution.py:640
  472.6 260.0 %all-to-all-start.3 = ((bf16[4,320,256]{2,1,0:T(8,128)(2,1)}), bf16[4,320,256]{2,1,0:T(8,128)(2,1)S(1)}, u32[]{:S(2)}, u32[]{:S(2)}) async-start(bf16[4,320,256]{2,1,0:T(8,128)(2,1)} %bitcast.56), calls=%async_computation.3 | async-start | bytes 1310720 | tf_op jit(solution)/shard_map/all_to_all | solution.py:678
  804.2 30.6 %collective-permute-start.32 = (bf16[4,40,1920]{2,1,0:T(8,128)(2,1)S(1)}, bf16[4,40,1920]{2,1,0:T(8,128)(2,1)S(1)}, u32[]{:S(2)}, u32[]{:S(2)}) collective-permute-start(bf16[4,40,1920]{2,1,0:T(8,128)(2,1)S(1)} %get-tuple-element.128), channel_id=1, source_target_pairs={{0,4},{4,0},{1,5},{5,1},{2,6},{6,2},{3,7},{7,3},{8,12},{12,8},{9,1... | collective-permute-start | bytes 1843208 | tf_op jit(solution)/shard_map/ppermute | solution.py:640
  804.8 29.9 %collective-permute-start.33 = (bf16[4,40,1920]{2,1,0:T(8,128)(2,1)S(1)}, bf16[4,40,1920]{2,1,0:T(8,128)(2,1)S(1)}, u32[]{:S(2)}, u32[]{:S(2)}) collective-permute-start(bf16[4,40,1920]{2,1,0:T(8,128)(2,1)S(1)} %get-tuple-element.127), channel_id=1, source_target_pairs={{0,2},{1,3},{2,0},{3,1},{4,6},{5,7},{6,4},{7,5},{8,10},{9,11},{10,... | collective-permute-start | bytes 1843208 | tf_op jit(solution)/shard_map/ppermute | solution.py:640
  807.1 27.5 %collective-permute-start.31 = (bf16[2,128,1280]{2,1,0:T(8,128)(2,1)S(1)}, bf16[2,128,1280]{2,1,0:T(8,128)(2,1)S(1)}, u32[]{:S(2)}, u32[]{:S(2)}) collective-permute-start(bf16[2,128,1280]{2,1,0:T(8,128)(2,1)S(1)} %fusion.99), channel_id=1, source_target_pairs={{0,2},{1,3},{2,0},{3,1},{4,6},{5,7},{6,4},{7,5},{8,10},{9,11},{10,... | collective-permute-start | bytes 1966088 | tf_op jit(solution)/shard_map/ppermute | solution.py:640
  815.5 48.8 %collective-permute-start.36 = (bf16[4,160,960]{2,1,0:T(8,128)(2,1)}, bf16[4,160,960]{2,1,0:T(8,128)(2,1)}, u32[]{:S(2)}, u32[]{:S(2)}) collective-permute-start(bf16[4,160,960]{2,1,0:T(8,128)(2,1)} %fusion.96), channel_id=1, source_target_pairs={{0,4},{4,0},{1,5},{5,1},{2,6},{6,2},{3,7},{7,3},{8,12},{12,8},{9,1... | collective-permute-start | bytes 3686408 | tf_op jit(solution)/shard_map/ppermute | solution.py:640
  841.6 38.0 %collective-permute-start.34 = (bf16[4,40,3840]{2,1,0:T(8,128)(2,1)}, bf16[4,40,3840]{2,1,0:T(8,128)(2,1)}, u32[]{:S(2)}, u32[]{:S(2)}) collective-permute-start(bf16[4,40,3840]{2,1,0:T(8,128)(2,1)} %pad_maximum_fusion.6), channel_id=1, source_target_pairs={{0,4},{4,0},{1,5},{5,1},{2,6},{6,2},{3,7},{7,3},{8,12},{12,8},{9,1... | collective-permute-start | bytes 3686408 | tf_op jit(solution)/shard_map/ppermute | solution.py:640
  844.4 35.2 %collective-permute-start.35 = (bf16[4,40,3840]{2,1,0:T(8,128)(2,1)}, bf16[4,40,3840]{2,1,0:T(8,128)(2,1)}, u32[]{:S(2)}, u32[]{:S(2)}) collective-permute-start(bf16[4,40,3840]{2,1,0:T(8,128)(2,1)} %pad_maximum_fusion.7), channel_id=1, source_target_pairs={{0,2},{1,3},{2,0},{3,1},{4,6},{5,7},{6,4},{7,5},{8,10},{9,11},{10,... | collective-permute-start | bytes 3686408 | tf_op jit(solution)/shard_map/ppermute | solution.py:640
  849.7 29.9 %all-to-all-start.5 = ((bf16[4,320,256]{2,1,0:T(8,128)(2,1)}), bf16[4,320,256]{2,1,0:T(8,128)(2,1)S(1)}, u32[]{:S(2)}, u32[]{:S(2)}) async-start(bf16[4,320,256]{2,1,0:T(8,128)(2,1)} %bitcast.80), calls=%async_computation.5 | async-start | bytes 1310720 | tf_op jit(solution)/shard_map/all_to_all | solution.py:678
  853.2 181.2 %reduce-scatter.7.cloned.1.call-start = ((), (), s32[]{:S(2)}) async-start(), calls=%async_computation.15 | async-start | bytes 1638400 | tf_op jit(solution)/shard_map/reduce_scatter | solution.py:721
  879.6 28.8 %collective-permute-start.37 = (bf16[4,2,2,40,3840]{4,3,2,1,0:T(8,128)(2,1)}, bf16[4,2,2,40,3840]{4,3,2,1,0:T(8,128)(2,1)}, u32[]{:S(2)}, u32[]{:S(2)}) collective-permute-start(bf16[4,2,2,40,3840]{4,3,2,1,0:T(8,128)(2,1)} %get-tuple-element.78), channel_id=1, source_target_pairs={{0,1},{1,0},{2,3},{3,2},{4,5},{5,4},{6,7},{7,6},{8,9},{9,8},{10,11... | collective-permute-start | bytes 14745608 | tf_op jit(solution)/shard_map/ppermute | solution.py:640
  887.3 167.8 %reduce-scatter.5.cloned.1.call-start = ((), (), s32[]{:S(2)}) async-start(), calls=%async_computation.14 | async-start | bytes 1638400 | tf_op jit(solution)/shard_map/reduce_scatter | solution.py:721
  911.5 31.2 %collective-permute-start.43 = (bf16[4,160,960]{2,1,0:T(8,128)(2,1)S(1)}, bf16[4,160,960]{2,1,0:T(8,128)(2,1)S(1)}, u32[]{:S(2)}, u32[]{:S(2)}) collective-permute-start(bf16[4,160,960]{2,1,0:T(8,128)(2,1)S(1)} %fusion.97), channel_id=1, source_target_pairs={{0,4},{4,0},{1,5},{5,1},{2,6},{6,2},{3,7},{7,3},{8,12},{12,8},{9,1... | collective-permute-start | bytes 3686408 | tf_op jit(solution)/shard_map/ppermute | solution.py:640
  944.3 123.6 %reduce-scatter.11.cloned.1.call-start = ((), (), s32[]{:S(2)}) async-start(), calls=%async_computation.17 | async-start | bytes 1536000 | tf_op jit(solution)/shard_map/reduce_scatter | solution.py:721
  948.4 81.5 %collective-permute-start.27 = (bf16[128,1280]{1,0:T(8,128)(2,1)S(1)}, bf16[128,1280]{1,0:T(8,128)(2,1)}, u32[]{:S(2)}, u32[]{:S(2)}) collective-permute-start(bf16[128,1280]{1,0:T(8,128)(2,1)S(1)} %dynamic-slice_bitcast_fusion.9), channel_id=1, source_target_pairs={{0,4},{4,0},{1,5},{5,1},{2,6},{6,2},{3,7},{7,3},{8,12},{12,8},{9,1... | collective-permute-start | bytes 983048 | tf_op jit(solution)/shard_map/ppermute | solution.py:640
  969.8 32.1 %collective-permute-start.47 = (f32[2,80]{1,0:T(2,128)S(1)}, f32[2,80]{1,0:T(2,128)S(1)}, u32[]{:S(2)}, u32[]{:S(2)}) collective-permute-start(f32[2,80]{1,0:T(2,128)S(1)} %fusion.110), channel_id=1, source_target_pairs={{0,2},{1,3},{2,0},{3,1},{4,6},{5,7},{6,4},{7,5},{8,10},{9,11},{10,... | collective-permute-start | bytes 1928 | tf_op jit(solution)/shard_map/ppermute | solution.py:640
  997.4 41.5 %collective-permute-start.45 = (bf16[4,40,3840]{2,1,0:T(8,128)(2,1)}, bf16[4,40,3840]{2,1,0:T(8,128)(2,1)S(1)}, u32[]{:S(2)}, u32[]{:S(2)}) collective-permute-start(bf16[4,40,3840]{2,1,0:T(8,128)(2,1)} %pad_maximum_fusion.9), channel_id=1, source_target_pairs={{0,2},{1,3},{2,0},{3,1},{4,6},{5,7},{6,4},{7,5},{8,10},{9,11},{10,... | collective-permute-start | bytes 3686408 | tf_op jit(solution)/shard_map/ppermute | solution.py:640
  1000.4 39.5 %collective-permute-start.44 = (bf16[4,40,3840]{2,1,0:T(8,128)(2,1)}, bf16[4,40,3840]{2,1,0:T(8,128)(2,1)}, u32[]{:S(2)}, u32[]{:S(2)}) collective-permute-start(bf16[4,40,3840]{2,1,0:T(8,128)(2,1)} %pad_maximum_fusion.8), channel_id=1, source_target_pairs={{0,4},{4,0},{1,5},{5,1},{2,6},{6,2},{3,7},{7,3},{8,12},{12,8},{9,1... | collective-permute-start | bytes 3686408 | tf_op jit(solution)/shard_map/ppermute | solution.py:640
  1038.4 35.0 %reduce-scatter.9.cloned.1.call-start = ((), (), s32[]{:S(2)}) async-start(), calls=%async_computation.16 | async-start | bytes 1536000 | tf_op jit(solution)/shard_map/reduce_scatter | solution.py:721
  (120 other events, 1189.9 us)
Sparse Core Ops, SparseCore 0:
  25.3 32.0 all-gather.6
  59.5 30.2 all-gather.10
  91.4 30.3 all-gather.12
  123.8 31.7 all-gather.8
  887.5 30.1 reduce-scatter.6
  944.4 30.1 reduce-scatter.4
  976.9 28.8 reduce-scatter.10
  1043.7 29.6 reduce-scatter.8

commit v6 on v5

--- a/solution.py
+++ b/solution.py
@@ -589,40 +589,31 @@
 
 
 def assemble_kernel(place_ref, *refs):
-    pieces, whole_ref, sems = refs[:10], refs[10], refs[11]
+    pieces, whole_ref = refs[:10], refs[10]
     half = whole_ref.shape[-1] // 2
     blk, row, core = place_ref[0], place_ref[1], place_ref[2]
-    copies = []
     for i in range(2):
         at_core = core if i == 0 else 1 - core
         own, across, beside, one, two = pieces[5 * i : 5 * i + 5]
-        for piece, at_blk, at_row, columns in (
-            (own, blk, row, None),
-            (across, 1 - blk, row, None),
-            (beside, blk, 1 - row, None),
-            (one, 1 - blk, 1 - row, pl.ds(0, half)),
-            (two, 1 - blk, 1 - row, pl.ds(half, half)),
-        ):
-            target = whole_ref.at[:, at_blk, at_row, at_core]
-            if columns is not None:
-                target = whole_ref.at[:, at_blk, at_row, at_core, :, columns]
-            copies.append(pltpu.make_async_copy(piece, target, sems.at[len(copies)]))
-    for copy in copies:
-        copy.start()
-    for copy in copies:
-        copy.wait()
+        whole_ref[0, blk, row, at_core] = own[0]
+        whole_ref[0, 1 - blk, row, at_core] = across[0]
+        whole_ref[0, blk, 1 - row, at_core] = beside[0]
+        whole_ref[0, 1 - blk, 1 - row, at_core, :, :half] = one[0]
+        whole_ref[0, 1 - blk, 1 - row, at_core, :, half:] = two[0]
 
 
 def assemble(pieces):
     batch, own, columns = pieces[0].shape
+    specs = [
+        pl.BlockSpec((1, own, piece.shape[-1]), lambda i, at: (i, 0, 0)) for piece in pieces
+    ]
     whole = pl.pallas_call(
         assemble_kernel,
         grid_spec=pltpu.PrefetchScalarGridSpec(
             num_scalar_prefetch=1,
-            grid=(1,),
-            in_specs=[pl.BlockSpec(memory_space=pl.ANY)] * 10,
-            out_specs=pl.BlockSpec(memory_space=pl.ANY),
-            scratch_shapes=[pltpu.SemaphoreType.DMA((10,))],
+            grid=(batch,),
+            in_specs=specs,
+            out_specs=pl.BlockSpec((1, 2, 2, 2, own, columns), lambda i, at: (i, 0, 0, 0, 0, 0)),
         ),
         out_shape=jax.ShapeDtypeStruct((batch, 2, 2, 2, own, columns), BF16),
         compiler_params=KERNEL,
@@ -888,7 +879,10 @@
         later = columns_over_blk(
             lax.dot_general(normed_all, bars, (((0,), (1,)), ((), ())), preferred_element_type=F32)
         )
-        normed_grad, diagonal = tied(normed_grad, diagonal)
+        if layer == 0:
+            normed_grad, diagonal, later = tied(normed_grad, diagonal, later)
+        else:
+            normed_grad, diagonal = tied(normed_grad, diagonal)
         sent = neighbours_sent(cored, *diagonal)
         if layer == 0:
             dense_grad[0] = over_batch(own_sum(cored, *sent))

time: 1090 us -> 606 us (0.56)
  Pallas kernels: 546 us -> 74.4 us
    pallas_call x2, Pallas kernels: 487 us -> 15.5 us  [assemble(): pl.pallas_call(assemble_kernel, grid_spec=pltpu.PrefetchScalarGridSpec(nu...]
    ppermute x51, waiting for transfers between devices: 170 us -> 159 us  [swapped(): return lax.ppermute(array, axis, [(i, i ^ mask) for i in range(size)])]
    unnamed x170 -> x176, local copies, waits for them, and re-layouts: 27 us -> 26.9 us
  transfers between devices with their start and end apart: 67 -> 67, of which waited for: 24 -> 25; matrix products, arithmetic and copies ran while one was open for 13% -> 23% of each run, Pallas kernels for 50% -> 12%
where the time goes in v6:
time: 606 us; the launch traced here: 600 us
  waiting for transfers between devices  234 us (39%)
  local copies, waits for them, and re-layouts  84.5 us (14%)
  Pallas kernels  74.4 us (12%)
  starting transfers between devices  69.3 us (11%)
  other arithmetic  66.3 us (11%)
  matrix products  55.4 us (9%)
  between operations  16.3 us (3%)
    ppermute x51, waiting for transfers between devices, swapped(): return lax.ppermute(array, axis, [(i, i ^ mask) for i in range(size)])  159 us
    ppermute x51, starting transfers between devices, swapped(): return lax.ppermute(array, axis, [(i, i ^ mask) for i in range(size)])  39.3 us
    all_gather x4, waiting for transfers between devices, along_batch(): return lax.all_gather(piece, 'batch', axis=0, tiled=False)  34.8 us
    all_to_all x8, waiting for transfers between devices, over_head(): lax.all_to_all(parts, 'head', split_axis=0, concat_axis=0, tiled=True)  30.3 us
    all_to_all x8, starting transfers between devices, over_head(): lax.all_to_all(parts, 'head', split_axis=0, concat_axis=0, tiled=True)  29.2 us
    unnamed x176, local copies, waits for them, and re-layouts  26.9 us
    pallas_call x2, Pallas kernels, attend_back_rows(): pl.pallas_call(functools.partial(attend_back_kernel, token_rows), grid=(l...  23.5 us
    pallas_call x2, Pallas kernels, attend_rows(): pl.pallas_call(functools.partial(attend_kernel, token_rows), grid=(local_...  21 us
  transfers between devices with their start and end apart: 67, of which 25 were waited for; matrix products, arithmetic and copies ran while one was open for 23% of the time, Pallas kernels for 12%

profile of v6, /device:TPU:0, one launch (start us, length us, event | category | flops | bytes accessed | tf_op | source)
XLA Modules:
  0.0 600.3 jit_solution(5730581332150480913)
XLA Ops:
  19.1 5.3 all-to-all-done
  33.3 11.4 %collective-permute-done.3 = bf16[256,1280]{1,0:T(8,128)(2,1)S(1)} collective-permute-done((bf16[256,1280]{1,0:T(8,128)(2,1)S(1)}, bf16[256,1280]{1,0:T(8,128)(2,1)S(1)}, u32[]{:S(2)}, u32[]{:S(2)}) %collective-permute-start.3) | collective-permute-done | bytes 655392 | tf_op jit(solution)/shard_map/ppermute | solution.py:631
  50.5 6.9 %all-gather.7.cloned.1.call-done = bf16[4,160,964]{2,1,0:T(8,128)(2,1)} async-done(((bf16[1,160,964]{2,1,0:T(8,128)(2,1)}), bf16[4,160,964]{2,1,0:T(8,128)(2,1)}) %all-gather.7.cloned.1.call-update) | async-done | bytes 1233936 | tf_op jit(solution)/shard_map/all_gather | solution.py:682
  62.0 27.9 %all-gather.11.cloned.1.call-done = bf16[160,3840]{1,0:T(8,128)(2,1)} async-done(((bf16[40,3840]{1,0:T(8,128)(2,1)}), bf16[160,3840]{1,0:T(8,128)(2,1)}) %all-gather.11.cloned.1.call-update) | async-done | bytes 1228816 | tf_op jit(solution)/shard_map/all_gather | solution.py:682
  105.2 4.7 fusion.116.proj_ref
  109.9 10.5 %shard_map.169 = (bf16[4,4,80,256]{3,2,1,0:T(8,128)(2,1)}, f32[4,1,1024]{2,1,0:T(1,128)S(1)}) custom-call(f32[3,4,80,1024]{3,2,1,0:T(8,128)} %fusion.116.proj_ref, f32[80,1]{1,0:T(8,128)S(1)} %copy.92.scale_ref, s32[1024,1]{1,0:T(8,128)S(1)} %copy.93.col_ref, s32[1,1024]{1,0:T(1,128)S(1)} %constant_dynamic-slice_fusion.6.row_ref), custom_call_target="tpu_custom_call" | custom-call | flops 1048576 | bytes 1048576 | tf_op jit(solution)/shard_map/pallas_call | solution.py:409
  124.6 13.4 %collective-permute-done.7.refs_3_ = bf16[4,40,1920]{2,1,0:T(8,128)(2,1)S(1)} collective-permute-done((bf16[4,40,1920]{2,1,0:T(8,128)(2,1)S(1)}, bf16[4,40,1920]{2,1,0:T(8,128)(2,1)S(1)}, u32[]{:S(2)}, u32[]{:S(2)}) %collective-permute-start.7) | collective-permute-done | bytes 614432 | tf_op jit(solution)/shard_map/ppermute | solution.py:631
  144.2 7.8 %shard_map.170 = bf16[4,2,2,2,40,3840]{5,4,3,2,1,0:T(8,128)(2,1)} custom-call(s32[3]{0:T(128)S(1)} %pad_add_fusion.place_ref, bf16[4,40,3840]{2,1,0:T(8,128)(2,1)S(1)} %bitcast.271, bf16[4,40,3840]{2,1,0:T(8,128)(2,1)} %collective-permute-done.5.refs_1_, bf16[4,40,3840]{2,1,0:T(8,128)(2,1)} %collective-permute-done.6.refs_2_, ...), custom_call_target="tpu_custom_call" | custom-call | flops 1048576 | bytes 1048576 | tf_op jit(solution)/shard_map/pallas_call | solution.py:610
  172.4 13.7 %collective-permute-done.16 = bf16[256,1280]{1,0:T(8,128)(2,1)} collective-permute-done((bf16[256,1280]{1,0:T(8,128)(2,1)}, bf16[256,1280]{1,0:T(8,128)(2,1)}, u32[]{:S(2)}, u32[]{:S(2)}) %collective-permute-start.16) | collective-permute-done | bytes 655392 | tf_op jit(solution)/shard_map/ppermute | solution.py:631
  188.6 11.5 %collective-permute-done.14 = bf16[4,160,960]{2,1,0:T(8,128)(2,1)} collective-permute-done((bf16[4,160,960]{2,1,0:T(8,128)(2,1)}, bf16[4,160,960]{2,1,0:T(8,128)(2,1)}, u32[]{:S(2)}, u32[]{:S(2)}) %collective-permute-start.14) | collective-permute-done | bytes 1228832 | tf_op jit(solution)/shard_map/ppermute | solution.py:631
  213.7 4.6 fusion.117.proj_ref
  218.3 10.5 %shard_map.171 = (bf16[4,4,80,256]{3,2,1,0:T(8,128)(2,1)}, f32[4,1,1024]{2,1,0:T(1,128)S(1)}) custom-call(f32[3,4,80,1024]{3,2,1,0:T(8,128)} %fusion.117.proj_ref, f32[80,1]{1,0:T(8,128)S(1)} %copy.98.scale_ref, s32[1024,1]{1,0:T(8,128)S(1)} %copy.93.col_ref, s32[1,1024]{1,0:T(1,128)S(1)} %constant_dynamic-slice_fusion.6.row_ref), custom_call_target="tpu_custom_call" | custom-call | flops 1048576 | bytes 1048576 | tf_op jit(solution)/shard_map/pallas_call | solution.py:409
  241.6 9.3 %collective-permute-done.20.refs_3_ = bf16[4,40,1920]{2,1,0:T(8,128)(2,1)S(1)} collective-permute-done((bf16[4,40,1920]{2,1,0:T(8,128)(2,1)}, bf16[4,40,1920]{2,1,0:T(8,128)(2,1)S(1)}, u32[]{:S(2)}, u32[]{:S(2)}) %collective-permute-start.20) | collective-permute-done | bytes 614432 | tf_op jit(solution)/shard_map/ppermute | solution.py:631
  254.1 7.8 %shard_map.172 = bf16[4,2,2,2,40,3840]{5,4,3,2,1,0:T(8,128)(2,1)} custom-call(s32[3]{0:T(128)S(1)} %pad_add_fusion.place_ref, bf16[4,40,3840]{2,1,0:T(8,128)(2,1)} %bitcast.40.refs_0_, bf16[4,40,3840]{2,1,0:T(8,128)(2,1)} %copy-done.48, bf16[4,40,3840]{2,1,0:T(8,128)(2,1)} %collective-permute-done.19.refs_2_, ...), custom_call_target="tpu_custom_call" | custom-call | flops 1048576 | bytes 1048576 | tf_op jit(solution)/shard_map/pallas_call | solution.py:610
  265.9 4.5 multiply_convert_fusion
  283.2 7.2 %shard_map.173 = (bf16[4,2,2,40,3840]{4,3,2,1,0:T(8,128)(2,1)}, bf16[4,2,2,40,3840]{4,3,2,1,0:T(8,128)(2,1)}) custom-call(s32[1]{0:T(128)} %bitcast.33.core_ref, bf16[1280,256]{1,0:T(8,128)(2,1)S(1)} %bitcast.264, bf16[256,1280]{1,0:T(8,128)(2,1)S(1)} %multiply_convert_fusion.1.normed_ref, bf16[256,1280]{1,0:T(8,128)(2,1)S(1)} %copy-done.13, ...), custom_call_target="tpu_custom_call" | custom-call | flops 1048576 | bytes 1048576 | tf_op jit(solution)/shard_map/pallas_call | solution.py:571
  290.3 5.0 copy.102
  295.8 4.5 copy.106
  300.3 11.7 %shard_map.174 = (bf16[3,4,80,1024]{3,2,1,0:T(8,128)(2,1)S(1)}, f32[80,128]{1,0:T(8,128)S(1)}) custom-call(f32[3,4,80,1024]{3,2,1,0:T(8,128)} %fusion.117.proj_ref, bf16[4,4,80,256]{3,2,1,0:T(8,128)(2,1)} %bitcast.70.grad_ref, f32[4,1,1024]{2,1,0:T(1,128)S(1)} %get-tuple-element.67.lse_ref, f32[80,1]{1,0:T(8,128)S(1)} %copy.98.scale_ref, ...), custom_call_target="tpu_custom_call" | custom-call | flops 1048576 | bytes 1048576 | tf_op jit(solution)/shard_map/pallas_call | solution.py:502
  313.3 5.9 dot_general.90
  319.3 5.5 fusion.84
  346.1 17.8 %collective-permute-done.31 = bf16[2,128,1280]{2,1,0:T(8,128)(2,1)S(1)} collective-permute-done((bf16[2,128,1280]{2,1,0:T(8,128)(2,1)S(1)}, bf16[2,128,1280]{2,1,0:T(8,128)(2,1)S(1)}, u32[]{:S(2)}, u32[]{:S(2)}) %collective-permute-start.31) | collective-permute-done | bytes 655392 | tf_op jit(solution)/shard_map/ppermute | solution.py:631
  386.2 7.2 %shard_map.175 = (bf16[4,2,2,40,3840]{4,3,2,1,0:T(8,128)(2,1)}, bf16[4,2,2,40,3840]{4,3,2,1,0:T(8,128)(2,1)}) custom-call(s32[1]{0:T(128)} %bitcast.33.core_ref, bf16[1280,256]{1,0:T(8,128)(2,1)S(1)} %bitcast.262, bf16[256,1280]{1,0:T(8,128)(2,1)S(1)} %multiply_convert_fusion.4.normed_ref, bf16[256,1280]{1,0:T(8,128)(2,1)S(1)} %copy-done.12, ...), custom_call_target="tpu_custom_call" | custom-call | flops 1048576 | bytes 1048576 | tf_op jit(solution)/shard_map/pallas_call | solution.py:571
  393.4 15.4 %all-to-all-done.5 = bf16[4,320,256]{2,1,0:T(8,128)(2,1)S(1)} async-done(((bf16[4,320,256]{2,1,0:T(8,128)(2,1)}), bf16[4,320,256]{2,1,0:T(8,128)(2,1)S(1)}, u32[]{:S(2)}, u32[]{:S(2)}) %all-to-all-start.5) | async-done | bytes 655392 | tf_op jit(solution)/shard_map/all_to_all | solution.py:669
  421.4 11.8 %shard_map.176 = (bf16[3,4,80,1024]{3,2,1,0:T(8,128)(2,1)S(1)}, f32[80,128]{1,0:T(8,128)S(1)}) custom-call(f32[3,4,80,1024]{3,2,1,0:T(8,128)} %fusion.116.proj_ref, bf16[4,4,80,256]{3,2,1,0:T(8,128)(2,1)S(1)} %bitcast.265, f32[4,1,1024]{2,1,0:T(1,128)S(1)} %get-tuple-element.78.lse_ref, f32[80,1]{1,0:T(8,128)S(1)} %copy.92.scale_ref, ...), custom_call_target="tpu_custom_call" | custom-call | flops 1048576 | bytes 1048576 | tf_op jit(solution)/shard_map/pallas_call | solution.py:502
  438.7 5.1 add_convert_fusion
  455.7 13.6 %collective-permute-done.39 = bf16[2,128,1280]{2,1,0:T(8,128)(2,1)S(1)} collective-permute-done((bf16[2,128,1280]{2,1,0:T(8,128)(2,1)S(1)}, bf16[2,128,1280]{2,1,0:T(8,128)(2,1)S(1)}, u32[]{:S(2)}, u32[]{:S(2)}) %collective-permute-start.39) | collective-permute-done | bytes 655392 | tf_op jit(solution)/shard_map/ppermute | solution.py:631
  470.5 24.5 %collective-permute-done.40 = bf16[4,40,1920]{2,1,0:T(8,128)(2,1)S(1)} collective-permute-done((bf16[4,40,1920]{2,1,0:T(8,128)(2,1)S(1)}, bf16[4,40,1920]{2,1,0:T(8,128)(2,1)S(1)}, u32[]{:S(2)}, u32[]{:S(2)}) %collective-permute-start.40) | collective-permute-done | bytes 614432 | tf_op jit(solution)/shard_map/ppermute | solution.py:631
  514.1 27.3 %collective-permute-done.48 = f32[2,80]{1,0:T(2,128)S(1)} collective-permute-done((f32[2,80]{1,0:T(2,128)S(1)}, f32[2,80]{1,0:T(2,128)S(1)}, u32[]{:S(2)}, u32[]{:S(2)}) %collective-permute-start.48) | collective-permute-done | bytes 672 | tf_op jit(solution)/shard_map/ppermute | solution.py:631
  560.1 6.4 %collective-permute-done.43 = bf16[128,1280]{1,0:T(8,128)(2,1)} collective-permute-done((bf16[128,1280]{1,0:T(8,128)(2,1)S(1)}, bf16[128,1280]{1,0:T(8,128)(2,1)}, u32[]{:S(2)}, u32[]{:S(2)}) %collective-permute-start.43) | collective-permute-done | bytes 327712 | tf_op jit(solution)/shard_map/ppermute | solution.py:631
  572.2 5.6 all-to-all-done.6
  580.3 9.9 %reduce-scatter.9.cloned.1.call-done = bf16[1,40,3840]{2,1,0:T(8,128)(2,1)} async-done(((bf16[4,40,3840]{2,1,0:T(8,128)(2,1)}), bf16[1,40,3840]{2,1,0:T(8,128)(2,1)}) %reduce-scatter.9.cloned.1.call-update) | async-done | bytes 307216 | tf_op jit(solution)/shard_map/reduce_scatter | solution.py:712
  (455 shorter events, 250.0 us)
Async XLA Ops:
  17.7 39.7 %all-gather.7.cloned.1.call-start = ((), (), s32[]{:S(2)}) async-start(), calls=%async_computation.12 | async-start | bytes 1638400 | tf_op jit(solution)/shard_map/all_gather | solution.py:682
  25.2 64.7 %all-gather.11.cloned.1.call-start = ((), (), s32[]{:S(2)}) async-start(), calls=%async_computation.18 | async-start | bytes 1536000 | tf_op jit(solution)/shard_map/all_gather | solution.py:682
  26.1 132.6 %all-gather.13.cloned.1.call-start = ((), (), s32[]{:S(2)}) async-start(), calls=%async_computation.19 | async-start | bytes 1536000 | tf_op jit(solution)/shard_map/all_gather | solution.py:682
  32.5 126.2 %all-gather.9.cloned.1.call-start = ((), (), s32[]{:S(2)}) async-start(), calls=%async_computation.13 | async-start | bytes 1638400 | tf_op jit(solution)/shard_map/all_gather | solution.py:682
  57.4 35.4 %collective-permute-start.1 = (bf16[4,160,964]{2,1,0:T(8,128)(2,1)}, bf16[4,160,964]{2,1,0:T(8,128)(2,1)}, u32[]{:S(2)}, u32[]{:S(2)}) collective-permute-start(bf16[4,160,964]{2,1,0:T(8,128)(2,1)} %all-gather.7.cloned.1.call-done), channel_id=1, source_target_pairs={{0,4},{4,0},{1,5},{5,1},{2,6},{6,2},{3,7},{7,3},{8,12},{12,8},{9,1... | collective-permute-start | bytes 3701768 | tf_op jit(solution)/shard_map/ppermute | solution.py:631
  89.9 30.5 %collective-permute-start.5 = (bf16[4,40,3840]{2,1,0:T(8,128)(2,1)}, bf16[4,40,3840]{2,1,0:T(8,128)(2,1)}, u32[]{:S(2)}, u32[]{:S(2)}) collective-permute-start(bf16[4,40,3840]{2,1,0:T(8,128)(2,1)} %bitcast.268), channel_id=1, source_target_pairs={{0,4},{4,0},{1,5},{5,1},{2,6},{6,2},{3,7},{7,3},{8,12},{12,8},{9,1... | collective-permute-start | bytes 3686408 | tf_op jit(solution)/shard_map/ppermute | solution.py:631
  91.3 29.1 %collective-permute-start.6 = (bf16[4,40,3840]{2,1,0:T(8,128)(2,1)}, bf16[4,40,3840]{2,1,0:T(8,128)(2,1)}, u32[]{:S(2)}, u32[]{:S(2)}) collective-permute-start(bf16[4,40,3840]{2,1,0:T(8,128)(2,1)} %bitcast.269), channel_id=1, source_target_pairs={{0,2},{1,3},{2,0},{3,1},{4,6},{5,7},{6,4},{7,5},{8,10},{9,11},{10,... | collective-permute-start | bytes 3686408 | tf_op jit(solution)/shard_map/ppermute | solution.py:631
  92.8 51.3 %collective-permute-start.9 = (bf16[4,40,3840]{2,1,0:T(8,128)(2,1)}, bf16[4,40,3840]{2,1,0:T(8,128)(2,1)}, u32[]{:S(2)}, u32[]{:S(2)}) collective-permute-start(bf16[4,40,3840]{2,1,0:T(8,128)(2,1)} %bitcast.270), channel_id=1, source_target_pairs={{0,1},{1,0},{2,3},{3,2},{4,5},{5,4},{6,7},{7,6},{8,9},{9,8},{10,11... | collective-permute-start | bytes 3686408 | tf_op jit(solution)/shard_map/ppermute | solution.py:631
  168.0 32.1 %collective-permute-start.14 = (bf16[4,160,960]{2,1,0:T(8,128)(2,1)}, bf16[4,160,960]{2,1,0:T(8,128)(2,1)}, u32[]{:S(2)}, u32[]{:S(2)}) collective-permute-start(bf16[4,160,960]{2,1,0:T(8,128)(2,1)} %all-gather.9.cloned.1.call-done), channel_id=1, source_target_pairs={{0,4},{4,0},{1,5},{5,1},{2,6},{6,2},{3,7},{7,3},{8,12},{12,8},{9,1... | collective-permute-start | bytes 3686408 | tf_op jit(solution)/shard_map/ppermute | solution.py:631
  170.8 66.9 %collective-permute-start.28 = (bf16[128,1280]{1,0:T(8,128)(2,1)}, bf16[128,1280]{1,0:T(8,128)(2,1)}, u32[]{:S(2)}, u32[]{:S(2)}) collective-permute-start(bf16[128,1280]{1,0:T(8,128)(2,1)} %dynamic-slice_bitcast_fusion.9), channel_id=1, source_target_pairs={{0,4},{4,0},{1,5},{5,1},{2,6},{6,2},{3,7},{7,3},{8,12},{12,8},{9,1... | collective-permute-start | bytes 983048 | tf_op jit(solution)/shard_map/ppermute | solution.py:631
  172.4 36.3 %collective-permute-start.15 = (bf16[256,1280]{1,0:T(8,128)(2,1)}, bf16[256,1280]{1,0:T(8,128)(2,1)}, u32[]{:S(2)}, u32[]{:S(2)}) collective-permute-start(bf16[256,1280]{1,0:T(8,128)(2,1)} %multiply_convert_fusion.2), channel_id=1, source_target_pairs={{0,1},{1,0},{2,3},{3,2},{4,5},{5,4},{6,7},{7,6},{8,9},{9,8},{10,11... | collective-permute-start | bytes 1966088 | tf_op jit(solution)/shard_map/ppermute | solution.py:631
  187.2 44.9 %collective-permute-start.18 = (bf16[4,40,3840]{2,1,0:T(8,128)(2,1)}, bf16[4,40,3840]{2,1,0:T(8,128)(2,1)S(1)}, u32[]{:S(2)}, u32[]{:S(2)}) collective-permute-start(bf16[4,40,3840]{2,1,0:T(8,128)(2,1)} %bitcast.40.refs_0_), channel_id=1, source_target_pairs={{0,4},{4,0},{1,5},{5,1},{2,6},{6,2},{3,7},{7,3},{8,12},{12,8},{9,1... | collective-permute-start | bytes 3686408 | tf_op jit(solution)/shard_map/ppermute | solution.py:631
  200.1 32.0 %collective-permute-start.19 = (bf16[4,40,3840]{2,1,0:T(8,128)(2,1)}, bf16[4,40,3840]{2,1,0:T(8,128)(2,1)}, u32[]{:S(2)}, u32[]{:S(2)}) collective-permute-start(bf16[4,40,3840]{2,1,0:T(8,128)(2,1)} %bitcast.40.refs_0_), channel_id=1, source_target_pairs={{0,2},{1,3},{2,0},{3,1},{4,6},{5,7},{6,4},{7,5},{8,10},{9,11},{10,... | collective-permute-start | bytes 3686408 | tf_op jit(solution)/shard_map/ppermute | solution.py:631
  333.4 30.6 %collective-permute-start.32 = (bf16[4,40,1920]{2,1,0:T(8,128)(2,1)S(1)}, bf16[4,40,1920]{2,1,0:T(8,128)(2,1)S(1)}, u32[]{:S(2)}, u32[]{:S(2)}) collective-permute-start(bf16[4,40,1920]{2,1,0:T(8,128)(2,1)S(1)} %get-tuple-element.132), channel_id=1, source_target_pairs={{0,4},{4,0},{1,5},{5,1},{2,6},{6,2},{3,7},{7,3},{8,12},{12,8},{9,1... | collective-permute-start | bytes 1843208 | tf_op jit(solution)/shard_map/ppermute | solution.py:631
  334.0 29.9 %collective-permute-start.33 = (bf16[4,40,1920]{2,1,0:T(8,128)(2,1)S(1)}, bf16[4,40,1920]{2,1,0:T(8,128)(2,1)S(1)}, u32[]{:S(2)}, u32[]{:S(2)}) collective-permute-start(bf16[4,40,1920]{2,1,0:T(8,128)(2,1)S(1)} %get-tuple-element.131), channel_id=1, source_target_pairs={{0,2},{1,3},{2,0},{3,1},{4,6},{5,7},{6,4},{7,5},{8,10},{9,11},{10,... | collective-permute-start | bytes 1843208 | tf_op jit(solution)/shard_map/ppermute | solution.py:631
  336.3 27.6 %collective-permute-start.31 = (bf16[2,128,1280]{2,1,0:T(8,128)(2,1)S(1)}, bf16[2,128,1280]{2,1,0:T(8,128)(2,1)S(1)}, u32[]{:S(2)}, u32[]{:S(2)}) collective-permute-start(bf16[2,128,1280]{2,1,0:T(8,128)(2,1)S(1)} %fusion.98), channel_id=1, source_target_pairs={{0,2},{1,3},{2,0},{3,1},{4,6},{5,7},{6,4},{7,5},{8,10},{9,11},{10,... | collective-permute-start | bytes 1966088 | tf_op jit(solution)/shard_map/ppermute | solution.py:631
  344.6 48.7 %collective-permute-start.36 = (bf16[4,160,960]{2,1,0:T(8,128)(2,1)}, bf16[4,160,960]{2,1,0:T(8,128)(2,1)}, u32[]{:S(2)}, u32[]{:S(2)}) collective-permute-start(bf16[4,160,960]{2,1,0:T(8,128)(2,1)} %fusion.95), channel_id=1, source_target_pairs={{0,4},{4,0},{1,5},{5,1},{2,6},{6,2},{3,7},{7,3},{8,12},{12,8},{9,1... | collective-permute-start | bytes 3686408 | tf_op jit(solution)/shard_map/ppermute | solution.py:631
  370.8 37.9 %collective-permute-start.34 = (bf16[4,40,3840]{2,1,0:T(8,128)(2,1)}, bf16[4,40,3840]{2,1,0:T(8,128)(2,1)}, u32[]{:S(2)}, u32[]{:S(2)}) collective-permute-start(bf16[4,40,3840]{2,1,0:T(8,128)(2,1)} %pad_maximum_fusion.6), channel_id=1, source_target_pairs={{0,4},{4,0},{1,5},{5,1},{2,6},{6,2},{3,7},{7,3},{8,12},{12,8},{9,1... | collective-permute-start | bytes 3686408 | tf_op jit(solution)/shard_map/ppermute | solution.py:631
  373.5 35.2 %collective-permute-start.35 = (bf16[4,40,3840]{2,1,0:T(8,128)(2,1)}, bf16[4,40,3840]{2,1,0:T(8,128)(2,1)}, u32[]{:S(2)}, u32[]{:S(2)}) collective-permute-start(bf16[4,40,3840]{2,1,0:T(8,128)(2,1)} %pad_maximum_fusion.7), channel_id=1, source_target_pairs={{0,2},{1,3},{2,0},{3,1},{4,6},{5,7},{6,4},{7,5},{8,10},{9,11},{10,... | collective-permute-start | bytes 3686408 | tf_op jit(solution)/shard_map/ppermute | solution.py:631
  378.9 29.9 %all-to-all-start.5 = ((bf16[4,320,256]{2,1,0:T(8,128)(2,1)}), bf16[4,320,256]{2,1,0:T(8,128)(2,1)S(1)}, u32[]{:S(2)}, u32[]{:S(2)}) async-start(bf16[4,320,256]{2,1,0:T(8,128)(2,1)} %bitcast.80), calls=%async_computation.5 | async-start | bytes 1310720 | tf_op jit(solution)/shard_map/all_to_all | solution.py:669
  382.4 164.5 %reduce-scatter.7.cloned.1.call-start = ((), (), s32[]{:S(2)}) async-start(), calls=%async_computation.15 | async-start | bytes 1638400 | tf_op jit(solution)/shard_map/reduce_scatter | solution.py:712
  408.8 24.5 %collective-permute-start.37 = (bf16[4,2,2,40,3840]{4,3,2,1,0:T(8,128)(2,1)}, bf16[4,2,2,40,3840]{4,3,2,1,0:T(8,128)(2,1)}, u32[]{:S(2)}, u32[]{:S(2)}) collective-permute-start(bf16[4,2,2,40,3840]{4,3,2,1,0:T(8,128)(2,1)} %get-tuple-element.80), channel_id=1, source_target_pairs={{0,1},{1,0},{2,3},{3,2},{4,5},{5,4},{6,7},{7,6},{8,9},{9,8},{10,11... | collective-permute-start | bytes 14745608 | tf_op jit(solution)/shard_map/ppermute | solution.py:631
  421.4 146.2 %reduce-scatter.5.cloned.1.call-start = ((), (), s32[]{:S(2)}) async-start(), calls=%async_computation.14 | async-start | bytes 1638400 | tf_op jit(solution)/shard_map/reduce_scatter | solution.py:712
  450.6 44.4 %collective-permute-start.42 = (bf16[4,160,960]{2,1,0:T(8,128)(2,1)S(1)}, bf16[4,160,960]{2,1,0:T(8,128)(2,1)S(1)}, u32[]{:S(2)}, u32[]{:S(2)}) collective-permute-start(bf16[4,160,960]{2,1,0:T(8,128)(2,1)S(1)} %fusion.96), channel_id=1, source_target_pairs={{0,4},{4,0},{1,5},{5,1},{2,6},{6,2},{3,7},{7,3},{8,12},{12,8},{9,1... | collective-permute-start | bytes 3686408 | tf_op jit(solution)/shard_map/ppermute | solution.py:631
  453.5 41.5 %collective-permute-start.40 = (bf16[4,40,1920]{2,1,0:T(8,128)(2,1)S(1)}, bf16[4,40,1920]{2,1,0:T(8,128)(2,1)S(1)}, u32[]{:S(2)}, u32[]{:S(2)}) collective-permute-start(bf16[4,40,1920]{2,1,0:T(8,128)(2,1)S(1)} %get-tuple-element.130), channel_id=1, source_target_pairs={{0,4},{4,0},{1,5},{5,1},{2,6},{6,2},{3,7},{7,3},{8,12},{12,8},{9,1... | collective-permute-start | bytes 1843208 | tf_op jit(solution)/shard_map/ppermute | solution.py:631
  455.0 40.0 %collective-permute-start.41 = (bf16[4,40,1920]{2,1,0:T(8,128)(2,1)S(1)}, bf16[4,40,1920]{2,1,0:T(8,128)(2,1)S(1)}, u32[]{:S(2)}, u32[]{:S(2)}) collective-permute-start(bf16[4,40,1920]{2,1,0:T(8,128)(2,1)S(1)} %get-tuple-element.129), channel_id=1, source_target_pairs={{0,2},{1,3},{2,0},{3,1},{4,6},{5,7},{6,4},{7,5},{8,10},{9,11},{10,... | collective-permute-start | bytes 1843208 | tf_op jit(solution)/shard_map/ppermute | solution.py:631
  497.5 82.8 %reduce-scatter.11.cloned.1.call-start = ((), (), s32[]{:S(2)}) async-start(), calls=%async_computation.17 | async-start | bytes 1536000 | tf_op jit(solution)/shard_map/reduce_scatter | solution.py:712
  501.6 40.7 %collective-permute-start.27 = (bf16[128,1280]{1,0:T(8,128)(2,1)S(1)}, bf16[128,1280]{1,0:T(8,128)(2,1)}, u32[]{:S(2)}, u32[]{:S(2)}) collective-permute-start(bf16[128,1280]{1,0:T(8,128)(2,1)S(1)} %dynamic-slice_bitcast_fusion.10), channel_id=1, source_target_pairs={{0,4},{4,0},{1,5},{5,1},{2,6},{6,2},{3,7},{7,3},{8,12},{12,8},{9,1... | collective-permute-start | bytes 983048 | tf_op jit(solution)/shard_map/ppermute | solution.py:631
  509.5 41.3 %collective-permute-start.45 = (bf16[4,40,3840]{2,1,0:T(8,128)(2,1)}, bf16[4,40,3840]{2,1,0:T(8,128)(2,1)}, u32[]{:S(2)}, u32[]{:S(2)}) collective-permute-start(bf16[4,40,3840]{2,1,0:T(8,128)(2,1)} %pad_maximum_fusion.9), channel_id=1, source_target_pairs={{0,2},{1,3},{2,0},{3,1},{4,6},{5,7},{6,4},{7,5},{8,10},{9,11},{10,... | collective-permute-start | bytes 3686408 | tf_op jit(solution)/shard_map/ppermute | solution.py:631
  512.0 38.8 %collective-permute-start.44 = (bf16[4,40,3840]{2,1,0:T(8,128)(2,1)}, bf16[4,40,3840]{2,1,0:T(8,128)(2,1)}, u32[]{:S(2)}, u32[]{:S(2)}) collective-permute-start(bf16[4,40,3840]{2,1,0:T(8,128)(2,1)} %pad_maximum_fusion.8), channel_id=1, source_target_pairs={{0,4},{4,0},{1,5},{5,1},{2,6},{6,2},{3,7},{7,3},{8,12},{12,8},{9,1... | collective-permute-start | bytes 3686408 | tf_op jit(solution)/shard_map/ppermute | solution.py:631
  513.5 27.9 %collective-permute-start.48 = (f32[2,80]{1,0:T(2,128)S(1)}, f32[2,80]{1,0:T(2,128)S(1)}, u32[]{:S(2)}, u32[]{:S(2)}) collective-permute-start(f32[2,80]{1,0:T(2,128)S(1)} %fusion.138), channel_id=1, source_target_pairs={{0,4},{4,0},{1,5},{5,1},{2,6},{6,2},{3,7},{7,3},{8,12},{12,8},{9,1... | collective-permute-start | bytes 1928 | tf_op jit(solution)/shard_map/ppermute | solution.py:631
  550.3 39.9 %reduce-scatter.9.cloned.1.call-start = ((), (), s32[]{:S(2)}) async-start(), calls=%async_computation.16 | async-start | bytes 1536000 | tf_op jit(solution)/shard_map/reduce_scatter | solution.py:712
  (123 other events, 1197.9 us)
Sparse Core Ops, SparseCore 0:
  25.3 32.0 all-gather.6
  59.5 30.2 all-gather.10
  91.4 30.3 all-gather.12
  123.8 31.7 all-gather.8
  421.5 30.1 reduce-scatter.6
  497.6 29.9 reduce-scatter.4
  529.9 28.9 reduce-scatter.10
  561.3 28.8 reduce-scatter.8

commit v7 on v6

--- a/solution.py
+++ b/solution.py
@@ -653,16 +653,17 @@
     return ordered.reshape(4, 2, -1, width).transpose(1, 0, 2, 3).reshape(-1, width)
 
 
-def scatter_rows(rows):
-    width = rows.shape[-1]
-    me = lax.axis_index("head")
-    row, core = me // 2, me % 2
-    parts = rows.reshape(2, 2, 2, -1, width)
-    halves = pick(parts, core, 2) + swapped(
-        pick(parts, 1 - core, 2).astype(BF16), "head", 1
-    ).astype(F32)
+def scatter_core(rows):
+    core = lax.axis_index("head") % 2
+    parts = rows.reshape(2, 2, 2, -1, rows.shape[-1])
+    got = swapped(pick(parts, 1 - core, 2).astype(BF16), "head", 1).astype(F32)
+    return pick(parts, core, 2) + got
+
+
+def scatter_row(halves):
+    row = lax.axis_index("head") // 2
     got = swapped(pick(halves, 1 - row, 1).astype(BF16), "head", 2).astype(F32)
-    return (pick(halves, row, 1) + got).reshape(-1, width)
+    return (pick(halves, row, 1) + got).reshape(-1, halves.shape[-1])
 
 
 def over_head(parts):
@@ -682,10 +683,9 @@
     return lax.all_gather(piece, "batch", axis=0, tiled=False)
 
 
-def along_blk(along):
-    other = swapped(along, "blk", 1)
+def in_rows(along, across):
     first = lax.axis_index("blk") == 0
-    both = jnp.stack([jnp.where(first, along, other), jnp.where(first, other, along)], axis=1)
+    both = jnp.stack([jnp.where(first, along, across), jnp.where(first, across, along)], axis=1)
     return both.reshape(-1, along.shape[-1])
 
 
@@ -697,22 +697,22 @@
     return swapped(along, "blk", 1), swapped(along, "head", 2)
 
 
-def to_diagonal(across, beside):
-    half = across.shape[-1] // 2
-    return swapped(across[..., :half], "head", 2), swapped(beside[..., half:], "blk", 1)
-
-
-def columns_over_blk(grad):
-    blk = lax.axis_index("blk")
-    parts = grad.reshape(4, 2, -1, grad.shape[1])
-    return pick(parts, blk, 1), swapped(pick(parts, 1 - blk, 1).astype(BF16), "blk", 1)
+def to_beside(across):
+    return swapped(across[..., : across.shape[-1] // 2], "head", 2)
+
+
+def to_across(beside):
+    return swapped(beside[..., beside.shape[-1] // 2 :], "blk", 1)
 
 
 def over_batch(parts):
     return lax.psum_scatter(parts.astype(BF16), "batch", scatter_dimension=0, tiled=False)
 
 
-def columns_to_rows(summed):
+def columns_to_rows(halves):
+    blk = lax.axis_index("blk")
+    got = swapped(pick(halves, 1 - blk), "blk", 1).astype(F32)
+    summed = (pick(halves, blk).astype(F32) + got).astype(BF16)
     moved = over_head(summed.reshape(4, -1, summed.shape[-1]))
     rows = moved.shape[1]
     return moved.reshape(4, rows, 3, -1).transpose(1, 2, 0, 3).reshape(rows, -1).astype(F32)
@@ -787,46 +787,59 @@
     dense_own = [
         jnp.concatenate([out_weight[i], up_weight[i], down_weight[i]], axis=1) for i in (0, 1)
     ]
+    dense_along = along_batch(dense_own[0])
+    first_columns, dense_along = tied(first_columns, dense_along)
+    across, beside = to_neighbours(dense_along)
     along = along_batch(first_columns)
-    dense_along = [along_batch(dense_own[0]), None]
-    with_gains = along_blk(along)
+    along, dense_next = tied(along, dense_own[1])
+    dense_next = along_batch(dense_next)
+    qkv_across = swapped(along, "blk", 1)
+    one = to_beside(across)
+    qkv_across, beside_after = tied(qkv_across, beside)
+    with_gains = in_rows(along, qkv_across)
+    two = to_across(beside_after)
     qkvs = [with_gains[:, :part3], None]
     gains = with_gains[:, part3:].T.astype(F32)
-    near = [to_neighbours(dense_along[0]), None]
-    next_along = along_batch(qkv_columns(qkv_weight[1], None).reshape(-1, part3))
-    dense_along[1] = along_batch(dense_own[1])
+    pieces = [(dense_along, across, beside, one, two)]
+    next_columns = qkv_columns(qkv_weight[1], None).reshape(-1, part3)
+    next_columns, dense_next = tied(next_columns, dense_next)
+    next_along = along_batch(next_columns)
+    beside = swapped(dense_next, "head", 2)
+    two, dense_after = tied(two, dense_next)
+    across = swapped(dense_after, "blk", 1)
+    across, next_along = tied(across, next_along)
+    next_across = swapped(next_along, "blk", 1)
+    one = to_beside(across)
+    next_across, beside_after = tied(next_across, beside)
+    two = to_across(beside_after)
+    pieces.append((dense_next, across, beside, one, two))
 
     def dense_of(layer):
-        pieces = (dense_along[layer],) + near[layer] + to_diagonal(*near[layer])
-        return assemble(pieces + tuple(other_core(piece) for piece in pieces))
+        return assemble(pieces[layer] + tuple(other_core(piece) for piece in pieces[layer]))
 
     kept, denses = [], []
     for layer in range(layers):
-        qkv = qkvs[layer]
         normed, factor_one = normalize(stream, gains[layer])
         if layer == 0:
             normed_all = normalize(first_all.astype(F32), gains[0])[0].astype(BF16)
         else:
-            normed_all = gather_rows(normed.astype(BF16))
+            normed, next_across = tied(normed.astype(BF16), next_across)
+            normed_all = gather_rows(normed)
+            qkvs[1] = in_rows(next_along, next_across)
+        qkv = qkvs[layer]
         projected = lax.dot_general(
             qkv, normed_all, (((0,), (1,)), ((), ())), preferred_element_type=F32
         )
         attended, log_total = attend_rows(
             projected, scale_vecs[layer], segments, 4, token_rows
         )
-        if layer == 0:
-            attended, near[0] = tied(attended, near[0])
-        else:
-            attended, near[1] = tied(attended, near[1])
+        attended, late = tied(attended, pieces[layer][3:])
+        pieces[layer] = pieces[layer][:3] + late
         denses.append(dense_of(layer))
         dense = denses[layer]
         out_w, up_w, down_w = dense[:, :width], dense[:, width:-width], dense[:, -width:]
         attended_t = over_head(attended).reshape(width, -1)
         middle = stream + dot_rows(attended_t, out_w)
-        if layer == 0:
-            middle, next_along, dense_along[1] = tied(middle, next_along, dense_along[1])
-            qkvs[1] = along_blk(next_along)
-            near[1] = to_neighbours(dense_along[1])
         normed_two, factor_two = normalize(middle, gains[layers + layer])
         normed_two = normed_two.astype(BF16)
         hidden = dot(normed_two, up_w)
@@ -841,7 +854,7 @@
     layer_out = swap_halves(stream.astype(BF16).reshape(tokens.shape))
     upper = swap_halves(cotangent).reshape(-1, width).astype(F32)
 
-    qkv_grads, dense_grad, scale_grads = [None] * layers, [None] * layers, [None] * layers
+    qkv_sums, dense_grad, scale_grads = [None] * layers, [None] * layers, [None] * layers
     for layer in reversed(range(layers)):
         (
             stream, factor_one, normed_all, projected, log_total, attended_t, middle,
@@ -861,9 +874,9 @@
         attended_grad = over_head(dot_cols(out_w, out_bar).astype(BF16).reshape(4, -1, out_bar.shape[0]))
         grads, others = dense_grads(attended_t, normed_two, active, out_bar, up_bar, down_bar)
         if layer == 0:
-            attended_grad, others, sent, later = tied(attended_grad, others, sent, later)
-            dense_grad[1] = over_batch(own_sum(cored, *sent))
-            qkv_sum = over_batch(later[0] + later[1].astype(F32))
+            attended_grad, others, diagonal = tied(attended_grad, others, diagonal)
+            sent = neighbours_sent(cored, *diagonal)
+            last = cored
         else:
             attended_grad, others = tied(attended_grad, others)
         others = other_core(others)
@@ -872,22 +885,26 @@
         )
         bars, others = tied(bars, others)
         cored = (grads.astype(F32) + others.astype(F32)).astype(BF16)
-        diagonal = diagonal_sent(cored)
-        normed_grad = scatter_rows(
+        halves = scatter_core(
             lax.dot_general(bars, qkv, (((0,), (1,)), ((), ())), preferred_element_type=F32)
         )
-        later = columns_over_blk(
-            lax.dot_general(normed_all, bars, (((0,), (1,)), ((), ())), preferred_element_type=F32)
-        )
+        qkv_grad = lax.dot_general(
+            normed_all, bars, (((0,), (1,)), ((), ())), preferred_element_type=F32
+        )
+        qkv_sums[layer] = over_batch(qkv_grad.reshape(4, 2, -1, qkv_grad.shape[-1]))
         if layer == 0:
-            normed_grad, diagonal, later = tied(normed_grad, diagonal, later)
+            diagonal = diagonal_sent(cored)
+            halves, diagonal = tied(halves, diagonal)
+            normed_grad = scatter_row(halves)
+            normed_grad, sent = tied(normed_grad, sent)
+            dense_grad[1] = over_batch(own_sum(last, *sent))
+            sent = neighbours_sent(cored, *diagonal)
+            dense_grad[0] = over_batch(own_sum(cored, *sent))
+            qkv_grads = [columns_to_rows(part) for part in qkv_sums]
         else:
-            normed_grad, diagonal = tied(normed_grad, diagonal)
-        sent = neighbours_sent(cored, *diagonal)
-        if layer == 0:
-            dense_grad[0] = over_batch(own_sum(cored, *sent))
-            qkv_grads[1] = columns_to_rows(qkv_sum)
-            qkv_grads[0] = columns_to_rows(over_batch(later[0] + later[1].astype(F32)))
+            normed_grad = scatter_row(halves)
+            normed_grad, cored = tied(normed_grad, cored)
+            diagonal = diagonal_sent(cored)
         upper = middle_grad + lower_of(normed_grad, stream, factor_one, gains[layer])
     input_grad = swap_halves(upper.astype(BF16).reshape(tokens.shape)).astype(F32)
     scale_total = sum_all(jnp.stack(scale_grads))

time: 606 us -> 653 us (1.078)
  waiting for transfers between devices: 234 us -> 267 us
    ppermute x51, waiting for transfers between devices: 159 us -> 212 us  [swapped(): return lax.ppermute(array, axis, [(i, i ^ mask) for i in range(size)])]
    all_to_all x8, waiting for transfers between devices: 30.3 us -> 12.9 us  [over_head(): lax.all_to_all(parts, 'head', split_axis=0, concat_axis=0, tiled=True)]
    all_gather x4, waiting for transfers between devices: 34.8 us -> 26.9 us  [along_batch(): return lax.all_gather(piece, 'batch', axis=0, tiled=False)]
    unnamed x176 -> x162, local copies, waits for them, and re-layouts: 26.9 us -> 21.5 us
where the time goes in v7:
time: 653 us; the launch traced here: 646 us
  waiting for transfers between devices  267 us (41%)
  local copies, waits for them, and re-layouts  82.8 us (13%)
  starting transfers between devices  75.2 us (12%)
  Pallas kernels  74.3 us (11%)
  other arithmetic  68.9 us (11%)
  matrix products  61.7 us (9%)
  between operations  16.2 us (2%)
    ppermute x51, waiting for transfers between devices, swapped(): return lax.ppermute(array, axis, [(i, i ^ mask) for i in range(size)])  212 us
    ppermute x51, starting transfers between devices, swapped(): return lax.ppermute(array, axis, [(i, i ^ mask) for i in range(size)])  44.9 us
    all_to_all x8, starting transfers between devices, over_head(): lax.all_to_all(parts, 'head', split_axis=0, concat_axis=0, tiled=True)  29.5 us
    all_gather x4, waiting for transfers between devices, along_batch(): return lax.all_gather(piece, 'batch', axis=0, tiled=False)  26.9 us
    pallas_call x2, Pallas kernels, attend_back_rows(): pl.pallas_call(functools.partial(attend_back_kernel, token_rows), grid=(l...  23.6 us
    unnamed x162, local copies, waits for them, and re-layouts  21.5 us
    pallas_call x2, Pallas kernels, attend_rows(): pl.pallas_call(functools.partial(attend_kernel, token_rows), grid=(local_...  21 us
    pallas_call x2, Pallas kernels, assemble(): pl.pallas_call(assemble_kernel, grid_spec=pltpu.PrefetchScalarGridSpec(nu...  15.5 us
  transfers between devices with their start and end apart: 67, of which 25 were waited for; matrix products, arithmetic and copies ran while one was open for 23% of the time, Pallas kernels for 12%

profile of v7, /device:TPU:0, one launch (start us, length us, event | category | flops | bytes accessed | tf_op | source)
XLA Modules:
  0.0 645.8 jit_solution(192620878420114971)
XLA Ops:
  20.8 5.5 all-to-all-done
  26.3 19.6 %all-gather.9.cloned.1.call-done = bf16[160,3840]{1,0:T(8,128)(2,1)} async-done(((bf16[40,3840]{1,0:T(8,128)(2,1)}), bf16[160,3840]{1,0:T(8,128)(2,1)}) %all-gather.9.cloned.1.call-update) | async-done | bytes 1228816 | tf_op jit(solution)/shard_map/all_gather | solution.py:683
  53.3 10.4 %collective-permute-done.4 = bf16[256,1280]{1,0:T(8,128)(2,1)} collective-permute-done((bf16[256,1280]{1,0:T(8,128)(2,1)S(1)}, bf16[256,1280]{1,0:T(8,128)(2,1)}, u32[]{:S(2)}, u32[]{:S(2)}) %collective-permute-start.4) | collective-permute-done | bytes 655392 | tf_op jit(solution)/shard_map/ppermute | solution.py:631
  72.6 7.3 %all-gather.11.cloned.1.call-done = bf16[640,964]{1,0:T(8,128)(2,1)} async-done(((bf16[160,964]{1,0:T(8,128)(2,1)}), bf16[640,964]{1,0:T(8,128)(2,1)}) %all-gather.11.cloned.1.call-update) | async-done | bytes 1233936 | tf_op jit(solution)/shard_map/all_gather | solution.py:683
  85.2 15.9 %collective-permute-done.6.refs_1_ = bf16[4,40,3840]{2,1,0:T(8,128)(2,1)} collective-permute-done((bf16[4,40,3840]{2,1,0:T(8,128)(2,1)S(1)}, bf16[4,40,3840]{2,1,0:T(8,128)(2,1)}, u32[]{:S(2)}, u32[]{:S(2)}) %collective-permute-start.6) | collective-permute-done | bytes 1228832 | tf_op jit(solution)/shard_map/ppermute | solution.py:631
  104.4 23.7 %collective-permute-done.1 = bf16[4,160,964]{2,1,0:T(8,128)(2,1)} collective-permute-done((bf16[4,160,964]{2,1,0:T(8,128)(2,1)}, bf16[4,160,964]{2,1,0:T(8,128)(2,1)}, u32[]{:S(2)}, u32[]{:S(2)}) %collective-permute-start.1) | collective-permute-done | bytes 1233952 | tf_op jit(solution)/shard_map/ppermute | solution.py:631
  146.8 7.1 %fusion.114.proj_ref = f32[3,4,80,1024]{3,2,1,0:T(8,128)} fusion(bf16[3,4,80,1280]{3,2,1,0:T(8,128)(2,1)} %bitcast.324, bf16[1024,1280,1,1]{1,0,3,2:T(8,128)(2,1)} %bitcast.322), kind=kOutput, calls=%fused_computation.217 | convolution fusion | flops 2516582400 | bytes 9011200 | tf_op jit(solution)/shard_map/dot_general | solution.py:830
  153.9 10.5 %shard_map.169 = (bf16[4,4,80,256]{3,2,1,0:T(8,128)(2,1)}, f32[4,1,1024]{2,1,0:T(1,128)S(1)}) custom-call(f32[3,4,80,1024]{3,2,1,0:T(8,128)} %fusion.114.proj_ref, f32[80,1]{1,0:T(8,128)S(1)} %copy.65.scale_ref, s32[1024,1]{1,0:T(8,128)S(1)} %copy.66.col_ref, s32[1,1024]{1,0:T(1,128)S(1)} %constant_dynamic-slice_fusion.6.row_ref), custom_call_target="tpu_custom_call" | custom-call | flops 1048576 | bytes 1048576 | tf_op jit(solution)/shard_map/pallas_call | solution.py:409
  171.4 7.7 %shard_map.170 = bf16[4,2,2,2,40,3840]{5,4,3,2,1,0:T(8,128)(2,1)} custom-call(s32[3]{0:T(128)S(1)} %pad_add_fusion.place_ref, bf16[4,40,3840]{2,1,0:T(8,128)(2,1)S(1)} %bitcast.274, bf16[4,40,3840]{2,1,0:T(8,128)(2,1)} %collective-permute-done.6.refs_1_, bf16[4,40,3840]{2,1,0:T(8,128)(2,1)} %collective-permute-done.2.refs_2_, ...), custom_call_target="tpu_custom_call" | custom-call | flops 1048576 | bytes 1048576 | tf_op jit(solution)/shard_map/pallas_call | solution.py:610
  184.1 14.4 %collective-permute-done.14.refs_1_ = bf16[4,40,3840]{2,1,0:T(8,128)(2,1)} collective-permute-done((bf16[4,40,3840]{2,1,0:T(8,128)(2,1)}, bf16[4,40,3840]{2,1,0:T(8,128)(2,1)}, u32[]{:S(2)}, u32[]{:S(2)}) %collective-permute-start.14) | collective-permute-done | bytes 1228832 | tf_op jit(solution)/shard_map/ppermute | solution.py:631
  206.6 22.5 %collective-permute-done.15 = bf16[4,160,960]{2,1,0:T(8,128)(2,1)S(1)} collective-permute-done((bf16[4,160,960]{2,1,0:T(8,128)(2,1)}, bf16[4,160,960]{2,1,0:T(8,128)(2,1)S(1)}, u32[]{:S(2)}, u32[]{:S(2)}) %collective-permute-start.15) | collective-permute-done | bytes 1228832 | tf_op jit(solution)/shard_map/ppermute | solution.py:631
  230.4 14.2 %collective-permute-done.18 = bf16[256,1280]{1,0:T(8,128)(2,1)} collective-permute-done((bf16[256,1280]{1,0:T(8,128)(2,1)S(1)}, bf16[256,1280]{1,0:T(8,128)(2,1)}, u32[]{:S(2)}, u32[]{:S(2)}) %collective-permute-start.18) | collective-permute-done | bytes 655392 | tf_op jit(solution)/shard_map/ppermute | solution.py:631
  261.3 12.6 %collective-permute-done.20.refs_3_ = bf16[4,40,1920]{2,1,0:T(8,128)(2,1)S(1)} collective-permute-done((bf16[4,40,1920]{2,1,0:T(8,128)(2,1)S(1)}, bf16[4,40,1920]{2,1,0:T(8,128)(2,1)S(1)}, u32[]{:S(2)}, u32[]{:S(2)}) %collective-permute-start.20) | collective-permute-done | bytes 614432 | tf_op jit(solution)/shard_map/ppermute | solution.py:631
  280.0 10.5 %shard_map.171 = (bf16[4,4,80,256]{3,2,1,0:T(8,128)(2,1)}, f32[4,1,1024]{2,1,0:T(1,128)S(1)}) custom-call(f32[3,4,80,1024]{3,2,1,0:T(8,128)} %fusion.115.proj_ref, f32[80,1]{1,0:T(8,128)S(1)} %copy.71.scale_ref, s32[1024,1]{1,0:T(8,128)S(1)} %copy.66.col_ref, s32[1,1024]{1,0:T(1,128)S(1)} %constant_dynamic-slice_fusion.6.row_ref), custom_call_target="tpu_custom_call" | custom-call | flops 1048576 | bytes 1048576 | tf_op jit(solution)/shard_map/pallas_call | solution.py:409
  298.0 7.8 %shard_map.172 = bf16[4,2,2,2,40,3840]{5,4,3,2,1,0:T(8,128)(2,1)} custom-call(s32[3]{0:T(128)S(1)} %pad_add_fusion.place_ref, bf16[4,40,3840]{2,1,0:T(8,128)(2,1)} %bitcast.41.refs_0_, bf16[4,40,3840]{2,1,0:T(8,128)(2,1)} %collective-permute-done.14.refs_1_, bf16[4,40,3840]{2,1,0:T(8,128)(2,1)} %collective-permute-done.16.refs_2_, ...), custom_call_target="tpu_custom_call" | custom-call | flops 1048576 | bytes 1048576 | tf_op jit(solution)/shard_map/pallas_call | solution.py:610
  327.0 7.1 %shard_map.173 = (bf16[4,2,2,40,3840]{4,3,2,1,0:T(8,128)(2,1)}, bf16[4,2,2,40,3840]{4,3,2,1,0:T(8,128)(2,1)}) custom-call(s32[1]{0:T(128)} %bitcast.37.core_ref, bf16[1280,256]{1,0:T(8,128)(2,1)S(1)} %bitcast.267, bf16[256,1280]{1,0:T(8,128)(2,1)S(1)} %multiply_convert_fusion.1.normed_ref, bf16[256,1280]{1,0:T(8,128)(2,1)S(1)} %copy-done.13, ...), custom_call_target="tpu_custom_call" | custom-call | flops 1048576 | bytes 1048576 | tf_op jit(solution)/shard_map/pallas_call | solution.py:571
  334.1 5.0 copy.75
  339.5 11.7 %shard_map.174 = (bf16[3,4,80,1024]{3,2,1,0:T(8,128)(2,1)S(1)}, f32[80,128]{1,0:T(8,128)S(1)}) custom-call(f32[3,4,80,1024]{3,2,1,0:T(8,128)} %fusion.115.proj_ref, bf16[4,4,80,256]{3,2,1,0:T(8,128)(2,1)} %bitcast.72.grad_ref, f32[4,1,1024]{2,1,0:T(1,128)S(1)} %get-tuple-element.89.lse_ref, f32[80,1]{1,0:T(8,128)S(1)} %copy.71.scale_ref, ...), custom_call_target="tpu_custom_call" | custom-call | flops 1048576 | bytes 1048576 | tf_op jit(solution)/shard_map/pallas_call | solution.py:502
  352.6 5.9 dot_general.90
  358.5 5.4 fusion.82
  373.8 5.0 add_convert_fusion.1
  378.8 10.2 %collective-permute-done.31 = bf16[2,128,1280]{2,1,0:T(8,128)(2,1)S(1)} collective-permute-done((bf16[2,128,1280]{2,1,0:T(8,128)(2,1)S(1)}, bf16[2,128,1280]{2,1,0:T(8,128)(2,1)S(1)}, u32[]{:S(2)}, u32[]{:S(2)}) %collective-permute-start.31) | collective-permute-done | bytes 655392 | tf_op jit(solution)/shard_map/ppermute | solution.py:631
  413.7 7.2 %shard_map.175 = (bf16[4,2,2,40,3840]{4,3,2,1,0:T(8,128)(2,1)}, bf16[4,2,2,40,3840]{4,3,2,1,0:T(8,128)(2,1)}) custom-call(s32[1]{0:T(128)} %bitcast.37.core_ref, bf16[1280,256]{1,0:T(8,128)(2,1)S(1)} %bitcast.265, bf16[256,1280]{1,0:T(8,128)(2,1)S(1)} %multiply_convert_fusion.4.normed_ref, bf16[256,1280]{1,0:T(8,128)(2,1)S(1)} %copy-done.12, ...), custom_call_target="tpu_custom_call" | custom-call | flops 1048576 | bytes 1048576 | tf_op jit(solution)/shard_map/pallas_call | solution.py:571
  432.0 4.6 copy.85
  450.7 11.9 %shard_map.176 = (bf16[3,4,80,1024]{3,2,1,0:T(8,128)(2,1)S(1)}, f32[80,128]{1,0:T(8,128)S(1)}) custom-call(f32[3,4,80,1024]{3,2,1,0:T(8,128)} %fusion.114.proj_ref, bf16[4,4,80,256]{3,2,1,0:T(8,128)(2,1)S(1)} %bitcast.268, f32[4,1,1024]{2,1,0:T(1,128)S(1)} %get-tuple-element.99.lse_ref, f32[80,1]{1,0:T(8,128)S(1)} %copy.65.scale_ref, ...), custom_call_target="tpu_custom_call" | custom-call | flops 1048576 | bytes 1048576 | tf_op jit(solution)/shard_map/pallas_call | solution.py:502
  471.4 6.4 add_convert_fusion
  490.8 9.8 %collective-permute-done.36 = bf16[4,40,1920]{2,1,0:T(8,128)(2,1)S(1)} collective-permute-done((bf16[4,40,1920]{2,1,0:T(8,128)(2,1)S(1)}, bf16[4,40,1920]{2,1,0:T(8,128)(2,1)S(1)}, u32[]{:S(2)}, u32[]{:S(2)}) %collective-permute-start.36) | collective-permute-done | bytes 614432 | tf_op jit(solution)/shard_map/ppermute | solution.py:631
  506.2 35.9 %collective-permute-done.38 = bf16[2,128,1280]{2,1,0:T(8,128)(2,1)S(1)} collective-permute-done((bf16[2,128,1280]{2,1,0:T(8,128)(2,1)S(1)}, bf16[2,128,1280]{2,1,0:T(8,128)(2,1)S(1)}, u32[]{:S(2)}, u32[]{:S(2)}) %collective-permute-start.38) | collective-permute-done | bytes 655392 | tf_op jit(solution)/shard_map/ppermute | solution.py:631
  550.4 25.9 %collective-permute-done.48 = f32[2,80]{1,0:T(2,128)S(1)} collective-permute-done((f32[2,80]{1,0:T(2,128)S(1)}, f32[2,80]{1,0:T(2,128)S(1)}, u32[]{:S(2)}, u32[]{:S(2)}) %collective-permute-start.48) | collective-permute-done | bytes 672 | tf_op jit(solution)/shard_map/ppermute | solution.py:631
  599.3 6.8 %collective-permute-done.41 = bf16[128,1280]{1,0:T(8,128)(2,1)S(1)} collective-permute-done((bf16[128,1280]{1,0:T(8,128)(2,1)S(1)}, bf16[128,1280]{1,0:T(8,128)(2,1)S(1)}, u32[]{:S(2)}, u32[]{:S(2)}) %collective-permute-start.41) | collective-permute-done | bytes 327712 | tf_op jit(solution)/shard_map/ppermute | solution.py:631
  609.5 14.3 %reduce-scatter.9.cloned.1.call-done = bf16[1,40,3840]{2,1,0:T(8,128)(2,1)} async-done(((bf16[4,40,3840]{2,1,0:T(8,128)(2,1)}), bf16[1,40,3840]{2,1,0:T(8,128)(2,1)}) %reduce-scatter.9.cloned.1.call-update) | async-done | bytes 307216 | tf_op jit(solution)/shard_map/reduce_scatter | solution.py:709
  630.9 5.0 all-to-all-done.6
  (436 shorter events, 262.0 us)
Async XLA Ops:
  7.2 38.7 %all-gather.9.cloned.1.call-start = ((), (), s32[]{:S(2)}) async-start(), calls=%async_computation.16 | async-start | bytes 1536000 | tf_op jit(solution)/shard_map/all_gather | solution.py:683
  19.6 60.2 %all-gather.11.cloned.1.call-start = ((), (), s32[]{:S(2)}) async-start(), calls=%async_computation.17 | async-start | bytes 1638400 | tf_op jit(solution)/shard_map/all_gather | solution.py:683
  49.2 96.9 %all-to-all-start.2 = ((bf16[4,40,960]{2,1,0:T(8,128)(2,1)}), bf16[4,40,960]{2,1,0:T(8,128)(2,1)S(1)}, u32[]{:S(2)}, u32[]{:S(2)}) async-start(bf16[4,40,960]{2,1,0:T(8,128)(2,1)} %reshape.289), calls=%async_computation.2 | async-start | bytes 655360 | tf_op jit(solution)/shard_map/all_to_all | solution.py:670
  52.7 93.4 %all-gather.13.cloned.1.call-start = ((), (), s32[]{:S(2)}) async-start(), calls=%async_computation.18 | async-start | bytes 1536000 | tf_op jit(solution)/shard_map/all_gather | solution.py:683
  69.6 34.0 %collective-permute-start.2 = (bf16[4,40,3840]{2,1,0:T(8,128)(2,1)S(1)}, bf16[4,40,3840]{2,1,0:T(8,128)(2,1)}, u32[]{:S(2)}, u32[]{:S(2)}) collective-permute-start(bf16[4,40,3840]{2,1,0:T(8,128)(2,1)S(1)} %bitcast.271), channel_id=1, source_target_pairs={{0,2},{1,3},{2,0},{3,1},{4,6},{5,7},{6,4},{7,5},{8,10},{9,11},{10,... | collective-permute-start | bytes 3686408 | tf_op jit(solution)/shard_map/ppermute | solution.py:631
  71.1 30.0 %collective-permute-start.6 = (bf16[4,40,3840]{2,1,0:T(8,128)(2,1)S(1)}, bf16[4,40,3840]{2,1,0:T(8,128)(2,1)}, u32[]{:S(2)}, u32[]{:S(2)}) collective-permute-start(bf16[4,40,3840]{2,1,0:T(8,128)(2,1)S(1)} %bitcast.272), channel_id=1, source_target_pairs={{0,4},{4,0},{1,5},{5,1},{2,6},{6,2},{3,7},{7,3},{8,12},{12,8},{9,1... | collective-permute-start | bytes 3686408 | tf_op jit(solution)/shard_map/ppermute | solution.py:631
  79.9 48.2 %collective-permute-start.1 = (bf16[4,160,964]{2,1,0:T(8,128)(2,1)}, bf16[4,160,964]{2,1,0:T(8,128)(2,1)}, u32[]{:S(2)}, u32[]{:S(2)}) collective-permute-start(bf16[4,160,964]{2,1,0:T(8,128)(2,1)} %bitcast.333), channel_id=1, source_target_pairs={{0,4},{4,0},{1,5},{5,1},{2,6},{6,2},{3,7},{7,3},{8,12},{12,8},{9,1... | collective-permute-start | bytes 3701768 | tf_op jit(solution)/shard_map/ppermute | solution.py:631
  85.1 83.6 %collective-permute-start.9 = (bf16[4,40,3840]{2,1,0:T(8,128)(2,1)S(1)}, bf16[4,40,3840]{2,1,0:T(8,128)(2,1)}, u32[]{:S(2)}, u32[]{:S(2)}) collective-permute-start(bf16[4,40,3840]{2,1,0:T(8,128)(2,1)S(1)} %bitcast.273), channel_id=1, source_target_pairs={{0,1},{1,0},{2,3},{3,2},{4,5},{5,4},{6,7},{7,6},{8,9},{9,8},{10,11... | collective-permute-start | bytes 3686408 | tf_op jit(solution)/shard_map/ppermute | solution.py:631
  103.1 61.3 %collective-permute-start.7 = (bf16[4,40,1920]{2,1,0:T(8,128)(2,1)}, bf16[4,40,1920]{2,1,0:T(8,128)(2,1)S(1)}, u32[]{:S(2)}, u32[]{:S(2)}) collective-permute-start(bf16[4,40,1920]{2,1,0:T(8,128)(2,1)} %slice.187), channel_id=1, source_target_pairs={{0,2},{1,3},{2,0},{3,1},{4,6},{5,7},{6,4},{7,5},{8,10},{9,11},{10,... | collective-permute-start | bytes 1843208 | tf_op jit(solution)/shard_map/ppermute | solution.py:631
  103.6 65.8 %collective-permute-start.10 = (bf16[4,40,3840]{2,1,0:T(8,128)(2,1)}, bf16[4,40,3840]{2,1,0:T(8,128)(2,1)}, u32[]{:S(2)}, u32[]{:S(2)}) collective-permute-start(bf16[4,40,3840]{2,1,0:T(8,128)(2,1)} %collective-permute-done.6.refs_1_), channel_id=1, source_target_pairs={{0,1},{1,0},{2,3},{3,2},{4,5},{5,4},{6,7},{7,6},{8,9},{9,8},{10,11... | collective-permute-start | bytes 3686408 | tf_op jit(solution)/shard_map/ppermute | solution.py:631
  103.6 67.8 %collective-permute-start.11 = (bf16[4,40,3840]{2,1,0:T(8,128)(2,1)}, bf16[4,40,3840]{2,1,0:T(8,128)(2,1)}, u32[]{:S(2)}, u32[]{:S(2)}) collective-permute-start(bf16[4,40,3840]{2,1,0:T(8,128)(2,1)} %collective-permute-done.2.refs_2_), channel_id=1, source_target_pairs={{0,1},{1,0},{2,3},{3,2},{4,5},{5,4},{6,7},{7,6},{8,9},{9,8},{10,11... | collective-permute-start | bytes 3686408 | tf_op jit(solution)/shard_map/ppermute | solution.py:631
  104.2 94.4 %all-gather.15.cloned.1.call-start = ((), (), s32[]{:S(2)}) async-start(), calls=%async_computation.19 | async-start | bytes 1638400 | tf_op jit(solution)/shard_map/all_gather | solution.py:683
  168.7 29.8 %collective-permute-start.14 = (bf16[4,40,3840]{2,1,0:T(8,128)(2,1)}, bf16[4,40,3840]{2,1,0:T(8,128)(2,1)}, u32[]{:S(2)}, u32[]{:S(2)}) collective-permute-start(bf16[4,40,3840]{2,1,0:T(8,128)(2,1)} %bitcast.41.refs_0_), channel_id=1, source_target_pairs={{0,4},{4,0},{1,5},{5,1},{2,6},{6,2},{3,7},{7,3},{8,12},{12,8},{9,1... | collective-permute-start | bytes 3686408 | tf_op jit(solution)/shard_map/ppermute | solution.py:631
  169.4 37.2 %collective-permute-start.16 = (bf16[4,40,3840]{2,1,0:T(8,128)(2,1)}, bf16[4,40,3840]{2,1,0:T(8,128)(2,1)}, u32[]{:S(2)}, u32[]{:S(2)}) collective-permute-start(bf16[4,40,3840]{2,1,0:T(8,128)(2,1)} %bitcast.41.refs_0_), channel_id=1, source_target_pairs={{0,2},{1,3},{2,0},{3,1},{4,6},{5,7},{6,4},{7,5},{8,10},{9,11},{10,... | collective-permute-start | bytes 3686408 | tf_op jit(solution)/shard_map/ppermute | solution.py:631
  198.5 30.6 %collective-permute-start.15 = (bf16[4,160,960]{2,1,0:T(8,128)(2,1)}, bf16[4,160,960]{2,1,0:T(8,128)(2,1)S(1)}, u32[]{:S(2)}, u32[]{:S(2)}) collective-permute-start(bf16[4,160,960]{2,1,0:T(8,128)(2,1)} %bitcast.331), channel_id=1, source_target_pairs={{0,4},{4,0},{1,5},{5,1},{2,6},{6,2},{3,7},{7,3},{8,12},{12,8},{9,1... | collective-permute-start | bytes 3686408 | tf_op jit(solution)/shard_map/ppermute | solution.py:631
  245.4 49.8 %collective-permute-start.28 = (bf16[128,1280]{1,0:T(8,128)(2,1)}, bf16[128,1280]{1,0:T(8,128)(2,1)}, u32[]{:S(2)}, u32[]{:S(2)}) collective-permute-start(bf16[128,1280]{1,0:T(8,128)(2,1)} %dynamic-slice_bitcast_fusion.9), channel_id=1, source_target_pairs={{0,4},{4,0},{1,5},{5,1},{2,6},{6,2},{3,7},{7,3},{8,12},{12,8},{9,1... | collective-permute-start | bytes 983048 | tf_op jit(solution)/shard_map/ppermute | solution.py:631
  246.0 50.4 %collective-permute-start.22 = (bf16[4,40,3840]{2,1,0:T(8,128)(2,1)}, bf16[4,40,3840]{2,1,0:T(8,128)(2,1)}, u32[]{:S(2)}, u32[]{:S(2)}) collective-permute-start(bf16[4,40,3840]{2,1,0:T(8,128)(2,1)} %bitcast.41.refs_0_), channel_id=1, source_target_pairs={{0,1},{1,0},{2,3},{3,2},{4,5},{5,4},{6,7},{7,6},{8,9},{9,8},{10,11... | collective-permute-start | bytes 3686408 | tf_op jit(solution)/shard_map/ppermute | solution.py:631
  246.3 50.1 %collective-permute-start.24 = (bf16[4,40,3840]{2,1,0:T(8,128)(2,1)}, bf16[4,40,3840]{2,1,0:T(8,128)(2,1)}, u32[]{:S(2)}, u32[]{:S(2)}) collective-permute-start(bf16[4,40,3840]{2,1,0:T(8,128)(2,1)} %collective-permute-done.16.refs_2_), channel_id=1, source_target_pairs={{0,1},{1,0},{2,3},{3,2},{4,5},{5,4},{6,7},{7,6},{8,9},{9,8},{10,11... | collective-permute-start | bytes 3686408 | tf_op jit(solution)/shard_map/ppermute | solution.py:631
  257.6 38.8 %collective-permute-start.23 = (bf16[4,40,3840]{2,1,0:T(8,128)(2,1)}, bf16[4,40,3840]{2,1,0:T(8,128)(2,1)}, u32[]{:S(2)}, u32[]{:S(2)}) collective-permute-start(bf16[4,40,3840]{2,1,0:T(8,128)(2,1)} %collective-permute-done.14.refs_1_), channel_id=1, source_target_pairs={{0,1},{1,0},{2,3},{3,2},{4,5},{5,4},{6,7},{7,6},{8,9},{9,8},{10,11... | collective-permute-start | bytes 3686408 | tf_op jit(solution)/shard_map/ppermute | solution.py:631
  410.3 166.9 %reduce-scatter.7.cloned.1.call-start = ((), (), s32[]{:S(2)}) async-start(), calls=%async_computation.13 | async-start | bytes 3276800 | tf_op jit(solution)/shard_map/reduce_scatter | solution.py:709
  423.0 42.5 %collective-permute-start.34 = (bf16[4,2,2,40,3840]{4,3,2,1,0:T(8,128)(2,1)}, bf16[4,2,2,40,3840]{4,3,2,1,0:T(8,128)(2,1)}, u32[]{:S(2)}, u32[]{:S(2)}) collective-permute-start(bf16[4,2,2,40,3840]{4,3,2,1,0:T(8,128)(2,1)} %get-tuple-element.101), channel_id=1, source_target_pairs={{0,1},{1,0},{2,3},{3,2},{4,5},{5,4},{6,7},{7,6},{8,9},{9,8},{10,11... | collective-permute-start | bytes 14745608 | tf_op jit(solution)/shard_map/ppermute | solution.py:631
  439.9 139.4 %collective-permute-start.27 = (bf16[128,1280]{1,0:T(8,128)(2,1)S(1)}, bf16[128,1280]{1,0:T(8,128)(2,1)}, u32[]{:S(2)}, u32[]{:S(2)}) collective-permute-start(bf16[128,1280]{1,0:T(8,128)(2,1)S(1)} %dynamic-slice_bitcast_fusion.10), channel_id=1, source_target_pairs={{0,4},{4,0},{1,5},{5,1},{2,6},{6,2},{3,7},{7,3},{8,12},{12,8},{9,1... | collective-permute-start | bytes 983048 | tf_op jit(solution)/shard_map/ppermute | solution.py:631
  445.9 161.4 %reduce-scatter.5.cloned.1.call-start = ((), (), s32[]{:S(2)}) async-start(), calls=%async_computation.12 | async-start | bytes 3276800 | tf_op jit(solution)/shard_map/reduce_scatter | solution.py:709
  450.1 93.8 %collective-permute-start.39 = (bf16[4,40,3840]{2,1,0:T(8,128)(2,1)}, bf16[4,40,3840]{2,1,0:T(8,128)(2,1)}, u32[]{:S(2)}, u32[]{:S(2)}) collective-permute-start(bf16[4,40,3840]{2,1,0:T(8,128)(2,1)} %pad_maximum_fusion.6), channel_id=1, source_target_pairs={{0,4},{4,0},{1,5},{5,1},{2,6},{6,2},{3,7},{7,3},{8,12},{12,8},{9,1... | collective-permute-start | bytes 3686408 | tf_op jit(solution)/shard_map/ppermute | solution.py:631
  482.1 127.4 %reduce-scatter.11.cloned.1.call-start = ((), (), s32[]{:S(2)}) async-start(), calls=%async_computation.15 | async-start | bytes 1536000 | tf_op jit(solution)/shard_map/reduce_scatter | solution.py:709
  488.0 55.9 %collective-permute-start.40 = (bf16[4,40,3840]{2,1,0:T(8,128)(2,1)S(1)}, bf16[4,40,3840]{2,1,0:T(8,128)(2,1)S(1)}, u32[]{:S(2)}, u32[]{:S(2)}) collective-permute-start(bf16[4,40,3840]{2,1,0:T(8,128)(2,1)S(1)} %copy-done.56), channel_id=1, source_target_pairs={{0,2},{1,3},{2,0},{3,1},{4,6},{5,7},{6,4},{7,5},{8,10},{9,11},{10,... | collective-permute-start | bytes 3686408 | tf_op jit(solution)/shard_map/ppermute | solution.py:631
  500.6 48.4 %collective-permute-start.47 = (f32[2,80]{1,0:T(2,128)S(1)}, f32[2,80]{1,0:T(2,128)S(1)}, u32[]{:S(2)}, u32[]{:S(2)}) collective-permute-start(f32[2,80]{1,0:T(2,128)S(1)} %fusion.107), channel_id=1, source_target_pairs={{0,2},{1,3},{2,0},{3,1},{4,6},{5,7},{6,4},{7,5},{8,10},{9,11},{10,... | collective-permute-start | bytes 1928 | tf_op jit(solution)/shard_map/ppermute | solution.py:631
  503.0 39.1 %collective-permute-start.38 = (bf16[2,128,1280]{2,1,0:T(8,128)(2,1)S(1)}, bf16[2,128,1280]{2,1,0:T(8,128)(2,1)S(1)}, u32[]{:S(2)}, u32[]{:S(2)}) collective-permute-start(bf16[2,128,1280]{2,1,0:T(8,128)(2,1)S(1)} %fusion.95), channel_id=1, source_target_pairs={{0,2},{1,3},{2,0},{3,1},{4,6},{5,7},{6,4},{7,5},{8,10},{9,11},{10,... | collective-permute-start | bytes 1966088 | tf_op jit(solution)/shard_map/ppermute | solution.py:631
  542.1 48.4 %collective-permute-start.45 = (bf16[4,40,3840]{2,1,0:T(8,128)(2,1)}, bf16[4,40,3840]{2,1,0:T(8,128)(2,1)}, u32[]{:S(2)}, u32[]{:S(2)}) collective-permute-start(bf16[4,40,3840]{2,1,0:T(8,128)(2,1)} %pad_maximum_fusion.9), channel_id=1, source_target_pairs={{0,2},{1,3},{2,0},{3,1},{4,6},{5,7},{6,4},{7,5},{8,10},{9,11},{10,... | collective-permute-start | bytes 3686408 | tf_op jit(solution)/shard_map/ppermute | solution.py:631
  548.2 42.3 %collective-permute-start.44 = (bf16[4,40,3840]{2,1,0:T(8,128)(2,1)}, bf16[4,40,3840]{2,1,0:T(8,128)(2,1)}, u32[]{:S(2)}, u32[]{:S(2)}) collective-permute-start(bf16[4,40,3840]{2,1,0:T(8,128)(2,1)} %pad_maximum_fusion.8), channel_id=1, source_target_pairs={{0,4},{4,0},{1,5},{5,1},{2,6},{6,2},{3,7},{7,3},{8,12},{12,8},{9,1... | collective-permute-start | bytes 3686408 | tf_op jit(solution)/shard_map/ppermute | solution.py:631
  549.0 27.2 %collective-permute-start.48 = (f32[2,80]{1,0:T(2,128)S(1)}, f32[2,80]{1,0:T(2,128)S(1)}, u32[]{:S(2)}, u32[]{:S(2)}) collective-permute-start(f32[2,80]{1,0:T(2,128)S(1)} %fusion.136), channel_id=1, source_target_pairs={{0,4},{4,0},{1,5},{5,1},{2,6},{6,2},{3,7},{7,3},{8,12},{12,8},{9,1... | collective-permute-start | bytes 1928 | tf_op jit(solution)/shard_map/ppermute | solution.py:631
  589.8 34.0 %reduce-scatter.9.cloned.1.call-start = ((), (), s32[]{:S(2)}) async-start(), calls=%async_computation.14 | async-start | bytes 1536000 | tf_op jit(solution)/shard_map/reduce_scatter | solution.py:709
  (116 other events, 1108.4 us)
Sparse Core Ops, SparseCore 0:
  14.3 31.6 all-gather.8
  48.1 31.7 all-gather.10
  104.3 30.3 all-gather.12
  146.9 29.9 all-gather.14
  446.0 50.6 reduce-scatter.6
  498.9 51.7 reduce-scatter.4
  553.7 29.7 reduce-scatter.10
  594.2 29.6 reduce-scatter.8

commit v8 on v7

--- a/solution.py
+++ b/solution.py
@@ -548,7 +548,7 @@
         active_t[...] = active_ref[...].astype(F32).T.astype(BF16)
 
     start = pl.multiple_of(tile * rows, rows)
-    first_core = core_ref[0] == 0
+    first_core = core_ref[2] == 0
     lefts = (attended_ref, normed_t, active_t)
     for i, (left, right) in enumerate(zip(lefts, (out_bar, up_bar, down_bar))):
         grad = jnp.dot(left[pl.ds(start, rows), :], right[...], preferred_element_type=F32)
@@ -580,12 +580,13 @@
         out_shape=[shape, shape],
         compiler_params=KERNEL,
         cost_estimate=LIGHT,
-    )(place()[2:], attended_t, normed, active, out_bar, up_bar, down_bar)
+    )(place(), attended_t, normed, active, out_bar, up_bar, down_bar)
 
 
 def place():
     head = lax.axis_index("head")
-    return jnp.stack([lax.axis_index("blk"), head // 2, head % 2]).astype(jnp.int32)
+    index = [lax.axis_index("blk"), head // 2, head % 2, lax.axis_index("batch")]
+    return jnp.stack(index).astype(jnp.int32)
 
 
 def assemble_kernel(place_ref, *refs):
@@ -605,7 +606,8 @@
 def assemble(pieces):
     batch, own, columns = pieces[0].shape
     specs = [
-        pl.BlockSpec((1, own, piece.shape[-1]), lambda i, at: (i, 0, 0)) for piece in pieces
+        pl.BlockSpec((1, own, piece.shape[-1]), lambda i, at: (i ^ at[3], 0, 0))
+        for piece in pieces
     ]
     whole = pl.pallas_call(
         assemble_kernel,
@@ -622,6 +624,144 @@
     return whole.reshape(-1, columns)
 
 
+def assemble_columns_kernel(place_ref, along_ref, across_ref, whole_ref, *extra_ref):
+    blk = place_ref[0]
+    columns = whole_ref.shape[-1]
+    whole_ref[0, blk] = along_ref[0, :, :columns]
+    whole_ref[0, 1 - blk] = across_ref[0, :, :columns]
+    for extra in extra_ref:
+        extra[0, blk] = along_ref[0, :, columns:]
+        extra[0, 1 - blk] = across_ref[0, :, columns:]
+
+
+def assemble_columns(along, across, columns):
+    batch, own, both = along.shape
+    rows = pl.BlockSpec((1, own, both), lambda i, at: (i ^ at[3], 0, 0))
+    shapes = [(batch, 2, own, columns)]
+    if both > columns:
+        shapes.append((batch, 2, own, both - columns))
+    parts = pl.pallas_call(
+        assemble_columns_kernel,
+        grid_spec=pltpu.PrefetchScalarGridSpec(
+            num_scalar_prefetch=1,
+            grid=(batch,),
+            in_specs=[rows, rows],
+            out_specs=[pl.BlockSpec((1,) + s[1:], lambda i, at: (i, 0, 0, 0)) for s in shapes],
+        ),
+        out_shape=[jax.ShapeDtypeStruct(s, BF16) for s in shapes],
+        compiler_params=KERNEL,
+        cost_estimate=LIGHT,
+    )(place(), along, across)
+    return [part.reshape(-1, part.shape[-1]) for part in parts]
+
+
+def project_kernel(with_norm, place_ref, *refs):
+    pieces, (gain_ref, weight_ref, normed_ref, projected_ref) = refs[:4], refs[4:]
+    head = place_ref[1] * 2 + place_ref[2]
+    rows = pieces[0].shape[0]
+    for i, piece in enumerate(pieces):
+        value = piece[...]
+        if with_norm:
+            stream = value.astype(F32)
+            factor = lax.rsqrt(jnp.mean(stream * stream, axis=-1, keepdims=True) + EPSILON)
+            value = (stream * factor * gain_ref[...]).astype(BF16)
+        normed_ref[pl.ds(pl.multiple_of((head ^ i) * rows, rows), rows), :] = value
+    projected = jnp.dot(normed_ref[...], weight_ref[...], preferred_element_type=F32)
+    projected_ref[...] = projected.T
+
+
+def project(pieces, gain, weight, with_norm, token_rows):
+    tokens, width = pieces[0].shape
+    length, columns = 4 * tokens, weight.shape[1]
+    groups = tokens // token_rows
+    piece = pl.BlockSpec((token_rows, width), lambda g, at: (g, 0))
+    return pl.pallas_call(
+        functools.partial(project_kernel, with_norm),
+        grid_spec=pltpu.PrefetchScalarGridSpec(
+            num_scalar_prefetch=1,
+            grid=(groups,),
+            in_specs=[piece] * 4
+            + [
+                pl.BlockSpec((1, width), lambda g, at: (0, 0)),
+                pl.BlockSpec((width, columns), lambda g, at: (0, 0)),
+            ],
+            out_specs=[
+                pl.BlockSpec((4 * token_rows, width), lambda g, at: (g, 0)),
+                pl.BlockSpec((columns, 4 * token_rows), lambda g, at: (0, g)),
+            ],
+        ),
+        out_shape=[
+            jax.ShapeDtypeStruct((length, width), BF16),
+            jax.ShapeDtypeStruct((columns, length), F32),
+        ],
+        compiler_params=KERNEL,
+        cost_estimate=LIGHT,
+    )(place(), *pieces, gain.reshape(1, width), weight)
+
+
+def project_back_kernel(
+    place_ref, bars_ref, weight_ref, normed_ref, own_ref, other_ref, mine_ref, sent_ref, total
+):
+    step = pl.program_id(0)
+    bars = bars_ref[...].astype(F32).T.astype(BF16)
+    upper = lax.dot_general(bars, weight_ref[...], NT, preferred_element_type=F32)
+    rows = upper.shape[0] // 2
+    first_core = place_ref[2] == 0
+    one, two = upper[:rows], upper[rows:]
+    own_ref[0, 0] = jnp.where(first_core, one, two)
+    other_ref[0, 0] = jnp.where(first_core, two, one).astype(BF16)
+    grad = lax.dot_general(normed_ref[...], bars, TN, preferred_element_type=F32)
+
+    @pl.when(step == 0)
+    def _():
+        total[...] = grad
+
+    @pl.when(step > 0)
+    def _():
+        total[...] += grad
+
+    @pl.when(step == pl.num_programs(0) - 1)
+    def _():
+        batch, own, columns = mine_ref.shape
+        first_blk = place_ref[0] == 0
+        for i in range(batch):
+            one = total[2 * i * own : (2 * i + 1) * own, :]
+            two = total[(2 * i + 1) * own : (2 * i + 2) * own, :]
+            mine_ref[i] = jnp.where(first_blk, one, two)
+            sent_ref[i] = jnp.where(first_blk, two, one).astype(BF16)
+
+
+def project_back(bars, weight, normed, token_rows):
+    columns, length = bars.shape
+    width = weight.shape[0]
+    pair = 2 * token_rows
+    quarter = pl.BlockSpec((1, 1, token_rows, width), lambda s, at: (s // 2, s % 2, 0, 0))
+    rows = (4, width // 8, columns)
+    whole = pl.BlockSpec(rows, lambda s, at: (0, 0, 0))
+    return pl.pallas_call(
+        project_back_kernel,
+        grid_spec=pltpu.PrefetchScalarGridSpec(
+            num_scalar_prefetch=1,
+            grid=(length // pair,),
+            in_specs=[
+                pl.BlockSpec((columns, pair), lambda s, at: (0, s)),
+                pl.BlockSpec((width, columns), lambda s, at: (0, 0)),
+                pl.BlockSpec((pair, width), lambda s, at: (s, 0)),
+            ],
+            out_specs=[quarter, quarter, whole, whole],
+            scratch_shapes=[pltpu.VMEM((width, columns), F32)],
+        ),
+        out_shape=[
+            jax.ShapeDtypeStruct((2, 2, token_rows, width), F32),
+            jax.ShapeDtypeStruct((2, 2, token_rows, width), BF16),
+            jax.ShapeDtypeStruct(rows, F32),
+            jax.ShapeDtypeStruct(rows, BF16),
+        ],
+        compiler_params=KERNEL,
+        cost_estimate=LIGHT,
+    )(place(), bars, weight, normed)
+
+
 def tied(*arrays):
     return lax.optimization_barrier(arrays)
 
@@ -640,24 +780,6 @@
     got = swapped(pick(array, 1 - me), "blk", 1)
     kept = pick(array, me)
     return jnp.stack([jnp.where(me == 0, kept, got), jnp.where(me == 0, got, kept)])
-
-
-def gather_rows(rows):
-    width = rows.shape[-1]
-    far = swapped(rows, "head", 2)
-    near = swapped(rows, "head", 1)
-    both = swapped(far, "head", 1)
-    pieces = jnp.stack([rows, near, far, both])
-    me = lax.axis_index("head")
-    ordered = jnp.stack([pick(pieces, me ^ i) for i in range(4)])
-    return ordered.reshape(4, 2, -1, width).transpose(1, 0, 2, 3).reshape(-1, width)
-
-
-def scatter_core(rows):
-    core = lax.axis_index("head") % 2
-    parts = rows.reshape(2, 2, 2, -1, rows.shape[-1])
-    got = swapped(pick(parts, 1 - core, 2).astype(BF16), "head", 1).astype(F32)
-    return pick(parts, core, 2) + got
 
 
 def scatter_row(halves):
@@ -680,13 +802,7 @@
 
 
 def along_batch(piece):
-    return lax.all_gather(piece, "batch", axis=0, tiled=False)
-
-
-def in_rows(along, across):
-    first = lax.axis_index("blk") == 0
-    both = jnp.stack([jnp.where(first, along, across), jnp.where(first, across, along)], axis=1)
-    return both.reshape(-1, along.shape[-1])
+    return jnp.stack([piece] + [swapped(piece, "batch", mask) for mask in (1, 2, 3)])
 
 
 def other_core(array):
@@ -706,27 +822,28 @@
 
 
 def over_batch(parts):
-    return lax.psum_scatter(parts.astype(BF16), "batch", scatter_dimension=0, tiled=False)
-
-
-def columns_to_rows(halves):
-    blk = lax.axis_index("blk")
-    got = swapped(pick(halves, 1 - blk), "blk", 1).astype(F32)
-    summed = (pick(halves, blk).astype(F32) + got).astype(BF16)
-    moved = over_head(summed.reshape(4, -1, summed.shape[-1]))
+    me = lax.axis_index("batch")
+    total = pick(parts, me).astype(F32)
+    for mask in (1, 2, 3):
+        total = total + swapped(pick(parts, me ^ mask).astype(BF16), "batch", mask).astype(F32)
+    return total
+
+
+def columns_to_rows(summed):
+    moved = over_head(summed.astype(BF16).reshape(4, -1, summed.shape[-1]))
     rows = moved.shape[1]
     return moved.reshape(4, rows, 3, -1).transpose(1, 2, 0, 3).reshape(rows, -1).astype(F32)
 
 
 def diagonal_sent(cored):
-    blk, row, _ = place()
+    blk, row = place()[:2]
     rows = pick(pick(cored, 1 - blk, 1), 1 - row, 1)
     half = rows.shape[-1] // 2
     return swapped(rows[..., :half], "blk", 1), swapped(rows[..., half:], "head", 2)
 
 
 def neighbours_sent(cored, one, two):
-    blk, row, _ = place()
+    blk, row = place()[:2]
     half = one.shape[-1]
     across = pick(pick(cored, 1 - blk, 1), row, 1)
     beside = pick(pick(cored, blk, 1), 1 - row, 1)
@@ -740,7 +857,7 @@
 
 
 def own_sum(cored, across, beside):
-    blk, row, _ = place()
+    blk, row = place()[:2]
     own = pick(pick(cored, blk, 1), row, 1)
     return own.astype(F32) + across.astype(F32) + beside.astype(F32)
 
@@ -777,68 +894,75 @@
     segments = pick(segments, lax.axis_index("blk"))
     own_gains = jnp.concatenate([attn_gain, mlp_gain], axis=0)
 
-    first = swap_halves(tokens).reshape(-1, width)
-    columns = [qkv_columns(qkv_weight[0], own_gains.T)]
-    columns[0], first = tied(columns[0], first)
-    first_all = gather_rows(first)
-    stream = first.astype(F32)
-    first_columns = columns[0].reshape(-1, columns[0].shape[-1])
     part3 = 3 * width // 4
     dense_own = [
         jnp.concatenate([out_weight[i], up_weight[i], down_weight[i]], axis=1) for i in (0, 1)
     ]
-    dense_along = along_batch(dense_own[0])
-    first_columns, dense_along = tied(first_columns, dense_along)
-    across, beside = to_neighbours(dense_along)
-    along = along_batch(first_columns)
-    along, dense_next = tied(along, dense_own[1])
-    dense_next = along_batch(dense_next)
+
+    first = swap_halves(tokens).reshape(-1, width)
+    stream = first.astype(F32)
+    dense_near = along_batch(dense_own[0])
+    columns = qkv_columns(qkv_weight[0], own_gains.T)
+    columns, first = tied(columns.reshape(-1, columns.shape[-1]), first)
+    along = along_batch(columns)
+    far = swapped(first, "head", 2)
+    near = other_core(first)
+    dense_near, far = tied(dense_near, far)
+    token_pieces = (first, near, far, other_core(far))
+    across, beside = swapped(dense_near, "blk", 1), swapped(dense_near, "head", 2)
+    along, across, beside, dense_next = tied(along, across, beside, dense_own[1])
     qkv_across = swapped(along, "blk", 1)
     one = to_beside(across)
-    qkv_across, beside_after = tied(qkv_across, beside)
-    with_gains = in_rows(along, qkv_across)
-    two = to_across(beside_after)
-    qkvs = [with_gains[:, :part3], None]
-    gains = with_gains[:, part3:].T.astype(F32)
-    pieces = [(dense_along, across, beside, one, two)]
+    dense_next = along_batch(dense_next)
     next_columns = qkv_columns(qkv_weight[1], None).reshape(-1, part3)
-    next_columns, dense_next = tied(next_columns, dense_next)
+    qkv_across, one, beside, dense_next, next_columns = tied(
+        qkv_across, one, beside, dense_next, next_columns
+    )
+    two = to_across(beside)
+    pieces = [(dense_near, across, beside, one, two)]
+    beside = swapped(dense_next, "head", 2)
     next_along = along_batch(next_columns)
-    beside = swapped(dense_next, "head", 2)
-    two, dense_after = tied(two, dense_next)
-    across = swapped(dense_after, "blk", 1)
-    across, next_along = tied(across, next_along)
-    next_across = swapped(next_along, "blk", 1)
-    one = to_beside(across)
-    next_across, beside_after = tied(next_across, beside)
-    two = to_across(beside_after)
-    pieces.append((dense_next, across, beside, one, two))
-
-    def dense_of(layer):
-        return assemble(pieces[layer] + tuple(other_core(piece) for piece in pieces[layer]))
+    weight, gains = assemble_columns(along, qkv_across, part3)
+    qkvs = [weight]
+    gains = gains.T.astype(F32)
 
     kept, denses = [], []
     for layer in range(layers):
         normed, factor_one = normalize(stream, gains[layer])
-        if layer == 0:
-            normed_all = normalize(first_all.astype(F32), gains[0])[0].astype(BF16)
-        else:
-            normed, next_across = tied(normed.astype(BF16), next_across)
-            normed_all = gather_rows(normed)
-            qkvs[1] = in_rows(next_along, next_across)
-        qkv = qkvs[layer]
-        projected = lax.dot_general(
-            qkv, normed_all, (((0,), (1,)), ((), ())), preferred_element_type=F32
+        if layer == 1:
+            normed, across = tied(normed.astype(BF16), across)
+            far = swapped(normed, "head", 2)
+            next_across = swapped(next_along, "blk", 1)
+            far, after = tied(far, across)
+            one = to_beside(after)
+            token_pieces = (normed, other_core(normed), far, other_core(far))
+            next_across, after = tied(next_across, beside)
+            two = to_across(after)
+            pieces.append((dense_next, across, beside, one, two))
+            qkvs.append(assemble_columns(next_along, next_across, part3)[0])
+        normed_all, projected = project(
+            token_pieces, gains[layer], qkvs[layer], layer == 0, token_rows
         )
         attended, log_total = attend_rows(
             projected, scale_vecs[layer], segments, 4, token_rows
         )
-        attended, late = tied(attended, pieces[layer][3:])
-        pieces[layer] = pieces[layer][:3] + late
-        denses.append(dense_of(layer))
+        if layer == 0:
+            attended, two, next_along = tied(attended, pieces[0][4], next_along)
+            pieces[0] = pieces[0][:4] + (two,)
+            across = swapped(dense_next, "blk", 1)
+        else:
+            attended, one, two = tied(attended, *pieces[1][3:])
+            pieces[1] = pieces[1][:3] + (one, two)
+        swaps = tuple(other_core(piece) for piece in pieces[layer])
+        attended_t = over_head(attended)
+        if layer == 0:
+            attended_t, beside, swaps = tied(attended_t, beside, swaps)
+        else:
+            attended_t, swaps = tied(attended_t, swaps)
+        attended_t = attended_t.reshape(width, -1)
+        denses.append(assemble(pieces[layer] + swaps))
         dense = denses[layer]
         out_w, up_w, down_w = dense[:, :width], dense[:, width:-width], dense[:, -width:]
-        attended_t = over_head(attended).reshape(width, -1)
         middle = stream + dot_rows(attended_t, out_w)
         normed_two, factor_two = normalize(middle, gains[layers + layer])
         normed_two = normed_two.astype(BF16)
@@ -854,7 +978,7 @@
     layer_out = swap_halves(stream.astype(BF16).reshape(tokens.shape))
     upper = swap_halves(cotangent).reshape(-1, width).astype(F32)
 
-    qkv_sums, dense_grad, scale_grads = [None] * layers, [None] * layers, [None] * layers
+    dense_grad, scale_grads = [None] * layers, [None] * layers
     for layer in reversed(range(layers)):
         (
             stream, factor_one, normed_all, projected, log_total, attended_t, middle,
@@ -883,28 +1007,30 @@
         bars, scale_grads[layer] = attend_back_rows(
             projected, attended_grad, log_total, scale_vecs[layer], segments, token_rows
         )
-        bars, others = tied(bars, others)
+        if layer == 0:
+            bars, others, got = tied(bars, others, got)
+            qkv_sums = [None, over_batch(mine + got.astype(F32))]
+        else:
+            bars, others = tied(bars, others)
         cored = (grads.astype(F32) + others.astype(F32)).astype(BF16)
-        halves = scatter_core(
-            lax.dot_general(bars, qkv, (((0,), (1,)), ((), ())), preferred_element_type=F32)
-        )
-        qkv_grad = lax.dot_general(
-            normed_all, bars, (((0,), (1,)), ((), ())), preferred_element_type=F32
-        )
-        qkv_sums[layer] = over_batch(qkv_grad.reshape(4, 2, -1, qkv_grad.shape[-1]))
+        halves, to_core, mine, got = project_back(bars, qkv, normed_all, token_rows)
+        halves = halves + other_core(to_core).astype(F32)
         if layer == 0:
+            got = swapped(got, "blk", 1)
             diagonal = diagonal_sent(cored)
-            halves, diagonal = tied(halves, diagonal)
-            normed_grad = scatter_row(halves)
-            normed_grad, sent = tied(normed_grad, sent)
+            halves, diagonal, sent = tied(halves, diagonal, sent)
             dense_grad[1] = over_batch(own_sum(last, *sent))
             sent = neighbours_sent(cored, *diagonal)
+            normed_grad = scatter_row(halves)
+            normed_grad, got, sent = tied(normed_grad, got, sent)
+            qkv_sums[0] = over_batch(mine + got.astype(F32))
             dense_grad[0] = over_batch(own_sum(cored, *sent))
             qkv_grads = [columns_to_rows(part) for part in qkv_sums]
         else:
             normed_grad = scatter_row(halves)
-            normed_grad, cored = tied(normed_grad, cored)
+            normed_grad, cored, got = tied(normed_grad, cored, got)
             diagonal = diagonal_sent(cored)
+            got = swapped(got, "blk", 1)
         upper = middle_grad + lower_of(normed_grad, stream, factor_one, gains[layer])
     input_grad = swap_halves(upper.astype(BF16).reshape(tokens.shape)).astype(F32)
     scale_total = sum_all(jnp.stack(scale_grads))

time: 653 us -> 684 us (1.047)
  starting transfers between devices: 75.2 us -> 140 us
  Pallas kernels: 74.3 us -> 129 us
  matrix products: 61.7 us -> 28.4 us
  local copies, waits for them, and re-layouts: 82.8 us -> 52.7 us
  other arithmetic: 68.9 us -> 53.6 us
  between operations: 16.2 us -> 2.42 us
    ppermute x51 -> x75, starting transfers between devices: 44.9 us -> 109 us  [swapped(): return lax.ppermute(array, axis, [(i, i ^ mask) for i in range(size)])]
    pallas_call x0 -> x6, Pallas kernels: none -> 53 us  [the longest x2 28.3 us: project_back(): pl.pallas_call(project_back_kernel, grid_spec=pltpu.PrefetchScalarGridSpe...]
    ppermute x51 -> x75, waiting for transfers between devices: 212 us -> 242 us  [swapped(): return lax.ppermute(array, axis, [(i, i ^ mask) for i in range(size)])]
    dot_general x6 -> x0, matrix products: 28.8 us -> none  [the longest x2 11.7 us: spread_device(): lax.dot_general(qkv, normed_all, (((0,), (1,)), ((), ())), preferred_elem...]
    all_gather x4 -> x0, waiting for transfers between devices: 26.9 us -> none  [along_batch(): return lax.all_gather(piece, 'batch', axis=0, tiled=False)]
    dot_general x6 -> x0, local copies, waits for them, and re-layouts: 25.6 us -> none  [the longest x3 10.5 us: spread_device(): lax.dot_general(qkv, normed_all, (((0,), (1,)), ((), ())), preferred_elem...]
    reduce_scatter x4 -> x0, waiting for transfers between devices: 14.3 us -> none  [over_batch(): lax.psum_scatter(parts.astype(BF16), 'batch', scatter_dimension=0, tiled=...]
    all_to_all x8, waiting for transfers between devices: 12.9 us -> 26 us  [over_head(): lax.all_to_all(parts, 'head', split_axis=0, concat_axis=0, tiled=True)]
  transfers between devices with their start and end apart: 67 -> 83, of which waited for: 25 -> 34; matrix products, arithmetic and copies ran while one was open for 23% -> 12% of each run, Pallas kernels for 12% -> 16%
where the time goes in v8:
time: 684 us; the launch traced here: 674 us
  waiting for transfers between devices  268 us (39%)
  starting transfers between devices  140 us (20%)
  Pallas kernels  129 us (19%)
  other arithmetic  53.6 us (8%)
  local copies, waits for them, and re-layouts  52.7 us (8%)
  matrix products  28.4 us (4%)
    ppermute x75, waiting for transfers between devices, swapped(): return lax.ppermute(array, axis, [(i, i ^ mask) for i in range(size)])  242 us
    ppermute x75, starting transfers between devices, swapped(): return lax.ppermute(array, axis, [(i, i ^ mask) for i in range(size)])  109 us
    all_to_all x8, starting transfers between devices, over_head(): lax.all_to_all(parts, 'head', split_axis=0, concat_axis=0, tiled=True)  31 us
    pallas_call x2, Pallas kernels, project_back(): pl.pallas_call(project_back_kernel, grid_spec=pltpu.PrefetchScalarGridSpe...  28.3 us
    all_to_all x8, waiting for transfers between devices, over_head(): lax.all_to_all(parts, 'head', split_axis=0, concat_axis=0, tiled=True)  26 us
    pallas_call x2, Pallas kernels, attend_back_rows(): pl.pallas_call(functools.partial(attend_back_kernel, token_rows), grid=(l...  23.5 us
    unnamed x164, local copies, waits for them, and re-layouts  21 us
    pallas_call x2, Pallas kernels, attend_rows(): pl.pallas_call(functools.partial(attend_kernel, token_rows), grid=(local_...  20.5 us
  transfers between devices with their start and end apart: 83, of which 34 were waited for; matrix products, arithmetic and copies ran while one was open for 12% of the time, Pallas kernels for 16%

profile of v8, /device:TPU:0, one launch (start us, length us, event | category | flops | bytes accessed | tf_op | source)
XLA Modules:
  0.0 674.2 jit_solution(17472595609384624005)
XLA Ops:
  24.3 10.9 %collective-permute-done.3 = bf16[40,3840]{1,0:T(8,128)(2,1)} collective-permute-done((bf16[40,3840]{1,0:T(8,128)(2,1)}, bf16[40,3840]{1,0:T(8,128)(2,1)}, u32[]{:S(2)}, u32[]{:S(2)}) %collective-permute-start.3) | collective-permute-done | bytes 307232 | tf_op jit(solution)/shard_map/ppermute | solution.py:771
  45.7 8.1 %collective-permute-done.9 = bf16[160,964]{1,0:T(8,128)(2,1)S(1)} collective-permute-done((bf16[160,964]{1,0:T(8,128)(2,1)S(1)}, bf16[160,964]{1,0:T(8,128)(2,1)S(1)}, u32[]{:S(2)}, u32[]{:S(2)}) %collective-permute-start.9) | collective-permute-done | bytes 308512 | tf_op jit(solution)/shard_map/ppermute | solution.py:771
  53.9 17.6 %collective-permute-done.8 = bf16[160,964]{1,0:T(8,128)(2,1)S(1)} collective-permute-done((bf16[160,964]{1,0:T(8,128)(2,1)S(1)}, bf16[160,964]{1,0:T(8,128)(2,1)S(1)}, u32[]{:S(2)}, u32[]{:S(2)}) %collective-permute-start.8) | collective-permute-done | bytes 308512 | tf_op jit(solution)/shard_map/ppermute | solution.py:771
  87.7 11.2 %collective-permute-done.15 = bf16[40,3840]{1,0:T(8,128)(2,1)} collective-permute-done((bf16[40,3840]{1,0:T(8,128)(2,1)S(1)}, bf16[40,3840]{1,0:T(8,128)(2,1)}, u32[]{:S(2)}, u32[]{:S(2)}) %collective-permute-start.15) | collective-permute-done | bytes 307232 | tf_op jit(solution)/shard_map/ppermute | solution.py:771
  115.3 16.4 %collective-permute-done.19 = bf16[160,960]{1,0:T(8,128)(2,1)} collective-permute-done((bf16[160,960]{1,0:T(8,128)(2,1)}, bf16[160,960]{1,0:T(8,128)(2,1)}, u32[]{:S(2)}, u32[]{:S(2)}) %collective-permute-start.19) | collective-permute-done | bytes 307232 | tf_op jit(solution)/shard_map/ppermute | solution.py:771
  134.0 8.6 %shard_map.170 = (bf16[1024,1280]{1,0:T(8,128)(2,1)}, f32[960,1024]{1,0:T(8,128)}) custom-call(s32[4]{0:T(128)S(1)} %pad_add_fusion.place_ref.core_ref, bf16[256,1280]{1,0:T(8,128)(2,1)S(1)} %bitcast.245, bf16[256,1280]{1,0:T(8,128)(2,1)S(1)} %copy-done.25, bf16[256,1280]{1,0:T(8,128)(2,1)} %collective-permute-done.5.refs_2_, ...), custom_call_target="tpu_custom_call" | custom-call | flops 1048576 | bytes 1048576 | tf_op jit(solution)/shard_map/pallas_call | solution.py:678
  142.6 9.9 %shard_map.171 = (bf16[4,4,80,256]{3,2,1,0:T(8,128)(2,1)S(1)}, f32[4,1,1024]{2,1,0:T(1,128)S(1)}) custom-call(f32[3,4,80,1024]{3,2,1,0:T(8,128)} %bitcast.256, f32[80,1]{1,0:T(8,128)S(1)} %copy.49.scale_ref, s32[1024,1]{1,0:T(8,128)S(1)} %copy.50.col_ref, s32[1,1024]{1,0:T(1,128)S(1)} %constant_dynamic-slice_fusion.row_ref), custom_call_target="tpu_custom_call" | custom-call | flops 1048576 | bytes 1048576 | tf_op jit(solution)/shard_map/pallas_call | solution.py:409
  160.6 8.1 %all-to-all-done.2 = bf16[4,320,256]{2,1,0:T(8,128)(2,1)S(1)} async-done(((bf16[4,320,256]{2,1,0:T(8,128)(2,1)}), bf16[4,320,256]{2,1,0:T(8,128)(2,1)S(1)}, u32[]{:S(2)}, u32[]{:S(2)}) %all-to-all-start.2) | async-done | bytes 655392 | tf_op jit(solution)/shard_map/all_to_all | solution.py:792
  170.2 7.9 %shard_map.172 = bf16[4,2,2,2,40,3840]{5,4,3,2,1,0:T(8,128)(2,1)} custom-call(s32[4]{0:T(128)S(1)} %pad_add_fusion.place_ref.core_ref, bf16[4,40,3840]{2,1,0:T(8,128)(2,1)S(1)} %copy-done.3, bf16[4,40,3840]{2,1,0:T(8,128)(2,1)} %collective-permute-done.10.refs_1_, bf16[4,40,3840]{2,1,0:T(8,128)(2,1)} %collective-permute-done.11.refs_2_, ...), custom_call_target="tpu_custom_call" | custom-call | flops 1048576 | bytes 1048576 | tf_op jit(solution)/shard_map/pallas_call | solution.py:612
  190.7 25.6 %collective-permute-done.31.across_ref = bf16[4,160,960]{2,1,0:T(8,128)(2,1)} collective-permute-done((bf16[4,160,960]{2,1,0:T(8,128)(2,1)S(1)}, bf16[4,160,960]{2,1,0:T(8,128)(2,1)}, u32[]{:S(2)}, u32[]{:S(2)}) %collective-permute-start.31) | collective-permute-done | bytes 1228832 | tf_op jit(solution)/shard_map/ppermute | solution.py:771
  223.4 9.7 %collective-permute-done.33.refs_4_ = bf16[4,40,1920]{2,1,0:T(8,128)(2,1)} collective-permute-done((bf16[4,40,1920]{2,1,0:T(8,128)(2,1)S(1)}, bf16[4,40,1920]{2,1,0:T(8,128)(2,1)}, u32[]{:S(2)}, u32[]{:S(2)}) %collective-permute-start.33) | collective-permute-done | bytes 614432 | tf_op jit(solution)/shard_map/ppermute | solution.py:771
  240.9 7.2 %shard_map.174 = (bf16[1024,1280]{1,0:T(8,128)(2,1)}, f32[960,1024]{1,0:T(8,128)}) custom-call(s32[4]{0:T(128)S(1)} %pad_add_fusion.place_ref.core_ref, bf16[256,1280]{1,0:T(8,128)(2,1)S(1)} %copy-done.11, bf16[256,1280]{1,0:T(8,128)(2,1)S(1)} %copy-done.29, bf16[256,1280]{1,0:T(8,128)(2,1)S(1)} %copy-done.27, bf16[256,1280]{1,0:T(8,128)(2,1)S(1)} %copy-done.31, ...), custom_call_target="tpu_custom_call" | custom-call | flops 1048576 | bytes 1048576 | tf_op jit(solution)/shard_map/pallas_call | solution.py:678
  248.1 10.5 %shard_map.175 = (bf16[4,4,80,256]{3,2,1,0:T(8,128)(2,1)}, f32[4,1,1024]{2,1,0:T(1,128)S(1)}) custom-call(f32[3,4,80,1024]{3,2,1,0:T(8,128)} %bitcast.258, f32[80,1]{1,0:T(8,128)S(1)} %copy.51.scale_ref, s32[1024,1]{1,0:T(8,128)S(1)} %copy.50.col_ref, s32[1,1024]{1,0:T(1,128)S(1)} %constant_dynamic-slice_fusion.row_ref), custom_call_target="tpu_custom_call" | custom-call | flops 1048576 | bytes 1048576 | tf_op jit(solution)/shard_map/pallas_call | solution.py:409
  264.5 8.4 %all-to-all-done.3 = bf16[4,320,256]{2,1,0:T(8,128)(2,1)S(1)} async-done(((bf16[4,320,256]{2,1,0:T(8,128)(2,1)}), bf16[4,320,256]{2,1,0:T(8,128)(2,1)S(1)}, u32[]{:S(2)}, u32[]{:S(2)}) %all-to-all-start.3) | async-done | bytes 655392 | tf_op jit(solution)/shard_map/all_to_all | solution.py:792
  272.9 8.4 %shard_map.176 = bf16[4,2,2,2,40,3840]{5,4,3,2,1,0:T(8,128)(2,1)} custom-call(s32[4]{0:T(128)S(1)} %pad_add_fusion.place_ref.core_ref, bf16[4,40,3840]{2,1,0:T(8,128)(2,1)} %pad_maximum_fusion.3.refs_0_, bf16[4,40,3840]{2,1,0:T(8,128)(2,1)} %collective-permute-done.27.refs_1_, bf16[4,40,3840]{2,1,0:T(8,128)(2,1)} %collective-permute-done.21.refs_2_, ...), custom_call_target="tpu_custom_call" | custom-call | flops 1048576 | bytes 1048576 | tf_op jit(solution)/shard_map/pallas_call | solution.py:612
  303.0 7.7 %shard_map.177 = (bf16[4,2,2,40,3840]{4,3,2,1,0:T(8,128)(2,1)}, bf16[4,2,2,40,3840]{4,3,2,1,0:T(8,128)(2,1)}) custom-call(s32[4]{0:T(128)S(1)} %pad_add_fusion.place_ref.core_ref, bf16[1280,256]{1,0:T(8,128)(2,1)S(1)} %bitcast.250, bf16[256,1280]{1,0:T(8,128)(2,1)S(1)} %multiply_convert_fusion.1.normed_ref, bf16[256,1280]{1,0:T(8,128)(2,1)S(1)} %copy-done.19, ...), custom_call_target="tpu_custom_call" | custom-call | flops 1048576 | bytes 1048576 | tf_op jit(solution)/shard_map/pallas_call | solution.py:571
  316.2 11.7 %shard_map.178 = (bf16[3,4,80,1024]{3,2,1,0:T(8,128)(2,1)S(1)}, f32[80,128]{1,0:T(8,128)S(1)}) custom-call(f32[3,4,80,1024]{3,2,1,0:T(8,128)} %bitcast.259, bf16[4,4,80,256]{3,2,1,0:T(8,128)(2,1)} %bitcast.63.grad_ref, f32[4,1,1024]{2,1,0:T(1,128)S(1)} %get-tuple-element.142.lse_ref, f32[80,1]{1,0:T(8,128)S(1)} %copy.51.scale_ref, ...), custom_call_target="tpu_custom_call" | custom-call | flops 1048576 | bytes 1048576 | tf_op jit(solution)/shard_map/pallas_call | solution.py:502
  329.2 14.7 %shard_map.179 = (f32[2,2,128,1280]{3,2,1,0:T(8,128)}, bf16[2,2,128,1280]{3,2,1,0:T(8,128)(2,1)}, f32[4,160,960]{2,1,0:T(8,128)}, bf16[4,160,960]{2,1,0:T(8,128)(2,1)S(1)}) custom-call(s32[4]{0:T(128)S(1)} %pad_add_fusion.place_ref.core_ref, bf16[960,1024]{1,0:T(8,128)(2,1)} %bitcast.252, bf16[1280,960]{1,0:T(8,128)(2,1)} %bitcast.255, ...), custom_call_target="tpu_custom_call" | custom-call | flops 1048576 | bytes 1048576 | tf_op jit(solution)/shard_map/pallas_call | solution.py:741
  357.5 10.2 %collective-permute-done.43 = bf16[2,128,1280]{2,1,0:T(8,128)(2,1)S(1)} collective-permute-done((bf16[2,128,1280]{2,1,0:T(8,128)(2,1)S(1)}, bf16[2,128,1280]{2,1,0:T(8,128)(2,1)S(1)}, u32[]{:S(2)}, u32[]{:S(2)}) %collective-permute-start.43) | collective-permute-done | bytes 655392 | tf_op jit(solution)/shard_map/ppermute | solution.py:771
  392.3 7.7 %shard_map.180 = (bf16[4,2,2,40,3840]{4,3,2,1,0:T(8,128)(2,1)}, bf16[4,2,2,40,3840]{4,3,2,1,0:T(8,128)(2,1)}) custom-call(s32[4]{0:T(128)S(1)} %pad_add_fusion.place_ref.core_ref, bf16[1280,256]{1,0:T(8,128)(2,1)S(1)} %bitcast.248, bf16[256,1280]{1,0:T(8,128)(2,1)S(1)} %multiply_convert_fusion.4.normed_ref, bf16[256,1280]{1,0:T(8,128)(2,1)S(1)} %copy-done.18, ...), custom_call_target="tpu_custom_call" | custom-call | flops 1048576 | bytes 1048576 | tf_op jit(solution)/shard_map/pallas_call | solution.py:571
  407.4 8.3 %collective-permute-done.39 = bf16[128,1280]{1,0:T(8,128)(2,1)S(1)} collective-permute-done((bf16[128,1280]{1,0:T(8,128)(2,1)S(1)}, bf16[128,1280]{1,0:T(8,128)(2,1)S(1)}, u32[]{:S(2)}, u32[]{:S(2)}) %collective-permute-start.39) | collective-permute-done | bytes 327712 | tf_op jit(solution)/shard_map/ppermute | solution.py:771
  415.9 11.8 %shard_map.181 = (bf16[3,4,80,1024]{3,2,1,0:T(8,128)(2,1)S(1)}, f32[80,128]{1,0:T(8,128)S(1)}) custom-call(f32[3,4,80,1024]{3,2,1,0:T(8,128)} %bitcast.257, bf16[4,4,80,256]{3,2,1,0:T(8,128)(2,1)} %bitcast.71.grad_ref, f32[4,1,1024]{2,1,0:T(1,128)S(1)} %get-tuple-element.156.lse_ref, f32[80,1]{1,0:T(8,128)S(1)} %copy.49.scale_ref, ...), custom_call_target="tpu_custom_call" | custom-call | flops 1048576 | bytes 1048576 | tf_op jit(solution)/shard_map/pallas_call | solution.py:502
  438.5 23.3 %collective-permute-done.72 = f32[2,80]{1,0:T(2,128)S(1)} collective-permute-done((f32[2,80]{1,0:T(2,128)S(1)}, f32[2,80]{1,0:T(2,128)S(1)}, u32[]{:S(2)}, u32[]{:S(2)}) %collective-permute-start.72) | collective-permute-done | bytes 672 | tf_op jit(solution)/shard_map/ppermute | solution.py:771
  470.4 13.6 %shard_map.182 = (f32[2,2,128,1280]{3,2,1,0:T(8,128)}, bf16[2,2,128,1280]{3,2,1,0:T(8,128)(2,1)}, f32[4,160,960]{2,1,0:T(8,128)}, bf16[4,160,960]{2,1,0:T(8,128)(2,1)S(1)}) custom-call(s32[4]{0:T(128)S(1)} %pad_add_fusion.place_ref.core_ref, bf16[960,1024]{1,0:T(8,128)(2,1)} %bitcast.251, bf16[1280,960]{1,0:T(8,128)(2,1)} %bitcast.265, ...), custom_call_target="tpu_custom_call" | custom-call | flops 1048576 | bytes 1048576 | tf_op jit(solution)/shard_map/pallas_call | solution.py:741
  500.8 16.4 %collective-permute-done.62 = bf16[160,960]{1,0:T(8,128)(2,1)S(1)} collective-permute-done((bf16[160,960]{1,0:T(8,128)(2,1)S(1)}, bf16[160,960]{1,0:T(8,128)(2,1)S(1)}, u32[]{:S(2)}, u32[]{:S(2)}) %collective-permute-start.62) | collective-permute-done | bytes 307232 | tf_op jit(solution)/shard_map/ppermute | solution.py:771
  553.5 11.4 %collective-permute-start.68 = (bf16[40,3840]{1,0:T(8,128)(2,1)S(1)}, bf16[40,3840]{1,0:T(8,128)(2,1)S(1)}, u32[]{:S(2)}, u32[]{:S(2)}) collective-permute-start(bf16[40,3840]{1,0:T(8,128)(2,1)S(1)} %get-tuple-element.209), channel_id=1, source_target_pairs={{0,16},{8,24},{16,0},{24,8},{1,17},{9,25},{17,1},{25,9},{2,18},{10... | collective-permute-start | bytes 921608 | tf_op jit(solution)/shard_map/ppermute | solution.py:771
  566.6 16.6 %collective-permute-done.68 = bf16[40,3840]{1,0:T(8,128)(2,1)S(1)} collective-permute-done((bf16[40,3840]{1,0:T(8,128)(2,1)S(1)}, bf16[40,3840]{1,0:T(8,128)(2,1)S(1)}, u32[]{:S(2)}, u32[]{:S(2)}) %collective-permute-start.68) | collective-permute-done | bytes 307232 | tf_op jit(solution)/shard_map/ppermute | solution.py:771
  584.6 10.6 %collective-permute-done.55 = bf16[4,40,3840]{2,1,0:T(8,128)(2,1)S(1)} collective-permute-done((bf16[4,40,3840]{2,1,0:T(8,128)(2,1)S(1)}, bf16[4,40,3840]{2,1,0:T(8,128)(2,1)S(1)}, u32[]{:S(2)}, u32[]{:S(2)}) %collective-permute-start.55) | collective-permute-done | bytes 1228832 | tf_op jit(solution)/shard_map/ppermute | solution.py:771
  595.2 14.9 %collective-permute-done.56 = bf16[4,40,3840]{2,1,0:T(8,128)(2,1)S(1)} collective-permute-done((bf16[4,40,3840]{2,1,0:T(8,128)(2,1)S(1)}, bf16[4,40,3840]{2,1,0:T(8,128)(2,1)S(1)}, u32[]{:S(2)}, u32[]{:S(2)}) %collective-permute-start.56) | collective-permute-done | bytes 1228832 | tf_op jit(solution)/shard_map/ppermute | solution.py:771
  623.8 20.4 %collective-permute-start.64 = (bf16[40,3840]{1,0:T(8,128)(2,1)}, bf16[40,3840]{1,0:T(8,128)(2,1)}, u32[]{:S(2)}, u32[]{:S(2)}) collective-permute-start(bf16[40,3840]{1,0:T(8,128)(2,1)} %get-tuple-element.210), channel_id=1, source_target_pairs={{0,8},{8,0},{16,24},{24,16},{1,9},{9,1},{17,25},{25,17},{2,10},{10... | collective-permute-start | bytes 921608 | tf_op jit(solution)/shard_map/ppermute | solution.py:771
  644.2 10.1 %collective-permute-done.59 = bf16[160,960]{1,0:T(8,128)(2,1)S(1)} collective-permute-done((bf16[160,960]{1,0:T(8,128)(2,1)S(1)}, bf16[160,960]{1,0:T(8,128)(2,1)S(1)}, u32[]{:S(2)}, u32[]{:S(2)}) %collective-permute-start.59) | collective-permute-done | bytes 307232 | tf_op jit(solution)/shard_map/ppermute | solution.py:771
  660.6 5.1 collective-permute-done.65
  (446 shorter events, 288.6 us)
Async XLA Ops:
  40.3 31.4 %collective-permute-start.10 = (bf16[4,40,3840]{2,1,0:T(8,128)(2,1)S(1)}, bf16[4,40,3840]{2,1,0:T(8,128)(2,1)}, u32[]{:S(2)}, u32[]{:S(2)}) collective-permute-start(bf16[4,40,3840]{2,1,0:T(8,128)(2,1)S(1)} %pad_maximum_fusion.2.refs_0_), channel_id=1, source_target_pairs={{0,4},{4,0},{1,5},{5,1},{2,6},{6,2},{3,7},{7,3},{8,12},{12,8},{9,1... | collective-permute-start | bytes 3686408 | tf_op jit(solution)/shard_map/ppermute | solution.py:771
  40.7 31.0 %collective-permute-start.11 = (bf16[4,40,3840]{2,1,0:T(8,128)(2,1)S(1)}, bf16[4,40,3840]{2,1,0:T(8,128)(2,1)}, u32[]{:S(2)}, u32[]{:S(2)}) collective-permute-start(bf16[4,40,3840]{2,1,0:T(8,128)(2,1)S(1)} %pad_maximum_fusion.2.refs_0_), channel_id=1, source_target_pairs={{0,2},{1,3},{2,0},{3,1},{4,6},{5,7},{6,4},{7,5},{8,10},{9,11},{10,... | collective-permute-start | bytes 3686408 | tf_op jit(solution)/shard_map/ppermute | solution.py:771
  71.7 30.7 %collective-permute-start.12 = (bf16[4,160,964]{2,1,0:T(8,128)(2,1)S(1)}, bf16[4,160,964]{2,1,0:T(8,128)(2,1)}, u32[]{:S(2)}, u32[]{:S(2)}) collective-permute-start(bf16[4,160,964]{2,1,0:T(8,128)(2,1)S(1)} %pad_maximum_fusion.along_ref), channel_id=1, source_target_pairs={{0,4},{4,0},{1,5},{5,1},{2,6},{6,2},{3,7},{7,3},{8,12},{12,8},{9,1... | collective-permute-start | bytes 3701768 | tf_op jit(solution)/shard_map/ppermute | solution.py:771
  99.0 55.3 %collective-permute-start.22 = (bf16[4,40,3840]{2,1,0:T(8,128)(2,1)}, bf16[4,40,3840]{2,1,0:T(8,128)(2,1)}, u32[]{:S(2)}, u32[]{:S(2)}) collective-permute-start(bf16[4,40,3840]{2,1,0:T(8,128)(2,1)} %copy-done.2), channel_id=1, source_target_pairs={{0,1},{1,0},{2,3},{3,2},{4,5},{5,4},{6,7},{7,6},{8,9},{9,8},{10,11... | collective-permute-start | bytes 3686408 | tf_op jit(solution)/shard_map/ppermute | solution.py:771
  114.4 44.1 %collective-permute-start.23 = (bf16[4,40,3840]{2,1,0:T(8,128)(2,1)}, bf16[4,40,3840]{2,1,0:T(8,128)(2,1)}, u32[]{:S(2)}, u32[]{:S(2)}) collective-permute-start(bf16[4,40,3840]{2,1,0:T(8,128)(2,1)} %collective-permute-done.10.refs_1_), channel_id=1, source_target_pairs={{0,1},{1,0},{2,3},{3,2},{4,5},{5,4},{6,7},{7,6},{8,9},{9,8},{10,11... | collective-permute-start | bytes 3686408 | tf_op jit(solution)/shard_map/ppermute | solution.py:771
  115.3 53.4 %collective-permute-start.24 = (bf16[4,40,3840]{2,1,0:T(8,128)(2,1)}, bf16[4,40,3840]{2,1,0:T(8,128)(2,1)}, u32[]{:S(2)}, u32[]{:S(2)}) collective-permute-start(bf16[4,40,3840]{2,1,0:T(8,128)(2,1)} %collective-permute-done.11.refs_2_), channel_id=1, source_target_pairs={{0,1},{1,0},{2,3},{3,2},{4,5},{5,4},{6,7},{7,6},{8,9},{9,8},{10,11... | collective-permute-start | bytes 3686408 | tf_op jit(solution)/shard_map/ppermute | solution.py:771
  132.2 36.5 %collective-permute-start.21 = (bf16[4,40,3840]{2,1,0:T(8,128)(2,1)}, bf16[4,40,3840]{2,1,0:T(8,128)(2,1)}, u32[]{:S(2)}, u32[]{:S(2)}) collective-permute-start(bf16[4,40,3840]{2,1,0:T(8,128)(2,1)} %pad_maximum_fusion.3.refs_0_), channel_id=1, source_target_pairs={{0,2},{1,3},{2,0},{3,1},{4,6},{5,7},{6,4},{7,5},{8,10},{9,11},{10,... | collective-permute-start | bytes 3686408 | tf_op jit(solution)/shard_map/ppermute | solution.py:771
  158.5 30.2 %collective-permute-start.27 = (bf16[4,40,3840]{2,1,0:T(8,128)(2,1)}, bf16[4,40,3840]{2,1,0:T(8,128)(2,1)}, u32[]{:S(2)}, u32[]{:S(2)}) collective-permute-start(bf16[4,40,3840]{2,1,0:T(8,128)(2,1)} %pad_maximum_fusion.3.refs_0_), channel_id=1, source_target_pairs={{0,4},{4,0},{1,5},{5,1},{2,6},{6,2},{3,7},{7,3},{8,12},{12,8},{9,1... | collective-permute-start | bytes 3686408 | tf_op jit(solution)/shard_map/ppermute | solution.py:771
  160.0 56.3 %collective-permute-start.31 = (bf16[4,160,960]{2,1,0:T(8,128)(2,1)S(1)}, bf16[4,160,960]{2,1,0:T(8,128)(2,1)}, u32[]{:S(2)}, u32[]{:S(2)}) collective-permute-start(bf16[4,160,960]{2,1,0:T(8,128)(2,1)S(1)} %pad_maximum_fusion.1.along_ref), channel_id=1, source_target_pairs={{0,4},{4,0},{1,5},{5,1},{2,6},{6,2},{3,7},{7,3},{8,12},{12,8},{9,1... | collective-permute-start | bytes 3686408 | tf_op jit(solution)/shard_map/ppermute | solution.py:771
  188.7 30.3 %collective-permute-start.29 = (bf16[256,1280]{1,0:T(8,128)(2,1)S(1)}, bf16[256,1280]{1,0:T(8,128)(2,1)S(1)}, u32[]{:S(2)}, u32[]{:S(2)}) collective-permute-start(bf16[256,1280]{1,0:T(8,128)(2,1)S(1)} %multiply_convert_fusion.2.refs_0_), channel_id=1, source_target_pairs={{0,2},{1,3},{2,0},{3,1},{4,6},{5,7},{6,4},{7,5},{8,10},{9,11},{10,... | collective-permute-start | bytes 1966088 | tf_op jit(solution)/shard_map/ppermute | solution.py:771
  190.7 32.2 %collective-permute-start.28 = (bf16[256,1280]{1,0:T(8,128)(2,1)S(1)}, bf16[256,1280]{1,0:T(8,128)(2,1)S(1)}, u32[]{:S(2)}, u32[]{:S(2)}) collective-permute-start(bf16[256,1280]{1,0:T(8,128)(2,1)S(1)} %multiply_convert_fusion.2.refs_0_), channel_id=1, source_target_pairs={{0,1},{1,0},{2,3},{3,2},{4,5},{5,4},{6,7},{7,6},{8,9},{9,8},{10,11... | collective-permute-start | bytes 1966088 | tf_op jit(solution)/shard_map/ppermute | solution.py:771
  221.2 37.5 %collective-permute-start.32 = (bf16[4,40,1920]{2,1,0:T(8,128)(2,1)}, bf16[4,40,1920]{2,1,0:T(8,128)(2,1)}, u32[]{:S(2)}, u32[]{:S(2)}) collective-permute-start(bf16[4,40,1920]{2,1,0:T(8,128)(2,1)} %slice.154), channel_id=1, source_target_pairs={{0,2},{1,3},{2,0},{3,1},{4,6},{5,7},{6,4},{7,5},{8,10},{9,11},{10,... | collective-permute-start | bytes 1843208 | tf_op jit(solution)/shard_map/ppermute | solution.py:771
  222.9 41.6 %collective-permute-start.34 = (bf16[4,40,3840]{2,1,0:T(8,128)(2,1)}, bf16[4,40,3840]{2,1,0:T(8,128)(2,1)}, u32[]{:S(2)}, u32[]{:S(2)}) collective-permute-start(bf16[4,40,3840]{2,1,0:T(8,128)(2,1)} %pad_maximum_fusion.3.refs_0_), channel_id=1, source_target_pairs={{0,1},{1,0},{2,3},{3,2},{4,5},{5,4},{6,7},{7,6},{8,9},{9,8},{10,11... | collective-permute-start | bytes 3686408 | tf_op jit(solution)/shard_map/ppermute | solution.py:771
  222.9 41.6 %collective-permute-start.35 = (bf16[4,40,3840]{2,1,0:T(8,128)(2,1)}, bf16[4,40,3840]{2,1,0:T(8,128)(2,1)}, u32[]{:S(2)}, u32[]{:S(2)}) collective-permute-start(bf16[4,40,3840]{2,1,0:T(8,128)(2,1)} %collective-permute-done.27.refs_1_), channel_id=1, source_target_pairs={{0,1},{1,0},{2,3},{3,2},{4,5},{5,4},{6,7},{7,6},{8,9},{9,8},{10,11... | collective-permute-start | bytes 3686408 | tf_op jit(solution)/shard_map/ppermute | solution.py:771
  233.1 31.4 %collective-permute-start.36 = (bf16[4,40,3840]{2,1,0:T(8,128)(2,1)}, bf16[4,40,3840]{2,1,0:T(8,128)(2,1)}, u32[]{:S(2)}, u32[]{:S(2)}) collective-permute-start(bf16[4,40,3840]{2,1,0:T(8,128)(2,1)} %collective-permute-done.21.refs_2_), channel_id=1, source_target_pairs={{0,1},{1,0},{2,3},{3,2},{4,5},{5,4},{6,7},{7,6},{8,9},{9,8},{10,11... | collective-permute-start | bytes 3686408 | tf_op jit(solution)/shard_map/ppermute | solution.py:771
  234.7 28.5 %collective-permute-start.40 = (bf16[128,1280]{1,0:T(8,128)(2,1)}, bf16[128,1280]{1,0:T(8,128)(2,1)}, u32[]{:S(2)}, u32[]{:S(2)}) collective-permute-start(bf16[128,1280]{1,0:T(8,128)(2,1)} %dynamic-slice_bitcast_fusion.7), channel_id=1, source_target_pairs={{0,4},{4,0},{1,5},{5,1},{2,6},{6,2},{3,7},{7,3},{8,12},{12,8},{9,1... | collective-permute-start | bytes 983048 | tf_op jit(solution)/shard_map/ppermute | solution.py:771
  401.9 68.5 %collective-permute-start.46 = (bf16[4,2,2,40,3840]{4,3,2,1,0:T(8,128)(2,1)}, bf16[4,2,2,40,3840]{4,3,2,1,0:T(8,128)(2,1)}, u32[]{:S(2)}, u32[]{:S(2)}) collective-permute-start(bf16[4,2,2,40,3840]{4,3,2,1,0:T(8,128)(2,1)} %get-tuple-element.158), channel_id=1, source_target_pairs={{0,1},{1,0},{2,3},{3,2},{4,5},{5,4},{6,7},{7,6},{8,9},{9,8},{10,11... | collective-permute-start | bytes 14745608 | tf_op jit(solution)/shard_map/ppermute | solution.py:771
  430.0 40.4 %collective-permute-start.47 = (bf16[4,160,960]{2,1,0:T(8,128)(2,1)S(1)}, bf16[4,160,960]{2,1,0:T(8,128)(2,1)S(1)}, u32[]{:S(2)}, u32[]{:S(2)}) collective-permute-start(bf16[4,160,960]{2,1,0:T(8,128)(2,1)S(1)} %copy-done.33), channel_id=1, source_target_pairs={{0,4},{4,0},{1,5},{5,1},{2,6},{6,2},{3,7},{7,3},{8,12},{12,8},{9,1... | collective-permute-start | bytes 3686408 | tf_op jit(solution)/shard_map/ppermute | solution.py:771
  437.0 100.5 %collective-permute-start.51 = (bf16[4,40,3840]{2,1,0:T(8,128)(2,1)}, bf16[4,40,3840]{2,1,0:T(8,128)(2,1)}, u32[]{:S(2)}, u32[]{:S(2)}) collective-permute-start(bf16[4,40,3840]{2,1,0:T(8,128)(2,1)} %pad_maximum_fusion.4), channel_id=1, source_target_pairs={{0,4},{4,0},{1,5},{5,1},{2,6},{6,2},{3,7},{7,3},{8,12},{12,8},{9,1... | collective-permute-start | bytes 3686408 | tf_op jit(solution)/shard_map/ppermute | solution.py:771
  484.0 49.4 %collective-permute-start.48 = (bf16[2,2,128,1280]{3,2,1,0:T(8,128)(2,1)}, bf16[2,2,128,1280]{3,2,1,0:T(8,128)(2,1)}, u32[]{:S(2)}, u32[]{:S(2)}) collective-permute-start(bf16[2,2,128,1280]{3,2,1,0:T(8,128)(2,1)} %get-tuple-element.163), channel_id=1, source_target_pairs={{0,1},{1,0},{2,3},{3,2},{4,5},{5,4},{6,7},{7,6},{8,9},{9,8},{10,11... | collective-permute-start | bytes 3932168 | tf_op jit(solution)/shard_map/ppermute | solution.py:771
  488.9 28.3 %collective-permute-start.62 = (bf16[160,960]{1,0:T(8,128)(2,1)S(1)}, bf16[160,960]{1,0:T(8,128)(2,1)S(1)}, u32[]{:S(2)}, u32[]{:S(2)}) collective-permute-start(bf16[160,960]{1,0:T(8,128)(2,1)S(1)} %get-tuple-element.206), channel_id=1, source_target_pairs={{0,16},{8,24},{16,0},{24,8},{1,17},{9,25},{17,1},{25,9},{2,18},{10... | collective-permute-start | bytes 921608 | tf_op jit(solution)/shard_map/ppermute | solution.py:771
  488.9 28.3 %collective-permute-start.61 = (bf16[160,960]{1,0:T(8,128)(2,1)S(1)}, bf16[160,960]{1,0:T(8,128)(2,1)S(1)}, u32[]{:S(2)}, u32[]{:S(2)}) collective-permute-start(bf16[160,960]{1,0:T(8,128)(2,1)S(1)} %get-tuple-element.204), channel_id=1, source_target_pairs={{0,8},{8,0},{16,24},{24,16},{1,9},{9,1},{17,25},{25,17},{2,10},{10... | collective-permute-start | bytes 921608 | tf_op jit(solution)/shard_map/ppermute | solution.py:771
  499.0 38.5 %collective-permute-start.52 = (bf16[4,40,3840]{2,1,0:T(8,128)(2,1)}, bf16[4,40,3840]{2,1,0:T(8,128)(2,1)}, u32[]{:S(2)}, u32[]{:S(2)}) collective-permute-start(bf16[4,40,3840]{2,1,0:T(8,128)(2,1)} %pad_maximum_fusion.5), channel_id=1, source_target_pairs={{0,2},{1,3},{2,0},{3,1},{4,6},{5,7},{6,4},{7,5},{8,10},{9,11},{10,... | collective-permute-start | bytes 3686408 | tf_op jit(solution)/shard_map/ppermute | solution.py:771
  533.5 51.1 %collective-permute-start.54 = (bf16[4,160,960]{2,1,0:T(8,128)(2,1)S(1)}, bf16[4,160,960]{2,1,0:T(8,128)(2,1)S(1)}, u32[]{:S(2)}, u32[]{:S(2)}) collective-permute-start(bf16[4,160,960]{2,1,0:T(8,128)(2,1)S(1)} %get-tuple-element.169), channel_id=1, source_target_pairs={{0,4},{4,0},{1,5},{5,1},{2,6},{6,2},{3,7},{7,3},{8,12},{12,8},{9,1... | collective-permute-start | bytes 3686408 | tf_op jit(solution)/shard_map/ppermute | solution.py:771
  544.3 40.2 %collective-permute-start.53 = (bf16[2,128,1280]{2,1,0:T(8,128)(2,1)S(1)}, bf16[2,128,1280]{2,1,0:T(8,128)(2,1)S(1)}, u32[]{:S(2)}, u32[]{:S(2)}) collective-permute-start(bf16[2,128,1280]{2,1,0:T(8,128)(2,1)S(1)} %fusion.79), channel_id=1, source_target_pairs={{0,2},{1,3},{2,0},{3,1},{4,6},{5,7},{6,4},{7,5},{8,10},{9,11},{10,... | collective-permute-start | bytes 1966088 | tf_op jit(solution)/shard_map/ppermute | solution.py:771
  553.5 29.8 %collective-permute-start.68 = (bf16[40,3840]{1,0:T(8,128)(2,1)S(1)}, bf16[40,3840]{1,0:T(8,128)(2,1)S(1)}, u32[]{:S(2)}, u32[]{:S(2)}) collective-permute-start(bf16[40,3840]{1,0:T(8,128)(2,1)S(1)} %get-tuple-element.209), channel_id=1, source_target_pairs={{0,16},{8,24},{16,0},{24,8},{1,17},{9,25},{17,1},{25,9},{2,18},{10... | collective-permute-start | bytes 921608 | tf_op jit(solution)/shard_map/ppermute | solution.py:771
  565.0 30.2 %collective-permute-start.55 = (bf16[4,40,3840]{2,1,0:T(8,128)(2,1)S(1)}, bf16[4,40,3840]{2,1,0:T(8,128)(2,1)S(1)}, u32[]{:S(2)}, u32[]{:S(2)}) collective-permute-start(bf16[4,40,3840]{2,1,0:T(8,128)(2,1)S(1)} %pad_maximum_fusion.6), channel_id=1, source_target_pairs={{0,4},{4,0},{1,5},{5,1},{2,6},{6,2},{3,7},{7,3},{8,12},{12,8},{9,1... | collective-permute-start | bytes 3686408 | tf_op jit(solution)/shard_map/ppermute | solution.py:771
  614.3 40.0 %collective-permute-start.59 = (bf16[160,960]{1,0:T(8,128)(2,1)S(1)}, bf16[160,960]{1,0:T(8,128)(2,1)S(1)}, u32[]{:S(2)}, u32[]{:S(2)}) collective-permute-start(bf16[160,960]{1,0:T(8,128)(2,1)S(1)} %get-tuple-element.203), channel_id=1, source_target_pairs={{0,16},{8,24},{16,0},{24,8},{1,17},{9,25},{17,1},{25,9},{2,18},{10... | collective-permute-start | bytes 921608 | tf_op jit(solution)/shard_map/ppermute | solution.py:771
  614.3 41.8 %collective-permute-start.58 = (bf16[160,960]{1,0:T(8,128)(2,1)S(1)}, bf16[160,960]{1,0:T(8,128)(2,1)S(1)}, u32[]{:S(2)}, u32[]{:S(2)}) collective-permute-start(bf16[160,960]{1,0:T(8,128)(2,1)S(1)} %get-tuple-element.201), channel_id=1, source_target_pairs={{0,8},{8,0},{16,24},{24,16},{1,9},{9,1},{17,25},{25,17},{2,10},{10... | collective-permute-start | bytes 921608 | tf_op jit(solution)/shard_map/ppermute | solution.py:771
  618.4 42.2 %collective-permute-start.66 = (bf16[40,3840]{1,0:T(8,128)(2,1)}, bf16[40,3840]{1,0:T(8,128)(2,1)}, u32[]{:S(2)}, u32[]{:S(2)}) collective-permute-start(bf16[40,3840]{1,0:T(8,128)(2,1)} %get-tuple-element.211), channel_id=1, source_target_pairs={{0,24},{8,16},{16,8},{24,0},{1,25},{9,17},{17,9},{25,1},{2,26},{10... | collective-permute-start | bytes 921608 | tf_op jit(solution)/shard_map/ppermute | solution.py:771
  621.4 44.4 %collective-permute-start.65 = (bf16[40,3840]{1,0:T(8,128)(2,1)}, bf16[40,3840]{1,0:T(8,128)(2,1)}, u32[]{:S(2)}, u32[]{:S(2)}) collective-permute-start(bf16[40,3840]{1,0:T(8,128)(2,1)} %get-tuple-element.212), channel_id=1, source_target_pairs={{0,16},{8,24},{16,0},{24,8},{1,17},{9,25},{17,1},{25,9},{2,18},{10... | collective-permute-start | bytes 921608 | tf_op jit(solution)/shard_map/ppermute | solution.py:771
  623.8 42.0 %collective-permute-start.64 = (bf16[40,3840]{1,0:T(8,128)(2,1)}, bf16[40,3840]{1,0:T(8,128)(2,1)}, u32[]{:S(2)}, u32[]{:S(2)}) collective-permute-start(bf16[40,3840]{1,0:T(8,128)(2,1)} %get-tuple-element.210), channel_id=1, source_target_pairs={{0,8},{8,0},{16,24},{24,16},{1,9},{9,1},{17,25},{25,17},{2,10},{10... | collective-permute-start | bytes 921608 | tf_op jit(solution)/shard_map/ppermute | solution.py:771
  (133 other events, 1577.2 us)

commit v9 on v8

--- a/solution.py
+++ b/solution.py
@@ -359,7 +359,7 @@
 
 
 Q_ROWS = 256
-KERNEL = pltpu.CompilerParams(vmem_limit_bytes=50 * 1024 * 1024)
+KERNEL = pltpu.CompilerParams(vmem_limit_bytes=32 * 1024 * 1024)
 LIGHT = pl.CostEstimate(flops=1 << 20, bytes_accessed=1 << 20, transcendentals=0)
 
 
@@ -540,7 +540,7 @@
     own_ref, other_ref, normed_t, active_t,
 ):
     tile = pl.program_id(0)
-    rows, width = own_ref.shape[2] * own_ref.shape[3] * 2, out_bar.shape[1]
+    rows, width = own_ref.shape[1] * own_ref.shape[3] * 2, out_bar.shape[1]
 
     @pl.when(tile == 0)
     def _():
@@ -554,10 +554,10 @@
         grad = jnp.dot(left[pl.ds(start, rows), :], right[...], preferred_element_type=F32)
         grad = grad.reshape(2, 2, rows // 4, width)
         one, two = grad[:, 0], grad[:, 1]
-        own_ref[0, 0, :, :, i * width : (i + 1) * width] = jnp.where(
+        own_ref[0, :, 0, :, i * width : (i + 1) * width] = jnp.where(
             first_core, one, two
         ).astype(BF16)
-        other_ref[0, 0, :, :, i * width : (i + 1) * width] = jnp.where(
+        other_ref[0, :, 0, :, i * width : (i + 1) * width] = jnp.where(
             first_core, two, one
         ).astype(BF16)
 
@@ -566,8 +566,8 @@
     width, tokens = attended_t.shape
     own = width // 32
     whole = pl.BlockSpec((tokens, width), lambda i, core: (0, 0))
-    rows = pl.BlockSpec((1, 1, 2, own, 3 * width), lambda i, core: (i // 2, i % 2, 0, 0, 0))
-    shape = jax.ShapeDtypeStruct((4, 2, 2, own, 3 * width), BF16)
+    rows = pl.BlockSpec((1, 2, 1, own, 3 * width), lambda i, core: (i % 2, 0, i // 2, 0, 0))
+    shape = jax.ShapeDtypeStruct((2, 2, 4, own, 3 * width), BF16)
     return pl.pallas_call(
         dense_grad_kernel,
         grid_spec=pltpu.PrefetchScalarGridSpec(
@@ -585,8 +585,7 @@
 
 def place():
     head = lax.axis_index("head")
-    index = [lax.axis_index("blk"), head // 2, head % 2, lax.axis_index("batch")]
-    return jnp.stack(index).astype(jnp.int32)
+    return jnp.stack([lax.axis_index("blk"), head // 2, head % 2]).astype(jnp.int32)
 
 
 def assemble_kernel(place_ref, *refs):
@@ -606,7 +605,7 @@
 def assemble(pieces):
     batch, own, columns = pieces[0].shape
     specs = [
-        pl.BlockSpec((1, own, piece.shape[-1]), lambda i, at: (i ^ at[3], 0, 0))
+        pl.BlockSpec((1, own, piece.shape[-1]), lambda i, at: (i, 0, 0))
         for piece in pieces
     ]
     whole = pl.pallas_call(
@@ -636,7 +635,7 @@
 
 def assemble_columns(along, across, columns):
     batch, own, both = along.shape
-    rows = pl.BlockSpec((1, own, both), lambda i, at: (i ^ at[3], 0, 0))
+    rows = pl.BlockSpec((1, own, both), lambda i, at: (i, 0, 0))
     shapes = [(batch, 2, own, columns)]
     if both > columns:
         shapes.append((batch, 2, own, both - columns))
@@ -700,56 +699,46 @@
 
 
 def project_back_kernel(
-    place_ref, bars_ref, weight_ref, normed_ref, own_ref, other_ref, mine_ref, sent_ref, total
+    place_ref, bars_ref, weight_ref, normed_ref, own_ref, other_ref, mine_ref, sent_ref, bars_t
 ):
-    step = pl.program_id(0)
-    bars = bars_ref[...].astype(F32).T.astype(BF16)
-    upper = lax.dot_general(bars, weight_ref[...], NT, preferred_element_type=F32)
-    rows = upper.shape[0] // 2
+    @pl.when(pl.program_id(0) == 0)
+    def _():
+        bars_t[...] = bars_ref[...].astype(F32).T.astype(BF16)
+
+    upper = lax.dot_general(bars_t[...], weight_ref[...], NT, preferred_element_type=F32)
+    upper = upper.reshape(2, 2, 2, -1, upper.shape[-1])
     first_core = place_ref[2] == 0
-    one, two = upper[:rows], upper[rows:]
-    own_ref[0, 0] = jnp.where(first_core, one, two)
-    other_ref[0, 0] = jnp.where(first_core, two, one).astype(BF16)
-    grad = lax.dot_general(normed_ref[...], bars, TN, preferred_element_type=F32)
-
-    @pl.when(step == 0)
-    def _():
-        total[...] = grad
-
-    @pl.when(step > 0)
-    def _():
-        total[...] += grad
-
-    @pl.when(step == pl.num_programs(0) - 1)
-    def _():
-        batch, own, columns = mine_ref.shape
-        first_blk = place_ref[0] == 0
-        for i in range(batch):
-            one = total[2 * i * own : (2 * i + 1) * own, :]
-            two = total[(2 * i + 1) * own : (2 * i + 2) * own, :]
-            mine_ref[i] = jnp.where(first_blk, one, two)
-            sent_ref[i] = jnp.where(first_blk, two, one).astype(BF16)
+    one, two = upper[:, :, 0], upper[:, :, 1]
+    own_ref[...] = jnp.where(first_core, one, two)
+    other_ref[...] = jnp.where(first_core, two, one).astype(BF16)
+    grad = lax.dot_general(normed_ref[...], bars_t[...], TN, preferred_element_type=F32)
+    batch, own, columns = mine_ref.shape
+    grad = grad.reshape(batch, 2, own, columns)
+    first_blk = place_ref[0] == 0
+    one, two = grad[:, 0], grad[:, 1]
+    mine_ref[...] = jnp.where(first_blk, one, two)
+    sent_ref[...] = jnp.where(first_blk, two, one).astype(BF16)
 
 
 def project_back(bars, weight, normed, token_rows):
     columns, length = bars.shape
     width = weight.shape[0]
-    pair = 2 * token_rows
-    quarter = pl.BlockSpec((1, 1, token_rows, width), lambda s, at: (s // 2, s % 2, 0, 0))
+    tile = width // 2
+    quarter = pl.BlockSpec((2, 2, token_rows, tile), lambda i, at: (0, 0, 0, i))
     rows = (4, width // 8, columns)
-    whole = pl.BlockSpec(rows, lambda s, at: (0, 0, 0))
+    half = pl.BlockSpec((2,) + rows[1:], lambda i, at: (i, 0, 0))
     return pl.pallas_call(
         project_back_kernel,
         grid_spec=pltpu.PrefetchScalarGridSpec(
             num_scalar_prefetch=1,
-            grid=(length // pair,),
+            grid=(2,),
             in_specs=[
-                pl.BlockSpec((columns, pair), lambda s, at: (0, s)),
-                pl.BlockSpec((width, columns), lambda s, at: (0, 0)),
-                pl.BlockSpec((pair, width), lambda s, at: (s, 0)),
+                pl.BlockSpec((columns, length), lambda i, at: (0, 0)),
+                pl.BlockSpec((tile, columns), lambda i, at: (i, 0)),
+                pl.BlockSpec((length, tile), lambda i, at: (0, i)),
             ],
-            out_specs=[quarter, quarter, whole, whole],
-            scratch_shapes=[pltpu.VMEM((width, columns), F32)],
+            out_specs=[quarter, quarter, half, half],
+            scratch_shapes=[pltpu.VMEM((length, columns), BF16)],
         ),
         out_shape=[
             jax.ShapeDtypeStruct((2, 2, token_rows, width), F32),
@@ -802,17 +791,13 @@
 
 
 def along_batch(piece):
-    return jnp.stack([piece] + [swapped(piece, "batch", mask) for mask in (1, 2, 3)])
+    return lax.all_gather(piece, "batch", axis=0, tiled=False)
 
 
 def other_core(array):
     return swapped(array, "head", 1)
 
 
-def to_neighbours(along):
-    return swapped(along, "blk", 1), swapped(along, "head", 2)
-
-
 def to_beside(across):
     return swapped(across[..., : across.shape[-1] // 2], "head", 2)
 
@@ -822,11 +807,7 @@
 
 
 def over_batch(parts):
-    me = lax.axis_index("batch")
-    total = pick(parts, me).astype(F32)
-    for mask in (1, 2, 3):
-        total = total + swapped(pick(parts, me ^ mask).astype(BF16), "batch", mask).astype(F32)
-    return total
+    return lax.psum_scatter(parts.astype(BF16), "batch", scatter_dimension=0, tiled=False)
 
 
 def columns_to_rows(summed):
@@ -837,7 +818,7 @@
 
 def diagonal_sent(cored):
     blk, row = place()[:2]
-    rows = pick(pick(cored, 1 - blk, 1), 1 - row, 1)
+    rows = pick(pick(cored, 1 - blk), 1 - row)
     half = rows.shape[-1] // 2
     return swapped(rows[..., :half], "blk", 1), swapped(rows[..., half:], "head", 2)
 
@@ -845,8 +826,8 @@
 def neighbours_sent(cored, one, two):
     blk, row = place()[:2]
     half = one.shape[-1]
-    across = pick(pick(cored, 1 - blk, 1), row, 1)
-    beside = pick(pick(cored, blk, 1), 1 - row, 1)
+    across = pick(pick(cored, 1 - blk), row)
+    beside = pick(pick(cored, blk), 1 - row)
     across = jnp.concatenate(
         [across[..., :half], across[..., half:].astype(F32) + two.astype(F32)], axis=-1
     ).astype(BF16)
@@ -858,7 +839,7 @@
 
 def own_sum(cored, across, beside):
     blk, row = place()[:2]
-    own = pick(pick(cored, blk, 1), row, 1)
+    own = pick(pick(cored, blk), row)
     return own.astype(F32) + across.astype(F32) + beside.astype(F32)
 
 
@@ -900,28 +881,30 @@
     ]
 
     first = swap_halves(tokens).reshape(-1, width)
-    stream = first.astype(F32)
+    upper = swap_halves(cotangent).reshape(-1, width)
     dense_near = along_batch(dense_own[0])
     columns = qkv_columns(qkv_weight[0], own_gains.T)
-    columns, first = tied(columns.reshape(-1, columns.shape[-1]), first)
+    columns, first, upper = tied(columns.reshape(-1, columns.shape[-1]), first, upper)
+    stream, upper = first.astype(F32), upper.astype(F32)
+    far, near = swapped(first, "head", 2), other_core(first)
+    both = other_core(far)
+    next_columns = qkv_columns(qkv_weight[1], None).reshape(-1, part3)
+    columns, dense_near, near, far, both, next_columns = tied(
+        columns, dense_near, near, far, both, next_columns
+    )
+    token_pieces = (first, near, far, both)
+    across, beside = swapped(dense_near, "blk", 1), swapped(dense_near, "head", 2)
     along = along_batch(columns)
-    far = swapped(first, "head", 2)
-    near = other_core(first)
-    dense_near, far = tied(dense_near, far)
-    token_pieces = (first, near, far, other_core(far))
-    across, beside = swapped(dense_near, "blk", 1), swapped(dense_near, "head", 2)
-    along, across, beside, dense_next = tied(along, across, beside, dense_own[1])
+    along, across, beside, next_columns = tied(along, across, beside, next_columns)
     qkv_across = swapped(along, "blk", 1)
     one = to_beside(across)
-    dense_next = along_batch(dense_next)
-    next_columns = qkv_columns(qkv_weight[1], None).reshape(-1, part3)
-    qkv_across, one, beside, dense_next, next_columns = tied(
-        qkv_across, one, beside, dense_next, next_columns
+    next_along = along_batch(next_columns)
+    qkv_across, one, beside, next_along, dense_next = tied(
+        qkv_across, one, beside, next_along, dense_own[1]
     )
     two = to_across(beside)
     pieces = [(dense_near, across, beside, one, two)]
-    beside = swapped(dense_next, "head", 2)
-    next_along = along_batch(next_columns)
+    dense_next = along_batch(dense_next)
     weight, gains = assemble_columns(along, qkv_across, part3)
     qkvs = [weight]
     gains = gains.T.astype(F32)
@@ -930,14 +913,12 @@
     for layer in range(layers):
         normed, factor_one = normalize(stream, gains[layer])
         if layer == 1:
-            normed, across = tied(normed.astype(BF16), across)
-            far = swapped(normed, "head", 2)
-            next_across = swapped(next_along, "blk", 1)
-            far, after = tied(far, across)
-            one = to_beside(after)
-            token_pieces = (normed, other_core(normed), far, other_core(far))
-            next_across, after = tied(next_across, beside)
-            two = to_across(after)
+            normed, next_across, dense_after = tied(normed.astype(BF16), next_across, dense_next)
+            far, near = swapped(normed, "head", 2), other_core(normed)
+            across = swapped(dense_after, "blk", 1)
+            far, near, across, beside = tied(far, near, across, beside)
+            token_pieces = (normed, near, far, other_core(far))
+            one, two = to_beside(across), to_across(beside)
             pieces.append((dense_next, across, beside, one, two))
             qkvs.append(assemble_columns(next_along, next_across, part3)[0])
         normed_all, projected = project(
@@ -946,17 +927,14 @@
         attended, log_total = attend_rows(
             projected, scale_vecs[layer], segments, 4, token_rows
         )
-        if layer == 0:
-            attended, two, next_along = tied(attended, pieces[0][4], next_along)
-            pieces[0] = pieces[0][:4] + (two,)
-            across = swapped(dense_next, "blk", 1)
-        else:
-            attended, one, two = tied(attended, *pieces[1][3:])
-            pieces[1] = pieces[1][:3] + (one, two)
+        attended, one, two = tied(attended, *pieces[layer][3:])
+        pieces[layer] = pieces[layer][:3] + (one, two)
         swaps = tuple(other_core(piece) for piece in pieces[layer])
         attended_t = over_head(attended)
         if layer == 0:
-            attended_t, beside, swaps = tied(attended_t, beside, swaps)
+            attended_t, swaps, dense_next = tied(attended_t, swaps, dense_next)
+            next_across = swapped(next_along, "blk", 1)
+            beside = swapped(dense_next, "head", 2)
         else:
             attended_t, swaps = tied(attended_t, swaps)
         attended_t = attended_t.reshape(width, -1)
@@ -976,7 +954,6 @@
         )
         stream = middle + dot(active, down_w)
     layer_out = swap_halves(stream.astype(BF16).reshape(tokens.shape))
-    upper = swap_halves(cotangent).reshape(-1, width).astype(F32)
 
     dense_grad, scale_grads = [None] * layers, [None] * layers
     for layer in reversed(range(layers)):
@@ -998,26 +975,25 @@
         attended_grad = over_head(dot_cols(out_w, out_bar).astype(BF16).reshape(4, -1, out_bar.shape[0]))
         grads, others = dense_grads(attended_t, normed_two, active, out_bar, up_bar, down_bar)
         if layer == 0:
-            attended_grad, others, diagonal = tied(attended_grad, others, diagonal)
+            attended_grad, others, diagonal, got = tied(attended_grad, others, diagonal, got)
             sent = neighbours_sent(cored, *diagonal)
             last = cored
+            qkv_sums = [None, over_batch(mine + got.astype(F32))]
         else:
-            attended_grad, others = tied(attended_grad, others)
+            attended_grad, others, layer_out = tied(attended_grad, others, layer_out)
         others = other_core(others)
         bars, scale_grads[layer] = attend_back_rows(
             projected, attended_grad, log_total, scale_vecs[layer], segments, token_rows
         )
+        bars, others = tied(bars, others)
+        cored = (grads.astype(F32) + others.astype(F32)).astype(BF16)
         if layer == 0:
-            bars, others, got = tied(bars, others, got)
-            qkv_sums = [None, over_batch(mine + got.astype(F32))]
-        else:
-            bars, others = tied(bars, others)
-        cored = (grads.astype(F32) + others.astype(F32)).astype(BF16)
+            bars, cored = tied(bars, cored)
+            diagonal = diagonal_sent(cored)
         halves, to_core, mine, got = project_back(bars, qkv, normed_all, token_rows)
         halves = halves + other_core(to_core).astype(F32)
         if layer == 0:
             got = swapped(got, "blk", 1)
-            diagonal = diagonal_sent(cored)
             halves, diagonal, sent = tied(halves, diagonal, sent)
             dense_grad[1] = over_batch(own_sum(last, *sent))
             sent = neighbours_sent(cored, *diagonal)

time: 684 us -> 650 us (0.950)
  starting transfers between devices: 140 us -> 68 us
  waiting for transfers between devices: 268 us -> 305 us
  Pallas kernels: 129 us -> 95.8 us
  local copies, waits for them, and re-layouts: 52.7 us -> 75.7 us
  between operations: 2.42 us -> 16 us
  matrix products: 28.4 us -> 17.9 us
  blocking collectives: 0 us -> 9.94 us
    ppermute x75 -> x51, starting transfers between devices: 109 us -> 40 us  [swapped(): return lax.ppermute(array, axis, [(i, i ^ mask) for i in range(size)])]
    reduce_scatter x0 -> x4, waiting for transfers between devices: none -> 49.1 us  [over_batch(): lax.psum_scatter(parts.astype(BF16), 'batch', scatter_dimension=0, tiled=...]
    unnamed x164 -> x230, local copies, waits for them, and re-layouts: 21 us -> 51.1 us
    ppermute x75 -> x51, waiting for transfers between devices: 242 us -> 230 us  [swapped(): return lax.ppermute(array, axis, [(i, i ^ mask) for i in range(size)])]
    pallas_call x2, Pallas kernels: 28.3 us -> 17.6 us  [project_back(): pl.pallas_call(project_back_kernel, grid_spec=pltpu.PrefetchScalarGridSpe...]
    all_to_all x0 -> x1, blocking collectives: none -> 9.94 us  [over_head(): lax.all_to_all(parts, 'head', split_axis=0, concat_axis=0, tiled=True)]
    convert_element_type x3 -> x5, other arithmetic: 2.04 us -> 12 us  [the longest x4 11.8 us: over_batch(): parts.astype(BF16)]
    another operation x10 -> x5, other arithmetic: 11.2 us -> 3.02 us  [the longest x5 6.19 us: along_batch(): jnp.stack([piece] + [swapped(piece, 'batch', mask) for mask in (1, 2, 3)])]
  transfers between devices with their start and end apart: 83 -> 66, of which waited for: 34 -> 26; matrix products, arithmetic and copies ran while one was open for 12% -> 12% of each run, Pallas kernels for 16% -> 13%
where the time goes in v9:
time: 650 us; the launch traced here: 641 us
  waiting for transfers between devices  305 us (47%)
  Pallas kernels  95.8 us (15%)
  local copies, waits for them, and re-layouts  75.7 us (12%)
  starting transfers between devices  68 us (10%)
  other arithmetic  52.7 us (8%)
  matrix products  17.9 us (3%)
  between operations  16 us (2%)
  blocking collectives  9.94 us (2%)
    ppermute x51, waiting for transfers between devices, swapped(): return lax.ppermute(array, axis, [(i, i ^ mask) for i in range(size)])  230 us
    unnamed x230, local copies, waits for them, and re-layouts  51.1 us
    reduce_scatter x4, waiting for transfers between devices, over_batch(): lax.psum_scatter(parts.astype(BF16), 'batch', scatter_dimension=0, tiled=...  49.1 us
    ppermute x51, starting transfers between devices, swapped(): return lax.ppermute(array, axis, [(i, i ^ mask) for i in range(size)])  40 us
    all_to_all x7, starting transfers between devices, over_head(): lax.all_to_all(parts, 'head', split_axis=0, concat_axis=0, tiled=True)  27.5 us
    pallas_call x2, Pallas kernels, attend_back_rows(): pl.pallas_call(functools.partial(attend_back_kernel, token_rows), grid=(l...  22.9 us
    all_to_all x7, waiting for transfers between devices, over_head(): lax.all_to_all(parts, 'head', split_axis=0, concat_axis=0, tiled=True)  19.8 us
    pallas_call x2, Pallas kernels, attend_rows(): pl.pallas_call(functools.partial(attend_kernel, token_rows), grid=(local_...  18.5 us
  transfers between devices with their start and end apart: 66, of which 26 were waited for; matrix products, arithmetic and copies ran while one was open for 12% of the time, Pallas kernels for 13%

profile of v9, /device:TPU:0, one launch (start us, length us, event | category | flops | bytes accessed | tf_op | source)
XLA Modules:
  0.0 641.2 jit_solution(11616858199530711390)
XLA Ops:
  21.3 5.0 collective-permute-done
  30.8 14.1 %collective-permute-done.3.refs_2_ = bf16[256,1280]{1,0:T(8,128)(2,1)S(1)} collective-permute-done((bf16[256,1280]{1,0:T(8,128)(2,1)S(1)}, bf16[256,1280]{1,0:T(8,128)(2,1)S(1)}, u32[]{:S(2)}, u32[]{:S(2)}) %collective-permute-start.3) | collective-permute-done | bytes 655392 | tf_op jit(solution)/shard_map/ppermute | solution.py:760
  46.0 9.9 %all_to_all.40 = bf16[4,40,960]{2,1,0:T(8,128)(2,1)} all-to-all(bf16[4,40,960]{2,1,0:T(8,128)(2,1)S(1)} %reshape.219), channel_id=1, replica_groups=mesh['batch'=4,'blk'=2,'head'=4] {'head'}, dimensions={0} | all-to-all | bytes 614400 | tf_op jit(solution)/shard_map/all_to_all | solution.py:781
  57.9 27.2 %collective-permute-done.6.refs_2_ = bf16[4,40,3840]{2,1,0:T(8,128)(2,1)} collective-permute-done((bf16[4,40,3840]{2,1,0:T(8,128)(2,1)}, bf16[4,40,3840]{2,1,0:T(8,128)(2,1)}, u32[]{:S(2)}, u32[]{:S(2)}) %collective-permute-start.6) | collective-permute-done | bytes 1228832 | tf_op jit(solution)/shard_map/ppermute | solution.py:760
  95.6 11.9 %collective-permute-done.8.refs_3_ = bf16[4,40,1920]{2,1,0:T(8,128)(2,1)S(1)} collective-permute-done((bf16[4,40,1920]{2,1,0:T(8,128)(2,1)}, bf16[4,40,1920]{2,1,0:T(8,128)(2,1)S(1)}, u32[]{:S(2)}, u32[]{:S(2)}) %collective-permute-start.8) | collective-permute-done | bytes 614432 | tf_op jit(solution)/shard_map/ppermute | solution.py:760
  107.5 11.8 %collective-permute-done.7.across_ref = bf16[4,160,964]{2,1,0:T(8,128)(2,1)S(1)} collective-permute-done((bf16[4,160,964]{2,1,0:T(8,128)(2,1)}, bf16[4,160,964]{2,1,0:T(8,128)(2,1)S(1)}, u32[]{:S(2)}, u32[]{:S(2)}) %collective-permute-start.7) | collective-permute-done | bytes 1233952 | tf_op jit(solution)/shard_map/ppermute | solution.py:760
  137.6 5.5 shard_map.170
  144.6 9.6 %shard_map.171 = (bf16[4,4,80,256]{3,2,1,0:T(8,128)(2,1)}, f32[4,1,1024]{2,1,0:T(1,128)S(1)}) custom-call(f32[3,4,80,1024]{3,2,1,0:T(8,128)S(1)} %bitcast.159, f32[80,1]{1,0:T(8,128)S(1)} %copy.43.scale_ref, s32[1024,1]{1,0:T(8,128)S(1)} %copy.44.col_ref, s32[1,1024]{1,0:T(1,128)S(1)} %constant_dynamic-slice_fusion.row_ref), custom_call_target="tpu_custom_call" | custom-call | flops 1048576 | bytes 1048576 | tf_op jit(solution)/shard_map/pallas_call | solution.py:409
  159.5 9.5 %all-to-all-done.2 = bf16[4,320,256]{2,1,0:T(8,128)(2,1)S(1)} async-done(((bf16[4,320,256]{2,1,0:T(8,128)(2,1)}), bf16[4,320,256]{2,1,0:T(8,128)(2,1)S(1)}, u32[]{:S(2)}, u32[]{:S(2)}) %all-to-all-start.2) | async-done | bytes 655392 | tf_op jit(solution)/shard_map/all_to_all | solution.py:781
  169.5 4.9 shard_map.172
  180.5 9.7 %collective-permute-done.15.across_ref = bf16[4,160,960]{2,1,0:T(8,128)(2,1)} collective-permute-done((bf16[4,160,960]{2,1,0:T(8,128)(2,1)S(1)}, bf16[4,160,960]{2,1,0:T(8,128)(2,1)}, u32[]{:S(2)}, u32[]{:S(2)}) %collective-permute-start.15) | collective-permute-done | bytes 1228832 | tf_op jit(solution)/shard_map/ppermute | solution.py:760
  194.1 18.0 %collective-permute-done.16.refs_2_ = bf16[256,1280]{1,0:T(8,128)(2,1)S(1)} collective-permute-done((bf16[256,1280]{1,0:T(8,128)(2,1)S(1)}, bf16[256,1280]{1,0:T(8,128)(2,1)S(1)}, u32[]{:S(2)}, u32[]{:S(2)}) %collective-permute-start.16) | collective-permute-done | bytes 655392 | tf_op jit(solution)/shard_map/ppermute | solution.py:760
  212.1 7.0 %collective-permute-done.18.refs_1_ = bf16[4,40,3840]{2,1,0:T(8,128)(2,1)} collective-permute-done((bf16[4,40,3840]{2,1,0:T(8,128)(2,1)}, bf16[4,40,3840]{2,1,0:T(8,128)(2,1)}, u32[]{:S(2)}, u32[]{:S(2)}) %collective-permute-start.18) | collective-permute-done | bytes 1228832 | tf_op jit(solution)/shard_map/ppermute | solution.py:760
  237.5 8.9 %shard_map.175 = (bf16[4,4,80,256]{3,2,1,0:T(8,128)(2,1)S(1)}, f32[4,1,1024]{2,1,0:T(1,128)S(1)}) custom-call(f32[3,4,80,1024]{3,2,1,0:T(8,128)S(1)} %bitcast.161, f32[80,1]{1,0:T(8,128)S(1)} %copy.45.scale_ref, s32[1024,1]{1,0:T(8,128)S(1)} %copy.44.col_ref, s32[1,1024]{1,0:T(1,128)S(1)} %constant_dynamic-slice_fusion.row_ref), custom_call_target="tpu_custom_call" | custom-call | flops 1048576 | bytes 1048576 | tf_op jit(solution)/shard_map/pallas_call | solution.py:409
  252.3 10.3 %all-to-all-done.3 = bf16[4,320,256]{2,1,0:T(8,128)(2,1)} async-done(((bf16[4,320,256]{2,1,0:T(8,128)(2,1)}), bf16[4,320,256]{2,1,0:T(8,128)(2,1)}, u32[]{:S(2)}, u32[]{:S(2)}) %all-to-all-start.3) | async-done | bytes 655392 | tf_op jit(solution)/shard_map/all_to_all | solution.py:781
  262.6 5.1 shard_map.176
  289.8 7.0 %shard_map.177 = (bf16[2,2,4,40,3840]{4,3,2,1,0:T(8,128)(2,1)S(1)}, bf16[2,2,4,40,3840]{4,3,2,1,0:T(8,128)(2,1)S(1)}) custom-call(s32[3]{0:T(128)S(1)} %pad_add_fusion.place_ref.core_ref, bf16[1280,256]{1,0:T(8,128)(2,1)} %bitcast.43.attended_ref, bf16[256,1280]{1,0:T(8,128)(2,1)S(1)} %copy-done.28, bf16[256,1280]{1,0:T(8,128)(2,1)S(1)} %copy-done.48, ...), custom_call_target="tpu_custom_call" | custom-call | flops 1048576 | bytes 1048576 | tf_op jit(solution)/shard_map/pallas_call | solution.py:571
  305.7 11.7 %shard_map.178 = (bf16[3,4,80,1024]{3,2,1,0:T(8,128)(2,1)S(1)}, f32[80,128]{1,0:T(8,128)S(1)}) custom-call(f32[3,4,80,1024]{3,2,1,0:T(8,128)S(1)} %bitcast.162, bf16[4,4,80,256]{3,2,1,0:T(8,128)(2,1)} %bitcast.50.grad_ref, f32[4,1,1024]{2,1,0:T(1,128)S(1)} %get-tuple-element.158.lse_ref, f32[80,1]{1,0:T(8,128)S(1)} %copy.45.scale_ref, ...), custom_call_target="tpu_custom_call" | custom-call | flops 1048576 | bytes 1048576 | tf_op jit(solution)/shard_map/pallas_call | solution.py:502
  319.7 9.4 %shard_map.179 = (f32[2,2,128,1280]{3,2,1,0:T(8,128)S(1)}, bf16[2,2,128,1280]{3,2,1,0:T(8,128)(2,1)}, f32[4,160,960]{2,1,0:T(8,128)S(1)}, bf16[4,160,960]{2,1,0:T(8,128)(2,1)}) custom-call(s32[3]{0:T(128)S(1)} %pad_add_fusion.place_ref.core_ref, bf16[960,1024]{1,0:T(8,128)(2,1)S(1)} %bitcast.193, bf16[1280,960]{1,0:T(8,128)(2,1)S(1)} %bitcast.158, ...), custom_call_target="tpu_custom_call" | custom-call | flops 1048576 | bytes 1048576 | tf_op jit(solution)/shard_map/pallas_call | solution.py:730
  340.6 5.2 add_convert_fusion.1
  345.8 10.2 %collective-permute-done.31 = bf16[2,128,1280]{2,1,0:T(8,128)(2,1)} collective-permute-done((bf16[2,128,1280]{2,1,0:T(8,128)(2,1)S(1)}, bf16[2,128,1280]{2,1,0:T(8,128)(2,1)}, u32[]{:S(2)}, u32[]{:S(2)}) %collective-permute-start.31) | collective-permute-done | bytes 655392 | tf_op jit(solution)/shard_map/ppermute | solution.py:760
  380.0 5.9 shard_map.180
  390.3 16.4 %collective-permute-done.32 = bf16[4,40,1920]{2,1,0:T(8,128)(2,1)} collective-permute-done((bf16[4,40,1920]{2,1,0:T(8,128)(2,1)}, bf16[4,40,1920]{2,1,0:T(8,128)(2,1)}, u32[]{:S(2)}, u32[]{:S(2)}) %collective-permute-start.32) | collective-permute-done | bytes 614432 | tf_op jit(solution)/shard_map/ppermute | solution.py:760
  416.8 11.2 %shard_map.181 = (bf16[3,4,80,1024]{3,2,1,0:T(8,128)(2,1)S(1)}, f32[80,128]{1,0:T(8,128)S(1)}) custom-call(f32[3,4,80,1024]{3,2,1,0:T(8,128)S(1)} %bitcast.160, bf16[4,4,80,256]{3,2,1,0:T(8,128)(2,1)S(1)} %bitcast.191, f32[4,1,1024]{2,1,0:T(1,128)S(1)} %get-tuple-element.173.lse_ref, f32[80,1]{1,0:T(8,128)S(1)} %copy.43.scale_ref, ...), custom_call_target="tpu_custom_call" | custom-call | flops 1048576 | bytes 1048576 | tf_op jit(solution)/shard_map/pallas_call | solution.py:502
  429.3 6.3 add_convert_fusion
  435.5 8.2 %shard_map.182 = (f32[2,2,128,1280]{3,2,1,0:T(8,128)S(1)}, bf16[2,2,128,1280]{3,2,1,0:T(8,128)(2,1)S(1)}, f32[4,160,960]{2,1,0:T(8,128)S(1)}, bf16[4,160,960]{2,1,0:T(8,128)(2,1)S(1)}) custom-call(s32[3]{0:T(128)S(1)} %pad_add_fusion.place_ref.core_ref, bf16[960,1024]{1,0:T(8,128)(2,1)S(1)} %bitcast.192, bf16[1280,960]{1,0:T(8,128)(2,1)S(1)} %bitcast.168, ...), custom_call_target="tpu_custom_call" | custom-call | flops 1048576 | bytes 1048576 | tf_op jit(solution)/shard_map/pallas_call | solution.py:730
  449.0 25.0 %collective-permute-done.40 = bf16[4,40,3840]{2,1,0:T(8,128)(2,1)S(1)} collective-permute-done((bf16[4,40,3840]{2,1,0:T(8,128)(2,1)S(1)}, bf16[4,40,3840]{2,1,0:T(8,128)(2,1)S(1)}, u32[]{:S(2)}, u32[]{:S(2)}) %collective-permute-start.40) | collective-permute-done | bytes 1228832 | tf_op jit(solution)/shard_map/ppermute | solution.py:760
  474.0 12.6 %collective-permute-done.38 = bf16[4,40,1920]{2,1,0:T(8,128)(2,1)S(1)} collective-permute-done((bf16[4,40,1920]{2,1,0:T(8,128)(2,1)S(1)}, bf16[4,40,1920]{2,1,0:T(8,128)(2,1)S(1)}, u32[]{:S(2)}, u32[]{:S(2)}) %collective-permute-start.38) | collective-permute-done | bytes 614432 | tf_op jit(solution)/shard_map/ppermute | solution.py:760
  494.1 39.7 %collective-permute-done.41 = bf16[2,128,1280]{2,1,0:T(8,128)(2,1)S(1)} collective-permute-done((bf16[2,128,1280]{2,1,0:T(8,128)(2,1)S(1)}, bf16[2,128,1280]{2,1,0:T(8,128)(2,1)S(1)}, u32[]{:S(2)}, u32[]{:S(2)}) %collective-permute-start.41) | collective-permute-done | bytes 655392 | tf_op jit(solution)/shard_map/ppermute | solution.py:760
  556.3 7.9 %collective-permute-done.48 = f32[2,80]{1,0:T(2,128)S(1)} collective-permute-done((f32[2,80]{1,0:T(2,128)S(1)}, f32[2,80]{1,0:T(2,128)S(1)}, u32[]{:S(2)}, u32[]{:S(2)}) %collective-permute-start.48) | collective-permute-done | bytes 672 | tf_op jit(solution)/shard_map/ppermute | solution.py:760
  579.7 17.8 %reduce-scatter.11.cloned.1.call-done = bf16[1,40,3840]{2,1,0:T(8,128)(2,1)} async-done(((bf16[4,40,3840]{2,1,0:T(8,128)(2,1)}), bf16[1,40,3840]{2,1,0:T(8,128)(2,1)}) %reduce-scatter.11.cloned.1.call-update) | async-done | bytes 307216 | tf_op jit(solution)/shard_map/reduce_scatter | solution.py:810
  597.4 31.3 %reduce-scatter.9.cloned.1.call-done = bf16[1,40,3840]{2,1,0:T(8,128)(2,1)} async-done(((bf16[4,40,3840]{2,1,0:T(8,128)(2,1)}), bf16[1,40,3840]{2,1,0:T(8,128)(2,1)}) %reduce-scatter.9.cloned.1.call-update) | async-done | bytes 307216 | tf_op jit(solution)/shard_map/reduce_scatter | solution.py:810
  (473 shorter events, 231.0 us)
Async XLA Ops:
  7.2 48.7 %all-gather.9.cloned.1.call-start = ((), (), s32[]{:S(2)}) async-start(), calls=%async_computation.16 | async-start | bytes 1536000 | tf_op jit(solution)/shard_map/all_gather | solution.py:794
  20.2 68.9 %all-gather.11.cloned.1.call-start = ((), (), s32[]{:S(2)}) async-start(), calls=%async_computation.17 | async-start | bytes 1638400 | tf_op jit(solution)/shard_map/all_gather | solution.py:794
  56.0 66.4 %all-gather.13.cloned.1.call-start = ((), (), s32[]{:S(2)}) async-start(), calls=%async_computation.18 | async-start | bytes 1638400 | tf_op jit(solution)/shard_map/all_gather | solution.py:794
  56.1 29.1 %collective-permute-start.6 = (bf16[4,40,3840]{2,1,0:T(8,128)(2,1)}, bf16[4,40,3840]{2,1,0:T(8,128)(2,1)}, u32[]{:S(2)}, u32[]{:S(2)}) collective-permute-start(bf16[4,40,3840]{2,1,0:T(8,128)(2,1)} %bitcast.19.refs_0_), channel_id=1, source_target_pairs={{0,2},{1,3},{2,0},{3,1},{4,6},{5,7},{6,4},{7,5},{8,10},{9,11},{10,... | collective-permute-start | bytes 3686408 | tf_op jit(solution)/shard_map/ppermute | solution.py:760
  56.5 28.7 %collective-permute-start.5 = (bf16[4,40,3840]{2,1,0:T(8,128)(2,1)}, bf16[4,40,3840]{2,1,0:T(8,128)(2,1)}, u32[]{:S(2)}, u32[]{:S(2)}) collective-permute-start(bf16[4,40,3840]{2,1,0:T(8,128)(2,1)} %bitcast.19.refs_0_), channel_id=1, source_target_pairs={{0,4},{4,0},{1,5},{5,1},{2,6},{6,2},{3,7},{7,3},{8,12},{12,8},{9,1... | collective-permute-start | bytes 3686408 | tf_op jit(solution)/shard_map/ppermute | solution.py:760
  89.1 80.0 %all-gather.15.cloned.1.call-start = ((), (), s32[]{:S(2)}) async-start(), calls=%async_computation.19 | async-start | bytes 1536000 | tf_op jit(solution)/shard_map/all_gather | solution.py:794
  89.2 30.1 %collective-permute-start.7 = (bf16[4,160,964]{2,1,0:T(8,128)(2,1)}, bf16[4,160,964]{2,1,0:T(8,128)(2,1)S(1)}, u32[]{:S(2)}, u32[]{:S(2)}) collective-permute-start(bf16[4,160,964]{2,1,0:T(8,128)(2,1)} %bitcast.194), channel_id=1, source_target_pairs={{0,4},{4,0},{1,5},{5,1},{2,6},{6,2},{3,7},{7,3},{8,12},{12,8},{9,1... | collective-permute-start | bytes 3701768 | tf_op jit(solution)/shard_map/ppermute | solution.py:760
  122.9 35.9 %collective-permute-start.10 = (bf16[4,40,3840]{2,1,0:T(8,128)(2,1)}, bf16[4,40,3840]{2,1,0:T(8,128)(2,1)}, u32[]{:S(2)}, u32[]{:S(2)}) collective-permute-start(bf16[4,40,3840]{2,1,0:T(8,128)(2,1)} %bitcast.19.refs_0_), channel_id=1, source_target_pairs={{0,1},{1,0},{2,3},{3,2},{4,5},{5,4},{6,7},{7,6},{8,9},{9,8},{10,11... | collective-permute-start | bytes 3686408 | tf_op jit(solution)/shard_map/ppermute | solution.py:760
  123.0 36.5 %collective-permute-start.11 = (bf16[4,40,3840]{2,1,0:T(8,128)(2,1)}, bf16[4,40,3840]{2,1,0:T(8,128)(2,1)}, u32[]{:S(2)}, u32[]{:S(2)}) collective-permute-start(bf16[4,40,3840]{2,1,0:T(8,128)(2,1)} %collective-permute-done.5.refs_1_), channel_id=1, source_target_pairs={{0,1},{1,0},{2,3},{3,2},{4,5},{5,4},{6,7},{7,6},{8,9},{9,8},{10,11... | collective-permute-start | bytes 3686408 | tf_op jit(solution)/shard_map/ppermute | solution.py:760
  125.4 43.6 %collective-permute-start.12 = (bf16[4,40,3840]{2,1,0:T(8,128)(2,1)}, bf16[4,40,3840]{2,1,0:T(8,128)(2,1)}, u32[]{:S(2)}, u32[]{:S(2)}) collective-permute-start(bf16[4,40,3840]{2,1,0:T(8,128)(2,1)} %collective-permute-done.6.refs_2_), channel_id=1, source_target_pairs={{0,1},{1,0},{2,3},{3,2},{4,5},{5,4},{6,7},{7,6},{8,9},{9,8},{10,11... | collective-permute-start | bytes 3686408 | tf_op jit(solution)/shard_map/ppermute | solution.py:760
  125.5 28.7 %collective-permute-start.9 = (bf16[4,40,1920]{2,1,0:T(8,128)(2,1)}, bf16[4,40,1920]{2,1,0:T(8,128)(2,1)}, u32[]{:S(2)}, u32[]{:S(2)}) collective-permute-start(bf16[4,40,1920]{2,1,0:T(8,128)(2,1)} %slice.147), channel_id=1, source_target_pairs={{0,4},{4,0},{1,5},{5,1},{2,6},{6,2},{3,7},{7,3},{8,12},{12,8},{9,1... | collective-permute-start | bytes 1843208 | tf_op jit(solution)/shard_map/ppermute | solution.py:760
  158.9 31.3 %collective-permute-start.15 = (bf16[4,160,960]{2,1,0:T(8,128)(2,1)S(1)}, bf16[4,160,960]{2,1,0:T(8,128)(2,1)}, u32[]{:S(2)}, u32[]{:S(2)}) collective-permute-start(bf16[4,160,960]{2,1,0:T(8,128)(2,1)S(1)} %bitcast.196), channel_id=1, source_target_pairs={{0,4},{4,0},{1,5},{5,1},{2,6},{6,2},{3,7},{7,3},{8,12},{12,8},{9,1... | collective-permute-start | bytes 3686408 | tf_op jit(solution)/shard_map/ppermute | solution.py:760
  169.1 43.0 %collective-permute-start.19 = (bf16[4,40,3840]{2,1,0:T(8,128)(2,1)}, bf16[4,40,3840]{2,1,0:T(8,128)(2,1)}, u32[]{:S(2)}, u32[]{:S(2)}) collective-permute-start(bf16[4,40,3840]{2,1,0:T(8,128)(2,1)} %bitcast.34.refs_0_), channel_id=1, source_target_pairs={{0,2},{1,3},{2,0},{3,1},{4,6},{5,7},{6,4},{7,5},{8,10},{9,11},{10,... | collective-permute-start | bytes 3686408 | tf_op jit(solution)/shard_map/ppermute | solution.py:760
  190.2 28.9 %collective-permute-start.18 = (bf16[4,40,3840]{2,1,0:T(8,128)(2,1)}, bf16[4,40,3840]{2,1,0:T(8,128)(2,1)}, u32[]{:S(2)}, u32[]{:S(2)}) collective-permute-start(bf16[4,40,3840]{2,1,0:T(8,128)(2,1)} %bitcast.34.refs_0_), channel_id=1, source_target_pairs={{0,4},{4,0},{1,5},{5,1},{2,6},{6,2},{3,7},{7,3},{8,12},{12,8},{9,1... | collective-permute-start | bytes 3686408 | tf_op jit(solution)/shard_map/ppermute | solution.py:760
  225.8 36.8 %collective-permute-start.24 = (bf16[4,40,3840]{2,1,0:T(8,128)(2,1)}, bf16[4,40,3840]{2,1,0:T(8,128)(2,1)}, u32[]{:S(2)}, u32[]{:S(2)}) collective-permute-start(bf16[4,40,3840]{2,1,0:T(8,128)(2,1)} %collective-permute-done.18.refs_1_), channel_id=1, source_target_pairs={{0,1},{1,0},{2,3},{3,2},{4,5},{5,4},{6,7},{7,6},{8,9},{9,8},{10,11... | collective-permute-start | bytes 3686408 | tf_op jit(solution)/shard_map/ppermute | solution.py:760
  227.1 35.4 %collective-permute-start.25 = (bf16[4,40,3840]{2,1,0:T(8,128)(2,1)}, bf16[4,40,3840]{2,1,0:T(8,128)(2,1)}, u32[]{:S(2)}, u32[]{:S(2)}) collective-permute-start(bf16[4,40,3840]{2,1,0:T(8,128)(2,1)} %collective-permute-done.19.refs_2_), channel_id=1, source_target_pairs={{0,1},{1,0},{2,3},{3,2},{4,5},{5,4},{6,7},{7,6},{8,9},{9,8},{10,11... | collective-permute-start | bytes 3686408 | tf_op jit(solution)/shard_map/ppermute | solution.py:760
  362.9 43.7 %collective-permute-start.34 = (bf16[4,160,960]{2,1,0:T(8,128)(2,1)}, bf16[4,160,960]{2,1,0:T(8,128)(2,1)}, u32[]{:S(2)}, u32[]{:S(2)}) collective-permute-start(bf16[4,160,960]{2,1,0:T(8,128)(2,1)} %get-tuple-element.171), channel_id=1, source_target_pairs={{0,4},{4,0},{1,5},{5,1},{2,6},{6,2},{3,7},{7,3},{8,12},{12,8},{9,1... | collective-permute-start | bytes 3686408 | tf_op jit(solution)/shard_map/ppermute | solution.py:760
  368.1 38.5 %collective-permute-start.32 = (bf16[4,40,1920]{2,1,0:T(8,128)(2,1)}, bf16[4,40,1920]{2,1,0:T(8,128)(2,1)}, u32[]{:S(2)}, u32[]{:S(2)}) collective-permute-start(bf16[4,40,1920]{2,1,0:T(8,128)(2,1)} %get-tuple-element.226), channel_id=1, source_target_pairs={{0,4},{4,0},{1,5},{5,1},{2,6},{6,2},{3,7},{7,3},{8,12},{12,8},{9,1... | collective-permute-start | bytes 1843208 | tf_op jit(solution)/shard_map/ppermute | solution.py:760
  376.7 166.9 %reduce-scatter.7.cloned.1.call-start = ((), (), s32[]{:S(2)}) async-start(), calls=%async_computation.13 | async-start | bytes 1638400 | tf_op jit(solution)/shard_map/reduce_scatter | solution.py:810
  412.4 163.7 %reduce-scatter.5.cloned.1.call-start = ((), (), s32[]{:S(2)}) async-start(), calls=%async_computation.12 | async-start | bytes 1638400 | tf_op jit(solution)/shard_map/reduce_scatter | solution.py:810
  416.2 32.8 %collective-permute-start.39 = (bf16[4,40,3840]{2,1,0:T(8,128)(2,1)}, bf16[4,40,3840]{2,1,0:T(8,128)(2,1)S(1)}, u32[]{:S(2)}, u32[]{:S(2)}) collective-permute-start(bf16[4,40,3840]{2,1,0:T(8,128)(2,1)} %pad_maximum_fusion), channel_id=1, source_target_pairs={{0,4},{4,0},{1,5},{5,1},{2,6},{6,2},{3,7},{7,3},{8,12},{12,8},{9,1... | collective-permute-start | bytes 3686408 | tf_op jit(solution)/shard_map/ppermute | solution.py:760
  444.1 29.9 %collective-permute-start.40 = (bf16[4,40,3840]{2,1,0:T(8,128)(2,1)S(1)}, bf16[4,40,3840]{2,1,0:T(8,128)(2,1)S(1)}, u32[]{:S(2)}, u32[]{:S(2)}) collective-permute-start(bf16[4,40,3840]{2,1,0:T(8,128)(2,1)S(1)} %pad_maximum_fusion.1), channel_id=1, source_target_pairs={{0,2},{1,3},{2,0},{3,1},{4,6},{5,7},{6,4},{7,5},{8,10},{9,11},{10,... | collective-permute-start | bytes 3686408 | tf_op jit(solution)/shard_map/ppermute | solution.py:760
  446.0 87.9 %collective-permute-start.42 = (bf16[4,160,960]{2,1,0:T(8,128)(2,1)S(1)}, bf16[4,160,960]{2,1,0:T(8,128)(2,1)S(1)}, u32[]{:S(2)}, u32[]{:S(2)}) collective-permute-start(bf16[4,160,960]{2,1,0:T(8,128)(2,1)S(1)} %get-tuple-element.187), channel_id=1, source_target_pairs={{0,4},{4,0},{1,5},{5,1},{2,6},{6,2},{3,7},{7,3},{8,12},{12,8},{9,1... | collective-permute-start | bytes 3686408 | tf_op jit(solution)/shard_map/ppermute | solution.py:760
  447.8 38.8 %collective-permute-start.38 = (bf16[4,40,1920]{2,1,0:T(8,128)(2,1)S(1)}, bf16[4,40,1920]{2,1,0:T(8,128)(2,1)S(1)}, u32[]{:S(2)}, u32[]{:S(2)}) collective-permute-start(bf16[4,40,1920]{2,1,0:T(8,128)(2,1)S(1)} %get-tuple-element.223), channel_id=1, source_target_pairs={{0,2},{1,3},{2,0},{3,1},{4,6},{5,7},{6,4},{7,5},{8,10},{9,11},{10,... | collective-permute-start | bytes 1843208 | tf_op jit(solution)/shard_map/ppermute | solution.py:760
  448.2 41.7 %collective-permute-start.37 = (bf16[4,40,1920]{2,1,0:T(8,128)(2,1)S(1)}, bf16[4,40,1920]{2,1,0:T(8,128)(2,1)S(1)}, u32[]{:S(2)}, u32[]{:S(2)}) collective-permute-start(bf16[4,40,1920]{2,1,0:T(8,128)(2,1)S(1)} %get-tuple-element.224), channel_id=1, source_target_pairs={{0,4},{4,0},{1,5},{5,1},{2,6},{6,2},{3,7},{7,3},{8,12},{12,8},{9,1... | collective-permute-start | bytes 1843208 | tf_op jit(solution)/shard_map/ppermute | solution.py:760
  490.3 43.7 %collective-permute-start.43 = (bf16[4,40,3840]{2,1,0:T(8,128)(2,1)S(1)}, bf16[4,40,3840]{2,1,0:T(8,128)(2,1)S(1)}, u32[]{:S(2)}, u32[]{:S(2)}) collective-permute-start(bf16[4,40,3840]{2,1,0:T(8,128)(2,1)S(1)} %pad_maximum_fusion.2), channel_id=1, source_target_pairs={{0,4},{4,0},{1,5},{5,1},{2,6},{6,2},{3,7},{7,3},{8,12},{12,8},{9,1... | collective-permute-start | bytes 3686408 | tf_op jit(solution)/shard_map/ppermute | solution.py:760
  491.9 42.1 %collective-permute-start.44 = (bf16[4,40,3840]{2,1,0:T(8,128)(2,1)S(1)}, bf16[4,40,3840]{2,1,0:T(8,128)(2,1)S(1)}, u32[]{:S(2)}, u32[]{:S(2)}) collective-permute-start(bf16[4,40,3840]{2,1,0:T(8,128)(2,1)S(1)} %pad_maximum_fusion.3), channel_id=1, source_target_pairs={{0,2},{1,3},{2,0},{3,1},{4,6},{5,7},{6,4},{7,5},{8,10},{9,11},{10,... | collective-permute-start | bytes 3686408 | tf_op jit(solution)/shard_map/ppermute | solution.py:760
  492.3 41.4 %collective-permute-start.41 = (bf16[2,128,1280]{2,1,0:T(8,128)(2,1)S(1)}, bf16[2,128,1280]{2,1,0:T(8,128)(2,1)S(1)}, u32[]{:S(2)}, u32[]{:S(2)}) collective-permute-start(bf16[2,128,1280]{2,1,0:T(8,128)(2,1)S(1)} %fusion.82), channel_id=1, source_target_pairs={{0,2},{1,3},{2,0},{3,1},{4,6},{5,7},{6,4},{7,5},{8,10},{9,11},{10,... | collective-permute-start | bytes 1966088 | tf_op jit(solution)/shard_map/ppermute | solution.py:760
  537.1 60.4 %reduce-scatter.11.cloned.1.call-start = ((), (), s32[]{:S(2)}) async-start(), calls=%async_computation.15 | async-start | bytes 1536000 | tf_op jit(solution)/shard_map/reduce_scatter | solution.py:810
  543.6 29.2 %all-to-all-start.7 = ((bf16[4,40,960]{2,1,0:T(8,128)(2,1)}), bf16[4,40,960]{2,1,0:T(8,128)(2,1)}, u32[]{:S(2)}, u32[]{:S(2)}) async-start(bf16[4,40,960]{2,1,0:T(8,128)(2,1)} %bitcast.217), calls=%async_computation.9 | async-start | bytes 655360 | tf_op jit(solution)/shard_map/all_to_all | solution.py:781
  547.7 81.1 %reduce-scatter.9.cloned.1.call-start = ((), (), s32[]{:S(2)}) async-start(), calls=%async_computation.14 | async-start | bytes 1536000 | tf_op jit(solution)/shard_map/reduce_scatter | solution.py:810
  576.1 55.5 %all-to-all-start.6 = ((bf16[4,40,960]{2,1,0:T(8,128)(2,1)}), bf16[4,40,960]{2,1,0:T(8,128)(2,1)S(1)}, u32[]{:S(2)}, u32[]{:S(2)}) async-start(bf16[4,40,960]{2,1,0:T(8,128)(2,1)} %bitcast.218), calls=%async_computation.7 | async-start | bytes 655360 | tf_op jit(solution)/shard_map/all_to_all | solution.py:781
  (149 other events, 1532.7 us)
Sparse Core Ops, SparseCore 0:
  14.8 32.9 all-gather.8
  56.1 32.9 all-gather.10
  90.7 31.6 all-gather.12
  124.4 30.3 all-gather.14
  412.5 29.8 reduce-scatter.6
  537.2 28.4 reduce-scatter.4
  568.5 28.8 reduce-scatter.10
  599.9 28.8 reduce-scatter.8

commit v10 on v9

--- a/solution.py
+++ b/solution.py
@@ -699,7 +699,7 @@
 
 
 def project_back_kernel(
-    place_ref, bars_ref, weight_ref, normed_ref, own_ref, other_ref, mine_ref, sent_ref, bars_t
+    place_ref, bars_ref, weight_ref, normed_ref, own_ref, other_ref, grad_ref, bars_t
 ):
     @pl.when(pl.program_id(0) == 0)
     def _():
@@ -712,12 +712,7 @@
     own_ref[...] = jnp.where(first_core, one, two)
     other_ref[...] = jnp.where(first_core, two, one).astype(BF16)
     grad = lax.dot_general(normed_ref[...], bars_t[...], TN, preferred_element_type=F32)
-    batch, own, columns = mine_ref.shape
-    grad = grad.reshape(batch, 2, own, columns)
-    first_blk = place_ref[0] == 0
-    one, two = grad[:, 0], grad[:, 1]
-    mine_ref[...] = jnp.where(first_blk, one, two)
-    sent_ref[...] = jnp.where(first_blk, two, one).astype(BF16)
+    grad_ref[...] = grad.astype(BF16)
 
 
 def project_back(bars, weight, normed, token_rows):
@@ -725,8 +720,6 @@
     width = weight.shape[0]
     tile = width // 2
     quarter = pl.BlockSpec((2, 2, token_rows, tile), lambda i, at: (0, 0, 0, i))
-    rows = (4, width // 8, columns)
-    half = pl.BlockSpec((2,) + rows[1:], lambda i, at: (i, 0, 0))
     return pl.pallas_call(
         project_back_kernel,
         grid_spec=pltpu.PrefetchScalarGridSpec(
@@ -737,14 +730,13 @@
                 pl.BlockSpec((tile, columns), lambda i, at: (i, 0)),
                 pl.BlockSpec((length, tile), lambda i, at: (0, i)),
             ],
-            out_specs=[quarter, quarter, half, half],
+            out_specs=[quarter, quarter, pl.BlockSpec((tile, columns), lambda i, at: (i, 0))],
             scratch_shapes=[pltpu.VMEM((length, columns), BF16)],
         ),
         out_shape=[
             jax.ShapeDtypeStruct((2, 2, token_rows, width), F32),
             jax.ShapeDtypeStruct((2, 2, token_rows, width), BF16),
-            jax.ShapeDtypeStruct(rows, F32),
-            jax.ShapeDtypeStruct(rows, BF16),
+            jax.ShapeDtypeStruct((width, columns), BF16),
         ],
         compiler_params=KERNEL,
         cost_estimate=LIGHT,
@@ -810,8 +802,14 @@
     return lax.psum_scatter(parts.astype(BF16), "batch", scatter_dimension=0, tiled=False)
 
 
+def across_sum(halves):
+    blk = lax.axis_index("blk")
+    got = swapped(pick(halves, 1 - blk), "blk", 1).astype(F32)
+    return (pick(halves, blk).astype(F32) + got).astype(BF16)
+
+
 def columns_to_rows(summed):
-    moved = over_head(summed.astype(BF16).reshape(4, -1, summed.shape[-1]))
+    moved = over_head(summed.reshape(4, -1, summed.shape[-1]))
     rows = moved.shape[1]
     return moved.reshape(4, rows, 3, -1).transpose(1, 2, 0, 3).reshape(rows, -1).astype(F32)
 
@@ -888,13 +886,11 @@
     stream, upper = first.astype(F32), upper.astype(F32)
     far, near = swapped(first, "head", 2), other_core(first)
     both = other_core(far)
-    next_columns = qkv_columns(qkv_weight[1], None).reshape(-1, part3)
-    columns, dense_near, near, far, both, next_columns = tied(
-        columns, dense_near, near, far, both, next_columns
-    )
+    columns, dense_near, near, far, both = tied(columns, dense_near, near, far, both)
     token_pieces = (first, near, far, both)
     across, beside = swapped(dense_near, "blk", 1), swapped(dense_near, "head", 2)
     along = along_batch(columns)
+    next_columns = qkv_columns(qkv_weight[1], None).reshape(-1, part3)
     along, across, beside, next_columns = tied(along, across, beside, next_columns)
     qkv_across = swapped(along, "blk", 1)
     one = to_beside(across)
@@ -903,6 +899,7 @@
         qkv_across, one, beside, next_along, dense_own[1]
     )
     two = to_across(beside)
+    next_across = swapped(next_along, "blk", 1)
     pieces = [(dense_near, across, beside, one, two)]
     dense_next = along_batch(dense_next)
     weight, gains = assemble_columns(along, qkv_across, part3)
@@ -913,9 +910,8 @@
     for layer in range(layers):
         normed, factor_one = normalize(stream, gains[layer])
         if layer == 1:
-            normed, next_across, dense_after = tied(normed.astype(BF16), next_across, dense_next)
+            normed, across, beside = tied(normed.astype(BF16), across, beside)
             far, near = swapped(normed, "head", 2), other_core(normed)
-            across = swapped(dense_after, "blk", 1)
             far, near, across, beside = tied(far, near, across, beside)
             token_pieces = (normed, near, far, other_core(far))
             one, two = to_beside(across), to_across(beside)
@@ -930,13 +926,10 @@
         attended, one, two = tied(attended, *pieces[layer][3:])
         pieces[layer] = pieces[layer][:3] + (one, two)
         swaps = tuple(other_core(piece) for piece in pieces[layer])
-        attended_t = over_head(attended)
         if layer == 0:
-            attended_t, swaps, dense_next = tied(attended_t, swaps, dense_next)
-            next_across = swapped(next_along, "blk", 1)
-            beside = swapped(dense_next, "head", 2)
-        else:
-            attended_t, swaps = tied(attended_t, swaps)
+            attended, next_across, dense_next = tied(attended, next_across, dense_next)
+            across, beside = swapped(dense_next, "blk", 1), swapped(dense_next, "head", 2)
+        attended_t, swaps = tied(over_head(attended), swaps)
         attended_t = attended_t.reshape(width, -1)
         denses.append(assemble(pieces[layer] + swaps))
         dense = denses[layer]
@@ -955,7 +948,7 @@
         stream = middle + dot(active, down_w)
     layer_out = swap_halves(stream.astype(BF16).reshape(tokens.shape))
 
-    dense_grad, scale_grads = [None] * layers, [None] * layers
+    scale_grads = [None] * layers
     for layer in reversed(range(layers)):
         (
             stream, factor_one, normed_all, projected, log_total, attended_t, middle,
@@ -972,41 +965,44 @@
             dot_cols(up_bar, up_w), middle, factor_two, gains[layers + layer]
         )
         out_bar = middle_grad.astype(BF16)
+        if layer == 0:
+            out_bar, diagonal = tied(out_bar, diagonal)
+            sent = neighbours_sent(cored, *diagonal)
         attended_grad = over_head(dot_cols(out_w, out_bar).astype(BF16).reshape(4, -1, out_bar.shape[0]))
         grads, others = dense_grads(attended_t, normed_two, active, out_bar, up_bar, down_bar)
         if layer == 0:
-            attended_grad, others, diagonal, got = tied(attended_grad, others, diagonal, got)
-            sent = neighbours_sent(cored, *diagonal)
-            last = cored
-            qkv_sums = [None, over_batch(mine + got.astype(F32))]
+            attended_grad, others, z_sum = tied(attended_grad, others, z_sum)
+            z_across = across_sum(z_sum)
         else:
             attended_grad, others, layer_out = tied(attended_grad, others, layer_out)
         others = other_core(others)
         bars, scale_grads[layer] = attend_back_rows(
             projected, attended_grad, log_total, scale_vecs[layer], segments, token_rows
         )
-        bars, others = tied(bars, others)
+        if layer == 0:
+            bars, others, sent, z_across = tied(bars, others, sent, z_across)
+            summed = own_sum(cored, *sent)
+        else:
+            bars, others = tied(bars, others)
         cored = (grads.astype(F32) + others.astype(F32)).astype(BF16)
         if layer == 0:
-            bars, cored = tied(bars, cored)
+            bars, cored, summed = tied(bars, cored, summed)
             diagonal = diagonal_sent(cored)
-        halves, to_core, mine, got = project_back(bars, qkv, normed_all, token_rows)
+            summed = over_batch(summed)
+        halves, to_core, qkv_grad = project_back(bars, qkv, normed_all, token_rows)
         halves = halves + other_core(to_core).astype(F32)
+        z_sum = over_batch(qkv_grad.reshape(4, 2, -1, qkv_grad.shape[-1]))
         if layer == 0:
-            got = swapped(got, "blk", 1)
-            halves, diagonal, sent = tied(halves, diagonal, sent)
-            dense_grad[1] = over_batch(own_sum(last, *sent))
+            halves, diagonal = tied(halves, diagonal)
             sent = neighbours_sent(cored, *diagonal)
             normed_grad = scatter_row(halves)
-            normed_grad, got, sent = tied(normed_grad, got, sent)
-            qkv_sums[0] = over_batch(mine + got.astype(F32))
-            dense_grad[0] = over_batch(own_sum(cored, *sent))
-            qkv_grads = [columns_to_rows(part) for part in qkv_sums]
+            normed_grad, sent, summed = tied(normed_grad, sent, summed)
+            dense_grad = [over_batch(own_sum(cored, *sent)), summed]
+            qkv_grads = [columns_to_rows(across_sum(z_sum)), columns_to_rows(z_across)]
         else:
             normed_grad = scatter_row(halves)
-            normed_grad, cored, got = tied(normed_grad, cored, got)
+            normed_grad, cored = tied(normed_grad, cored)
             diagonal = diagonal_sent(cored)
-            got = swapped(got, "blk", 1)
         upper = middle_grad + lower_of(normed_grad, stream, factor_one, gains[layer])
     input_grad = swap_halves(upper.astype(BF16).reshape(tokens.shape)).astype(F32)
     scale_total = sum_all(jnp.stack(scale_grads))

time: 650 us -> 587 us (0.903)
  waiting for transfers between devices: 305 us -> 215 us
  blocking collectives: 9.94 us -> 28.5 us
    ppermute x51, waiting for transfers between devices: 230 us -> 183 us  [swapped(): return lax.ppermute(array, axis, [(i, i ^ mask) for i in range(size)])]
    reduce_scatter x4, waiting for transfers between devices: 49.1 us -> 6.24 us  [over_batch(): lax.psum_scatter(parts.astype(BF16), 'batch', scatter_dimension=0, tiled=...]
    all_to_all x1, blocking collectives: 9.94 us -> 28.5 us  [over_head(): lax.all_to_all(parts, 'head', split_axis=0, concat_axis=0, tiled=True)]
    convert_element_type x4 -> x1, other arithmetic: 11.8 us -> 3.5 us  [over_batch(): parts.astype(BF16)]
    unnamed x230 -> x248, local copies, waits for them, and re-layouts: 51.1 us -> 52.9 us
  transfers between devices with their start and end apart: 66 -> 66, of which waited for: 26 -> 29; matrix products, arithmetic and copies ran while one was open for 12% -> 13% of each run, Pallas kernels for 13% -> 14%
where the time goes in v10:
time: 587 us; the launch traced here: 578 us
  waiting for transfers between devices  215 us (37%)
  Pallas kernels  95.9 us (16%)
  local copies, waits for them, and re-layouts  79.5 us (14%)
  starting transfers between devices  73.7 us (13%)
  other arithmetic  51 us (9%)
  blocking collectives  28.5 us (5%)
  matrix products  17.8 us (3%)
  between operations  15.9 us (3%)
    ppermute x51, waiting for transfers between devices, swapped(): return lax.ppermute(array, axis, [(i, i ^ mask) for i in range(size)])  183 us
    unnamed x248, local copies, waits for them, and re-layouts  52.9 us
    ppermute x51, starting transfers between devices, swapped(): return lax.ppermute(array, axis, [(i, i ^ mask) for i in range(size)])  45.4 us
    all_to_all x1, blocking collectives, over_head(): lax.all_to_all(parts, 'head', split_axis=0, concat_axis=0, tiled=True)  28.5 us
    all_to_all x7, starting transfers between devices, over_head(): lax.all_to_all(parts, 'head', split_axis=0, concat_axis=0, tiled=True)  27.2 us
    pallas_call x2, Pallas kernels, attend_back_rows(): pl.pallas_call(functools.partial(attend_back_kernel, token_rows), grid=(l...  22.5 us
    all_to_all x7, waiting for transfers between devices, over_head(): lax.all_to_all(parts, 'head', split_axis=0, concat_axis=0, tiled=True)  22.5 us
    pallas_call x2, Pallas kernels, attend_rows(): pl.pallas_call(functools.partial(attend_kernel, token_rows), grid=(local_...  18.5 us
  transfers between devices with their start and end apart: 66, of which 29 were waited for; matrix products, arithmetic and copies ran while one was open for 13% of the time, Pallas kernels for 14%

profile of v10, /device:TPU:0, one launch (start us, length us, event | category | flops | bytes accessed | tf_op | source)
XLA Modules:
  0.0 577.8 jit_solution(12784021315216292992)
XLA Ops:
  22.0 5.1 collective-permute-done
  31.0 14.1 %collective-permute-done.3.refs_2_ = bf16[256,1280]{1,0:T(8,128)(2,1)S(1)} collective-permute-done((bf16[256,1280]{1,0:T(8,128)(2,1)S(1)}, bf16[256,1280]{1,0:T(8,128)(2,1)S(1)}, u32[]{:S(2)}, u32[]{:S(2)}) %collective-permute-start.3) | collective-permute-done | bytes 655392 | tf_op jit(solution)/shard_map/ppermute | solution.py:752
  52.5 28.5 %all_to_all.40 = bf16[4,40,960]{2,1,0:T(8,128)(2,1)} all-to-all(bf16[4,40,960]{2,1,0:T(8,128)(2,1)S(1)} %reshape.239), channel_id=1, replica_groups=mesh['batch'=4,'blk'=2,'head'=4] {'head'}, dimensions={0} | all-to-all | bytes 614400 | tf_op jit(solution)/shard_map/all_to_all | solution.py:773
  87.4 12.4 %collective-permute-done.8.refs_3_ = bf16[4,40,1920]{2,1,0:T(8,128)(2,1)S(1)} collective-permute-done((bf16[4,40,1920]{2,1,0:T(8,128)(2,1)S(1)}, bf16[4,40,1920]{2,1,0:T(8,128)(2,1)S(1)}, u32[]{:S(2)}, u32[]{:S(2)}) %collective-permute-start.8) | collective-permute-done | bytes 614432 | tf_op jit(solution)/shard_map/ppermute | solution.py:752
  99.9 12.8 %collective-permute-done.7.across_ref = bf16[4,160,964]{2,1,0:T(8,128)(2,1)S(1)} collective-permute-done((bf16[4,160,964]{2,1,0:T(8,128)(2,1)}, bf16[4,160,964]{2,1,0:T(8,128)(2,1)S(1)}, u32[]{:S(2)}, u32[]{:S(2)}) %collective-permute-start.7) | collective-permute-done | bytes 1233952 | tf_op jit(solution)/shard_map/ppermute | solution.py:752
  131.5 5.4 shard_map.170
  138.5 9.6 %shard_map.171 = (bf16[4,4,80,256]{3,2,1,0:T(8,128)(2,1)}, f32[4,1,1024]{2,1,0:T(1,128)S(1)}) custom-call(f32[3,4,80,1024]{3,2,1,0:T(8,128)S(1)} %bitcast.174, f32[80,1]{1,0:T(8,128)S(1)} %copy.41.scale_ref, s32[1024,1]{1,0:T(8,128)S(1)} %copy.42.col_ref, s32[1,1024]{1,0:T(1,128)S(1)} %constant_dynamic-slice_fusion.row_ref), custom_call_target="tpu_custom_call" | custom-call | flops 1048576 | bytes 1048576 | tf_op jit(solution)/shard_map/pallas_call | solution.py:409
  148.1 11.1 %collective-permute-done.9.refs_4_ = bf16[4,40,1920]{2,1,0:T(8,128)(2,1)} collective-permute-done((bf16[4,40,1920]{2,1,0:T(8,128)(2,1)}, bf16[4,40,1920]{2,1,0:T(8,128)(2,1)}, u32[]{:S(2)}, u32[]{:S(2)}) %collective-permute-start.9) | collective-permute-done | bytes 614432 | tf_op jit(solution)/shard_map/ppermute | solution.py:752
  167.3 7.1 %all-to-all-done.2 = bf16[4,320,256]{2,1,0:T(8,128)(2,1)S(1)} async-done(((bf16[4,320,256]{2,1,0:T(8,128)(2,1)}), bf16[4,320,256]{2,1,0:T(8,128)(2,1)S(1)}, u32[]{:S(2)}, u32[]{:S(2)}) %all-to-all-start.2) | async-done | bytes 655392 | tf_op jit(solution)/shard_map/all_to_all | solution.py:773
  174.4 4.8 shard_map.172
  185.2 15.2 %collective-permute-done.17.refs_2_ = bf16[4,40,3840]{2,1,0:T(8,128)(2,1)} collective-permute-done((bf16[4,40,3840]{2,1,0:T(8,128)(2,1)}, bf16[4,40,3840]{2,1,0:T(8,128)(2,1)}, u32[]{:S(2)}, u32[]{:S(2)}) %collective-permute-start.17) | collective-permute-done | bytes 1228832 | tf_op jit(solution)/shard_map/ppermute | solution.py:752
  203.3 14.2 %collective-permute-done.18.refs_2_ = bf16[256,1280]{1,0:T(8,128)(2,1)S(1)} collective-permute-done((bf16[256,1280]{1,0:T(8,128)(2,1)S(1)}, bf16[256,1280]{1,0:T(8,128)(2,1)S(1)}, u32[]{:S(2)}, u32[]{:S(2)}) %collective-permute-start.18) | collective-permute-done | bytes 655392 | tf_op jit(solution)/shard_map/ppermute | solution.py:752
  235.8 9.0 %shard_map.175 = (bf16[4,4,80,256]{3,2,1,0:T(8,128)(2,1)S(1)}, f32[4,1,1024]{2,1,0:T(1,128)S(1)}) custom-call(f32[3,4,80,1024]{3,2,1,0:T(8,128)S(1)} %bitcast.176, f32[80,1]{1,0:T(8,128)S(1)} %copy.43.scale_ref, s32[1024,1]{1,0:T(8,128)S(1)} %copy.42.col_ref, s32[1,1024]{1,0:T(1,128)S(1)} %constant_dynamic-slice_fusion.row_ref), custom_call_target="tpu_custom_call" | custom-call | flops 1048576 | bytes 1048576 | tf_op jit(solution)/shard_map/pallas_call | solution.py:409
  246.2 4.4 all-to-all-start.3
  250.6 10.3 %all-to-all-done.3 = bf16[4,320,256]{2,1,0:T(8,128)(2,1)} async-done(((bf16[4,320,256]{2,1,0:T(8,128)(2,1)}), bf16[4,320,256]{2,1,0:T(8,128)(2,1)}, u32[]{:S(2)}, u32[]{:S(2)}) %all-to-all-start.3) | async-done | bytes 655392 | tf_op jit(solution)/shard_map/all_to_all | solution.py:773
  260.9 5.1 shard_map.176
  287.3 7.0 %shard_map.177 = (bf16[2,2,4,40,3840]{4,3,2,1,0:T(8,128)(2,1)S(1)}, bf16[2,2,4,40,3840]{4,3,2,1,0:T(8,128)(2,1)S(1)}) custom-call(s32[3]{0:T(128)S(1)} %pad_add_fusion.place_ref.core_ref, bf16[1280,256]{1,0:T(8,128)(2,1)} %bitcast.43.attended_ref, bf16[256,1280]{1,0:T(8,128)(2,1)S(1)} %copy-done.31, bf16[256,1280]{1,0:T(8,128)(2,1)S(1)} %copy-done.52, ...), custom_call_target="tpu_custom_call" | custom-call | flops 1048576 | bytes 1048576 | tf_op jit(solution)/shard_map/pallas_call | solution.py:571
  303.2 11.7 %shard_map.178 = (bf16[3,4,80,1024]{3,2,1,0:T(8,128)(2,1)S(1)}, f32[80,128]{1,0:T(8,128)S(1)}) custom-call(f32[3,4,80,1024]{3,2,1,0:T(8,128)S(1)} %bitcast.177, bf16[4,4,80,256]{3,2,1,0:T(8,128)(2,1)} %bitcast.50.grad_ref, f32[4,1,1024]{2,1,0:T(1,128)S(1)} %get-tuple-element.160.lse_ref, f32[80,1]{1,0:T(8,128)S(1)} %copy.43.scale_ref, ...), custom_call_target="tpu_custom_call" | custom-call | flops 1048576 | bytes 1048576 | tf_op jit(solution)/shard_map/pallas_call | solution.py:502
  314.9 9.2 %shard_map.179 = (f32[2,2,128,1280]{3,2,1,0:T(8,128)S(1)}, bf16[2,2,128,1280]{3,2,1,0:T(8,128)(2,1)}, bf16[1280,960]{1,0:T(8,128)(2,1)S(1)}) custom-call(s32[3]{0:T(128)S(1)} %pad_add_fusion.place_ref.core_ref, bf16[960,1024]{1,0:T(8,128)(2,1)S(1)} %bitcast.210, bf16[1280,960]{1,0:T(8,128)(2,1)S(1)} %bitcast.173, bf16[1024,1280]{1,0:T(8,128)(2,1)S(1)} %copy-done.21), custom_call_target="tpu_custom_call" | custom-call | flops 1048576 | bytes 1048576 | tf_op jit(solution)/shard_map/pallas_call | solution.py:723
  334.1 5.2 add_convert_fusion.1
  339.3 10.1 %collective-permute-done.31 = bf16[2,128,1280]{2,1,0:T(8,128)(2,1)S(1)} collective-permute-done((bf16[2,128,1280]{2,1,0:T(8,128)(2,1)S(1)}, bf16[2,128,1280]{2,1,0:T(8,128)(2,1)S(1)}, u32[]{:S(2)}, u32[]{:S(2)}) %collective-permute-start.31) | collective-permute-done | bytes 655392 | tf_op jit(solution)/shard_map/ppermute | solution.py:752
  360.3 6.6 %collective-permute-done.33 = bf16[4,40,1920]{2,1,0:T(8,128)(2,1)S(1)} collective-permute-done((bf16[4,40,1920]{2,1,0:T(8,128)(2,1)S(1)}, bf16[4,40,1920]{2,1,0:T(8,128)(2,1)S(1)}, u32[]{:S(2)}, u32[]{:S(2)}) %collective-permute-start.33) | collective-permute-done | bytes 614432 | tf_op jit(solution)/shard_map/ppermute | solution.py:752
  377.3 6.2 %shard_map.180 = (bf16[2,2,4,40,3840]{4,3,2,1,0:T(8,128)(2,1)S(1)}, bf16[2,2,4,40,3840]{4,3,2,1,0:T(8,128)(2,1)S(1)}) custom-call(s32[3]{0:T(128)S(1)} %pad_add_fusion.place_ref.core_ref, bf16[1280,256]{1,0:T(8,128)(2,1)S(1)} %bitcast.207, bf16[256,1280]{1,0:T(8,128)(2,1)S(1)} %copy-done.29, bf16[256,1280]{1,0:T(8,128)(2,1)S(1)} %copy-done.48, ...), custom_call_target="tpu_custom_call" | custom-call | flops 1048576 | bytes 1048576 | tf_op jit(solution)/shard_map/pallas_call | solution.py:571
  395.5 10.8 %shard_map.181 = (bf16[3,4,80,1024]{3,2,1,0:T(8,128)(2,1)S(1)}, f32[80,128]{1,0:T(8,128)S(1)}) custom-call(f32[3,4,80,1024]{3,2,1,0:T(8,128)S(1)} %bitcast.175, bf16[4,4,80,256]{3,2,1,0:T(8,128)(2,1)S(1)} %bitcast.208, f32[4,1,1024]{2,1,0:T(1,128)S(1)} %get-tuple-element.175.lse_ref, f32[80,1]{1,0:T(8,128)S(1)} %copy.41.scale_ref, ...), custom_call_target="tpu_custom_call" | custom-call | flops 1048576 | bytes 1048576 | tf_op jit(solution)/shard_map/pallas_call | solution.py:502
  406.3 22.9 %collective-permute-done.37 = bf16[160,960]{1,0:T(8,128)(2,1)S(1)} collective-permute-done((bf16[160,960]{1,0:T(8,128)(2,1)S(1)}, bf16[160,960]{1,0:T(8,128)(2,1)S(1)}, u32[]{:S(2)}, u32[]{:S(2)}) %collective-permute-start.37) | collective-permute-done | bytes 307232 | tf_op jit(solution)/shard_map/ppermute | solution.py:752
  432.9 7.3 %add_convert_fusion = bf16[2,2,4,40,3840]{4,3,2,1,0:T(8,128)(2,1)} fusion(bf16[2,2,4,40,3840]{4,3,2,1,0:T(8,128)(2,1)} %collective-permute-done.34, bf16[2,2,4,40,3840]{4,3,2,1,0:T(8,128)(2,1)} %copy-done.17), kind=kLoop, calls=%fused_computation | loop fusion | flops 9830400 | bytes 14745600 | tf_op jit(solution)/shard_map/convert_element_type | solution.py:987
  443.6 9.0 %shard_map.182 = (f32[2,2,128,1280]{3,2,1,0:T(8,128)S(1)}, bf16[2,2,128,1280]{3,2,1,0:T(8,128)(2,1)}, bf16[1280,960]{1,0:T(8,128)(2,1)S(1)}) custom-call(s32[3]{0:T(128)S(1)} %pad_add_fusion.place_ref.core_ref, bf16[960,1024]{1,0:T(8,128)(2,1)S(1)} %bitcast.209, bf16[1280,960]{1,0:T(8,128)(2,1)S(1)} %bitcast.183, bf16[1024,1280]{1,0:T(8,128)(2,1)S(1)} %copy-done.19), custom_call_target="tpu_custom_call" | custom-call | flops 1048576 | bytes 1048576 | tf_op jit(solution)/shard_map/pallas_call | solution.py:723
  464.0 8.9 %collective-permute-done.40 = bf16[4,40,1920]{2,1,0:T(8,128)(2,1)} collective-permute-done((bf16[4,40,1920]{2,1,0:T(8,128)(2,1)}, bf16[4,40,1920]{2,1,0:T(8,128)(2,1)}, u32[]{:S(2)}, u32[]{:S(2)}) %collective-permute-start.40) | collective-permute-done | bytes 614432 | tf_op jit(solution)/shard_map/ppermute | solution.py:752
  489.5 30.2 %collective-permute-done.41 = bf16[2,128,1280]{2,1,0:T(8,128)(2,1)S(1)} collective-permute-done((bf16[2,128,1280]{2,1,0:T(8,128)(2,1)S(1)}, bf16[2,128,1280]{2,1,0:T(8,128)(2,1)S(1)}, u32[]{:S(2)}, u32[]{:S(2)}) %collective-permute-start.41) | collective-permute-done | bytes 655392 | tf_op jit(solution)/shard_map/ppermute | solution.py:752
  529.7 5.0 collective-permute-done.48
  549.9 6.2 %reduce-scatter.11.cloned.1.call-done = bf16[1,40,3840]{2,1,0:T(8,128)(2,1)} async-done(((bf16[4,40,3840]{2,1,0:T(8,128)(2,1)}), bf16[1,40,3840]{2,1,0:T(8,128)(2,1)}) %reduce-scatter.11.cloned.1.call-update) | async-done | bytes 307216 | tf_op jit(solution)/shard_map/reduce_scatter | solution.py:802
  563.2 5.1 all-to-all-done.6
  (492 shorter events, 231.6 us)
Async XLA Ops:
  7.2 41.3 %all-gather.9.cloned.1.call-start = ((), (), s32[]{:S(2)}) async-start(), calls=%async_computation.16 | async-start | bytes 1536000 | tf_op jit(solution)/shard_map/all_gather | solution.py:786
  20.8 61.6 %all-gather.11.cloned.1.call-start = ((), (), s32[]{:S(2)}) async-start(), calls=%async_computation.17 | async-start | bytes 1638400 | tf_op jit(solution)/shard_map/all_gather | solution.py:786
  48.5 67.2 %all-gather.13.cloned.1.call-start = ((), (), s32[]{:S(2)}) async-start(), calls=%async_computation.18 | async-start | bytes 1638400 | tf_op jit(solution)/shard_map/all_gather | solution.py:786
  48.6 32.5 %collective-permute-start.6 = (bf16[4,40,3840]{2,1,0:T(8,128)(2,1)}, bf16[4,40,3840]{2,1,0:T(8,128)(2,1)}, u32[]{:S(2)}, u32[]{:S(2)}) collective-permute-start(bf16[4,40,3840]{2,1,0:T(8,128)(2,1)} %bitcast.19.refs_0_), channel_id=1, source_target_pairs={{0,2},{1,3},{2,0},{3,1},{4,6},{5,7},{6,4},{7,5},{8,10},{9,11},{10,... | collective-permute-start | bytes 3686408 | tf_op jit(solution)/shard_map/ppermute | solution.py:752
  50.1 31.0 %collective-permute-start.5 = (bf16[4,40,3840]{2,1,0:T(8,128)(2,1)}, bf16[4,40,3840]{2,1,0:T(8,128)(2,1)}, u32[]{:S(2)}, u32[]{:S(2)}) collective-permute-start(bf16[4,40,3840]{2,1,0:T(8,128)(2,1)} %bitcast.19.refs_0_), channel_id=1, source_target_pairs={{0,4},{4,0},{1,5},{5,1},{2,6},{6,2},{3,7},{7,3},{8,12},{12,8},{9,1... | collective-permute-start | bytes 3686408 | tf_op jit(solution)/shard_map/ppermute | solution.py:752
  82.5 77.3 %all-gather.15.cloned.1.call-start = ((), (), s32[]{:S(2)}) async-start(), calls=%async_computation.19 | async-start | bytes 1536000 | tf_op jit(solution)/shard_map/all_gather | solution.py:786
  82.5 30.1 %collective-permute-start.7 = (bf16[4,160,964]{2,1,0:T(8,128)(2,1)}, bf16[4,160,964]{2,1,0:T(8,128)(2,1)S(1)}, u32[]{:S(2)}, u32[]{:S(2)}) collective-permute-start(bf16[4,160,964]{2,1,0:T(8,128)(2,1)} %bitcast.211), channel_id=1, source_target_pairs={{0,4},{4,0},{1,5},{5,1},{2,6},{6,2},{3,7},{7,3},{8,12},{12,8},{9,1... | collective-permute-start | bytes 3701768 | tf_op jit(solution)/shard_map/ppermute | solution.py:752
  115.8 43.4 %collective-permute-start.10 = (bf16[4,160,960]{2,1,0:T(8,128)(2,1)}, bf16[4,160,960]{2,1,0:T(8,128)(2,1)}, u32[]{:S(2)}, u32[]{:S(2)}) collective-permute-start(bf16[4,160,960]{2,1,0:T(8,128)(2,1)} %bitcast.213), channel_id=1, source_target_pairs={{0,4},{4,0},{1,5},{5,1},{2,6},{6,2},{3,7},{7,3},{8,12},{12,8},{9,1... | collective-permute-start | bytes 3686408 | tf_op jit(solution)/shard_map/ppermute | solution.py:752
  117.8 46.0 %collective-permute-start.11 = (bf16[4,40,3840]{2,1,0:T(8,128)(2,1)}, bf16[4,40,3840]{2,1,0:T(8,128)(2,1)}, u32[]{:S(2)}, u32[]{:S(2)}) collective-permute-start(bf16[4,40,3840]{2,1,0:T(8,128)(2,1)} %bitcast.19.refs_0_), channel_id=1, source_target_pairs={{0,1},{1,0},{2,3},{3,2},{4,5},{5,4},{6,7},{7,6},{8,9},{9,8},{10,11... | collective-permute-start | bytes 3686408 | tf_op jit(solution)/shard_map/ppermute | solution.py:752
  117.9 47.9 %collective-permute-start.12 = (bf16[4,40,3840]{2,1,0:T(8,128)(2,1)}, bf16[4,40,3840]{2,1,0:T(8,128)(2,1)}, u32[]{:S(2)}, u32[]{:S(2)}) collective-permute-start(bf16[4,40,3840]{2,1,0:T(8,128)(2,1)} %collective-permute-done.5.refs_1_), channel_id=1, source_target_pairs={{0,1},{1,0},{2,3},{3,2},{4,5},{5,4},{6,7},{7,6},{8,9},{9,8},{10,11... | collective-permute-start | bytes 3686408 | tf_op jit(solution)/shard_map/ppermute | solution.py:752
  120.3 47.0 %collective-permute-start.13 = (bf16[4,40,3840]{2,1,0:T(8,128)(2,1)}, bf16[4,40,3840]{2,1,0:T(8,128)(2,1)}, u32[]{:S(2)}, u32[]{:S(2)}) collective-permute-start(bf16[4,40,3840]{2,1,0:T(8,128)(2,1)} %collective-permute-done.6.refs_2_), channel_id=1, source_target_pairs={{0,1},{1,0},{2,3},{3,2},{4,5},{5,4},{6,7},{7,6},{8,9},{9,8},{10,11... | collective-permute-start | bytes 3686408 | tf_op jit(solution)/shard_map/ppermute | solution.py:752
  120.4 38.8 %collective-permute-start.9 = (bf16[4,40,1920]{2,1,0:T(8,128)(2,1)}, bf16[4,40,1920]{2,1,0:T(8,128)(2,1)}, u32[]{:S(2)}, u32[]{:S(2)}) collective-permute-start(bf16[4,40,1920]{2,1,0:T(8,128)(2,1)} %slice.147), channel_id=1, source_target_pairs={{0,4},{4,0},{1,5},{5,1},{2,6},{6,2},{3,7},{7,3},{8,12},{12,8},{9,1... | collective-permute-start | bytes 1843208 | tf_op jit(solution)/shard_map/ppermute | solution.py:752
  163.8 36.6 %collective-permute-start.17 = (bf16[4,40,3840]{2,1,0:T(8,128)(2,1)}, bf16[4,40,3840]{2,1,0:T(8,128)(2,1)}, u32[]{:S(2)}, u32[]{:S(2)}) collective-permute-start(bf16[4,40,3840]{2,1,0:T(8,128)(2,1)} %bitcast.34.refs_0_), channel_id=1, source_target_pairs={{0,2},{1,3},{2,0},{3,1},{4,6},{5,7},{6,4},{7,5},{8,10},{9,11},{10,... | collective-permute-start | bytes 3686408 | tf_op jit(solution)/shard_map/ppermute | solution.py:752
  165.8 34.6 %collective-permute-start.16 = (bf16[4,40,3840]{2,1,0:T(8,128)(2,1)}, bf16[4,40,3840]{2,1,0:T(8,128)(2,1)}, u32[]{:S(2)}, u32[]{:S(2)}) collective-permute-start(bf16[4,40,3840]{2,1,0:T(8,128)(2,1)} %bitcast.34.refs_0_), channel_id=1, source_target_pairs={{0,4},{4,0},{1,5},{5,1},{2,6},{6,2},{3,7},{7,3},{8,12},{12,8},{9,1... | collective-permute-start | bytes 3686408 | tf_op jit(solution)/shard_map/ppermute | solution.py:752
  222.3 23.3 %collective-permute-start.22 = (bf16[4,40,1920]{2,1,0:T(8,128)(2,1)}, bf16[4,40,1920]{2,1,0:T(8,128)(2,1)}, u32[]{:S(2)}, u32[]{:S(2)}) collective-permute-start(bf16[4,40,1920]{2,1,0:T(8,128)(2,1)} %slice.155), channel_id=1, source_target_pairs={{0,4},{4,0},{1,5},{5,1},{2,6},{6,2},{3,7},{7,3},{8,12},{12,8},{9,1... | collective-permute-start | bytes 1843208 | tf_op jit(solution)/shard_map/ppermute | solution.py:752
  224.1 26.4 %collective-permute-start.23 = (bf16[4,40,3840]{2,1,0:T(8,128)(2,1)}, bf16[4,40,3840]{2,1,0:T(8,128)(2,1)}, u32[]{:S(2)}, u32[]{:S(2)}) collective-permute-start(bf16[4,40,3840]{2,1,0:T(8,128)(2,1)} %bitcast.34.refs_0_), channel_id=1, source_target_pairs={{0,1},{1,0},{2,3},{3,2},{4,5},{5,4},{6,7},{7,6},{8,9},{9,8},{10,11... | collective-permute-start | bytes 3686408 | tf_op jit(solution)/shard_map/ppermute | solution.py:752
  224.1 36.7 %collective-permute-start.24 = (bf16[4,40,3840]{2,1,0:T(8,128)(2,1)}, bf16[4,40,3840]{2,1,0:T(8,128)(2,1)}, u32[]{:S(2)}, u32[]{:S(2)}) collective-permute-start(bf16[4,40,3840]{2,1,0:T(8,128)(2,1)} %collective-permute-done.16.refs_1_), channel_id=1, source_target_pairs={{0,1},{1,0},{2,3},{3,2},{4,5},{5,4},{6,7},{7,6},{8,9},{9,8},{10,11... | collective-permute-start | bytes 3686408 | tf_op jit(solution)/shard_map/ppermute | solution.py:752
  225.5 35.4 %collective-permute-start.25 = (bf16[4,40,3840]{2,1,0:T(8,128)(2,1)}, bf16[4,40,3840]{2,1,0:T(8,128)(2,1)}, u32[]{:S(2)}, u32[]{:S(2)}) collective-permute-start(bf16[4,40,3840]{2,1,0:T(8,128)(2,1)} %collective-permute-done.17.refs_2_), channel_id=1, source_target_pairs={{0,1},{1,0},{2,3},{3,2},{4,5},{5,4},{6,7},{7,6},{8,9},{9,8},{10,11... | collective-permute-start | bytes 3686408 | tf_op jit(solution)/shard_map/ppermute | solution.py:752
  271.5 27.2 %collective-permute-start.28 = (bf16[128,1280]{1,0:T(8,128)(2,1)}, bf16[128,1280]{1,0:T(8,128)(2,1)}, u32[]{:S(2)}, u32[]{:S(2)}) collective-permute-start(bf16[128,1280]{1,0:T(8,128)(2,1)} %dynamic-slice_bitcast_fusion.9), channel_id=1, source_target_pairs={{0,4},{4,0},{1,5},{5,1},{2,6},{6,2},{3,7},{7,3},{8,12},{12,8},{9,1... | collective-permute-start | bytes 983048 | tf_op jit(solution)/shard_map/ppermute | solution.py:752
  281.6 106.2 %reduce-scatter.5.cloned.1.call-start = ((), (), s32[]{:S(2)}) async-start(), calls=%async_computation.12 | async-start | bytes 3276800 | tf_op jit(solution)/shard_map/reduce_scatter | solution.py:802
  373.9 147.2 %reduce-scatter.7.cloned.1.call-start = ((), (), s32[]{:S(2)}) async-start(), calls=%async_computation.13 | async-start | bytes 1536000 | tf_op jit(solution)/shard_map/reduce_scatter | solution.py:802
  387.8 42.2 %collective-permute-start.34 = (bf16[2,2,4,40,3840]{4,3,2,1,0:T(8,128)(2,1)}, bf16[2,2,4,40,3840]{4,3,2,1,0:T(8,128)(2,1)}, u32[]{:S(2)}, u32[]{:S(2)}) collective-permute-start(bf16[2,2,4,40,3840]{4,3,2,1,0:T(8,128)(2,1)} %copy-done.69), channel_id=1, source_target_pairs={{0,1},{1,0},{2,3},{3,2},{4,5},{5,4},{6,7},{7,6},{8,9},{9,8},{10,11... | collective-permute-start | bytes 14745608 | tf_op jit(solution)/shard_map/ppermute | solution.py:752
  391.1 38.9 %collective-permute-start.36 = (bf16[4,40,3840]{2,1,0:T(8,128)(2,1)S(1)}, bf16[4,40,3840]{2,1,0:T(8,128)(2,1)S(1)}, u32[]{:S(2)}, u32[]{:S(2)}) collective-permute-start(bf16[4,40,3840]{2,1,0:T(8,128)(2,1)S(1)} %pad_maximum_fusion.1), channel_id=1, source_target_pairs={{0,2},{1,3},{2,0},{3,1},{4,6},{5,7},{6,4},{7,5},{8,10},{9,11},{10,... | collective-permute-start | bytes 3686408 | tf_op jit(solution)/shard_map/ppermute | solution.py:752
  393.3 36.7 %collective-permute-start.35 = (bf16[4,40,3840]{2,1,0:T(8,128)(2,1)S(1)}, bf16[4,40,3840]{2,1,0:T(8,128)(2,1)S(1)}, u32[]{:S(2)}, u32[]{:S(2)}) collective-permute-start(bf16[4,40,3840]{2,1,0:T(8,128)(2,1)S(1)} %pad_maximum_fusion), channel_id=1, source_target_pairs={{0,4},{4,0},{1,5},{5,1},{2,6},{6,2},{3,7},{7,3},{8,12},{12,8},{9,1... | collective-permute-start | bytes 3686408 | tf_op jit(solution)/shard_map/ppermute | solution.py:752
  394.8 34.4 %collective-permute-start.37 = (bf16[160,960]{1,0:T(8,128)(2,1)S(1)}, bf16[160,960]{1,0:T(8,128)(2,1)S(1)}, u32[]{:S(2)}, u32[]{:S(2)}) collective-permute-start(bf16[160,960]{1,0:T(8,128)(2,1)S(1)} %dynamic-slice_bitcast_fusion.8), channel_id=1, source_target_pairs={{0,4},{4,0},{1,5},{5,1},{2,6},{6,2},{3,7},{7,3},{8,12},{12,8},{9,1... | collective-permute-start | bytes 921608 | tf_op jit(solution)/shard_map/ppermute | solution.py:752
  440.2 107.1 %reduce-scatter.9.cloned.1.call-start = ((), (), s32[]{:S(2)}) async-start(), calls=%async_computation.14 | async-start | bytes 3276800 | tf_op jit(solution)/shard_map/reduce_scatter | solution.py:802
  476.6 44.6 %collective-permute-start.43 = (bf16[4,40,3840]{2,1,0:T(8,128)(2,1)}, bf16[4,40,3840]{2,1,0:T(8,128)(2,1)}, u32[]{:S(2)}, u32[]{:S(2)}) collective-permute-start(bf16[4,40,3840]{2,1,0:T(8,128)(2,1)} %pad_maximum_fusion.3), channel_id=1, source_target_pairs={{0,2},{1,3},{2,0},{3,1},{4,6},{5,7},{6,4},{7,5},{8,10},{9,11},{10,... | collective-permute-start | bytes 3686408 | tf_op jit(solution)/shard_map/ppermute | solution.py:752
  479.6 41.6 %collective-permute-start.42 = (bf16[4,40,3840]{2,1,0:T(8,128)(2,1)}, bf16[4,40,3840]{2,1,0:T(8,128)(2,1)}, u32[]{:S(2)}, u32[]{:S(2)}) collective-permute-start(bf16[4,40,3840]{2,1,0:T(8,128)(2,1)} %pad_maximum_fusion.2), channel_id=1, source_target_pairs={{0,4},{4,0},{1,5},{5,1},{2,6},{6,2},{3,7},{7,3},{8,12},{12,8},{9,1... | collective-permute-start | bytes 3686408 | tf_op jit(solution)/shard_map/ppermute | solution.py:752
  481.2 38.5 %collective-permute-start.41 = (bf16[2,128,1280]{2,1,0:T(8,128)(2,1)S(1)}, bf16[2,128,1280]{2,1,0:T(8,128)(2,1)S(1)}, u32[]{:S(2)}, u32[]{:S(2)}) collective-permute-start(bf16[2,128,1280]{2,1,0:T(8,128)(2,1)S(1)} %fusion.81), channel_id=1, source_target_pairs={{0,2},{1,3},{2,0},{3,1},{4,6},{5,7},{6,4},{7,5},{8,10},{9,11},{10,... | collective-permute-start | bytes 1966088 | tf_op jit(solution)/shard_map/ppermute | solution.py:752
  484.2 44.9 %collective-permute-start.47 = (f32[2,80]{1,0:T(2,128)S(1)}, f32[2,80]{1,0:T(2,128)S(1)}, u32[]{:S(2)}, u32[]{:S(2)}) collective-permute-start(f32[2,80]{1,0:T(2,128)S(1)} %fusion.93), channel_id=1, source_target_pairs={{0,2},{1,3},{2,0},{3,1},{4,6},{5,7},{6,4},{7,5},{8,10},{9,11},{10,... | collective-permute-start | bytes 1928 | tf_op jit(solution)/shard_map/ppermute | solution.py:752
  484.8 59.2 %all-to-all-start.7 = ((bf16[4,40,960]{2,1,0:T(8,128)(2,1)}), bf16[4,40,960]{2,1,0:T(8,128)(2,1)}, u32[]{:S(2)}, u32[]{:S(2)}) async-start(bf16[4,40,960]{2,1,0:T(8,128)(2,1)} %bitcast.83), calls=%async_computation.10 | async-start | bytes 655360 | tf_op jit(solution)/shard_map/all_to_all | solution.py:773
  488.9 67.2 %reduce-scatter.11.cloned.1.call-start = ((), (), s32[]{:S(2)}) async-start(), calls=%async_computation.15 | async-start | bytes 1536000 | tf_op jit(solution)/shard_map/reduce_scatter | solution.py:802
  (158 other events, 1226.2 us)
Sparse Core Ops, SparseCore 0:
  15.4 32.9 all-gather.8
  50.6 31.7 all-gather.10
  84.0 31.6 all-gather.12
  117.7 30.2 all-gather.14
  327.4 52.3 reduce-scatter.4
  440.3 29.5 reduce-scatter.6
  472.4 50.8 reduce-scatter.8
  526.3 29.8 reduce-scatter.10

commit v11 on v10

--- a/solution.py
+++ b/solution.py
@@ -363,6 +363,10 @@
 LIGHT = pl.CostEstimate(flops=1 << 20, bytes_accessed=1 << 20, transcendentals=0)
 
 
+def in_hbm(*arrays):
+    return [pltpu.with_memory_space_constraint(array, pltpu.HBM) for array in arrays]
+
+
 def allowed_keys(col, row, first):
     count = first + row.shape[1]
     key_place = lax.broadcasted_iota(jnp.int32, (count, row.shape[1]), 0)
@@ -420,13 +424,13 @@
             pl.BlockSpec((1, 1, length), lambda h: (h, 0, 0)),
         ],
         out_shape=[
-            jax.ShapeDtypeStruct((owners, local_heads, head_dim, tokens), BF16),
-            jax.ShapeDtypeStruct((local_heads, 1, length), F32),
+            pltpu.HBM((owners, local_heads, head_dim, tokens), BF16),
+            pltpu.HBM((local_heads, 1, length), F32),
         ],
         compiler_params=KERNEL,
         cost_estimate=LIGHT,
     )(
-        projected.reshape(3, local_heads, head_dim, length),
+        *in_hbm(projected.reshape(3, local_heads, head_dim, length)),
         scale_vec.reshape(head_dim, 1),
         segments.reshape(length, 1),
         segments.reshape(1, length),
@@ -515,8 +519,8 @@
             pl.BlockSpec((head_dim, lanes), lambda h: (0, 0)),
         ],
         out_shape=[
-            jax.ShapeDtypeStruct((3, local_heads, head_dim, length), BF16),
-            jax.ShapeDtypeStruct((head_dim, lanes), F32),
+            pltpu.HBM((3, local_heads, head_dim, length), BF16),
+            pltpu.HBM((head_dim, lanes), F32),
         ],
         scratch_shapes=[
             pltpu.VMEM((head_dim, length), F32),
@@ -525,8 +529,10 @@
         compiler_params=KERNEL,
         cost_estimate=LIGHT,
     )(
-        projected.reshape(3, local_heads, head_dim, length),
-        attended_grad.reshape(owners, local_heads, head_dim, tokens),
+        *in_hbm(
+            projected.reshape(3, local_heads, head_dim, length),
+            attended_grad.reshape(owners, local_heads, head_dim, tokens),
+        ),
         log_total,
         scale_vec.reshape(head_dim, 1),
         segments.reshape(length, 1),
@@ -567,7 +573,7 @@
     own = width // 32
     whole = pl.BlockSpec((tokens, width), lambda i, core: (0, 0))
     rows = pl.BlockSpec((1, 2, 1, own, 3 * width), lambda i, core: (i % 2, 0, i // 2, 0, 0))
-    shape = jax.ShapeDtypeStruct((2, 2, 4, own, 3 * width), BF16)
+    shape = pltpu.HBM((2, 2, 4, own, 3 * width), BF16)
     return pl.pallas_call(
         dense_grad_kernel,
         grid_spec=pltpu.PrefetchScalarGridSpec(
@@ -580,7 +586,7 @@
         out_shape=[shape, shape],
         compiler_params=KERNEL,
         cost_estimate=LIGHT,
-    )(place(), attended_t, normed, active, out_bar, up_bar, down_bar)
+    )(place(), *in_hbm(attended_t, normed, active, out_bar, up_bar, down_bar))
 
 
 def place():
@@ -616,10 +622,10 @@
             in_specs=specs,
             out_specs=pl.BlockSpec((1, 2, 2, 2, own, columns), lambda i, at: (i, 0, 0, 0, 0, 0)),
         ),
-        out_shape=jax.ShapeDtypeStruct((batch, 2, 2, 2, own, columns), BF16),
+        out_shape=pltpu.HBM((batch, 2, 2, 2, own, columns), BF16),
         compiler_params=KERNEL,
         cost_estimate=LIGHT,
-    )(place(), *pieces)
+    )(place(), *in_hbm(*pieces))
     return whole.reshape(-1, columns)
 
 
@@ -647,10 +653,10 @@
             in_specs=[rows, rows],
             out_specs=[pl.BlockSpec((1,) + s[1:], lambda i, at: (i, 0, 0, 0)) for s in shapes],
         ),
-        out_shape=[jax.ShapeDtypeStruct(s, BF16) for s in shapes],
+        out_shape=[pltpu.HBM(s, BF16) for s in shapes],
         compiler_params=KERNEL,
         cost_estimate=LIGHT,
-    )(place(), along, across)
+    )(place(), *in_hbm(along, across))
     return [part.reshape(-1, part.shape[-1]) for part in parts]
 
 
@@ -690,12 +696,12 @@
             ],
         ),
         out_shape=[
-            jax.ShapeDtypeStruct((length, width), BF16),
-            jax.ShapeDtypeStruct((columns, length), F32),
+            pltpu.HBM((length, width), BF16),
+            pltpu.HBM((columns, length), F32),
         ],
         compiler_params=KERNEL,
         cost_estimate=LIGHT,
-    )(place(), *pieces, gain.reshape(1, width), weight)
+    )(place(), *in_hbm(*pieces), gain.reshape(1, width), *in_hbm(weight))
 
 
 def project_back_kernel(
@@ -734,13 +740,13 @@
             scratch_shapes=[pltpu.VMEM((length, columns), BF16)],
         ),
         out_shape=[
-            jax.ShapeDtypeStruct((2, 2, token_rows, width), F32),
-            jax.ShapeDtypeStruct((2, 2, token_rows, width), BF16),
-            jax.ShapeDtypeStruct((width, columns), BF16),
+            pltpu.HBM((2, 2, token_rows, width), F32),
+            pltpu.HBM((2, 2, token_rows, width), BF16),
+            pltpu.HBM((width, columns), BF16),
         ],
         compiler_params=KERNEL,
         cost_estimate=LIGHT,
-    )(place(), bars, weight, normed)
+    )(place(), *in_hbm(bars, weight, normed))
 
 
 def tied(*arrays):
@@ -814,14 +820,14 @@
     return moved.reshape(4, rows, 3, -1).transpose(1, 2, 0, 3).reshape(rows, -1).astype(F32)
 
 
-def diagonal_sent(cored):
+def diagonal_rows(cored):
     blk, row = place()[:2]
     rows = pick(pick(cored, 1 - blk), 1 - row)
     half = rows.shape[-1] // 2
-    return swapped(rows[..., :half], "blk", 1), swapped(rows[..., half:], "head", 2)
-
-
-def neighbours_sent(cored, one, two):
+    return rows[..., :half], rows[..., half:]
+
+
+def neighbour_rows(cored, one, two):
     blk, row = place()[:2]
     half = one.shape[-1]
     across = pick(pick(cored, 1 - blk), row)
@@ -832,6 +838,10 @@
     beside = jnp.concatenate(
         [beside[..., :half].astype(F32) + one.astype(F32), beside[..., half:]], axis=-1
     ).astype(BF16)
+    return across, beside
+
+
+def sent_beside_and_across(across, beside):
     return swapped(across, "blk", 1), swapped(beside, "head", 2)
 
 
@@ -898,7 +908,7 @@
     qkv_across, one, beside, next_along, dense_next = tied(
         qkv_across, one, beside, next_along, dense_own[1]
     )
-    two = to_across(beside)
+    two, next_along = tied(to_across(beside), next_along)
     next_across = swapped(next_along, "blk", 1)
     pieces = [(dense_near, across, beside, one, two)]
     dense_next = along_batch(dense_next)
@@ -910,7 +920,7 @@
     for layer in range(layers):
         normed, factor_one = normalize(stream, gains[layer])
         if layer == 1:
-            normed, across, beside = tied(normed.astype(BF16), across, beside)
+            normed, beside = tied(normed.astype(BF16), beside)
             far, near = swapped(normed, "head", 2), other_core(normed)
             far, near, across, beside = tied(far, near, across, beside)
             token_pieces = (normed, near, far, other_core(far))
@@ -927,9 +937,14 @@
         pieces[layer] = pieces[layer][:3] + (one, two)
         swaps = tuple(other_core(piece) for piece in pieces[layer])
         if layer == 0:
-            attended, next_across, dense_next = tied(attended, next_across, dense_next)
-            across, beside = swapped(dense_next, "blk", 1), swapped(dense_next, "head", 2)
-        attended_t, swaps = tied(over_head(attended), swaps)
+            attended, dense_next = tied(attended, dense_next)
+            beside = swapped(dense_next, "head", 2)
+            attended_t, swaps, next_across, dense_next = tied(
+                over_head(attended), swaps, next_across, dense_next
+            )
+            across = swapped(dense_next, "blk", 1)
+        else:
+            attended_t, swaps = tied(over_head(attended), swaps)
         attended_t = attended_t.reshape(width, -1)
         denses.append(assemble(pieces[layer] + swaps))
         dense = denses[layer]
@@ -967,7 +982,8 @@
         out_bar = middle_grad.astype(BF16)
         if layer == 0:
             out_bar, diagonal = tied(out_bar, diagonal)
-            sent = neighbours_sent(cored, *diagonal)
+            out_bar, rows = tied(out_bar, neighbour_rows(cored, *diagonal))
+            sent = sent_beside_and_across(*rows)
         attended_grad = over_head(dot_cols(out_w, out_bar).astype(BF16).reshape(4, -1, out_bar.shape[0]))
         grads, others = dense_grads(attended_t, normed_two, active, out_bar, up_bar, down_bar)
         if layer == 0:
@@ -980,29 +996,30 @@
             projected, attended_grad, log_total, scale_vecs[layer], segments, token_rows
         )
         if layer == 0:
-            bars, others, sent, z_across = tied(bars, others, sent, z_across)
+            bars, others, sent = tied(bars, others, sent)
             summed = own_sum(cored, *sent)
         else:
             bars, others = tied(bars, others)
         cored = (grads.astype(F32) + others.astype(F32)).astype(BF16)
         if layer == 0:
-            bars, cored, summed = tied(bars, cored, summed)
-            diagonal = diagonal_sent(cored)
+            bars, summed, rows = tied(bars, summed, diagonal_rows(cored))
+            diagonal = sent_beside_and_across(*rows)
             summed = over_batch(summed)
         halves, to_core, qkv_grad = project_back(bars, qkv, normed_all, token_rows)
         halves = halves + other_core(to_core).astype(F32)
         z_sum = over_batch(qkv_grad.reshape(4, 2, -1, qkv_grad.shape[-1]))
         if layer == 0:
             halves, diagonal = tied(halves, diagonal)
-            sent = neighbours_sent(cored, *diagonal)
+            halves, rows = tied(halves, neighbour_rows(cored, *diagonal))
+            sent = sent_beside_and_across(*rows)
             normed_grad = scatter_row(halves)
-            normed_grad, sent, summed = tied(normed_grad, sent, summed)
+            normed_grad, sent, summed, z_across = tied(normed_grad, sent, summed, z_across)
             dense_grad = [over_batch(own_sum(cored, *sent)), summed]
             qkv_grads = [columns_to_rows(across_sum(z_sum)), columns_to_rows(z_across)]
         else:
             normed_grad = scatter_row(halves)
             normed_grad, cored = tied(normed_grad, cored)
-            diagonal = diagonal_sent(cored)
+            diagonal = sent_beside_and_across(*diagonal_rows(cored))
         upper = middle_grad + lower_of(normed_grad, stream, factor_one, gains[layer])
     input_grad = swap_halves(upper.astype(BF16).reshape(tokens.shape)).astype(F32)
     scale_total = sum_all(jnp.stack(scale_grads))

time: 587 us -> 583 us (level)
  local copies, waits for them, and re-layouts: 79.5 us -> 34.1 us
  Pallas kernels: 95.9 us -> 132 us
  waiting for transfers between devices: 215 us -> 223 us
    unnamed x248 -> x152, local copies, waits for them, and re-layouts: 52.9 us -> 11.3 us
    ppermute x51, waiting for transfers between devices: 183 us -> 193 us  [swapped(): return lax.ppermute(array, axis, [(i, i ^ mask) for i in range(size)])]
    pallas_call x2, Pallas kernels: 13.1 us -> 20.1 us  [dense_grads(): pl.pallas_call(dense_grad_kernel, grid_spec=pltpu.PrefetchScalarGridSpec(...]
    pallas_call x2, Pallas kernels: 9.79 us -> 16.6 us  [project(): pl.pallas_call(functools.partial(project_kernel, with_norm), grid_spec=pl...]
    pallas_call x2, Pallas kernels: 9.87 us -> 16.5 us  [assemble(): pl.pallas_call(assemble_kernel, grid_spec=pltpu.PrefetchScalarGridSpec(nu...]
    reduce_scatter x4, waiting for transfers between devices: 6.24 us -> 0.06 us  [over_batch(): lax.psum_scatter(parts.astype(BF16), 'batch', scatter_dimension=0, tiled=...]
  transfers between devices with their start and end apart: 66 -> 66, of which waited for: 29 -> 29; matrix products, arithmetic and copies ran while one was open for 13% -> 12% of each run, Pallas kernels for 14% -> 19%
where the time goes in v11:
time: 583 us; the launch traced here: 575 us
  waiting for transfers between devices  223 us (38%)
  Pallas kernels  132 us (23%)
  starting transfers between devices  70.2 us (12%)
  other arithmetic  48.7 us (8%)
  local copies, waits for them, and re-layouts  34.1 us (6%)
  blocking collectives  28 us (5%)
  matrix products  22.7 us (4%)
  between operations  16.1 us (3%)
    ppermute x51, waiting for transfers between devices, swapped(): return lax.ppermute(array, axis, [(i, i ^ mask) for i in range(size)])  193 us
    ppermute x51, starting transfers between devices, swapped(): return lax.ppermute(array, axis, [(i, i ^ mask) for i in range(size)])  43 us
    all_to_all x1, blocking collectives, over_head(): lax.all_to_all(parts, 'head', split_axis=0, concat_axis=0, tiled=True)  28 us
    all_to_all x7, starting transfers between devices, over_head(): lax.all_to_all(parts, 'head', split_axis=0, concat_axis=0, tiled=True)  26.7 us
    pallas_call x2, Pallas kernels, attend_back_rows(): pl.pallas_call(functools.partial(attend_back_kernel, token_rows), grid=(l...  24.7 us
    pallas_call x2, Pallas kernels, project_back(): pl.pallas_call(project_back_kernel, grid_spec=pltpu.PrefetchScalarGridSpe...  23.6 us
    all_to_all x7, waiting for transfers between devices, over_head(): lax.all_to_all(parts, 'head', split_axis=0, concat_axis=0, tiled=True)  23.5 us
    pallas_call x2, Pallas kernels, attend_rows(): pl.pallas_call(functools.partial(attend_kernel, token_rows), grid=(local_...  21.2 us
  transfers between devices with their start and end apart: 66, of which 29 were waited for; matrix products, arithmetic and copies ran while one was open for 12% of the time, Pallas kernels for 19%

profile of v11, /device:TPU:0, one launch (start us, length us, event | category | flops | bytes accessed | tf_op | source)
XLA Modules:
  0.0 574.7 jit_solution(15071357545968843180)
XLA Ops:
  22.0 5.1 collective-permute-done
  31.0 14.1 %collective-permute-done.3.refs_2_ = bf16[256,1280]{1,0:T(8,128)(2,1)S(1)} collective-permute-done((bf16[256,1280]{1,0:T(8,128)(2,1)S(1)}, bf16[256,1280]{1,0:T(8,128)(2,1)S(1)}, u32[]{:S(2)}, u32[]{:S(2)}) %collective-permute-start.3) | collective-permute-done | bytes 655392 | tf_op jit(solution)/shard_map/ppermute | solution.py:758
  52.6 28.0 %all_to_all.40 = bf16[4,40,960]{2,1,0:T(8,128)(2,1)} all-to-all(bf16[4,40,960]{2,1,0:T(8,128)(2,1)S(1)} %reshape.239), channel_id=1, replica_groups=mesh['batch'=4,'blk'=2,'head'=4] {'head'}, dimensions={0} | all-to-all | bytes 614400 | tf_op jit(solution)/shard_map/all_to_all | solution.py:779
  87.5 12.5 %collective-permute-done.8.refs_3_ = bf16[4,40,1920]{2,1,0:T(8,128)(2,1)} collective-permute-done((bf16[4,40,1920]{2,1,0:T(8,128)(2,1)S(1)}, bf16[4,40,1920]{2,1,0:T(8,128)(2,1)}, u32[]{:S(2)}, u32[]{:S(2)}) %collective-permute-start.8) | collective-permute-done | bytes 614432 | tf_op jit(solution)/shard_map/ppermute | solution.py:758
  100.0 12.7 %collective-permute-done.7.across_ref = bf16[4,160,964]{2,1,0:T(8,128)(2,1)} collective-permute-done((bf16[4,160,964]{2,1,0:T(8,128)(2,1)}, bf16[4,160,964]{2,1,0:T(8,128)(2,1)}, u32[]{:S(2)}, u32[]{:S(2)}) %collective-permute-start.7) | collective-permute-done | bytes 1233952 | tf_op jit(solution)/shard_map/ppermute | solution.py:758
  118.6 4.6 shard_map.169
  123.2 7.7 %collective-permute-done.9.refs_4_ = bf16[4,40,1920]{2,1,0:T(8,128)(2,1)} collective-permute-done((bf16[4,40,1920]{2,1,0:T(8,128)(2,1)S(1)}, bf16[4,40,1920]{2,1,0:T(8,128)(2,1)}, u32[]{:S(2)}, u32[]{:S(2)}) %collective-permute-start.9) | collective-permute-done | bytes 614432 | tf_op jit(solution)/shard_map/ppermute | solution.py:758
  133.7 8.9 %shard_map.170 = (bf16[1024,1280]{1,0:T(8,128)(2,1)}, f32[960,1024]{1,0:T(8,128)}) custom-call(s32[3]{0:T(128)S(1)} %pad_add_fusion.place_ref.core_ref, bf16[256,1280]{1,0:T(8,128)(2,1)} %bitcast.190, bf16[256,1280]{1,0:T(8,128)(2,1)} %copy-done.52, bf16[256,1280]{1,0:T(8,128)(2,1)} %copy-done.51, bf16[256,1280]{1,0:T(8,128)(2,1)} %collective-permute-done.4.refs_3_, ...), custom_call_target="tpu_custom_call" | custom-call | flops 1048576 | bytes 1048576 | tf_op jit(solution)/shard_map/pallas_call | solution.py:683
  142.6 10.6 %shard_map.171 = (bf16[4,4,80,256]{3,2,1,0:T(8,128)(2,1)}, f32[4,1,1024]{2,1,0:T(1,128)}) custom-call(f32[3,4,80,1024]{3,2,1,0:T(8,128)} %bitcast.174, f32[80,1]{1,0:T(8,128)S(1)} %copy.41.scale_ref, s32[1024,1]{1,0:T(8,128)S(1)} %copy.42.col_ref, s32[1,1024]{1,0:T(1,128)S(1)} %constant_dynamic-slice_fusion.row_ref), custom_call_target="tpu_custom_call" | custom-call | flops 1048576 | bytes 1048576 | tf_op jit(solution)/shard_map/pallas_call | solution.py:413
  160.2 8.2 %all-to-all-done.2 = bf16[4,320,256]{2,1,0:T(8,128)(2,1)S(1)} async-done(((bf16[4,320,256]{2,1,0:T(8,128)(2,1)}), bf16[4,320,256]{2,1,0:T(8,128)(2,1)S(1)}, u32[]{:S(2)}, u32[]{:S(2)}) %all-to-all-start.2) | async-done | bytes 655392 | tf_op jit(solution)/shard_map/all_to_all | solution.py:779
  169.0 8.3 %shard_map.172 = bf16[4,2,2,2,40,3840]{5,4,3,2,1,0:T(8,128)(2,1)} custom-call(s32[3]{0:T(128)S(1)} %pad_add_fusion.place_ref.core_ref, bf16[4,40,3840]{2,1,0:T(8,128)(2,1)} %bitcast.19.refs_0_, bf16[4,40,3840]{2,1,0:T(8,128)(2,1)} %collective-permute-done.5.refs_1_, bf16[4,40,3840]{2,1,0:T(8,128)(2,1)} %copy-done.21, ...), custom_call_target="tpu_custom_call" | custom-call | flops 1048576 | bytes 1048576 | tf_op jit(solution)/shard_map/pallas_call | solution.py:617
  186.0 8.4 %collective-permute-done.16.refs_2_ = bf16[4,40,3840]{2,1,0:T(8,128)(2,1)} collective-permute-done((bf16[4,40,3840]{2,1,0:T(8,128)(2,1)}, bf16[4,40,3840]{2,1,0:T(8,128)(2,1)}, u32[]{:S(2)}, u32[]{:S(2)}) %collective-permute-start.16) | collective-permute-done | bytes 1228832 | tf_op jit(solution)/shard_map/ppermute | solution.py:758
  196.8 14.7 %collective-permute-done.17.refs_2_ = bf16[256,1280]{1,0:T(8,128)(2,1)S(1)} collective-permute-done((bf16[256,1280]{1,0:T(8,128)(2,1)S(1)}, bf16[256,1280]{1,0:T(8,128)(2,1)S(1)}, u32[]{:S(2)}, u32[]{:S(2)}) %collective-permute-start.17) | collective-permute-done | bytes 655392 | tf_op jit(solution)/shard_map/ppermute | solution.py:758
  218.1 4.5 shard_map.173
  222.7 7.8 %shard_map.174 = (bf16[1024,1280]{1,0:T(8,128)(2,1)}, f32[960,1024]{1,0:T(8,128)}) custom-call(s32[3]{0:T(128)S(1)} %pad_add_fusion.place_ref.core_ref, bf16[256,1280]{1,0:T(8,128)(2,1)} %copy-done.30, bf16[256,1280]{1,0:T(8,128)(2,1)} %copy-done.53, bf16[256,1280]{1,0:T(8,128)(2,1)} %copy-done.54, bf16[256,1280]{1,0:T(8,128)(2,1)} %copy-done.55, ...), custom_call_target="tpu_custom_call" | custom-call | flops 1048576 | bytes 1048576 | tf_op jit(solution)/shard_map/pallas_call | solution.py:683
  230.4 10.6 %shard_map.175 = (bf16[4,4,80,256]{3,2,1,0:T(8,128)(2,1)}, f32[4,1,1024]{2,1,0:T(1,128)}) custom-call(f32[3,4,80,1024]{3,2,1,0:T(8,128)} %bitcast.176, f32[80,1]{1,0:T(8,128)S(1)} %copy.43.scale_ref, s32[1024,1]{1,0:T(8,128)S(1)} %copy.42.col_ref, s32[1,1024]{1,0:T(1,128)S(1)} %constant_dynamic-slice_fusion.row_ref), custom_call_target="tpu_custom_call" | custom-call | flops 1048576 | bytes 1048576 | tf_op jit(solution)/shard_map/pallas_call | solution.py:413
  245.3 10.2 %all-to-all-done.3 = bf16[4,320,256]{2,1,0:T(8,128)(2,1)S(1)} async-done(((bf16[4,320,256]{2,1,0:T(8,128)(2,1)}), bf16[4,320,256]{2,1,0:T(8,128)(2,1)S(1)}, u32[]{:S(2)}, u32[]{:S(2)}) %all-to-all-start.3) | async-done | bytes 655392 | tf_op jit(solution)/shard_map/all_to_all | solution.py:779
  256.3 8.3 %shard_map.176 = bf16[4,2,2,2,40,3840]{5,4,3,2,1,0:T(8,128)(2,1)} custom-call(s32[3]{0:T(128)S(1)} %pad_add_fusion.place_ref.core_ref, bf16[4,40,3840]{2,1,0:T(8,128)(2,1)} %bitcast.34.refs_0_, bf16[4,40,3840]{2,1,0:T(8,128)(2,1)} %collective-permute-done.19.refs_1_, bf16[4,40,3840]{2,1,0:T(8,128)(2,1)} %collective-permute-done.16.refs_2_, ...), custom_call_target="tpu_custom_call" | custom-call | flops 1048576 | bytes 1048576 | tf_op jit(solution)/shard_map/pallas_call | solution.py:617
  285.5 9.9 %shard_map.177 = (bf16[2,2,4,40,3840]{4,3,2,1,0:T(8,128)(2,1)}, bf16[2,2,4,40,3840]{4,3,2,1,0:T(8,128)(2,1)}) custom-call(s32[3]{0:T(128)S(1)} %pad_add_fusion.place_ref.core_ref, bf16[1280,256]{1,0:T(8,128)(2,1)} %bitcast.217, bf16[256,1280]{1,0:T(8,128)(2,1)} %copy-done.26, bf16[256,1280]{1,0:T(8,128)(2,1)} %copy-done.49, bf16[256,1280]{1,0:T(8,128)(2,1)} %copy-done.27, ...), custom_call_target="tpu_custom_call" | custom-call | flops 1048576 | bytes 1048576 | tf_op jit(solution)/shard_map/pallas_call | solution.py:577
  297.8 12.3 %shard_map.178 = (bf16[3,4,80,1024]{3,2,1,0:T(8,128)(2,1)}, f32[80,128]{1,0:T(8,128)}) custom-call(f32[3,4,80,1024]{3,2,1,0:T(8,128)} %bitcast.177, bf16[4,4,80,256]{3,2,1,0:T(8,128)(2,1)} %bitcast.50.grad_ref, f32[4,1,1024]{2,1,0:T(1,128)S(1)} %copy-done.3, f32[80,1]{1,0:T(8,128)S(1)} %copy.43.scale_ref, s32[1024,1]{1,0:T(8,128)S(1)} %copy.42.col_ref, ...), custom_call_target="tpu_custom_call" | custom-call | flops 1048576 | bytes 1048576 | tf_op jit(solution)/shard_map/pallas_call | solution.py:506
  310.1 12.5 %shard_map.179 = (f32[2,2,128,1280]{3,2,1,0:T(8,128)}, bf16[2,2,128,1280]{3,2,1,0:T(8,128)(2,1)}, bf16[1280,960]{1,0:T(8,128)(2,1)}) custom-call(s32[3]{0:T(128)S(1)} %pad_add_fusion.place_ref.core_ref, bf16[960,1024]{1,0:T(8,128)(2,1)} %bitcast.220, bf16[1280,960]{1,0:T(8,128)(2,1)} %bitcast.173, bf16[1024,1280]{1,0:T(8,128)(2,1)} %get-tuple-element.175.normed_ref), custom_call_target="tpu_custom_call" | custom-call | flops 1048576 | bytes 1048576 | tf_op jit(solution)/shard_map/pallas_call | solution.py:729
  334.3 11.5 %collective-permute-done.31 = bf16[2,128,1280]{2,1,0:T(8,128)(2,1)} collective-permute-done((bf16[2,128,1280]{2,1,0:T(8,128)(2,1)S(1)}, bf16[2,128,1280]{2,1,0:T(8,128)(2,1)}, u32[]{:S(2)}, u32[]{:S(2)}) %collective-permute-start.31) | collective-permute-done | bytes 655392 | tf_op jit(solution)/shard_map/ppermute | solution.py:758
  356.2 9.2 %collective-permute-done.33 = bf16[4,40,1920]{2,1,0:T(8,128)(2,1)S(1)} collective-permute-done((bf16[4,40,1920]{2,1,0:T(8,128)(2,1)S(1)}, bf16[4,40,1920]{2,1,0:T(8,128)(2,1)S(1)}, u32[]{:S(2)}, u32[]{:S(2)}) %collective-permute-start.33) | collective-permute-done | bytes 614432 | tf_op jit(solution)/shard_map/ppermute | solution.py:758
  374.9 10.2 %shard_map.180 = (bf16[2,2,4,40,3840]{4,3,2,1,0:T(8,128)(2,1)}, bf16[2,2,4,40,3840]{4,3,2,1,0:T(8,128)(2,1)}) custom-call(s32[3]{0:T(128)S(1)} %pad_add_fusion.place_ref.core_ref, bf16[1280,256]{1,0:T(8,128)(2,1)} %bitcast.215, bf16[256,1280]{1,0:T(8,128)(2,1)} %copy-done.23, bf16[256,1280]{1,0:T(8,128)(2,1)} %copy-done.45, bf16[256,1280]{1,0:T(8,128)(2,1)} %copy-done.32, ...), custom_call_target="tpu_custom_call" | custom-call | flops 1048576 | bytes 1048576 | tf_op jit(solution)/shard_map/pallas_call | solution.py:577
  387.7 12.4 %shard_map.181 = (bf16[3,4,80,1024]{3,2,1,0:T(8,128)(2,1)}, f32[80,128]{1,0:T(8,128)}) custom-call(f32[3,4,80,1024]{3,2,1,0:T(8,128)} %bitcast.175, bf16[4,4,80,256]{3,2,1,0:T(8,128)(2,1)} %bitcast.218, f32[4,1,1024]{2,1,0:T(1,128)S(1)} %copy-done.2, f32[80,1]{1,0:T(8,128)S(1)} %copy.41.scale_ref, s32[1024,1]{1,0:T(8,128)S(1)} %copy.42.col_ref, ...), custom_call_target="tpu_custom_call" | custom-call | flops 1048576 | bytes 1048576 | tf_op jit(solution)/shard_map/pallas_call | solution.py:506
  400.1 14.7 %collective-permute-done.35 = bf16[4,40,3840]{2,1,0:T(8,128)(2,1)S(1)} collective-permute-done((bf16[4,40,3840]{2,1,0:T(8,128)(2,1)}, bf16[4,40,3840]{2,1,0:T(8,128)(2,1)S(1)}, u32[]{:S(2)}, u32[]{:S(2)}) %collective-permute-start.35) | collective-permute-done | bytes 1228832 | tf_op jit(solution)/shard_map/ppermute | solution.py:758
  425.7 11.1 %shard_map.182 = (f32[2,2,128,1280]{3,2,1,0:T(8,128)}, bf16[2,2,128,1280]{3,2,1,0:T(8,128)(2,1)}, bf16[1280,960]{1,0:T(8,128)(2,1)}) custom-call(s32[3]{0:T(128)S(1)} %pad_add_fusion.place_ref.core_ref, bf16[960,1024]{1,0:T(8,128)(2,1)} %bitcast.219, bf16[1280,960]{1,0:T(8,128)(2,1)} %bitcast.187, bf16[1024,1280]{1,0:T(8,128)(2,1)} %get-tuple-element.200.normed_ref), custom_call_target="tpu_custom_call" | custom-call | flops 1048576 | bytes 1048576 | tf_op jit(solution)/shard_map/pallas_call | solution.py:729
  445.8 15.4 %collective-permute-done.38 = bf16[4,40,1920]{2,1,0:T(8,128)(2,1)S(1)} collective-permute-done((bf16[4,40,1920]{2,1,0:T(8,128)(2,1)}, bf16[4,40,1920]{2,1,0:T(8,128)(2,1)S(1)}, u32[]{:S(2)}, u32[]{:S(2)}) %collective-permute-start.38) | collective-permute-done | bytes 614432 | tf_op jit(solution)/shard_map/ppermute | solution.py:758
  475.6 35.5 %collective-permute-done.40 = bf16[2,128,1280]{2,1,0:T(8,128)(2,1)S(1)} collective-permute-done((bf16[2,128,1280]{2,1,0:T(8,128)(2,1)S(1)}, bf16[2,128,1280]{2,1,0:T(8,128)(2,1)S(1)}, u32[]{:S(2)}, u32[]{:S(2)}) %collective-permute-start.40) | collective-permute-done | bytes 655392 | tf_op jit(solution)/shard_map/ppermute | solution.py:758
  524.3 8.0 %collective-permute-done.48 = f32[2,80]{1,0:T(2,128)S(1)} collective-permute-done((f32[2,80]{1,0:T(2,128)S(1)}, f32[2,80]{1,0:T(2,128)S(1)}, u32[]{:S(2)}, u32[]{:S(2)}) %collective-permute-start.48) | collective-permute-done | bytes 672 | tf_op jit(solution)/shard_map/ppermute | solution.py:758
  547.8 5.9 %collective-permute-done.45 = bf16[160,960]{1,0:T(8,128)(2,1)S(1)} collective-permute-done((bf16[160,960]{1,0:T(8,128)(2,1)S(1)}, bf16[160,960]{1,0:T(8,128)(2,1)S(1)}, u32[]{:S(2)}, u32[]{:S(2)}) %collective-permute-start.45) | collective-permute-done | bytes 307232 | tf_op jit(solution)/shard_map/ppermute | solution.py:758
  559.7 5.1 all-to-all-done.6
  (397 shorter events, 199.5 us)
Async XLA Ops:
  7.2 41.3 %all-gather.9.cloned.1.call-start = ((), (), s32[]{:S(2)}) async-start(), calls=%async_computation.16 | async-start | bytes 1536000 | tf_op jit(solution)/shard_map/all_gather | solution.py:792
  20.8 61.6 %all-gather.11.cloned.1.call-start = ((), (), s32[]{:S(2)}) async-start(), calls=%async_computation.17 | async-start | bytes 1638400 | tf_op jit(solution)/shard_map/all_gather | solution.py:792
  48.6 67.2 %all-gather.13.cloned.1.call-start = ((), (), s32[]{:S(2)}) async-start(), calls=%async_computation.18 | async-start | bytes 1638400 | tf_op jit(solution)/shard_map/all_gather | solution.py:792
  48.6 32.1 %collective-permute-start.6 = (bf16[4,40,3840]{2,1,0:T(8,128)(2,1)}, bf16[4,40,3840]{2,1,0:T(8,128)(2,1)S(1)}, u32[]{:S(2)}, u32[]{:S(2)}) collective-permute-start(bf16[4,40,3840]{2,1,0:T(8,128)(2,1)} %bitcast.19.refs_0_), channel_id=1, source_target_pairs={{0,2},{1,3},{2,0},{3,1},{4,6},{5,7},{6,4},{7,5},{8,10},{9,11},{10,... | collective-permute-start | bytes 3686408 | tf_op jit(solution)/shard_map/ppermute | solution.py:758
  50.2 30.5 %collective-permute-start.5 = (bf16[4,40,3840]{2,1,0:T(8,128)(2,1)}, bf16[4,40,3840]{2,1,0:T(8,128)(2,1)}, u32[]{:S(2)}, u32[]{:S(2)}) collective-permute-start(bf16[4,40,3840]{2,1,0:T(8,128)(2,1)} %bitcast.19.refs_0_), channel_id=1, source_target_pairs={{0,4},{4,0},{1,5},{5,1},{2,6},{6,2},{3,7},{7,3},{8,12},{12,8},{9,1... | collective-permute-start | bytes 3686408 | tf_op jit(solution)/shard_map/ppermute | solution.py:758
  82.5 71.2 %all-gather.15.cloned.1.call-start = ((), (), s32[]{:S(2)}) async-start(), calls=%async_computation.19 | async-start | bytes 1536000 | tf_op jit(solution)/shard_map/all_gather | solution.py:792
  82.5 30.2 %collective-permute-start.7 = (bf16[4,160,964]{2,1,0:T(8,128)(2,1)}, bf16[4,160,964]{2,1,0:T(8,128)(2,1)}, u32[]{:S(2)}, u32[]{:S(2)}) collective-permute-start(bf16[4,160,964]{2,1,0:T(8,128)(2,1)} %bitcast.228), channel_id=1, source_target_pairs={{0,4},{4,0},{1,5},{5,1},{2,6},{6,2},{3,7},{7,3},{8,12},{12,8},{9,1... | collective-permute-start | bytes 3701768 | tf_op jit(solution)/shard_map/ppermute | solution.py:758
  117.4 35.8 %collective-permute-start.10 = (bf16[4,40,3840]{2,1,0:T(8,128)(2,1)}, bf16[4,40,3840]{2,1,0:T(8,128)(2,1)}, u32[]{:S(2)}, u32[]{:S(2)}) collective-permute-start(bf16[4,40,3840]{2,1,0:T(8,128)(2,1)} %bitcast.19.refs_0_), channel_id=1, source_target_pairs={{0,1},{1,0},{2,3},{3,2},{4,5},{5,4},{6,7},{7,6},{8,9},{9,8},{10,11... | collective-permute-start | bytes 3686408 | tf_op jit(solution)/shard_map/ppermute | solution.py:758
  118.0 39.8 %collective-permute-start.11 = (bf16[4,40,3840]{2,1,0:T(8,128)(2,1)}, bf16[4,40,3840]{2,1,0:T(8,128)(2,1)}, u32[]{:S(2)}, u32[]{:S(2)}) collective-permute-start(bf16[4,40,3840]{2,1,0:T(8,128)(2,1)} %collective-permute-done.5.refs_1_), channel_id=1, source_target_pairs={{0,1},{1,0},{2,3},{3,2},{4,5},{5,4},{6,7},{7,6},{8,9},{9,8},{10,11... | collective-permute-start | bytes 3686408 | tf_op jit(solution)/shard_map/ppermute | solution.py:758
  118.5 41.3 %collective-permute-start.12 = (bf16[4,40,3840]{2,1,0:T(8,128)(2,1)S(1)}, bf16[4,40,3840]{2,1,0:T(8,128)(2,1)}, u32[]{:S(2)}, u32[]{:S(2)}) collective-permute-start(bf16[4,40,3840]{2,1,0:T(8,128)(2,1)S(1)} %collective-permute-done.6.refs_2_), channel_id=1, source_target_pairs={{0,1},{1,0},{2,3},{3,2},{4,5},{5,4},{6,7},{7,6},{8,9},{9,8},{10,11... | collective-permute-start | bytes 3686408 | tf_op jit(solution)/shard_map/ppermute | solution.py:758
  131.0 29.3 %collective-permute-start.15 = (bf16[4,160,960]{2,1,0:T(8,128)(2,1)}, bf16[4,160,960]{2,1,0:T(8,128)(2,1)}, u32[]{:S(2)}, u32[]{:S(2)}) collective-permute-start(bf16[4,160,960]{2,1,0:T(8,128)(2,1)} %bitcast.23.along_ref), channel_id=1, source_target_pairs={{0,4},{4,0},{1,5},{5,1},{2,6},{6,2},{3,7},{7,3},{8,12},{12,8},{9,1... | collective-permute-start | bytes 3686408 | tf_op jit(solution)/shard_map/ppermute | solution.py:758
  157.8 36.6 %collective-permute-start.16 = (bf16[4,40,3840]{2,1,0:T(8,128)(2,1)}, bf16[4,40,3840]{2,1,0:T(8,128)(2,1)}, u32[]{:S(2)}, u32[]{:S(2)}) collective-permute-start(bf16[4,40,3840]{2,1,0:T(8,128)(2,1)} %bitcast.34.refs_0_), channel_id=1, source_target_pairs={{0,2},{1,3},{2,0},{3,1},{4,6},{5,7},{6,4},{7,5},{8,10},{9,11},{10,... | collective-permute-start | bytes 3686408 | tf_op jit(solution)/shard_map/ppermute | solution.py:758
  168.4 28.4 %collective-permute-start.19 = (bf16[4,40,3840]{2,1,0:T(8,128)(2,1)}, bf16[4,40,3840]{2,1,0:T(8,128)(2,1)}, u32[]{:S(2)}, u32[]{:S(2)}) collective-permute-start(bf16[4,40,3840]{2,1,0:T(8,128)(2,1)} %bitcast.34.refs_0_), channel_id=1, source_target_pairs={{0,4},{4,0},{1,5},{5,1},{2,6},{6,2},{3,7},{7,3},{8,12},{12,8},{9,1... | collective-permute-start | bytes 3686408 | tf_op jit(solution)/shard_map/ppermute | solution.py:758
  215.7 25.3 %collective-permute-start.22 = (bf16[4,40,1920]{2,1,0:T(8,128)(2,1)}, bf16[4,40,1920]{2,1,0:T(8,128)(2,1)}, u32[]{:S(2)}, u32[]{:S(2)}) collective-permute-start(bf16[4,40,1920]{2,1,0:T(8,128)(2,1)} %slice.155), channel_id=1, source_target_pairs={{0,4},{4,0},{1,5},{5,1},{2,6},{6,2},{3,7},{7,3},{8,12},{12,8},{9,1... | collective-permute-start | bytes 1843208 | tf_op jit(solution)/shard_map/ppermute | solution.py:758
  216.3 24.7 %collective-permute-start.21 = (bf16[4,40,1920]{2,1,0:T(8,128)(2,1)}, bf16[4,40,1920]{2,1,0:T(8,128)(2,1)}, u32[]{:S(2)}, u32[]{:S(2)}) collective-permute-start(bf16[4,40,1920]{2,1,0:T(8,128)(2,1)} %slice.154), channel_id=1, source_target_pairs={{0,2},{1,3},{2,0},{3,1},{4,6},{5,7},{6,4},{7,5},{8,10},{9,11},{10,... | collective-permute-start | bytes 1843208 | tf_op jit(solution)/shard_map/ppermute | solution.py:758
  216.6 28.6 %collective-permute-start.23 = (bf16[4,40,3840]{2,1,0:T(8,128)(2,1)}, bf16[4,40,3840]{2,1,0:T(8,128)(2,1)}, u32[]{:S(2)}, u32[]{:S(2)}) collective-permute-start(bf16[4,40,3840]{2,1,0:T(8,128)(2,1)} %bitcast.34.refs_0_), channel_id=1, source_target_pairs={{0,1},{1,0},{2,3},{3,2},{4,5},{5,4},{6,7},{7,6},{8,9},{9,8},{10,11... | collective-permute-start | bytes 3686408 | tf_op jit(solution)/shard_map/ppermute | solution.py:758
  216.6 38.8 %collective-permute-start.24 = (bf16[4,40,3840]{2,1,0:T(8,128)(2,1)}, bf16[4,40,3840]{2,1,0:T(8,128)(2,1)}, u32[]{:S(2)}, u32[]{:S(2)}) collective-permute-start(bf16[4,40,3840]{2,1,0:T(8,128)(2,1)} %collective-permute-done.19.refs_1_), channel_id=1, source_target_pairs={{0,1},{1,0},{2,3},{3,2},{4,5},{5,4},{6,7},{7,6},{8,9},{9,8},{10,11... | collective-permute-start | bytes 3686408 | tf_op jit(solution)/shard_map/ppermute | solution.py:758
  217.2 38.3 %collective-permute-start.25 = (bf16[4,40,3840]{2,1,0:T(8,128)(2,1)}, bf16[4,40,3840]{2,1,0:T(8,128)(2,1)}, u32[]{:S(2)}, u32[]{:S(2)}) collective-permute-start(bf16[4,40,3840]{2,1,0:T(8,128)(2,1)} %collective-permute-done.16.refs_2_), channel_id=1, source_target_pairs={{0,1},{1,0},{2,3},{3,2},{4,5},{5,4},{6,7},{7,6},{8,9},{9,8},{10,11... | collective-permute-start | bytes 3686408 | tf_op jit(solution)/shard_map/ppermute | solution.py:758
  285.2 99.8 %reduce-scatter.5.cloned.1.call-start = ((), (), s32[]{:S(2)}) async-start(), calls=%async_computation.12 | async-start | bytes 3276800 | tf_op jit(solution)/shard_map/reduce_scatter | solution.py:808
  374.8 136.4 %reduce-scatter.7.cloned.1.call-start = ((), (), s32[]{:S(2)}) async-start(), calls=%async_computation.13 | async-start | bytes 1536000 | tf_op jit(solution)/shard_map/reduce_scatter | solution.py:808
  385.1 30.1 %collective-permute-start.34 = (bf16[2,2,4,40,3840]{4,3,2,1,0:T(8,128)(2,1)}, bf16[2,2,4,40,3840]{4,3,2,1,0:T(8,128)(2,1)}, u32[]{:S(2)}, u32[]{:S(2)}) collective-permute-start(bf16[2,2,4,40,3840]{4,3,2,1,0:T(8,128)(2,1)} %get-tuple-element.191), channel_id=1, source_target_pairs={{0,1},{1,0},{2,3},{3,2},{4,5},{5,4},{6,7},{7,6},{8,9},{9,8},{10,11... | collective-permute-start | bytes 14745608 | tf_op jit(solution)/shard_map/ppermute | solution.py:758
  385.5 29.2 %collective-permute-start.35 = (bf16[4,40,3840]{2,1,0:T(8,128)(2,1)}, bf16[4,40,3840]{2,1,0:T(8,128)(2,1)S(1)}, u32[]{:S(2)}, u32[]{:S(2)}) collective-permute-start(bf16[4,40,3840]{2,1,0:T(8,128)(2,1)} %pad_maximum_fusion), channel_id=1, source_target_pairs={{0,4},{4,0},{1,5},{5,1},{2,6},{6,2},{3,7},{7,3},{8,12},{12,8},{9,1... | collective-permute-start | bytes 3686408 | tf_op jit(solution)/shard_map/ppermute | solution.py:758
  386.0 29.1 %collective-permute-start.36 = (bf16[4,40,3840]{2,1,0:T(8,128)(2,1)}, bf16[4,40,3840]{2,1,0:T(8,128)(2,1)S(1)}, u32[]{:S(2)}, u32[]{:S(2)}) collective-permute-start(bf16[4,40,3840]{2,1,0:T(8,128)(2,1)} %pad_maximum_fusion.1), channel_id=1, source_target_pairs={{0,2},{1,3},{2,0},{3,1},{4,6},{5,7},{6,4},{7,5},{8,10},{9,11},{10,... | collective-permute-start | bytes 3686408 | tf_op jit(solution)/shard_map/ppermute | solution.py:758
  425.6 119.9 %reduce-scatter.9.cloned.1.call-start = ((), (), s32[]{:S(2)}) async-start(), calls=%async_computation.14 | async-start | bytes 3276800 | tf_op jit(solution)/shard_map/reduce_scatter | solution.py:808
  437.7 36.2 %collective-permute-start.43 = (bf16[160,960]{1,0:T(8,128)(2,1)}, bf16[160,960]{1,0:T(8,128)(2,1)}, u32[]{:S(2)}, u32[]{:S(2)}) collective-permute-start(bf16[160,960]{1,0:T(8,128)(2,1)} %dynamic-slice_bitcast_fusion.8), channel_id=1, source_target_pairs={{0,4},{4,0},{1,5},{5,1},{2,6},{6,2},{3,7},{7,3},{8,12},{12,8},{9,1... | collective-permute-start | bytes 921608 | tf_op jit(solution)/shard_map/ppermute | solution.py:758
  443.2 103.4 %reduce-scatter.11.cloned.1.call-start = ((), (), s32[]{:S(2)}) async-start(), calls=%async_computation.15 | async-start | bytes 1536000 | tf_op jit(solution)/shard_map/reduce_scatter | solution.py:808
  466.9 44.3 %collective-permute-start.41 = (bf16[4,40,3840]{2,1,0:T(8,128)(2,1)}, bf16[4,40,3840]{2,1,0:T(8,128)(2,1)}, u32[]{:S(2)}, u32[]{:S(2)}) collective-permute-start(bf16[4,40,3840]{2,1,0:T(8,128)(2,1)} %pad_maximum_fusion.2), channel_id=1, source_target_pairs={{0,4},{4,0},{1,5},{5,1},{2,6},{6,2},{3,7},{7,3},{8,12},{12,8},{9,1... | collective-permute-start | bytes 3686408 | tf_op jit(solution)/shard_map/ppermute | solution.py:758
  468.5 42.8 %collective-permute-start.42 = (bf16[4,40,3840]{2,1,0:T(8,128)(2,1)}, bf16[4,40,3840]{2,1,0:T(8,128)(2,1)}, u32[]{:S(2)}, u32[]{:S(2)}) collective-permute-start(bf16[4,40,3840]{2,1,0:T(8,128)(2,1)} %pad_maximum_fusion.3), channel_id=1, source_target_pairs={{0,2},{1,3},{2,0},{3,1},{4,6},{5,7},{6,4},{7,5},{8,10},{9,11},{10,... | collective-permute-start | bytes 3686408 | tf_op jit(solution)/shard_map/ppermute | solution.py:758
  470.3 40.8 %collective-permute-start.40 = (bf16[2,128,1280]{2,1,0:T(8,128)(2,1)S(1)}, bf16[2,128,1280]{2,1,0:T(8,128)(2,1)S(1)}, u32[]{:S(2)}, u32[]{:S(2)}) collective-permute-start(bf16[2,128,1280]{2,1,0:T(8,128)(2,1)S(1)} %fusion.81), channel_id=1, source_target_pairs={{0,2},{1,3},{2,0},{3,1},{4,6},{5,7},{6,4},{7,5},{8,10},{9,11},{10,... | collective-permute-start | bytes 1966088 | tf_op jit(solution)/shard_map/ppermute | solution.py:758
  472.0 50.6 %collective-permute-start.47 = (f32[2,80]{1,0:T(2,128)S(1)}, f32[2,80]{1,0:T(2,128)S(1)}, u32[]{:S(2)}, u32[]{:S(2)}) collective-permute-start(f32[2,80]{1,0:T(2,128)S(1)} %fusion.93), channel_id=1, source_target_pairs={{0,2},{1,3},{2,0},{3,1},{4,6},{5,7},{6,4},{7,5},{8,10},{9,11},{10,... | collective-permute-start | bytes 1928 | tf_op jit(solution)/shard_map/ppermute | solution.py:758
  516.3 25.9 %all-to-all-start.7 = ((bf16[4,40,960]{2,1,0:T(8,128)(2,1)}), bf16[4,40,960]{2,1,0:T(8,128)(2,1)}, u32[]{:S(2)}, u32[]{:S(2)}) async-start(bf16[4,40,960]{2,1,0:T(8,128)(2,1)} %bitcast.225), calls=%async_computation.10 | async-start | bytes 655360 | tf_op jit(solution)/shard_map/all_to_all | solution.py:779
  522.1 22.2 %collective-permute-start.44 = (bf16[128,1280]{1,0:T(8,128)(2,1)S(1)}, bf16[128,1280]{1,0:T(8,128)(2,1)S(1)}, u32[]{:S(2)}, u32[]{:S(2)}) collective-permute-start(bf16[128,1280]{1,0:T(8,128)(2,1)S(1)} %dynamic-slice_bitcast_fusion.7), channel_id=1, source_target_pairs={{0,4},{4,0},{1,5},{5,1},{2,6},{6,2},{3,7},{7,3},{8,12},{12,8},{9,1... | collective-permute-start | bytes 983048 | tf_op jit(solution)/shard_map/ppermute | solution.py:758
  (110 other events, 1190.1 us)
Sparse Core Ops, SparseCore 0:
  15.5 32.9 all-gather.8
  50.7 31.7 all-gather.10
  84.0 31.6 all-gather.12
  117.8 30.2 all-gather.14
  322.9 51.4 reduce-scatter.4
  425.7 30.1 reduce-scatter.6
  458.3 50.8 reduce-scatter.8
  514.9 29.3 reduce-scatter.10

commit v12 on v11

--- a/solution.py
+++ b/solution.py
@@ -360,7 +360,13 @@
 
 Q_ROWS = 256
 KERNEL = pltpu.CompilerParams(vmem_limit_bytes=32 * 1024 * 1024)
-LIGHT = pl.CostEstimate(flops=1 << 20, bytes_accessed=1 << 20, transcendentals=0)
+
+
+def lasting(microseconds):
+    weight = 10 * microseconds
+    return pl.CostEstimate(
+        flops=weight * 10**9, bytes_accessed=weight * 3 * 10**6, transcendentals=0
+    )
 
 
 def in_hbm(*arrays):
@@ -424,13 +430,13 @@
             pl.BlockSpec((1, 1, length), lambda h: (h, 0, 0)),
         ],
         out_shape=[
-            pltpu.HBM((owners, local_heads, head_dim, tokens), BF16),
-            pltpu.HBM((local_heads, 1, length), F32),
+            jax.ShapeDtypeStruct((owners, local_heads, head_dim, tokens), BF16),
+            jax.ShapeDtypeStruct((local_heads, 1, length), F32),
         ],
         compiler_params=KERNEL,
-        cost_estimate=LIGHT,
+        cost_estimate=lasting(10),
     )(
-        *in_hbm(projected.reshape(3, local_heads, head_dim, length)),
+        projected.reshape(3, local_heads, head_dim, length),
         scale_vec.reshape(head_dim, 1),
         segments.reshape(length, 1),
         segments.reshape(1, length),
@@ -527,7 +533,7 @@
             pltpu.VMEM((head_dim, length), F32),
         ],
         compiler_params=KERNEL,
-        cost_estimate=LIGHT,
+        cost_estimate=lasting(12),
     )(
         *in_hbm(
             projected.reshape(3, local_heads, head_dim, length),
@@ -585,13 +591,14 @@
         ),
         out_shape=[shape, shape],
         compiler_params=KERNEL,
-        cost_estimate=LIGHT,
+        cost_estimate=lasting(8),
     )(place(), *in_hbm(attended_t, normed, active, out_bar, up_bar, down_bar))
 
 
 def place():
     head = lax.axis_index("head")
-    return jnp.stack([lax.axis_index("blk"), head // 2, head % 2]).astype(jnp.int32)
+    index = [lax.axis_index("blk"), head // 2, head % 2, lax.axis_index("batch")]
+    return jnp.stack(index).astype(jnp.int32)
 
 
 def assemble_kernel(place_ref, *refs):
@@ -622,10 +629,10 @@
             in_specs=specs,
             out_specs=pl.BlockSpec((1, 2, 2, 2, own, columns), lambda i, at: (i, 0, 0, 0, 0, 0)),
         ),
-        out_shape=pltpu.HBM((batch, 2, 2, 2, own, columns), BF16),
+        out_shape=jax.ShapeDtypeStruct((batch, 2, 2, 2, own, columns), BF16),
         compiler_params=KERNEL,
-        cost_estimate=LIGHT,
-    )(place(), *in_hbm(*pieces))
+        cost_estimate=lasting(6),
+    )(place(), *pieces)
     return whole.reshape(-1, columns)
 
 
@@ -639,9 +646,11 @@
         extra[0, 1 - blk] = across_ref[0, :, columns:]
 
 
-def assemble_columns(along, across, columns):
+def assemble_columns(along, across, columns, by_distance):
     batch, own, both = along.shape
-    rows = pl.BlockSpec((1, own, both), lambda i, at: (i, 0, 0))
+    rows = pl.BlockSpec(
+        (1, own, both), lambda i, at: (i ^ at[3] if by_distance else i, 0, 0)
+    )
     shapes = [(batch, 2, own, columns)]
     if both > columns:
         shapes.append((batch, 2, own, both - columns))
@@ -655,7 +664,7 @@
         ),
         out_shape=[pltpu.HBM(s, BF16) for s in shapes],
         compiler_params=KERNEL,
-        cost_estimate=LIGHT,
+        cost_estimate=lasting(3),
     )(place(), *in_hbm(along, across))
     return [part.reshape(-1, part.shape[-1]) for part in parts]
 
@@ -700,7 +709,7 @@
             pltpu.HBM((columns, length), F32),
         ],
         compiler_params=KERNEL,
-        cost_estimate=LIGHT,
+        cost_estimate=lasting(7),
     )(place(), *in_hbm(*pieces), gain.reshape(1, width), *in_hbm(weight))
 
 
@@ -745,7 +754,7 @@
             pltpu.HBM((width, columns), BF16),
         ],
         compiler_params=KERNEL,
-        cost_estimate=LIGHT,
+        cost_estimate=lasting(11),
     )(place(), *in_hbm(bars, weight, normed))
 
 
@@ -889,30 +898,26 @@
     ]
 
     first = swap_halves(tokens).reshape(-1, width)
-    upper = swap_halves(cotangent).reshape(-1, width)
     dense_near = along_batch(dense_own[0])
     columns = qkv_columns(qkv_weight[0], own_gains.T)
-    columns, first, upper = tied(columns.reshape(-1, columns.shape[-1]), first, upper)
-    stream, upper = first.astype(F32), upper.astype(F32)
+    columns, first = tied(columns.reshape(-1, columns.shape[-1]), first)
+    stream = first.astype(F32)
+    along = [columns] + [swapped(columns, "batch", mask) for mask in (1, 2, 3)]
     far, near = swapped(first, "head", 2), other_core(first)
+    far, along = tied(far, along)
     both = other_core(far)
-    columns, dense_near, near, far, both = tied(columns, dense_near, near, far, both)
+    next_columns = qkv_columns(qkv_weight[1], None).reshape(-1, part3)
+    along, dense_near, near, both, next_columns = tied(
+        along, dense_near, near, both, next_columns
+    )
     token_pieces = (first, near, far, both)
-    across, beside = swapped(dense_near, "blk", 1), swapped(dense_near, "head", 2)
-    along = along_batch(columns)
-    next_columns = qkv_columns(qkv_weight[1], None).reshape(-1, part3)
-    along, across, beside, next_columns = tied(along, across, beside, next_columns)
+    along = jnp.stack(along)
     qkv_across = swapped(along, "blk", 1)
-    one = to_beside(across)
+    beside = swapped(dense_near, "head", 2)
     next_along = along_batch(next_columns)
-    qkv_across, one, beside, next_along, dense_next = tied(
-        qkv_across, one, beside, next_along, dense_own[1]
-    )
-    two, next_along = tied(to_across(beside), next_along)
-    next_across = swapped(next_along, "blk", 1)
-    pieces = [(dense_near, across, beside, one, two)]
-    dense_next = along_batch(dense_next)
-    weight, gains = assemble_columns(along, qkv_across, part3)
+    qkv_across, dense_near, beside = tied(qkv_across, dense_near, beside)
+    across = swapped(dense_near, "blk", 1)
+    weight, gains = assemble_columns(along, qkv_across, part3, True)
     qkvs = [weight]
     gains = gains.T.astype(F32)
 
@@ -920,33 +925,45 @@
     for layer in range(layers):
         normed, factor_one = normalize(stream, gains[layer])
         if layer == 1:
-            normed, beside = tied(normed.astype(BF16), beside)
+            normed, beside, next_across, dense_after = tied(
+                normed.astype(BF16), beside, next_across, dense_next
+            )
             far, near = swapped(normed, "head", 2), other_core(normed)
-            far, near, across, beside = tied(far, near, across, beside)
+            across = swapped(dense_after, "blk", 1)
             token_pieces = (normed, near, far, other_core(far))
-            one, two = to_beside(across), to_across(beside)
-            pieces.append((dense_next, across, beside, one, two))
-            qkvs.append(assemble_columns(next_along, next_across, part3)[0])
+            qkvs.append(assemble_columns(next_along, next_across, part3, False)[0])
         normed_all, projected = project(
             token_pieces, gains[layer], qkvs[layer], layer == 0, token_rows
         )
+        if layer == 0:
+            projected, next_along, dense_next = tied(projected, next_along, dense_own[1])
+            dense_next = along_batch(dense_next)
+        else:
+            projected, across, beside = tied(projected, across, beside)
+            one, two = to_beside(across), to_across(beside)
         attended, log_total = attend_rows(
             projected, scale_vecs[layer], segments, 4, token_rows
         )
-        attended, one, two = tied(attended, *pieces[layer][3:])
-        pieces[layer] = pieces[layer][:3] + (one, two)
-        swaps = tuple(other_core(piece) for piece in pieces[layer])
         if layer == 0:
-            attended, dense_next = tied(attended, dense_next)
+            attended, across = tied(attended, across)
+            one, two = to_beside(across), to_across(beside)
+            pieces = (dense_near, across, beside, one, two)
+            swaps = tuple(other_core(piece) for piece in pieces)
+            attended_t, swaps, one, two, next_along, dense_next = tied(
+                over_head(attended), swaps, one, two, next_along, dense_next
+            )
+            pieces = pieces[:3] + (one, two) + swaps
+            next_across = swapped(next_along, "blk", 1)
             beside = swapped(dense_next, "head", 2)
-            attended_t, swaps, next_across, dense_next = tied(
-                over_head(attended), swaps, next_across, dense_next
-            )
-            across = swapped(dense_next, "blk", 1)
         else:
-            attended_t, swaps = tied(over_head(attended), swaps)
+            attended, one, two = tied(attended, one, two)
+            pieces = (dense_next, across, beside, one, two)
+            swaps = tuple(other_core(piece) for piece in pieces)
+            attended_t, swaps, cotangent = tied(over_head(attended), swaps, cotangent)
+            pieces += swaps
+            upper = swap_halves(cotangent)
         attended_t = attended_t.reshape(width, -1)
-        denses.append(assemble(pieces[layer] + swaps))
+        denses.append(assemble(pieces))
         dense = denses[layer]
         out_w, up_w, down_w = dense[:, :width], dense[:, width:-width], dense[:, -width:]
         middle = stream + dot_rows(attended_t, out_w)
@@ -962,6 +979,7 @@
         )
         stream = middle + dot(active, down_w)
     layer_out = swap_halves(stream.astype(BF16).reshape(tokens.shape))
+    upper = upper.reshape(-1, width).astype(F32)
 
     scale_grads = [None] * layers
     for layer in reversed(range(layers)):

time: 583 us -> 626 us (1.074)
  waiting for transfers between devices: 223 us -> 300 us
  blocking collectives: 28 us -> 0 us
  Pallas kernels: 132 us -> 122 us
    ppermute x51 -> x54, waiting for transfers between devices: 193 us -> 253 us  [swapped(): return lax.ppermute(array, axis, [(i, i ^ mask) for i in range(size)])]
    all_to_all x1 -> x0, blocking collectives: 28 us -> none  [over_head(): lax.all_to_all(parts, 'head', split_axis=0, concat_axis=0, tiled=True)]
    all_to_all x7 -> x8, waiting for transfers between devices: 23.5 us -> 46.9 us  [over_head(): lax.all_to_all(parts, 'head', split_axis=0, concat_axis=0, tiled=True)]
    pallas_call x2, Pallas kernels: 16.5 us -> 8.97 us  [assemble(): pl.pallas_call(assemble_kernel, grid_spec=pltpu.PrefetchScalarGridSpec(nu...]
    unnamed x152 -> x194, local copies, waits for them, and re-layouts: 11.3 us -> 18 us
    all_to_all x7 -> x8, starting transfers between devices: 26.7 us -> 31.5 us  [over_head(): lax.all_to_all(parts, 'head', split_axis=0, concat_axis=0, tiled=True)]
    ppermute x51 -> x54, starting transfers between devices: 43 us -> 40.9 us  [swapped(): return lax.ppermute(array, axis, [(i, i ^ mask) for i in range(size)])]
  transfers between devices with their start and end apart: 66 -> 69, of which waited for: 29 -> 31; matrix products, arithmetic and copies ran while one was open for 12% -> 12% of each run, Pallas kernels for 19% -> 18%
where the time goes in v12:
time: 626 us; the launch traced here: 618 us
  waiting for transfers between devices  300 us (48%)
  Pallas kernels  122 us (19%)
  starting transfers between devices  72.9 us (12%)
  other arithmetic  48 us (8%)
  local copies, waits for them, and re-layouts  39 us (6%)
  matrix products  18.9 us (3%)
  between operations  16.4 us (3%)
    ppermute x54, waiting for transfers between devices, swapped(): return lax.ppermute(array, axis, [(i, i ^ mask) for i in range(size)])  253 us
    all_to_all x8, waiting for transfers between devices, over_head(): lax.all_to_all(parts, 'head', split_axis=0, concat_axis=0, tiled=True)  46.9 us
    ppermute x54, starting transfers between devices, swapped(): return lax.ppermute(array, axis, [(i, i ^ mask) for i in range(size)])  40.9 us
    all_to_all x8, starting transfers between devices, over_head(): lax.all_to_all(parts, 'head', split_axis=0, concat_axis=0, tiled=True)  31.5 us
    pallas_call x2, Pallas kernels, attend_back_rows(): pl.pallas_call(functools.partial(attend_back_kernel, token_rows), grid=(l...  24.9 us
    pallas_call x2, Pallas kernels, project_back(): pl.pallas_call(project_back_kernel, grid_spec=pltpu.PrefetchScalarGridSpe...  23.6 us
    pallas_call x2, Pallas kernels, dense_grads(): pl.pallas_call(dense_grad_kernel, grid_spec=pltpu.PrefetchScalarGridSpec(...  20.1 us
    pallas_call x2, Pallas kernels, attend_rows(): pl.pallas_call(functools.partial(attend_kernel, token_rows), grid=(local_...  19.2 us
  transfers between devices with their start and end apart: 69, of which 31 were waited for; matrix products, arithmetic and copies ran while one was open for 12% of the time, Pallas kernels for 18%

profile of v12, /device:TPU:0, one launch (start us, length us, event | category | flops | bytes accessed | tf_op | source)
XLA Modules:
  0.0 617.9 jit_solution(13016883889733529614)
XLA Ops:
  21.1 6.5 %all-to-all-done = bf16[4,40,964]{2,1,0:T(8,128)(2,1)S(1)} async-done(((bf16[4,40,964]{2,1,0:T(8,128)(2,1)}), bf16[4,40,964]{2,1,0:T(8,128)(2,1)S(1)}, u32[]{:S(2)}, u32[]{:S(2)}) %all-to-all-start) | async-done | bytes 308512 | tf_op jit(solution)/shard_map/all_to_all | solution.py:788
  32.4 15.0 %collective-permute-done.4 = bf16[160,964]{1,0:T(8,128)(2,1)S(1)} collective-permute-done((bf16[160,964]{1,0:T(8,128)(2,1)S(1)}, bf16[160,964]{1,0:T(8,128)(2,1)S(1)}, u32[]{:S(2)}, u32[]{:S(2)}) %collective-permute-start.4) | collective-permute-done | bytes 308512 | tf_op jit(solution)/shard_map/ppermute | solution.py:767
  47.4 27.7 %collective-permute-done.3 = bf16[160,964]{1,0:T(8,128)(2,1)S(1)} collective-permute-done((bf16[160,964]{1,0:T(8,128)(2,1)S(1)}, bf16[160,964]{1,0:T(8,128)(2,1)S(1)}, u32[]{:S(2)}, u32[]{:S(2)}) %collective-permute-start.3) | collective-permute-done | bytes 308512 | tf_op jit(solution)/shard_map/ppermute | solution.py:767
  80.4 6.6 %all-to-all-done.1 = bf16[4,40,960]{2,1,0:T(8,128)(2,1)S(1)} async-done(((bf16[4,40,960]{2,1,0:T(8,128)(2,1)}), bf16[4,40,960]{2,1,0:T(8,128)(2,1)S(1)}, u32[]{:S(2)}, u32[]{:S(2)}) %all-to-all-start.1) | async-done | bytes 307232 | tf_op jit(solution)/shard_map/all_to_all | solution.py:788
  92.4 23.6 %collective-permute-done.8.refs_2_ = bf16[4,40,3840]{2,1,0:T(8,128)(2,1)} collective-permute-done((bf16[4,40,3840]{2,1,0:T(8,128)(2,1)}, bf16[4,40,3840]{2,1,0:T(8,128)(2,1)}, u32[]{:S(2)}, u32[]{:S(2)}) %collective-permute-start.8) | collective-permute-done | bytes 1228832 | tf_op jit(solution)/shard_map/ppermute | solution.py:767
  130.1 8.8 %shard_map.170 = (bf16[1024,1280]{1,0:T(8,128)(2,1)}, f32[960,1024]{1,0:T(8,128)}) custom-call(s32[4]{0:T(128)S(1)} %pad_add_fusion.place_ref.core_ref, bf16[256,1280]{1,0:T(8,128)(2,1)} %bitcast.208, bf16[256,1280]{1,0:T(8,128)(2,1)} %collective-permute-done.5.refs_1_, bf16[256,1280]{1,0:T(8,128)(2,1)} %collective-permute-done.1.refs_2_, ...), custom_call_target="tpu_custom_call" | custom-call | flops 70000001024 | bytes 210000000 | tf_op jit(solution)/shard_map/pallas_call | solution.py:692
  141.2 9.6 %shard_map.171 = (bf16[4,4,80,256]{3,2,1,0:T(8,128)(2,1)}, f32[4,1,1024]{2,1,0:T(1,128)S(1)}) custom-call(f32[3,4,80,1024]{3,2,1,0:T(8,128)S(1)} %bitcast.197, f32[80,1]{1,0:T(8,128)S(1)} %copy.42.scale_ref, s32[1024,1]{1,0:T(8,128)S(1)} %copy.43.col_ref, s32[1,1024]{1,0:T(1,128)S(1)} %constant_dynamic-slice_fusion.row_ref), custom_call_target="tpu_custom_call" | custom-call | flops 99999997952 | bytes 300000000 | tf_op jit(solution)/shard_map/pallas_call | solution.py:419
  153.3 9.0 %collective-permute-done.15.refs_4_ = bf16[4,40,1920]{2,1,0:T(8,128)(2,1)} collective-permute-done((bf16[4,40,1920]{2,1,0:T(8,128)(2,1)}, bf16[4,40,1920]{2,1,0:T(8,128)(2,1)}, u32[]{:S(2)}, u32[]{:S(2)}) %collective-permute-start.15) | collective-permute-done | bytes 614432 | tf_op jit(solution)/shard_map/ppermute | solution.py:767
  162.4 5.3 collective-permute-done.13.refs_3_
  173.2 9.5 %all-to-all-done.2 = bf16[4,320,256]{2,1,0:T(8,128)(2,1)} async-done(((bf16[4,320,256]{2,1,0:T(8,128)(2,1)}), bf16[4,320,256]{2,1,0:T(8,128)(2,1)}, u32[]{:S(2)}, u32[]{:S(2)}) %all-to-all-start.2) | async-done | bytes 655392 | tf_op jit(solution)/shard_map/all_to_all | solution.py:788
  198.9 12.6 %collective-permute-done.17.refs_2_ = bf16[4,40,3840]{2,1,0:T(8,128)(2,1)S(1)} collective-permute-done((bf16[4,40,3840]{2,1,0:T(8,128)(2,1)}, bf16[4,40,3840]{2,1,0:T(8,128)(2,1)S(1)}, u32[]{:S(2)}, u32[]{:S(2)}) %collective-permute-start.17) | collective-permute-done | bytes 1228832 | tf_op jit(solution)/shard_map/ppermute | solution.py:767
  215.7 13.7 %collective-permute-done.20.refs_2_ = bf16[256,1280]{1,0:T(8,128)(2,1)} collective-permute-done((bf16[256,1280]{1,0:T(8,128)(2,1)}, bf16[256,1280]{1,0:T(8,128)(2,1)}, u32[]{:S(2)}, u32[]{:S(2)}) %collective-permute-start.20) | collective-permute-done | bytes 655392 | tf_op jit(solution)/shard_map/ppermute | solution.py:767
  236.5 7.8 %shard_map.174 = (bf16[1024,1280]{1,0:T(8,128)(2,1)}, f32[960,1024]{1,0:T(8,128)}) custom-call(s32[4]{0:T(128)S(1)} %pad_add_fusion.place_ref.core_ref, bf16[256,1280]{1,0:T(8,128)(2,1)} %multiply_convert_fusion.2.refs_0_, bf16[256,1280]{1,0:T(8,128)(2,1)} %copy-done.85, bf16[256,1280]{1,0:T(8,128)(2,1)} %collective-permute-done.20.refs_2_, ...), custom_call_target="tpu_custom_call" | custom-call | flops 70000001024 | bytes 210000000 | tf_op jit(solution)/shard_map/pallas_call | solution.py:692
  244.2 19.4 %collective-permute-done.22.refs_1_ = bf16[4,40,3840]{2,1,0:T(8,128)(2,1)S(1)} collective-permute-done((bf16[4,40,3840]{2,1,0:T(8,128)(2,1)}, bf16[4,40,3840]{2,1,0:T(8,128)(2,1)S(1)}, u32[]{:S(2)}, u32[]{:S(2)}) %collective-permute-start.22) | collective-permute-done | bytes 1228832 | tf_op jit(solution)/shard_map/ppermute | solution.py:767
  268.9 9.6 %shard_map.175 = (bf16[4,4,80,256]{3,2,1,0:T(8,128)(2,1)}, f32[4,1,1024]{2,1,0:T(1,128)S(1)}) custom-call(f32[3,4,80,1024]{3,2,1,0:T(8,128)S(1)} %bitcast.199, f32[80,1]{1,0:T(8,128)S(1)} %copy.44.scale_ref, s32[1024,1]{1,0:T(8,128)S(1)} %copy.43.col_ref, s32[1,1024]{1,0:T(1,128)S(1)} %copy-done.5), custom_call_target="tpu_custom_call" | custom-call | flops 99999997952 | bytes 300000000 | tf_op jit(solution)/shard_map/pallas_call | solution.py:419
  286.3 10.3 %all-to-all-done.3 = bf16[4,320,256]{2,1,0:T(8,128)(2,1)} async-done(((bf16[4,320,256]{2,1,0:T(8,128)(2,1)}), bf16[4,320,256]{2,1,0:T(8,128)(2,1)}, u32[]{:S(2)}, u32[]{:S(2)}) %all-to-all-start.3) | async-done | bytes 655392 | tf_op jit(solution)/shard_map/all_to_all | solution.py:788
  313.9 9.9 %shard_map.177 = (bf16[2,2,4,40,3840]{4,3,2,1,0:T(8,128)(2,1)}, bf16[2,2,4,40,3840]{4,3,2,1,0:T(8,128)(2,1)}) custom-call(s32[4]{0:T(128)S(1)} %pad_add_fusion.place_ref.core_ref, bf16[1280,256]{1,0:T(8,128)(2,1)} %bitcast.47.attended_ref, bf16[256,1280]{1,0:T(8,128)(2,1)} %copy-done.45, bf16[256,1280]{1,0:T(8,128)(2,1)} %copy-done.90, ...), custom_call_target="tpu_custom_call" | custom-call | flops 80000000000 | bytes 240000000 | tf_op jit(solution)/shard_map/pallas_call | solution.py:583
  330.4 9.0 %all-to-all-done.4 = bf16[4,320,256]{2,1,0:T(8,128)(2,1)S(1)} async-done(((bf16[4,320,256]{2,1,0:T(8,128)(2,1)}), bf16[4,320,256]{2,1,0:T(8,128)(2,1)S(1)}, u32[]{:S(2)}, u32[]{:S(2)}) %all-to-all-start.4) | async-done | bytes 655392 | tf_op jit(solution)/shard_map/all_to_all | solution.py:788
  340.2 12.3 %shard_map.178 = (bf16[3,4,80,1024]{3,2,1,0:T(8,128)(2,1)}, f32[80,128]{1,0:T(8,128)}) custom-call(f32[3,4,80,1024]{3,2,1,0:T(8,128)} %bitcast.198, bf16[4,4,80,256]{3,2,1,0:T(8,128)(2,1)} %bitcast.230, f32[4,1,1024]{2,1,0:T(1,128)S(1)} %get-tuple-element.177.lse_ref, f32[80,1]{1,0:T(8,128)S(1)} %copy.44.scale_ref, s32[1024,1]{1,0:T(8,128)S(1)} %copy.43.col_ref, ...), custom_call_target="tpu_custom_call" | custom-call | flops 120000004096 | bytes 360000000 | tf_op jit(solution)/shard_map/pallas_call | solution.py:512
  352.6 12.5 %shard_map.179 = (f32[2,2,128,1280]{3,2,1,0:T(8,128)}, bf16[2,2,128,1280]{3,2,1,0:T(8,128)(2,1)}, bf16[1280,960]{1,0:T(8,128)(2,1)}) custom-call(s32[4]{0:T(128)S(1)} %pad_add_fusion.place_ref.core_ref, bf16[960,1024]{1,0:T(8,128)(2,1)} %bitcast.250, bf16[1280,960]{1,0:T(8,128)(2,1)} %bitcast.248, bf16[1024,1280]{1,0:T(8,128)(2,1)} %get-tuple-element.181.normed_ref), custom_call_target="tpu_custom_call" | custom-call | flops 109999996928 | bytes 330000000 | tf_op jit(solution)/shard_map/pallas_call | solution.py:738
  370.8 5.2 add_convert_fusion.1
  376.0 11.3 %collective-permute-done.34 = bf16[2,128,1280]{2,1,0:T(8,128)(2,1)S(1)} collective-permute-done((bf16[2,128,1280]{2,1,0:T(8,128)(2,1)S(1)}, bf16[2,128,1280]{2,1,0:T(8,128)(2,1)S(1)}, u32[]{:S(2)}, u32[]{:S(2)}) %collective-permute-start.34) | collective-permute-done | bytes 655392 | tf_op jit(solution)/shard_map/ppermute | solution.py:767
  395.9 12.9 %collective-permute-done.36 = bf16[4,40,1920]{2,1,0:T(8,128)(2,1)S(1)} collective-permute-done((bf16[4,40,1920]{2,1,0:T(8,128)(2,1)S(1)}, bf16[4,40,1920]{2,1,0:T(8,128)(2,1)S(1)}, u32[]{:S(2)}, u32[]{:S(2)}) %collective-permute-start.36) | collective-permute-done | bytes 614432 | tf_op jit(solution)/shard_map/ppermute | solution.py:767
  416.5 10.2 %shard_map.180 = (bf16[2,2,4,40,3840]{4,3,2,1,0:T(8,128)(2,1)}, bf16[2,2,4,40,3840]{4,3,2,1,0:T(8,128)(2,1)}) custom-call(s32[4]{0:T(128)S(1)} %pad_add_fusion.place_ref.core_ref, bf16[1280,256]{1,0:T(8,128)(2,1)} %bitcast.34.attended_ref, bf16[256,1280]{1,0:T(8,128)(2,1)} %copy-done.44, bf16[256,1280]{1,0:T(8,128)(2,1)} %copy-done.89, ...), custom_call_target="tpu_custom_call" | custom-call | flops 80000000000 | bytes 240000000 | tf_op jit(solution)/shard_map/pallas_call | solution.py:583
  429.1 12.5 %shard_map.181 = (bf16[3,4,80,1024]{3,2,1,0:T(8,128)(2,1)}, f32[80,128]{1,0:T(8,128)}) custom-call(f32[3,4,80,1024]{3,2,1,0:T(8,128)} %bitcast.196, bf16[4,4,80,256]{3,2,1,0:T(8,128)(2,1)} %bitcast.65.grad_ref, f32[4,1,1024]{2,1,0:T(1,128)S(1)} %get-tuple-element.195.lse_ref, f32[80,1]{1,0:T(8,128)S(1)} %copy-done.3, s32[1024,1]{1,0:T(8,128)S(1)} %copy.43.col_ref, ...), custom_call_target="tpu_custom_call" | custom-call | flops 120000004096 | bytes 360000000 | tf_op jit(solution)/shard_map/pallas_call | solution.py:512
  441.7 14.6 %collective-permute-done.38 = bf16[4,40,3840]{2,1,0:T(8,128)(2,1)S(1)} collective-permute-done((bf16[4,40,3840]{2,1,0:T(8,128)(2,1)}, bf16[4,40,3840]{2,1,0:T(8,128)(2,1)S(1)}, u32[]{:S(2)}, u32[]{:S(2)}) %collective-permute-start.38) | collective-permute-done | bytes 1228832 | tf_op jit(solution)/shard_map/ppermute | solution.py:767
  470.1 11.1 %shard_map.182 = (f32[2,2,128,1280]{3,2,1,0:T(8,128)}, bf16[2,2,128,1280]{3,2,1,0:T(8,128)(2,1)}, bf16[1280,960]{1,0:T(8,128)(2,1)}) custom-call(s32[4]{0:T(128)S(1)} %pad_add_fusion.place_ref.core_ref, bf16[960,1024]{1,0:T(8,128)(2,1)} %bitcast.249, bf16[1280,960]{1,0:T(8,128)(2,1)} %bitcast.246, bf16[1024,1280]{1,0:T(8,128)(2,1)} %get-tuple-element.206.normed_ref), custom_call_target="tpu_custom_call" | custom-call | flops 109999996928 | bytes 330000000 | tf_op jit(solution)/shard_map/pallas_call | solution.py:738
  489.2 16.5 %collective-permute-done.41 = bf16[4,40,1920]{2,1,0:T(8,128)(2,1)} collective-permute-done((bf16[4,40,1920]{2,1,0:T(8,128)(2,1)}, bf16[4,40,1920]{2,1,0:T(8,128)(2,1)}, u32[]{:S(2)}, u32[]{:S(2)}) %collective-permute-start.41) | collective-permute-done | bytes 614432 | tf_op jit(solution)/shard_map/ppermute | solution.py:767
  517.9 36.4 %collective-permute-done.43 = bf16[2,128,1280]{2,1,0:T(8,128)(2,1)S(1)} collective-permute-done((bf16[2,128,1280]{2,1,0:T(8,128)(2,1)S(1)}, bf16[2,128,1280]{2,1,0:T(8,128)(2,1)S(1)}, u32[]{:S(2)}, u32[]{:S(2)}) %collective-permute-start.43) | collective-permute-done | bytes 655392 | tf_op jit(solution)/shard_map/ppermute | solution.py:767
  567.2 8.0 %collective-permute-done.51 = f32[2,80]{1,0:T(2,128)S(1)} collective-permute-done((f32[2,80]{1,0:T(2,128)S(1)}, f32[2,80]{1,0:T(2,128)S(1)}, u32[]{:S(2)}, u32[]{:S(2)}) %collective-permute-start.51) | collective-permute-done | bytes 672 | tf_op jit(solution)/shard_map/ppermute | solution.py:767
  591.3 5.6 collective-permute-done.48
  602.9 5.0 all-to-all-done.6
  (444 shorter events, 213.5 us)
Async XLA Ops:
  7.2 79.9 %all-gather.7.cloned.1.call-start = ((), (), s32[]{:S(2)}) async-start(), calls=%async_computation.16 | async-start | bytes 1536000 | tf_op jit(solution)/shard_map/all_gather | solution.py:801
  27.6 47.5 %collective-permute-start.1 = (bf16[256,1280]{1,0:T(8,128)(2,1)S(1)}, bf16[256,1280]{1,0:T(8,128)(2,1)}, u32[]{:S(2)}, u32[]{:S(2)}) collective-permute-start(bf16[256,1280]{1,0:T(8,128)(2,1)S(1)} %bitcast.206), channel_id=1, source_target_pairs={{0,2},{1,3},{2,0},{3,1},{4,6},{5,7},{6,4},{7,5},{8,10},{9,11},{10,... | collective-permute-start | bytes 1966088 | tf_op jit(solution)/shard_map/ppermute | solution.py:767
  31.6 43.5 %collective-permute-start.3 = (bf16[160,964]{1,0:T(8,128)(2,1)S(1)}, bf16[160,964]{1,0:T(8,128)(2,1)S(1)}, u32[]{:S(2)}, u32[]{:S(2)}) collective-permute-start(bf16[160,964]{1,0:T(8,128)(2,1)S(1)} %bitcast.223), channel_id=1, source_target_pairs={{0,16},{8,24},{16,0},{24,8},{1,17},{9,25},{17,1},{25,9},{2,18},{10... | collective-permute-start | bytes 925448 | tf_op jit(solution)/shard_map/ppermute | solution.py:767
  31.6 43.5 %collective-permute-start.2 = (bf16[160,964]{1,0:T(8,128)(2,1)S(1)}, bf16[160,964]{1,0:T(8,128)(2,1)S(1)}, u32[]{:S(2)}, u32[]{:S(2)}) collective-permute-start(bf16[160,964]{1,0:T(8,128)(2,1)S(1)} %bitcast.224), channel_id=1, source_target_pairs={{0,8},{8,0},{16,24},{24,16},{1,9},{9,1},{17,25},{25,17},{2,10},{10... | collective-permute-start | bytes 925448 | tf_op jit(solution)/shard_map/ppermute | solution.py:767
  32.4 54.7 %collective-permute-start.5 = (bf16[256,1280]{1,0:T(8,128)(2,1)S(1)}, bf16[256,1280]{1,0:T(8,128)(2,1)}, u32[]{:S(2)}, u32[]{:S(2)}) collective-permute-start(bf16[256,1280]{1,0:T(8,128)(2,1)S(1)} %bitcast.207), channel_id=1, source_target_pairs={{0,1},{1,0},{2,3},{3,2},{4,5},{5,4},{6,7},{7,6},{8,9},{9,8},{10,11... | collective-permute-start | bytes 1966088 | tf_op jit(solution)/shard_map/ppermute | solution.py:767
  80.4 58.6 %all-gather.9.cloned.1.call-start = ((), (), s32[]{:S(2)}) async-start(), calls=%async_computation.17 | async-start | bytes 1638400 | tf_op jit(solution)/shard_map/all_gather | solution.py:801
  87.1 28.9 %collective-permute-start.8 = (bf16[4,40,3840]{2,1,0:T(8,128)(2,1)}, bf16[4,40,3840]{2,1,0:T(8,128)(2,1)}, u32[]{:S(2)}, u32[]{:S(2)}) collective-permute-start(bf16[4,40,3840]{2,1,0:T(8,128)(2,1)} %bitcast.15.refs_0_), channel_id=1, source_target_pairs={{0,2},{1,3},{2,0},{3,1},{4,6},{5,7},{6,4},{7,5},{8,10},{9,11},{10,... | collective-permute-start | bytes 3686408 | tf_op jit(solution)/shard_map/ppermute | solution.py:767
  89.0 30.5 %collective-permute-start.7 = (bf16[4,160,964]{2,1,0:T(8,128)(2,1)S(1)}, bf16[4,160,964]{2,1,0:T(8,128)(2,1)}, u32[]{:S(2)}, u32[]{:S(2)}) collective-permute-start(bf16[4,160,964]{2,1,0:T(8,128)(2,1)S(1)} %pad_maximum_fusion.along_ref), channel_id=1, source_target_pairs={{0,4},{4,0},{1,5},{5,1},{2,6},{6,2},{3,7},{7,3},{8,12},{12,8},{9,1... | collective-permute-start | bytes 3701768 | tf_op jit(solution)/shard_map/ppermute | solution.py:767
  92.4 90.3 %all-gather.11.cloned.1.call-start = ((), (), s32[]{:S(2)}) async-start(), calls=%async_computation.18 | async-start | bytes 1536000 | tf_op jit(solution)/shard_map/all_gather | solution.py:801
  119.5 53.8 %collective-permute-start.10 = (bf16[4,40,3840]{2,1,0:T(8,128)(2,1)}, bf16[4,40,3840]{2,1,0:T(8,128)(2,1)}, u32[]{:S(2)}, u32[]{:S(2)}) collective-permute-start(bf16[4,40,3840]{2,1,0:T(8,128)(2,1)} %bitcast.15.refs_0_), channel_id=1, source_target_pairs={{0,1},{1,0},{2,3},{3,2},{4,5},{5,4},{6,7},{7,6},{8,9},{9,8},{10,11... | collective-permute-start | bytes 3686408 | tf_op jit(solution)/shard_map/ppermute | solution.py:767
  119.5 31.3 %collective-permute-start.9 = (bf16[4,40,3840]{2,1,0:T(8,128)(2,1)}, bf16[4,40,3840]{2,1,0:T(8,128)(2,1)}, u32[]{:S(2)}, u32[]{:S(2)}) collective-permute-start(bf16[4,40,3840]{2,1,0:T(8,128)(2,1)} %bitcast.15.refs_0_), channel_id=1, source_target_pairs={{0,4},{4,0},{1,5},{5,1},{2,6},{6,2},{3,7},{7,3},{8,12},{12,8},{9,1... | collective-permute-start | bytes 3686408 | tf_op jit(solution)/shard_map/ppermute | solution.py:767
  122.9 50.4 %collective-permute-start.12 = (bf16[4,40,3840]{2,1,0:T(8,128)(2,1)}, bf16[4,40,3840]{2,1,0:T(8,128)(2,1)}, u32[]{:S(2)}, u32[]{:S(2)}) collective-permute-start(bf16[4,40,3840]{2,1,0:T(8,128)(2,1)} %collective-permute-done.8.refs_2_), channel_id=1, source_target_pairs={{0,1},{1,0},{2,3},{3,2},{4,5},{5,4},{6,7},{7,6},{8,9},{9,8},{10,11... | collective-permute-start | bytes 3686408 | tf_op jit(solution)/shard_map/ppermute | solution.py:767
  129.6 32.8 %collective-permute-start.15 = (bf16[4,40,1920]{2,1,0:T(8,128)(2,1)}, bf16[4,40,1920]{2,1,0:T(8,128)(2,1)}, u32[]{:S(2)}, u32[]{:S(2)}) collective-permute-start(bf16[4,40,1920]{2,1,0:T(8,128)(2,1)} %slice.147), channel_id=1, source_target_pairs={{0,4},{4,0},{1,5},{5,1},{2,6},{6,2},{3,7},{7,3},{8,12},{12,8},{9,1... | collective-permute-start | bytes 1843208 | tf_op jit(solution)/shard_map/ppermute | solution.py:767
  153.3 29.4 %collective-permute-start.11 = (bf16[4,40,3840]{2,1,0:T(8,128)(2,1)}, bf16[4,40,3840]{2,1,0:T(8,128)(2,1)S(1)}, u32[]{:S(2)}, u32[]{:S(2)}) collective-permute-start(bf16[4,40,3840]{2,1,0:T(8,128)(2,1)} %collective-permute-done.9.refs_1_), channel_id=1, source_target_pairs={{0,1},{1,0},{2,3},{3,2},{4,5},{5,4},{6,7},{7,6},{8,9},{9,8},{10,11... | collective-permute-start | bytes 3686408 | tf_op jit(solution)/shard_map/ppermute | solution.py:767
  182.7 28.8 %collective-permute-start.17 = (bf16[4,40,3840]{2,1,0:T(8,128)(2,1)}, bf16[4,40,3840]{2,1,0:T(8,128)(2,1)S(1)}, u32[]{:S(2)}, u32[]{:S(2)}) collective-permute-start(bf16[4,40,3840]{2,1,0:T(8,128)(2,1)} %bitcast.33.refs_0_), channel_id=1, source_target_pairs={{0,2},{1,3},{2,0},{3,1},{4,6},{5,7},{6,4},{7,5},{8,10},{9,11},{10,... | collective-permute-start | bytes 3686408 | tf_op jit(solution)/shard_map/ppermute | solution.py:767
  183.2 30.5 %collective-permute-start.18 = (bf16[4,160,960]{2,1,0:T(8,128)(2,1)}, bf16[4,160,960]{2,1,0:T(8,128)(2,1)S(1)}, u32[]{:S(2)}, u32[]{:S(2)}) collective-permute-start(bf16[4,160,960]{2,1,0:T(8,128)(2,1)} %bitcast.243), channel_id=1, source_target_pairs={{0,4},{4,0},{1,5},{5,1},{2,6},{6,2},{3,7},{7,3},{8,12},{12,8},{9,1... | collective-permute-start | bytes 3686408 | tf_op jit(solution)/shard_map/ppermute | solution.py:767
  215.2 71.2 %collective-permute-start.25 = (bf16[4,40,3840]{2,1,0:T(8,128)(2,1)}, bf16[4,40,3840]{2,1,0:T(8,128)(2,1)}, u32[]{:S(2)}, u32[]{:S(2)}) collective-permute-start(bf16[4,40,3840]{2,1,0:T(8,128)(2,1)} %bitcast.33.refs_0_), channel_id=1, source_target_pairs={{0,1},{1,0},{2,3},{3,2},{4,5},{5,4},{6,7},{7,6},{8,9},{9,8},{10,11... | collective-permute-start | bytes 3686408 | tf_op jit(solution)/shard_map/ppermute | solution.py:767
  233.9 29.6 %collective-permute-start.22 = (bf16[4,40,3840]{2,1,0:T(8,128)(2,1)}, bf16[4,40,3840]{2,1,0:T(8,128)(2,1)S(1)}, u32[]{:S(2)}, u32[]{:S(2)}) collective-permute-start(bf16[4,40,3840]{2,1,0:T(8,128)(2,1)} %bitcast.33.refs_0_), channel_id=1, source_target_pairs={{0,4},{4,0},{1,5},{5,1},{2,6},{6,2},{3,7},{7,3},{8,12},{12,8},{9,1... | collective-permute-start | bytes 3686408 | tf_op jit(solution)/shard_map/ppermute | solution.py:767
  263.6 33.0 %collective-permute-start.26 = (bf16[4,40,3840]{2,1,0:T(8,128)(2,1)S(1)}, bf16[4,40,3840]{2,1,0:T(8,128)(2,1)}, u32[]{:S(2)}, u32[]{:S(2)}) collective-permute-start(bf16[4,40,3840]{2,1,0:T(8,128)(2,1)S(1)} %collective-permute-done.22.refs_1_), channel_id=1, source_target_pairs={{0,1},{1,0},{2,3},{3,2},{4,5},{5,4},{6,7},{7,6},{8,9},{9,8},{10,11... | collective-permute-start | bytes 3686408 | tf_op jit(solution)/shard_map/ppermute | solution.py:767
  263.8 32.9 %collective-permute-start.27 = (bf16[4,40,3840]{2,1,0:T(8,128)(2,1)S(1)}, bf16[4,40,3840]{2,1,0:T(8,128)(2,1)}, u32[]{:S(2)}, u32[]{:S(2)}) collective-permute-start(bf16[4,40,3840]{2,1,0:T(8,128)(2,1)S(1)} %collective-permute-done.17.refs_2_), channel_id=1, source_target_pairs={{0,1},{1,0},{2,3},{3,2},{4,5},{5,4},{6,7},{7,6},{8,9},{9,8},{10,11... | collective-permute-start | bytes 3686408 | tf_op jit(solution)/shard_map/ppermute | solution.py:767
  329.2 99.9 %reduce-scatter.5.cloned.1.call-start = ((), (), s32[]{:S(2)}) async-start(), calls=%async_computation.12 | async-start | bytes 3276800 | tf_op jit(solution)/shard_map/reduce_scatter | solution.py:817
  416.5 138.0 %reduce-scatter.7.cloned.1.call-start = ((), (), s32[]{:S(2)}) async-start(), calls=%async_computation.13 | async-start | bytes 1536000 | tf_op jit(solution)/shard_map/reduce_scatter | solution.py:817
  426.7 29.5 %collective-permute-start.38 = (bf16[4,40,3840]{2,1,0:T(8,128)(2,1)}, bf16[4,40,3840]{2,1,0:T(8,128)(2,1)S(1)}, u32[]{:S(2)}, u32[]{:S(2)}) collective-permute-start(bf16[4,40,3840]{2,1,0:T(8,128)(2,1)} %pad_maximum_fusion.1), channel_id=1, source_target_pairs={{0,4},{4,0},{1,5},{5,1},{2,6},{6,2},{3,7},{7,3},{8,12},{12,8},{9,1... | collective-permute-start | bytes 3686408 | tf_op jit(solution)/shard_map/ppermute | solution.py:767
  427.2 29.2 %collective-permute-start.39 = (bf16[4,40,3840]{2,1,0:T(8,128)(2,1)S(1)}, bf16[4,40,3840]{2,1,0:T(8,128)(2,1)}, u32[]{:S(2)}, u32[]{:S(2)}) collective-permute-start(bf16[4,40,3840]{2,1,0:T(8,128)(2,1)S(1)} %pad_maximum_fusion.2), channel_id=1, source_target_pairs={{0,2},{1,3},{2,0},{3,1},{4,6},{5,7},{6,4},{7,5},{8,10},{9,11},{10,... | collective-permute-start | bytes 3686408 | tf_op jit(solution)/shard_map/ppermute | solution.py:767
  429.1 27.3 %collective-permute-start.37 = (bf16[2,2,4,40,3840]{4,3,2,1,0:T(8,128)(2,1)}, bf16[2,2,4,40,3840]{4,3,2,1,0:T(8,128)(2,1)S(1)}, u32[]{:S(2)}, u32[]{:S(2)}) collective-permute-start(bf16[2,2,4,40,3840]{4,3,2,1,0:T(8,128)(2,1)} %get-tuple-element.197), channel_id=1, source_target_pairs={{0,1},{1,0},{2,3},{3,2},{4,5},{5,4},{6,7},{7,6},{8,9},{9,8},{10,11... | collective-permute-start | bytes 14745608 | tf_op jit(solution)/shard_map/ppermute | solution.py:767
  470.0 117.7 %reduce-scatter.9.cloned.1.call-start = ((), (), s32[]{:S(2)}) async-start(), calls=%async_computation.14 | async-start | bytes 3276800 | tf_op jit(solution)/shard_map/reduce_scatter | solution.py:817
  482.0 35.0 %collective-permute-start.46 = (bf16[160,960]{1,0:T(8,128)(2,1)}, bf16[160,960]{1,0:T(8,128)(2,1)S(1)}, u32[]{:S(2)}, u32[]{:S(2)}) collective-permute-start(bf16[160,960]{1,0:T(8,128)(2,1)} %dynamic-slice_bitcast_fusion.8), channel_id=1, source_target_pairs={{0,4},{4,0},{1,5},{5,1},{2,6},{6,2},{3,7},{7,3},{8,12},{12,8},{9,1... | collective-permute-start | bytes 921608 | tf_op jit(solution)/shard_map/ppermute | solution.py:767
  486.7 103.5 %reduce-scatter.11.cloned.1.call-start = ((), (), s32[]{:S(2)}) async-start(), calls=%async_computation.15 | async-start | bytes 1536000 | tf_op jit(solution)/shard_map/reduce_scatter | solution.py:817
  510.6 43.9 %collective-permute-start.44 = (bf16[4,40,3840]{2,1,0:T(8,128)(2,1)}, bf16[4,40,3840]{2,1,0:T(8,128)(2,1)S(1)}, u32[]{:S(2)}, u32[]{:S(2)}) collective-permute-start(bf16[4,40,3840]{2,1,0:T(8,128)(2,1)} %pad_maximum_fusion.3), channel_id=1, source_target_pairs={{0,4},{4,0},{1,5},{5,1},{2,6},{6,2},{3,7},{7,3},{8,12},{12,8},{9,1... | collective-permute-start | bytes 3686408 | tf_op jit(solution)/shard_map/ppermute | solution.py:767
  511.8 42.7 %collective-permute-start.45 = (bf16[4,40,3840]{2,1,0:T(8,128)(2,1)}, bf16[4,40,3840]{2,1,0:T(8,128)(2,1)}, u32[]{:S(2)}, u32[]{:S(2)}) collective-permute-start(bf16[4,40,3840]{2,1,0:T(8,128)(2,1)} %pad_maximum_fusion.4), channel_id=1, source_target_pairs={{0,2},{1,3},{2,0},{3,1},{4,6},{5,7},{6,4},{7,5},{8,10},{9,11},{10,... | collective-permute-start | bytes 3686408 | tf_op jit(solution)/shard_map/ppermute | solution.py:767
  513.5 40.8 %collective-permute-start.43 = (bf16[2,128,1280]{2,1,0:T(8,128)(2,1)S(1)}, bf16[2,128,1280]{2,1,0:T(8,128)(2,1)S(1)}, u32[]{:S(2)}, u32[]{:S(2)}) collective-permute-start(bf16[2,128,1280]{2,1,0:T(8,128)(2,1)S(1)} %fusion.81), channel_id=1, source_target_pairs={{0,2},{1,3},{2,0},{3,1},{4,6},{5,7},{6,4},{7,5},{8,10},{9,11},{10,... | collective-permute-start | bytes 1966088 | tf_op jit(solution)/shard_map/ppermute | solution.py:767
  515.3 50.8 %collective-permute-start.50 = (f32[2,80]{1,0:T(2,128)S(1)}, f32[2,80]{1,0:T(2,128)S(1)}, u32[]{:S(2)}, u32[]{:S(2)}) collective-permute-start(f32[2,80]{1,0:T(2,128)S(1)} %fusion.93), channel_id=1, source_target_pairs={{0,2},{1,3},{2,0},{3,1},{4,6},{5,7},{6,4},{7,5},{8,10},{9,11},{10,... | collective-permute-start | bytes 1928 | tf_op jit(solution)/shard_map/ppermute | solution.py:767
  (134 other events, 1435.9 us)
Sparse Core Ops, SparseCore 0:
  15.6 53.4 all-gather.6
  92.5 30.8 all-gather.8
  139.1 30.1 all-gather.10
  365.4 49.2 reduce-scatter.4
  470.1 28.6 reduce-scatter.6
  501.1 50.8 reduce-scatter.8
  557.9 28.4 reduce-scatter.10

commit v13 on v11

--- a/solution.py
+++ b/solution.py
@@ -424,13 +424,13 @@
             pl.BlockSpec((1, 1, length), lambda h: (h, 0, 0)),
         ],
         out_shape=[
-            pltpu.HBM((owners, local_heads, head_dim, tokens), BF16),
-            pltpu.HBM((local_heads, 1, length), F32),
+            jax.ShapeDtypeStruct((owners, local_heads, head_dim, tokens), BF16),
+            jax.ShapeDtypeStruct((local_heads, 1, length), F32),
         ],
         compiler_params=KERNEL,
         cost_estimate=LIGHT,
     )(
-        *in_hbm(projected.reshape(3, local_heads, head_dim, length)),
+        projected.reshape(3, local_heads, head_dim, length),
         scale_vec.reshape(head_dim, 1),
         segments.reshape(length, 1),
         segments.reshape(1, length),
@@ -622,10 +622,10 @@
             in_specs=specs,
             out_specs=pl.BlockSpec((1, 2, 2, 2, own, columns), lambda i, at: (i, 0, 0, 0, 0, 0)),
         ),
-        out_shape=pltpu.HBM((batch, 2, 2, 2, own, columns), BF16),
+        out_shape=jax.ShapeDtypeStruct((batch, 2, 2, 2, own, columns), BF16),
         compiler_params=KERNEL,
         cost_estimate=LIGHT,
-    )(place(), *in_hbm(*pieces))
+    )(place(), *pieces)
     return whole.reshape(-1, columns)
 
 
@@ -749,6 +749,68 @@
     )(place(), *in_hbm(bars, weight, normed))
 
 
+def rows_back_kernel(place_ref, bars_ref, weight_ref, own_ref, other_ref, bars_t):
+    @pl.when(pl.program_id(0) == 0)
+    def _():
+        bars_t[...] = bars_ref[...].astype(F32).T.astype(BF16)
+
+    upper = lax.dot_general(bars_t[...], weight_ref[...], NT, preferred_element_type=F32)
+    upper = upper.reshape(2, 2, 2, -1, upper.shape[-1])
+    first_core = place_ref[2] == 0
+    one, two = upper[:, :, 0], upper[:, :, 1]
+    own_ref[...] = jnp.where(first_core, one, two)
+    other_ref[...] = jnp.where(first_core, two, one).astype(BF16)
+
+
+def rows_back(bars, weight, token_rows):
+    columns, length = bars.shape
+    width = weight.shape[0]
+    tile = width // 2
+    quarter = pl.BlockSpec((2, 2, token_rows, tile), lambda i, at: (0, 0, 0, i))
+    return pl.pallas_call(
+        rows_back_kernel,
+        grid_spec=pltpu.PrefetchScalarGridSpec(
+            num_scalar_prefetch=1,
+            grid=(2,),
+            in_specs=[
+                pl.BlockSpec((columns, length), lambda i, at: (0, 0)),
+                pl.BlockSpec((tile, columns), lambda i, at: (i, 0)),
+            ],
+            out_specs=[quarter, quarter],
+            scratch_shapes=[pltpu.VMEM((length, columns), BF16)],
+        ),
+        out_shape=[
+            pltpu.HBM((2, 2, token_rows, width), F32),
+            pltpu.HBM((2, 2, token_rows, width), BF16),
+        ],
+        compiler_params=KERNEL,
+        cost_estimate=LIGHT,
+    )(place(), *in_hbm(bars, weight))
+
+
+def weight_back_kernel(bars_ref, normed_ref, grad_ref):
+    grad = jnp.dot(bars_ref[...], normed_ref[...], preferred_element_type=F32)
+    grad_ref[...] = grad.T.astype(BF16)
+
+
+def weight_back(bars, normed):
+    columns, length = bars.shape
+    width = normed.shape[1]
+    tile = width // 5
+    return pl.pallas_call(
+        weight_back_kernel,
+        grid=(5,),
+        in_specs=[
+            pl.BlockSpec((columns, length), lambda i: (0, 0)),
+            pl.BlockSpec((length, tile), lambda i: (0, i)),
+        ],
+        out_specs=pl.BlockSpec((tile, columns), lambda i: (i, 0)),
+        out_shape=pltpu.HBM((width, columns), BF16),
+        compiler_params=KERNEL,
+        cost_estimate=LIGHT,
+    )(*in_hbm(bars, normed))
+
+
 def tied(*arrays):
     return lax.optimization_barrier(arrays)
 
@@ -843,6 +905,10 @@
 
 def sent_beside_and_across(across, beside):
     return swapped(across, "blk", 1), swapped(beside, "head", 2)
+
+
+def heads_grad(weight, out_bar):
+    return dot_cols(weight, out_bar).astype(BF16).reshape(4, -1, out_bar.shape[0])
 
 
 def own_sum(cored, across, beside):
@@ -889,29 +955,20 @@
     ]
 
     first = swap_halves(tokens).reshape(-1, width)
-    upper = swap_halves(cotangent).reshape(-1, width)
-    dense_near = along_batch(dense_own[0])
     columns = qkv_columns(qkv_weight[0], own_gains.T)
-    columns, first, upper = tied(columns.reshape(-1, columns.shape[-1]), first, upper)
-    stream, upper = first.astype(F32), upper.astype(F32)
+    columns, first = tied(columns.reshape(-1, columns.shape[-1]), first)
+    stream = first.astype(F32)
+    along = along_batch(columns)
     far, near = swapped(first, "head", 2), other_core(first)
     both = other_core(far)
-    columns, dense_near, near, far, both = tied(columns, dense_near, near, far, both)
+    along, near, far, both, dense_near = tied(along, near, far, both, dense_own[0])
     token_pieces = (first, near, far, both)
+    dense_near = along_batch(dense_near)
+    qkv_across = swapped(along, "blk", 1)
+    next_columns = qkv_columns(qkv_weight[1], None).reshape(-1, part3)
+    qkv_across, dense_near, next_columns = tied(qkv_across, dense_near, next_columns)
     across, beside = swapped(dense_near, "blk", 1), swapped(dense_near, "head", 2)
-    along = along_batch(columns)
-    next_columns = qkv_columns(qkv_weight[1], None).reshape(-1, part3)
-    along, across, beside, next_columns = tied(along, across, beside, next_columns)
-    qkv_across = swapped(along, "blk", 1)
-    one = to_beside(across)
     next_along = along_batch(next_columns)
-    qkv_across, one, beside, next_along, dense_next = tied(
-        qkv_across, one, beside, next_along, dense_own[1]
-    )
-    two, next_along = tied(to_across(beside), next_along)
-    next_across = swapped(next_along, "blk", 1)
-    pieces = [(dense_near, across, beside, one, two)]
-    dense_next = along_batch(dense_next)
     weight, gains = assemble_columns(along, qkv_across, part3)
     qkvs = [weight]
     gains = gains.T.astype(F32)
@@ -920,12 +977,12 @@
     for layer in range(layers):
         normed, factor_one = normalize(stream, gains[layer])
         if layer == 1:
-            normed, beside = tied(normed.astype(BF16), beside)
+            normed, next_across, dense_next = tied(normed.astype(BF16), next_across, dense_next)
             far, near = swapped(normed, "head", 2), other_core(normed)
-            far, near, across, beside = tied(far, near, across, beside)
+            across = swapped(dense_next, "blk", 1)
+            far, dense_after = tied(far, dense_next)
+            beside = swapped(dense_after, "head", 2)
             token_pieces = (normed, near, far, other_core(far))
-            one, two = to_beside(across), to_across(beside)
-            pieces.append((dense_next, across, beside, one, two))
             qkvs.append(assemble_columns(next_along, next_across, part3)[0])
         normed_all, projected = project(
             token_pieces, gains[layer], qkvs[layer], layer == 0, token_rows
@@ -933,20 +990,21 @@
         attended, log_total = attend_rows(
             projected, scale_vecs[layer], segments, 4, token_rows
         )
-        attended, one, two = tied(attended, *pieces[layer][3:])
-        pieces[layer] = pieces[layer][:3] + (one, two)
-        swaps = tuple(other_core(piece) for piece in pieces[layer])
+        attended, across, beside = tied(attended, across, beside)
+        one, two = to_beside(across), to_across(beside)
         if layer == 0:
-            attended, dense_next = tied(attended, dense_next)
-            beside = swapped(dense_next, "head", 2)
-            attended_t, swaps, next_across, dense_next = tied(
-                over_head(attended), swaps, next_across, dense_next
-            )
-            across = swapped(dense_next, "blk", 1)
+            next_along, dense_next = tied(next_along, dense_own[1])
+            dense_next = along_batch(dense_next)
+            attended_t, one, two, next_along = tied(over_head(attended), one, two, next_along)
+            next_across = swapped(next_along, "blk", 1)
         else:
-            attended_t, swaps = tied(over_head(attended), swaps)
+            dense_near = dense_next
+            attended_t, one, two, cotangent = tied(over_head(attended), one, two, cotangent)
+            upper = swap_halves(cotangent)
+        pieces = (dense_near, across, beside, one, two)
+        pieces += tuple(other_core(piece) for piece in pieces)
         attended_t = attended_t.reshape(width, -1)
-        denses.append(assemble(pieces[layer] + swaps))
+        denses.append(assemble(pieces))
         dense = denses[layer]
         out_w, up_w, down_w = dense[:, :width], dense[:, width:-width], dense[:, -width:]
         middle = stream + dot_rows(attended_t, out_w)
@@ -962,6 +1020,7 @@
         )
         stream = middle + dot(active, down_w)
     layer_out = swap_halves(stream.astype(BF16).reshape(tokens.shape))
+    upper = upper.reshape(-1, width).astype(F32)
 
     scale_grads = [None] * layers
     for layer in reversed(range(layers)):
@@ -981,45 +1040,56 @@
         )
         out_bar = middle_grad.astype(BF16)
         if layer == 0:
-            out_bar, diagonal = tied(out_bar, diagonal)
-            out_bar, rows = tied(out_bar, neighbour_rows(cored, *diagonal))
-            sent = sent_beside_and_across(*rows)
-        attended_grad = over_head(dot_cols(out_w, out_bar).astype(BF16).reshape(4, -1, out_bar.shape[0]))
-        grads, others = dense_grads(attended_t, normed_two, active, out_bar, up_bar, down_bar)
-        if layer == 0:
-            attended_grad, others, z_sum = tied(attended_grad, others, z_sum)
+            attended_grad = over_head(heads_grad(out_w, out_bar))
+            grads, others = dense_grads(attended_t, normed_two, active, out_bar, up_bar, down_bar)
+            attended_grad, others, z_sum, across, beside = tied(
+                attended_grad, others, z_sum, across, beside
+            )
+            others = other_core(others)
+            attended_grad, summed = tied(attended_grad, own_sum(cored, across, beside))
+            summed = over_batch(summed)
             z_across = across_sum(z_sum)
         else:
+            attended_grad = over_head(heads_grad(out_w, out_bar))
+            grads, others = dense_grads(attended_t, normed_two, active, out_bar, up_bar, down_bar)
             attended_grad, others, layer_out = tied(attended_grad, others, layer_out)
-        others = other_core(others)
+            others = other_core(others)
         bars, scale_grads[layer] = attend_back_rows(
             projected, attended_grad, log_total, scale_vecs[layer], segments, token_rows
         )
         if layer == 0:
-            bars, others, sent = tied(bars, others, sent)
-            summed = own_sum(cored, *sent)
+            bars, others = tied(bars, others)
+            qkv_grad = weight_back(bars, normed_all)
+            bars, qkv_grad = tied(bars, qkv_grad)
+            z_sum = over_batch(qkv_grad.reshape(4, 2, -1, qkv_grad.shape[-1]))
+            cored = (grads.astype(F32) + others.astype(F32)).astype(BF16)
+            bars, rows = tied(bars, diagonal_rows(cored))
+            diagonal = sent_beside_and_across(*rows)
+            halves, to_core = rows_back(bars, qkv, token_rows)
+            halves, to_core, diagonal, summed = tied(halves, to_core, diagonal, summed)
+            halves, to_core, rows = tied(halves, to_core, neighbour_rows(cored, *diagonal))
+            sent = sent_beside_and_across(*rows)
+            halves = halves + other_core(to_core).astype(F32)
+            halves, sent = tied(halves, sent)
+            dense_first = over_batch(own_sum(cored, *sent))
+            normed_grad = scatter_row(halves)
+            normed_grad, z_sum, z_across = tied(normed_grad, z_sum, z_across)
+            dense_grad = [dense_first, summed]
+            qkv_grads = [columns_to_rows(across_sum(z_sum)), columns_to_rows(z_across)]
         else:
             bars, others = tied(bars, others)
-        cored = (grads.astype(F32) + others.astype(F32)).astype(BF16)
-        if layer == 0:
-            bars, summed, rows = tied(bars, summed, diagonal_rows(cored))
+            cored = (grads.astype(F32) + others.astype(F32)).astype(BF16)
+            bars, rows = tied(bars, diagonal_rows(cored))
             diagonal = sent_beside_and_across(*rows)
-            summed = over_batch(summed)
-        halves, to_core, qkv_grad = project_back(bars, qkv, normed_all, token_rows)
-        halves = halves + other_core(to_core).astype(F32)
-        z_sum = over_batch(qkv_grad.reshape(4, 2, -1, qkv_grad.shape[-1]))
-        if layer == 0:
-            halves, diagonal = tied(halves, diagonal)
-            halves, rows = tied(halves, neighbour_rows(cored, *diagonal))
-            sent = sent_beside_and_across(*rows)
+            halves, to_core, qkv_grad = project_back(bars, qkv, normed_all, token_rows)
+            z_sum = over_batch(qkv_grad.reshape(4, 2, -1, qkv_grad.shape[-1]))
+            to_core, halves, diagonal = tied(to_core, halves, diagonal)
+            to_core, rows = tied(to_core, neighbour_rows(cored, *diagonal))
+            across = swapped(rows[0], "blk", 1)
+            halves = halves + other_core(to_core).astype(F32)
             normed_grad = scatter_row(halves)
-            normed_grad, sent, summed, z_across = tied(normed_grad, sent, summed, z_across)
-            dense_grad = [over_batch(own_sum(cored, *sent)), summed]
-            qkv_grads = [columns_to_rows(across_sum(z_sum)), columns_to_rows(z_across)]
-        else:
-            normed_grad = scatter_row(halves)
-            normed_grad, cored = tied(normed_grad, cored)
-            diagonal = sent_beside_and_across(*diagonal_rows(cored))
+            normed_grad, beside = tied(normed_grad, rows[1])
+            beside = swapped(beside, "head", 2)
         upper = middle_grad + lower_of(normed_grad, stream, factor_one, gains[layer])
     input_grad = swap_halves(upper.astype(BF16).reshape(tokens.shape)).astype(F32)
     scale_total = sum_all(jnp.stack(scale_grads))

time: 583 us -> 598 us (1.026)
  waiting for transfers between devices: 223 us -> 274 us
  blocking collectives: 28 us -> 0 us
  Pallas kernels: 132 us -> 124 us
    reduce_scatter x4, waiting for transfers between devices: 0.06 us -> 57.4 us  [over_batch(): lax.psum_scatter(parts.astype(BF16), 'batch', scatter_dimension=0, tiled=...]
    ppermute x51, waiting for transfers between devices: 193 us -> 145 us  [swapped(): return lax.ppermute(array, axis, [(i, i ^ mask) for i in range(size)])]
    all_to_all x7 -> x8, waiting for transfers between devices: 23.5 us -> 55.9 us  [over_head(): lax.all_to_all(parts, 'head', split_axis=0, concat_axis=0, tiled=True)]
    all_to_all x1 -> x0, blocking collectives: 28 us -> none  [over_head(): lax.all_to_all(parts, 'head', split_axis=0, concat_axis=0, tiled=True)]
    pallas_call x0 -> x2, Pallas kernels: none -> 15.7 us  [the longest x1 8.26 us: rows_back(): pl.pallas_call(rows_back_kernel, grid_spec=pltpu.PrefetchScalarGridSpec(n...]
    pallas_call x2 -> x1, Pallas kernels: 23.6 us -> 11.3 us  [project_back(): pl.pallas_call(project_back_kernel, grid_spec=pltpu.PrefetchScalarGridSpe...]
    all_gather x4, waiting for transfers between devices: 5.91 us -> 15.6 us  [along_batch(): return lax.all_gather(piece, 'batch', axis=0, tiled=False)]
    pallas_call x2, Pallas kernels: 16.5 us -> 8.57 us  [assemble(): pl.pallas_call(assemble_kernel, grid_spec=pltpu.PrefetchScalarGridSpec(nu...]
  transfers between devices with their start and end apart: 66 -> 67, of which waited for: 29 -> 36; matrix products, arithmetic and copies ran while one was open for 12% -> 11% of each run, Pallas kernels for 19% -> 20%
where the time goes in v13:
time: 598 us; the launch traced here: 590 us
  waiting for transfers between devices  274 us (46%)
  Pallas kernels  124 us (21%)
  starting transfers between devices  73.3 us (12%)
  other arithmetic  43 us (7%)
  local copies, waits for them, and re-layouts  38 us (6%)
  matrix products  21.5 us (4%)
  between operations  16.1 us (3%)
    ppermute x51, waiting for transfers between devices, swapped(): return lax.ppermute(array, axis, [(i, i ^ mask) for i in range(size)])  145 us
    reduce_scatter x4, waiting for transfers between devices, over_batch(): lax.psum_scatter(parts.astype(BF16), 'batch', scatter_dimension=0, tiled=...  57.4 us
    all_to_all x8, waiting for transfers between devices, over_head(): lax.all_to_all(parts, 'head', split_axis=0, concat_axis=0, tiled=True)  55.9 us
    ppermute x51, starting transfers between devices, swapped(): return lax.ppermute(array, axis, [(i, i ^ mask) for i in range(size)])  42.4 us
    all_to_all x8, starting transfers between devices, over_head(): lax.all_to_all(parts, 'head', split_axis=0, concat_axis=0, tiled=True)  30 us
    pallas_call x2, Pallas kernels, attend_back_rows(): pl.pallas_call(functools.partial(attend_back_kernel, token_rows), grid=(l...  25 us
    pallas_call x2, Pallas kernels, dense_grads(): pl.pallas_call(dense_grad_kernel, grid_spec=pltpu.PrefetchScalarGridSpec(...  19.8 us
    pallas_call x2, Pallas kernels, attend_rows(): pl.pallas_call(functools.partial(attend_kernel, token_rows), grid=(local_...  17.9 us
  transfers between devices with their start and end apart: 67, of which 36 were waited for; matrix products, arithmetic and copies ran while one was open for 11% of the time, Pallas kernels for 20%

profile of v13, /device:TPU:0, one launch (start us, length us, event | category | flops | bytes accessed | tf_op | source)
XLA Modules:
  0.0 590.3 jit_solution(17024141739028176829)
XLA Ops:
  19.1 5.4 all-to-all-done
  26.3 15.2 %collective-permute-done.2.refs_2_ = bf16[256,1280]{1,0:T(8,128)(2,1)S(1)} collective-permute-done((bf16[256,1280]{1,0:T(8,128)(2,1)S(1)}, bf16[256,1280]{1,0:T(8,128)(2,1)S(1)}, u32[]{:S(2)}, u32[]{:S(2)}) %collective-permute-start.2) | collective-permute-done | bytes 655392 | tf_op jit(solution)/shard_map/ppermute | solution.py:820
  44.1 13.3 %all-gather.9.cloned.1.call-done = bf16[640,964]{1,0:T(8,128)(2,1)} async-done(((bf16[160,964]{1,0:T(8,128)(2,1)}), bf16[640,964]{1,0:T(8,128)(2,1)}) %all-gather.9.cloned.1.call-update) | async-done | bytes 1233936 | tf_op jit(solution)/shard_map/all_gather | solution.py:854
  64.2 6.6 %all-to-all-done.1 = bf16[4,40,960]{2,1,0:T(8,128)(2,1)S(1)} async-done(((bf16[4,40,960]{2,1,0:T(8,128)(2,1)}), bf16[4,40,960]{2,1,0:T(8,128)(2,1)S(1)}, u32[]{:S(2)}, u32[]{:S(2)}) %all-to-all-start.1) | async-done | bytes 307232 | tf_op jit(solution)/shard_map/all_to_all | solution.py:841
  70.8 16.7 %collective-permute-done.4.across_ref = bf16[4,160,964]{2,1,0:T(8,128)(2,1)S(1)} collective-permute-done((bf16[4,160,964]{2,1,0:T(8,128)(2,1)}, bf16[4,160,964]{2,1,0:T(8,128)(2,1)S(1)}, u32[]{:S(2)}, u32[]{:S(2)}) %collective-permute-start.4) | collective-permute-done | bytes 1233952 | tf_op jit(solution)/shard_map/ppermute | solution.py:820
  93.3 4.6 shard_map.169
  101.2 8.8 %shard_map.170 = (bf16[1024,1280]{1,0:T(8,128)(2,1)}, f32[960,1024]{1,0:T(8,128)}) custom-call(s32[3]{0:T(128)S(1)} %pad_add_fusion.place_ref.core_ref, bf16[256,1280]{1,0:T(8,128)(2,1)} %bitcast.216, bf16[256,1280]{1,0:T(8,128)(2,1)} %copy-done.57, bf16[256,1280]{1,0:T(8,128)(2,1)} %copy-done.56, bf16[256,1280]{1,0:T(8,128)(2,1)} %collective-permute-done.3.refs_3_, ...), custom_call_target="tpu_custom_call" | custom-call | flops 1048576 | bytes 1048576 | tf_op jit(solution)/shard_map/pallas_call | solution.py:683
  112.2 8.9 %shard_map.171 = (bf16[4,4,80,256]{3,2,1,0:T(8,128)(2,1)S(1)}, f32[4,1,1024]{2,1,0:T(1,128)S(1)}) custom-call(f32[3,4,80,1024]{3,2,1,0:T(8,128)S(1)} %bitcast.180, f32[80,1]{1,0:T(8,128)S(1)} %copy.41.scale_ref, s32[1024,1]{1,0:T(8,128)S(1)} %copy.42.col_ref, s32[1,1024]{1,0:T(1,128)S(1)} %constant_dynamic-slice_fusion.row_ref), custom_call_target="tpu_custom_call" | custom-call | flops 1048576 | bytes 1048576 | tf_op jit(solution)/shard_map/pallas_call | solution.py:413
  130.1 15.0 %all-to-all-done.2 = bf16[4,320,256]{2,1,0:T(8,128)(2,1)} async-done(((bf16[4,320,256]{2,1,0:T(8,128)(2,1)}), bf16[4,320,256]{2,1,0:T(8,128)(2,1)}, u32[]{:S(2)}, u32[]{:S(2)}) %all-to-all-start.2) | async-done | bytes 655392 | tf_op jit(solution)/shard_map/all_to_all | solution.py:841
  148.3 4.6 shard_map.172
  159.4 17.3 %collective-permute-done.14.across_ref = bf16[4,160,960]{2,1,0:T(8,128)(2,1)} collective-permute-done((bf16[4,160,960]{2,1,0:T(8,128)(2,1)}, bf16[4,160,960]{2,1,0:T(8,128)(2,1)}, u32[]{:S(2)}, u32[]{:S(2)}) %collective-permute-start.14) | collective-permute-done | bytes 1228832 | tf_op jit(solution)/shard_map/ppermute | solution.py:820
  179.0 13.7 %collective-permute-done.16.refs_2_ = bf16[256,1280]{1,0:T(8,128)(2,1)} collective-permute-done((bf16[256,1280]{1,0:T(8,128)(2,1)S(1)}, bf16[256,1280]{1,0:T(8,128)(2,1)}, u32[]{:S(2)}, u32[]{:S(2)}) %collective-permute-start.16) | collective-permute-done | bytes 655392 | tf_op jit(solution)/shard_map/ppermute | solution.py:820
  194.1 4.6 shard_map.173
  198.7 7.8 %shard_map.174 = (bf16[1024,1280]{1,0:T(8,128)(2,1)}, f32[960,1024]{1,0:T(8,128)}) custom-call(s32[3]{0:T(128)S(1)} %pad_add_fusion.place_ref.core_ref, bf16[256,1280]{1,0:T(8,128)(2,1)} %copy-done.35, bf16[256,1280]{1,0:T(8,128)(2,1)} %collective-permute-done.15.refs_1_, bf16[256,1280]{1,0:T(8,128)(2,1)} %collective-permute-done.16.refs_2_, ...), custom_call_target="tpu_custom_call" | custom-call | flops 1048576 | bytes 1048576 | tf_op jit(solution)/shard_map/pallas_call | solution.py:683
  208.5 9.0 %shard_map.175 = (bf16[4,4,80,256]{3,2,1,0:T(8,128)(2,1)S(1)}, f32[4,1,1024]{2,1,0:T(1,128)S(1)}) custom-call(f32[3,4,80,1024]{3,2,1,0:T(8,128)S(1)} %bitcast.182, f32[80,1]{1,0:T(8,128)S(1)} %copy.43.scale_ref, s32[1024,1]{1,0:T(8,128)S(1)} %copy.42.col_ref, s32[1,1024]{1,0:T(1,128)S(1)} %constant_dynamic-slice_fusion.row_ref), custom_call_target="tpu_custom_call" | custom-call | flops 1048576 | bytes 1048576 | tf_op jit(solution)/shard_map/pallas_call | solution.py:413
  224.2 4.3 all-to-all-start.3
  229.6 14.1 %all-to-all-done.3 = bf16[4,320,256]{2,1,0:T(8,128)(2,1)} async-done(((bf16[4,320,256]{2,1,0:T(8,128)(2,1)}), bf16[4,320,256]{2,1,0:T(8,128)(2,1)}, u32[]{:S(2)}, u32[]{:S(2)}) %all-to-all-start.3) | async-done | bytes 655392 | tf_op jit(solution)/shard_map/all_to_all | solution.py:841
  245.3 7.1 %collective-permute-done.27 = bf16[128,1280]{1,0:T(8,128)(2,1)S(1)} collective-permute-done((bf16[128,1280]{1,0:T(8,128)(2,1)S(1)}, bf16[128,1280]{1,0:T(8,128)(2,1)S(1)}, u32[]{:S(2)}, u32[]{:S(2)}) %collective-permute-start.27) | collective-permute-done | bytes 327712 | tf_op jit(solution)/shard_map/ppermute | solution.py:820
  273.0 9.9 %shard_map.177 = (bf16[2,2,4,40,3840]{4,3,2,1,0:T(8,128)(2,1)}, bf16[2,2,4,40,3840]{4,3,2,1,0:T(8,128)(2,1)}) custom-call(s32[3]{0:T(128)S(1)} %pad_add_fusion.place_ref.core_ref, bf16[1280,256]{1,0:T(8,128)(2,1)} %bitcast.43.attended_ref, bf16[256,1280]{1,0:T(8,128)(2,1)} %copy-done.33, bf16[256,1280]{1,0:T(8,128)(2,1)} %copy-done.54, ...), custom_call_target="tpu_custom_call" | custom-call | flops 1048576 | bytes 1048576 | tf_op jit(solution)/shard_map/pallas_call | solution.py:577
  284.7 12.4 %shard_map.178 = (bf16[3,4,80,1024]{3,2,1,0:T(8,128)(2,1)}, f32[80,128]{1,0:T(8,128)}) custom-call(f32[3,4,80,1024]{3,2,1,0:T(8,128)} %bitcast.181, bf16[4,4,80,256]{3,2,1,0:T(8,128)(2,1)} %bitcast.225, f32[4,1,1024]{2,1,0:T(1,128)S(1)} %get-tuple-element.149.lse_ref, f32[80,1]{1,0:T(8,128)S(1)} %copy.43.scale_ref, s32[1024,1]{1,0:T(8,128)S(1)} %copy.42.col_ref, ...), custom_call_target="tpu_custom_call" | custom-call | flops 1048576 | bytes 1048576 | tf_op jit(solution)/shard_map/pallas_call | solution.py:506
  306.8 11.3 %shard_map.179 = (f32[2,2,128,1280]{3,2,1,0:T(8,128)}, bf16[2,2,128,1280]{3,2,1,0:T(8,128)(2,1)}, bf16[1280,960]{1,0:T(8,128)(2,1)}) custom-call(s32[3]{0:T(128)S(1)} %pad_add_fusion.place_ref.core_ref, bf16[960,1024]{1,0:T(8,128)(2,1)} %bitcast.227, bf16[1280,960]{1,0:T(8,128)(2,1)} %bitcast.204, bf16[1024,1280]{1,0:T(8,128)(2,1)} %get-tuple-element.156.normed_ref), custom_call_target="tpu_custom_call" | custom-call | flops 1048576 | bytes 1048576 | tf_op jit(solution)/shard_map/pallas_call | solution.py:729
  331.3 14.5 %collective-permute-done.33 = bf16[2,128,1280]{2,1,0:T(8,128)(2,1)} collective-permute-done((bf16[2,128,1280]{2,1,0:T(8,128)(2,1)S(1)}, bf16[2,128,1280]{2,1,0:T(8,128)(2,1)}, u32[]{:S(2)}, u32[]{:S(2)}) %collective-permute-start.33) | collective-permute-done | bytes 655392 | tf_op jit(solution)/shard_map/ppermute | solution.py:820
  363.6 9.9 %shard_map.180 = (bf16[2,2,4,40,3840]{4,3,2,1,0:T(8,128)(2,1)}, bf16[2,2,4,40,3840]{4,3,2,1,0:T(8,128)(2,1)}) custom-call(s32[3]{0:T(128)S(1)} %pad_add_fusion.place_ref.core_ref, bf16[1280,256]{1,0:T(8,128)(2,1)} %bitcast.29.attended_ref, bf16[256,1280]{1,0:T(8,128)(2,1)} %copy-done.30, bf16[256,1280]{1,0:T(8,128)(2,1)} %copy-done.50, ...), custom_call_target="tpu_custom_call" | custom-call | flops 1048576 | bytes 1048576 | tf_op jit(solution)/shard_map/pallas_call | solution.py:577
  373.5 9.5 %all-to-all-done.5 = bf16[4,320,256]{2,1,0:T(8,128)(2,1)S(1)} async-done(((bf16[4,320,256]{2,1,0:T(8,128)(2,1)}), bf16[4,320,256]{2,1,0:T(8,128)(2,1)S(1)}, u32[]{:S(2)}, u32[]{:S(2)}) %all-to-all-start.5) | async-done | bytes 655392 | tf_op jit(solution)/shard_map/all_to_all | solution.py:841
  386.9 12.6 %shard_map.181 = (bf16[3,4,80,1024]{3,2,1,0:T(8,128)(2,1)}, f32[80,128]{1,0:T(8,128)}) custom-call(f32[3,4,80,1024]{3,2,1,0:T(8,128)} %bitcast.179, bf16[4,4,80,256]{3,2,1,0:T(8,128)(2,1)} %bitcast.226, f32[4,1,1024]{2,1,0:T(1,128)S(1)} %get-tuple-element.176.lse_ref, f32[80,1]{1,0:T(8,128)S(1)} %copy.41.scale_ref, s32[1024,1]{1,0:T(8,128)S(1)} %copy.42.col_ref, ...), custom_call_target="tpu_custom_call" | custom-call | flops 1048576 | bytes 1048576 | tf_op jit(solution)/shard_map/pallas_call | solution.py:506
  399.5 7.5 %shard_map.182 = bf16[1280,960]{1,0:T(8,128)(2,1)} custom-call(bf16[960,1024]{1,0:T(8,128)(2,1)} %bitcast.220, bf16[1024,1280]{1,0:T(8,128)(2,1)} %get-tuple-element.180.normed_ref), custom_call_target="tpu_custom_call" | custom-call | flops 1048576 | bytes 1048576 | tf_op jit(solution)/shard_map/pallas_call | solution.py:800
  418.3 8.3 %shard_map.183 = (f32[2,2,128,1280]{3,2,1,0:T(8,128)}, bf16[2,2,128,1280]{3,2,1,0:T(8,128)(2,1)}) custom-call(s32[3]{0:T(128)S(1)} %pad_add_fusion.place_ref.core_ref, bf16[960,1024]{1,0:T(8,128)(2,1)} %bitcast.221, bf16[1280,960]{1,0:T(8,128)(2,1)} %bitcast.213), custom_call_target="tpu_custom_call" | custom-call | flops 1048576 | bytes 1048576 | tf_op jit(solution)/shard_map/pallas_call | solution.py:770
  438.5 26.1 %collective-permute-done.40 = bf16[4,40,3840]{2,1,0:T(8,128)(2,1)S(1)} collective-permute-done((bf16[4,40,3840]{2,1,0:T(8,128)(2,1)S(1)}, bf16[4,40,3840]{2,1,0:T(8,128)(2,1)S(1)}, u32[]{:S(2)}, u32[]{:S(2)}) %collective-permute-start.40) | collective-permute-done | bytes 1228832 | tf_op jit(solution)/shard_map/ppermute | solution.py:820
  475.6 4.4 collective-permute-done.48
  491.8 6.4 %reduce-scatter.11.cloned.1.call-done = bf16[1,40,3840]{2,1,0:T(8,128)(2,1)} async-done(((bf16[4,40,3840]{2,1,0:T(8,128)(2,1)}), bf16[1,40,3840]{2,1,0:T(8,128)(2,1)}) %reduce-scatter.11.cloned.1.call-update) | async-done | bytes 307216 | tf_op jit(solution)/shard_map/reduce_scatter | solution.py:870
  500.3 51.1 %reduce-scatter.9.cloned.1.call-done = bf16[1,2,160,960]{3,2,1,0:T(8,128)(2,1)} async-done(((bf16[4,2,160,960]{3,2,1,0:T(8,128)(2,1)}), bf16[1,2,160,960]{3,2,1,0:T(8,128)(2,1)}) %reduce-scatter.9.cloned.1.call-update) | async-done | bytes 614416 | tf_op jit(solution)/shard_map/reduce_scatter | solution.py:870
  576.1 4.3 all-to-all-done.6
  (404 shorter events, 209.1 us)
Async XLA Ops:
  17.7 39.7 %all-gather.9.cloned.1.call-start = ((), (), s32[]{:S(2)}) async-start(), calls=%async_computation.16 | async-start | bytes 1638400 | tf_op jit(solution)/shard_map/all_gather | solution.py:854
  25.2 64.7 %all-gather.11.cloned.1.call-start = ((), (), s32[]{:S(2)}) async-start(), calls=%async_computation.17 | async-start | bytes 1536000 | tf_op jit(solution)/shard_map/all_gather | solution.py:854
  57.4 30.1 %collective-permute-start.4 = (bf16[4,160,964]{2,1,0:T(8,128)(2,1)}, bf16[4,160,964]{2,1,0:T(8,128)(2,1)S(1)}, u32[]{:S(2)}, u32[]{:S(2)}) collective-permute-start(bf16[4,160,964]{2,1,0:T(8,128)(2,1)} %bitcast.235), channel_id=1, source_target_pairs={{0,4},{4,0},{1,5},{5,1},{2,6},{6,2},{3,7},{7,3},{8,12},{12,8},{9,1... | collective-permute-start | bytes 3701768 | tf_op jit(solution)/shard_map/ppermute | solution.py:820
  64.1 65.9 %all-gather.13.cloned.1.call-start = ((), (), s32[]{:S(2)}) async-start(), calls=%async_computation.18 | async-start | bytes 1638400 | tf_op jit(solution)/shard_map/all_gather | solution.py:854
  89.9 31.3 %collective-permute-start.6 = (bf16[4,40,3840]{2,1,0:T(8,128)(2,1)}, bf16[4,40,3840]{2,1,0:T(8,128)(2,1)S(1)}, u32[]{:S(2)}, u32[]{:S(2)}) collective-permute-start(bf16[4,40,3840]{2,1,0:T(8,128)(2,1)} %bitcast.15.refs_0_), channel_id=1, source_target_pairs={{0,2},{1,3},{2,0},{3,1},{4,6},{5,7},{6,4},{7,5},{8,10},{9,11},{10,... | collective-permute-start | bytes 3686408 | tf_op jit(solution)/shard_map/ppermute | solution.py:820
  91.3 29.8 %collective-permute-start.5 = (bf16[4,40,3840]{2,1,0:T(8,128)(2,1)}, bf16[4,40,3840]{2,1,0:T(8,128)(2,1)S(1)}, u32[]{:S(2)}, u32[]{:S(2)}) collective-permute-start(bf16[4,40,3840]{2,1,0:T(8,128)(2,1)} %bitcast.15.refs_0_), channel_id=1, source_target_pairs={{0,4},{4,0},{1,5},{5,1},{2,6},{6,2},{3,7},{7,3},{8,12},{12,8},{9,1... | collective-permute-start | bytes 3686408 | tf_op jit(solution)/shard_map/ppermute | solution.py:820
  123.0 22.1 %collective-permute-start.8 = (bf16[4,40,1920]{2,1,0:T(8,128)(2,1)}, bf16[4,40,1920]{2,1,0:T(8,128)(2,1)}, u32[]{:S(2)}, u32[]{:S(2)}) collective-permute-start(bf16[4,40,1920]{2,1,0:T(8,128)(2,1)} %slice.144), channel_id=1, source_target_pairs={{0,4},{4,0},{1,5},{5,1},{2,6},{6,2},{3,7},{7,3},{8,12},{12,8},{9,1... | collective-permute-start | bytes 1843208 | tf_op jit(solution)/shard_map/ppermute | solution.py:820
  123.5 21.5 %collective-permute-start.7 = (bf16[4,40,1920]{2,1,0:T(8,128)(2,1)}, bf16[4,40,1920]{2,1,0:T(8,128)(2,1)}, u32[]{:S(2)}, u32[]{:S(2)}) collective-permute-start(bf16[4,40,1920]{2,1,0:T(8,128)(2,1)} %slice.143), channel_id=1, source_target_pairs={{0,2},{1,3},{2,0},{3,1},{4,6},{5,7},{6,4},{7,5},{8,10},{9,11},{10,... | collective-permute-start | bytes 1843208 | tf_op jit(solution)/shard_map/ppermute | solution.py:820
  124.1 21.5 %collective-permute-start.9 = (bf16[4,40,3840]{2,1,0:T(8,128)(2,1)}, bf16[4,40,3840]{2,1,0:T(8,128)(2,1)}, u32[]{:S(2)}, u32[]{:S(2)}) collective-permute-start(bf16[4,40,3840]{2,1,0:T(8,128)(2,1)} %bitcast.15.refs_0_), channel_id=1, source_target_pairs={{0,1},{1,0},{2,3},{3,2},{4,5},{5,4},{6,7},{7,6},{8,9},{9,8},{10,11... | collective-permute-start | bytes 3686408 | tf_op jit(solution)/shard_map/ppermute | solution.py:820
  124.1 24.2 %collective-permute-start.10 = (bf16[4,40,3840]{2,1,0:T(8,128)(2,1)S(1)}, bf16[4,40,3840]{2,1,0:T(8,128)(2,1)}, u32[]{:S(2)}, u32[]{:S(2)}) collective-permute-start(bf16[4,40,3840]{2,1,0:T(8,128)(2,1)S(1)} %collective-permute-done.5.refs_1_), channel_id=1, source_target_pairs={{0,1},{1,0},{2,3},{3,2},{4,5},{5,4},{6,7},{7,6},{8,9},{9,8},{10,11... | collective-permute-start | bytes 3686408 | tf_op jit(solution)/shard_map/ppermute | solution.py:820
  124.6 23.7 %collective-permute-start.11 = (bf16[4,40,3840]{2,1,0:T(8,128)(2,1)S(1)}, bf16[4,40,3840]{2,1,0:T(8,128)(2,1)}, u32[]{:S(2)}, u32[]{:S(2)}) collective-permute-start(bf16[4,40,3840]{2,1,0:T(8,128)(2,1)S(1)} %collective-permute-done.6.refs_2_), channel_id=1, source_target_pairs={{0,1},{1,0},{2,3},{3,2},{4,5},{5,4},{6,7},{7,6},{8,9},{9,8},{10,11... | collective-permute-start | bytes 3686408 | tf_op jit(solution)/shard_map/ppermute | solution.py:820
  124.6 20.4 %all-to-all-start.2 = ((bf16[4,320,256]{2,1,0:T(8,128)(2,1)}), bf16[4,320,256]{2,1,0:T(8,128)(2,1)}, u32[]{:S(2)}, u32[]{:S(2)}) async-start(bf16[4,320,256]{2,1,0:T(8,128)(2,1)} %bitcast.201), calls=%async_computation.2 | async-start | bytes 1310720 | tf_op jit(solution)/shard_map/all_to_all | solution.py:841
  128.8 48.0 %all-gather.15.cloned.1.call-start = ((), (), s32[]{:S(2)}) async-start(), calls=%async_computation.19 | async-start | bytes 1536000 | tf_op jit(solution)/shard_map/all_gather | solution.py:854
  145.6 31.1 %collective-permute-start.14 = (bf16[4,160,960]{2,1,0:T(8,128)(2,1)}, bf16[4,160,960]{2,1,0:T(8,128)(2,1)}, u32[]{:S(2)}, u32[]{:S(2)}) collective-permute-start(bf16[4,160,960]{2,1,0:T(8,128)(2,1)} %bitcast.237), channel_id=1, source_target_pairs={{0,4},{4,0},{1,5},{5,1},{2,6},{6,2},{3,7},{7,3},{8,12},{12,8},{9,1... | collective-permute-start | bytes 3686408 | tf_op jit(solution)/shard_map/ppermute | solution.py:820
  177.5 40.0 %collective-permute-start.18 = (bf16[4,40,3840]{2,1,0:T(8,128)(2,1)}, bf16[4,40,3840]{2,1,0:T(8,128)(2,1)S(1)}, u32[]{:S(2)}, u32[]{:S(2)}) collective-permute-start(bf16[4,40,3840]{2,1,0:T(8,128)(2,1)} %bitcast.197), channel_id=1, source_target_pairs={{0,4},{4,0},{1,5},{5,1},{2,6},{6,2},{3,7},{7,3},{8,12},{12,8},{9,1... | collective-permute-start | bytes 3686408 | tf_op jit(solution)/shard_map/ppermute | solution.py:820
  192.7 27.4 %collective-permute-start.19 = (bf16[4,40,3840]{2,1,0:T(8,128)(2,1)}, bf16[4,40,3840]{2,1,0:T(8,128)(2,1)S(1)}, u32[]{:S(2)}, u32[]{:S(2)}) collective-permute-start(bf16[4,40,3840]{2,1,0:T(8,128)(2,1)} %bitcast.198), channel_id=1, source_target_pairs={{0,2},{1,3},{2,0},{3,1},{4,6},{5,7},{6,4},{7,5},{8,10},{9,11},{10,... | collective-permute-start | bytes 3686408 | tf_op jit(solution)/shard_map/ppermute | solution.py:820
  221.9 21.7 %collective-permute-start.21 = (bf16[4,40,1920]{2,1,0:T(8,128)(2,1)}, bf16[4,40,1920]{2,1,0:T(8,128)(2,1)}, u32[]{:S(2)}, u32[]{:S(2)}) collective-permute-start(bf16[4,40,1920]{2,1,0:T(8,128)(2,1)} %slice.155), channel_id=1, source_target_pairs={{0,4},{4,0},{1,5},{5,1},{2,6},{6,2},{3,7},{7,3},{8,12},{12,8},{9,1... | collective-permute-start | bytes 1843208 | tf_op jit(solution)/shard_map/ppermute | solution.py:820
  223.4 20.3 %collective-permute-start.20 = (bf16[4,40,1920]{2,1,0:T(8,128)(2,1)}, bf16[4,40,1920]{2,1,0:T(8,128)(2,1)}, u32[]{:S(2)}, u32[]{:S(2)}) collective-permute-start(bf16[4,40,1920]{2,1,0:T(8,128)(2,1)} %slice.154), channel_id=1, source_target_pairs={{0,2},{1,3},{2,0},{3,1},{4,6},{5,7},{6,4},{7,5},{8,10},{9,11},{10,... | collective-permute-start | bytes 1843208 | tf_op jit(solution)/shard_map/ppermute | solution.py:820
  228.5 25.0 %collective-permute-start.22 = (bf16[4,40,3840]{2,1,0:T(8,128)(2,1)}, bf16[4,40,3840]{2,1,0:T(8,128)(2,1)}, u32[]{:S(2)}, u32[]{:S(2)}) collective-permute-start(bf16[4,40,3840]{2,1,0:T(8,128)(2,1)} %bitcast.199), channel_id=1, source_target_pairs={{0,1},{1,0},{2,3},{3,2},{4,5},{5,4},{6,7},{7,6},{8,9},{9,8},{10,11... | collective-permute-start | bytes 3686408 | tf_op jit(solution)/shard_map/ppermute | solution.py:820
  229.1 25.6 %collective-permute-start.23 = (bf16[4,40,3840]{2,1,0:T(8,128)(2,1)S(1)}, bf16[4,40,3840]{2,1,0:T(8,128)(2,1)}, u32[]{:S(2)}, u32[]{:S(2)}) collective-permute-start(bf16[4,40,3840]{2,1,0:T(8,128)(2,1)S(1)} %collective-permute-done.18.refs_1_), channel_id=1, source_target_pairs={{0,1},{1,0},{2,3},{3,2},{4,5},{5,4},{6,7},{7,6},{8,9},{9,8},{10,11... | collective-permute-start | bytes 3686408 | tf_op jit(solution)/shard_map/ppermute | solution.py:820
  229.1 25.5 %collective-permute-start.24 = (bf16[4,40,3840]{2,1,0:T(8,128)(2,1)S(1)}, bf16[4,40,3840]{2,1,0:T(8,128)(2,1)}, u32[]{:S(2)}, u32[]{:S(2)}) collective-permute-start(bf16[4,40,3840]{2,1,0:T(8,128)(2,1)S(1)} %collective-permute-done.19.refs_2_), channel_id=1, source_target_pairs={{0,1},{1,0},{2,3},{3,2},{4,5},{5,4},{6,7},{7,6},{8,9},{9,8},{10,11... | collective-permute-start | bytes 3686408 | tf_op jit(solution)/shard_map/ppermute | solution.py:820
  263.3 19.6 %collective-permute-start.28 = (bf16[128,1280]{1,0:T(8,128)(2,1)S(1)}, bf16[128,1280]{1,0:T(8,128)(2,1)S(1)}, u32[]{:S(2)}, u32[]{:S(2)}) collective-permute-start(bf16[128,1280]{1,0:T(8,128)(2,1)S(1)} %dynamic-slice_bitcast_fusion.9), channel_id=1, source_target_pairs={{0,4},{4,0},{1,5},{5,1},{2,6},{6,2},{3,7},{7,3},{8,12},{12,8},{9,1... | collective-permute-start | bytes 983048 | tf_op jit(solution)/shard_map/ppermute | solution.py:820
  272.8 110.3 %reduce-scatter.5.cloned.1.call-start = ((), (), s32[]{:S(2)}) async-start(), calls=%async_computation.12 | async-start | bytes 3276800 | tf_op jit(solution)/shard_map/reduce_scatter | solution.py:870
  330.7 42.9 %collective-permute-start.34 = (bf16[4,40,3840]{2,1,0:T(8,128)(2,1)}, bf16[4,40,3840]{2,1,0:T(8,128)(2,1)}, u32[]{:S(2)}, u32[]{:S(2)}) collective-permute-start(bf16[4,40,3840]{2,1,0:T(8,128)(2,1)} %pad_maximum_fusion), channel_id=1, source_target_pairs={{0,4},{4,0},{1,5},{5,1},{2,6},{6,2},{3,7},{7,3},{8,12},{12,8},{9,1... | collective-permute-start | bytes 3686408 | tf_op jit(solution)/shard_map/ppermute | solution.py:820
  347.5 35.5 %collective-permute-start.35 = (bf16[4,40,3840]{2,1,0:T(8,128)(2,1)}, bf16[4,40,3840]{2,1,0:T(8,128)(2,1)}, u32[]{:S(2)}, u32[]{:S(2)}) collective-permute-start(bf16[4,40,3840]{2,1,0:T(8,128)(2,1)} %pad_maximum_fusion.1), channel_id=1, source_target_pairs={{0,2},{1,3},{2,0},{3,1},{4,6},{5,7},{6,4},{7,5},{8,10},{9,11},{10,... | collective-permute-start | bytes 3686408 | tf_op jit(solution)/shard_map/ppermute | solution.py:820
  360.1 22.9 %all-to-all-start.5 = ((bf16[4,320,256]{2,1,0:T(8,128)(2,1)}), bf16[4,320,256]{2,1,0:T(8,128)(2,1)S(1)}, u32[]{:S(2)}, u32[]{:S(2)}) async-start(bf16[4,320,256]{2,1,0:T(8,128)(2,1)} %bitcast.58), calls=%async_computation.5 | async-start | bytes 1310720 | tf_op jit(solution)/shard_map/all_to_all | solution.py:841
  363.6 63.0 %reduce-scatter.7.cloned.1.call-start = ((), (), s32[]{:S(2)}) async-start(), calls=%async_computation.13 | async-start | bytes 1536000 | tf_op jit(solution)/shard_map/reduce_scatter | solution.py:870
  386.8 111.3 %reduce-scatter.11.cloned.1.call-start = ((), (), s32[]{:S(2)}) async-start(), calls=%async_computation.15 | async-start | bytes 1536000 | tf_op jit(solution)/shard_map/reduce_scatter | solution.py:870
  435.2 29.4 %collective-permute-start.40 = (bf16[4,40,3840]{2,1,0:T(8,128)(2,1)S(1)}, bf16[4,40,3840]{2,1,0:T(8,128)(2,1)S(1)}, u32[]{:S(2)}, u32[]{:S(2)}) collective-permute-start(bf16[4,40,3840]{2,1,0:T(8,128)(2,1)S(1)} %pad_maximum_fusion.2), channel_id=1, source_target_pairs={{0,4},{4,0},{1,5},{5,1},{2,6},{6,2},{3,7},{7,3},{8,12},{12,8},{9,1... | collective-permute-start | bytes 3686408 | tf_op jit(solution)/shard_map/ppermute | solution.py:820
  436.6 29.2 %collective-permute-start.41 = (bf16[4,40,3840]{2,1,0:T(8,128)(2,1)S(1)}, bf16[4,40,3840]{2,1,0:T(8,128)(2,1)S(1)}, u32[]{:S(2)}, u32[]{:S(2)}) collective-permute-start(bf16[4,40,3840]{2,1,0:T(8,128)(2,1)S(1)} %pad_maximum_fusion.3), channel_id=1, source_target_pairs={{0,2},{1,3},{2,0},{3,1},{4,6},{5,7},{6,4},{7,5},{8,10},{9,11},{10,... | collective-permute-start | bytes 3686408 | tf_op jit(solution)/shard_map/ppermute | solution.py:820
  468.6 82.8 %reduce-scatter.9.cloned.1.call-start = ((), (), s32[]{:S(2)}) async-start(), calls=%async_computation.14 | async-start | bytes 3276800 | tf_op jit(solution)/shard_map/reduce_scatter | solution.py:870
  469.8 19.6 %collective-permute-start.43 = (bf16[160,960]{1,0:T(8,128)(2,1)S(1)}, bf16[160,960]{1,0:T(8,128)(2,1)S(1)}, u32[]{:S(2)}, u32[]{:S(2)}) collective-permute-start(bf16[160,960]{1,0:T(8,128)(2,1)S(1)} %dynamic-slice_bitcast_fusion.8), channel_id=1, source_target_pairs={{0,4},{4,0},{1,5},{5,1},{2,6},{6,2},{3,7},{7,3},{8,12},{12,8},{9,1... | collective-permute-start | bytes 921608 | tf_op jit(solution)/shard_map/ppermute | solution.py:820
  (114 other events, 1158.4 us)
Sparse Core Ops, SparseCore 0:
  25.3 32.0 all-gather.8
  59.5 30.2 all-gather.10
  93.0 30.8 all-gather.12
  145.7 30.2 all-gather.14
  330.8 50.1 reduce-scatter.4
  386.9 29.3 reduce-scatter.6
  468.7 29.3 reduce-scatter.10
  500.4 50.8 reduce-scatter.8

commit v14 on v13

--- a/solution.py
+++ b/solution.py
@@ -966,9 +966,11 @@
     dense_near = along_batch(dense_near)
     qkv_across = swapped(along, "blk", 1)
     next_columns = qkv_columns(qkv_weight[1], None).reshape(-1, part3)
-    qkv_across, dense_near, next_columns = tied(qkv_across, dense_near, next_columns)
+    qkv_across, dense_near, next_columns, dense_next = tied(
+        qkv_across, dense_near, next_columns, dense_own[1]
+    )
     across, beside = swapped(dense_near, "blk", 1), swapped(dense_near, "head", 2)
-    next_along = along_batch(next_columns)
+    next_along, dense_next = along_batch(next_columns), along_batch(dense_next)
     weight, gains = assemble_columns(along, qkv_across, part3)
     qkvs = [weight]
     gains = gains.T.astype(F32)
@@ -977,30 +979,31 @@
     for layer in range(layers):
         normed, factor_one = normalize(stream, gains[layer])
         if layer == 1:
-            normed, next_across, dense_next = tied(normed.astype(BF16), next_across, dense_next)
+            normed, next_across = tied(normed.astype(BF16), next_across)
             far, near = swapped(normed, "head", 2), other_core(normed)
-            across = swapped(dense_next, "blk", 1)
-            far, dense_after = tied(far, dense_next)
-            beside = swapped(dense_after, "head", 2)
+            far, dense_next = tied(far, dense_next)
+            across, beside = swapped(dense_next, "blk", 1), swapped(dense_next, "head", 2)
             token_pieces = (normed, near, far, other_core(far))
             qkvs.append(assemble_columns(next_along, next_across, part3)[0])
         normed_all, projected = project(
             token_pieces, gains[layer], qkvs[layer], layer == 0, token_rows
         )
+        if layer == 1:
+            projected, cotangent = tied(projected, cotangent)
+            upper = swap_halves(cotangent)
         attended, log_total = attend_rows(
             projected, scale_vecs[layer], segments, 4, token_rows
         )
+        if layer == 1:
+            attended, upper = tied(attended, upper)
         attended, across, beside = tied(attended, across, beside)
         one, two = to_beside(across), to_across(beside)
         if layer == 0:
-            next_along, dense_next = tied(next_along, dense_own[1])
-            dense_next = along_batch(dense_next)
-            attended_t, one, two, next_along = tied(over_head(attended), one, two, next_along)
+            two, next_along = tied(two, next_along)
             next_across = swapped(next_along, "blk", 1)
         else:
             dense_near = dense_next
-            attended_t, one, two, cotangent = tied(over_head(attended), one, two, cotangent)
-            upper = swap_halves(cotangent)
+        attended_t, one, two = tied(over_head(attended), one, two)
         pieces = (dense_near, across, beside, one, two)
         pieces += tuple(other_core(piece) for piece in pieces)
         attended_t = attended_t.reshape(width, -1)
@@ -1070,10 +1073,10 @@
             halves, to_core, rows = tied(halves, to_core, neighbour_rows(cored, *diagonal))
             sent = sent_beside_and_across(*rows)
             halves = halves + other_core(to_core).astype(F32)
-            halves, sent = tied(halves, sent)
+            halves, sent, z_sum = tied(halves, sent, z_sum)
             dense_first = over_batch(own_sum(cored, *sent))
             normed_grad = scatter_row(halves)
-            normed_grad, z_sum, z_across = tied(normed_grad, z_sum, z_across)
+            normed_grad, z_across = tied(normed_grad, z_across)
             dense_grad = [dense_first, summed]
             qkv_grads = [columns_to_rows(across_sum(z_sum)), columns_to_rows(z_across)]
         else:

time: 598 us -> 553 us (0.925)
  waiting for transfers between devices: 274 us -> 211 us
  blocking collectives: 0 us -> 20 us
    reduce_scatter x4, waiting for transfers between devices: 57.4 us -> 4.11 us  [over_batch(): lax.psum_scatter(parts.astype(BF16), 'batch', scatter_dimension=0, tiled=...]
    all_to_all x0 -> x1, blocking collectives: none -> 20 us  [over_head(): lax.all_to_all(parts, 'head', split_axis=0, concat_axis=0, tiled=True)]
    all_to_all x8 -> x7, waiting for transfers between devices: 55.9 us -> 37.3 us  [over_head(): lax.all_to_all(parts, 'head', split_axis=0, concat_axis=0, tiled=True)]
    ppermute x51, waiting for transfers between devices: 145 us -> 154 us  [swapped(): return lax.ppermute(array, axis, [(i, i ^ mask) for i in range(size)])]
    all_to_all x8 -> x7, starting transfers between devices: 30 us -> 26.8 us  [over_head(): lax.all_to_all(parts, 'head', split_axis=0, concat_axis=0, tiled=True)]
    unnamed x158 -> x144, local copies, waits for them, and re-layouts: 15.8 us -> 14.6 us
  transfers between devices with their start and end apart: 67 -> 66, of which waited for: 36 -> 34; matrix products, arithmetic and copies ran while one was open for 11% -> 13% of each run, Pallas kernels for 20% -> 22%
where the time goes in v14:
time: 553 us; the launch traced here: 545 us
  waiting for transfers between devices  211 us (38%)
  Pallas kernels  123 us (22%)
  starting transfers between devices  71.1 us (13%)
  other arithmetic  45 us (8%)
  local copies, waits for them, and re-layouts  38.5 us (7%)
  matrix products  20.3 us (4%)
  blocking collectives  20 us (4%)
  between operations  16.1 us (3%)
    ppermute x51, waiting for transfers between devices, swapped(): return lax.ppermute(array, axis, [(i, i ^ mask) for i in range(size)])  154 us
    ppermute x51, starting transfers between devices, swapped(): return lax.ppermute(array, axis, [(i, i ^ mask) for i in range(size)])  43.3 us
    all_to_all x7, waiting for transfers between devices, over_head(): lax.all_to_all(parts, 'head', split_axis=0, concat_axis=0, tiled=True)  37.3 us
    all_to_all x7, starting transfers between devices, over_head(): lax.all_to_all(parts, 'head', split_axis=0, concat_axis=0, tiled=True)  26.8 us
    pallas_call x2, Pallas kernels, attend_back_rows(): pl.pallas_call(functools.partial(attend_back_kernel, token_rows), grid=(l...  25.1 us
    all_to_all x1, blocking collectives, over_head(): lax.all_to_all(parts, 'head', split_axis=0, concat_axis=0, tiled=True)  20 us
    pallas_call x2, Pallas kernels, dense_grads(): pl.pallas_call(dense_grad_kernel, grid_spec=pltpu.PrefetchScalarGridSpec(...  19.7 us
    pallas_call x2, Pallas kernels, attend_rows(): pl.pallas_call(functools.partial(attend_kernel, token_rows), grid=(local_...  17.9 us
  transfers between devices with their start and end apart: 66, of which 34 were waited for; matrix products, arithmetic and copies ran while one was open for 13% of the time, Pallas kernels for 22%

profile of v14, /device:TPU:0, one launch (start us, length us, event | category | flops | bytes accessed | tf_op | source)
XLA Modules:
  0.0 545.2 jit_solution(1214730700452892757)
XLA Ops:
  19.1 5.4 all-to-all-done
  26.4 15.2 %collective-permute-done.2.refs_2_ = bf16[256,1280]{1,0:T(8,128)(2,1)S(1)} collective-permute-done((bf16[256,1280]{1,0:T(8,128)(2,1)S(1)}, bf16[256,1280]{1,0:T(8,128)(2,1)S(1)}, u32[]{:S(2)}, u32[]{:S(2)}) %collective-permute-start.2) | collective-permute-done | bytes 655392 | tf_op jit(solution)/shard_map/ppermute | solution.py:820
  44.1 13.3 %all-gather.9.cloned.1.call-done = bf16[640,964]{1,0:T(8,128)(2,1)} async-done(((bf16[160,964]{1,0:T(8,128)(2,1)}), bf16[640,964]{1,0:T(8,128)(2,1)}) %all-gather.9.cloned.1.call-update) | async-done | bytes 1233936 | tf_op jit(solution)/shard_map/all_gather | solution.py:854
  65.0 5.9 %all-to-all-done.1 = bf16[4,40,960]{2,1,0:T(8,128)(2,1)S(1)} async-done(((bf16[4,40,960]{2,1,0:T(8,128)(2,1)}), bf16[4,40,960]{2,1,0:T(8,128)(2,1)S(1)}, u32[]{:S(2)}, u32[]{:S(2)}) %all-to-all-start.1) | async-done | bytes 307232 | tf_op jit(solution)/shard_map/all_to_all | solution.py:841
  70.9 16.7 %collective-permute-done.4.across_ref = bf16[4,160,964]{2,1,0:T(8,128)(2,1)S(1)} collective-permute-done((bf16[4,160,964]{2,1,0:T(8,128)(2,1)}, bf16[4,160,964]{2,1,0:T(8,128)(2,1)S(1)}, u32[]{:S(2)}, u32[]{:S(2)}) %collective-permute-start.4) | collective-permute-done | bytes 1233952 | tf_op jit(solution)/shard_map/ppermute | solution.py:820
  93.3 4.6 shard_map.169
  101.1 8.9 %shard_map.170 = (bf16[1024,1280]{1,0:T(8,128)(2,1)}, f32[960,1024]{1,0:T(8,128)}) custom-call(s32[3]{0:T(128)S(1)} %pad_add_fusion.place_ref.core_ref, bf16[256,1280]{1,0:T(8,128)(2,1)} %bitcast.212, bf16[256,1280]{1,0:T(8,128)(2,1)} %copy-done.55, bf16[256,1280]{1,0:T(8,128)(2,1)} %copy-done.54, bf16[256,1280]{1,0:T(8,128)(2,1)} %collective-permute-done.3.refs_3_, ...), custom_call_target="tpu_custom_call" | custom-call | flops 1048576 | bytes 1048576 | tf_op jit(solution)/shard_map/pallas_call | solution.py:683
  112.2 8.9 %shard_map.171 = (bf16[4,4,80,256]{3,2,1,0:T(8,128)(2,1)S(1)}, f32[4,1,1024]{2,1,0:T(1,128)S(1)}) custom-call(f32[3,4,80,1024]{3,2,1,0:T(8,128)S(1)} %bitcast.180, f32[80,1]{1,0:T(8,128)S(1)} %copy.41.scale_ref, s32[1024,1]{1,0:T(8,128)S(1)} %copy.42.col_ref, s32[1,1024]{1,0:T(1,128)S(1)} %constant_dynamic-slice_fusion.row_ref), custom_call_target="tpu_custom_call" | custom-call | flops 1048576 | bytes 1048576 | tf_op jit(solution)/shard_map/pallas_call | solution.py:413
  129.4 7.5 %collective-permute-done.8.refs_4_ = bf16[4,40,1920]{2,1,0:T(8,128)(2,1)} collective-permute-done((bf16[4,40,1920]{2,1,0:T(8,128)(2,1)}, bf16[4,40,1920]{2,1,0:T(8,128)(2,1)}, u32[]{:S(2)}, u32[]{:S(2)}) %collective-permute-start.8) | collective-permute-done | bytes 614432 | tf_op jit(solution)/shard_map/ppermute | solution.py:820
  136.9 8.2 %all-to-all-done.2 = bf16[4,320,256]{2,1,0:T(8,128)(2,1)} async-done(((bf16[4,320,256]{2,1,0:T(8,128)(2,1)}), bf16[4,320,256]{2,1,0:T(8,128)(2,1)}, u32[]{:S(2)}, u32[]{:S(2)}) %all-to-all-start.2) | async-done | bytes 655392 | tf_op jit(solution)/shard_map/all_to_all | solution.py:841
  148.4 4.6 shard_map.172
  161.3 15.4 %collective-permute-done.14.across_ref = bf16[4,160,960]{2,1,0:T(8,128)(2,1)} collective-permute-done((bf16[4,160,960]{2,1,0:T(8,128)(2,1)}, bf16[4,160,960]{2,1,0:T(8,128)(2,1)}, u32[]{:S(2)}, u32[]{:S(2)}) %collective-permute-start.14) | collective-permute-done | bytes 1228832 | tf_op jit(solution)/shard_map/ppermute | solution.py:820
  177.4 15.4 %collective-permute-done.15.refs_2_ = bf16[256,1280]{1,0:T(8,128)(2,1)} collective-permute-done((bf16[256,1280]{1,0:T(8,128)(2,1)}, bf16[256,1280]{1,0:T(8,128)(2,1)}, u32[]{:S(2)}, u32[]{:S(2)}) %collective-permute-start.15) | collective-permute-done | bytes 655392 | tf_op jit(solution)/shard_map/ppermute | solution.py:820
  192.8 4.6 shard_map.173
  200.3 7.7 %shard_map.174 = (bf16[1024,1280]{1,0:T(8,128)(2,1)}, f32[960,1024]{1,0:T(8,128)}) custom-call(s32[3]{0:T(128)S(1)} %pad_add_fusion.place_ref.core_ref, bf16[256,1280]{1,0:T(8,128)(2,1)} %multiply_convert_fusion.2.refs_0_, bf16[256,1280]{1,0:T(8,128)(2,1)} %collective-permute-done.16.refs_1_, bf16[256,1280]{1,0:T(8,128)(2,1)} %collective-permute-done.15.refs_2_, ...), custom_call_target="tpu_custom_call" | custom-call | flops 1048576 | bytes 1048576 | tf_op jit(solution)/shard_map/pallas_call | solution.py:683
  211.0 8.9 %shard_map.175 = (bf16[4,4,80,256]{3,2,1,0:T(8,128)(2,1)S(1)}, f32[4,1,1024]{2,1,0:T(1,128)S(1)}) custom-call(f32[3,4,80,1024]{3,2,1,0:T(8,128)S(1)} %bitcast.182, f32[80,1]{1,0:T(8,128)S(1)} %copy.43.scale_ref, s32[1024,1]{1,0:T(8,128)S(1)} %copy.42.col_ref, s32[1,1024]{1,0:T(1,128)S(1)} %constant_dynamic-slice_fusion.row_ref), custom_call_target="tpu_custom_call" | custom-call | flops 1048576 | bytes 1048576 | tf_op jit(solution)/shard_map/pallas_call | solution.py:413
  220.0 14.6 %collective-permute-done.18 = bf16[128,1280]{1,0:T(8,128)(2,1)} collective-permute-done((bf16[128,1280]{1,0:T(8,128)(2,1)S(1)}, bf16[128,1280]{1,0:T(8,128)(2,1)}, u32[]{:S(2)}, u32[]{:S(2)}) %collective-permute-start.18) | collective-permute-done | bytes 327712 | tf_op jit(solution)/shard_map/ppermute | solution.py:820
  239.2 20.0 %all_to_all.40 = bf16[4,320,256]{2,1,0:T(8,128)(2,1)S(1)} all-to-all(bf16[4,320,256]{2,1,0:T(8,128)(2,1)S(1)} %bitcast.198), channel_id=1, replica_groups=mesh['batch'=4,'blk'=2,'head'=4] {'head'}, dimensions={0} | all-to-all | bytes 1310720 | tf_op jit(solution)/shard_map/all_to_all | solution.py:841
  279.5 9.9 %shard_map.177 = (bf16[2,2,4,40,3840]{4,3,2,1,0:T(8,128)(2,1)}, bf16[2,2,4,40,3840]{4,3,2,1,0:T(8,128)(2,1)}) custom-call(s32[3]{0:T(128)S(1)} %pad_add_fusion.place_ref.core_ref, bf16[1280,256]{1,0:T(8,128)(2,1)} %bitcast.222, bf16[256,1280]{1,0:T(8,128)(2,1)} %copy-done.29, bf16[256,1280]{1,0:T(8,128)(2,1)} %copy-done.52, bf16[256,1280]{1,0:T(8,128)(2,1)} %copy-done.30, ...), custom_call_target="tpu_custom_call" | custom-call | flops 1048576 | bytes 1048576 | tf_op jit(solution)/shard_map/pallas_call | solution.py:577
  291.7 12.5 %shard_map.178 = (bf16[3,4,80,1024]{3,2,1,0:T(8,128)(2,1)}, f32[80,128]{1,0:T(8,128)}) custom-call(f32[3,4,80,1024]{3,2,1,0:T(8,128)} %bitcast.181, bf16[4,4,80,256]{3,2,1,0:T(8,128)(2,1)} %bitcast.50.grad_ref, f32[4,1,1024]{2,1,0:T(1,128)S(1)} %get-tuple-element.153.lse_ref, f32[80,1]{1,0:T(8,128)S(1)} %copy.43.scale_ref, s32[1024,1]{1,0:T(8,128)S(1)} %copy.42.col_ref, ...), custom_call_target="tpu_custom_call" | custom-call | flops 1048576 | bytes 1048576 | tf_op jit(solution)/shard_map/pallas_call | solution.py:506
  313.2 11.3 %shard_map.179 = (f32[2,2,128,1280]{3,2,1,0:T(8,128)}, bf16[2,2,128,1280]{3,2,1,0:T(8,128)(2,1)}, bf16[1280,960]{1,0:T(8,128)(2,1)}) custom-call(s32[3]{0:T(128)S(1)} %pad_add_fusion.place_ref.core_ref, bf16[960,1024]{1,0:T(8,128)(2,1)} %bitcast.224, bf16[1280,960]{1,0:T(8,128)(2,1)} %bitcast.200, bf16[1024,1280]{1,0:T(8,128)(2,1)} %get-tuple-element.160.normed_ref), custom_call_target="tpu_custom_call" | custom-call | flops 1048576 | bytes 1048576 | tf_op jit(solution)/shard_map/pallas_call | solution.py:729
  338.7 14.6 %collective-permute-done.33 = bf16[2,128,1280]{2,1,0:T(8,128)(2,1)} collective-permute-done((bf16[2,128,1280]{2,1,0:T(8,128)(2,1)}, bf16[2,128,1280]{2,1,0:T(8,128)(2,1)}, u32[]{:S(2)}, u32[]{:S(2)}) %collective-permute-start.33) | collective-permute-done | bytes 655392 | tf_op jit(solution)/shard_map/ppermute | solution.py:820
  371.1 9.9 %shard_map.180 = (bf16[2,2,4,40,3840]{4,3,2,1,0:T(8,128)(2,1)}, bf16[2,2,4,40,3840]{4,3,2,1,0:T(8,128)(2,1)}) custom-call(s32[3]{0:T(128)S(1)} %pad_add_fusion.place_ref.core_ref, bf16[1280,256]{1,0:T(8,128)(2,1)} %bitcast.29.attended_ref, bf16[256,1280]{1,0:T(8,128)(2,1)} %copy-done.26, bf16[256,1280]{1,0:T(8,128)(2,1)} %copy-done.48, ...), custom_call_target="tpu_custom_call" | custom-call | flops 1048576 | bytes 1048576 | tf_op jit(solution)/shard_map/pallas_call | solution.py:577
  381.0 9.5 %all-to-all-done.5 = bf16[4,320,256]{2,1,0:T(8,128)(2,1)S(1)} async-done(((bf16[4,320,256]{2,1,0:T(8,128)(2,1)}), bf16[4,320,256]{2,1,0:T(8,128)(2,1)S(1)}, u32[]{:S(2)}, u32[]{:S(2)}) %all-to-all-start.5) | async-done | bytes 655392 | tf_op jit(solution)/shard_map/all_to_all | solution.py:841
  394.3 12.6 %shard_map.181 = (bf16[3,4,80,1024]{3,2,1,0:T(8,128)(2,1)}, f32[80,128]{1,0:T(8,128)}) custom-call(f32[3,4,80,1024]{3,2,1,0:T(8,128)} %bitcast.179, bf16[4,4,80,256]{3,2,1,0:T(8,128)(2,1)} %bitcast.223, f32[4,1,1024]{2,1,0:T(1,128)S(1)} %get-tuple-element.180.lse_ref, f32[80,1]{1,0:T(8,128)S(1)} %copy.41.scale_ref, s32[1024,1]{1,0:T(8,128)S(1)} %copy.42.col_ref, ...), custom_call_target="tpu_custom_call" | custom-call | flops 1048576 | bytes 1048576 | tf_op jit(solution)/shard_map/pallas_call | solution.py:506
  407.0 7.5 %shard_map.182 = bf16[1280,960]{1,0:T(8,128)(2,1)} custom-call(bf16[960,1024]{1,0:T(8,128)(2,1)} %bitcast.216, bf16[1024,1280]{1,0:T(8,128)(2,1)} %get-tuple-element.184.normed_ref), custom_call_target="tpu_custom_call" | custom-call | flops 1048576 | bytes 1048576 | tf_op jit(solution)/shard_map/pallas_call | solution.py:800
  426.5 8.2 %shard_map.183 = (f32[2,2,128,1280]{3,2,1,0:T(8,128)}, bf16[2,2,128,1280]{3,2,1,0:T(8,128)(2,1)}) custom-call(s32[3]{0:T(128)S(1)} %pad_add_fusion.place_ref.core_ref, bf16[960,1024]{1,0:T(8,128)(2,1)} %bitcast.217, bf16[1280,960]{1,0:T(8,128)(2,1)} %bitcast.209), custom_call_target="tpu_custom_call" | custom-call | flops 1048576 | bytes 1048576 | tf_op jit(solution)/shard_map/pallas_call | solution.py:770
  434.7 4.8 collective-permute-done.37
  451.0 25.7 %collective-permute-done.48 = f32[2,80]{1,0:T(2,128)S(1)} collective-permute-done((f32[2,80]{1,0:T(2,128)S(1)}, f32[2,80]{1,0:T(2,128)S(1)}, u32[]{:S(2)}, u32[]{:S(2)}) %collective-permute-start.48) | collective-permute-done | bytes 672 | tf_op jit(solution)/shard_map/ppermute | solution.py:820
  488.2 5.8 %collective-permute-done.43 = bf16[160,960]{1,0:T(8,128)(2,1)} collective-permute-done((bf16[160,960]{1,0:T(8,128)(2,1)}, bf16[160,960]{1,0:T(8,128)(2,1)}, u32[]{:S(2)}, u32[]{:S(2)}) %collective-permute-start.43) | collective-permute-done | bytes 307232 | tf_op jit(solution)/shard_map/ppermute | solution.py:820
  505.4 4.7 all-to-all-done.6
  513.3 4.6 all-to-all-start.7
  (389 shorter events, 201.8 us)
Async XLA Ops:
  17.7 39.7 %all-gather.9.cloned.1.call-start = ((), (), s32[]{:S(2)}) async-start(), calls=%async_computation.16 | async-start | bytes 1638400 | tf_op jit(solution)/shard_map/all_gather | solution.py:854
  25.2 64.7 %all-gather.11.cloned.1.call-start = ((), (), s32[]{:S(2)}) async-start(), calls=%async_computation.17 | async-start | bytes 1536000 | tf_op jit(solution)/shard_map/all_gather | solution.py:854
  57.4 30.1 %collective-permute-start.4 = (bf16[4,160,964]{2,1,0:T(8,128)(2,1)}, bf16[4,160,964]{2,1,0:T(8,128)(2,1)S(1)}, u32[]{:S(2)}, u32[]{:S(2)}) collective-permute-start(bf16[4,160,964]{2,1,0:T(8,128)(2,1)} %bitcast.232), channel_id=1, source_target_pairs={{0,4},{4,0},{1,5},{5,1},{2,6},{6,2},{3,7},{7,3},{8,12},{12,8},{9,1... | collective-permute-start | bytes 3701768 | tf_op jit(solution)/shard_map/ppermute | solution.py:820
  64.2 65.3 %all-gather.13.cloned.1.call-start = ((), (), s32[]{:S(2)}) async-start(), calls=%async_computation.18 | async-start | bytes 1638400 | tf_op jit(solution)/shard_map/all_gather | solution.py:854
  89.9 31.3 %collective-permute-start.6 = (bf16[4,40,3840]{2,1,0:T(8,128)(2,1)}, bf16[4,40,3840]{2,1,0:T(8,128)(2,1)S(1)}, u32[]{:S(2)}, u32[]{:S(2)}) collective-permute-start(bf16[4,40,3840]{2,1,0:T(8,128)(2,1)} %bitcast.15.refs_0_), channel_id=1, source_target_pairs={{0,2},{1,3},{2,0},{3,1},{4,6},{5,7},{6,4},{7,5},{8,10},{9,11},{10,... | collective-permute-start | bytes 3686408 | tf_op jit(solution)/shard_map/ppermute | solution.py:820
  91.3 29.8 %collective-permute-start.5 = (bf16[4,40,3840]{2,1,0:T(8,128)(2,1)}, bf16[4,40,3840]{2,1,0:T(8,128)(2,1)S(1)}, u32[]{:S(2)}, u32[]{:S(2)}) collective-permute-start(bf16[4,40,3840]{2,1,0:T(8,128)(2,1)} %bitcast.15.refs_0_), channel_id=1, source_target_pairs={{0,4},{4,0},{1,5},{5,1},{2,6},{6,2},{3,7},{7,3},{8,12},{12,8},{9,1... | collective-permute-start | bytes 3686408 | tf_op jit(solution)/shard_map/ppermute | solution.py:820
  123.6 21.5 %collective-permute-start.7 = (bf16[4,40,1920]{2,1,0:T(8,128)(2,1)}, bf16[4,40,1920]{2,1,0:T(8,128)(2,1)}, u32[]{:S(2)}, u32[]{:S(2)}) collective-permute-start(bf16[4,40,1920]{2,1,0:T(8,128)(2,1)} %slice.146), channel_id=1, source_target_pairs={{0,2},{1,3},{2,0},{3,1},{4,6},{5,7},{6,4},{7,5},{8,10},{9,11},{10,... | collective-permute-start | bytes 1843208 | tf_op jit(solution)/shard_map/ppermute | solution.py:820
  124.1 21.5 %collective-permute-start.9 = (bf16[4,40,3840]{2,1,0:T(8,128)(2,1)}, bf16[4,40,3840]{2,1,0:T(8,128)(2,1)}, u32[]{:S(2)}, u32[]{:S(2)}) collective-permute-start(bf16[4,40,3840]{2,1,0:T(8,128)(2,1)} %bitcast.15.refs_0_), channel_id=1, source_target_pairs={{0,1},{1,0},{2,3},{3,2},{4,5},{5,4},{6,7},{7,6},{8,9},{9,8},{10,11... | collective-permute-start | bytes 3686408 | tf_op jit(solution)/shard_map/ppermute | solution.py:820
  124.1 24.2 %collective-permute-start.10 = (bf16[4,40,3840]{2,1,0:T(8,128)(2,1)S(1)}, bf16[4,40,3840]{2,1,0:T(8,128)(2,1)}, u32[]{:S(2)}, u32[]{:S(2)}) collective-permute-start(bf16[4,40,3840]{2,1,0:T(8,128)(2,1)S(1)} %collective-permute-done.5.refs_1_), channel_id=1, source_target_pairs={{0,1},{1,0},{2,3},{3,2},{4,5},{5,4},{6,7},{7,6},{8,9},{9,8},{10,11... | collective-permute-start | bytes 3686408 | tf_op jit(solution)/shard_map/ppermute | solution.py:820
  124.7 23.7 %collective-permute-start.11 = (bf16[4,40,3840]{2,1,0:T(8,128)(2,1)S(1)}, bf16[4,40,3840]{2,1,0:T(8,128)(2,1)}, u32[]{:S(2)}, u32[]{:S(2)}) collective-permute-start(bf16[4,40,3840]{2,1,0:T(8,128)(2,1)S(1)} %collective-permute-done.6.refs_2_), channel_id=1, source_target_pairs={{0,1},{1,0},{2,3},{3,2},{4,5},{5,4},{6,7},{7,6},{8,9},{9,8},{10,11... | collective-permute-start | bytes 3686408 | tf_op jit(solution)/shard_map/ppermute | solution.py:820
  128.8 48.5 %all-gather.15.cloned.1.call-start = ((), (), s32[]{:S(2)}) async-start(), calls=%async_computation.19 | async-start | bytes 1536000 | tf_op jit(solution)/shard_map/all_gather | solution.py:854
  145.7 31.1 %collective-permute-start.14 = (bf16[4,160,960]{2,1,0:T(8,128)(2,1)}, bf16[4,160,960]{2,1,0:T(8,128)(2,1)}, u32[]{:S(2)}, u32[]{:S(2)}) collective-permute-start(bf16[4,160,960]{2,1,0:T(8,128)(2,1)} %bitcast.234), channel_id=1, source_target_pairs={{0,4},{4,0},{1,5},{5,1},{2,6},{6,2},{3,7},{7,3},{8,12},{12,8},{9,1... | collective-permute-start | bytes 3686408 | tf_op jit(solution)/shard_map/ppermute | solution.py:820
  177.4 22.1 %collective-permute-start.16 = (bf16[256,1280]{1,0:T(8,128)(2,1)}, bf16[256,1280]{1,0:T(8,128)(2,1)}, u32[]{:S(2)}, u32[]{:S(2)}) collective-permute-start(bf16[256,1280]{1,0:T(8,128)(2,1)} %multiply_convert_fusion.2.refs_0_), channel_id=1, source_target_pairs={{0,1},{1,0},{2,3},{3,2},{4,5},{5,4},{6,7},{7,6},{8,9},{9,8},{10,11... | collective-permute-start | bytes 1966088 | tf_op jit(solution)/shard_map/ppermute | solution.py:820
  197.4 38.3 %collective-permute-start.20 = (bf16[4,40,3840]{2,1,0:T(8,128)(2,1)}, bf16[4,40,3840]{2,1,0:T(8,128)(2,1)S(1)}, u32[]{:S(2)}, u32[]{:S(2)}) collective-permute-start(bf16[4,40,3840]{2,1,0:T(8,128)(2,1)} %bitcast.32.refs_0_), channel_id=1, source_target_pairs={{0,2},{1,3},{2,0},{3,1},{4,6},{5,7},{6,4},{7,5},{8,10},{9,11},{10,... | collective-permute-start | bytes 3686408 | tf_op jit(solution)/shard_map/ppermute | solution.py:820
  198.1 37.6 %collective-permute-start.19 = (bf16[4,40,3840]{2,1,0:T(8,128)(2,1)}, bf16[4,40,3840]{2,1,0:T(8,128)(2,1)S(1)}, u32[]{:S(2)}, u32[]{:S(2)}) collective-permute-start(bf16[4,40,3840]{2,1,0:T(8,128)(2,1)} %bitcast.32.refs_0_), channel_id=1, source_target_pairs={{0,4},{4,0},{1,5},{5,1},{2,6},{6,2},{3,7},{7,3},{8,12},{12,8},{9,1... | collective-permute-start | bytes 3686408 | tf_op jit(solution)/shard_map/ppermute | solution.py:820
  208.1 26.5 %collective-permute-start.18 = (bf16[128,1280]{1,0:T(8,128)(2,1)S(1)}, bf16[128,1280]{1,0:T(8,128)(2,1)}, u32[]{:S(2)}, u32[]{:S(2)}) collective-permute-start(bf16[128,1280]{1,0:T(8,128)(2,1)S(1)} %dynamic-slice_bitcast_fusion.10), channel_id=1, source_target_pairs={{0,4},{4,0},{1,5},{5,1},{2,6},{6,2},{3,7},{7,3},{8,12},{12,8},{9,1... | collective-permute-start | bytes 983048 | tf_op jit(solution)/shard_map/ppermute | solution.py:820
  235.8 23.4 %collective-permute-start.22 = (bf16[4,40,1920]{2,1,0:T(8,128)(2,1)S(1)}, bf16[4,40,1920]{2,1,0:T(8,128)(2,1)S(1)}, u32[]{:S(2)}, u32[]{:S(2)}) collective-permute-start(bf16[4,40,1920]{2,1,0:T(8,128)(2,1)S(1)} %slice.155), channel_id=1, source_target_pairs={{0,4},{4,0},{1,5},{5,1},{2,6},{6,2},{3,7},{7,3},{8,12},{12,8},{9,1... | collective-permute-start | bytes 1843208 | tf_op jit(solution)/shard_map/ppermute | solution.py:820
  237.3 21.9 %collective-permute-start.21 = (bf16[4,40,1920]{2,1,0:T(8,128)(2,1)S(1)}, bf16[4,40,1920]{2,1,0:T(8,128)(2,1)S(1)}, u32[]{:S(2)}, u32[]{:S(2)}) collective-permute-start(bf16[4,40,1920]{2,1,0:T(8,128)(2,1)S(1)} %slice.154), channel_id=1, source_target_pairs={{0,2},{1,3},{2,0},{3,1},{4,6},{5,7},{6,4},{7,5},{8,10},{9,11},{10,... | collective-permute-start | bytes 1843208 | tf_op jit(solution)/shard_map/ppermute | solution.py:820
  238.7 21.1 %collective-permute-start.23 = (bf16[4,40,3840]{2,1,0:T(8,128)(2,1)}, bf16[4,40,3840]{2,1,0:T(8,128)(2,1)S(1)}, u32[]{:S(2)}, u32[]{:S(2)}) collective-permute-start(bf16[4,40,3840]{2,1,0:T(8,128)(2,1)} %bitcast.32.refs_0_), channel_id=1, source_target_pairs={{0,1},{1,0},{2,3},{3,2},{4,5},{5,4},{6,7},{7,6},{8,9},{9,8},{10,11... | collective-permute-start | bytes 3686408 | tf_op jit(solution)/shard_map/ppermute | solution.py:820
  238.7 23.5 %collective-permute-start.24 = (bf16[4,40,3840]{2,1,0:T(8,128)(2,1)S(1)}, bf16[4,40,3840]{2,1,0:T(8,128)(2,1)S(1)}, u32[]{:S(2)}, u32[]{:S(2)}) collective-permute-start(bf16[4,40,3840]{2,1,0:T(8,128)(2,1)S(1)} %collective-permute-done.19.refs_1_), channel_id=1, source_target_pairs={{0,1},{1,0},{2,3},{3,2},{4,5},{5,4},{6,7},{7,6},{8,9},{9,8},{10,11... | collective-permute-start | bytes 3686408 | tf_op jit(solution)/shard_map/ppermute | solution.py:820
  239.2 23.0 %collective-permute-start.25 = (bf16[4,40,3840]{2,1,0:T(8,128)(2,1)S(1)}, bf16[4,40,3840]{2,1,0:T(8,128)(2,1)S(1)}, u32[]{:S(2)}, u32[]{:S(2)}) collective-permute-start(bf16[4,40,3840]{2,1,0:T(8,128)(2,1)S(1)} %collective-permute-done.20.refs_2_), channel_id=1, source_target_pairs={{0,1},{1,0},{2,3},{3,2},{4,5},{5,4},{6,7},{7,6},{8,9},{9,8},{10,11... | collective-permute-start | bytes 3686408 | tf_op jit(solution)/shard_map/ppermute | solution.py:820
  279.2 111.3 %reduce-scatter.5.cloned.1.call-start = ((), (), s32[]{:S(2)}) async-start(), calls=%async_computation.12 | async-start | bytes 3276800 | tf_op jit(solution)/shard_map/reduce_scatter | solution.py:870
  338.0 43.0 %collective-permute-start.34 = (bf16[4,40,3840]{2,1,0:T(8,128)(2,1)}, bf16[4,40,3840]{2,1,0:T(8,128)(2,1)}, u32[]{:S(2)}, u32[]{:S(2)}) collective-permute-start(bf16[4,40,3840]{2,1,0:T(8,128)(2,1)} %pad_maximum_fusion), channel_id=1, source_target_pairs={{0,4},{4,0},{1,5},{5,1},{2,6},{6,2},{3,7},{7,3},{8,12},{12,8},{9,1... | collective-permute-start | bytes 3686408 | tf_op jit(solution)/shard_map/ppermute | solution.py:820
  354.9 35.5 %collective-permute-start.35 = (bf16[4,40,3840]{2,1,0:T(8,128)(2,1)}, bf16[4,40,3840]{2,1,0:T(8,128)(2,1)}, u32[]{:S(2)}, u32[]{:S(2)}) collective-permute-start(bf16[4,40,3840]{2,1,0:T(8,128)(2,1)} %pad_maximum_fusion.1), channel_id=1, source_target_pairs={{0,2},{1,3},{2,0},{3,1},{4,6},{5,7},{6,4},{7,5},{8,10},{9,11},{10,... | collective-permute-start | bytes 3686408 | tf_op jit(solution)/shard_map/ppermute | solution.py:820
  367.6 22.9 %all-to-all-start.5 = ((bf16[4,320,256]{2,1,0:T(8,128)(2,1)}), bf16[4,320,256]{2,1,0:T(8,128)(2,1)S(1)}, u32[]{:S(2)}, u32[]{:S(2)}) async-start(bf16[4,320,256]{2,1,0:T(8,128)(2,1)} %bitcast.58), calls=%async_computation.5 | async-start | bytes 1310720 | tf_op jit(solution)/shard_map/all_to_all | solution.py:841
  371.0 63.6 %reduce-scatter.7.cloned.1.call-start = ((), (), s32[]{:S(2)}) async-start(), calls=%async_computation.13 | async-start | bytes 1536000 | tf_op jit(solution)/shard_map/reduce_scatter | solution.py:870
  394.3 91.3 %reduce-scatter.9.cloned.1.call-start = ((), (), s32[]{:S(2)}) async-start(), calls=%async_computation.14 | async-start | bytes 3276800 | tf_op jit(solution)/shard_map/reduce_scatter | solution.py:870
  442.8 42.4 %collective-permute-start.39 = (bf16[2,2,128,1280]{3,2,1,0:T(8,128)(2,1)S(1)}, bf16[2,2,128,1280]{3,2,1,0:T(8,128)(2,1)S(1)}, u32[]{:S(2)}, u32[]{:S(2)}) collective-permute-start(bf16[2,2,128,1280]{3,2,1,0:T(8,128)(2,1)S(1)} %copy-done.66), channel_id=1, source_target_pairs={{0,1},{1,0},{2,3},{3,2},{4,5},{5,4},{6,7},{7,6},{8,9},{9,8},{10,11... | collective-permute-start | bytes 3932168 | tf_op jit(solution)/shard_map/ppermute | solution.py:820
  447.7 37.8 %collective-permute-start.40 = (bf16[4,40,3840]{2,1,0:T(8,128)(2,1)S(1)}, bf16[4,40,3840]{2,1,0:T(8,128)(2,1)}, u32[]{:S(2)}, u32[]{:S(2)}) collective-permute-start(bf16[4,40,3840]{2,1,0:T(8,128)(2,1)S(1)} %pad_maximum_fusion.2), channel_id=1, source_target_pairs={{0,4},{4,0},{1,5},{5,1},{2,6},{6,2},{3,7},{7,3},{8,12},{12,8},{9,1... | collective-permute-start | bytes 3686408 | tf_op jit(solution)/shard_map/ppermute | solution.py:820
  449.1 36.5 %collective-permute-start.41 = (bf16[4,40,3840]{2,1,0:T(8,128)(2,1)S(1)}, bf16[4,40,3840]{2,1,0:T(8,128)(2,1)}, u32[]{:S(2)}, u32[]{:S(2)}) collective-permute-start(bf16[4,40,3840]{2,1,0:T(8,128)(2,1)S(1)} %pad_maximum_fusion.3), channel_id=1, source_target_pairs={{0,2},{1,3},{2,0},{3,1},{4,6},{5,7},{6,4},{7,5},{8,10},{9,11},{10,... | collective-permute-start | bytes 3686408 | tf_op jit(solution)/shard_map/ppermute | solution.py:820
  449.6 27.0 %collective-permute-start.48 = (f32[2,80]{1,0:T(2,128)S(1)}, f32[2,80]{1,0:T(2,128)S(1)}, u32[]{:S(2)}, u32[]{:S(2)}) collective-permute-start(f32[2,80]{1,0:T(2,128)S(1)} %fusion.112), channel_id=1, source_target_pairs={{0,4},{4,0},{1,5},{5,1},{2,6},{6,2},{3,7},{7,3},{8,12},{12,8},{9,1... | collective-permute-start | bytes 1928 | tf_op jit(solution)/shard_map/ppermute | solution.py:820
  501.8 33.4 %reduce-scatter.11.cloned.1.call-start = ((), (), s32[]{:S(2)}) async-start(), calls=%async_computation.15 | async-start | bytes 1536000 | tf_op jit(solution)/shard_map/reduce_scatter | solution.py:870
  (106 other events, 978.2 us)
Sparse Core Ops, SparseCore 0:
  25.3 32.0 all-gather.8
  59.5 30.2 all-gather.10
  93.0 30.8 all-gather.12
  145.8 30.2 all-gather.14
  338.1 50.2 reduce-scatter.4
  394.4 29.4 reduce-scatter.6
  426.2 50.8 reduce-scatter.8
  505.5 29.5 reduce-scatter.10

commit v15 on v13

--- a/solution.py
+++ b/solution.py
@@ -660,6 +660,34 @@
     return [part.reshape(-1, part.shape[-1]) for part in parts]
 
 
+def assemble_wide_kernel(place_ref, along_ref, across_ref, whole_ref):
+    blk = place_ref[0]
+    own, columns = along_ref.shape[1], whole_ref.shape[-1]
+    for i in range(along_ref.shape[-1] // columns):
+        place, part = slice(i * own, (i + 1) * own), slice(i * columns, (i + 1) * columns)
+        whole_ref[0, blk, place, :] = along_ref[0, :, part]
+        whole_ref[0, 1 - blk, place, :] = across_ref[0, :, part]
+
+
+def assemble_wide(along, across, columns):
+    batch, own, wide = along.shape
+    rows = own * (wide // columns)
+    piece = pl.BlockSpec((1, own, wide), lambda i, at: (i, 0, 0))
+    whole = pl.pallas_call(
+        assemble_wide_kernel,
+        grid_spec=pltpu.PrefetchScalarGridSpec(
+            num_scalar_prefetch=1,
+            grid=(batch,),
+            in_specs=[piece, piece],
+            out_specs=pl.BlockSpec((1, 2, rows, columns), lambda i, at: (i, 0, 0, 0)),
+        ),
+        out_shape=pltpu.HBM((batch, 2, rows, columns), BF16),
+        compiler_params=KERNEL,
+        cost_estimate=LIGHT,
+    )(place(), *in_hbm(along, across))
+    return whole.reshape(-1, columns)
+
+
 def project_kernel(with_norm, place_ref, *refs):
     pieces, (gain_ref, weight_ref, normed_ref, projected_ref) = refs[:4], refs[4:]
     head = place_ref[1] * 2 + place_ref[2]
@@ -965,10 +993,10 @@
     token_pieces = (first, near, far, both)
     dense_near = along_batch(dense_near)
     qkv_across = swapped(along, "blk", 1)
-    next_columns = qkv_columns(qkv_weight[1], None).reshape(-1, part3)
+    next_columns = jnp.concatenate(list(qkv_columns(qkv_weight[1], None)), axis=1)
     qkv_across, dense_near, next_columns = tied(qkv_across, dense_near, next_columns)
     across, beside = swapped(dense_near, "blk", 1), swapped(dense_near, "head", 2)
-    next_along = along_batch(next_columns)
+    next_both = along_batch(jnp.stack([next_columns, dense_own[1]]))
     weight, gains = assemble_columns(along, qkv_across, part3)
     qkvs = [weight]
     gains = gains.T.astype(F32)
@@ -977,32 +1005,38 @@
     for layer in range(layers):
         normed, factor_one = normalize(stream, gains[layer])
         if layer == 1:
-            normed, next_across, dense_next = tied(normed.astype(BF16), next_across, dense_next)
+            normed, next_across, beside, dense_next = tied(
+                normed.astype(BF16), next_across, beside, dense_next
+            )
             far, near = swapped(normed, "head", 2), other_core(normed)
             across = swapped(dense_next, "blk", 1)
-            far, dense_after = tied(far, dense_next)
-            beside = swapped(dense_after, "head", 2)
             token_pieces = (normed, near, far, other_core(far))
-            qkvs.append(assemble_columns(next_along, next_across, part3)[0])
+            qkvs.append(assemble_wide(next_along, next_across, part3))
         normed_all, projected = project(
             token_pieces, gains[layer], qkvs[layer], layer == 0, token_rows
         )
+        if layer == 1:
+            projected, across = tied(projected, across)
+            one, two = to_beside(across), to_across(beside)
         attended, log_total = attend_rows(
             projected, scale_vecs[layer], segments, 4, token_rows
         )
-        attended, across, beside = tied(attended, across, beside)
-        one, two = to_beside(across), to_across(beside)
         if layer == 0:
-            next_along, dense_next = tied(next_along, dense_own[1])
-            dense_next = along_batch(dense_next)
-            attended_t, one, two, next_along = tied(over_head(attended), one, two, next_along)
+            attended, across, beside = tied(attended, across, beside)
+            one, two = to_beside(across), to_across(beside)
+        if layer == 0:
+            attended_t, one, two, next_both = tied(over_head(attended), one, two, next_both)
+            next_along, dense_next = next_both[:, 0], next_both[:, 1]
             next_across = swapped(next_along, "blk", 1)
         else:
             dense_near = dense_next
-            attended_t, one, two, cotangent = tied(over_head(attended), one, two, cotangent)
+            attended, one, two, cotangent = tied(attended, one, two, cotangent)
             upper = swap_halves(cotangent)
+            attended_t, upper = tied(over_head(attended), upper)
         pieces = (dense_near, across, beside, one, two)
         pieces += tuple(other_core(piece) for piece in pieces)
+        if layer == 0:
+            beside = swapped(dense_next, "head", 2)
         attended_t = attended_t.reshape(width, -1)
         denses.append(assemble(pieces))
         dense = denses[layer]
@@ -1070,10 +1104,11 @@
             halves, to_core, rows = tied(halves, to_core, neighbour_rows(cored, *diagonal))
             sent = sent_beside_and_across(*rows)
             halves = halves + other_core(to_core).astype(F32)
-            halves, sent = tied(halves, sent)
-            dense_first = over_batch(own_sum(cored, *sent))
+            halves, sent, z_sum = tied(halves, sent, z_sum)
+            halves, own = tied(halves, own_sum(cored, *sent))
+            dense_first = over_batch(own)
             normed_grad = scatter_row(halves)
-            normed_grad, z_sum, z_across = tied(normed_grad, z_sum, z_across)
+            normed_grad, z_across, scale_grads[0] = tied(normed_grad, z_across, scale_grads[0])
             dense_grad = [dense_first, summed]
             qkv_grads = [columns_to_rows(across_sum(z_sum)), columns_to_rows(z_across)]
         else:

time: 598 us -> 539 us (0.901)
  waiting for transfers between devices: 274 us -> 203 us
  local copies, waits for them, and re-layouts: 38 us -> 46.6 us
    reduce_scatter x4, waiting for transfers between devices: 57.4 us -> 2.81 us  [over_batch(): lax.psum_scatter(parts.astype(BF16), 'batch', scatter_dimension=0, tiled=...]
    all_to_all x8, waiting for transfers between devices: 55.9 us -> 45.9 us  [over_head(): lax.all_to_all(parts, 'head', split_axis=0, concat_axis=0, tiled=True)]
    ppermute x51, waiting for transfers between devices: 145 us -> 138 us  [swapped(): return lax.ppermute(array, axis, [(i, i ^ mask) for i in range(size)])]
    all_gather x4 -> x3, waiting for transfers between devices: 15.6 us -> 15.8 us  [along_batch(): return lax.all_gather(piece, 'batch', axis=0, tiled=False)]
  transfers between devices with their start and end apart: 67 -> 66, of which waited for: 36 -> 34; matrix products, arithmetic and copies ran while one was open for 11% -> 13% of each run, Pallas kernels for 20% -> 23%
where the time goes in v15:
time: 539 us; the launch traced here: 532 us
  waiting for transfers between devices  203 us (38%)
  Pallas kernels  125 us (23%)
  starting transfers between devices  75.9 us (14%)
  local copies, waits for them, and re-layouts  46.6 us (9%)
  other arithmetic  44.4 us (8%)
  matrix products  20.7 us (4%)
  between operations  16.1 us (3%)
    ppermute x51, waiting for transfers between devices, swapped(): return lax.ppermute(array, axis, [(i, i ^ mask) for i in range(size)])  138 us
    all_to_all x8, waiting for transfers between devices, over_head(): lax.all_to_all(parts, 'head', split_axis=0, concat_axis=0, tiled=True)  45.9 us
    ppermute x51, starting transfers between devices, swapped(): return lax.ppermute(array, axis, [(i, i ^ mask) for i in range(size)])  45.2 us
    all_to_all x8, starting transfers between devices, over_head(): lax.all_to_all(parts, 'head', split_axis=0, concat_axis=0, tiled=True)  30.1 us
    pallas_call x2, Pallas kernels, attend_back_rows(): pl.pallas_call(functools.partial(attend_back_kernel, token_rows), grid=(l...  25 us
    pallas_call x2, Pallas kernels, dense_grads(): pl.pallas_call(dense_grad_kernel, grid_spec=pltpu.PrefetchScalarGridSpec(...  19.8 us
    unnamed x158, local copies, waits for them, and re-layouts  19.8 us
    pallas_call x2, Pallas kernels, attend_rows(): pl.pallas_call(functools.partial(attend_kernel, token_rows), grid=(local_...  18.5 us
  transfers between devices with their start and end apart: 66, of which 34 were waited for; matrix products, arithmetic and copies ran while one was open for 13% of the time, Pallas kernels for 23%

profile of v15, /device:TPU:0, one launch (start us, length us, event | category | flops | bytes accessed | tf_op | source)
XLA Modules:
  0.0 531.6 jit_solution(1690833749140744154)
XLA Ops:
  19.1 5.3 %all-to-all-done = bf16[4,40,964]{2,1,0:T(8,128)(2,1)S(1)} async-done(((bf16[4,40,964]{2,1,0:T(8,128)(2,1)}), bf16[4,40,964]{2,1,0:T(8,128)(2,1)S(1)}, u32[]{:S(2)}, u32[]{:S(2)}) %all-to-all-start) | async-done | bytes 308512 | tf_op jit(solution)/shard_map/all_to_all | solution.py:869
  26.7 14.9 %collective-permute-done.2.refs_2_ = bf16[256,1280]{1,0:T(8,128)(2,1)S(1)} collective-permute-done((bf16[256,1280]{1,0:T(8,128)(2,1)S(1)}, bf16[256,1280]{1,0:T(8,128)(2,1)S(1)}, u32[]{:S(2)}, u32[]{:S(2)}) %collective-permute-start.2) | collective-permute-done | bytes 655392 | tf_op jit(solution)/shard_map/ppermute | solution.py:848
  43.8 13.6 %all-gather.7.cloned.1.call-done = bf16[640,964]{1,0:T(8,128)(2,1)} async-done(((bf16[160,964]{1,0:T(8,128)(2,1)}), bf16[640,964]{1,0:T(8,128)(2,1)}) %all-gather.7.cloned.1.call-update) | async-done | bytes 1233936 | tf_op jit(solution)/shard_map/all_gather | solution.py:882
  64.2 6.6 %all-to-all-done.1 = bf16[4,40,960]{2,1,0:T(8,128)(2,1)S(1)} async-done(((bf16[4,40,960]{2,1,0:T(8,128)(2,1)}), bf16[4,40,960]{2,1,0:T(8,128)(2,1)S(1)}, u32[]{:S(2)}, u32[]{:S(2)}) %all-to-all-start.1) | async-done | bytes 307232 | tf_op jit(solution)/shard_map/all_to_all | solution.py:869
  71.0 16.6 %collective-permute-done.4.across_ref = bf16[4,160,964]{2,1,0:T(8,128)(2,1)} collective-permute-done((bf16[4,160,964]{2,1,0:T(8,128)(2,1)}, bf16[4,160,964]{2,1,0:T(8,128)(2,1)}, u32[]{:S(2)}, u32[]{:S(2)}) %collective-permute-start.4) | collective-permute-done | bytes 1233952 | tf_op jit(solution)/shard_map/ppermute | solution.py:848
  94.8 4.6 shard_map.169
  100.7 8.9 %shard_map.170 = (bf16[1024,1280]{1,0:T(8,128)(2,1)}, f32[960,1024]{1,0:T(8,128)}) custom-call(s32[3]{0:T(128)S(1)} %pad_add_fusion.place_ref.core_ref, bf16[256,1280]{1,0:T(8,128)(2,1)} %bitcast.228, bf16[256,1280]{1,0:T(8,128)(2,1)} %copy-done.62, bf16[256,1280]{1,0:T(8,128)(2,1)} %copy-done.61, bf16[256,1280]{1,0:T(8,128)(2,1)} %collective-permute-done.3.refs_3_, ...), custom_call_target="tpu_custom_call" | custom-call | flops 1048576 | bytes 1048576 | tf_op jit(solution)/shard_map/pallas_call | solution.py:711
  111.8 9.6 %shard_map.171 = (bf16[4,4,80,256]{3,2,1,0:T(8,128)(2,1)}, f32[4,1,1024]{2,1,0:T(1,128)S(1)}) custom-call(f32[3,4,80,1024]{3,2,1,0:T(8,128)S(1)} %bitcast.193, f32[80,1]{1,0:T(8,128)S(1)} %copy.60.scale_ref, s32[1024,1]{1,0:T(8,128)S(1)} %copy.61.col_ref, s32[1,1024]{1,0:T(1,128)S(1)} %constant_dynamic-slice_fusion.row_ref), custom_call_target="tpu_custom_call" | custom-call | flops 1048576 | bytes 1048576 | tf_op jit(solution)/shard_map/pallas_call | solution.py:413
  126.7 4.0 all-to-all-start.2
  131.8 15.5 %all-to-all-done.2 = bf16[4,320,256]{2,1,0:T(8,128)(2,1)S(1)} async-done(((bf16[4,320,256]{2,1,0:T(8,128)(2,1)}), bf16[4,320,256]{2,1,0:T(8,128)(2,1)S(1)}, u32[]{:S(2)}, u32[]{:S(2)}) %all-to-all-start.2) | async-done | bytes 655392 | tf_op jit(solution)/shard_map/all_to_all | solution.py:869
  152.2 4.5 shard_map.172
  162.8 16.8 %collective-permute-done.15.refs_2_ = bf16[4,40,3840]{2,1,0:T(8,128)(2,1)S(1)} collective-permute-done((bf16[4,40,3840]{2,1,0:T(8,128)(2,1)S(1)}, bf16[4,40,3840]{2,1,0:T(8,128)(2,1)S(1)}, u32[]{:S(2)}, u32[]{:S(2)}) %collective-permute-start.15) | collective-permute-done | bytes 1228832 | tf_op jit(solution)/shard_map/ppermute | solution.py:848
  182.6 13.3 %collective-permute-done.17.refs_2_ = bf16[256,1280]{1,0:T(8,128)(2,1)S(1)} collective-permute-done((bf16[256,1280]{1,0:T(8,128)(2,1)S(1)}, bf16[256,1280]{1,0:T(8,128)(2,1)S(1)}, u32[]{:S(2)}, u32[]{:S(2)}) %collective-permute-start.17) | collective-permute-done | bytes 655392 | tf_op jit(solution)/shard_map/ppermute | solution.py:848
  198.3 4.8 shard_map.173
  204.1 7.7 %shard_map.174 = (bf16[1024,1280]{1,0:T(8,128)(2,1)}, f32[960,1024]{1,0:T(8,128)}) custom-call(s32[3]{0:T(128)S(1)} %pad_add_fusion.place_ref.core_ref, bf16[256,1280]{1,0:T(8,128)(2,1)} %copy-done.40, bf16[256,1280]{1,0:T(8,128)(2,1)} %copy-done.64, bf16[256,1280]{1,0:T(8,128)(2,1)} %copy-done.63, bf16[256,1280]{1,0:T(8,128)(2,1)} %copy-done.65, ...), custom_call_target="tpu_custom_call" | custom-call | flops 1048576 | bytes 1048576 | tf_op jit(solution)/shard_map/pallas_call | solution.py:711
  217.9 9.0 %shard_map.175 = (bf16[4,4,80,256]{3,2,1,0:T(8,128)(2,1)S(1)}, f32[4,1,1024]{2,1,0:T(1,128)S(1)}) custom-call(f32[3,4,80,1024]{3,2,1,0:T(8,128)S(1)} %bitcast.195, f32[80,1]{1,0:T(8,128)S(1)} %copy.64.scale_ref, s32[1024,1]{1,0:T(8,128)S(1)} %copy.61.col_ref, s32[1,1024]{1,0:T(1,128)S(1)} %constant_dynamic-slice_fusion.row_ref), custom_call_target="tpu_custom_call" | custom-call | flops 1048576 | bytes 1048576 | tf_op jit(solution)/shard_map/pallas_call | solution.py:413
  231.3 4.3 all-to-all-start.3
  242.0 3.9 all-to-all-done.3
  247.3 4.2 shard_map.176
  267.6 9.9 %shard_map.177 = (bf16[2,2,4,40,3840]{4,3,2,1,0:T(8,128)(2,1)}, bf16[2,2,4,40,3840]{4,3,2,1,0:T(8,128)(2,1)}) custom-call(s32[3]{0:T(128)S(1)} %pad_add_fusion.place_ref.core_ref, bf16[1280,256]{1,0:T(8,128)(2,1)} %bitcast.49.attended_ref, bf16[256,1280]{1,0:T(8,128)(2,1)} %copy-done.36, bf16[256,1280]{1,0:T(8,128)(2,1)} %copy-done.59, ...), custom_call_target="tpu_custom_call" | custom-call | flops 1048576 | bytes 1048576 | tf_op jit(solution)/shard_map/pallas_call | solution.py:577
  280.3 12.4 %shard_map.178 = (bf16[3,4,80,1024]{3,2,1,0:T(8,128)(2,1)}, f32[80,128]{1,0:T(8,128)}) custom-call(f32[3,4,80,1024]{3,2,1,0:T(8,128)} %bitcast.194, bf16[4,4,80,256]{3,2,1,0:T(8,128)(2,1)} %bitcast.239, f32[4,1,1024]{2,1,0:T(1,128)S(1)} %get-tuple-element.148.lse_ref, f32[80,1]{1,0:T(8,128)S(1)} %copy.64.scale_ref, s32[1024,1]{1,0:T(8,128)S(1)} %copy.61.col_ref, ...), custom_call_target="tpu_custom_call" | custom-call | flops 1048576 | bytes 1048576 | tf_op jit(solution)/shard_map/pallas_call | solution.py:506
  301.5 11.3 %shard_map.179 = (f32[2,2,128,1280]{3,2,1,0:T(8,128)}, bf16[2,2,128,1280]{3,2,1,0:T(8,128)(2,1)}, bf16[1280,960]{1,0:T(8,128)(2,1)}) custom-call(s32[3]{0:T(128)S(1)} %pad_add_fusion.place_ref.core_ref, bf16[960,1024]{1,0:T(8,128)(2,1)} %bitcast.242, bf16[1280,960]{1,0:T(8,128)(2,1)} %bitcast.216, bf16[1024,1280]{1,0:T(8,128)(2,1)} %get-tuple-element.155.normed_ref), custom_call_target="tpu_custom_call" | custom-call | flops 1048576 | bytes 1048576 | tf_op jit(solution)/shard_map/pallas_call | solution.py:757
  326.8 13.7 %collective-permute-done.33 = bf16[2,128,1280]{2,1,0:T(8,128)(2,1)} collective-permute-done((bf16[2,128,1280]{2,1,0:T(8,128)(2,1)S(1)}, bf16[2,128,1280]{2,1,0:T(8,128)(2,1)}, u32[]{:S(2)}, u32[]{:S(2)}) %collective-permute-start.33) | collective-permute-done | bytes 655392 | tf_op jit(solution)/shard_map/ppermute | solution.py:848
  358.4 9.9 %shard_map.180 = (bf16[2,2,4,40,3840]{4,3,2,1,0:T(8,128)(2,1)}, bf16[2,2,4,40,3840]{4,3,2,1,0:T(8,128)(2,1)}) custom-call(s32[3]{0:T(128)S(1)} %pad_add_fusion.place_ref.core_ref, bf16[1280,256]{1,0:T(8,128)(2,1)} %bitcast.237, bf16[256,1280]{1,0:T(8,128)(2,1)} %copy-done.33, bf16[256,1280]{1,0:T(8,128)(2,1)} %copy-done.55, bf16[256,1280]{1,0:T(8,128)(2,1)} %copy-done.43, ...), custom_call_target="tpu_custom_call" | custom-call | flops 1048576 | bytes 1048576 | tf_op jit(solution)/shard_map/pallas_call | solution.py:577
  368.3 9.5 %all-to-all-done.5 = bf16[4,320,256]{2,1,0:T(8,128)(2,1)S(1)} async-done(((bf16[4,320,256]{2,1,0:T(8,128)(2,1)}), bf16[4,320,256]{2,1,0:T(8,128)(2,1)S(1)}, u32[]{:S(2)}, u32[]{:S(2)}) %all-to-all-start.5) | async-done | bytes 655392 | tf_op jit(solution)/shard_map/all_to_all | solution.py:869
  381.6 12.6 %shard_map.181 = (bf16[3,4,80,1024]{3,2,1,0:T(8,128)(2,1)}, f32[80,128]{1,0:T(8,128)}) custom-call(f32[3,4,80,1024]{3,2,1,0:T(8,128)} %bitcast.192, bf16[4,4,80,256]{3,2,1,0:T(8,128)(2,1)} %bitcast.240, f32[4,1,1024]{2,1,0:T(1,128)S(1)} %get-tuple-element.175.lse_ref, f32[80,1]{1,0:T(8,128)S(1)} %copy.60.scale_ref, s32[1024,1]{1,0:T(8,128)S(1)} %copy.61.col_ref, ...), custom_call_target="tpu_custom_call" | custom-call | flops 1048576 | bytes 1048576 | tf_op jit(solution)/shard_map/pallas_call | solution.py:506
  394.2 7.5 %shard_map.182 = bf16[1280,960]{1,0:T(8,128)(2,1)} custom-call(bf16[960,1024]{1,0:T(8,128)(2,1)} %bitcast.232, bf16[1024,1280]{1,0:T(8,128)(2,1)} %get-tuple-element.179.normed_ref), custom_call_target="tpu_custom_call" | custom-call | flops 1048576 | bytes 1048576 | tf_op jit(solution)/shard_map/pallas_call | solution.py:828
  415.5 8.2 %shard_map.183 = (f32[2,2,128,1280]{3,2,1,0:T(8,128)}, bf16[2,2,128,1280]{3,2,1,0:T(8,128)(2,1)}) custom-call(s32[3]{0:T(128)S(1)} %pad_add_fusion.place_ref.core_ref, bf16[960,1024]{1,0:T(8,128)(2,1)} %bitcast.233, bf16[1280,960]{1,0:T(8,128)(2,1)} %bitcast.225), custom_call_target="tpu_custom_call" | custom-call | flops 1048576 | bytes 1048576 | tf_op jit(solution)/shard_map/pallas_call | solution.py:798
  435.6 26.2 %collective-permute-done.40 = bf16[4,40,3840]{2,1,0:T(8,128)(2,1)} collective-permute-done((bf16[4,40,3840]{2,1,0:T(8,128)(2,1)S(1)}, bf16[4,40,3840]{2,1,0:T(8,128)(2,1)}, u32[]{:S(2)}, u32[]{:S(2)}) %collective-permute-start.40) | collective-permute-done | bytes 1228832 | tf_op jit(solution)/shard_map/ppermute | solution.py:848
  474.3 6.0 %collective-permute-done.45 = bf16[160,960]{1,0:T(8,128)(2,1)S(1)} collective-permute-done((bf16[160,960]{1,0:T(8,128)(2,1)S(1)}, bf16[160,960]{1,0:T(8,128)(2,1)S(1)}, u32[]{:S(2)}, u32[]{:S(2)}) %collective-permute-start.45) | collective-permute-done | bytes 307232 | tf_op jit(solution)/shard_map/ppermute | solution.py:848
  486.8 5.0 all-to-all-done.6
  500.7 4.4 all-to-all-start.7
  (405 shorter events, 210.6 us)
Async XLA Ops:
  17.7 39.7 %all-gather.7.cloned.1.call-start = ((), (), s32[]{:S(2)}) async-start(), calls=%async_computation.16 | async-start | bytes 1638400 | tf_op jit(solution)/shard_map/all_gather | solution.py:882
  25.2 64.7 %all-gather.9.cloned.1.call-start = ((), (), s32[]{:S(2)}) async-start(), calls=%async_computation.17 | async-start | bytes 1536000 | tf_op jit(solution)/shard_map/all_gather | solution.py:882
  57.4 30.2 %collective-permute-start.4 = (bf16[4,160,964]{2,1,0:T(8,128)(2,1)}, bf16[4,160,964]{2,1,0:T(8,128)(2,1)}, u32[]{:S(2)}, u32[]{:S(2)}) collective-permute-start(bf16[4,160,964]{2,1,0:T(8,128)(2,1)} %bitcast.249), channel_id=1, source_target_pairs={{0,4},{4,0},{1,5},{5,1},{2,6},{6,2},{3,7},{7,3},{8,12},{12,8},{9,1... | collective-permute-start | bytes 3701768 | tf_op jit(solution)/shard_map/ppermute | solution.py:848
  64.1 83.2 %all-gather.11.cloned.1.call-start = ((), (), s32[]{:S(2)}) async-start(), calls=%async_computation.18 | async-start | bytes 3072000 | tf_op jit(solution)/shard_map/all_gather | solution.py:882
  91.4 30.0 %collective-permute-start.6 = (bf16[4,40,3840]{2,1,0:T(8,128)(2,1)S(1)}, bf16[4,40,3840]{2,1,0:T(8,128)(2,1)}, u32[]{:S(2)}, u32[]{:S(2)}) collective-permute-start(bf16[4,40,3840]{2,1,0:T(8,128)(2,1)S(1)} %bitcast.210), channel_id=1, source_target_pairs={{0,2},{1,3},{2,0},{3,1},{4,6},{5,7},{6,4},{7,5},{8,10},{9,11},{10,... | collective-permute-start | bytes 3686408 | tf_op jit(solution)/shard_map/ppermute | solution.py:848
  92.9 28.5 %collective-permute-start.5 = (bf16[4,40,3840]{2,1,0:T(8,128)(2,1)S(1)}, bf16[4,40,3840]{2,1,0:T(8,128)(2,1)}, u32[]{:S(2)}, u32[]{:S(2)}) collective-permute-start(bf16[4,40,3840]{2,1,0:T(8,128)(2,1)S(1)} %bitcast.211), channel_id=1, source_target_pairs={{0,4},{4,0},{1,5},{5,1},{2,6},{6,2},{3,7},{7,3},{8,12},{12,8},{9,1... | collective-permute-start | bytes 3686408 | tf_op jit(solution)/shard_map/ppermute | solution.py:848
  125.3 22.1 %collective-permute-start.8 = (bf16[4,40,1920]{2,1,0:T(8,128)(2,1)}, bf16[4,40,1920]{2,1,0:T(8,128)(2,1)}, u32[]{:S(2)}, u32[]{:S(2)}) collective-permute-start(bf16[4,40,1920]{2,1,0:T(8,128)(2,1)} %slice.150), channel_id=1, source_target_pairs={{0,4},{4,0},{1,5},{5,1},{2,6},{6,2},{3,7},{7,3},{8,12},{12,8},{9,1... | collective-permute-start | bytes 1843208 | tf_op jit(solution)/shard_map/ppermute | solution.py:848
  126.2 21.1 %collective-permute-start.7 = (bf16[4,40,1920]{2,1,0:T(8,128)(2,1)}, bf16[4,40,1920]{2,1,0:T(8,128)(2,1)}, u32[]{:S(2)}, u32[]{:S(2)}) collective-permute-start(bf16[4,40,1920]{2,1,0:T(8,128)(2,1)} %slice.149), channel_id=1, source_target_pairs={{0,2},{1,3},{2,0},{3,1},{4,6},{5,7},{6,4},{7,5},{8,10},{9,11},{10,... | collective-permute-start | bytes 1843208 | tf_op jit(solution)/shard_map/ppermute | solution.py:848
  126.7 20.6 %all-to-all-start.2 = ((bf16[4,320,256]{2,1,0:T(8,128)(2,1)}), bf16[4,320,256]{2,1,0:T(8,128)(2,1)S(1)}, u32[]{:S(2)}, u32[]{:S(2)}) async-start(bf16[4,320,256]{2,1,0:T(8,128)(2,1)} %bitcast.27), calls=%async_computation.2 | async-start | bytes 1310720 | tf_op jit(solution)/shard_map/all_to_all | solution.py:869
  130.8 19.3 %collective-permute-start.9 = (bf16[4,40,3840]{2,1,0:T(8,128)(2,1)S(1)}, bf16[4,40,3840]{2,1,0:T(8,128)(2,1)}, u32[]{:S(2)}, u32[]{:S(2)}) collective-permute-start(bf16[4,40,3840]{2,1,0:T(8,128)(2,1)S(1)} %bitcast.212), channel_id=1, source_target_pairs={{0,1},{1,0},{2,3},{3,2},{4,5},{5,4},{6,7},{7,6},{8,9},{9,8},{10,11... | collective-permute-start | bytes 3686408 | tf_op jit(solution)/shard_map/ppermute | solution.py:848
  131.3 19.4 %collective-permute-start.10 = (bf16[4,40,3840]{2,1,0:T(8,128)(2,1)}, bf16[4,40,3840]{2,1,0:T(8,128)(2,1)}, u32[]{:S(2)}, u32[]{:S(2)}) collective-permute-start(bf16[4,40,3840]{2,1,0:T(8,128)(2,1)} %collective-permute-done.5.refs_1_), channel_id=1, source_target_pairs={{0,1},{1,0},{2,3},{3,2},{4,5},{5,4},{6,7},{7,6},{8,9},{9,8},{10,11... | collective-permute-start | bytes 3686408 | tf_op jit(solution)/shard_map/ppermute | solution.py:848
  131.4 20.8 %collective-permute-start.11 = (bf16[4,40,3840]{2,1,0:T(8,128)(2,1)}, bf16[4,40,3840]{2,1,0:T(8,128)(2,1)}, u32[]{:S(2)}, u32[]{:S(2)}) collective-permute-start(bf16[4,40,3840]{2,1,0:T(8,128)(2,1)} %collective-permute-done.6.refs_2_), channel_id=1, source_target_pairs={{0,1},{1,0},{2,3},{3,2},{4,5},{5,4},{6,7},{7,6},{8,9},{9,8},{10,11... | collective-permute-start | bytes 3686408 | tf_op jit(solution)/shard_map/ppermute | solution.py:848
  150.0 29.5 %collective-permute-start.15 = (bf16[4,40,3840]{2,1,0:T(8,128)(2,1)S(1)}, bf16[4,40,3840]{2,1,0:T(8,128)(2,1)S(1)}, u32[]{:S(2)}, u32[]{:S(2)}) collective-permute-start(bf16[4,40,3840]{2,1,0:T(8,128)(2,1)S(1)} %get-tuple-element.131.refs_0_), channel_id=1, source_target_pairs={{0,2},{1,3},{2,0},{3,1},{4,6},{5,7},{6,4},{7,5},{8,10},{9,11},{10,... | collective-permute-start | bytes 3686408 | tf_op jit(solution)/shard_map/ppermute | solution.py:848
  150.7 29.2 %collective-permute-start.14 = (bf16[4,40,3840]{2,1,0:T(8,128)(2,1)S(1)}, bf16[4,40,3840]{2,1,0:T(8,128)(2,1)S(1)}, u32[]{:S(2)}, u32[]{:S(2)}) collective-permute-start(bf16[4,40,3840]{2,1,0:T(8,128)(2,1)S(1)} %get-tuple-element.232.along_ref), channel_id=1, source_target_pairs={{0,4},{4,0},{1,5},{5,1},{2,6},{6,2},{3,7},{7,3},{8,12},{12,8},{9,1... | collective-permute-start | bytes 3686408 | tf_op jit(solution)/shard_map/ppermute | solution.py:848
  181.3 30.5 %collective-permute-start.19 = (bf16[4,40,3840]{2,1,0:T(8,128)(2,1)S(1)}, bf16[4,40,3840]{2,1,0:T(8,128)(2,1)S(1)}, u32[]{:S(2)}, u32[]{:S(2)}) collective-permute-start(bf16[4,40,3840]{2,1,0:T(8,128)(2,1)S(1)} %get-tuple-element.131.refs_0_), channel_id=1, source_target_pairs={{0,4},{4,0},{1,5},{5,1},{2,6},{6,2},{3,7},{7,3},{8,12},{12,8},{9,1... | collective-permute-start | bytes 3686408 | tf_op jit(solution)/shard_map/ppermute | solution.py:848
  182.6 20.5 %collective-permute-start.16 = (bf16[256,1280]{1,0:T(8,128)(2,1)S(1)}, bf16[256,1280]{1,0:T(8,128)(2,1)S(1)}, u32[]{:S(2)}, u32[]{:S(2)}) collective-permute-start(bf16[256,1280]{1,0:T(8,128)(2,1)S(1)} %multiply_convert_fusion.2.refs_0_), channel_id=1, source_target_pairs={{0,1},{1,0},{2,3},{3,2},{4,5},{5,4},{6,7},{7,6},{8,9},{9,8},{10,11... | collective-permute-start | bytes 1966088 | tf_op jit(solution)/shard_map/ppermute | solution.py:848
  196.9 30.0 %collective-permute-start.21 = (bf16[4,40,1920]{2,1,0:T(8,128)(2,1)}, bf16[4,40,1920]{2,1,0:T(8,128)(2,1)}, u32[]{:S(2)}, u32[]{:S(2)}) collective-permute-start(bf16[4,40,1920]{2,1,0:T(8,128)(2,1)} %slice.163), channel_id=1, source_target_pairs={{0,4},{4,0},{1,5},{5,1},{2,6},{6,2},{3,7},{7,3},{8,12},{12,8},{9,1... | collective-permute-start | bytes 1843208 | tf_op jit(solution)/shard_map/ppermute | solution.py:848
  215.1 30.9 %collective-permute-start.22 = (bf16[4,40,3840]{2,1,0:T(8,128)(2,1)S(1)}, bf16[4,40,3840]{2,1,0:T(8,128)(2,1)}, u32[]{:S(2)}, u32[]{:S(2)}) collective-permute-start(bf16[4,40,3840]{2,1,0:T(8,128)(2,1)S(1)} %get-tuple-element.131.refs_0_), channel_id=1, source_target_pairs={{0,1},{1,0},{2,3},{3,2},{4,5},{5,4},{6,7},{7,6},{8,9},{9,8},{10,11... | collective-permute-start | bytes 3686408 | tf_op jit(solution)/shard_map/ppermute | solution.py:848
  215.2 30.8 %collective-permute-start.24 = (bf16[4,40,3840]{2,1,0:T(8,128)(2,1)S(1)}, bf16[4,40,3840]{2,1,0:T(8,128)(2,1)}, u32[]{:S(2)}, u32[]{:S(2)}) collective-permute-start(bf16[4,40,3840]{2,1,0:T(8,128)(2,1)S(1)} %collective-permute-done.15.refs_2_), channel_id=1, source_target_pairs={{0,1},{1,0},{2,3},{3,2},{4,5},{5,4},{6,7},{7,6},{8,9},{9,8},{10,11... | collective-permute-start | bytes 3686408 | tf_op jit(solution)/shard_map/ppermute | solution.py:848
  215.7 30.3 %collective-permute-start.23 = (bf16[4,40,3840]{2,1,0:T(8,128)(2,1)}, bf16[4,40,3840]{2,1,0:T(8,128)(2,1)}, u32[]{:S(2)}, u32[]{:S(2)}) collective-permute-start(bf16[4,40,3840]{2,1,0:T(8,128)(2,1)} %copy-done.5), channel_id=1, source_target_pairs={{0,1},{1,0},{2,3},{3,2},{4,5},{5,4},{6,7},{7,6},{8,9},{9,8},{10,11... | collective-permute-start | bytes 3686408 | tf_op jit(solution)/shard_map/ppermute | solution.py:848
  257.0 20.5 %collective-permute-start.28 = (bf16[128,1280]{1,0:T(8,128)(2,1)S(1)}, bf16[128,1280]{1,0:T(8,128)(2,1)}, u32[]{:S(2)}, u32[]{:S(2)}) collective-permute-start(bf16[128,1280]{1,0:T(8,128)(2,1)S(1)} %dynamic-slice_bitcast_fusion.9), channel_id=1, source_target_pairs={{0,4},{4,0},{1,5},{5,1},{2,6},{6,2},{3,7},{7,3},{8,12},{12,8},{9,1... | collective-permute-start | bytes 983048 | tf_op jit(solution)/shard_map/ppermute | solution.py:848
  267.3 110.4 %reduce-scatter.5.cloned.1.call-start = ((), (), s32[]{:S(2)}) async-start(), calls=%async_computation.12 | async-start | bytes 3276800 | tf_op jit(solution)/shard_map/reduce_scatter | solution.py:898
  323.6 16.9 %collective-permute-start.33 = (bf16[2,128,1280]{2,1,0:T(8,128)(2,1)S(1)}, bf16[2,128,1280]{2,1,0:T(8,128)(2,1)}, u32[]{:S(2)}, u32[]{:S(2)}) collective-permute-start(bf16[2,128,1280]{2,1,0:T(8,128)(2,1)S(1)} %fusion.79), channel_id=1, source_target_pairs={{0,2},{1,3},{2,0},{3,1},{4,6},{5,7},{6,4},{7,5},{8,10},{9,11},{10,... | collective-permute-start | bytes 1966088 | tf_op jit(solution)/shard_map/ppermute | solution.py:848
  325.3 43.0 %collective-permute-start.34 = (bf16[4,40,3840]{2,1,0:T(8,128)(2,1)}, bf16[4,40,3840]{2,1,0:T(8,128)(2,1)}, u32[]{:S(2)}, u32[]{:S(2)}) collective-permute-start(bf16[4,40,3840]{2,1,0:T(8,128)(2,1)} %pad_maximum_fusion), channel_id=1, source_target_pairs={{0,4},{4,0},{1,5},{5,1},{2,6},{6,2},{3,7},{7,3},{8,12},{12,8},{9,1... | collective-permute-start | bytes 3686408 | tf_op jit(solution)/shard_map/ppermute | solution.py:848
  342.2 35.5 %collective-permute-start.35 = (bf16[4,40,3840]{2,1,0:T(8,128)(2,1)}, bf16[4,40,3840]{2,1,0:T(8,128)(2,1)}, u32[]{:S(2)}, u32[]{:S(2)}) collective-permute-start(bf16[4,40,3840]{2,1,0:T(8,128)(2,1)} %pad_maximum_fusion.1), channel_id=1, source_target_pairs={{0,2},{1,3},{2,0},{3,1},{4,6},{5,7},{6,4},{7,5},{8,10},{9,11},{10,... | collective-permute-start | bytes 3686408 | tf_op jit(solution)/shard_map/ppermute | solution.py:848
  354.8 22.9 %all-to-all-start.5 = ((bf16[4,320,256]{2,1,0:T(8,128)(2,1)}), bf16[4,320,256]{2,1,0:T(8,128)(2,1)S(1)}, u32[]{:S(2)}, u32[]{:S(2)}) async-start(bf16[4,320,256]{2,1,0:T(8,128)(2,1)} %bitcast.64), calls=%async_computation.5 | async-start | bytes 1310720 | tf_op jit(solution)/shard_map/all_to_all | solution.py:869
  358.3 65.4 %reduce-scatter.7.cloned.1.call-start = ((), (), s32[]{:S(2)}) async-start(), calls=%async_computation.13 | async-start | bytes 1536000 | tf_op jit(solution)/shard_map/reduce_scatter | solution.py:898
  381.5 83.5 %reduce-scatter.9.cloned.1.call-start = ((), (), s32[]{:S(2)}) async-start(), calls=%async_computation.14 | async-start | bytes 3276800 | tf_op jit(solution)/shard_map/reduce_scatter | solution.py:898
  432.3 29.5 %collective-permute-start.40 = (bf16[4,40,3840]{2,1,0:T(8,128)(2,1)S(1)}, bf16[4,40,3840]{2,1,0:T(8,128)(2,1)}, u32[]{:S(2)}, u32[]{:S(2)}) collective-permute-start(bf16[4,40,3840]{2,1,0:T(8,128)(2,1)S(1)} %pad_maximum_fusion.2), channel_id=1, source_target_pairs={{0,4},{4,0},{1,5},{5,1},{2,6},{6,2},{3,7},{7,3},{8,12},{12,8},{9,1... | collective-permute-start | bytes 3686408 | tf_op jit(solution)/shard_map/ppermute | solution.py:848
  432.9 29.3 %collective-permute-start.41 = (bf16[4,40,3840]{2,1,0:T(8,128)(2,1)S(1)}, bf16[4,40,3840]{2,1,0:T(8,128)(2,1)}, u32[]{:S(2)}, u32[]{:S(2)}) collective-permute-start(bf16[4,40,3840]{2,1,0:T(8,128)(2,1)S(1)} %pad_maximum_fusion.3), channel_id=1, source_target_pairs={{0,2},{1,3},{2,0},{3,1},{4,6},{5,7},{6,4},{7,5},{8,10},{9,11},{10,... | collective-permute-start | bytes 3686408 | tf_op jit(solution)/shard_map/ppermute | solution.py:848
  472.0 21.2 %collective-permute-start.42 = (bf16[2,128,1280]{2,1,0:T(8,128)(2,1)}, bf16[2,128,1280]{2,1,0:T(8,128)(2,1)S(1)}, u32[]{:S(2)}, u32[]{:S(2)}) collective-permute-start(bf16[2,128,1280]{2,1,0:T(8,128)(2,1)} %fusion.80), channel_id=1, source_target_pairs={{0,2},{1,3},{2,0},{3,1},{4,6},{5,7},{6,4},{7,5},{8,10},{9,11},{10,... | collective-permute-start | bytes 1966088 | tf_op jit(solution)/shard_map/ppermute | solution.py:848
  484.6 36.9 %reduce-scatter.11.cloned.1.call-start = ((), (), s32[]{:S(2)}) async-start(), calls=%async_computation.15 | async-start | bytes 1536000 | tf_op jit(solution)/shard_map/reduce_scatter | solution.py:898
  (113 other events, 963.3 us)
Sparse Core Ops, SparseCore 0:
  25.3 32.0 all-gather.6
  59.5 30.2 all-gather.8
  91.4 51.1 all-gather.10
  325.4 51.0 reduce-scatter.4
  381.6 30.1 reduce-scatter.6
  414.1 50.8 reduce-scatter.8
  487.9 30.3 reduce-scatter.10

commit v16 on v15

--- a/solution.py
+++ b/solution.py
@@ -1005,43 +1005,38 @@
     for layer in range(layers):
         normed, factor_one = normalize(stream, gains[layer])
         if layer == 1:
-            normed, next_across, beside, dense_next = tied(
-                normed.astype(BF16), next_across, beside, dense_next
-            )
+            normed = normed.astype(BF16)
             far, near = swapped(normed, "head", 2), other_core(normed)
-            across = swapped(dense_next, "blk", 1)
+            far, next_across, dense_next = tied(far, next_across, dense_next)
+            across, beside = swapped(dense_next, "blk", 1), swapped(dense_next, "head", 2)
             token_pieces = (normed, near, far, other_core(far))
             qkvs.append(assemble_wide(next_along, next_across, part3))
         normed_all, projected = project(
             token_pieces, gains[layer], qkvs[layer], layer == 0, token_rows
         )
-        if layer == 1:
-            projected, across = tied(projected, across)
-            one, two = to_beside(across), to_across(beside)
         attended, log_total = attend_rows(
             projected, scale_vecs[layer], segments, 4, token_rows
         )
+        attended, across, beside = tied(attended, across, beside)
+        one, two = to_beside(across), to_across(beside)
         if layer == 0:
-            attended, across, beside = tied(attended, across, beside)
-            one, two = to_beside(across), to_across(beside)
-        if layer == 0:
-            attended_t, one, two, next_both = tied(over_head(attended), one, two, next_both)
+            two, next_both = tied(two, next_both)
             next_along, dense_next = next_both[:, 0], next_both[:, 1]
             next_across = swapped(next_along, "blk", 1)
+            attended_t, one, two = tied(over_head(attended), one, two)
         else:
             dense_near = dense_next
-            attended, one, two, cotangent = tied(attended, one, two, cotangent)
+            attended_t, one, two, cotangent = tied(over_head(attended), one, two, cotangent)
             upper = swap_halves(cotangent)
-            attended_t, upper = tied(over_head(attended), upper)
         pieces = (dense_near, across, beside, one, two)
         pieces += tuple(other_core(piece) for piece in pieces)
-        if layer == 0:
-            beside = swapped(dense_next, "head", 2)
         attended_t = attended_t.reshape(width, -1)
         denses.append(assemble(pieces))
         dense = denses[layer]
         out_w, up_w, down_w = dense[:, :width], dense[:, width:-width], dense[:, -width:]
         middle = stream + dot_rows(attended_t, out_w)
+        if layer == 1:
+            middle, upper = tied(middle, upper)
         normed_two, factor_two = normalize(middle, gains[layers + layer])
         normed_two = normed_two.astype(BF16)
         hidden = dot(normed_two, up_w)
@@ -1092,7 +1087,7 @@
             projected, attended_grad, log_total, scale_vecs[layer], segments, token_rows
         )
         if layer == 0:
-            bars, others = tied(bars, others)
+            bars, others, z_across = tied(bars, others, z_across)
             qkv_grad = weight_back(bars, normed_all)
             bars, qkv_grad = tied(bars, qkv_grad)
             z_sum = over_batch(qkv_grad.reshape(4, 2, -1, qkv_grad.shape[-1]))
@@ -1101,16 +1096,17 @@
             diagonal = sent_beside_and_across(*rows)
             halves, to_core = rows_back(bars, qkv, token_rows)
             halves, to_core, diagonal, summed = tied(halves, to_core, diagonal, summed)
+            qkv_rows = columns_to_rows(z_across)
             halves, to_core, rows = tied(halves, to_core, neighbour_rows(cored, *diagonal))
             sent = sent_beside_and_across(*rows)
             halves = halves + other_core(to_core).astype(F32)
-            halves, sent, z_sum = tied(halves, sent, z_sum)
-            halves, own = tied(halves, own_sum(cored, *sent))
+            sent, z_sum, qkv_rows = tied(sent, z_sum, qkv_rows)
+            own, z_sum = tied(own_sum(cored, *sent), z_sum)
             dense_first = over_batch(own)
             normed_grad = scatter_row(halves)
-            normed_grad, z_across, scale_grads[0] = tied(normed_grad, z_across, scale_grads[0])
+            normed_grad, scale_grads[0] = tied(normed_grad, scale_grads[0])
             dense_grad = [dense_first, summed]
-            qkv_grads = [columns_to_rows(across_sum(z_sum)), columns_to_rows(z_across)]
+            qkv_grads = [columns_to_rows(across_sum(z_sum)), qkv_rows]
         else:
             bars, others = tied(bars, others)
             cored = (grads.astype(F32) + others.astype(F32)).astype(BF16)

time: 539 us -> 547 us (1.015)
  waiting for transfers between devices: 203 us -> 214 us
    all_to_all x8, waiting for transfers between devices: 45.9 us -> 60.9 us  [over_head(): lax.all_to_all(parts, 'head', split_axis=0, concat_axis=0, tiled=True)]
    ppermute x51, waiting for transfers between devices: 138 us -> 131 us  [swapped(): return lax.ppermute(array, axis, [(i, i ^ mask) for i in range(size)])]
    all_gather x3, waiting for transfers between devices: 15.8 us -> 21.8 us  [along_batch(): return lax.all_gather(piece, 'batch', axis=0, tiled=False)]
    unnamed x158 -> x142, local copies, waits for them, and re-layouts: 19.8 us -> 16.5 us
  transfers between devices with their start and end apart: 66 -> 66, of which waited for: 34 -> 33; matrix products, arithmetic and copies ran while one was open for 13% -> 14% of each run, Pallas kernels for 23% -> 22%
where the time goes in v16:
time: 547 us; the launch traced here: 539 us
  waiting for transfers between devices  214 us (39%)
  Pallas kernels  125 us (23%)
  starting transfers between devices  72.2 us (13%)
  other arithmetic  45.9 us (8%)
  local copies, waits for them, and re-layouts  45.1 us (8%)
  matrix products  20.4 us (4%)
  between operations  15.7 us (3%)
    ppermute x51, waiting for transfers between devices, swapped(): return lax.ppermute(array, axis, [(i, i ^ mask) for i in range(size)])  131 us
    all_to_all x8, waiting for transfers between devices, over_head(): lax.all_to_all(parts, 'head', split_axis=0, concat_axis=0, tiled=True)  60.9 us
    ppermute x51, starting transfers between devices, swapped(): return lax.ppermute(array, axis, [(i, i ^ mask) for i in range(size)])  41.9 us
    all_to_all x8, starting transfers between devices, over_head(): lax.all_to_all(parts, 'head', split_axis=0, concat_axis=0, tiled=True)  29.8 us
    pallas_call x2, Pallas kernels, attend_back_rows(): pl.pallas_call(functools.partial(attend_back_kernel, token_rows), grid=(l...  25 us
    all_gather x3, waiting for transfers between devices, along_batch(): return lax.all_gather(piece, 'batch', axis=0, tiled=False)  21.8 us
    pallas_call x2, Pallas kernels, dense_grads(): pl.pallas_call(dense_grad_kernel, grid_spec=pltpu.PrefetchScalarGridSpec(...  19.8 us
    pallas_call x2, Pallas kernels, attend_rows(): pl.pallas_call(functools.partial(attend_kernel, token_rows), grid=(local_...  18.5 us
  transfers between devices with their start and end apart: 66, of which 33 were waited for; matrix products, arithmetic and copies ran while one was open for 14% of the time, Pallas kernels for 22%

profile of v16, /device:TPU:0, one launch (start us, length us, event | category | flops | bytes accessed | tf_op | source)
XLA Modules:
  0.0 538.6 jit_solution(4718987604640464096)
XLA Ops:
  19.1 5.4 all-to-all-done
  26.4 15.2 %collective-permute-done.2.refs_2_ = bf16[256,1280]{1,0:T(8,128)(2,1)S(1)} collective-permute-done((bf16[256,1280]{1,0:T(8,128)(2,1)S(1)}, bf16[256,1280]{1,0:T(8,128)(2,1)S(1)}, u32[]{:S(2)}, u32[]{:S(2)}) %collective-permute-start.2) | collective-permute-done | bytes 655392 | tf_op jit(solution)/shard_map/ppermute | solution.py:848
  44.1 13.3 %all-gather.7.cloned.1.call-done = bf16[640,964]{1,0:T(8,128)(2,1)} async-done(((bf16[160,964]{1,0:T(8,128)(2,1)}), bf16[640,964]{1,0:T(8,128)(2,1)}) %all-gather.7.cloned.1.call-update) | async-done | bytes 1233936 | tf_op jit(solution)/shard_map/all_gather | solution.py:882
  64.3 6.6 %all-to-all-done.1 = bf16[4,40,960]{2,1,0:T(8,128)(2,1)S(1)} async-done(((bf16[4,40,960]{2,1,0:T(8,128)(2,1)}), bf16[4,40,960]{2,1,0:T(8,128)(2,1)S(1)}, u32[]{:S(2)}, u32[]{:S(2)}) %all-to-all-start.1) | async-done | bytes 307232 | tf_op jit(solution)/shard_map/all_to_all | solution.py:869
  71.1 16.5 %collective-permute-done.4.across_ref = bf16[4,160,964]{2,1,0:T(8,128)(2,1)S(1)} collective-permute-done((bf16[4,160,964]{2,1,0:T(8,128)(2,1)}, bf16[4,160,964]{2,1,0:T(8,128)(2,1)S(1)}, u32[]{:S(2)}, u32[]{:S(2)}) %collective-permute-start.4) | collective-permute-done | bytes 1233952 | tf_op jit(solution)/shard_map/ppermute | solution.py:848
  94.3 4.6 shard_map.169
  100.3 8.8 %shard_map.170 = (bf16[1024,1280]{1,0:T(8,128)(2,1)}, f32[960,1024]{1,0:T(8,128)}) custom-call(s32[3]{0:T(128)S(1)} %pad_add_fusion.place_ref.core_ref, bf16[256,1280]{1,0:T(8,128)(2,1)} %bitcast.225, bf16[256,1280]{1,0:T(8,128)(2,1)} %copy-done.51, bf16[256,1280]{1,0:T(8,128)(2,1)} %copy-done.50, bf16[256,1280]{1,0:T(8,128)(2,1)} %collective-permute-done.3.refs_3_, ...), custom_call_target="tpu_custom_call" | custom-call | flops 1048576 | bytes 1048576 | tf_op jit(solution)/shard_map/pallas_call | solution.py:711
  111.2 9.6 %shard_map.171 = (bf16[4,4,80,256]{3,2,1,0:T(8,128)(2,1)}, f32[4,1,1024]{2,1,0:T(1,128)S(1)}) custom-call(f32[3,4,80,1024]{3,2,1,0:T(8,128)S(1)} %bitcast.194, f32[80,1]{1,0:T(8,128)S(1)} %copy.60.scale_ref, s32[1024,1]{1,0:T(8,128)S(1)} %copy.61.col_ref, s32[1,1024]{1,0:T(1,128)S(1)} %constant_dynamic-slice_fusion.row_ref), custom_call_target="tpu_custom_call" | custom-call | flops 1048576 | bytes 1048576 | tf_op jit(solution)/shard_map/pallas_call | solution.py:413
  130.4 6.1 %collective-permute-done.8.refs_4_ = bf16[4,40,1920]{2,1,0:T(8,128)(2,1)} collective-permute-done((bf16[4,40,1920]{2,1,0:T(8,128)(2,1)}, bf16[4,40,1920]{2,1,0:T(8,128)(2,1)}, u32[]{:S(2)}, u32[]{:S(2)}) %collective-permute-start.8) | collective-permute-done | bytes 614432 | tf_op jit(solution)/shard_map/ppermute | solution.py:848
  136.4 6.2 %all-gather.11.cloned.1.call-done = bf16[8,40,3840]{2,1,0:T(8,128)(2,1)} async-done(((bf16[2,40,3840]{2,1,0:T(8,128)(2,1)}), bf16[8,40,3840]{2,1,0:T(8,128)(2,1)}) %all-gather.11.cloned.1.call-update) | async-done | bytes 2457616 | tf_op jit(solution)/shard_map/all_gather | solution.py:882
  149.8 4.5 shard_map.172
  162.2 15.7 %collective-permute-done.15.across_ref = bf16[4,40,3840]{2,1,0:T(8,128)(2,1)S(1)} collective-permute-done((bf16[4,40,3840]{2,1,0:T(8,128)(2,1)S(1)}, bf16[4,40,3840]{2,1,0:T(8,128)(2,1)S(1)}, u32[]{:S(2)}, u32[]{:S(2)}) %collective-permute-start.15) | collective-permute-done | bytes 1228832 | tf_op jit(solution)/shard_map/ppermute | solution.py:848
  180.6 4.8 shard_map.173
  185.4 7.8 %shard_map.174 = (bf16[1024,1280]{1,0:T(8,128)(2,1)}, f32[960,1024]{1,0:T(8,128)}) custom-call(s32[3]{0:T(128)S(1)} %pad_add_fusion.place_ref.core_ref, bf16[256,1280]{1,0:T(8,128)(2,1)} %multiply_convert_fusion.2.refs_0_, bf16[256,1280]{1,0:T(8,128)(2,1)} %collective-permute-done.16.refs_1_, bf16[256,1280]{1,0:T(8,128)(2,1)} %collective-permute-done.14.refs_2_, ...), custom_call_target="tpu_custom_call" | custom-call | flops 1048576 | bytes 1048576 | tf_op jit(solution)/shard_map/pallas_call | solution.py:711
  195.3 8.9 %shard_map.175 = (bf16[4,4,80,256]{3,2,1,0:T(8,128)(2,1)S(1)}, f32[4,1,1024]{2,1,0:T(1,128)S(1)}) custom-call(f32[3,4,80,1024]{3,2,1,0:T(8,128)S(1)} %bitcast.196, f32[80,1]{1,0:T(8,128)S(1)} %copy.64.scale_ref, s32[1024,1]{1,0:T(8,128)S(1)} %copy.61.col_ref, s32[1,1024]{1,0:T(1,128)S(1)} %constant_dynamic-slice_fusion.row_ref), custom_call_target="tpu_custom_call" | custom-call | flops 1048576 | bytes 1048576 | tf_op jit(solution)/shard_map/pallas_call | solution.py:413
  212.7 4.3 all-to-all-start.3
  218.1 14.8 %all-to-all-done.3 = bf16[4,320,256]{2,1,0:T(8,128)(2,1)} async-done(((bf16[4,320,256]{2,1,0:T(8,128)(2,1)}), bf16[4,320,256]{2,1,0:T(8,128)(2,1)}, u32[]{:S(2)}, u32[]{:S(2)}) %all-to-all-start.3) | async-done | bytes 655392 | tf_op jit(solution)/shard_map/all_to_all | solution.py:869
  234.5 7.1 %collective-permute-done.27 = bf16[128,1280]{1,0:T(8,128)(2,1)S(1)} collective-permute-done((bf16[128,1280]{1,0:T(8,128)(2,1)S(1)}, bf16[128,1280]{1,0:T(8,128)(2,1)S(1)}, u32[]{:S(2)}, u32[]{:S(2)}) %collective-permute-start.27) | collective-permute-done | bytes 327712 | tf_op jit(solution)/shard_map/ppermute | solution.py:848
  243.9 4.2 shard_map.176
  263.4 9.9 %shard_map.177 = (bf16[2,2,4,40,3840]{4,3,2,1,0:T(8,128)(2,1)}, bf16[2,2,4,40,3840]{4,3,2,1,0:T(8,128)(2,1)}) custom-call(s32[3]{0:T(128)S(1)} %pad_add_fusion.place_ref.core_ref, bf16[1280,256]{1,0:T(8,128)(2,1)} %bitcast.44.attended_ref, bf16[256,1280]{1,0:T(8,128)(2,1)} %copy-done.27, bf16[256,1280]{1,0:T(8,128)(2,1)} %copy-done.48, ...), custom_call_target="tpu_custom_call" | custom-call | flops 1048576 | bytes 1048576 | tf_op jit(solution)/shard_map/pallas_call | solution.py:577
  275.7 12.5 %shard_map.178 = (bf16[3,4,80,1024]{3,2,1,0:T(8,128)(2,1)}, f32[80,128]{1,0:T(8,128)}) custom-call(f32[3,4,80,1024]{3,2,1,0:T(8,128)} %bitcast.195, bf16[4,4,80,256]{3,2,1,0:T(8,128)(2,1)} %bitcast.56.grad_ref, f32[4,1,1024]{2,1,0:T(1,128)S(1)} %get-tuple-element.150.lse_ref, f32[80,1]{1,0:T(8,128)S(1)} %copy.64.scale_ref, s32[1024,1]{1,0:T(8,128)S(1)} %copy.61.col_ref, ...), custom_call_target="tpu_custom_call" | custom-call | flops 1048576 | bytes 1048576 | tf_op jit(solution)/shard_map/pallas_call | solution.py:506
  297.2 11.5 %shard_map.179 = (f32[2,2,128,1280]{3,2,1,0:T(8,128)}, bf16[2,2,128,1280]{3,2,1,0:T(8,128)(2,1)}, bf16[1280,960]{1,0:T(8,128)(2,1)}) custom-call(s32[3]{0:T(128)S(1)} %pad_add_fusion.place_ref.core_ref, bf16[960,1024]{1,0:T(8,128)(2,1)} %bitcast.243, bf16[1280,960]{1,0:T(8,128)(2,1)} %bitcast.213, bf16[1024,1280]{1,0:T(8,128)(2,1)} %get-tuple-element.157.normed_ref), custom_call_target="tpu_custom_call" | custom-call | flops 1048576 | bytes 1048576 | tf_op jit(solution)/shard_map/pallas_call | solution.py:757
  322.7 14.7 %collective-permute-done.33 = bf16[2,128,1280]{2,1,0:T(8,128)(2,1)} collective-permute-done((bf16[2,128,1280]{2,1,0:T(8,128)(2,1)}, bf16[2,128,1280]{2,1,0:T(8,128)(2,1)}, u32[]{:S(2)}, u32[]{:S(2)}) %collective-permute-start.33) | collective-permute-done | bytes 655392 | tf_op jit(solution)/shard_map/ppermute | solution.py:848
  354.1 10.0 %shard_map.180 = (bf16[2,2,4,40,3840]{4,3,2,1,0:T(8,128)(2,1)}, bf16[2,2,4,40,3840]{4,3,2,1,0:T(8,128)(2,1)}) custom-call(s32[3]{0:T(128)S(1)} %pad_add_fusion.place_ref.core_ref, bf16[1280,256]{1,0:T(8,128)(2,1)} %bitcast.238, bf16[256,1280]{1,0:T(8,128)(2,1)} %copy-done.26, bf16[256,1280]{1,0:T(8,128)(2,1)} %copy-done.44, bf16[256,1280]{1,0:T(8,128)(2,1)} %copy-done.32, ...), custom_call_target="tpu_custom_call" | custom-call | flops 1048576 | bytes 1048576 | tf_op jit(solution)/shard_map/pallas_call | solution.py:577
  364.0 10.5 %all-to-all-done.5 = bf16[4,320,256]{2,1,0:T(8,128)(2,1)S(1)} async-done(((bf16[4,320,256]{2,1,0:T(8,128)(2,1)}), bf16[4,320,256]{2,1,0:T(8,128)(2,1)S(1)}, u32[]{:S(2)}, u32[]{:S(2)}) %all-to-all-start.5) | async-done | bytes 655392 | tf_op jit(solution)/shard_map/all_to_all | solution.py:869
  380.7 12.6 %shard_map.181 = (bf16[3,4,80,1024]{3,2,1,0:T(8,128)(2,1)}, f32[80,128]{1,0:T(8,128)}) custom-call(f32[3,4,80,1024]{3,2,1,0:T(8,128)} %bitcast.193, bf16[4,4,80,256]{3,2,1,0:T(8,128)(2,1)} %bitcast.240, f32[4,1,1024]{2,1,0:T(1,128)S(1)} %get-tuple-element.177.lse_ref, f32[80,1]{1,0:T(8,128)S(1)} %copy.60.scale_ref, s32[1024,1]{1,0:T(8,128)S(1)} %copy.61.col_ref, ...), custom_call_target="tpu_custom_call" | custom-call | flops 1048576 | bytes 1048576 | tf_op jit(solution)/shard_map/pallas_call | solution.py:506
  395.2 7.4 %shard_map.182 = bf16[1280,960]{1,0:T(8,128)(2,1)} custom-call(bf16[960,1024]{1,0:T(8,128)(2,1)} %bitcast.229, bf16[1024,1280]{1,0:T(8,128)(2,1)} %get-tuple-element.182.normed_ref), custom_call_target="tpu_custom_call" | custom-call | flops 1048576 | bytes 1048576 | tf_op jit(solution)/shard_map/pallas_call | solution.py:828
  414.7 8.1 %shard_map.183 = (f32[2,2,128,1280]{3,2,1,0:T(8,128)}, bf16[2,2,128,1280]{3,2,1,0:T(8,128)(2,1)}) custom-call(s32[3]{0:T(128)S(1)} %pad_add_fusion.place_ref.core_ref, bf16[960,1024]{1,0:T(8,128)(2,1)} %bitcast.230, bf16[1280,960]{1,0:T(8,128)(2,1)} %bitcast.222), custom_call_target="tpu_custom_call" | custom-call | flops 1048576 | bytes 1048576 | tf_op jit(solution)/shard_map/pallas_call | solution.py:798
  443.9 15.0 %all-to-all-done.6 = bf16[4,40,960]{2,1,0:T(8,128)(2,1)S(1)} async-done(((bf16[4,40,960]{2,1,0:T(8,128)(2,1)}), bf16[4,40,960]{2,1,0:T(8,128)(2,1)S(1)}, u32[]{:S(2)}, u32[]{:S(2)}) %all-to-all-start.6) | async-done | bytes 307232 | tf_op jit(solution)/shard_map/all_to_all | solution.py:869
  467.1 23.4 %collective-permute-done.47 = f32[2,80]{1,0:T(2,128)S(1)} collective-permute-done((f32[2,80]{1,0:T(2,128)S(1)}, f32[2,80]{1,0:T(2,128)S(1)}, u32[]{:S(2)}, u32[]{:S(2)}) %collective-permute-start.47) | collective-permute-done | bytes 672 | tf_op jit(solution)/shard_map/ppermute | solution.py:848
  505.6 5.2 collective-permute-done.42
  519.8 5.6 %all-to-all-done.7 = bf16[4,40,960]{2,1,0:T(8,128)(2,1)S(1)} async-done(((bf16[4,40,960]{2,1,0:T(8,128)(2,1)}), bf16[4,40,960]{2,1,0:T(8,128)(2,1)S(1)}, u32[]{:S(2)}, u32[]{:S(2)}) %all-to-all-start.7) | async-done | bytes 307232 | tf_op jit(solution)/shard_map/all_to_all | solution.py:869
  (391 shorter events, 212.3 us)
Async XLA Ops:
  17.7 39.7 %all-gather.7.cloned.1.call-start = ((), (), s32[]{:S(2)}) async-start(), calls=%async_computation.16 | async-start | bytes 1638400 | tf_op jit(solution)/shard_map/all_gather | solution.py:882
  25.2 64.7 %all-gather.9.cloned.1.call-start = ((), (), s32[]{:S(2)}) async-start(), calls=%async_computation.17 | async-start | bytes 1536000 | tf_op jit(solution)/shard_map/all_gather | solution.py:882
  57.4 30.1 %collective-permute-start.4 = (bf16[4,160,964]{2,1,0:T(8,128)(2,1)}, bf16[4,160,964]{2,1,0:T(8,128)(2,1)S(1)}, u32[]{:S(2)}, u32[]{:S(2)}) collective-permute-start(bf16[4,160,964]{2,1,0:T(8,128)(2,1)} %bitcast.247), channel_id=1, source_target_pairs={{0,4},{4,0},{1,5},{5,1},{2,6},{6,2},{3,7},{7,3},{8,12},{12,8},{9,1... | collective-permute-start | bytes 3701768 | tf_op jit(solution)/shard_map/ppermute | solution.py:848
  64.2 78.5 %all-gather.11.cloned.1.call-start = ((), (), s32[]{:S(2)}) async-start(), calls=%async_computation.18 | async-start | bytes 3072000 | tf_op jit(solution)/shard_map/all_gather | solution.py:882
  90.8 30.0 %collective-permute-start.6 = (bf16[4,40,3840]{2,1,0:T(8,128)(2,1)}, bf16[4,40,3840]{2,1,0:T(8,128)(2,1)S(1)}, u32[]{:S(2)}, u32[]{:S(2)}) collective-permute-start(bf16[4,40,3840]{2,1,0:T(8,128)(2,1)} %bitcast.15.refs_0_), channel_id=1, source_target_pairs={{0,2},{1,3},{2,0},{3,1},{4,6},{5,7},{6,4},{7,5},{8,10},{9,11},{10,... | collective-permute-start | bytes 3686408 | tf_op jit(solution)/shard_map/ppermute | solution.py:848
  92.4 28.5 %collective-permute-start.5 = (bf16[4,40,3840]{2,1,0:T(8,128)(2,1)}, bf16[4,40,3840]{2,1,0:T(8,128)(2,1)}, u32[]{:S(2)}, u32[]{:S(2)}) collective-permute-start(bf16[4,40,3840]{2,1,0:T(8,128)(2,1)} %bitcast.15.refs_0_), channel_id=1, source_target_pairs={{0,4},{4,0},{1,5},{5,1},{2,6},{6,2},{3,7},{7,3},{8,12},{12,8},{9,1... | collective-permute-start | bytes 3686408 | tf_op jit(solution)/shard_map/ppermute | solution.py:848
  124.8 20.9 %collective-permute-start.7 = (bf16[4,40,1920]{2,1,0:T(8,128)(2,1)}, bf16[4,40,1920]{2,1,0:T(8,128)(2,1)}, u32[]{:S(2)}, u32[]{:S(2)}) collective-permute-start(bf16[4,40,1920]{2,1,0:T(8,128)(2,1)} %slice.149), channel_id=1, source_target_pairs={{0,2},{1,3},{2,0},{3,1},{4,6},{5,7},{6,4},{7,5},{8,10},{9,11},{10,... | collective-permute-start | bytes 1843208 | tf_op jit(solution)/shard_map/ppermute | solution.py:848
  125.4 20.4 %all-to-all-start.2 = ((bf16[4,320,256]{2,1,0:T(8,128)(2,1)}), bf16[4,320,256]{2,1,0:T(8,128)(2,1)S(1)}, u32[]{:S(2)}, u32[]{:S(2)}) async-start(bf16[4,320,256]{2,1,0:T(8,128)(2,1)} %bitcast.27), calls=%async_computation.2 | async-start | bytes 1310720 | tf_op jit(solution)/shard_map/all_to_all | solution.py:869
  129.9 19.9 %collective-permute-start.10 = (bf16[4,40,3840]{2,1,0:T(8,128)(2,1)}, bf16[4,40,3840]{2,1,0:T(8,128)(2,1)}, u32[]{:S(2)}, u32[]{:S(2)}) collective-permute-start(bf16[4,40,3840]{2,1,0:T(8,128)(2,1)} %collective-permute-done.5.refs_1_), channel_id=1, source_target_pairs={{0,1},{1,0},{2,3},{3,2},{4,5},{5,4},{6,7},{7,6},{8,9},{9,8},{10,11... | collective-permute-start | bytes 3686408 | tf_op jit(solution)/shard_map/ppermute | solution.py:848
  130.0 19.9 %collective-permute-start.11 = (bf16[4,40,3840]{2,1,0:T(8,128)(2,1)S(1)}, bf16[4,40,3840]{2,1,0:T(8,128)(2,1)}, u32[]{:S(2)}, u32[]{:S(2)}) collective-permute-start(bf16[4,40,3840]{2,1,0:T(8,128)(2,1)S(1)} %collective-permute-done.6.refs_2_), channel_id=1, source_target_pairs={{0,1},{1,0},{2,3},{3,2},{4,5},{5,4},{6,7},{7,6},{8,9},{9,8},{10,11... | collective-permute-start | bytes 3686408 | tf_op jit(solution)/shard_map/ppermute | solution.py:848
  148.5 29.5 %collective-permute-start.15 = (bf16[4,40,3840]{2,1,0:T(8,128)(2,1)S(1)}, bf16[4,40,3840]{2,1,0:T(8,128)(2,1)S(1)}, u32[]{:S(2)}, u32[]{:S(2)}) collective-permute-start(bf16[4,40,3840]{2,1,0:T(8,128)(2,1)S(1)} %get-tuple-element.234.along_ref), channel_id=1, source_target_pairs={{0,4},{4,0},{1,5},{5,1},{2,6},{6,2},{3,7},{7,3},{8,12},{12,8},{9,1... | collective-permute-start | bytes 3686408 | tf_op jit(solution)/shard_map/ppermute | solution.py:848
  178.7 28.3 %collective-permute-start.19 = (bf16[4,40,3840]{2,1,0:T(8,128)(2,1)S(1)}, bf16[4,40,3840]{2,1,0:T(8,128)(2,1)S(1)}, u32[]{:S(2)}, u32[]{:S(2)}) collective-permute-start(bf16[4,40,3840]{2,1,0:T(8,128)(2,1)S(1)} %get-tuple-element.133.refs_0_), channel_id=1, source_target_pairs={{0,2},{1,3},{2,0},{3,1},{4,6},{5,7},{6,4},{7,5},{8,10},{9,11},{10,... | collective-permute-start | bytes 3686408 | tf_op jit(solution)/shard_map/ppermute | solution.py:848
  179.4 28.2 %collective-permute-start.18 = (bf16[4,40,3840]{2,1,0:T(8,128)(2,1)S(1)}, bf16[4,40,3840]{2,1,0:T(8,128)(2,1)}, u32[]{:S(2)}, u32[]{:S(2)}) collective-permute-start(bf16[4,40,3840]{2,1,0:T(8,128)(2,1)S(1)} %get-tuple-element.133.refs_0_), channel_id=1, source_target_pairs={{0,4},{4,0},{1,5},{5,1},{2,6},{6,2},{3,7},{7,3},{8,12},{12,8},{9,1... | collective-permute-start | bytes 3686408 | tf_op jit(solution)/shard_map/ppermute | solution.py:848
  210.4 22.5 %collective-permute-start.21 = (bf16[4,40,1920]{2,1,0:T(8,128)(2,1)}, bf16[4,40,1920]{2,1,0:T(8,128)(2,1)}, u32[]{:S(2)}, u32[]{:S(2)}) collective-permute-start(bf16[4,40,1920]{2,1,0:T(8,128)(2,1)} %slice.163), channel_id=1, source_target_pairs={{0,4},{4,0},{1,5},{5,1},{2,6},{6,2},{3,7},{7,3},{8,12},{12,8},{9,1... | collective-permute-start | bytes 1843208 | tf_op jit(solution)/shard_map/ppermute | solution.py:848
  211.4 21.5 %collective-permute-start.20 = (bf16[4,40,1920]{2,1,0:T(8,128)(2,1)}, bf16[4,40,1920]{2,1,0:T(8,128)(2,1)}, u32[]{:S(2)}, u32[]{:S(2)}) collective-permute-start(bf16[4,40,1920]{2,1,0:T(8,128)(2,1)} %slice.162), channel_id=1, source_target_pairs={{0,2},{1,3},{2,0},{3,1},{4,6},{5,7},{6,4},{7,5},{8,10},{9,11},{10,... | collective-permute-start | bytes 1843208 | tf_op jit(solution)/shard_map/ppermute | solution.py:848
  212.7 20.2 %all-to-all-start.3 = ((bf16[4,320,256]{2,1,0:T(8,128)(2,1)}), bf16[4,320,256]{2,1,0:T(8,128)(2,1)}, u32[]{:S(2)}, u32[]{:S(2)}) async-start(bf16[4,320,256]{2,1,0:T(8,128)(2,1)} %bitcast.211), calls=%async_computation.3 | async-start | bytes 1310720 | tf_op jit(solution)/shard_map/all_to_all | solution.py:869
  217.0 25.7 %collective-permute-start.22 = (bf16[4,40,3840]{2,1,0:T(8,128)(2,1)S(1)}, bf16[4,40,3840]{2,1,0:T(8,128)(2,1)}, u32[]{:S(2)}, u32[]{:S(2)}) collective-permute-start(bf16[4,40,3840]{2,1,0:T(8,128)(2,1)S(1)} %get-tuple-element.133.refs_0_), channel_id=1, source_target_pairs={{0,1},{1,0},{2,3},{3,2},{4,5},{5,4},{6,7},{7,6},{8,9},{9,8},{10,11... | collective-permute-start | bytes 3686408 | tf_op jit(solution)/shard_map/ppermute | solution.py:848
  217.6 26.3 %collective-permute-start.23 = (bf16[4,40,3840]{2,1,0:T(8,128)(2,1)}, bf16[4,40,3840]{2,1,0:T(8,128)(2,1)}, u32[]{:S(2)}, u32[]{:S(2)}) collective-permute-start(bf16[4,40,3840]{2,1,0:T(8,128)(2,1)} %collective-permute-done.18.refs_1_), channel_id=1, source_target_pairs={{0,1},{1,0},{2,3},{3,2},{4,5},{5,4},{6,7},{7,6},{8,9},{9,8},{10,11... | collective-permute-start | bytes 3686408 | tf_op jit(solution)/shard_map/ppermute | solution.py:848
  217.7 26.2 %collective-permute-start.24 = (bf16[4,40,3840]{2,1,0:T(8,128)(2,1)S(1)}, bf16[4,40,3840]{2,1,0:T(8,128)(2,1)}, u32[]{:S(2)}, u32[]{:S(2)}) collective-permute-start(bf16[4,40,3840]{2,1,0:T(8,128)(2,1)S(1)} %collective-permute-done.19.refs_2_), channel_id=1, source_target_pairs={{0,1},{1,0},{2,3},{3,2},{4,5},{5,4},{6,7},{7,6},{8,9},{9,8},{10,11... | collective-permute-start | bytes 3686408 | tf_op jit(solution)/shard_map/ppermute | solution.py:848
  253.7 19.6 %collective-permute-start.28 = (bf16[128,1280]{1,0:T(8,128)(2,1)}, bf16[128,1280]{1,0:T(8,128)(2,1)}, u32[]{:S(2)}, u32[]{:S(2)}) collective-permute-start(bf16[128,1280]{1,0:T(8,128)(2,1)} %dynamic-slice_bitcast_fusion.9), channel_id=1, source_target_pairs={{0,4},{4,0},{1,5},{5,1},{2,6},{6,2},{3,7},{7,3},{8,12},{12,8},{9,1... | collective-permute-start | bytes 983048 | tf_op jit(solution)/shard_map/ppermute | solution.py:848
  263.2 111.4 %reduce-scatter.5.cloned.1.call-start = ((), (), s32[]{:S(2)}) async-start(), calls=%async_computation.12 | async-start | bytes 3276800 | tf_op jit(solution)/shard_map/reduce_scatter | solution.py:898
  322.0 42.0 %collective-permute-start.34 = (bf16[4,40,3840]{2,1,0:T(8,128)(2,1)}, bf16[4,40,3840]{2,1,0:T(8,128)(2,1)}, u32[]{:S(2)}, u32[]{:S(2)}) collective-permute-start(bf16[4,40,3840]{2,1,0:T(8,128)(2,1)} %pad_maximum_fusion), channel_id=1, source_target_pairs={{0,4},{4,0},{1,5},{5,1},{2,6},{6,2},{3,7},{7,3},{8,12},{12,8},{9,1... | collective-permute-start | bytes 3686408 | tf_op jit(solution)/shard_map/ppermute | solution.py:848
  339.0 35.6 %collective-permute-start.35 = (bf16[4,40,3840]{2,1,0:T(8,128)(2,1)}, bf16[4,40,3840]{2,1,0:T(8,128)(2,1)}, u32[]{:S(2)}, u32[]{:S(2)}) collective-permute-start(bf16[4,40,3840]{2,1,0:T(8,128)(2,1)} %pad_maximum_fusion.1), channel_id=1, source_target_pairs={{0,2},{1,3},{2,0},{3,1},{4,6},{5,7},{6,4},{7,5},{8,10},{9,11},{10,... | collective-permute-start | bytes 3686408 | tf_op jit(solution)/shard_map/ppermute | solution.py:848
  350.5 24.0 %all-to-all-start.5 = ((bf16[4,320,256]{2,1,0:T(8,128)(2,1)}), bf16[4,320,256]{2,1,0:T(8,128)(2,1)S(1)}, u32[]{:S(2)}, u32[]{:S(2)}) async-start(bf16[4,320,256]{2,1,0:T(8,128)(2,1)} %bitcast.255), calls=%async_computation.5 | async-start | bytes 1310720 | tf_op jit(solution)/shard_map/all_to_all | solution.py:869
  354.0 68.8 %reduce-scatter.7.cloned.1.call-start = ((), (), s32[]{:S(2)}) async-start(), calls=%async_computation.13 | async-start | bytes 1536000 | tf_op jit(solution)/shard_map/reduce_scatter | solution.py:898
  374.5 20.7 %collective-permute-start.36 = (bf16[2,2,4,40,3840]{4,3,2,1,0:T(8,128)(2,1)}, bf16[2,2,4,40,3840]{4,3,2,1,0:T(8,128)(2,1)}, u32[]{:S(2)}, u32[]{:S(2)}) collective-permute-start(bf16[2,2,4,40,3840]{4,3,2,1,0:T(8,128)(2,1)} %get-tuple-element.179), channel_id=1, source_target_pairs={{0,1},{1,0},{2,3},{3,2},{4,5},{5,4},{6,7},{7,6},{8,9},{9,8},{10,11... | collective-permute-start | bytes 14745608 | tf_op jit(solution)/shard_map/ppermute | solution.py:848
  380.6 114.7 %reduce-scatter.9.cloned.1.call-start = ((), (), s32[]{:S(2)}) async-start(), calls=%async_computation.14 | async-start | bytes 3276800 | tf_op jit(solution)/shard_map/reduce_scatter | solution.py:898
  438.4 25.4 %collective-permute-start.41 = (bf16[2,128,1280]{2,1,0:T(8,128)(2,1)}, bf16[2,128,1280]{2,1,0:T(8,128)(2,1)}, u32[]{:S(2)}, u32[]{:S(2)}) collective-permute-start(bf16[2,128,1280]{2,1,0:T(8,128)(2,1)} %fusion.80), channel_id=1, source_target_pairs={{0,2},{1,3},{2,0},{3,1},{4,6},{5,7},{6,4},{7,5},{8,10},{9,11},{10,... | collective-permute-start | bytes 1966088 | tf_op jit(solution)/shard_map/ppermute | solution.py:848
  443.6 85.2 %reduce-scatter.11.cloned.1.call-start = ((), (), s32[]{:S(2)}) async-start(), calls=%async_computation.15 | async-start | bytes 1536000 | tf_op jit(solution)/shard_map/reduce_scatter | solution.py:898
  461.1 34.3 %collective-permute-start.43 = (bf16[4,40,3840]{2,1,0:T(8,128)(2,1)}, bf16[4,40,3840]{2,1,0:T(8,128)(2,1)}, u32[]{:S(2)}, u32[]{:S(2)}) collective-permute-start(bf16[4,40,3840]{2,1,0:T(8,128)(2,1)} %pad_maximum_fusion.2), channel_id=1, source_target_pairs={{0,4},{4,0},{1,5},{5,1},{2,6},{6,2},{3,7},{7,3},{8,12},{12,8},{9,1... | collective-permute-start | bytes 3686408 | tf_op jit(solution)/shard_map/ppermute | solution.py:848
  462.1 33.3 %collective-permute-start.44 = (bf16[4,40,3840]{2,1,0:T(8,128)(2,1)}, bf16[4,40,3840]{2,1,0:T(8,128)(2,1)}, u32[]{:S(2)}, u32[]{:S(2)}) collective-permute-start(bf16[4,40,3840]{2,1,0:T(8,128)(2,1)} %pad_maximum_fusion.3), channel_id=1, source_target_pairs={{0,2},{1,3},{2,0},{3,1},{4,6},{5,7},{6,4},{7,5},{8,10},{9,11},{10,... | collective-permute-start | bytes 3686408 | tf_op jit(solution)/shard_map/ppermute | solution.py:848
  466.7 23.8 %collective-permute-start.47 = (f32[2,80]{1,0:T(2,128)S(1)}, f32[2,80]{1,0:T(2,128)S(1)}, u32[]{:S(2)}, u32[]{:S(2)}) collective-permute-start(f32[2,80]{1,0:T(2,128)S(1)} %fusion.92), channel_id=1, source_target_pairs={{0,2},{1,3},{2,0},{3,1},{4,6},{5,7},{6,4},{7,5},{8,10},{9,11},{10,... | collective-permute-start | bytes 1928 | tf_op jit(solution)/shard_map/ppermute | solution.py:848
  (105 other events, 852.3 us)
Sparse Core Ops, SparseCore 0:
  25.3 32.0 all-gather.6
  59.5 30.2 all-gather.8
  91.4 51.1 all-gather.10
  322.1 50.5 reduce-scatter.4
  380.7 29.9 reduce-scatter.6
  414.8 50.6 reduce-scatter.8
  499.0 29.4 reduce-scatter.10

commit v17 on v16

--- a/solution.py
+++ b/solution.py
@@ -904,8 +904,7 @@
     return (pick(halves, blk).astype(F32) + got).astype(BF16)
 
 
-def columns_to_rows(summed):
-    moved = over_head(summed.reshape(4, -1, summed.shape[-1]))
+def columns_to_rows(moved):
     rows = moved.shape[1]
     return moved.reshape(4, rows, 3, -1).transpose(1, 2, 0, 3).reshape(rows, -1).astype(F32)
 
@@ -945,8 +944,8 @@
     return own.astype(F32) + across.astype(F32) + beside.astype(F32)
 
 
-def sum_all(array):
-    for axis, mask in (("head", 1), ("head", 2), ("blk", 1), ("batch", 1), ("batch", 2)):
+def sum_over(array, *hops):
+    for axis, mask in hops:
         array = array + swapped(array, axis, mask)
     return array
 
@@ -989,7 +988,10 @@
     along = along_batch(columns)
     far, near = swapped(first, "head", 2), other_core(first)
     both = other_core(far)
-    along, near, far, both, dense_near = tied(along, near, far, both, dense_own[0])
+    upper = swap_halves(cotangent)
+    along, near, far, both, dense_near, upper = tied(
+        along, near, far, both, dense_own[0], upper
+    )
     token_pieces = (first, near, far, both)
     dense_near = along_batch(dense_near)
     qkv_across = swapped(along, "blk", 1)
@@ -1026,8 +1028,7 @@
             attended_t, one, two = tied(over_head(attended), one, two)
         else:
             dense_near = dense_next
-            attended_t, one, two, cotangent = tied(over_head(attended), one, two, cotangent)
-            upper = swap_halves(cotangent)
+            attended_t, one, two = tied(over_head(attended), one, two)
         pieces = (dense_near, across, beside, one, two)
         pieces += tuple(other_core(piece) for piece in pieces)
         attended_t = attended_t.reshape(width, -1)
@@ -1035,8 +1036,6 @@
         dense = denses[layer]
         out_w, up_w, down_w = dense[:, :width], dense[:, width:-width], dense[:, -width:]
         middle = stream + dot_rows(attended_t, out_w)
-        if layer == 1:
-            middle, upper = tied(middle, upper)
         normed_two, factor_two = normalize(middle, gains[layers + layer])
         normed_two = normed_two.astype(BF16)
         hidden = dot(normed_two, up_w)
@@ -1088,25 +1087,27 @@
         )
         if layer == 0:
             bars, others, z_across = tied(bars, others, z_across)
+            moved = over_head(z_across.reshape(4, -1, z_across.shape[-1]))
             qkv_grad = weight_back(bars, normed_all)
-            bars, qkv_grad = tied(bars, qkv_grad)
+            bars, qkv_grad, moved = tied(bars, qkv_grad, moved)
             z_sum = over_batch(qkv_grad.reshape(4, 2, -1, qkv_grad.shape[-1]))
             cored = (grads.astype(F32) + others.astype(F32)).astype(BF16)
             bars, rows = tied(bars, diagonal_rows(cored))
             diagonal = sent_beside_and_across(*rows)
             halves, to_core = rows_back(bars, qkv, token_rows)
             halves, to_core, diagonal, summed = tied(halves, to_core, diagonal, summed)
-            qkv_rows = columns_to_rows(z_across)
             halves, to_core, rows = tied(halves, to_core, neighbour_rows(cored, *diagonal))
             sent = sent_beside_and_across(*rows)
             halves = halves + other_core(to_core).astype(F32)
-            sent, z_sum, qkv_rows = tied(sent, z_sum, qkv_rows)
-            own, z_sum = tied(own_sum(cored, *sent), z_sum)
+            scale_sum = sum_over(jnp.stack(scale_grads), ("head", 1), ("batch", 1), ("batch", 2))
+            halves, sent, z_sum, scale_sum = tied(halves, sent, z_sum, scale_sum)
+            halves, own = tied(halves, own_sum(cored, *sent))
             dense_first = over_batch(own)
             normed_grad = scatter_row(halves)
-            normed_grad, scale_grads[0] = tied(normed_grad, scale_grads[0])
             dense_grad = [dense_first, summed]
-            qkv_grads = [columns_to_rows(across_sum(z_sum)), qkv_rows]
+            z_across = across_sum(z_sum)
+            z_across = over_head(z_across.reshape(4, -1, z_across.shape[-1]))
+            qkv_grads = [columns_to_rows(z_across), columns_to_rows(moved)]
         else:
             bars, others = tied(bars, others)
             cored = (grads.astype(F32) + others.astype(F32)).astype(BF16)
@@ -1123,7 +1124,7 @@
             beside = swapped(beside, "head", 2)
         upper = middle_grad + lower_of(normed_grad, stream, factor_one, gains[layer])
     input_grad = swap_halves(upper.astype(BF16).reshape(tokens.shape)).astype(F32)
-    scale_total = sum_all(jnp.stack(scale_grads))
+    scale_total = sum_over(scale_sum, ("head", 2), ("blk", 1))
     scale_grad = scale_total * (SCALE_BASE / math.sqrt(head_dim)) * jax.nn.sigmoid(scale_param)
     dense_all = jnp.stack([part.astype(F32) for part in dense_grad])
     qkv_all = jnp.stack(qkv_grads)

time: 547 us -> 536 us (0.980)
  waiting for transfers between devices: 214 us -> 189 us
  blocking collectives: 0 us -> 19.3 us
    all_to_all x8 -> x7, waiting for transfers between devices: 60.9 us -> 19.3 us  [over_head(): lax.all_to_all(parts, 'head', split_axis=0, concat_axis=0, tiled=True)]
    all_to_all x0 -> x1, blocking collectives: none -> 19.3 us  [over_head(): lax.all_to_all(parts, 'head', split_axis=0, concat_axis=0, tiled=True)]
    reduce_scatter x4, waiting for transfers between devices: 0.01 us -> 13.7 us  [over_batch(): lax.psum_scatter(parts.astype(BF16), 'batch', scatter_dimension=0, tiled=...]
    all_to_all x8 -> x7, starting transfers between devices: 29.8 us -> 25.9 us  [over_head(): lax.all_to_all(parts, 'head', split_axis=0, concat_axis=0, tiled=True)]
    unnamed x142 -> x138, local copies, waits for them, and re-layouts: 16.5 us -> 19.2 us
  transfers between devices with their start and end apart: 66 -> 65, of which waited for: 33 -> 31; matrix products, arithmetic and copies ran while one was open for 14% -> 13% of each run, Pallas kernels for 22% -> 23%
where the time goes in v17:
time: 536 us; the launch traced here: 528 us
  waiting for transfers between devices  189 us (35%)
  Pallas kernels  124 us (23%)
  starting transfers between devices  70.9 us (13%)
  other arithmetic  45.7 us (9%)
  local copies, waits for them, and re-layouts  44.3 us (8%)
  matrix products  19.6 us (4%)
  blocking collectives  19.3 us (4%)
  between operations  15.9 us (3%)
    ppermute x51, waiting for transfers between devices, swapped(): return lax.ppermute(array, axis, [(i, i ^ mask) for i in range(size)])  132 us
    ppermute x51, starting transfers between devices, swapped(): return lax.ppermute(array, axis, [(i, i ^ mask) for i in range(size)])  44.6 us
    all_to_all x7, starting transfers between devices, over_head(): lax.all_to_all(parts, 'head', split_axis=0, concat_axis=0, tiled=True)  25.9 us
    pallas_call x2, Pallas kernels, attend_back_rows(): pl.pallas_call(functools.partial(attend_back_kernel, token_rows), grid=(l...  24.8 us
    all_gather x3, waiting for transfers between devices, along_batch(): return lax.all_gather(piece, 'batch', axis=0, tiled=False)  23.7 us
    pallas_call x2, Pallas kernels, dense_grads(): pl.pallas_call(dense_grad_kernel, grid_spec=pltpu.PrefetchScalarGridSpec(...  19.8 us
    all_to_all x1, blocking collectives, over_head(): lax.all_to_all(parts, 'head', split_axis=0, concat_axis=0, tiled=True)  19.3 us
    all_to_all x7, waiting for transfers between devices, over_head(): lax.all_to_all(parts, 'head', split_axis=0, concat_axis=0, tiled=True)  19.3 us
  transfers between devices with their start and end apart: 65, of which 31 were waited for; matrix products, arithmetic and copies ran while one was open for 13% of the time, Pallas kernels for 23%

profile of v17, /device:TPU:0, one launch (start us, length us, event | category | flops | bytes accessed | tf_op | source)
XLA Modules:
  0.0 528.3 jit_solution(17239864968368785618)
XLA Ops:
  17.9 8.1 %collective-permute-done = bf16[128,1280]{1,0:T(8,128)(2,1)S(1)} collective-permute-done((bf16[128,1280]{1,0:T(8,128)(2,1)S(1)}, bf16[128,1280]{1,0:T(8,128)(2,1)S(1)}, u32[]{:S(2)}, u32[]{:S(2)}) %collective-permute-start) | collective-permute-done | bytes 327712 | tf_op jit(solution)/shard_map/ppermute | solution.py:848
  30.6 12.4 %collective-permute-done.2.refs_2_ = bf16[256,1280]{1,0:T(8,128)(2,1)S(1)} collective-permute-done((bf16[256,1280]{1,0:T(8,128)(2,1)S(1)}, bf16[256,1280]{1,0:T(8,128)(2,1)S(1)}, u32[]{:S(2)}, u32[]{:S(2)}) %collective-permute-start.2) | collective-permute-done | bytes 655392 | tf_op jit(solution)/shard_map/ppermute | solution.py:848
  46.1 15.2 %all-gather.7.cloned.1.call-done = bf16[640,964]{1,0:T(8,128)(2,1)} async-done(((bf16[160,964]{1,0:T(8,128)(2,1)}), bf16[640,964]{1,0:T(8,128)(2,1)}) %all-gather.7.cloned.1.call-update) | async-done | bytes 1233936 | tf_op jit(solution)/shard_map/all_gather | solution.py:882
  68.1 6.6 %all-to-all-done.1 = bf16[4,40,960]{2,1,0:T(8,128)(2,1)S(1)} async-done(((bf16[4,40,960]{2,1,0:T(8,128)(2,1)}), bf16[4,40,960]{2,1,0:T(8,128)(2,1)S(1)}, u32[]{:S(2)}, u32[]{:S(2)}) %all-to-all-start.1) | async-done | bytes 307232 | tf_op jit(solution)/shard_map/all_to_all | solution.py:869
  74.9 16.5 %collective-permute-done.5.across_ref = bf16[4,160,964]{2,1,0:T(8,128)(2,1)S(1)} collective-permute-done((bf16[4,160,964]{2,1,0:T(8,128)(2,1)}, bf16[4,160,964]{2,1,0:T(8,128)(2,1)S(1)}, u32[]{:S(2)}, u32[]{:S(2)}) %collective-permute-start.5) | collective-permute-done | bytes 1233952 | tf_op jit(solution)/shard_map/ppermute | solution.py:848
  98.2 4.6 shard_map.169
  104.2 8.9 %shard_map.170 = (bf16[1024,1280]{1,0:T(8,128)(2,1)}, f32[960,1024]{1,0:T(8,128)}) custom-call(s32[3]{0:T(128)S(1)} %pad_add_fusion.place_ref.core_ref, bf16[256,1280]{1,0:T(8,128)(2,1)} %bitcast.227, bf16[256,1280]{1,0:T(8,128)(2,1)} %copy-done.53, bf16[256,1280]{1,0:T(8,128)(2,1)} %copy-done.52, bf16[256,1280]{1,0:T(8,128)(2,1)} %collective-permute-done.3.refs_3_, ...), custom_call_target="tpu_custom_call" | custom-call | flops 1048576 | bytes 1048576 | tf_op jit(solution)/shard_map/pallas_call | solution.py:711
  115.2 9.6 %shard_map.171 = (bf16[4,4,80,256]{3,2,1,0:T(8,128)(2,1)}, f32[4,1,1024]{2,1,0:T(1,128)S(1)}) custom-call(f32[3,4,80,1024]{3,2,1,0:T(8,128)S(1)} %bitcast.198, f32[80,1]{1,0:T(8,128)S(1)} %copy.60.scale_ref, s32[1024,1]{1,0:T(8,128)S(1)} %copy.61.col_ref, s32[1,1024]{1,0:T(1,128)S(1)} %constant_dynamic-slice_fusion.row_ref), custom_call_target="tpu_custom_call" | custom-call | flops 1048576 | bytes 1048576 | tf_op jit(solution)/shard_map/pallas_call | solution.py:413
  134.1 6.2 %collective-permute-done.9.refs_4_ = bf16[4,40,1920]{2,1,0:T(8,128)(2,1)} collective-permute-done((bf16[4,40,1920]{2,1,0:T(8,128)(2,1)}, bf16[4,40,1920]{2,1,0:T(8,128)(2,1)}, u32[]{:S(2)}, u32[]{:S(2)}) %collective-permute-start.9) | collective-permute-done | bytes 614432 | tf_op jit(solution)/shard_map/ppermute | solution.py:848
  140.4 6.2 %all-gather.11.cloned.1.call-done = bf16[8,40,3840]{2,1,0:T(8,128)(2,1)} async-done(((bf16[2,40,3840]{2,1,0:T(8,128)(2,1)}), bf16[8,40,3840]{2,1,0:T(8,128)(2,1)}) %all-gather.11.cloned.1.call-update) | async-done | bytes 2457616 | tf_op jit(solution)/shard_map/all_gather | solution.py:882
  153.8 4.5 shard_map.172
  166.2 15.7 %collective-permute-done.16.across_ref = bf16[4,40,3840]{2,1,0:T(8,128)(2,1)S(1)} collective-permute-done((bf16[4,40,3840]{2,1,0:T(8,128)(2,1)S(1)}, bf16[4,40,3840]{2,1,0:T(8,128)(2,1)S(1)}, u32[]{:S(2)}, u32[]{:S(2)}) %collective-permute-start.16) | collective-permute-done | bytes 1228832 | tf_op jit(solution)/shard_map/ppermute | solution.py:848
  184.6 4.8 shard_map.173
  189.4 7.7 %shard_map.174 = (bf16[1024,1280]{1,0:T(8,128)(2,1)}, f32[960,1024]{1,0:T(8,128)}) custom-call(s32[3]{0:T(128)S(1)} %pad_add_fusion.place_ref.core_ref, bf16[256,1280]{1,0:T(8,128)(2,1)} %multiply_convert_fusion.2.refs_0_, bf16[256,1280]{1,0:T(8,128)(2,1)} %collective-permute-done.17.refs_1_, bf16[256,1280]{1,0:T(8,128)(2,1)} %collective-permute-done.15.refs_2_, ...), custom_call_target="tpu_custom_call" | custom-call | flops 1048576 | bytes 1048576 | tf_op jit(solution)/shard_map/pallas_call | solution.py:711
  199.2 8.9 %shard_map.175 = (bf16[4,4,80,256]{3,2,1,0:T(8,128)(2,1)S(1)}, f32[4,1,1024]{2,1,0:T(1,128)S(1)}) custom-call(f32[3,4,80,1024]{3,2,1,0:T(8,128)S(1)} %bitcast.200, f32[80,1]{1,0:T(8,128)S(1)} %copy.64.scale_ref, s32[1024,1]{1,0:T(8,128)S(1)} %copy.61.col_ref, s32[1,1024]{1,0:T(1,128)S(1)} %constant_dynamic-slice_fusion.row_ref), custom_call_target="tpu_custom_call" | custom-call | flops 1048576 | bytes 1048576 | tf_op jit(solution)/shard_map/pallas_call | solution.py:413
  215.6 19.3 %all_to_all.40 = bf16[4,320,256]{2,1,0:T(8,128)(2,1)S(1)} all-to-all(bf16[4,320,256]{2,1,0:T(8,128)(2,1)S(1)} %bitcast.215), channel_id=1, replica_groups=mesh['batch'=4,'blk'=2,'head'=4] {'head'}, dimensions={0} | all-to-all | bytes 1310720 | tf_op jit(solution)/shard_map/all_to_all | solution.py:869
  251.5 4.2 all-to-all-start.4
  256.0 9.9 %shard_map.177 = (bf16[2,2,4,40,3840]{4,3,2,1,0:T(8,128)(2,1)}, bf16[2,2,4,40,3840]{4,3,2,1,0:T(8,128)(2,1)}) custom-call(s32[3]{0:T(128)S(1)} %pad_add_fusion.place_ref.core_ref, bf16[1280,256]{1,0:T(8,128)(2,1)} %bitcast.239, bf16[256,1280]{1,0:T(8,128)(2,1)} %copy-done.25, bf16[256,1280]{1,0:T(8,128)(2,1)} %copy-done.50, bf16[256,1280]{1,0:T(8,128)(2,1)} %copy-done.26, ...), custom_call_target="tpu_custom_call" | custom-call | flops 1048576 | bytes 1048576 | tf_op jit(solution)/shard_map/pallas_call | solution.py:577
  268.2 12.5 %shard_map.178 = (bf16[3,4,80,1024]{3,2,1,0:T(8,128)(2,1)}, f32[80,128]{1,0:T(8,128)}) custom-call(f32[3,4,80,1024]{3,2,1,0:T(8,128)} %bitcast.199, bf16[4,4,80,256]{3,2,1,0:T(8,128)(2,1)} %bitcast.56.grad_ref, f32[4,1,1024]{2,1,0:T(1,128)S(1)} %get-tuple-element.146.lse_ref, f32[80,1]{1,0:T(8,128)S(1)} %copy.64.scale_ref, s32[1024,1]{1,0:T(8,128)S(1)} %copy.61.col_ref, ...), custom_call_target="tpu_custom_call" | custom-call | flops 1048576 | bytes 1048576 | tf_op jit(solution)/shard_map/pallas_call | solution.py:506
  289.7 11.3 %shard_map.179 = (f32[2,2,128,1280]{3,2,1,0:T(8,128)}, bf16[2,2,128,1280]{3,2,1,0:T(8,128)(2,1)}, bf16[1280,960]{1,0:T(8,128)(2,1)}) custom-call(s32[3]{0:T(128)S(1)} %pad_add_fusion.place_ref.core_ref, bf16[960,1024]{1,0:T(8,128)(2,1)} %bitcast.242, bf16[1280,960]{1,0:T(8,128)(2,1)} %bitcast.217, bf16[1024,1280]{1,0:T(8,128)(2,1)} %get-tuple-element.153.normed_ref), custom_call_target="tpu_custom_call" | custom-call | flops 1048576 | bytes 1048576 | tf_op jit(solution)/shard_map/pallas_call | solution.py:757
  315.2 14.6 %collective-permute-done.33 = bf16[2,128,1280]{2,1,0:T(8,128)(2,1)} collective-permute-done((bf16[2,128,1280]{2,1,0:T(8,128)(2,1)}, bf16[2,128,1280]{2,1,0:T(8,128)(2,1)}, u32[]{:S(2)}, u32[]{:S(2)}) %collective-permute-start.33) | collective-permute-done | bytes 655392 | tf_op jit(solution)/shard_map/ppermute | solution.py:848
  347.6 9.9 %shard_map.180 = (bf16[2,2,4,40,3840]{4,3,2,1,0:T(8,128)(2,1)}, bf16[2,2,4,40,3840]{4,3,2,1,0:T(8,128)(2,1)}) custom-call(s32[3]{0:T(128)S(1)} %pad_add_fusion.place_ref.core_ref, bf16[1280,256]{1,0:T(8,128)(2,1)} %bitcast.236, bf16[256,1280]{1,0:T(8,128)(2,1)} %copy-done.24, bf16[256,1280]{1,0:T(8,128)(2,1)} %copy-done.46, bf16[256,1280]{1,0:T(8,128)(2,1)} %copy-done.31, ...), custom_call_target="tpu_custom_call" | custom-call | flops 1048576 | bytes 1048576 | tf_op jit(solution)/shard_map/pallas_call | solution.py:577
  357.5 9.5 %all-to-all-done.5 = bf16[4,320,256]{2,1,0:T(8,128)(2,1)S(1)} async-done(((bf16[4,320,256]{2,1,0:T(8,128)(2,1)}), bf16[4,320,256]{2,1,0:T(8,128)(2,1)S(1)}, u32[]{:S(2)}, u32[]{:S(2)}) %all-to-all-start.5) | async-done | bytes 655392 | tf_op jit(solution)/shard_map/all_to_all | solution.py:869
  372.6 12.3 %shard_map.181 = (bf16[3,4,80,1024]{3,2,1,0:T(8,128)(2,1)}, f32[80,128]{1,0:T(8,128)}) custom-call(f32[3,4,80,1024]{3,2,1,0:T(8,128)} %bitcast.197, bf16[4,4,80,256]{3,2,1,0:T(8,128)(2,1)} %bitcast.240, f32[4,1,1024]{2,1,0:T(1,128)S(1)} %get-tuple-element.173.lse_ref, f32[80,1]{1,0:T(8,128)S(1)} %copy.60.scale_ref, s32[1024,1]{1,0:T(8,128)S(1)} %copy.61.col_ref, ...), custom_call_target="tpu_custom_call" | custom-call | flops 1048576 | bytes 1048576 | tf_op jit(solution)/shard_map/pallas_call | solution.py:506
  389.3 5.1 add_convert_fusion
  397.0 7.6 %shard_map.182 = bf16[1280,960]{1,0:T(8,128)(2,1)} custom-call(bf16[960,1024]{1,0:T(8,128)(2,1)} %bitcast.231, bf16[1024,1280]{1,0:T(8,128)(2,1)} %get-tuple-element.178.normed_ref), custom_call_target="tpu_custom_call" | custom-call | flops 1048576 | bytes 1048576 | tf_op jit(solution)/shard_map/pallas_call | solution.py:828
  411.3 8.3 %shard_map.183 = (f32[2,2,128,1280]{3,2,1,0:T(8,128)}, bf16[2,2,128,1280]{3,2,1,0:T(8,128)(2,1)}) custom-call(s32[3]{0:T(128)S(1)} %pad_add_fusion.place_ref.core_ref, bf16[960,1024]{1,0:T(8,128)(2,1)} %bitcast.232, bf16[1280,960]{1,0:T(8,128)(2,1)} %bitcast.224), custom_call_target="tpu_custom_call" | custom-call | flops 1048576 | bytes 1048576 | tf_op jit(solution)/shard_map/pallas_call | solution.py:798
  441.9 16.5 %collective-permute-done.41 = bf16[4,40,3840]{2,1,0:T(8,128)(2,1)S(1)} collective-permute-done((bf16[4,40,3840]{2,1,0:T(8,128)(2,1)S(1)}, bf16[4,40,3840]{2,1,0:T(8,128)(2,1)S(1)}, u32[]{:S(2)}, u32[]{:S(2)}) %collective-permute-start.41) | collective-permute-done | bytes 1228832 | tf_op jit(solution)/shard_map/ppermute | solution.py:848
  467.5 6.1 %collective-permute-done.48 = bf16[160,960]{1,0:T(8,128)(2,1)S(1)} collective-permute-done((bf16[160,960]{1,0:T(8,128)(2,1)S(1)}, bf16[160,960]{1,0:T(8,128)(2,1)S(1)}, u32[]{:S(2)}, u32[]{:S(2)}) %collective-permute-start.48) | collective-permute-done | bytes 307232 | tf_op jit(solution)/shard_map/ppermute | solution.py:848
  480.4 5.2 collective-permute-done.49
  498.3 5.1 collective-permute-done.47
  504.6 13.7 %reduce-scatter.11.cloned.1.call-done = bf16[1,40,3840]{2,1,0:T(8,128)(2,1)} async-done(((bf16[4,40,3840]{2,1,0:T(8,128)(2,1)}), bf16[1,40,3840]{2,1,0:T(8,128)(2,1)}) %reduce-scatter.11.cloned.1.call-update) | async-done | bytes 307216 | tf_op jit(solution)/shard_map/reduce_scatter | solution.py:898
  (384 shorter events, 205.3 us)
Async XLA Ops:
  8.3 34.7 %collective-permute-start.4 = (bf16[128,1280]{1,0:T(8,128)(2,1)S(1)}, bf16[128,1280]{1,0:T(8,128)(2,1)}, u32[]{:S(2)}, u32[]{:S(2)}) collective-permute-start(bf16[128,1280]{1,0:T(8,128)(2,1)S(1)} %dynamic-slice_bitcast_fusion.10), channel_id=1, source_target_pairs={{0,4},{4,0},{1,5},{5,1},{2,6},{6,2},{3,7},{7,3},{8,12},{12,8},{9,1... | collective-permute-start | bytes 983048 | tf_op jit(solution)/shard_map/ppermute | solution.py:848
  17.8 43.5 %all-gather.7.cloned.1.call-start = ((), (), s32[]{:S(2)}) async-start(), calls=%async_computation.16 | async-start | bytes 1638400 | tf_op jit(solution)/shard_map/all_gather | solution.py:882
  26.9 66.8 %all-gather.9.cloned.1.call-start = ((), (), s32[]{:S(2)}) async-start(), calls=%async_computation.17 | async-start | bytes 1536000 | tf_op jit(solution)/shard_map/all_gather | solution.py:882
  61.3 30.1 %collective-permute-start.5 = (bf16[4,160,964]{2,1,0:T(8,128)(2,1)}, bf16[4,160,964]{2,1,0:T(8,128)(2,1)S(1)}, u32[]{:S(2)}, u32[]{:S(2)}) collective-permute-start(bf16[4,160,964]{2,1,0:T(8,128)(2,1)} %bitcast.248), channel_id=1, source_target_pairs={{0,4},{4,0},{1,5},{5,1},{2,6},{6,2},{3,7},{7,3},{8,12},{12,8},{9,1... | collective-permute-start | bytes 3701768 | tf_op jit(solution)/shard_map/ppermute | solution.py:848
  68.0 78.5 %all-gather.11.cloned.1.call-start = ((), (), s32[]{:S(2)}) async-start(), calls=%async_computation.18 | async-start | bytes 3072000 | tf_op jit(solution)/shard_map/all_gather | solution.py:882
  94.7 30.0 %collective-permute-start.7 = (bf16[4,40,3840]{2,1,0:T(8,128)(2,1)}, bf16[4,40,3840]{2,1,0:T(8,128)(2,1)S(1)}, u32[]{:S(2)}, u32[]{:S(2)}) collective-permute-start(bf16[4,40,3840]{2,1,0:T(8,128)(2,1)} %bitcast.19.refs_0_), channel_id=1, source_target_pairs={{0,2},{1,3},{2,0},{3,1},{4,6},{5,7},{6,4},{7,5},{8,10},{9,11},{10,... | collective-permute-start | bytes 3686408 | tf_op jit(solution)/shard_map/ppermute | solution.py:848
  96.3 28.5 %collective-permute-start.6 = (bf16[4,40,3840]{2,1,0:T(8,128)(2,1)}, bf16[4,40,3840]{2,1,0:T(8,128)(2,1)}, u32[]{:S(2)}, u32[]{:S(2)}) collective-permute-start(bf16[4,40,3840]{2,1,0:T(8,128)(2,1)} %bitcast.19.refs_0_), channel_id=1, source_target_pairs={{0,4},{4,0},{1,5},{5,1},{2,6},{6,2},{3,7},{7,3},{8,12},{12,8},{9,1... | collective-permute-start | bytes 3686408 | tf_op jit(solution)/shard_map/ppermute | solution.py:848
  128.7 21.0 %collective-permute-start.8 = (bf16[4,40,1920]{2,1,0:T(8,128)(2,1)}, bf16[4,40,1920]{2,1,0:T(8,128)(2,1)}, u32[]{:S(2)}, u32[]{:S(2)}) collective-permute-start(bf16[4,40,1920]{2,1,0:T(8,128)(2,1)} %slice.149), channel_id=1, source_target_pairs={{0,2},{1,3},{2,0},{3,1},{4,6},{5,7},{6,4},{7,5},{8,10},{9,11},{10,... | collective-permute-start | bytes 1843208 | tf_op jit(solution)/shard_map/ppermute | solution.py:848
  129.3 20.4 %all-to-all-start.2 = ((bf16[4,320,256]{2,1,0:T(8,128)(2,1)}), bf16[4,320,256]{2,1,0:T(8,128)(2,1)S(1)}, u32[]{:S(2)}, u32[]{:S(2)}) async-start(bf16[4,320,256]{2,1,0:T(8,128)(2,1)} %bitcast.31), calls=%async_computation.2 | async-start | bytes 1310720 | tf_op jit(solution)/shard_map/all_to_all | solution.py:869
  133.1 19.3 %collective-permute-start.10 = (bf16[4,40,3840]{2,1,0:T(8,128)(2,1)}, bf16[4,40,3840]{2,1,0:T(8,128)(2,1)}, u32[]{:S(2)}, u32[]{:S(2)}) collective-permute-start(bf16[4,40,3840]{2,1,0:T(8,128)(2,1)} %bitcast.19.refs_0_), channel_id=1, source_target_pairs={{0,1},{1,0},{2,3},{3,2},{4,5},{5,4},{6,7},{7,6},{8,9},{9,8},{10,11... | collective-permute-start | bytes 3686408 | tf_op jit(solution)/shard_map/ppermute | solution.py:848
  133.6 20.2 %collective-permute-start.11 = (bf16[4,40,3840]{2,1,0:T(8,128)(2,1)}, bf16[4,40,3840]{2,1,0:T(8,128)(2,1)}, u32[]{:S(2)}, u32[]{:S(2)}) collective-permute-start(bf16[4,40,3840]{2,1,0:T(8,128)(2,1)} %collective-permute-done.6.refs_1_), channel_id=1, source_target_pairs={{0,1},{1,0},{2,3},{3,2},{4,5},{5,4},{6,7},{7,6},{8,9},{9,8},{10,11... | collective-permute-start | bytes 3686408 | tf_op jit(solution)/shard_map/ppermute | solution.py:848
  133.7 20.1 %collective-permute-start.12 = (bf16[4,40,3840]{2,1,0:T(8,128)(2,1)S(1)}, bf16[4,40,3840]{2,1,0:T(8,128)(2,1)}, u32[]{:S(2)}, u32[]{:S(2)}) collective-permute-start(bf16[4,40,3840]{2,1,0:T(8,128)(2,1)S(1)} %collective-permute-done.7.refs_2_), channel_id=1, source_target_pairs={{0,1},{1,0},{2,3},{3,2},{4,5},{5,4},{6,7},{7,6},{8,9},{9,8},{10,11... | collective-permute-start | bytes 3686408 | tf_op jit(solution)/shard_map/ppermute | solution.py:848
  152.4 29.5 %collective-permute-start.16 = (bf16[4,40,3840]{2,1,0:T(8,128)(2,1)S(1)}, bf16[4,40,3840]{2,1,0:T(8,128)(2,1)S(1)}, u32[]{:S(2)}, u32[]{:S(2)}) collective-permute-start(bf16[4,40,3840]{2,1,0:T(8,128)(2,1)S(1)} %get-tuple-element.230.along_ref), channel_id=1, source_target_pairs={{0,4},{4,0},{1,5},{5,1},{2,6},{6,2},{3,7},{7,3},{8,12},{12,8},{9,1... | collective-permute-start | bytes 3686408 | tf_op jit(solution)/shard_map/ppermute | solution.py:848
  182.7 28.3 %collective-permute-start.20 = (bf16[4,40,3840]{2,1,0:T(8,128)(2,1)S(1)}, bf16[4,40,3840]{2,1,0:T(8,128)(2,1)S(1)}, u32[]{:S(2)}, u32[]{:S(2)}) collective-permute-start(bf16[4,40,3840]{2,1,0:T(8,128)(2,1)S(1)} %get-tuple-element.131.refs_0_), channel_id=1, source_target_pairs={{0,2},{1,3},{2,0},{3,1},{4,6},{5,7},{6,4},{7,5},{8,10},{9,11},{10,... | collective-permute-start | bytes 3686408 | tf_op jit(solution)/shard_map/ppermute | solution.py:848
  183.4 28.2 %collective-permute-start.19 = (bf16[4,40,3840]{2,1,0:T(8,128)(2,1)S(1)}, bf16[4,40,3840]{2,1,0:T(8,128)(2,1)}, u32[]{:S(2)}, u32[]{:S(2)}) collective-permute-start(bf16[4,40,3840]{2,1,0:T(8,128)(2,1)S(1)} %get-tuple-element.131.refs_0_), channel_id=1, source_target_pairs={{0,4},{4,0},{1,5},{5,1},{2,6},{6,2},{3,7},{7,3},{8,12},{12,8},{9,1... | collective-permute-start | bytes 3686408 | tf_op jit(solution)/shard_map/ppermute | solution.py:848
  212.7 22.2 %collective-permute-start.22 = (bf16[4,40,1920]{2,1,0:T(8,128)(2,1)S(1)}, bf16[4,40,1920]{2,1,0:T(8,128)(2,1)S(1)}, u32[]{:S(2)}, u32[]{:S(2)}) collective-permute-start(bf16[4,40,1920]{2,1,0:T(8,128)(2,1)S(1)} %slice.163), channel_id=1, source_target_pairs={{0,4},{4,0},{1,5},{5,1},{2,6},{6,2},{3,7},{7,3},{8,12},{12,8},{9,1... | collective-permute-start | bytes 1843208 | tf_op jit(solution)/shard_map/ppermute | solution.py:848
  213.8 21.1 %collective-permute-start.21 = (bf16[4,40,1920]{2,1,0:T(8,128)(2,1)S(1)}, bf16[4,40,1920]{2,1,0:T(8,128)(2,1)S(1)}, u32[]{:S(2)}, u32[]{:S(2)}) collective-permute-start(bf16[4,40,1920]{2,1,0:T(8,128)(2,1)S(1)} %slice.162), channel_id=1, source_target_pairs={{0,2},{1,3},{2,0},{3,1},{4,6},{5,7},{6,4},{7,5},{8,10},{9,11},{10,... | collective-permute-start | bytes 1843208 | tf_op jit(solution)/shard_map/ppermute | solution.py:848
  215.1 20.4 %collective-permute-start.23 = (bf16[4,40,3840]{2,1,0:T(8,128)(2,1)S(1)}, bf16[4,40,3840]{2,1,0:T(8,128)(2,1)S(1)}, u32[]{:S(2)}, u32[]{:S(2)}) collective-permute-start(bf16[4,40,3840]{2,1,0:T(8,128)(2,1)S(1)} %get-tuple-element.131.refs_0_), channel_id=1, source_target_pairs={{0,1},{1,0},{2,3},{3,2},{4,5},{5,4},{6,7},{7,6},{8,9},{9,8},{10,11... | collective-permute-start | bytes 3686408 | tf_op jit(solution)/shard_map/ppermute | solution.py:848
  215.1 22.9 %collective-permute-start.24 = (bf16[4,40,3840]{2,1,0:T(8,128)(2,1)}, bf16[4,40,3840]{2,1,0:T(8,128)(2,1)S(1)}, u32[]{:S(2)}, u32[]{:S(2)}) collective-permute-start(bf16[4,40,3840]{2,1,0:T(8,128)(2,1)} %collective-permute-done.19.refs_1_), channel_id=1, source_target_pairs={{0,1},{1,0},{2,3},{3,2},{4,5},{5,4},{6,7},{7,6},{8,9},{9,8},{10,11... | collective-permute-start | bytes 3686408 | tf_op jit(solution)/shard_map/ppermute | solution.py:848
  215.6 22.3 %collective-permute-start.25 = (bf16[4,40,3840]{2,1,0:T(8,128)(2,1)S(1)}, bf16[4,40,3840]{2,1,0:T(8,128)(2,1)S(1)}, u32[]{:S(2)}, u32[]{:S(2)}) collective-permute-start(bf16[4,40,3840]{2,1,0:T(8,128)(2,1)S(1)} %collective-permute-done.20.refs_2_), channel_id=1, source_target_pairs={{0,1},{1,0},{2,3},{3,2},{4,5},{5,4},{6,7},{7,6},{8,9},{9,8},{10,11... | collective-permute-start | bytes 3686408 | tf_op jit(solution)/shard_map/ppermute | solution.py:848
  246.2 19.7 %collective-permute-start.28 = (bf16[128,1280]{1,0:T(8,128)(2,1)}, bf16[128,1280]{1,0:T(8,128)(2,1)}, u32[]{:S(2)}, u32[]{:S(2)}) collective-permute-start(bf16[128,1280]{1,0:T(8,128)(2,1)} %dynamic-slice_bitcast_fusion.9), channel_id=1, source_target_pairs={{0,4},{4,0},{1,5},{5,1},{2,6},{6,2},{3,7},{7,3},{8,12},{12,8},{9,1... | collective-permute-start | bytes 983048 | tf_op jit(solution)/shard_map/ppermute | solution.py:848
  255.7 111.3 %reduce-scatter.5.cloned.1.call-start = ((), (), s32[]{:S(2)}) async-start(), calls=%async_computation.12 | async-start | bytes 3276800 | tf_op jit(solution)/shard_map/reduce_scatter | solution.py:898
  314.5 43.0 %collective-permute-start.34 = (bf16[4,40,3840]{2,1,0:T(8,128)(2,1)}, bf16[4,40,3840]{2,1,0:T(8,128)(2,1)}, u32[]{:S(2)}, u32[]{:S(2)}) collective-permute-start(bf16[4,40,3840]{2,1,0:T(8,128)(2,1)} %pad_maximum_fusion), channel_id=1, source_target_pairs={{0,4},{4,0},{1,5},{5,1},{2,6},{6,2},{3,7},{7,3},{8,12},{12,8},{9,1... | collective-permute-start | bytes 3686408 | tf_op jit(solution)/shard_map/ppermute | solution.py:848
  331.5 35.5 %collective-permute-start.35 = (bf16[4,40,3840]{2,1,0:T(8,128)(2,1)}, bf16[4,40,3840]{2,1,0:T(8,128)(2,1)}, u32[]{:S(2)}, u32[]{:S(2)}) collective-permute-start(bf16[4,40,3840]{2,1,0:T(8,128)(2,1)} %pad_maximum_fusion.1), channel_id=1, source_target_pairs={{0,2},{1,3},{2,0},{3,1},{4,6},{5,7},{6,4},{7,5},{8,10},{9,11},{10,... | collective-permute-start | bytes 3686408 | tf_op jit(solution)/shard_map/ppermute | solution.py:848
  344.1 22.9 %all-to-all-start.5 = ((bf16[4,320,256]{2,1,0:T(8,128)(2,1)}), bf16[4,320,256]{2,1,0:T(8,128)(2,1)S(1)}, u32[]{:S(2)}, u32[]{:S(2)}) async-start(bf16[4,320,256]{2,1,0:T(8,128)(2,1)} %bitcast.64), calls=%async_computation.5 | async-start | bytes 1310720 | tf_op jit(solution)/shard_map/all_to_all | solution.py:869
  347.6 72.0 %reduce-scatter.7.cloned.1.call-start = ((), (), s32[]{:S(2)}) async-start(), calls=%async_computation.13 | async-start | bytes 1536000 | tf_op jit(solution)/shard_map/reduce_scatter | solution.py:898
  385.8 18.8 %all-to-all-start.6 = ((bf16[4,40,960]{2,1,0:T(8,128)(2,1)}), bf16[4,40,960]{2,1,0:T(8,128)(2,1)S(1)}, u32[]{:S(2)}, u32[]{:S(2)}) async-start(bf16[4,40,960]{2,1,0:T(8,128)(2,1)} %bitcast.72), calls=%async_computation.7 | async-start | bytes 655360 | tf_op jit(solution)/shard_map/all_to_all | solution.py:869
  389.2 70.2 %reduce-scatter.9.cloned.1.call-start = ((), (), s32[]{:S(2)}) async-start(), calls=%async_computation.14 | async-start | bytes 3276800 | tf_op jit(solution)/shard_map/reduce_scatter | solution.py:898
  428.9 29.5 %collective-permute-start.41 = (bf16[4,40,3840]{2,1,0:T(8,128)(2,1)S(1)}, bf16[4,40,3840]{2,1,0:T(8,128)(2,1)S(1)}, u32[]{:S(2)}, u32[]{:S(2)}) collective-permute-start(bf16[4,40,3840]{2,1,0:T(8,128)(2,1)S(1)} %pad_maximum_fusion.2), channel_id=1, source_target_pairs={{0,4},{4,0},{1,5},{5,1},{2,6},{6,2},{3,7},{7,3},{8,12},{12,8},{9,1... | collective-permute-start | bytes 3686408 | tf_op jit(solution)/shard_map/ppermute | solution.py:848
  429.6 29.8 %collective-permute-start.42 = (bf16[4,40,3840]{2,1,0:T(8,128)(2,1)S(1)}, bf16[4,40,3840]{2,1,0:T(8,128)(2,1)}, u32[]{:S(2)}, u32[]{:S(2)}) collective-permute-start(bf16[4,40,3840]{2,1,0:T(8,128)(2,1)S(1)} %pad_maximum_fusion.3), channel_id=1, source_target_pairs={{0,2},{1,3},{2,0},{3,1},{4,6},{5,7},{6,4},{7,5},{8,10},{9,11},{10,... | collective-permute-start | bytes 3686408 | tf_op jit(solution)/shard_map/ppermute | solution.py:848
  465.8 26.1 %collective-permute-start.46 = (bf16[2,128,1280]{2,1,0:T(8,128)(2,1)}, bf16[2,128,1280]{2,1,0:T(8,128)(2,1)}, u32[]{:S(2)}, u32[]{:S(2)}) collective-permute-start(bf16[2,128,1280]{2,1,0:T(8,128)(2,1)} %fusion.80), channel_id=1, source_target_pairs={{0,2},{1,3},{2,0},{3,1},{4,6},{5,7},{6,4},{7,5},{8,10},{9,11},{10,... | collective-permute-start | bytes 1966088 | tf_op jit(solution)/shard_map/ppermute | solution.py:848
  478.4 39.8 %reduce-scatter.11.cloned.1.call-start = ((), (), s32[]{:S(2)}) async-start(), calls=%async_computation.15 | async-start | bytes 1536000 | tf_op jit(solution)/shard_map/reduce_scatter | solution.py:898
  (102 other events, 786.5 us)
Sparse Core Ops, SparseCore 0:
  27.1 34.1 all-gather.6
  63.4 30.2 all-gather.8
  95.3 51.1 all-gather.10
  314.6 50.4 reduce-scatter.4
  370.9 29.6 reduce-scatter.6
  404.7 52.1 reduce-scatter.8
  488.7 29.5 reduce-scatter.10

commit v18 on v17

--- a/solution.py
+++ b/solution.py
@@ -546,7 +546,7 @@
     own_ref, other_ref, normed_t, active_t,
 ):
     tile = pl.program_id(0)
-    rows, width = own_ref.shape[1] * own_ref.shape[3] * 2, out_bar.shape[1]
+    rows, width = 8 * own_ref.shape[3], out_bar.shape[1]
 
     @pl.when(tile == 0)
     def _():
@@ -558,12 +558,12 @@
     lefts = (attended_ref, normed_t, active_t)
     for i, (left, right) in enumerate(zip(lefts, (out_bar, up_bar, down_bar))):
         grad = jnp.dot(left[pl.ds(start, rows), :], right[...], preferred_element_type=F32)
-        grad = grad.reshape(2, 2, rows // 4, width)
-        one, two = grad[:, 0], grad[:, 1]
-        own_ref[0, :, 0, :, i * width : (i + 1) * width] = jnp.where(
+        grad = grad.reshape(2, 2, 2, rows // 8, width)
+        one, two = grad[:, :, 0], grad[:, :, 1]
+        own_ref[:, :, 0, :, i * width : (i + 1) * width] = jnp.where(
             first_core, one, two
         ).astype(BF16)
-        other_ref[0, :, 0, :, i * width : (i + 1) * width] = jnp.where(
+        other_ref[:, :, 0, :, i * width : (i + 1) * width] = jnp.where(
             first_core, two, one
         ).astype(BF16)
 
@@ -572,13 +572,13 @@
     width, tokens = attended_t.shape
     own = width // 32
     whole = pl.BlockSpec((tokens, width), lambda i, core: (0, 0))
-    rows = pl.BlockSpec((1, 2, 1, own, 3 * width), lambda i, core: (i % 2, 0, i // 2, 0, 0))
+    rows = pl.BlockSpec((2, 2, 1, own, 3 * width), lambda i, core: (0, 0, i, 0, 0))
     shape = pltpu.HBM((2, 2, 4, own, 3 * width), BF16)
     return pl.pallas_call(
         dense_grad_kernel,
         grid_spec=pltpu.PrefetchScalarGridSpec(
             num_scalar_prefetch=1,
-            grid=(8,),
+            grid=(4,),
             in_specs=[pl.BlockSpec((width, tokens), lambda i, core: (0, 0))] + [whole] * 5,
             out_specs=[rows, rows],
             scratch_shapes=[pltpu.VMEM((width, tokens), BF16)] * 2,
@@ -909,25 +909,25 @@
     return moved.reshape(4, rows, 3, -1).transpose(1, 2, 0, 3).reshape(rows, -1).astype(F32)
 
 
-def diagonal_rows(cored):
+def quarter(parts, blk, row):
+    one, two = (pick(pick(part, blk), row).astype(F32) for part in parts)
+    return one + two
+
+
+def diagonal_rows(parts):
     blk, row = place()[:2]
-    rows = pick(pick(cored, 1 - blk), 1 - row)
+    rows = quarter(parts, 1 - blk, 1 - row).astype(BF16)
     half = rows.shape[-1] // 2
     return rows[..., :half], rows[..., half:]
 
 
-def neighbour_rows(cored, one, two):
+def neighbour_rows(parts, one, two):
     blk, row = place()[:2]
     half = one.shape[-1]
-    across = pick(pick(cored, 1 - blk), row)
-    beside = pick(pick(cored, blk), 1 - row)
-    across = jnp.concatenate(
-        [across[..., :half], across[..., half:].astype(F32) + two.astype(F32)], axis=-1
-    ).astype(BF16)
-    beside = jnp.concatenate(
-        [beside[..., :half].astype(F32) + one.astype(F32), beside[..., half:]], axis=-1
-    ).astype(BF16)
-    return across, beside
+    across, beside = quarter(parts, 1 - blk, row), quarter(parts, blk, 1 - row)
+    across = jnp.concatenate([across[..., :half], across[..., half:] + two.astype(F32)], axis=-1)
+    beside = jnp.concatenate([beside[..., :half] + one.astype(F32), beside[..., half:]], axis=-1)
+    return across.astype(BF16), beside.astype(BF16)
 
 
 def sent_beside_and_across(across, beside):
@@ -938,10 +938,9 @@
     return dot_cols(weight, out_bar).astype(BF16).reshape(4, -1, out_bar.shape[0])
 
 
-def own_sum(cored, across, beside):
+def own_sum(parts, across, beside):
     blk, row = place()[:2]
-    own = pick(pick(cored, blk), row)
-    return own.astype(F32) + across.astype(F32) + beside.astype(F32)
+    return quarter(parts, blk, row) + across.astype(F32) + beside.astype(F32)
 
 
 def sum_over(array, *hops):
@@ -1091,7 +1090,7 @@
             qkv_grad = weight_back(bars, normed_all)
             bars, qkv_grad, moved = tied(bars, qkv_grad, moved)
             z_sum = over_batch(qkv_grad.reshape(4, 2, -1, qkv_grad.shape[-1]))
-            cored = (grads.astype(F32) + others.astype(F32)).astype(BF16)
+            cored = (grads, others)
             bars, rows = tied(bars, diagonal_rows(cored))
             diagonal = sent_beside_and_across(*rows)
             halves, to_core = rows_back(bars, qkv, token_rows)
@@ -1104,13 +1103,13 @@
             halves, own = tied(halves, own_sum(cored, *sent))
             dense_first = over_batch(own)
             normed_grad = scatter_row(halves)
+            z_across, dense_first = tied(across_sum(z_sum), dense_first)
+            z_across = over_head(z_across.reshape(4, -1, z_across.shape[-1]))
             dense_grad = [dense_first, summed]
-            z_across = across_sum(z_sum)
-            z_across = over_head(z_across.reshape(4, -1, z_across.shape[-1]))
             qkv_grads = [columns_to_rows(z_across), columns_to_rows(moved)]
         else:
             bars, others = tied(bars, others)
-            cored = (grads.astype(F32) + others.astype(F32)).astype(BF16)
+            cored = (grads, others)
             bars, rows = tied(bars, diagonal_rows(cored))
             diagonal = sent_beside_and_across(*rows)
             halves, to_core, qkv_grad = project_back(bars, qkv, normed_all, token_rows)

time: 536 us -> 517 us (0.965)
  waiting for transfers between devices: 189 us -> 181 us
  local copies, waits for them, and re-layouts: 44.3 us -> 37.1 us
    reduce_scatter x4, waiting for transfers between devices: 13.7 us -> 1.39 us  [over_batch(): lax.psum_scatter(parts.astype(BF16), 'batch', scatter_dimension=0, tiled=...]
    add x2 -> x4, other arithmetic: 7.16 us -> 16.8 us  [the longest x2 8.55 us: quarter(): return one + two]
    convert_element_type x2 -> x0, other arithmetic: 8.6 us -> none  [spread_device(): cored = (grads.astype(F32) + others.astype(F32)).astype(BF16)]
    all_to_all x7, waiting for transfers between devices: 19.3 us -> 24.7 us  [over_head(): lax.all_to_all(parts, 'head', split_axis=0, concat_axis=0, tiled=True)]
    unnamed x138 -> x130, local copies, waits for them, and re-layouts: 19.2 us -> 14.1 us
where the time goes in v18:
time: 517 us; the launch traced here: 509 us
  waiting for transfers between devices  181 us (35%)
  Pallas kernels  121 us (23%)
  starting transfers between devices  67.9 us (13%)
  other arithmetic  46.9 us (9%)
  local copies, waits for them, and re-layouts  37.1 us (7%)
  matrix products  19.5 us (4%)
  blocking collectives  19.4 us (4%)
  between operations  15.9 us (3%)
    ppermute x51, waiting for transfers between devices, swapped(): return lax.ppermute(array, axis, [(i, i ^ mask) for i in range(size)])  131 us
    ppermute x51, starting transfers between devices, swapped(): return lax.ppermute(array, axis, [(i, i ^ mask) for i in range(size)])  42.2 us
    all_to_all x7, starting transfers between devices, over_head(): lax.all_to_all(parts, 'head', split_axis=0, concat_axis=0, tiled=True)  25.3 us
    pallas_call x2, Pallas kernels, attend_back_rows(): pl.pallas_call(functools.partial(attend_back_kernel, token_rows), grid=(l...  24.8 us
    all_to_all x7, waiting for transfers between devices, over_head(): lax.all_to_all(parts, 'head', split_axis=0, concat_axis=0, tiled=True)  24.7 us
    all_gather x3, waiting for transfers between devices, along_batch(): return lax.all_gather(piece, 'batch', axis=0, tiled=False)  23.7 us
    all_to_all x1, blocking collectives, over_head(): lax.all_to_all(parts, 'head', split_axis=0, concat_axis=0, tiled=True)  19.4 us
    pallas_call x2, Pallas kernels, attend_rows(): pl.pallas_call(functools.partial(attend_kernel, token_rows), grid=(local_...  18.5 us
  transfers between devices with their start and end apart: 65, of which 31 were waited for; matrix products, arithmetic and copies ran while one was open for 13% of the time, Pallas kernels for 23%

profile of v18, /device:TPU:0, one launch (start us, length us, event | category | flops | bytes accessed | tf_op | source)
XLA Modules:
  0.0 508.8 jit_solution(5149099038717169867)
XLA Ops:
  17.9 8.1 %collective-permute-done = bf16[128,1280]{1,0:T(8,128)(2,1)S(1)} collective-permute-done((bf16[128,1280]{1,0:T(8,128)(2,1)S(1)}, bf16[128,1280]{1,0:T(8,128)(2,1)S(1)}, u32[]{:S(2)}, u32[]{:S(2)}) %collective-permute-start) | collective-permute-done | bytes 327712 | tf_op jit(solution)/shard_map/ppermute | solution.py:848
  30.6 12.4 %collective-permute-done.2.refs_2_ = bf16[256,1280]{1,0:T(8,128)(2,1)S(1)} collective-permute-done((bf16[256,1280]{1,0:T(8,128)(2,1)S(1)}, bf16[256,1280]{1,0:T(8,128)(2,1)S(1)}, u32[]{:S(2)}, u32[]{:S(2)}) %collective-permute-start.2) | collective-permute-done | bytes 655392 | tf_op jit(solution)/shard_map/ppermute | solution.py:848
  46.1 15.2 %all-gather.7.cloned.1.call-done = bf16[640,964]{1,0:T(8,128)(2,1)} async-done(((bf16[160,964]{1,0:T(8,128)(2,1)}), bf16[640,964]{1,0:T(8,128)(2,1)}) %all-gather.7.cloned.1.call-update) | async-done | bytes 1233936 | tf_op jit(solution)/shard_map/all_gather | solution.py:882
  68.1 6.6 %all-to-all-done.1 = bf16[4,40,960]{2,1,0:T(8,128)(2,1)S(1)} async-done(((bf16[4,40,960]{2,1,0:T(8,128)(2,1)}), bf16[4,40,960]{2,1,0:T(8,128)(2,1)S(1)}, u32[]{:S(2)}, u32[]{:S(2)}) %all-to-all-start.1) | async-done | bytes 307232 | tf_op jit(solution)/shard_map/all_to_all | solution.py:869
  74.9 16.5 %collective-permute-done.5.across_ref = bf16[4,160,964]{2,1,0:T(8,128)(2,1)S(1)} collective-permute-done((bf16[4,160,964]{2,1,0:T(8,128)(2,1)}, bf16[4,160,964]{2,1,0:T(8,128)(2,1)S(1)}, u32[]{:S(2)}, u32[]{:S(2)}) %collective-permute-start.5) | collective-permute-done | bytes 1233952 | tf_op jit(solution)/shard_map/ppermute | solution.py:848
  98.2 4.6 shard_map.169
  104.1 8.9 %shard_map.170 = (bf16[1024,1280]{1,0:T(8,128)(2,1)}, f32[960,1024]{1,0:T(8,128)}) custom-call(s32[3]{0:T(128)S(1)} %pad_add_fusion.place_ref.core_ref, bf16[256,1280]{1,0:T(8,128)(2,1)} %bitcast.231, bf16[256,1280]{1,0:T(8,128)(2,1)} %copy-done.49, bf16[256,1280]{1,0:T(8,128)(2,1)} %copy-done.48, bf16[256,1280]{1,0:T(8,128)(2,1)} %collective-permute-done.3.refs_3_, ...), custom_call_target="tpu_custom_call" | custom-call | flops 1048576 | bytes 1048576 | tf_op jit(solution)/shard_map/pallas_call | solution.py:711
  115.2 9.6 %shard_map.171 = (bf16[4,4,80,256]{3,2,1,0:T(8,128)(2,1)}, f32[4,1,1024]{2,1,0:T(1,128)S(1)}) custom-call(f32[3,4,80,1024]{3,2,1,0:T(8,128)S(1)} %bitcast.202, f32[80,1]{1,0:T(8,128)S(1)} %copy.60.scale_ref, s32[1024,1]{1,0:T(8,128)S(1)} %copy.61.col_ref, s32[1,1024]{1,0:T(1,128)S(1)} %constant_dynamic-slice_fusion.row_ref), custom_call_target="tpu_custom_call" | custom-call | flops 1048576 | bytes 1048576 | tf_op jit(solution)/shard_map/pallas_call | solution.py:413
  134.1 6.2 %collective-permute-done.9.refs_4_ = bf16[4,40,1920]{2,1,0:T(8,128)(2,1)} collective-permute-done((bf16[4,40,1920]{2,1,0:T(8,128)(2,1)}, bf16[4,40,1920]{2,1,0:T(8,128)(2,1)}, u32[]{:S(2)}, u32[]{:S(2)}) %collective-permute-start.9) | collective-permute-done | bytes 614432 | tf_op jit(solution)/shard_map/ppermute | solution.py:848
  140.4 6.2 %all-gather.11.cloned.1.call-done = bf16[8,40,3840]{2,1,0:T(8,128)(2,1)} async-done(((bf16[2,40,3840]{2,1,0:T(8,128)(2,1)}), bf16[8,40,3840]{2,1,0:T(8,128)(2,1)}) %all-gather.11.cloned.1.call-update) | async-done | bytes 2457616 | tf_op jit(solution)/shard_map/all_gather | solution.py:882
  153.8 4.5 shard_map.172
  166.2 15.7 %collective-permute-done.16.across_ref = bf16[4,40,3840]{2,1,0:T(8,128)(2,1)S(1)} collective-permute-done((bf16[4,40,3840]{2,1,0:T(8,128)(2,1)S(1)}, bf16[4,40,3840]{2,1,0:T(8,128)(2,1)S(1)}, u32[]{:S(2)}, u32[]{:S(2)}) %collective-permute-start.16) | collective-permute-done | bytes 1228832 | tf_op jit(solution)/shard_map/ppermute | solution.py:848
  184.6 4.7 shard_map.173
  189.3 7.8 %shard_map.174 = (bf16[1024,1280]{1,0:T(8,128)(2,1)}, f32[960,1024]{1,0:T(8,128)}) custom-call(s32[3]{0:T(128)S(1)} %pad_add_fusion.place_ref.core_ref, bf16[256,1280]{1,0:T(8,128)(2,1)} %multiply_convert_fusion.2.refs_0_, bf16[256,1280]{1,0:T(8,128)(2,1)} %collective-permute-done.17.refs_1_, bf16[256,1280]{1,0:T(8,128)(2,1)} %collective-permute-done.15.refs_2_, ...), custom_call_target="tpu_custom_call" | custom-call | flops 1048576 | bytes 1048576 | tf_op jit(solution)/shard_map/pallas_call | solution.py:711
  199.2 8.9 %shard_map.175 = (bf16[4,4,80,256]{3,2,1,0:T(8,128)(2,1)S(1)}, f32[4,1,1024]{2,1,0:T(1,128)S(1)}) custom-call(f32[3,4,80,1024]{3,2,1,0:T(8,128)S(1)} %bitcast.204, f32[80,1]{1,0:T(8,128)S(1)} %copy.64.scale_ref, s32[1024,1]{1,0:T(8,128)S(1)} %copy.61.col_ref, s32[1,1024]{1,0:T(1,128)S(1)} %constant_dynamic-slice_fusion.row_ref), custom_call_target="tpu_custom_call" | custom-call | flops 1048576 | bytes 1048576 | tf_op jit(solution)/shard_map/pallas_call | solution.py:413
  215.6 19.4 %all_to_all.40 = bf16[4,320,256]{2,1,0:T(8,128)(2,1)S(1)} all-to-all(bf16[4,320,256]{2,1,0:T(8,128)(2,1)S(1)} %bitcast.219), channel_id=1, replica_groups=mesh['batch'=4,'blk'=2,'head'=4] {'head'}, dimensions={0} | all-to-all | bytes 1310720 | tf_op jit(solution)/shard_map/all_to_all | solution.py:869
  250.7 4.2 all-to-all-start.4
  255.2 8.5 %shard_map.177 = (bf16[2,2,4,40,3840]{4,3,2,1,0:T(8,128)(2,1)}, bf16[2,2,4,40,3840]{4,3,2,1,0:T(8,128)(2,1)}) custom-call(s32[3]{0:T(128)S(1)} %pad_add_fusion.place_ref.core_ref, bf16[1280,256]{1,0:T(8,128)(2,1)} %bitcast.243, bf16[256,1280]{1,0:T(8,128)(2,1)} %copy-done.23, bf16[256,1280]{1,0:T(8,128)(2,1)} %copy-done.46, bf16[256,1280]{1,0:T(8,128)(2,1)} %copy-done.24, ...), custom_call_target="tpu_custom_call" | custom-call | flops 1048576 | bytes 1048576 | tf_op jit(solution)/shard_map/pallas_call | solution.py:577
  266.0 12.5 %shard_map.178 = (bf16[3,4,80,1024]{3,2,1,0:T(8,128)(2,1)}, f32[80,128]{1,0:T(8,128)}) custom-call(f32[3,4,80,1024]{3,2,1,0:T(8,128)} %bitcast.203, bf16[4,4,80,256]{3,2,1,0:T(8,128)(2,1)} %bitcast.56.grad_ref, f32[4,1,1024]{2,1,0:T(1,128)S(1)} %get-tuple-element.148.lse_ref, f32[80,1]{1,0:T(8,128)S(1)} %copy.64.scale_ref, s32[1024,1]{1,0:T(8,128)S(1)} %copy.61.col_ref, ...), custom_call_target="tpu_custom_call" | custom-call | flops 1048576 | bytes 1048576 | tf_op jit(solution)/shard_map/pallas_call | solution.py:506
  284.7 11.3 %shard_map.179 = (f32[2,2,128,1280]{3,2,1,0:T(8,128)}, bf16[2,2,128,1280]{3,2,1,0:T(8,128)(2,1)}, bf16[1280,960]{1,0:T(8,128)(2,1)}) custom-call(s32[3]{0:T(128)S(1)} %pad_add_fusion.place_ref.core_ref, bf16[960,1024]{1,0:T(8,128)(2,1)} %bitcast.246, bf16[1280,960]{1,0:T(8,128)(2,1)} %bitcast.221, bf16[1024,1280]{1,0:T(8,128)(2,1)} %get-tuple-element.155.normed_ref), custom_call_target="tpu_custom_call" | custom-call | flops 1048576 | bytes 1048576 | tf_op jit(solution)/shard_map/pallas_call | solution.py:757
  310.1 14.6 %collective-permute-done.33 = bf16[2,128,1280]{2,1,0:T(8,128)(2,1)} collective-permute-done((bf16[2,128,1280]{2,1,0:T(8,128)(2,1)}, bf16[2,128,1280]{2,1,0:T(8,128)(2,1)}, u32[]{:S(2)}, u32[]{:S(2)}) %collective-permute-start.33) | collective-permute-done | bytes 655392 | tf_op jit(solution)/shard_map/ppermute | solution.py:848
  342.5 8.5 %shard_map.180 = (bf16[2,2,4,40,3840]{4,3,2,1,0:T(8,128)(2,1)}, bf16[2,2,4,40,3840]{4,3,2,1,0:T(8,128)(2,1)}) custom-call(s32[3]{0:T(128)S(1)} %pad_add_fusion.place_ref.core_ref, bf16[1280,256]{1,0:T(8,128)(2,1)} %bitcast.240, bf16[256,1280]{1,0:T(8,128)(2,1)} %copy-done.22, bf16[256,1280]{1,0:T(8,128)(2,1)} %copy-done.42, bf16[256,1280]{1,0:T(8,128)(2,1)} %copy-done.29, ...), custom_call_target="tpu_custom_call" | custom-call | flops 1048576 | bytes 1048576 | tf_op jit(solution)/shard_map/pallas_call | solution.py:577
  351.0 10.9 %all-to-all-done.5 = bf16[4,320,256]{2,1,0:T(8,128)(2,1)S(1)} async-done(((bf16[4,320,256]{2,1,0:T(8,128)(2,1)}), bf16[4,320,256]{2,1,0:T(8,128)(2,1)S(1)}, u32[]{:S(2)}, u32[]{:S(2)}) %all-to-all-start.5) | async-done | bytes 655392 | tf_op jit(solution)/shard_map/all_to_all | solution.py:869
  362.0 4.2 fusion.70
  368.0 12.3 %shard_map.181 = (bf16[3,4,80,1024]{3,2,1,0:T(8,128)(2,1)}, f32[80,128]{1,0:T(8,128)}) custom-call(f32[3,4,80,1024]{3,2,1,0:T(8,128)} %bitcast.201, bf16[4,4,80,256]{3,2,1,0:T(8,128)(2,1)} %bitcast.244, f32[4,1,1024]{2,1,0:T(1,128)S(1)} %get-tuple-element.175.lse_ref, f32[80,1]{1,0:T(8,128)S(1)} %copy.60.scale_ref, s32[1024,1]{1,0:T(8,128)S(1)} %copy.61.col_ref, ...), custom_call_target="tpu_custom_call" | custom-call | flops 1048576 | bytes 1048576 | tf_op jit(solution)/shard_map/pallas_call | solution.py:506
  384.7 5.8 %add_bitcast_fusion = (f32[4,40,3840]{2,1,0:T(8,128)}, f32[4,40,3840]{2,1,0:T(8,128)S(1)}, bf16[4,40,3840]{2,1,0:T(8,128)(2,1)}) fusion(bf16[2,2,4,40,3840]{4,3,2,1,0:T(8,128)(2,1)} %collective-permute-done.36, s32[]{:T(128)S(6)} %select_n.174, s32[]{:T(128)S(6)} %select_n.171, bf16[2,2,4,40,3840]{4,3,2,1,0:T(8,128)(2,1)} %get-tuple-element.183, ...), kind=kLoop, calls=%fused_computation.45 | loop fusion | flops 6144000 | bytes 13516816 | tf_op jit(solution)/shard_map/add | solution.py:914
  390.4 7.3 %shard_map.182 = bf16[1280,960]{1,0:T(8,128)(2,1)} custom-call(bf16[960,1024]{1,0:T(8,128)(2,1)} %bitcast.235, bf16[1024,1280]{1,0:T(8,128)(2,1)} %get-tuple-element.180.normed_ref), custom_call_target="tpu_custom_call" | custom-call | flops 1048576 | bytes 1048576 | tf_op jit(solution)/shard_map/pallas_call | solution.py:828
  406.1 8.5 %shard_map.183 = (f32[2,2,128,1280]{3,2,1,0:T(8,128)}, bf16[2,2,128,1280]{3,2,1,0:T(8,128)(2,1)}) custom-call(s32[3]{0:T(128)S(1)} %pad_add_fusion.place_ref.core_ref, bf16[960,1024]{1,0:T(8,128)(2,1)} %bitcast.236, bf16[1280,960]{1,0:T(8,128)(2,1)} %bitcast.228), custom_call_target="tpu_custom_call" | custom-call | flops 1048576 | bytes 1048576 | tf_op jit(solution)/shard_map/pallas_call | solution.py:798
  436.2 15.9 %collective-permute-done.41 = bf16[4,40,3840]{2,1,0:T(8,128)(2,1)} collective-permute-done((bf16[4,40,3840]{2,1,0:T(8,128)(2,1)S(1)}, bf16[4,40,3840]{2,1,0:T(8,128)(2,1)}, u32[]{:S(2)}, u32[]{:S(2)}) %collective-permute-start.41) | collective-permute-done | bytes 1228832 | tf_op jit(solution)/shard_map/ppermute | solution.py:848
  452.5 4.0 fusion.69
  462.8 11.0 %collective-permute-done.49 = f32[2,80]{1,0:T(2,128)S(1)} collective-permute-done((f32[2,80]{1,0:T(2,128)S(1)}, f32[2,80]{1,0:T(2,128)S(1)}, u32[]{:S(2)}, u32[]{:S(2)}) %collective-permute-start.49) | collective-permute-done | bytes 672 | tf_op jit(solution)/shard_map/ppermute | solution.py:848
  480.4 5.8 %collective-permute-done.47 = bf16[128,1280]{1,0:T(8,128)(2,1)S(1)} collective-permute-done((bf16[128,1280]{1,0:T(8,128)(2,1)S(1)}, bf16[128,1280]{1,0:T(8,128)(2,1)S(1)}, u32[]{:S(2)}, u32[]{:S(2)}) %collective-permute-start.47) | collective-permute-done | bytes 327712 | tf_op jit(solution)/shard_map/ppermute | solution.py:848
  (374 shorter events, 192.2 us)
Async XLA Ops:
  8.3 34.7 %collective-permute-start.4 = (bf16[128,1280]{1,0:T(8,128)(2,1)S(1)}, bf16[128,1280]{1,0:T(8,128)(2,1)}, u32[]{:S(2)}, u32[]{:S(2)}) collective-permute-start(bf16[128,1280]{1,0:T(8,128)(2,1)S(1)} %dynamic-slice_bitcast_fusion.4), channel_id=1, source_target_pairs={{0,4},{4,0},{1,5},{5,1},{2,6},{6,2},{3,7},{7,3},{8,12},{12,8},{9,1... | collective-permute-start | bytes 983048 | tf_op jit(solution)/shard_map/ppermute | solution.py:848
  17.8 43.5 %all-gather.7.cloned.1.call-start = ((), (), s32[]{:S(2)}) async-start(), calls=%async_computation.16 | async-start | bytes 1638400 | tf_op jit(solution)/shard_map/all_gather | solution.py:882
  26.9 66.8 %all-gather.9.cloned.1.call-start = ((), (), s32[]{:S(2)}) async-start(), calls=%async_computation.17 | async-start | bytes 1536000 | tf_op jit(solution)/shard_map/all_gather | solution.py:882
  61.3 30.1 %collective-permute-start.5 = (bf16[4,160,964]{2,1,0:T(8,128)(2,1)}, bf16[4,160,964]{2,1,0:T(8,128)(2,1)S(1)}, u32[]{:S(2)}, u32[]{:S(2)}) collective-permute-start(bf16[4,160,964]{2,1,0:T(8,128)(2,1)} %bitcast.252), channel_id=1, source_target_pairs={{0,4},{4,0},{1,5},{5,1},{2,6},{6,2},{3,7},{7,3},{8,12},{12,8},{9,1... | collective-permute-start | bytes 3701768 | tf_op jit(solution)/shard_map/ppermute | solution.py:848
  68.0 78.5 %all-gather.11.cloned.1.call-start = ((), (), s32[]{:S(2)}) async-start(), calls=%async_computation.18 | async-start | bytes 3072000 | tf_op jit(solution)/shard_map/all_gather | solution.py:882
  94.7 30.0 %collective-permute-start.7 = (bf16[4,40,3840]{2,1,0:T(8,128)(2,1)}, bf16[4,40,3840]{2,1,0:T(8,128)(2,1)S(1)}, u32[]{:S(2)}, u32[]{:S(2)}) collective-permute-start(bf16[4,40,3840]{2,1,0:T(8,128)(2,1)} %bitcast.19.refs_0_), channel_id=1, source_target_pairs={{0,2},{1,3},{2,0},{3,1},{4,6},{5,7},{6,4},{7,5},{8,10},{9,11},{10,... | collective-permute-start | bytes 3686408 | tf_op jit(solution)/shard_map/ppermute | solution.py:848
  96.3 28.5 %collective-permute-start.6 = (bf16[4,40,3840]{2,1,0:T(8,128)(2,1)}, bf16[4,40,3840]{2,1,0:T(8,128)(2,1)}, u32[]{:S(2)}, u32[]{:S(2)}) collective-permute-start(bf16[4,40,3840]{2,1,0:T(8,128)(2,1)} %bitcast.19.refs_0_), channel_id=1, source_target_pairs={{0,4},{4,0},{1,5},{5,1},{2,6},{6,2},{3,7},{7,3},{8,12},{12,8},{9,1... | collective-permute-start | bytes 3686408 | tf_op jit(solution)/shard_map/ppermute | solution.py:848
  128.7 21.0 %collective-permute-start.8 = (bf16[4,40,1920]{2,1,0:T(8,128)(2,1)}, bf16[4,40,1920]{2,1,0:T(8,128)(2,1)}, u32[]{:S(2)}, u32[]{:S(2)}) collective-permute-start(bf16[4,40,1920]{2,1,0:T(8,128)(2,1)} %slice.153), channel_id=1, source_target_pairs={{0,2},{1,3},{2,0},{3,1},{4,6},{5,7},{6,4},{7,5},{8,10},{9,11},{10,... | collective-permute-start | bytes 1843208 | tf_op jit(solution)/shard_map/ppermute | solution.py:848
  129.3 20.4 %all-to-all-start.2 = ((bf16[4,320,256]{2,1,0:T(8,128)(2,1)}), bf16[4,320,256]{2,1,0:T(8,128)(2,1)S(1)}, u32[]{:S(2)}, u32[]{:S(2)}) async-start(bf16[4,320,256]{2,1,0:T(8,128)(2,1)} %bitcast.31), calls=%async_computation.2 | async-start | bytes 1310720 | tf_op jit(solution)/shard_map/all_to_all | solution.py:869
  133.1 19.3 %collective-permute-start.10 = (bf16[4,40,3840]{2,1,0:T(8,128)(2,1)}, bf16[4,40,3840]{2,1,0:T(8,128)(2,1)}, u32[]{:S(2)}, u32[]{:S(2)}) collective-permute-start(bf16[4,40,3840]{2,1,0:T(8,128)(2,1)} %bitcast.19.refs_0_), channel_id=1, source_target_pairs={{0,1},{1,0},{2,3},{3,2},{4,5},{5,4},{6,7},{7,6},{8,9},{9,8},{10,11... | collective-permute-start | bytes 3686408 | tf_op jit(solution)/shard_map/ppermute | solution.py:848
  133.6 20.2 %collective-permute-start.11 = (bf16[4,40,3840]{2,1,0:T(8,128)(2,1)}, bf16[4,40,3840]{2,1,0:T(8,128)(2,1)}, u32[]{:S(2)}, u32[]{:S(2)}) collective-permute-start(bf16[4,40,3840]{2,1,0:T(8,128)(2,1)} %collective-permute-done.6.refs_1_), channel_id=1, source_target_pairs={{0,1},{1,0},{2,3},{3,2},{4,5},{5,4},{6,7},{7,6},{8,9},{9,8},{10,11... | collective-permute-start | bytes 3686408 | tf_op jit(solution)/shard_map/ppermute | solution.py:848
  133.7 20.1 %collective-permute-start.12 = (bf16[4,40,3840]{2,1,0:T(8,128)(2,1)S(1)}, bf16[4,40,3840]{2,1,0:T(8,128)(2,1)}, u32[]{:S(2)}, u32[]{:S(2)}) collective-permute-start(bf16[4,40,3840]{2,1,0:T(8,128)(2,1)S(1)} %collective-permute-done.7.refs_2_), channel_id=1, source_target_pairs={{0,1},{1,0},{2,3},{3,2},{4,5},{5,4},{6,7},{7,6},{8,9},{9,8},{10,11... | collective-permute-start | bytes 3686408 | tf_op jit(solution)/shard_map/ppermute | solution.py:848
  152.4 29.5 %collective-permute-start.16 = (bf16[4,40,3840]{2,1,0:T(8,128)(2,1)S(1)}, bf16[4,40,3840]{2,1,0:T(8,128)(2,1)S(1)}, u32[]{:S(2)}, u32[]{:S(2)}) collective-permute-start(bf16[4,40,3840]{2,1,0:T(8,128)(2,1)S(1)} %get-tuple-element.234.along_ref), channel_id=1, source_target_pairs={{0,4},{4,0},{1,5},{5,1},{2,6},{6,2},{3,7},{7,3},{8,12},{12,8},{9,1... | collective-permute-start | bytes 3686408 | tf_op jit(solution)/shard_map/ppermute | solution.py:848
  182.6 28.3 %collective-permute-start.20 = (bf16[4,40,3840]{2,1,0:T(8,128)(2,1)S(1)}, bf16[4,40,3840]{2,1,0:T(8,128)(2,1)S(1)}, u32[]{:S(2)}, u32[]{:S(2)}) collective-permute-start(bf16[4,40,3840]{2,1,0:T(8,128)(2,1)S(1)} %get-tuple-element.133.refs_0_), channel_id=1, source_target_pairs={{0,2},{1,3},{2,0},{3,1},{4,6},{5,7},{6,4},{7,5},{8,10},{9,11},{10,... | collective-permute-start | bytes 3686408 | tf_op jit(solution)/shard_map/ppermute | solution.py:848
  183.4 28.2 %collective-permute-start.19 = (bf16[4,40,3840]{2,1,0:T(8,128)(2,1)S(1)}, bf16[4,40,3840]{2,1,0:T(8,128)(2,1)}, u32[]{:S(2)}, u32[]{:S(2)}) collective-permute-start(bf16[4,40,3840]{2,1,0:T(8,128)(2,1)S(1)} %get-tuple-element.133.refs_0_), channel_id=1, source_target_pairs={{0,4},{4,0},{1,5},{5,1},{2,6},{6,2},{3,7},{7,3},{8,12},{12,8},{9,1... | collective-permute-start | bytes 3686408 | tf_op jit(solution)/shard_map/ppermute | solution.py:848
  212.7 22.2 %collective-permute-start.22 = (bf16[4,40,1920]{2,1,0:T(8,128)(2,1)S(1)}, bf16[4,40,1920]{2,1,0:T(8,128)(2,1)S(1)}, u32[]{:S(2)}, u32[]{:S(2)}) collective-permute-start(bf16[4,40,1920]{2,1,0:T(8,128)(2,1)S(1)} %slice.167), channel_id=1, source_target_pairs={{0,4},{4,0},{1,5},{5,1},{2,6},{6,2},{3,7},{7,3},{8,12},{12,8},{9,1... | collective-permute-start | bytes 1843208 | tf_op jit(solution)/shard_map/ppermute | solution.py:848
  213.8 21.2 %collective-permute-start.21 = (bf16[4,40,1920]{2,1,0:T(8,128)(2,1)S(1)}, bf16[4,40,1920]{2,1,0:T(8,128)(2,1)S(1)}, u32[]{:S(2)}, u32[]{:S(2)}) collective-permute-start(bf16[4,40,1920]{2,1,0:T(8,128)(2,1)S(1)} %slice.166), channel_id=1, source_target_pairs={{0,2},{1,3},{2,0},{3,1},{4,6},{5,7},{6,4},{7,5},{8,10},{9,11},{10,... | collective-permute-start | bytes 1843208 | tf_op jit(solution)/shard_map/ppermute | solution.py:848
  215.0 20.5 %collective-permute-start.23 = (bf16[4,40,3840]{2,1,0:T(8,128)(2,1)S(1)}, bf16[4,40,3840]{2,1,0:T(8,128)(2,1)S(1)}, u32[]{:S(2)}, u32[]{:S(2)}) collective-permute-start(bf16[4,40,3840]{2,1,0:T(8,128)(2,1)S(1)} %get-tuple-element.133.refs_0_), channel_id=1, source_target_pairs={{0,1},{1,0},{2,3},{3,2},{4,5},{5,4},{6,7},{7,6},{8,9},{9,8},{10,11... | collective-permute-start | bytes 3686408 | tf_op jit(solution)/shard_map/ppermute | solution.py:848
  215.0 22.9 %collective-permute-start.24 = (bf16[4,40,3840]{2,1,0:T(8,128)(2,1)}, bf16[4,40,3840]{2,1,0:T(8,128)(2,1)S(1)}, u32[]{:S(2)}, u32[]{:S(2)}) collective-permute-start(bf16[4,40,3840]{2,1,0:T(8,128)(2,1)} %collective-permute-done.19.refs_1_), channel_id=1, source_target_pairs={{0,1},{1,0},{2,3},{3,2},{4,5},{5,4},{6,7},{7,6},{8,9},{9,8},{10,11... | collective-permute-start | bytes 3686408 | tf_op jit(solution)/shard_map/ppermute | solution.py:848
  215.6 22.4 %collective-permute-start.25 = (bf16[4,40,3840]{2,1,0:T(8,128)(2,1)S(1)}, bf16[4,40,3840]{2,1,0:T(8,128)(2,1)S(1)}, u32[]{:S(2)}, u32[]{:S(2)}) collective-permute-start(bf16[4,40,3840]{2,1,0:T(8,128)(2,1)S(1)} %collective-permute-done.20.refs_2_), channel_id=1, source_target_pairs={{0,1},{1,0},{2,3},{3,2},{4,5},{5,4},{6,7},{7,6},{8,9},{9,8},{10,11... | collective-permute-start | bytes 3686408 | tf_op jit(solution)/shard_map/ppermute | solution.py:848
  245.4 18.2 %collective-permute-start.28 = (bf16[128,1280]{1,0:T(8,128)(2,1)}, bf16[128,1280]{1,0:T(8,128)(2,1)}, u32[]{:S(2)}, u32[]{:S(2)}) collective-permute-start(bf16[128,1280]{1,0:T(8,128)(2,1)} %dynamic-slice_bitcast_fusion.3), channel_id=1, source_target_pairs={{0,4},{4,0},{1,5},{5,1},{2,6},{6,2},{3,7},{7,3},{8,12},{12,8},{9,1... | collective-permute-start | bytes 983048 | tf_op jit(solution)/shard_map/ppermute | solution.py:848
  254.9 107.0 %reduce-scatter.5.cloned.1.call-start = ((), (), s32[]{:S(2)}) async-start(), calls=%async_computation.12 | async-start | bytes 3276800 | tf_op jit(solution)/shard_map/reduce_scatter | solution.py:898
  309.4 41.6 %collective-permute-start.34 = (bf16[4,40,3840]{2,1,0:T(8,128)(2,1)}, bf16[4,40,3840]{2,1,0:T(8,128)(2,1)}, u32[]{:S(2)}, u32[]{:S(2)}) collective-permute-start(bf16[4,40,3840]{2,1,0:T(8,128)(2,1)} %pad_maximum_fusion), channel_id=1, source_target_pairs={{0,4},{4,0},{1,5},{5,1},{2,6},{6,2},{3,7},{7,3},{8,12},{12,8},{9,1... | collective-permute-start | bytes 3686408 | tf_op jit(solution)/shard_map/ppermute | solution.py:848
  326.4 35.5 %collective-permute-start.35 = (bf16[4,40,3840]{2,1,0:T(8,128)(2,1)}, bf16[4,40,3840]{2,1,0:T(8,128)(2,1)}, u32[]{:S(2)}, u32[]{:S(2)}) collective-permute-start(bf16[4,40,3840]{2,1,0:T(8,128)(2,1)} %pad_maximum_fusion.1), channel_id=1, source_target_pairs={{0,2},{1,3},{2,0},{3,1},{4,6},{5,7},{6,4},{7,5},{8,10},{9,11},{10,... | collective-permute-start | bytes 3686408 | tf_op jit(solution)/shard_map/ppermute | solution.py:848
  339.0 22.9 %all-to-all-start.5 = ((bf16[4,320,256]{2,1,0:T(8,128)(2,1)}), bf16[4,320,256]{2,1,0:T(8,128)(2,1)S(1)}, u32[]{:S(2)}, u32[]{:S(2)}) async-start(bf16[4,320,256]{2,1,0:T(8,128)(2,1)} %bitcast.64), calls=%async_computation.5 | async-start | bytes 1310720 | tf_op jit(solution)/shard_map/all_to_all | solution.py:869
  342.5 72.1 %reduce-scatter.7.cloned.1.call-start = ((), (), s32[]{:S(2)}) async-start(), calls=%async_computation.13 | async-start | bytes 1536000 | tf_op jit(solution)/shard_map/reduce_scatter | solution.py:898
  362.0 19.2 %collective-permute-start.36 = (bf16[2,2,4,40,3840]{4,3,2,1,0:T(8,128)(2,1)}, bf16[2,2,4,40,3840]{4,3,2,1,0:T(8,128)(2,1)}, u32[]{:S(2)}, u32[]{:S(2)}) collective-permute-start(bf16[2,2,4,40,3840]{4,3,2,1,0:T(8,128)(2,1)} %get-tuple-element.177), channel_id=1, source_target_pairs={{0,1},{1,0},{2,3},{3,2},{4,5},{5,4},{6,7},{7,6},{8,9},{9,8},{10,11... | collective-permute-start | bytes 14745608 | tf_op jit(solution)/shard_map/ppermute | solution.py:848
  384.6 67.9 %reduce-scatter.9.cloned.1.call-start = ((), (), s32[]{:S(2)}) async-start(), calls=%async_computation.14 | async-start | bytes 3276800 | tf_op jit(solution)/shard_map/reduce_scatter | solution.py:898
  397.8 91.0 %reduce-scatter.11.cloned.1.call-start = ((), (), s32[]{:S(2)}) async-start(), calls=%async_computation.15 | async-start | bytes 1536000 | tf_op jit(solution)/shard_map/reduce_scatter | solution.py:898
  422.5 29.6 %collective-permute-start.41 = (bf16[4,40,3840]{2,1,0:T(8,128)(2,1)S(1)}, bf16[4,40,3840]{2,1,0:T(8,128)(2,1)}, u32[]{:S(2)}, u32[]{:S(2)}) collective-permute-start(bf16[4,40,3840]{2,1,0:T(8,128)(2,1)S(1)} %pad_maximum_fusion.2), channel_id=1, source_target_pairs={{0,4},{4,0},{1,5},{5,1},{2,6},{6,2},{3,7},{7,3},{8,12},{12,8},{9,1... | collective-permute-start | bytes 3686408 | tf_op jit(solution)/shard_map/ppermute | solution.py:848
  423.2 29.3 %collective-permute-start.42 = (bf16[4,40,3840]{2,1,0:T(8,128)(2,1)S(1)}, bf16[4,40,3840]{2,1,0:T(8,128)(2,1)}, u32[]{:S(2)}, u32[]{:S(2)}) collective-permute-start(bf16[4,40,3840]{2,1,0:T(8,128)(2,1)S(1)} %pad_maximum_fusion.3), channel_id=1, source_target_pairs={{0,2},{1,3},{2,0},{3,1},{4,6},{5,7},{6,4},{7,5},{8,10},{9,11},{10,... | collective-permute-start | bytes 3686408 | tf_op jit(solution)/shard_map/ppermute | solution.py:848
  461.3 18.3 %collective-permute-start.48 = (bf16[160,960]{1,0:T(8,128)(2,1)S(1)}, bf16[160,960]{1,0:T(8,128)(2,1)S(1)}, u32[]{:S(2)}, u32[]{:S(2)}) collective-permute-start(bf16[160,960]{1,0:T(8,128)(2,1)S(1)} %dynamic-slice_bitcast_fusion), channel_id=1, source_target_pairs={{0,4},{4,0},{1,5},{5,1},{2,6},{6,2},{3,7},{7,3},{8,12},{12,8},{9,1... | collective-permute-start | bytes 921608 | tf_op jit(solution)/shard_map/ppermute | solution.py:848
  (98 other events, 762.2 us)
Sparse Core Ops, SparseCore 0:
  27.1 34.1 all-gather.6
  63.4 30.2 all-gather.8
  95.3 51.1 all-gather.10
  309.6 50.4 reduce-scatter.4
  366.4 29.6 reduce-scatter.6
  398.3 51.7 reduce-scatter.8
  460.0 28.7 reduce-scatter.10

commit v19 on v18

--- a/solution.py
+++ b/solution.py
@@ -914,11 +914,49 @@
     return one + two
 
 
+def quarter_kernel(place_ref, one_ref, two_ref, *refs):
+    total = one_ref[0, 0, 0].astype(F32) + two_ref[0, 0, 0].astype(F32)
+    for ref in refs[:-1]:
+        total = total + ref[0].astype(F32)
+    refs[-1][0] = total.astype(BF16)
+
+
+def quarter_rows(parts, flipped, *more):
+    _, _, batch, own, columns = parts[0].shape
+    rows = pl.BlockSpec((1, own, columns), lambda i, at: (i, 0, 0))
+
+    def quarter_at(i, at):
+        return (1 - at[0], 1 - at[1], i, 0, 0) if flipped else (at[0], at[1], i, 0, 0)
+
+    part = pl.BlockSpec((1, 1, 1, own, columns), quarter_at)
+    return pl.pallas_call(
+        quarter_kernel,
+        grid_spec=pltpu.PrefetchScalarGridSpec(
+            num_scalar_prefetch=1,
+            grid=(batch,),
+            in_specs=[part, part] + [rows] * len(more),
+            out_specs=rows,
+        ),
+        out_shape=pltpu.HBM((batch, own, columns), BF16),
+        compiler_params=KERNEL,
+        cost_estimate=LIGHT,
+    )(place(), *in_hbm(*parts, *more))
+
+
 def diagonal_rows(parts):
-    blk, row = place()[:2]
-    rows = quarter(parts, 1 - blk, 1 - row).astype(BF16)
+    rows = quarter_rows(parts, True)
     half = rows.shape[-1] // 2
     return rows[..., :half], rows[..., half:]
+
+
+def beside_rows(parts, diagonal):
+    blk, row = place()[:2]
+    return (quarter(parts, blk, 1 - row) + diagonal.astype(F32)).astype(BF16)
+
+
+def across_rows(parts):
+    blk, row = place()[:2]
+    return quarter(parts, 1 - blk, row).astype(BF16)
 
 
 def neighbour_rows(parts, one, two):
@@ -939,8 +977,7 @@
 
 
 def own_sum(parts, across, beside):
-    blk, row = place()[:2]
-    return quarter(parts, blk, row) + across.astype(F32) + beside.astype(F32)
+    return quarter_rows(parts, False, across, beside)
 
 
 def sum_over(array, *hops):
@@ -1067,6 +1104,9 @@
         )
         out_bar = middle_grad.astype(BF16)
         if layer == 0:
+            out_bar, diagonal = tied(out_bar, diagonal)
+            out_bar, rows = tied(out_bar, beside_rows(cored, diagonal))
+            beside = swapped(rows, "head", 2)
             attended_grad = over_head(heads_grad(out_w, out_bar))
             grads, others = dense_grads(attended_t, normed_two, active, out_bar, up_bar, down_bar)
             attended_grad, others, z_sum, across, beside = tied(
@@ -1103,24 +1143,24 @@
             halves, own = tied(halves, own_sum(cored, *sent))
             dense_first = over_batch(own)
             normed_grad = scatter_row(halves)
-            z_across, dense_first = tied(across_sum(z_sum), dense_first)
+            z_across = across_sum(z_sum)
             z_across = over_head(z_across.reshape(4, -1, z_across.shape[-1]))
+            z_across, dense_first = tied(z_across, dense_first)
             dense_grad = [dense_first, summed]
             qkv_grads = [columns_to_rows(z_across), columns_to_rows(moved)]
         else:
             bars, others = tied(bars, others)
             cored = (grads, others)
-            bars, rows = tied(bars, diagonal_rows(cored))
-            diagonal = sent_beside_and_across(*rows)
             halves, to_core, qkv_grad = project_back(bars, qkv, normed_all, token_rows)
             z_sum = over_batch(qkv_grad.reshape(4, 2, -1, qkv_grad.shape[-1]))
-            to_core, halves, diagonal = tied(to_core, halves, diagonal)
-            to_core, rows = tied(to_core, neighbour_rows(cored, *diagonal))
-            across = swapped(rows[0], "blk", 1)
+            to_core, grads = tied(to_core, grads)
+            rows = quarter_rows((grads, others), True)
             halves = halves + other_core(to_core).astype(F32)
+            halves, rows = tied(halves, rows)
+            diagonal = swapped(rows, "blk", 1)
             normed_grad = scatter_row(halves)
-            normed_grad, beside = tied(normed_grad, rows[1])
-            beside = swapped(beside, "head", 2)
+            normed_grad, rows = tied(normed_grad, across_rows(cored))
+            across = swapped(rows, "blk", 1)
         upper = middle_grad + lower_of(normed_grad, stream, factor_one, gains[layer])
     input_grad = swap_halves(upper.astype(BF16).reshape(tokens.shape)).astype(F32)
     scale_total = sum_over(scale_sum, ("head", 2), ("blk", 1))

time: 517 us -> 520 us (level)
  Pallas kernels: 121 us -> 141 us
  other arithmetic: 46.9 us -> 35.3 us
    pallas_call x0 -> x4, Pallas kernels: none -> 18.8 us  [quarter_rows(): pl.pallas_call(quarter_kernel, grid_spec=pltpu.PrefetchScalarGridSpec(num...]
    ppermute x51 -> x50, waiting for transfers between devices: 131 us -> 123 us  [swapped(): return lax.ppermute(array, axis, [(i, i ^ mask) for i in range(size)])]
    add x2 -> x0, other arithmetic: 8.21 us -> none  [own_sum(): return quarter(parts, blk, row) + across.astype(F32) + beside.astype(F32)]
    all_to_all x7, waiting for transfers between devices: 24.7 us -> 31.6 us  [over_head(): lax.all_to_all(parts, 'head', split_axis=0, concat_axis=0, tiled=True)]
    convert_element_type x0 -> x2, other arithmetic: none -> 5.27 us  [the longest x1 3.13 us: across_rows(): return quarter(parts, 1 - blk, row).astype(BF16)]
    unnamed x130 -> x154, local copies, waits for them, and re-layouts: 14.1 us -> 19.4 us
    add x2 -> x1, other arithmetic: 8.55 us -> 3.33 us  [quarter(): return one + two]
    ppermute x51 -> x50, starting transfers between devices: 42.2 us -> 40.2 us  [swapped(): return lax.ppermute(array, axis, [(i, i ^ mask) for i in range(size)])]
  transfers between devices with their start and end apart: 65 -> 64, of which waited for: 31 -> 28; matrix products, arithmetic and copies ran while one was open for 13% -> 11% of each run, Pallas kernels for 23% -> 24%
where the time goes in v19:
time: 520 us; the launch traced here: 512 us
  waiting for transfers between devices  178 us (34%)
  Pallas kernels  141 us (27%)
  starting transfers between devices  65.5 us (13%)
  local copies, waits for them, and re-layouts  37.6 us (7%)
  other arithmetic  35.3 us (7%)
  blocking collectives  19.4 us (4%)
  matrix products  19.3 us (4%)
  between operations  15.7 us (3%)
    ppermute x50, waiting for transfers between devices, swapped(): return lax.ppermute(array, axis, [(i, i ^ mask) for i in range(size)])  123 us
    ppermute x50, starting transfers between devices, swapped(): return lax.ppermute(array, axis, [(i, i ^ mask) for i in range(size)])  40.2 us
    all_to_all x7, waiting for transfers between devices, over_head(): lax.all_to_all(parts, 'head', split_axis=0, concat_axis=0, tiled=True)  31.6 us
    pallas_call x2, Pallas kernels, attend_back_rows(): pl.pallas_call(functools.partial(attend_back_kernel, token_rows), grid=(l...  24.6 us
    all_to_all x7, starting transfers between devices, over_head(): lax.all_to_all(parts, 'head', split_axis=0, concat_axis=0, tiled=True)  24.5 us
    all_gather x3, waiting for transfers between devices, along_batch(): return lax.all_gather(piece, 'batch', axis=0, tiled=False)  23.7 us
    unnamed x154, local copies, waits for them, and re-layouts  19.4 us
    all_to_all x1, blocking collectives, over_head(): lax.all_to_all(parts, 'head', split_axis=0, concat_axis=0, tiled=True)  19.4 us
  transfers between devices with their start and end apart: 64, of which 28 were waited for; matrix products, arithmetic and copies ran while one was open for 11% of the time, Pallas kernels for 24%

profile of v19, /device:TPU:0, one launch (start us, length us, event | category | flops | bytes accessed | tf_op | source)
XLA Modules:
  0.0 511.8 jit_solution(3282419357161636677)
XLA Ops:
  18.6 8.3 %collective-permute-done = bf16[128,1280]{1,0:T(8,128)(2,1)S(1)} collective-permute-done((bf16[128,1280]{1,0:T(8,128)(2,1)S(1)}, bf16[128,1280]{1,0:T(8,128)(2,1)S(1)}, u32[]{:S(2)}, u32[]{:S(2)}) %collective-permute-start) | collective-permute-done | bytes 327712 | tf_op jit(solution)/shard_map/ppermute | solution.py:848
  31.5 12.4 %collective-permute-done.2.refs_2_ = bf16[256,1280]{1,0:T(8,128)(2,1)S(1)} collective-permute-done((bf16[256,1280]{1,0:T(8,128)(2,1)S(1)}, bf16[256,1280]{1,0:T(8,128)(2,1)S(1)}, u32[]{:S(2)}, u32[]{:S(2)}) %collective-permute-start.2) | collective-permute-done | bytes 655392 | tf_op jit(solution)/shard_map/ppermute | solution.py:848
  47.0 15.2 %all-gather.7.cloned.1.call-done = bf16[640,964]{1,0:T(8,128)(2,1)} async-done(((bf16[160,964]{1,0:T(8,128)(2,1)}), bf16[640,964]{1,0:T(8,128)(2,1)}) %all-gather.7.cloned.1.call-update) | async-done | bytes 1233936 | tf_op jit(solution)/shard_map/all_gather | solution.py:882
  68.9 6.6 %all-to-all-done.1 = bf16[4,40,960]{2,1,0:T(8,128)(2,1)S(1)} async-done(((bf16[4,40,960]{2,1,0:T(8,128)(2,1)}), bf16[4,40,960]{2,1,0:T(8,128)(2,1)S(1)}, u32[]{:S(2)}, u32[]{:S(2)}) %all-to-all-start.1) | async-done | bytes 307232 | tf_op jit(solution)/shard_map/all_to_all | solution.py:869
  75.8 16.5 %collective-permute-done.5.across_ref = bf16[4,160,964]{2,1,0:T(8,128)(2,1)S(1)} collective-permute-done((bf16[4,160,964]{2,1,0:T(8,128)(2,1)}, bf16[4,160,964]{2,1,0:T(8,128)(2,1)S(1)}, u32[]{:S(2)}, u32[]{:S(2)}) %collective-permute-start.5) | collective-permute-done | bytes 1233952 | tf_op jit(solution)/shard_map/ppermute | solution.py:848
  99.0 4.6 shard_map.169
  105.0 8.8 %shard_map.170 = (bf16[1024,1280]{1,0:T(8,128)(2,1)}, f32[960,1024]{1,0:T(8,128)}) custom-call(s32[3]{0:T(128)S(1)} %pad_add_fusion.place_ref.core_ref, bf16[256,1280]{1,0:T(8,128)(2,1)} %bitcast.221, bf16[256,1280]{1,0:T(8,128)(2,1)} %copy-done.56, bf16[256,1280]{1,0:T(8,128)(2,1)} %copy-done.55, bf16[256,1280]{1,0:T(8,128)(2,1)} %collective-permute-done.3.refs_3_, ...), custom_call_target="tpu_custom_call" | custom-call | flops 1048576 | bytes 1048576 | tf_op jit(solution)/shard_map/pallas_call | solution.py:711
  116.0 9.6 %shard_map.171 = (bf16[4,4,80,256]{3,2,1,0:T(8,128)(2,1)}, f32[4,1,1024]{2,1,0:T(1,128)S(1)}) custom-call(f32[3,4,80,1024]{3,2,1,0:T(8,128)S(1)} %bitcast.192, f32[80,1]{1,0:T(8,128)S(1)} %copy.60.scale_ref, s32[1024,1]{1,0:T(8,128)S(1)} %copy.61.col_ref, s32[1,1024]{1,0:T(1,128)S(1)} %constant_dynamic-slice_fusion.row_ref), custom_call_target="tpu_custom_call" | custom-call | flops 1048576 | bytes 1048576 | tf_op jit(solution)/shard_map/pallas_call | solution.py:413
  134.1 7.1 %collective-permute-done.9.refs_4_ = bf16[4,40,1920]{2,1,0:T(8,128)(2,1)} collective-permute-done((bf16[4,40,1920]{2,1,0:T(8,128)(2,1)}, bf16[4,40,1920]{2,1,0:T(8,128)(2,1)}, u32[]{:S(2)}, u32[]{:S(2)}) %collective-permute-start.9) | collective-permute-done | bytes 614432 | tf_op jit(solution)/shard_map/ppermute | solution.py:848
  141.2 6.2 %all-gather.11.cloned.1.call-done = bf16[8,40,3840]{2,1,0:T(8,128)(2,1)} async-done(((bf16[2,40,3840]{2,1,0:T(8,128)(2,1)}), bf16[8,40,3840]{2,1,0:T(8,128)(2,1)}) %all-gather.11.cloned.1.call-update) | async-done | bytes 2457616 | tf_op jit(solution)/shard_map/all_gather | solution.py:882
  153.6 4.5 shard_map.172
  166.0 15.7 %collective-permute-done.16.across_ref = bf16[4,40,3840]{2,1,0:T(8,128)(2,1)S(1)} collective-permute-done((bf16[4,40,3840]{2,1,0:T(8,128)(2,1)S(1)}, bf16[4,40,3840]{2,1,0:T(8,128)(2,1)S(1)}, u32[]{:S(2)}, u32[]{:S(2)}) %collective-permute-start.16) | collective-permute-done | bytes 1228832 | tf_op jit(solution)/shard_map/ppermute | solution.py:848
  184.4 4.7 shard_map.173
  189.1 7.8 %shard_map.174 = (bf16[1024,1280]{1,0:T(8,128)(2,1)}, f32[960,1024]{1,0:T(8,128)}) custom-call(s32[3]{0:T(128)S(1)} %pad_add_fusion.place_ref.core_ref, bf16[256,1280]{1,0:T(8,128)(2,1)} %multiply_convert_fusion.2.refs_0_, bf16[256,1280]{1,0:T(8,128)(2,1)} %collective-permute-done.17.refs_1_, bf16[256,1280]{1,0:T(8,128)(2,1)} %collective-permute-done.15.refs_2_, ...), custom_call_target="tpu_custom_call" | custom-call | flops 1048576 | bytes 1048576 | tf_op jit(solution)/shard_map/pallas_call | solution.py:711
  199.0 8.9 %shard_map.175 = (bf16[4,4,80,256]{3,2,1,0:T(8,128)(2,1)S(1)}, f32[4,1,1024]{2,1,0:T(1,128)S(1)}) custom-call(f32[3,4,80,1024]{3,2,1,0:T(8,128)S(1)} %bitcast.194, f32[80,1]{1,0:T(8,128)S(1)} %copy.64.scale_ref, s32[1024,1]{1,0:T(8,128)S(1)} %copy.61.col_ref, s32[1,1024]{1,0:T(1,128)S(1)} %constant_dynamic-slice_fusion.row_ref), custom_call_target="tpu_custom_call" | custom-call | flops 1048576 | bytes 1048576 | tf_op jit(solution)/shard_map/pallas_call | solution.py:413
  215.4 19.4 %all_to_all.40 = bf16[4,320,256]{2,1,0:T(8,128)(2,1)S(1)} all-to-all(bf16[4,320,256]{2,1,0:T(8,128)(2,1)S(1)} %bitcast.209), channel_id=1, replica_groups=mesh['batch'=4,'blk'=2,'head'=4] {'head'}, dimensions={0} | all-to-all | bytes 1310720 | tf_op jit(solution)/shard_map/all_to_all | solution.py:869
  255.2 8.5 %shard_map.177 = (bf16[2,2,4,40,3840]{4,3,2,1,0:T(8,128)(2,1)}, bf16[2,2,4,40,3840]{4,3,2,1,0:T(8,128)(2,1)}) custom-call(s32[3]{0:T(128)S(1)} %pad_add_fusion.place_ref.core_ref, bf16[1280,256]{1,0:T(8,128)(2,1)} %bitcast.233, bf16[256,1280]{1,0:T(8,128)(2,1)} %copy-done.28, bf16[256,1280]{1,0:T(8,128)(2,1)} %copy-done.53, bf16[256,1280]{1,0:T(8,128)(2,1)} %copy-done.29, ...), custom_call_target="tpu_custom_call" | custom-call | flops 1048576 | bytes 1048576 | tf_op jit(solution)/shard_map/pallas_call | solution.py:577
  265.7 12.3 %shard_map.178 = (bf16[3,4,80,1024]{3,2,1,0:T(8,128)(2,1)}, f32[80,128]{1,0:T(8,128)}) custom-call(f32[3,4,80,1024]{3,2,1,0:T(8,128)} %bitcast.193, bf16[4,4,80,256]{3,2,1,0:T(8,128)(2,1)} %bitcast.235, f32[4,1,1024]{2,1,0:T(1,128)S(1)} %get-tuple-element.146.lse_ref, f32[80,1]{1,0:T(8,128)S(1)} %copy.64.scale_ref, s32[1024,1]{1,0:T(8,128)S(1)} %copy.61.col_ref, ...), custom_call_target="tpu_custom_call" | custom-call | flops 1048576 | bytes 1048576 | tf_op jit(solution)/shard_map/pallas_call | solution.py:506
  278.1 12.3 %shard_map.179 = (f32[2,2,128,1280]{3,2,1,0:T(8,128)}, bf16[2,2,128,1280]{3,2,1,0:T(8,128)(2,1)}, bf16[1280,960]{1,0:T(8,128)(2,1)}) custom-call(s32[3]{0:T(128)S(1)} %pad_add_fusion.place_ref.core_ref, bf16[960,1024]{1,0:T(8,128)(2,1)} %bitcast.237, bf16[1280,960]{1,0:T(8,128)(2,1)} %bitcast.211, bf16[1024,1280]{1,0:T(8,128)(2,1)} %get-tuple-element.150.normed_ref), custom_call_target="tpu_custom_call" | custom-call | flops 1048576 | bytes 1048576 | tf_op jit(solution)/shard_map/pallas_call | solution.py:757
  290.6 4.7 shard_map.180
  304.9 10.8 %collective-permute-done.31 = bf16[2,128,1280]{2,1,0:T(8,128)(2,1)} collective-permute-done((bf16[2,128,1280]{2,1,0:T(8,128)(2,1)S(1)}, bf16[2,128,1280]{2,1,0:T(8,128)(2,1)}, u32[]{:S(2)}, u32[]{:S(2)}) %collective-permute-start.31) | collective-permute-done | bytes 655392 | tf_op jit(solution)/shard_map/ppermute | solution.py:848
  326.9 6.6 %collective-permute-done.32 = bf16[4,40,3840]{2,1,0:T(8,128)(2,1)S(1)} collective-permute-done((bf16[4,40,3840]{2,1,0:T(8,128)(2,1)}, bf16[4,40,3840]{2,1,0:T(8,128)(2,1)S(1)}, u32[]{:S(2)}, u32[]{:S(2)}) %collective-permute-start.32) | collective-permute-done | bytes 1228832 | tf_op jit(solution)/shard_map/ppermute | solution.py:848
  341.5 8.6 %shard_map.181 = (bf16[2,2,4,40,3840]{4,3,2,1,0:T(8,128)(2,1)}, bf16[2,2,4,40,3840]{4,3,2,1,0:T(8,128)(2,1)}) custom-call(s32[3]{0:T(128)S(1)} %pad_add_fusion.place_ref.core_ref, bf16[1280,256]{1,0:T(8,128)(2,1)} %bitcast.230, bf16[256,1280]{1,0:T(8,128)(2,1)} %copy-done.27, bf16[256,1280]{1,0:T(8,128)(2,1)} %copy-done.49, bf16[256,1280]{1,0:T(8,128)(2,1)} %copy-done.35, ...), custom_call_target="tpu_custom_call" | custom-call | flops 1048576 | bytes 1048576 | tf_op jit(solution)/shard_map/pallas_call | solution.py:577
  350.1 20.0 %all-to-all-done.5 = bf16[4,320,256]{2,1,0:T(8,128)(2,1)S(1)} async-done(((bf16[4,320,256]{2,1,0:T(8,128)(2,1)}), bf16[4,320,256]{2,1,0:T(8,128)(2,1)S(1)}, u32[]{:S(2)}, u32[]{:S(2)}) %all-to-all-start.5) | async-done | bytes 655392 | tf_op jit(solution)/shard_map/all_to_all | solution.py:869
  370.2 4.9 shard_map.182
  377.7 12.3 %shard_map.183 = (bf16[3,4,80,1024]{3,2,1,0:T(8,128)(2,1)}, f32[80,128]{1,0:T(8,128)}) custom-call(f32[3,4,80,1024]{3,2,1,0:T(8,128)} %bitcast.191, bf16[4,4,80,256]{3,2,1,0:T(8,128)(2,1)} %bitcast.234, f32[4,1,1024]{2,1,0:T(1,128)S(1)} %get-tuple-element.171.lse_ref, f32[80,1]{1,0:T(8,128)S(1)} %copy.60.scale_ref, s32[1024,1]{1,0:T(8,128)S(1)} %copy.61.col_ref, ...), custom_call_target="tpu_custom_call" | custom-call | flops 1048576 | bytes 1048576 | tf_op jit(solution)/shard_map/pallas_call | solution.py:506
  394.4 7.3 %shard_map.184 = bf16[1280,960]{1,0:T(8,128)(2,1)} custom-call(bf16[960,1024]{1,0:T(8,128)(2,1)} %bitcast.225, bf16[1024,1280]{1,0:T(8,128)(2,1)} %get-tuple-element.176.normed_ref), custom_call_target="tpu_custom_call" | custom-call | flops 1048576 | bytes 1048576 | tf_op jit(solution)/shard_map/pallas_call | solution.py:828
  401.7 4.3 shard_map.185
  416.8 8.5 %shard_map.186 = (f32[2,2,128,1280]{3,2,1,0:T(8,128)}, bf16[2,2,128,1280]{3,2,1,0:T(8,128)(2,1)}) custom-call(s32[3]{0:T(128)S(1)} %pad_add_fusion.place_ref.core_ref, bf16[960,1024]{1,0:T(8,128)(2,1)} %bitcast.226, bf16[1280,960]{1,0:T(8,128)(2,1)} %bitcast.218), custom_call_target="tpu_custom_call" | custom-call | flops 1048576 | bytes 1048576 | tf_op jit(solution)/shard_map/pallas_call | solution.py:798
  444.3 15.2 %collective-permute-done.40.refs_0_ = bf16[4,40,3840]{2,1,0:T(8,128)(2,1)S(1)} collective-permute-done((bf16[4,40,3840]{2,1,0:T(8,128)(2,1)S(1)}, bf16[4,40,3840]{2,1,0:T(8,128)(2,1)S(1)}, u32[]{:S(2)}, u32[]{:S(2)}) %collective-permute-start.40) | collective-permute-done | bytes 1228832 | tf_op jit(solution)/shard_map/ppermute | solution.py:848
  460.8 4.9 shard_map.187
  471.7 11.4 %collective-permute-done.48 = f32[2,80]{1,0:T(2,128)S(1)} collective-permute-done((f32[2,80]{1,0:T(2,128)S(1)}, f32[2,80]{1,0:T(2,128)S(1)}, u32[]{:S(2)}, u32[]{:S(2)}) %collective-permute-start.48) | collective-permute-done | bytes 672 | tf_op jit(solution)/shard_map/ppermute | solution.py:848
  (392 shorter events, 187.1 us)
Async XLA Ops:
  9.0 34.9 %collective-permute-start.4 = (bf16[128,1280]{1,0:T(8,128)(2,1)}, bf16[128,1280]{1,0:T(8,128)(2,1)}, u32[]{:S(2)}, u32[]{:S(2)}) collective-permute-start(bf16[128,1280]{1,0:T(8,128)(2,1)} %dynamic-slice_bitcast_fusion.4), channel_id=1, source_target_pairs={{0,4},{4,0},{1,5},{5,1},{2,6},{6,2},{3,7},{7,3},{8,12},{12,8},{9,1... | collective-permute-start | bytes 983048 | tf_op jit(solution)/shard_map/ppermute | solution.py:848
  18.5 43.7 %all-gather.7.cloned.1.call-start = ((), (), s32[]{:S(2)}) async-start(), calls=%async_computation.16 | async-start | bytes 1638400 | tf_op jit(solution)/shard_map/all_gather | solution.py:882
  27.8 66.8 %all-gather.9.cloned.1.call-start = ((), (), s32[]{:S(2)}) async-start(), calls=%async_computation.17 | async-start | bytes 1536000 | tf_op jit(solution)/shard_map/all_gather | solution.py:882
  62.2 30.1 %collective-permute-start.5 = (bf16[4,160,964]{2,1,0:T(8,128)(2,1)}, bf16[4,160,964]{2,1,0:T(8,128)(2,1)S(1)}, u32[]{:S(2)}, u32[]{:S(2)}) collective-permute-start(bf16[4,160,964]{2,1,0:T(8,128)(2,1)} %bitcast.243), channel_id=1, source_target_pairs={{0,4},{4,0},{1,5},{5,1},{2,6},{6,2},{3,7},{7,3},{8,12},{12,8},{9,1... | collective-permute-start | bytes 3701768 | tf_op jit(solution)/shard_map/ppermute | solution.py:848
  68.9 78.5 %all-gather.11.cloned.1.call-start = ((), (), s32[]{:S(2)}) async-start(), calls=%async_computation.18 | async-start | bytes 3072000 | tf_op jit(solution)/shard_map/all_gather | solution.py:882
  95.6 30.0 %collective-permute-start.7 = (bf16[4,40,3840]{2,1,0:T(8,128)(2,1)}, bf16[4,40,3840]{2,1,0:T(8,128)(2,1)S(1)}, u32[]{:S(2)}, u32[]{:S(2)}) collective-permute-start(bf16[4,40,3840]{2,1,0:T(8,128)(2,1)} %bitcast.19.refs_0_), channel_id=1, source_target_pairs={{0,2},{1,3},{2,0},{3,1},{4,6},{5,7},{6,4},{7,5},{8,10},{9,11},{10,... | collective-permute-start | bytes 3686408 | tf_op jit(solution)/shard_map/ppermute | solution.py:848
  97.1 28.5 %collective-permute-start.6 = (bf16[4,40,3840]{2,1,0:T(8,128)(2,1)}, bf16[4,40,3840]{2,1,0:T(8,128)(2,1)}, u32[]{:S(2)}, u32[]{:S(2)}) collective-permute-start(bf16[4,40,3840]{2,1,0:T(8,128)(2,1)} %bitcast.19.refs_0_), channel_id=1, source_target_pairs={{0,4},{4,0},{1,5},{5,1},{2,6},{6,2},{3,7},{7,3},{8,12},{12,8},{9,1... | collective-permute-start | bytes 3686408 | tf_op jit(solution)/shard_map/ppermute | solution.py:848
  128.8 20.8 %collective-permute-start.8 = (bf16[4,40,1920]{2,1,0:T(8,128)(2,1)S(1)}, bf16[4,40,1920]{2,1,0:T(8,128)(2,1)}, u32[]{:S(2)}, u32[]{:S(2)}) collective-permute-start(bf16[4,40,1920]{2,1,0:T(8,128)(2,1)S(1)} %slice.133), channel_id=1, source_target_pairs={{0,2},{1,3},{2,0},{3,1},{4,6},{5,7},{6,4},{7,5},{8,10},{9,11},{10,... | collective-permute-start | bytes 1843208 | tf_op jit(solution)/shard_map/ppermute | solution.py:848
  129.4 20.2 %all-to-all-start.2 = ((bf16[4,320,256]{2,1,0:T(8,128)(2,1)}), bf16[4,320,256]{2,1,0:T(8,128)(2,1)S(1)}, u32[]{:S(2)}, u32[]{:S(2)}) async-start(bf16[4,320,256]{2,1,0:T(8,128)(2,1)} %bitcast.31), calls=%async_computation.2 | async-start | bytes 1310720 | tf_op jit(solution)/shard_map/all_to_all | solution.py:869
  133.1 19.2 %collective-permute-start.10 = (bf16[4,40,3840]{2,1,0:T(8,128)(2,1)}, bf16[4,40,3840]{2,1,0:T(8,128)(2,1)}, u32[]{:S(2)}, u32[]{:S(2)}) collective-permute-start(bf16[4,40,3840]{2,1,0:T(8,128)(2,1)} %bitcast.19.refs_0_), channel_id=1, source_target_pairs={{0,1},{1,0},{2,3},{3,2},{4,5},{5,4},{6,7},{7,6},{8,9},{9,8},{10,11... | collective-permute-start | bytes 3686408 | tf_op jit(solution)/shard_map/ppermute | solution.py:848
  133.6 20.0 %collective-permute-start.11 = (bf16[4,40,3840]{2,1,0:T(8,128)(2,1)}, bf16[4,40,3840]{2,1,0:T(8,128)(2,1)}, u32[]{:S(2)}, u32[]{:S(2)}) collective-permute-start(bf16[4,40,3840]{2,1,0:T(8,128)(2,1)} %collective-permute-done.6.refs_1_), channel_id=1, source_target_pairs={{0,1},{1,0},{2,3},{3,2},{4,5},{5,4},{6,7},{7,6},{8,9},{9,8},{10,11... | collective-permute-start | bytes 3686408 | tf_op jit(solution)/shard_map/ppermute | solution.py:848
  133.7 19.9 %collective-permute-start.12 = (bf16[4,40,3840]{2,1,0:T(8,128)(2,1)S(1)}, bf16[4,40,3840]{2,1,0:T(8,128)(2,1)}, u32[]{:S(2)}, u32[]{:S(2)}) collective-permute-start(bf16[4,40,3840]{2,1,0:T(8,128)(2,1)S(1)} %collective-permute-done.7.refs_2_), channel_id=1, source_target_pairs={{0,1},{1,0},{2,3},{3,2},{4,5},{5,4},{6,7},{7,6},{8,9},{9,8},{10,11... | collective-permute-start | bytes 3686408 | tf_op jit(solution)/shard_map/ppermute | solution.py:848
  152.3 29.5 %collective-permute-start.16 = (bf16[4,40,3840]{2,1,0:T(8,128)(2,1)S(1)}, bf16[4,40,3840]{2,1,0:T(8,128)(2,1)S(1)}, u32[]{:S(2)}, u32[]{:S(2)}) collective-permute-start(bf16[4,40,3840]{2,1,0:T(8,128)(2,1)S(1)} %get-tuple-element.226.along_ref), channel_id=1, source_target_pairs={{0,4},{4,0},{1,5},{5,1},{2,6},{6,2},{3,7},{7,3},{8,12},{12,8},{9,1... | collective-permute-start | bytes 3686408 | tf_op jit(solution)/shard_map/ppermute | solution.py:848
  182.5 28.3 %collective-permute-start.20 = (bf16[4,40,3840]{2,1,0:T(8,128)(2,1)S(1)}, bf16[4,40,3840]{2,1,0:T(8,128)(2,1)S(1)}, u32[]{:S(2)}, u32[]{:S(2)}) collective-permute-start(bf16[4,40,3840]{2,1,0:T(8,128)(2,1)S(1)} %get-tuple-element.131.refs_0_), channel_id=1, source_target_pairs={{0,2},{1,3},{2,0},{3,1},{4,6},{5,7},{6,4},{7,5},{8,10},{9,11},{10,... | collective-permute-start | bytes 3686408 | tf_op jit(solution)/shard_map/ppermute | solution.py:848
  183.2 28.2 %collective-permute-start.19 = (bf16[4,40,3840]{2,1,0:T(8,128)(2,1)S(1)}, bf16[4,40,3840]{2,1,0:T(8,128)(2,1)}, u32[]{:S(2)}, u32[]{:S(2)}) collective-permute-start(bf16[4,40,3840]{2,1,0:T(8,128)(2,1)S(1)} %get-tuple-element.131.refs_0_), channel_id=1, source_target_pairs={{0,4},{4,0},{1,5},{5,1},{2,6},{6,2},{3,7},{7,3},{8,12},{12,8},{9,1... | collective-permute-start | bytes 3686408 | tf_op jit(solution)/shard_map/ppermute | solution.py:848
  212.6 22.2 %collective-permute-start.22 = (bf16[4,40,1920]{2,1,0:T(8,128)(2,1)S(1)}, bf16[4,40,1920]{2,1,0:T(8,128)(2,1)S(1)}, u32[]{:S(2)}, u32[]{:S(2)}) collective-permute-start(bf16[4,40,1920]{2,1,0:T(8,128)(2,1)S(1)} %slice.147), channel_id=1, source_target_pairs={{0,4},{4,0},{1,5},{5,1},{2,6},{6,2},{3,7},{7,3},{8,12},{12,8},{9,1... | collective-permute-start | bytes 1843208 | tf_op jit(solution)/shard_map/ppermute | solution.py:848
  213.6 21.2 %collective-permute-start.21 = (bf16[4,40,1920]{2,1,0:T(8,128)(2,1)S(1)}, bf16[4,40,1920]{2,1,0:T(8,128)(2,1)S(1)}, u32[]{:S(2)}, u32[]{:S(2)}) collective-permute-start(bf16[4,40,1920]{2,1,0:T(8,128)(2,1)S(1)} %slice.146), channel_id=1, source_target_pairs={{0,2},{1,3},{2,0},{3,1},{4,6},{5,7},{6,4},{7,5},{8,10},{9,11},{10,... | collective-permute-start | bytes 1843208 | tf_op jit(solution)/shard_map/ppermute | solution.py:848
  214.9 20.5 %collective-permute-start.23 = (bf16[4,40,3840]{2,1,0:T(8,128)(2,1)S(1)}, bf16[4,40,3840]{2,1,0:T(8,128)(2,1)S(1)}, u32[]{:S(2)}, u32[]{:S(2)}) collective-permute-start(bf16[4,40,3840]{2,1,0:T(8,128)(2,1)S(1)} %get-tuple-element.131.refs_0_), channel_id=1, source_target_pairs={{0,1},{1,0},{2,3},{3,2},{4,5},{5,4},{6,7},{7,6},{8,9},{9,8},{10,11... | collective-permute-start | bytes 3686408 | tf_op jit(solution)/shard_map/ppermute | solution.py:848
  214.9 22.9 %collective-permute-start.24 = (bf16[4,40,3840]{2,1,0:T(8,128)(2,1)}, bf16[4,40,3840]{2,1,0:T(8,128)(2,1)S(1)}, u32[]{:S(2)}, u32[]{:S(2)}) collective-permute-start(bf16[4,40,3840]{2,1,0:T(8,128)(2,1)} %collective-permute-done.19.refs_1_), channel_id=1, source_target_pairs={{0,1},{1,0},{2,3},{3,2},{4,5},{5,4},{6,7},{7,6},{8,9},{9,8},{10,11... | collective-permute-start | bytes 3686408 | tf_op jit(solution)/shard_map/ppermute | solution.py:848
  215.4 22.4 %collective-permute-start.25 = (bf16[4,40,3840]{2,1,0:T(8,128)(2,1)S(1)}, bf16[4,40,3840]{2,1,0:T(8,128)(2,1)S(1)}, u32[]{:S(2)}, u32[]{:S(2)}) collective-permute-start(bf16[4,40,3840]{2,1,0:T(8,128)(2,1)S(1)} %collective-permute-done.20.refs_2_), channel_id=1, source_target_pairs={{0,1},{1,0},{2,3},{3,2},{4,5},{5,4},{6,7},{7,6},{8,9},{9,8},{10,11... | collective-permute-start | bytes 3686408 | tf_op jit(solution)/shard_map/ppermute | solution.py:848
  254.7 115.4 %reduce-scatter.5.cloned.1.call-start = ((), (), s32[]{:S(2)}) async-start(), calls=%async_computation.12 | async-start | bytes 3276800 | tf_op jit(solution)/shard_map/reduce_scatter | solution.py:898
  303.4 30.1 %collective-permute-start.32 = (bf16[4,40,3840]{2,1,0:T(8,128)(2,1)}, bf16[4,40,3840]{2,1,0:T(8,128)(2,1)S(1)}, u32[]{:S(2)}, u32[]{:S(2)}) collective-permute-start(bf16[4,40,3840]{2,1,0:T(8,128)(2,1)} %shard_map.180), channel_id=1, source_target_pairs={{0,4},{4,0},{1,5},{5,1},{2,6},{6,2},{3,7},{7,3},{8,12},{12,8},{9,1... | collective-permute-start | bytes 3686408 | tf_op jit(solution)/shard_map/ppermute | solution.py:848
  317.1 52.9 %collective-permute-start.33 = (bf16[4,40,3840]{2,1,0:T(8,128)(2,1)}, bf16[4,40,3840]{2,1,0:T(8,128)(2,1)}, u32[]{:S(2)}, u32[]{:S(2)}) collective-permute-start(bf16[4,40,3840]{2,1,0:T(8,128)(2,1)} %fusion.78), channel_id=1, source_target_pairs={{0,4},{4,0},{1,5},{5,1},{2,6},{6,2},{3,7},{7,3},{8,12},{12,8},{9,1... | collective-permute-start | bytes 3686408 | tf_op jit(solution)/shard_map/ppermute | solution.py:848
  335.6 34.4 %collective-permute-start.34 = (bf16[4,40,3840]{2,1,0:T(8,128)(2,1)S(1)}, bf16[4,40,3840]{2,1,0:T(8,128)(2,1)}, u32[]{:S(2)}, u32[]{:S(2)}) collective-permute-start(bf16[4,40,3840]{2,1,0:T(8,128)(2,1)S(1)} %fusion.69), channel_id=1, source_target_pairs={{0,2},{1,3},{2,0},{3,1},{4,6},{5,7},{6,4},{7,5},{8,10},{9,11},{10,... | collective-permute-start | bytes 3686408 | tf_op jit(solution)/shard_map/ppermute | solution.py:848
  338.0 32.1 %all-to-all-start.5 = ((bf16[4,320,256]{2,1,0:T(8,128)(2,1)}), bf16[4,320,256]{2,1,0:T(8,128)(2,1)S(1)}, u32[]{:S(2)}, u32[]{:S(2)}) async-start(bf16[4,320,256]{2,1,0:T(8,128)(2,1)} %bitcast.251), calls=%async_computation.5 | async-start | bytes 1310720 | tf_op jit(solution)/shard_map/all_to_all | solution.py:869
  341.5 83.8 %reduce-scatter.7.cloned.1.call-start = ((), (), s32[]{:S(2)}) async-start(), calls=%async_computation.13 | async-start | bytes 1536000 | tf_op jit(solution)/shard_map/reduce_scatter | solution.py:898
  370.1 20.8 %collective-permute-start.35 = (bf16[2,2,4,40,3840]{4,3,2,1,0:T(8,128)(2,1)}, bf16[2,2,4,40,3840]{4,3,2,1,0:T(8,128)(2,1)}, u32[]{:S(2)}, u32[]{:S(2)}) collective-permute-start(bf16[2,2,4,40,3840]{4,3,2,1,0:T(8,128)(2,1)} %get-tuple-element.173), channel_id=1, source_target_pairs={{0,1},{1,0},{2,3},{3,2},{4,5},{5,4},{6,7},{7,6},{8,9},{9,8},{10,11... | collective-permute-start | bytes 14745608 | tf_op jit(solution)/shard_map/ppermute | solution.py:848
  394.3 66.5 %reduce-scatter.9.cloned.1.call-start = ((), (), s32[]{:S(2)}) async-start(), calls=%async_computation.14 | async-start | bytes 3276800 | tf_op jit(solution)/shard_map/reduce_scatter | solution.py:898
  406.1 93.9 %reduce-scatter.11.cloned.1.call-start = ((), (), s32[]{:S(2)}) async-start(), calls=%async_computation.15 | async-start | bytes 1536000 | tf_op jit(solution)/shard_map/reduce_scatter | solution.py:898
  430.0 29.5 %collective-permute-start.40 = (bf16[4,40,3840]{2,1,0:T(8,128)(2,1)S(1)}, bf16[4,40,3840]{2,1,0:T(8,128)(2,1)S(1)}, u32[]{:S(2)}, u32[]{:S(2)}) collective-permute-start(bf16[4,40,3840]{2,1,0:T(8,128)(2,1)S(1)} %pad_maximum_fusion), channel_id=1, source_target_pairs={{0,4},{4,0},{1,5},{5,1},{2,6},{6,2},{3,7},{7,3},{8,12},{12,8},{9,1... | collective-permute-start | bytes 3686408 | tf_op jit(solution)/shard_map/ppermute | solution.py:848
  431.5 29.3 %collective-permute-start.41 = (bf16[4,40,3840]{2,1,0:T(8,128)(2,1)S(1)}, bf16[4,40,3840]{2,1,0:T(8,128)(2,1)}, u32[]{:S(2)}, u32[]{:S(2)}) collective-permute-start(bf16[4,40,3840]{2,1,0:T(8,128)(2,1)S(1)} %pad_maximum_fusion.1), channel_id=1, source_target_pairs={{0,2},{1,3},{2,0},{3,1},{4,6},{5,7},{6,4},{7,5},{8,10},{9,11},{10,... | collective-permute-start | bytes 3686408 | tf_op jit(solution)/shard_map/ppermute | solution.py:848
  470.5 18.4 %collective-permute-start.47 = (bf16[160,960]{1,0:T(8,128)(2,1)S(1)}, bf16[160,960]{1,0:T(8,128)(2,1)S(1)}, u32[]{:S(2)}, u32[]{:S(2)}) collective-permute-start(bf16[160,960]{1,0:T(8,128)(2,1)S(1)} %dynamic-slice_bitcast_fusion), channel_id=1, source_target_pairs={{0,4},{4,0},{1,5},{5,1},{2,6},{6,2},{3,7},{7,3},{8,12},{12,8},{9,1... | collective-permute-start | bytes 921608 | tf_op jit(solution)/shard_map/ppermute | solution.py:848
  (109 other events, 791.8 us)
Sparse Core Ops, SparseCore 0:
  27.9 34.1 all-gather.6
  64.3 30.2 all-gather.8
  96.2 51.1 all-gather.10
  300.4 50.7 reduce-scatter.4
  375.2 28.9 reduce-scatter.6
  406.4 51.6 reduce-scatter.8
  469.1 28.5 reduce-scatter.10

commit v20 on v18

--- a/solution.py
+++ b/solution.py
@@ -1069,12 +1069,12 @@
         if layer == 0:
             attended_grad = over_head(heads_grad(out_w, out_bar))
             grads, others = dense_grads(attended_t, normed_two, active, out_bar, up_bar, down_bar)
-            attended_grad, others, z_sum, across, beside = tied(
-                attended_grad, others, z_sum, across, beside
-            )
+            others, diagonal = tied(others, diagonal)
+            others, rows = tied(others, neighbour_rows(cored, *diagonal))
+            sent = sent_beside_and_across(*rows)
+            attended_grad, others, z_sum = tied(attended_grad, others, z_sum)
             others = other_core(others)
-            attended_grad, summed = tied(attended_grad, own_sum(cored, across, beside))
-            summed = over_batch(summed)
+            last = cored
             z_across = across_sum(z_sum)
         else:
             attended_grad = over_head(heads_grad(out_w, out_bar))
@@ -1088,39 +1088,38 @@
             bars, others, z_across = tied(bars, others, z_across)
             moved = over_head(z_across.reshape(4, -1, z_across.shape[-1]))
             qkv_grad = weight_back(bars, normed_all)
-            bars, qkv_grad, moved = tied(bars, qkv_grad, moved)
+            bars, qkv_grad = tied(bars, qkv_grad)
             z_sum = over_batch(qkv_grad.reshape(4, 2, -1, qkv_grad.shape[-1]))
             cored = (grads, others)
             bars, rows = tied(bars, diagonal_rows(cored))
             diagonal = sent_beside_and_across(*rows)
             halves, to_core = rows_back(bars, qkv, token_rows)
-            halves, to_core, diagonal, summed = tied(halves, to_core, diagonal, summed)
+            halves, to_core, diagonal, sent = tied(halves, to_core, diagonal, sent)
+            halves, summed = tied(halves, own_sum(last, *sent))
+            summed = over_batch(summed)
             halves, to_core, rows = tied(halves, to_core, neighbour_rows(cored, *diagonal))
             sent = sent_beside_and_across(*rows)
             halves = halves + other_core(to_core).astype(F32)
             scale_sum = sum_over(jnp.stack(scale_grads), ("head", 1), ("batch", 1), ("batch", 2))
-            halves, sent, z_sum, scale_sum = tied(halves, sent, z_sum, scale_sum)
+            halves, sent, z_sum, scale_sum, moved = tied(halves, sent, z_sum, scale_sum, moved)
             halves, own = tied(halves, own_sum(cored, *sent))
             dense_first = over_batch(own)
             normed_grad = scatter_row(halves)
-            z_across, dense_first = tied(across_sum(z_sum), dense_first)
+            z_across = across_sum(z_sum)
             z_across = over_head(z_across.reshape(4, -1, z_across.shape[-1]))
+            z_across, dense_first = tied(z_across, dense_first)
             dense_grad = [dense_first, summed]
             qkv_grads = [columns_to_rows(z_across), columns_to_rows(moved)]
         else:
             bars, others = tied(bars, others)
             cored = (grads, others)
-            bars, rows = tied(bars, diagonal_rows(cored))
-            diagonal = sent_beside_and_across(*rows)
             halves, to_core, qkv_grad = project_back(bars, qkv, normed_all, token_rows)
             z_sum = over_batch(qkv_grad.reshape(4, 2, -1, qkv_grad.shape[-1]))
-            to_core, halves, diagonal = tied(to_core, halves, diagonal)
-            to_core, rows = tied(to_core, neighbour_rows(cored, *diagonal))
-            across = swapped(rows[0], "blk", 1)
+            to_core, others = tied(to_core, others)
             halves = halves + other_core(to_core).astype(F32)
+            halves, rows = tied(halves, diagonal_rows((grads, others)))
+            diagonal = sent_beside_and_across(*rows)
             normed_grad = scatter_row(halves)
-            normed_grad, beside = tied(normed_grad, rows[1])
-            beside = swapped(beside, "head", 2)
         upper = middle_grad + lower_of(normed_grad, stream, factor_one, gains[layer])
     input_grad = swap_halves(upper.astype(BF16).reshape(tokens.shape)).astype(F32)
     scale_total = sum_over(scale_sum, ("head", 2), ("blk", 1))

time: 517 us -> 536 us (1.037)
  other arithmetic: 46.9 us -> 59.6 us
  local copies, waits for them, and re-layouts: 37.1 us -> 42.5 us
    ppermute x51, waiting for transfers between devices: 131 us -> 103 us  [swapped(): return lax.ppermute(array, axis, [(i, i ^ mask) for i in range(size)])]
    reduce_scatter x4, waiting for transfers between devices: 1.39 us -> 27.7 us  [over_batch(): lax.psum_scatter(parts.astype(BF16), 'batch', scatter_dimension=0, tiled=...]
    unnamed x130 -> x132, local copies, waits for them, and re-layouts: 14.1 us -> 14.1 us
  transfers between devices with their start and end apart: 65 -> 65, of which waited for: 31 -> 26; matrix products, arithmetic and copies ran while one was open for 13% -> 17% of each run, Pallas kernels for 23% -> 20%
where the time goes in v20:
time: 536 us; the launch traced here: 528 us
  waiting for transfers between devices  183 us (34%)
  Pallas kernels  122 us (23%)
  starting transfers between devices  66.1 us (12%)
  other arithmetic  59.6 us (11%)
  local copies, waits for them, and re-layouts  42.5 us (8%)
  matrix products  19.5 us (4%)
  blocking collectives  19.4 us (4%)
  between operations  15.9 us (3%)
    ppermute x51, waiting for transfers between devices, swapped(): return lax.ppermute(array, axis, [(i, i ^ mask) for i in range(size)])  103 us
    ppermute x51, starting transfers between devices, swapped(): return lax.ppermute(array, axis, [(i, i ^ mask) for i in range(size)])  39.1 us
    all_to_all x7, waiting for transfers between devices, over_head(): lax.all_to_all(parts, 'head', split_axis=0, concat_axis=0, tiled=True)  29 us
    reduce_scatter x4, waiting for transfers between devices, over_batch(): lax.psum_scatter(parts.astype(BF16), 'batch', scatter_dimension=0, tiled=...  27.7 us
    all_to_all x7, starting transfers between devices, over_head(): lax.all_to_all(parts, 'head', split_axis=0, concat_axis=0, tiled=True)  26.1 us
    pallas_call x2, Pallas kernels, attend_back_rows(): pl.pallas_call(functools.partial(attend_back_kernel, token_rows), grid=(l...  24.6 us
    all_gather x3, waiting for transfers between devices, along_batch(): return lax.all_gather(piece, 'batch', axis=0, tiled=False)  23.7 us
    all_to_all x1, blocking collectives, over_head(): lax.all_to_all(parts, 'head', split_axis=0, concat_axis=0, tiled=True)  19.4 us
  transfers between devices with their start and end apart: 65, of which 26 were waited for; matrix products, arithmetic and copies ran while one was open for 17% of the time, Pallas kernels for 20%

profile of v20, /device:TPU:0, one launch (start us, length us, event | category | flops | bytes accessed | tf_op | source)
XLA Modules:
  0.0 528.0 jit_solution(871371779803633989)
XLA Ops:
  17.9 8.1 %collective-permute-done = bf16[128,1280]{1,0:T(8,128)(2,1)S(1)} collective-permute-done((bf16[128,1280]{1,0:T(8,128)(2,1)S(1)}, bf16[128,1280]{1,0:T(8,128)(2,1)S(1)}, u32[]{:S(2)}, u32[]{:S(2)}) %collective-permute-start) | collective-permute-done | bytes 327712 | tf_op jit(solution)/shard_map/ppermute | solution.py:848
  30.6 12.4 %collective-permute-done.2.refs_2_ = bf16[256,1280]{1,0:T(8,128)(2,1)S(1)} collective-permute-done((bf16[256,1280]{1,0:T(8,128)(2,1)S(1)}, bf16[256,1280]{1,0:T(8,128)(2,1)S(1)}, u32[]{:S(2)}, u32[]{:S(2)}) %collective-permute-start.2) | collective-permute-done | bytes 655392 | tf_op jit(solution)/shard_map/ppermute | solution.py:848
  46.1 15.2 %all-gather.7.cloned.1.call-done = bf16[640,964]{1,0:T(8,128)(2,1)} async-done(((bf16[160,964]{1,0:T(8,128)(2,1)}), bf16[640,964]{1,0:T(8,128)(2,1)}) %all-gather.7.cloned.1.call-update) | async-done | bytes 1233936 | tf_op jit(solution)/shard_map/all_gather | solution.py:882
  68.1 6.6 %all-to-all-done.1 = bf16[4,40,960]{2,1,0:T(8,128)(2,1)S(1)} async-done(((bf16[4,40,960]{2,1,0:T(8,128)(2,1)}), bf16[4,40,960]{2,1,0:T(8,128)(2,1)S(1)}, u32[]{:S(2)}, u32[]{:S(2)}) %all-to-all-start.1) | async-done | bytes 307232 | tf_op jit(solution)/shard_map/all_to_all | solution.py:869
  74.9 16.5 %collective-permute-done.5.across_ref = bf16[4,160,964]{2,1,0:T(8,128)(2,1)S(1)} collective-permute-done((bf16[4,160,964]{2,1,0:T(8,128)(2,1)}, bf16[4,160,964]{2,1,0:T(8,128)(2,1)S(1)}, u32[]{:S(2)}, u32[]{:S(2)}) %collective-permute-start.5) | collective-permute-done | bytes 1233952 | tf_op jit(solution)/shard_map/ppermute | solution.py:848
  98.2 4.6 shard_map.169
  104.1 8.8 %shard_map.170 = (bf16[1024,1280]{1,0:T(8,128)(2,1)}, f32[960,1024]{1,0:T(8,128)}) custom-call(s32[3]{0:T(128)S(1)} %pad_add_fusion.place_ref.core_ref, bf16[256,1280]{1,0:T(8,128)(2,1)} %bitcast.233, bf16[256,1280]{1,0:T(8,128)(2,1)} %copy-done.52, bf16[256,1280]{1,0:T(8,128)(2,1)} %copy-done.51, bf16[256,1280]{1,0:T(8,128)(2,1)} %collective-permute-done.3.refs_3_, ...), custom_call_target="tpu_custom_call" | custom-call | flops 1048576 | bytes 1048576 | tf_op jit(solution)/shard_map/pallas_call | solution.py:711
  115.1 9.6 %shard_map.171 = (bf16[4,4,80,256]{3,2,1,0:T(8,128)(2,1)}, f32[4,1,1024]{2,1,0:T(1,128)S(1)}) custom-call(f32[3,4,80,1024]{3,2,1,0:T(8,128)S(1)} %bitcast.206, f32[80,1]{1,0:T(8,128)S(1)} %copy.60.scale_ref, s32[1024,1]{1,0:T(8,128)S(1)} %copy.61.col_ref, s32[1,1024]{1,0:T(1,128)S(1)} %constant_dynamic-slice_fusion.row_ref), custom_call_target="tpu_custom_call" | custom-call | flops 1048576 | bytes 1048576 | tf_op jit(solution)/shard_map/pallas_call | solution.py:413
  134.4 5.9 %collective-permute-done.9.refs_4_ = bf16[4,40,1920]{2,1,0:T(8,128)(2,1)} collective-permute-done((bf16[4,40,1920]{2,1,0:T(8,128)(2,1)}, bf16[4,40,1920]{2,1,0:T(8,128)(2,1)}, u32[]{:S(2)}, u32[]{:S(2)}) %collective-permute-start.9) | collective-permute-done | bytes 614432 | tf_op jit(solution)/shard_map/ppermute | solution.py:848
  140.3 6.2 %all-gather.11.cloned.1.call-done = bf16[8,40,3840]{2,1,0:T(8,128)(2,1)} async-done(((bf16[2,40,3840]{2,1,0:T(8,128)(2,1)}), bf16[8,40,3840]{2,1,0:T(8,128)(2,1)}) %all-gather.11.cloned.1.call-update) | async-done | bytes 2457616 | tf_op jit(solution)/shard_map/all_gather | solution.py:882
  153.7 4.5 shard_map.172
  166.1 15.8 %collective-permute-done.16.across_ref = bf16[4,40,3840]{2,1,0:T(8,128)(2,1)S(1)} collective-permute-done((bf16[4,40,3840]{2,1,0:T(8,128)(2,1)S(1)}, bf16[4,40,3840]{2,1,0:T(8,128)(2,1)S(1)}, u32[]{:S(2)}, u32[]{:S(2)}) %collective-permute-start.16) | collective-permute-done | bytes 1228832 | tf_op jit(solution)/shard_map/ppermute | solution.py:848
  184.5 4.7 shard_map.173
  189.2 7.8 %shard_map.174 = (bf16[1024,1280]{1,0:T(8,128)(2,1)}, f32[960,1024]{1,0:T(8,128)}) custom-call(s32[3]{0:T(128)S(1)} %pad_add_fusion.place_ref.core_ref, bf16[256,1280]{1,0:T(8,128)(2,1)} %multiply_convert_fusion.2.refs_0_, bf16[256,1280]{1,0:T(8,128)(2,1)} %collective-permute-done.17.refs_1_, bf16[256,1280]{1,0:T(8,128)(2,1)} %collective-permute-done.15.refs_2_, ...), custom_call_target="tpu_custom_call" | custom-call | flops 1048576 | bytes 1048576 | tf_op jit(solution)/shard_map/pallas_call | solution.py:711
  199.1 8.9 %shard_map.175 = (bf16[4,4,80,256]{3,2,1,0:T(8,128)(2,1)S(1)}, f32[4,1,1024]{2,1,0:T(1,128)S(1)}) custom-call(f32[3,4,80,1024]{3,2,1,0:T(8,128)S(1)} %bitcast.208, f32[80,1]{1,0:T(8,128)S(1)} %copy.64.scale_ref, s32[1024,1]{1,0:T(8,128)S(1)} %copy.61.col_ref, s32[1,1024]{1,0:T(1,128)S(1)} %constant_dynamic-slice_fusion.row_ref), custom_call_target="tpu_custom_call" | custom-call | flops 1048576 | bytes 1048576 | tf_op jit(solution)/shard_map/pallas_call | solution.py:413
  215.5 19.4 %all_to_all.40 = bf16[4,320,256]{2,1,0:T(8,128)(2,1)S(1)} all-to-all(bf16[4,320,256]{2,1,0:T(8,128)(2,1)S(1)} %bitcast.223), channel_id=1, replica_groups=mesh['batch'=4,'blk'=2,'head'=4] {'head'}, dimensions={0} | all-to-all | bytes 1310720 | tf_op jit(solution)/shard_map/all_to_all | solution.py:869
  255.8 8.5 %shard_map.177 = (bf16[2,2,4,40,3840]{4,3,2,1,0:T(8,128)(2,1)}, bf16[2,2,4,40,3840]{4,3,2,1,0:T(8,128)(2,1)}) custom-call(s32[3]{0:T(128)S(1)} %pad_add_fusion.place_ref.core_ref, bf16[1280,256]{1,0:T(8,128)(2,1)} %bitcast.245, bf16[256,1280]{1,0:T(8,128)(2,1)} %copy-done.25, bf16[256,1280]{1,0:T(8,128)(2,1)} %copy-done.49, bf16[256,1280]{1,0:T(8,128)(2,1)} %copy-done.26, ...), custom_call_target="tpu_custom_call" | custom-call | flops 1048576 | bytes 1048576 | tf_op jit(solution)/shard_map/pallas_call | solution.py:577
  266.7 12.3 %shard_map.178 = (bf16[3,4,80,1024]{3,2,1,0:T(8,128)(2,1)}, f32[80,128]{1,0:T(8,128)}) custom-call(f32[3,4,80,1024]{3,2,1,0:T(8,128)} %bitcast.207, bf16[4,4,80,256]{3,2,1,0:T(8,128)(2,1)} %bitcast.56.grad_ref, f32[4,1,1024]{2,1,0:T(1,128)S(1)} %get-tuple-element.146.lse_ref, f32[80,1]{1,0:T(8,128)S(1)} %copy.64.scale_ref, s32[1024,1]{1,0:T(8,128)S(1)} %copy.61.col_ref, ...), custom_call_target="tpu_custom_call" | custom-call | flops 1048576 | bytes 1048576 | tf_op jit(solution)/shard_map/pallas_call | solution.py:506
  279.0 12.5 %shard_map.179 = (f32[2,2,128,1280]{3,2,1,0:T(8,128)}, bf16[2,2,128,1280]{3,2,1,0:T(8,128)(2,1)}, bf16[1280,960]{1,0:T(8,128)(2,1)}) custom-call(s32[3]{0:T(128)S(1)} %pad_add_fusion.place_ref.core_ref, bf16[960,1024]{1,0:T(8,128)(2,1)} %bitcast.247, bf16[1280,960]{1,0:T(8,128)(2,1)} %bitcast.225, bf16[1024,1280]{1,0:T(8,128)(2,1)} %get-tuple-element.150.normed_ref), custom_call_target="tpu_custom_call" | custom-call | flops 1048576 | bytes 1048576 | tf_op jit(solution)/shard_map/pallas_call | solution.py:757
  291.6 6.2 %add_bitcast_fusion.2 = (f32[4,40,3840]{2,1,0:T(8,128)}, f32[4,40,3840]{2,1,0:T(8,128)}, bf16[4,40,3840]{2,1,0:T(8,128)(2,1)S(1)}) fusion(bf16[2,2,4,40,3840]{4,3,2,1,0:T(8,128)(2,1)} %copy-done.19, s32[]{:T(128)S(6)} %select_n.174, s32[]{:T(128)S(6)} %select_n.171, bf16[2,2,4,40,3840]{4,3,2,1,0:T(8,128)(2,1)} %get-tuple-element.155, s32[]{:T(128)S(6)} %select_n.169, ...), kind=kLoop, calls=%fused_computation.48 | loop fusion | flops 6144000 | bytes 13516816 | tf_op jit(solution)/shard_map/add | solution.py:914
  310.9 9.9 %collective-permute-done.31 = bf16[2,128,1280]{2,1,0:T(8,128)(2,1)} collective-permute-done((bf16[2,128,1280]{2,1,0:T(8,128)(2,1)}, bf16[2,128,1280]{2,1,0:T(8,128)(2,1)}, u32[]{:S(2)}, u32[]{:S(2)}) %collective-permute-start.31) | collective-permute-done | bytes 655392 | tf_op jit(solution)/shard_map/ppermute | solution.py:848
  338.5 8.9 %shard_map.180 = (bf16[2,2,4,40,3840]{4,3,2,1,0:T(8,128)(2,1)}, bf16[2,2,4,40,3840]{4,3,2,1,0:T(8,128)(2,1)}) custom-call(s32[3]{0:T(128)S(1)} %pad_add_fusion.place_ref.core_ref, bf16[1280,256]{1,0:T(8,128)(2,1)} %bitcast.242, bf16[256,1280]{1,0:T(8,128)(2,1)} %copy-done.24, bf16[256,1280]{1,0:T(8,128)(2,1)} %copy-done.45, bf16[256,1280]{1,0:T(8,128)(2,1)} %copy-done.30, ...), custom_call_target="tpu_custom_call" | custom-call | flops 1048576 | bytes 1048576 | tf_op jit(solution)/shard_map/pallas_call | solution.py:577
  360.5 12.3 %shard_map.181 = (bf16[3,4,80,1024]{3,2,1,0:T(8,128)(2,1)}, f32[80,128]{1,0:T(8,128)}) custom-call(f32[3,4,80,1024]{3,2,1,0:T(8,128)} %bitcast.205, bf16[4,4,80,256]{3,2,1,0:T(8,128)(2,1)} %bitcast.67.grad_ref, f32[4,1,1024]{2,1,0:T(1,128)S(1)} %get-tuple-element.167.lse_ref, f32[80,1]{1,0:T(8,128)S(1)} %copy.60.scale_ref, s32[1024,1]{1,0:T(8,128)S(1)} %copy.61.col_ref, ...), custom_call_target="tpu_custom_call" | custom-call | flops 1048576 | bytes 1048576 | tf_op jit(solution)/shard_map/pallas_call | solution.py:506
  373.6 6.3 %add_bitcast_fusion = (f32[4,40,3840]{2,1,0:T(8,128)}, f32[4,40,3840]{2,1,0:T(8,128)S(1)}, bf16[4,40,3840]{2,1,0:T(8,128)(2,1)S(1)}) fusion(bf16[2,2,4,40,3840]{4,3,2,1,0:T(8,128)(2,1)S(1)} %collective-permute-done.34, s32[]{:T(128)S(6)} %select_n.174, s32[]{:T(128)S(6)} %select_n.171, bf16[2,2,4,40,3840]{4,3,2,1,0:T(8,128)(2,1)} %get-tuple-element.174, ...), kind=kLoop, calls=%fused_computation.45 | loop fusion | flops 6144000 | bytes 13516816 | tf_op jit(solution)/shard_map/add | solution.py:914
  380.0 7.3 %shard_map.182 = bf16[1280,960]{1,0:T(8,128)(2,1)} custom-call(bf16[960,1024]{1,0:T(8,128)(2,1)} %bitcast.237, bf16[1024,1280]{1,0:T(8,128)(2,1)} %get-tuple-element.172.normed_ref), custom_call_target="tpu_custom_call" | custom-call | flops 1048576 | bytes 1048576 | tf_op jit(solution)/shard_map/pallas_call | solution.py:828
  392.8 8.2 %shard_map.183 = (f32[2,2,128,1280]{3,2,1,0:T(8,128)}, bf16[2,2,128,1280]{3,2,1,0:T(8,128)(2,1)}) custom-call(s32[3]{0:T(128)S(1)} %pad_add_fusion.place_ref.core_ref, bf16[960,1024]{1,0:T(8,128)(2,1)} %bitcast.238, bf16[1280,960]{1,0:T(8,128)(2,1)} %bitcast.230), custom_call_target="tpu_custom_call" | custom-call | flops 1048576 | bytes 1048576 | tf_op jit(solution)/shard_map/pallas_call | solution.py:798
  401.0 5.7 %collective-permute-done.36 = bf16[4,40,1920]{2,1,0:T(8,128)(2,1)} collective-permute-done((bf16[4,40,1920]{2,1,0:T(8,128)(2,1)}, bf16[4,40,1920]{2,1,0:T(8,128)(2,1)}, u32[]{:S(2)}, u32[]{:S(2)}) %collective-permute-start.36) | collective-permute-done | bytes 614432 | tf_op jit(solution)/shard_map/ppermute | solution.py:848
  421.6 4.6 collective-permute-done.44
  436.8 14.3 %all-to-all-done.6 = bf16[4,40,960]{2,1,0:T(8,128)(2,1)S(1)} async-done(((bf16[4,40,960]{2,1,0:T(8,128)(2,1)}), bf16[4,40,960]{2,1,0:T(8,128)(2,1)S(1)}, u32[]{:S(2)}, u32[]{:S(2)}) %all-to-all-start.6) | async-done | bytes 307232 | tf_op jit(solution)/shard_map/all_to_all | solution.py:869
  461.6 11.2 %collective-permute-done.49 = f32[2,80]{1,0:T(2,128)S(1)} collective-permute-done((f32[2,80]{1,0:T(2,128)S(1)}, f32[2,80]{1,0:T(2,128)S(1)}, u32[]{:S(2)}, u32[]{:S(2)}) %collective-permute-start.49) | collective-permute-done | bytes 672 | tf_op jit(solution)/shard_map/ppermute | solution.py:848
  485.6 5.0 all-to-all-done.7
  491.4 24.7 %reduce-scatter.11.cloned.1.call-done = bf16[1,40,3840]{2,1,0:T(8,128)(2,1)} async-done(((bf16[4,40,3840]{2,1,0:T(8,128)(2,1)}), bf16[1,40,3840]{2,1,0:T(8,128)(2,1)}) %reduce-scatter.11.cloned.1.call-update) | async-done | bytes 307216 | tf_op jit(solution)/shard_map/reduce_scatter | solution.py:898
  (376 shorter events, 198.8 us)
Async XLA Ops:
  8.3 34.7 %collective-permute-start.4 = (bf16[128,1280]{1,0:T(8,128)(2,1)S(1)}, bf16[128,1280]{1,0:T(8,128)(2,1)}, u32[]{:S(2)}, u32[]{:S(2)}) collective-permute-start(bf16[128,1280]{1,0:T(8,128)(2,1)S(1)} %dynamic-slice_bitcast_fusion.4), channel_id=1, source_target_pairs={{0,4},{4,0},{1,5},{5,1},{2,6},{6,2},{3,7},{7,3},{8,12},{12,8},{9,1... | collective-permute-start | bytes 983048 | tf_op jit(solution)/shard_map/ppermute | solution.py:848
  17.8 43.5 %all-gather.7.cloned.1.call-start = ((), (), s32[]{:S(2)}) async-start(), calls=%async_computation.16 | async-start | bytes 1638400 | tf_op jit(solution)/shard_map/all_gather | solution.py:882
  26.9 66.8 %all-gather.9.cloned.1.call-start = ((), (), s32[]{:S(2)}) async-start(), calls=%async_computation.17 | async-start | bytes 1536000 | tf_op jit(solution)/shard_map/all_gather | solution.py:882
  61.3 30.1 %collective-permute-start.5 = (bf16[4,160,964]{2,1,0:T(8,128)(2,1)}, bf16[4,160,964]{2,1,0:T(8,128)(2,1)S(1)}, u32[]{:S(2)}, u32[]{:S(2)}) collective-permute-start(bf16[4,160,964]{2,1,0:T(8,128)(2,1)} %bitcast.253), channel_id=1, source_target_pairs={{0,4},{4,0},{1,5},{5,1},{2,6},{6,2},{3,7},{7,3},{8,12},{12,8},{9,1... | collective-permute-start | bytes 3701768 | tf_op jit(solution)/shard_map/ppermute | solution.py:848
  68.0 78.5 %all-gather.11.cloned.1.call-start = ((), (), s32[]{:S(2)}) async-start(), calls=%async_computation.18 | async-start | bytes 3072000 | tf_op jit(solution)/shard_map/all_gather | solution.py:882
  94.7 30.0 %collective-permute-start.7 = (bf16[4,40,3840]{2,1,0:T(8,128)(2,1)}, bf16[4,40,3840]{2,1,0:T(8,128)(2,1)S(1)}, u32[]{:S(2)}, u32[]{:S(2)}) collective-permute-start(bf16[4,40,3840]{2,1,0:T(8,128)(2,1)} %bitcast.19.refs_0_), channel_id=1, source_target_pairs={{0,2},{1,3},{2,0},{3,1},{4,6},{5,7},{6,4},{7,5},{8,10},{9,11},{10,... | collective-permute-start | bytes 3686408 | tf_op jit(solution)/shard_map/ppermute | solution.py:848
  96.2 28.5 %collective-permute-start.6 = (bf16[4,40,3840]{2,1,0:T(8,128)(2,1)}, bf16[4,40,3840]{2,1,0:T(8,128)(2,1)}, u32[]{:S(2)}, u32[]{:S(2)}) collective-permute-start(bf16[4,40,3840]{2,1,0:T(8,128)(2,1)} %bitcast.19.refs_0_), channel_id=1, source_target_pairs={{0,4},{4,0},{1,5},{5,1},{2,6},{6,2},{3,7},{7,3},{8,12},{12,8},{9,1... | collective-permute-start | bytes 3686408 | tf_op jit(solution)/shard_map/ppermute | solution.py:848
  128.7 20.9 %collective-permute-start.8 = (bf16[4,40,1920]{2,1,0:T(8,128)(2,1)}, bf16[4,40,1920]{2,1,0:T(8,128)(2,1)}, u32[]{:S(2)}, u32[]{:S(2)}) collective-permute-start(bf16[4,40,1920]{2,1,0:T(8,128)(2,1)} %slice.153), channel_id=1, source_target_pairs={{0,2},{1,3},{2,0},{3,1},{4,6},{5,7},{6,4},{7,5},{8,10},{9,11},{10,... | collective-permute-start | bytes 1843208 | tf_op jit(solution)/shard_map/ppermute | solution.py:848
  129.3 20.3 %all-to-all-start.2 = ((bf16[4,320,256]{2,1,0:T(8,128)(2,1)}), bf16[4,320,256]{2,1,0:T(8,128)(2,1)S(1)}, u32[]{:S(2)}, u32[]{:S(2)}) async-start(bf16[4,320,256]{2,1,0:T(8,128)(2,1)} %bitcast.31), calls=%async_computation.2 | async-start | bytes 1310720 | tf_op jit(solution)/shard_map/all_to_all | solution.py:869
  133.3 19.0 %collective-permute-start.10 = (bf16[4,40,3840]{2,1,0:T(8,128)(2,1)}, bf16[4,40,3840]{2,1,0:T(8,128)(2,1)}, u32[]{:S(2)}, u32[]{:S(2)}) collective-permute-start(bf16[4,40,3840]{2,1,0:T(8,128)(2,1)} %bitcast.19.refs_0_), channel_id=1, source_target_pairs={{0,1},{1,0},{2,3},{3,2},{4,5},{5,4},{6,7},{7,6},{8,9},{9,8},{10,11... | collective-permute-start | bytes 3686408 | tf_op jit(solution)/shard_map/ppermute | solution.py:848
  133.9 19.8 %collective-permute-start.11 = (bf16[4,40,3840]{2,1,0:T(8,128)(2,1)}, bf16[4,40,3840]{2,1,0:T(8,128)(2,1)}, u32[]{:S(2)}, u32[]{:S(2)}) collective-permute-start(bf16[4,40,3840]{2,1,0:T(8,128)(2,1)} %collective-permute-done.6.refs_1_), channel_id=1, source_target_pairs={{0,1},{1,0},{2,3},{3,2},{4,5},{5,4},{6,7},{7,6},{8,9},{9,8},{10,11... | collective-permute-start | bytes 3686408 | tf_op jit(solution)/shard_map/ppermute | solution.py:848
  133.9 19.8 %collective-permute-start.12 = (bf16[4,40,3840]{2,1,0:T(8,128)(2,1)S(1)}, bf16[4,40,3840]{2,1,0:T(8,128)(2,1)}, u32[]{:S(2)}, u32[]{:S(2)}) collective-permute-start(bf16[4,40,3840]{2,1,0:T(8,128)(2,1)S(1)} %collective-permute-done.7.refs_2_), channel_id=1, source_target_pairs={{0,1},{1,0},{2,3},{3,2},{4,5},{5,4},{6,7},{7,6},{8,9},{9,8},{10,11... | collective-permute-start | bytes 3686408 | tf_op jit(solution)/shard_map/ppermute | solution.py:848
  152.3 29.5 %collective-permute-start.16 = (bf16[4,40,3840]{2,1,0:T(8,128)(2,1)S(1)}, bf16[4,40,3840]{2,1,0:T(8,128)(2,1)S(1)}, u32[]{:S(2)}, u32[]{:S(2)}) collective-permute-start(bf16[4,40,3840]{2,1,0:T(8,128)(2,1)S(1)} %get-tuple-element.230.along_ref), channel_id=1, source_target_pairs={{0,4},{4,0},{1,5},{5,1},{2,6},{6,2},{3,7},{7,3},{8,12},{12,8},{9,1... | collective-permute-start | bytes 3686408 | tf_op jit(solution)/shard_map/ppermute | solution.py:848
  182.5 28.3 %collective-permute-start.20 = (bf16[4,40,3840]{2,1,0:T(8,128)(2,1)S(1)}, bf16[4,40,3840]{2,1,0:T(8,128)(2,1)S(1)}, u32[]{:S(2)}, u32[]{:S(2)}) collective-permute-start(bf16[4,40,3840]{2,1,0:T(8,128)(2,1)S(1)} %get-tuple-element.131.refs_0_), channel_id=1, source_target_pairs={{0,2},{1,3},{2,0},{3,1},{4,6},{5,7},{6,4},{7,5},{8,10},{9,11},{10,... | collective-permute-start | bytes 3686408 | tf_op jit(solution)/shard_map/ppermute | solution.py:848
  183.2 28.2 %collective-permute-start.19 = (bf16[4,40,3840]{2,1,0:T(8,128)(2,1)S(1)}, bf16[4,40,3840]{2,1,0:T(8,128)(2,1)}, u32[]{:S(2)}, u32[]{:S(2)}) collective-permute-start(bf16[4,40,3840]{2,1,0:T(8,128)(2,1)S(1)} %get-tuple-element.131.refs_0_), channel_id=1, source_target_pairs={{0,4},{4,0},{1,5},{5,1},{2,6},{6,2},{3,7},{7,3},{8,12},{12,8},{9,1... | collective-permute-start | bytes 3686408 | tf_op jit(solution)/shard_map/ppermute | solution.py:848
  212.6 22.3 %collective-permute-start.22 = (bf16[4,40,1920]{2,1,0:T(8,128)(2,1)S(1)}, bf16[4,40,1920]{2,1,0:T(8,128)(2,1)S(1)}, u32[]{:S(2)}, u32[]{:S(2)}) collective-permute-start(bf16[4,40,1920]{2,1,0:T(8,128)(2,1)S(1)} %slice.167), channel_id=1, source_target_pairs={{0,4},{4,0},{1,5},{5,1},{2,6},{6,2},{3,7},{7,3},{8,12},{12,8},{9,1... | collective-permute-start | bytes 1843208 | tf_op jit(solution)/shard_map/ppermute | solution.py:848
  213.7 21.2 %collective-permute-start.21 = (bf16[4,40,1920]{2,1,0:T(8,128)(2,1)S(1)}, bf16[4,40,1920]{2,1,0:T(8,128)(2,1)S(1)}, u32[]{:S(2)}, u32[]{:S(2)}) collective-permute-start(bf16[4,40,1920]{2,1,0:T(8,128)(2,1)S(1)} %slice.166), channel_id=1, source_target_pairs={{0,2},{1,3},{2,0},{3,1},{4,6},{5,7},{6,4},{7,5},{8,10},{9,11},{10,... | collective-permute-start | bytes 1843208 | tf_op jit(solution)/shard_map/ppermute | solution.py:848
  215.0 20.5 %collective-permute-start.23 = (bf16[4,40,3840]{2,1,0:T(8,128)(2,1)S(1)}, bf16[4,40,3840]{2,1,0:T(8,128)(2,1)S(1)}, u32[]{:S(2)}, u32[]{:S(2)}) collective-permute-start(bf16[4,40,3840]{2,1,0:T(8,128)(2,1)S(1)} %get-tuple-element.131.refs_0_), channel_id=1, source_target_pairs={{0,1},{1,0},{2,3},{3,2},{4,5},{5,4},{6,7},{7,6},{8,9},{9,8},{10,11... | collective-permute-start | bytes 3686408 | tf_op jit(solution)/shard_map/ppermute | solution.py:848
  215.0 22.9 %collective-permute-start.24 = (bf16[4,40,3840]{2,1,0:T(8,128)(2,1)}, bf16[4,40,3840]{2,1,0:T(8,128)(2,1)S(1)}, u32[]{:S(2)}, u32[]{:S(2)}) collective-permute-start(bf16[4,40,3840]{2,1,0:T(8,128)(2,1)} %collective-permute-done.19.refs_1_), channel_id=1, source_target_pairs={{0,1},{1,0},{2,3},{3,2},{4,5},{5,4},{6,7},{7,6},{8,9},{9,8},{10,11... | collective-permute-start | bytes 3686408 | tf_op jit(solution)/shard_map/ppermute | solution.py:848
  215.5 22.4 %collective-permute-start.25 = (bf16[4,40,3840]{2,1,0:T(8,128)(2,1)S(1)}, bf16[4,40,3840]{2,1,0:T(8,128)(2,1)S(1)}, u32[]{:S(2)}, u32[]{:S(2)}) collective-permute-start(bf16[4,40,3840]{2,1,0:T(8,128)(2,1)S(1)} %collective-permute-done.20.refs_2_), channel_id=1, source_target_pairs={{0,1},{1,0},{2,3},{3,2},{4,5},{5,4},{6,7},{7,6},{8,9},{9,8},{10,11... | collective-permute-start | bytes 3686408 | tf_op jit(solution)/shard_map/ppermute | solution.py:848
  255.6 100.3 %reduce-scatter.5.cloned.1.call-start = ((), (), s32[]{:S(2)}) async-start(), calls=%async_computation.12 | async-start | bytes 3276800 | tf_op jit(solution)/shard_map/reduce_scatter | solution.py:898
  309.3 38.0 %collective-permute-start.32 = (bf16[4,40,1920]{2,1,0:T(8,128)(2,1)}, bf16[4,40,1920]{2,1,0:T(8,128)(2,1)}, u32[]{:S(2)}, u32[]{:S(2)}) collective-permute-start(bf16[4,40,1920]{2,1,0:T(8,128)(2,1)} %get-tuple-element.159), channel_id=1, source_target_pairs={{0,4},{4,0},{1,5},{5,1},{2,6},{6,2},{3,7},{7,3},{8,12},{12,8},{9,1... | collective-permute-start | bytes 1843208 | tf_op jit(solution)/shard_map/ppermute | solution.py:848
  310.8 36.5 %collective-permute-start.33 = (bf16[4,40,1920]{2,1,0:T(8,128)(2,1)}, bf16[4,40,1920]{2,1,0:T(8,128)(2,1)}, u32[]{:S(2)}, u32[]{:S(2)}) collective-permute-start(bf16[4,40,1920]{2,1,0:T(8,128)(2,1)} %get-tuple-element.160), channel_id=1, source_target_pairs={{0,2},{1,3},{2,0},{3,1},{4,6},{5,7},{6,4},{7,5},{8,10},{9,11},{10,... | collective-permute-start | bytes 1843208 | tf_op jit(solution)/shard_map/ppermute | solution.py:848
  334.2 18.7 %all-to-all-start.5 = ((bf16[4,320,256]{2,1,0:T(8,128)(2,1)}), bf16[4,320,256]{2,1,0:T(8,128)(2,1)}, u32[]{:S(2)}, u32[]{:S(2)}) async-start(bf16[4,320,256]{2,1,0:T(8,128)(2,1)} %bitcast.62), calls=%async_computation.5 | async-start | bytes 1310720 | tf_op jit(solution)/shard_map/all_to_all | solution.py:869
  338.4 112.7 %reduce-scatter.7.cloned.1.call-start = ((), (), s32[]{:S(2)}) async-start(), calls=%async_computation.13 | async-start | bytes 3276800 | tf_op jit(solution)/shard_map/reduce_scatter | solution.py:898
  358.4 42.5 %collective-permute-start.38 = (bf16[4,40,3840]{2,1,0:T(8,128)(2,1)}, bf16[4,40,3840]{2,1,0:T(8,128)(2,1)}, u32[]{:S(2)}, u32[]{:S(2)}) collective-permute-start(bf16[4,40,3840]{2,1,0:T(8,128)(2,1)} %pad_maximum_fusion), channel_id=1, source_target_pairs={{0,4},{4,0},{1,5},{5,1},{2,6},{6,2},{3,7},{7,3},{8,12},{12,8},{9,1... | collective-permute-start | bytes 3686408 | tf_op jit(solution)/shard_map/ppermute | solution.py:848
  359.0 42.0 %collective-permute-start.39 = (bf16[4,40,3840]{2,1,0:T(8,128)(2,1)}, bf16[4,40,3840]{2,1,0:T(8,128)(2,1)}, u32[]{:S(2)}, u32[]{:S(2)}) collective-permute-start(bf16[4,40,3840]{2,1,0:T(8,128)(2,1)} %pad_maximum_fusion.1), channel_id=1, source_target_pairs={{0,2},{1,3},{2,0},{3,1},{4,6},{5,7},{6,4},{7,5},{8,10},{9,11},{10,... | collective-permute-start | bytes 3686408 | tf_op jit(solution)/shard_map/ppermute | solution.py:848
  416.7 34.4 %collective-permute-start.41 = (bf16[4,40,3840]{2,1,0:T(8,128)(2,1)}, bf16[4,40,3840]{2,1,0:T(8,128)(2,1)}, u32[]{:S(2)}, u32[]{:S(2)}) collective-permute-start(bf16[4,40,3840]{2,1,0:T(8,128)(2,1)} %pad_maximum_fusion.2), channel_id=1, source_target_pairs={{0,4},{4,0},{1,5},{5,1},{2,6},{6,2},{3,7},{7,3},{8,12},{12,8},{9,1... | collective-permute-start | bytes 3686408 | tf_op jit(solution)/shard_map/ppermute | solution.py:848
  418.2 32.9 %collective-permute-start.42 = (bf16[4,40,3840]{2,1,0:T(8,128)(2,1)}, bf16[4,40,3840]{2,1,0:T(8,128)(2,1)}, u32[]{:S(2)}, u32[]{:S(2)}) collective-permute-start(bf16[4,40,3840]{2,1,0:T(8,128)(2,1)} %pad_maximum_fusion.3), channel_id=1, source_target_pairs={{0,2},{1,3},{2,0},{3,1},{4,6},{5,7},{6,4},{7,5},{8,10},{9,11},{10,... | collective-permute-start | bytes 3686408 | tf_op jit(solution)/shard_map/ppermute | solution.py:848
  430.9 20.2 %all-to-all-start.6 = ((bf16[4,40,960]{2,1,0:T(8,128)(2,1)}), bf16[4,40,960]{2,1,0:T(8,128)(2,1)S(1)}, u32[]{:S(2)}, u32[]{:S(2)}) async-start(bf16[4,40,960]{2,1,0:T(8,128)(2,1)} %bitcast.77), calls=%async_computation.8 | async-start | bytes 655360 | tf_op jit(solution)/shard_map/all_to_all | solution.py:869
  434.4 56.2 %reduce-scatter.9.cloned.1.call-start = ((), (), s32[]{:S(2)}) async-start(), calls=%async_computation.14 | async-start | bytes 1536000 | tf_op jit(solution)/shard_map/reduce_scatter | solution.py:898
  455.2 60.9 %reduce-scatter.11.cloned.1.call-start = ((), (), s32[]{:S(2)}) async-start(), calls=%async_computation.15 | async-start | bytes 1536000 | tf_op jit(solution)/shard_map/reduce_scatter | solution.py:898
  (99 other events, 821.1 us)
Sparse Core Ops, SparseCore 0:
  27.1 34.1 all-gather.6
  63.4 30.2 all-gather.8
  95.3 51.1 all-gather.10
  305.1 50.7 reduce-scatter.4
  390.6 50.8 reduce-scatter.6
  455.3 28.8 reduce-scatter.8
  487.2 28.8 reduce-scatter.10

commit v21 on v18

--- a/solution.py
+++ b/solution.py
@@ -374,13 +374,24 @@
     return (col[:count] == row) & (key_place <= query_place)
 
 
-def token_places(length, heads, token_rows):
-    for first in range(0, length, Q_ROWS):
+def allowed_piece(col, row, start, first):
+    same = col == row
+    if start + col.shape[0] <= first:
+        return same
+    key_place = lax.broadcasted_iota(jnp.int32, same.shape, 0) + start
+    return same & (key_place <= lax.broadcasted_iota(jnp.int32, same.shape, 1) + first)
+
+
+def token_places(length, heads, token_rows, block_rows=Q_ROWS):
+    for first in range(0, length, block_rows):
         parts = []
-        for start in range(0, Q_ROWS, token_rows):
+        for start in range(0, block_rows, token_rows):
             place = (first + start) // token_rows
             parts.append((start, place % heads, place // heads * token_rows))
         yield first, parts
+
+
+FORWARD_ROWS, FORWARD_KEYS = 1024, 512
 
 
 def attend_kernel(token_rows, proj_ref, scale_ref, col_ref, row_ref, out_ref, lse_ref):
@@ -388,16 +399,27 @@
     queries = (proj_ref[0, 0] * scale_ref[...]).astype(BF16)
     keys = proj_ref[1, 0].T.astype(BF16)
     values = proj_ref[2, 0].astype(BF16)
-    for first, parts in token_places(length, out_ref.shape[0], token_rows):
-        end = first + Q_ROWS
-        scores = jnp.dot(keys[:end], queries[:, first:end], preferred_element_type=F32)
-        allowed = allowed_keys(col_ref[...], row_ref[:, first:end], first)
-        scores = jnp.where(allowed, scores, MASKED_SCORE)
-        top = jnp.max(scores, axis=0, keepdims=True)
-        terms = jnp.exp(scores - top)
-        total = jnp.sum(terms, axis=0, keepdims=True)
-        probs = (terms * (1.0 / total)).astype(BF16)
-        attended = jnp.dot(values[:, :end], probs, preferred_element_type=F32).astype(BF16)
+    for first, parts in token_places(length, out_ref.shape[0], token_rows, FORWARD_ROWS):
+        end = first + FORWARD_ROWS
+        block, row = queries[:, first:end], row_ref[:, first:end]
+        pieces = []
+        for start in range(0, end, FORWARD_KEYS):
+            scores = jnp.dot(keys[start : start + FORWARD_KEYS], block, preferred_element_type=F32)
+            allowed = allowed_piece(col_ref[start : start + FORWARD_KEYS], row, start, first)
+            pieces.append(jnp.where(allowed, scores, MASKED_SCORE))
+        top = functools.reduce(
+            jnp.maximum, [jnp.max(piece, axis=0, keepdims=True) for piece in pieces]
+        )
+        total, attended = 0.0, 0.0
+        for i, piece in enumerate(pieces):
+            terms = jnp.exp(piece - top)
+            total += jnp.sum(terms, axis=0, keepdims=True)
+            attended += jnp.dot(
+                values[:, i * FORWARD_KEYS : (i + 1) * FORWARD_KEYS],
+                terms.astype(BF16),
+                preferred_element_type=F32,
+            )
+        attended = (attended * (1.0 / total)).astype(BF16)
         lse_ref[0, :, first:end] = top + jnp.log(total)
         for start, owner, offset in parts:
             out_ref[owner, 0, :, offset : offset + token_rows] = attended[
@@ -725,7 +747,7 @@
         ),
         out_shape=[
             pltpu.HBM((length, width), BF16),
-            pltpu.HBM((columns, length), F32),
+            jax.ShapeDtypeStruct((columns, length), F32),
         ],
         compiler_params=KERNEL,
         cost_estimate=LIGHT,
@@ -938,9 +960,13 @@
     return dot_cols(weight, out_bar).astype(BF16).reshape(4, -1, out_bar.shape[0])
 
 
-def own_sum(parts, across, beside):
+def own_quarter(parts):
     blk, row = place()[:2]
-    return quarter(parts, blk, row) + across.astype(F32) + beside.astype(F32)
+    return quarter(parts, blk, row)
+
+
+def own_sum(own, *more):
+    return sum((part.astype(F32) for part in more), own).astype(BF16)
 
 
 def sum_over(array, *hops):
@@ -982,7 +1008,7 @@
 
     first = swap_halves(tokens).reshape(-1, width)
     columns = qkv_columns(qkv_weight[0], own_gains.T)
-    columns, first = tied(columns.reshape(-1, columns.shape[-1]), first)
+    columns, first, cotangent = tied(columns.reshape(-1, columns.shape[-1]), first, cotangent)
     stream = first.astype(F32)
     along = along_batch(columns)
     far, near = swapped(first, "head", 2), other_core(first)
@@ -1069,11 +1095,11 @@
         if layer == 0:
             attended_grad = over_head(heads_grad(out_w, out_bar))
             grads, others = dense_grads(attended_t, normed_two, active, out_bar, up_bar, down_bar)
-            attended_grad, others, z_sum, across, beside = tied(
-                attended_grad, others, z_sum, across, beside
-            )
+            others, across = tied(others, across)
+            others, own = tied(others, own_quarter(cored) + across.astype(F32))
+            attended_grad, others, z_sum, beside = tied(attended_grad, others, z_sum, beside)
             others = other_core(others)
-            attended_grad, summed = tied(attended_grad, own_sum(cored, across, beside))
+            attended_grad, summed = tied(attended_grad, own_sum(own, beside))
             summed = over_batch(summed)
             z_across = across_sum(z_sum)
         else:
@@ -1099,11 +1125,12 @@
             sent = sent_beside_and_across(*rows)
             halves = halves + other_core(to_core).astype(F32)
             scale_sum = sum_over(jnp.stack(scale_grads), ("head", 1), ("batch", 1), ("batch", 2))
-            halves, sent, z_sum, scale_sum = tied(halves, sent, z_sum, scale_sum)
-            halves, own = tied(halves, own_sum(cored, *sent))
+            own = own_quarter(cored)
+            halves, sent, z_sum, scale_sum, own = tied(halves, sent, z_sum, scale_sum, own)
+            halves, own = tied(halves, own_sum(own, *sent))
             dense_first = over_batch(own)
             normed_grad = scatter_row(halves)
-            z_across, dense_first = tied(across_sum(z_sum), dense_first)
+            z_across = across_sum(z_sum)
             z_across = over_head(z_across.reshape(4, -1, z_across.shape[-1]))
             dense_grad = [dense_first, summed]
             qkv_grads = [columns_to_rows(z_across), columns_to_rows(moved)]
@@ -1123,7 +1150,9 @@
             beside = swapped(beside, "head", 2)
         upper = middle_grad + lower_of(normed_grad, stream, factor_one, gains[layer])
     input_grad = swap_halves(upper.astype(BF16).reshape(tokens.shape)).astype(F32)
-    scale_total = sum_over(scale_sum, ("head", 2), ("blk", 1))
+    scale_total = sum_over(scale_sum, ("head", 2))
+    scale_total, dense_grad[0] = tied(scale_total, dense_grad[0])
+    scale_total = sum_over(scale_total, ("blk", 1))
     scale_grad = scale_total * (SCALE_BASE / math.sqrt(head_dim)) * jax.nn.sigmoid(scale_param)
     dense_all = jnp.stack([part.astype(F32) for part in dense_grad])
     qkv_all = jnp.stack(qkv_grads)
@@ -1152,7 +1181,7 @@
         and tokens.shape[1] % 128 == 0
         and Q_ROWS % tokens.shape[1] == 0
         and segments.shape[1] <= WINDOW
-        and segments.shape[1] % Q_ROWS == 0
+        and segments.shape[1] % FORWARD_ROWS == 0
         and heads % 4 == 0
         and tokens.shape[2] % 256 == 0
     )

time: 517 us -> 521 us (level)
  Pallas kernels: 121 us -> 113 us
  starting transfers between devices: 67.9 us -> 73.6 us
    reduce_scatter x4, waiting for transfers between devices: 1.39 us -> 7.27 us  [over_batch(): lax.psum_scatter(parts.astype(BF16), 'batch', scatter_dimension=0, tiled=...]
    add x2 -> x1, other arithmetic: 8.21 us -> 2.43 us  [spread_device(): others, own = tied(others, own_quarter(cored) + across.astype(F32))]
    pallas_call x2, Pallas kernels: 18.5 us -> 12.8 us  [attend_rows(): pl.pallas_call(functools.partial(attend_kernel, token_rows), grid=(local_...]
    convert_element_type x0 -> x2, other arithmetic: none -> 5.66 us  [own_sum(): return sum((part.astype(F32) for part in more), own).astype(BF16)]
  transfers between devices with their start and end apart: 65 -> 65, of which waited for: 31 -> 33; matrix products, arithmetic and copies ran while one was open for 13% -> 16% of each run, Pallas kernels for 23% -> 21%
where the time goes in v21:
time: 521 us; the launch traced here: 513 us
  waiting for transfers between devices  182 us (35%)
  Pallas kernels  113 us (22%)
  starting transfers between devices  73.6 us (14%)
  other arithmetic  50.5 us (10%)
  local copies, waits for them, and re-layouts  39.3 us (8%)
  matrix products  19.7 us (4%)
  blocking collectives  18.8 us (4%)
  between operations  15.8 us (3%)
    ppermute x51, waiting for transfers between devices, swapped(): return lax.ppermute(array, axis, [(i, i ^ mask) for i in range(size)])  129 us
    ppermute x51, starting transfers between devices, swapped(): return lax.ppermute(array, axis, [(i, i ^ mask) for i in range(size)])  46.5 us
    all_to_all x7, starting transfers between devices, over_head(): lax.all_to_all(parts, 'head', split_axis=0, concat_axis=0, tiled=True)  26.6 us
    pallas_call x2, Pallas kernels, attend_back_rows(): pl.pallas_call(functools.partial(attend_back_kernel, token_rows), grid=(l...  24.7 us
    all_to_all x7, waiting for transfers between devices, over_head(): lax.all_to_all(parts, 'head', split_axis=0, concat_axis=0, tiled=True)  23.3 us
    all_gather x3, waiting for transfers between devices, along_batch(): return lax.all_gather(piece, 'batch', axis=0, tiled=False)  22.1 us
    all_to_all x1, blocking collectives, over_head(): lax.all_to_all(parts, 'head', split_axis=0, concat_axis=0, tiled=True)  18.8 us
    pallas_call x2, Pallas kernels, dense_grads(): pl.pallas_call(dense_grad_kernel, grid_spec=pltpu.PrefetchScalarGridSpec(...  17.1 us
  transfers between devices with their start and end apart: 65, of which 33 were waited for; matrix products, arithmetic and copies ran while one was open for 16% of the time, Pallas kernels for 21%

profile of v21, /device:TPU:0, one launch (start us, length us, event | category | flops | bytes accessed | tf_op | source)
XLA Modules:
  0.0 512.9 jit_solution(7138663818524366534)
XLA Ops:
  19.1 6.0 %all-to-all-done = bf16[4,40,964]{2,1,0:T(8,128)(2,1)S(1)} async-done(((bf16[4,40,964]{2,1,0:T(8,128)(2,1)}), bf16[4,40,964]{2,1,0:T(8,128)(2,1)S(1)}, u32[]{:S(2)}, u32[]{:S(2)}) %all-to-all-start) | async-done | bytes 308512 | tf_op jit(solution)/shard_map/all_to_all | solution.py:891
  27.2 15.1 %collective-permute-done.2.refs_2_ = bf16[256,1280]{1,0:T(8,128)(2,1)S(1)} collective-permute-done((bf16[256,1280]{1,0:T(8,128)(2,1)S(1)}, bf16[256,1280]{1,0:T(8,128)(2,1)S(1)}, u32[]{:S(2)}, u32[]{:S(2)}) %collective-permute-start.2) | collective-permute-done | bytes 655392 | tf_op jit(solution)/shard_map/ppermute | solution.py:870
  45.3 12.7 %all-gather.7.cloned.1.call-done = bf16[640,964]{1,0:T(8,128)(2,1)} async-done(((bf16[160,964]{1,0:T(8,128)(2,1)}), bf16[640,964]{1,0:T(8,128)(2,1)}) %all-gather.7.cloned.1.call-update) | async-done | bytes 1233936 | tf_op jit(solution)/shard_map/all_gather | solution.py:904
  64.8 6.6 %all-to-all-done.1 = bf16[4,40,960]{2,1,0:T(8,128)(2,1)S(1)} async-done(((bf16[4,40,960]{2,1,0:T(8,128)(2,1)}), bf16[4,40,960]{2,1,0:T(8,128)(2,1)S(1)}, u32[]{:S(2)}, u32[]{:S(2)}) %all-to-all-start.1) | async-done | bytes 307232 | tf_op jit(solution)/shard_map/all_to_all | solution.py:891
  71.7 16.5 %collective-permute-done.5.across_ref = bf16[4,160,964]{2,1,0:T(8,128)(2,1)S(1)} collective-permute-done((bf16[4,160,964]{2,1,0:T(8,128)(2,1)}, bf16[4,160,964]{2,1,0:T(8,128)(2,1)S(1)}, u32[]{:S(2)}, u32[]{:S(2)}) %collective-permute-start.5) | collective-permute-done | bytes 1233952 | tf_op jit(solution)/shard_map/ppermute | solution.py:870
  94.9 4.6 shard_map.169
  100.9 7.7 %shard_map.170 = (bf16[1024,1280]{1,0:T(8,128)(2,1)}, f32[960,1024]{1,0:T(8,128)S(1)}) custom-call(s32[3]{0:T(128)S(1)} %pad_add_fusion.place_ref.core_ref, bf16[256,1280]{1,0:T(8,128)(2,1)} %bitcast.227, bf16[256,1280]{1,0:T(8,128)(2,1)} %copy-done.50, bf16[256,1280]{1,0:T(8,128)(2,1)} %copy-done.49, bf16[256,1280]{1,0:T(8,128)(2,1)} %collective-permute-done.3.refs_3_, ...), custom_call_target="tpu_custom_call" | custom-call | flops 1048576 | bytes 1048576 | tf_op jit(solution)/shard_map/pallas_call | solution.py:733
  108.7 6.7 %shard_map.171 = (bf16[4,4,80,256]{3,2,1,0:T(8,128)(2,1)}, f32[4,1,1024]{2,1,0:T(1,128)S(1)}) custom-call(f32[3,4,80,1024]{3,2,1,0:T(8,128)S(1)} %bitcast.197, f32[80,1]{1,0:T(8,128)S(1)} %copy.60.scale_ref, s32[1024,1]{1,0:T(8,128)S(1)} %copy.61.col_ref, s32[1,1024]{1,0:T(1,128)S(1)} %constant_dynamic-slice_fusion.row_ref), custom_call_target="tpu_custom_call" | custom-call | flops 1048576 | bytes 1048576 | tf_op jit(solution)/shard_map/pallas_call | solution.py:435
  115.4 4.5 collective-permute-done.7.refs_2_
  130.9 5.3 %collective-permute-done.9.refs_4_ = bf16[4,40,1920]{2,1,0:T(8,128)(2,1)} collective-permute-done((bf16[4,40,1920]{2,1,0:T(8,128)(2,1)}, bf16[4,40,1920]{2,1,0:T(8,128)(2,1)}, u32[]{:S(2)}, u32[]{:S(2)}) %collective-permute-start.9) | collective-permute-done | bytes 614432 | tf_op jit(solution)/shard_map/ppermute | solution.py:870
  136.2 7.1 %all-gather.11.cloned.1.call-done = bf16[8,40,3840]{2,1,0:T(8,128)(2,1)} async-done(((bf16[2,40,3840]{2,1,0:T(8,128)(2,1)}), bf16[8,40,3840]{2,1,0:T(8,128)(2,1)}) %all-gather.11.cloned.1.call-update) | async-done | bytes 2457616 | tf_op jit(solution)/shard_map/all_gather | solution.py:904
  149.6 4.5 shard_map.172
  161.8 16.6 %collective-permute-done.16.across_ref = bf16[4,40,3840]{2,1,0:T(8,128)(2,1)S(1)} collective-permute-done((bf16[4,40,3840]{2,1,0:T(8,128)(2,1)S(1)}, bf16[4,40,3840]{2,1,0:T(8,128)(2,1)S(1)}, u32[]{:S(2)}, u32[]{:S(2)}) %collective-permute-start.16) | collective-permute-done | bytes 1228832 | tf_op jit(solution)/shard_map/ppermute | solution.py:870
  181.1 4.7 shard_map.173
  185.9 6.6 %shard_map.174 = (bf16[1024,1280]{1,0:T(8,128)(2,1)}, f32[960,1024]{1,0:T(8,128)S(1)}) custom-call(s32[3]{0:T(128)S(1)} %pad_add_fusion.place_ref.core_ref, bf16[256,1280]{1,0:T(8,128)(2,1)} %multiply_convert_fusion.2.refs_0_, bf16[256,1280]{1,0:T(8,128)(2,1)} %collective-permute-done.17.refs_1_, bf16[256,1280]{1,0:T(8,128)(2,1)} %collective-permute-done.15.refs_2_, ...), custom_call_target="tpu_custom_call" | custom-call | flops 1048576 | bytes 1048576 | tf_op jit(solution)/shard_map/pallas_call | solution.py:733
  192.5 6.1 %shard_map.175 = (bf16[4,4,80,256]{3,2,1,0:T(8,128)(2,1)S(1)}, f32[4,1,1024]{2,1,0:T(1,128)S(1)}) custom-call(f32[3,4,80,1024]{3,2,1,0:T(8,128)S(1)} %bitcast.199, f32[80,1]{1,0:T(8,128)S(1)} %copy.64.scale_ref, s32[1024,1]{1,0:T(8,128)S(1)} %copy.61.col_ref, s32[1,1024]{1,0:T(1,128)S(1)} %constant_dynamic-slice_fusion.row_ref), custom_call_target="tpu_custom_call" | custom-call | flops 1048576 | bytes 1048576 | tf_op jit(solution)/shard_map/pallas_call | solution.py:435
  198.6 8.6 %collective-permute-done.20.refs_2_ = bf16[4,40,3840]{2,1,0:T(8,128)(2,1)S(1)} collective-permute-done((bf16[4,40,3840]{2,1,0:T(8,128)(2,1)S(1)}, bf16[4,40,3840]{2,1,0:T(8,128)(2,1)S(1)}, u32[]{:S(2)}, u32[]{:S(2)}) %collective-permute-start.20) | collective-permute-done | bytes 1228832 | tf_op jit(solution)/shard_map/ppermute | solution.py:870
  211.9 18.8 %all_to_all.40 = bf16[4,320,256]{2,1,0:T(8,128)(2,1)S(1)} all-to-all(bf16[4,320,256]{2,1,0:T(8,128)(2,1)S(1)} %bitcast.215), channel_id=1, replica_groups=mesh['batch'=4,'blk'=2,'head'=4] {'head'}, dimensions={0} | all-to-all | bytes 1310720 | tf_op jit(solution)/shard_map/all_to_all | solution.py:891
  252.5 8.5 %shard_map.177 = (bf16[2,2,4,40,3840]{4,3,2,1,0:T(8,128)(2,1)}, bf16[2,2,4,40,3840]{4,3,2,1,0:T(8,128)(2,1)}) custom-call(s32[3]{0:T(128)S(1)} %pad_add_fusion.place_ref.core_ref, bf16[1280,256]{1,0:T(8,128)(2,1)} %bitcast.239, bf16[256,1280]{1,0:T(8,128)(2,1)} %copy-done.25, bf16[256,1280]{1,0:T(8,128)(2,1)} %copy-done.47, bf16[256,1280]{1,0:T(8,128)(2,1)} %copy-done.26, ...), custom_call_target="tpu_custom_call" | custom-call | flops 1048576 | bytes 1048576 | tf_op jit(solution)/shard_map/pallas_call | solution.py:599
  263.4 12.4 %shard_map.178 = (bf16[3,4,80,1024]{3,2,1,0:T(8,128)(2,1)}, f32[80,128]{1,0:T(8,128)}) custom-call(f32[3,4,80,1024]{3,2,1,0:T(8,128)} %bitcast.200, bf16[4,4,80,256]{3,2,1,0:T(8,128)(2,1)} %bitcast.56.grad_ref, f32[4,1,1024]{2,1,0:T(1,128)S(1)} %get-tuple-element.154.lse_ref, f32[80,1]{1,0:T(8,128)S(1)} %copy.64.scale_ref, s32[1024,1]{1,0:T(8,128)S(1)} %copy.61.col_ref, ...), custom_call_target="tpu_custom_call" | custom-call | flops 1048576 | bytes 1048576 | tf_op jit(solution)/shard_map/pallas_call | solution.py:528
  281.5 11.3 %shard_map.179 = (f32[2,2,128,1280]{3,2,1,0:T(8,128)}, bf16[2,2,128,1280]{3,2,1,0:T(8,128)(2,1)}, bf16[1280,960]{1,0:T(8,128)(2,1)}) custom-call(s32[3]{0:T(128)S(1)} %pad_add_fusion.place_ref.core_ref, bf16[960,1024]{1,0:T(8,128)(2,1)} %bitcast.241, bf16[1280,960]{1,0:T(8,128)(2,1)} %bitcast.217, bf16[1024,1280]{1,0:T(8,128)(2,1)} %get-tuple-element.161.normed_ref), custom_call_target="tpu_custom_call" | custom-call | flops 1048576 | bytes 1048576 | tf_op jit(solution)/shard_map/pallas_call | solution.py:779
  307.8 13.8 %collective-permute-done.33 = bf16[2,128,1280]{2,1,0:T(8,128)(2,1)} collective-permute-done((bf16[2,128,1280]{2,1,0:T(8,128)(2,1)}, bf16[2,128,1280]{2,1,0:T(8,128)(2,1)}, u32[]{:S(2)}, u32[]{:S(2)}) %collective-permute-start.33) | collective-permute-done | bytes 655392 | tf_op jit(solution)/shard_map/ppermute | solution.py:870
  340.1 8.6 %shard_map.180 = (bf16[2,2,4,40,3840]{4,3,2,1,0:T(8,128)(2,1)}, bf16[2,2,4,40,3840]{4,3,2,1,0:T(8,128)(2,1)}) custom-call(s32[3]{0:T(128)S(1)} %pad_add_fusion.place_ref.core_ref, bf16[1280,256]{1,0:T(8,128)(2,1)} %bitcast.236, bf16[256,1280]{1,0:T(8,128)(2,1)} %copy-done.24, bf16[256,1280]{1,0:T(8,128)(2,1)} %copy-done.43, bf16[256,1280]{1,0:T(8,128)(2,1)} %copy-done.30, ...), custom_call_target="tpu_custom_call" | custom-call | flops 1048576 | bytes 1048576 | tf_op jit(solution)/shard_map/pallas_call | solution.py:599
  351.1 7.7 %all-to-all-done.5 = bf16[4,320,256]{2,1,0:T(8,128)(2,1)} async-done(((bf16[4,320,256]{2,1,0:T(8,128)(2,1)}), bf16[4,320,256]{2,1,0:T(8,128)(2,1)}, u32[]{:S(2)}, u32[]{:S(2)}) %all-to-all-start.5) | async-done | bytes 655392 | tf_op jit(solution)/shard_map/all_to_all | solution.py:891
  364.1 12.3 %shard_map.181 = (bf16[3,4,80,1024]{3,2,1,0:T(8,128)(2,1)}, f32[80,128]{1,0:T(8,128)}) custom-call(f32[3,4,80,1024]{3,2,1,0:T(8,128)} %bitcast.198, bf16[4,4,80,256]{3,2,1,0:T(8,128)(2,1)} %bitcast.68.grad_ref, f32[4,1,1024]{2,1,0:T(1,128)S(1)} %get-tuple-element.184.lse_ref, f32[80,1]{1,0:T(8,128)S(1)} %copy.60.scale_ref, s32[1024,1]{1,0:T(8,128)S(1)} %copy.61.col_ref, ...), custom_call_target="tpu_custom_call" | custom-call | flops 1048576 | bytes 1048576 | tf_op jit(solution)/shard_map/pallas_call | solution.py:528
  380.7 6.7 %add_bitcast_fusion = (f32[4,40,3840]{2,1,0:T(8,128)S(1)}, f32[4,40,3840]{2,1,0:T(8,128)}, f32[4,40,3840]{2,1,0:T(8,128)}, bf16[4,40,3840]{2,1,0:T(8,128)(2,1)}) fusion(bf16[2,2,4,40,3840]{4,3,2,1,0:T(8,128)(2,1)} %collective-permute-done.36, s32[]{:T(128)S(6)} %select_n.174, s32[]{:T(128)S(6)} %select_n.173, ...), kind=kLoop, calls=%fused_computation.43 | loop fusion | flops 7987200 | bytes 18432016 | tf_op jit(solution)/shard_map/add | solution.py:936
  387.4 7.6 %shard_map.182 = bf16[1280,960]{1,0:T(8,128)(2,1)} custom-call(bf16[960,1024]{1,0:T(8,128)(2,1)} %bitcast.231, bf16[1024,1280]{1,0:T(8,128)(2,1)} %get-tuple-element.189.normed_ref), custom_call_target="tpu_custom_call" | custom-call | flops 1048576 | bytes 1048576 | tf_op jit(solution)/shard_map/pallas_call | solution.py:850
  403.5 8.2 %shard_map.183 = (f32[2,2,128,1280]{3,2,1,0:T(8,128)}, bf16[2,2,128,1280]{3,2,1,0:T(8,128)(2,1)}) custom-call(s32[3]{0:T(128)S(1)} %pad_add_fusion.place_ref.core_ref, bf16[960,1024]{1,0:T(8,128)(2,1)} %bitcast.232, bf16[1280,960]{1,0:T(8,128)(2,1)} %bitcast.224), custom_call_target="tpu_custom_call" | custom-call | flops 1048576 | bytes 1048576 | tf_op jit(solution)/shard_map/pallas_call | solution.py:820
  435.3 14.7 %collective-permute-done.41 = bf16[4,40,3840]{2,1,0:T(8,128)(2,1)} collective-permute-done((bf16[4,40,3840]{2,1,0:T(8,128)(2,1)S(1)}, bf16[4,40,3840]{2,1,0:T(8,128)(2,1)}, u32[]{:S(2)}, u32[]{:S(2)}) %collective-permute-start.41) | collective-permute-done | bytes 1228832 | tf_op jit(solution)/shard_map/ppermute | solution.py:870
  470.6 7.9 %collective-permute-done.49 = f32[2,80]{1,0:T(2,128)S(1)} collective-permute-done((f32[2,80]{1,0:T(2,128)S(1)}, f32[2,80]{1,0:T(2,128)S(1)}, u32[]{:S(2)}, u32[]{:S(2)}) %collective-permute-start.49) | collective-permute-done | bytes 672 | tf_op jit(solution)/shard_map/ppermute | solution.py:870
  487.0 5.3 %collective-permute-done.47 = bf16[128,1280]{1,0:T(8,128)(2,1)S(1)} collective-permute-done((bf16[128,1280]{1,0:T(8,128)(2,1)S(1)}, bf16[128,1280]{1,0:T(8,128)(2,1)S(1)}, u32[]{:S(2)}, u32[]{:S(2)}) %collective-permute-start.47) | collective-permute-done | bytes 327712 | tf_op jit(solution)/shard_map/ppermute | solution.py:870
  493.6 7.3 %reduce-scatter.11.cloned.1.call-done = bf16[1,40,3840]{2,1,0:T(8,128)(2,1)} async-done(((bf16[4,40,3840]{2,1,0:T(8,128)(2,1)}), bf16[1,40,3840]{2,1,0:T(8,128)(2,1)}) %reduce-scatter.11.cloned.1.call-update) | async-done | bytes 307216 | tf_op jit(solution)/shard_map/reduce_scatter | solution.py:920
  (375 shorter events, 205.7 us)
Async XLA Ops:
  18.4 39.7 %all-gather.7.cloned.1.call-start = ((), (), s32[]{:S(2)}) async-start(), calls=%async_computation.16 | async-start | bytes 1638400 | tf_op jit(solution)/shard_map/all_gather | solution.py:904
  25.8 64.7 %all-gather.9.cloned.1.call-start = ((), (), s32[]{:S(2)}) async-start(), calls=%async_computation.17 | async-start | bytes 1536000 | tf_op jit(solution)/shard_map/all_gather | solution.py:904
  58.1 30.1 %collective-permute-start.5 = (bf16[4,160,964]{2,1,0:T(8,128)(2,1)}, bf16[4,160,964]{2,1,0:T(8,128)(2,1)S(1)}, u32[]{:S(2)}, u32[]{:S(2)}) collective-permute-start(bf16[4,160,964]{2,1,0:T(8,128)(2,1)} %bitcast.247), channel_id=1, source_target_pairs={{0,4},{4,0},{1,5},{5,1},{2,6},{6,2},{3,7},{7,3},{8,12},{12,8},{9,1... | collective-permute-start | bytes 3701768 | tf_op jit(solution)/shard_map/ppermute | solution.py:870
  64.8 78.5 %all-gather.11.cloned.1.call-start = ((), (), s32[]{:S(2)}) async-start(), calls=%async_computation.18 | async-start | bytes 3072000 | tf_op jit(solution)/shard_map/all_gather | solution.py:904
  91.5 28.4 %collective-permute-start.7 = (bf16[4,40,3840]{2,1,0:T(8,128)(2,1)}, bf16[4,40,3840]{2,1,0:T(8,128)(2,1)S(1)}, u32[]{:S(2)}, u32[]{:S(2)}) collective-permute-start(bf16[4,40,3840]{2,1,0:T(8,128)(2,1)} %bitcast.19.refs_0_), channel_id=1, source_target_pairs={{0,2},{1,3},{2,0},{3,1},{4,6},{5,7},{6,4},{7,5},{8,10},{9,11},{10,... | collective-permute-start | bytes 3686408 | tf_op jit(solution)/shard_map/ppermute | solution.py:870
  93.0 28.2 %collective-permute-start.6 = (bf16[4,40,3840]{2,1,0:T(8,128)(2,1)}, bf16[4,40,3840]{2,1,0:T(8,128)(2,1)}, u32[]{:S(2)}, u32[]{:S(2)}) collective-permute-start(bf16[4,40,3840]{2,1,0:T(8,128)(2,1)} %bitcast.19.refs_0_), channel_id=1, source_target_pairs={{0,4},{4,0},{1,5},{5,1},{2,6},{6,2},{3,7},{7,3},{8,12},{12,8},{9,1... | collective-permute-start | bytes 3686408 | tf_op jit(solution)/shard_map/ppermute | solution.py:870
  125.5 20.7 %collective-permute-start.8 = (bf16[4,40,1920]{2,1,0:T(8,128)(2,1)}, bf16[4,40,1920]{2,1,0:T(8,128)(2,1)}, u32[]{:S(2)}, u32[]{:S(2)}) collective-permute-start(bf16[4,40,1920]{2,1,0:T(8,128)(2,1)} %slice.153), channel_id=1, source_target_pairs={{0,2},{1,3},{2,0},{3,1},{4,6},{5,7},{6,4},{7,5},{8,10},{9,11},{10,... | collective-permute-start | bytes 1843208 | tf_op jit(solution)/shard_map/ppermute | solution.py:870
  126.0 20.2 %all-to-all-start.2 = ((bf16[4,320,256]{2,1,0:T(8,128)(2,1)}), bf16[4,320,256]{2,1,0:T(8,128)(2,1)S(1)}, u32[]{:S(2)}, u32[]{:S(2)}) async-start(bf16[4,320,256]{2,1,0:T(8,128)(2,1)} %bitcast.31), calls=%async_computation.2 | async-start | bytes 1310720 | tf_op jit(solution)/shard_map/all_to_all | solution.py:891
  129.8 19.1 %collective-permute-start.10 = (bf16[4,40,3840]{2,1,0:T(8,128)(2,1)}, bf16[4,40,3840]{2,1,0:T(8,128)(2,1)}, u32[]{:S(2)}, u32[]{:S(2)}) collective-permute-start(bf16[4,40,3840]{2,1,0:T(8,128)(2,1)} %bitcast.19.refs_0_), channel_id=1, source_target_pairs={{0,1},{1,0},{2,3},{3,2},{4,5},{5,4},{6,7},{7,6},{8,9},{9,8},{10,11... | collective-permute-start | bytes 3686408 | tf_op jit(solution)/shard_map/ppermute | solution.py:870
  130.4 19.2 %collective-permute-start.11 = (bf16[4,40,3840]{2,1,0:T(8,128)(2,1)}, bf16[4,40,3840]{2,1,0:T(8,128)(2,1)}, u32[]{:S(2)}, u32[]{:S(2)}) collective-permute-start(bf16[4,40,3840]{2,1,0:T(8,128)(2,1)} %collective-permute-done.6.refs_1_), channel_id=1, source_target_pairs={{0,1},{1,0},{2,3},{3,2},{4,5},{5,4},{6,7},{7,6},{8,9},{9,8},{10,11... | collective-permute-start | bytes 3686408 | tf_op jit(solution)/shard_map/ppermute | solution.py:870
  130.4 19.2 %collective-permute-start.12 = (bf16[4,40,3840]{2,1,0:T(8,128)(2,1)S(1)}, bf16[4,40,3840]{2,1,0:T(8,128)(2,1)}, u32[]{:S(2)}, u32[]{:S(2)}) collective-permute-start(bf16[4,40,3840]{2,1,0:T(8,128)(2,1)S(1)} %collective-permute-done.7.refs_2_), channel_id=1, source_target_pairs={{0,1},{1,0},{2,3},{3,2},{4,5},{5,4},{6,7},{7,6},{8,9},{9,8},{10,11... | collective-permute-start | bytes 3686408 | tf_op jit(solution)/shard_map/ppermute | solution.py:870
  149.0 29.5 %collective-permute-start.16 = (bf16[4,40,3840]{2,1,0:T(8,128)(2,1)S(1)}, bf16[4,40,3840]{2,1,0:T(8,128)(2,1)S(1)}, u32[]{:S(2)}, u32[]{:S(2)}) collective-permute-start(bf16[4,40,3840]{2,1,0:T(8,128)(2,1)S(1)} %get-tuple-element.245.along_ref), channel_id=1, source_target_pairs={{0,4},{4,0},{1,5},{5,1},{2,6},{6,2},{3,7},{7,3},{8,12},{12,8},{9,1... | collective-permute-start | bytes 3686408 | tf_op jit(solution)/shard_map/ppermute | solution.py:870
  178.5 28.8 %collective-permute-start.20 = (bf16[4,40,3840]{2,1,0:T(8,128)(2,1)S(1)}, bf16[4,40,3840]{2,1,0:T(8,128)(2,1)S(1)}, u32[]{:S(2)}, u32[]{:S(2)}) collective-permute-start(bf16[4,40,3840]{2,1,0:T(8,128)(2,1)S(1)} %get-tuple-element.139.refs_0_), channel_id=1, source_target_pairs={{0,2},{1,3},{2,0},{3,1},{4,6},{5,7},{6,4},{7,5},{8,10},{9,11},{10,... | collective-permute-start | bytes 3686408 | tf_op jit(solution)/shard_map/ppermute | solution.py:870
  179.0 28.6 %collective-permute-start.19 = (bf16[4,40,3840]{2,1,0:T(8,128)(2,1)S(1)}, bf16[4,40,3840]{2,1,0:T(8,128)(2,1)}, u32[]{:S(2)}, u32[]{:S(2)}) collective-permute-start(bf16[4,40,3840]{2,1,0:T(8,128)(2,1)S(1)} %get-tuple-element.139.refs_0_), channel_id=1, source_target_pairs={{0,4},{4,0},{1,5},{5,1},{2,6},{6,2},{3,7},{7,3},{8,12},{12,8},{9,1... | collective-permute-start | bytes 3686408 | tf_op jit(solution)/shard_map/ppermute | solution.py:870
  208.8 21.8 %collective-permute-start.22 = (bf16[4,40,1920]{2,1,0:T(8,128)(2,1)S(1)}, bf16[4,40,1920]{2,1,0:T(8,128)(2,1)S(1)}, u32[]{:S(2)}, u32[]{:S(2)}) collective-permute-start(bf16[4,40,1920]{2,1,0:T(8,128)(2,1)S(1)} %slice.167), channel_id=1, source_target_pairs={{0,4},{4,0},{1,5},{5,1},{2,6},{6,2},{3,7},{7,3},{8,12},{12,8},{9,1... | collective-permute-start | bytes 1843208 | tf_op jit(solution)/shard_map/ppermute | solution.py:870
  209.9 20.7 %collective-permute-start.21 = (bf16[4,40,1920]{2,1,0:T(8,128)(2,1)S(1)}, bf16[4,40,1920]{2,1,0:T(8,128)(2,1)S(1)}, u32[]{:S(2)}, u32[]{:S(2)}) collective-permute-start(bf16[4,40,1920]{2,1,0:T(8,128)(2,1)S(1)} %slice.166), channel_id=1, source_target_pairs={{0,2},{1,3},{2,0},{3,1},{4,6},{5,7},{6,4},{7,5},{8,10},{9,11},{10,... | collective-permute-start | bytes 1843208 | tf_op jit(solution)/shard_map/ppermute | solution.py:870
  211.3 19.9 %collective-permute-start.23 = (bf16[4,40,3840]{2,1,0:T(8,128)(2,1)S(1)}, bf16[4,40,3840]{2,1,0:T(8,128)(2,1)S(1)}, u32[]{:S(2)}, u32[]{:S(2)}) collective-permute-start(bf16[4,40,3840]{2,1,0:T(8,128)(2,1)S(1)} %get-tuple-element.139.refs_0_), channel_id=1, source_target_pairs={{0,1},{1,0},{2,3},{3,2},{4,5},{5,4},{6,7},{7,6},{8,9},{9,8},{10,11... | collective-permute-start | bytes 3686408 | tf_op jit(solution)/shard_map/ppermute | solution.py:870
  211.3 22.3 %collective-permute-start.24 = (bf16[4,40,3840]{2,1,0:T(8,128)(2,1)}, bf16[4,40,3840]{2,1,0:T(8,128)(2,1)S(1)}, u32[]{:S(2)}, u32[]{:S(2)}) collective-permute-start(bf16[4,40,3840]{2,1,0:T(8,128)(2,1)} %collective-permute-done.19.refs_1_), channel_id=1, source_target_pairs={{0,1},{1,0},{2,3},{3,2},{4,5},{5,4},{6,7},{7,6},{8,9},{9,8},{10,11... | collective-permute-start | bytes 3686408 | tf_op jit(solution)/shard_map/ppermute | solution.py:870
  211.9 21.8 %collective-permute-start.25 = (bf16[4,40,3840]{2,1,0:T(8,128)(2,1)S(1)}, bf16[4,40,3840]{2,1,0:T(8,128)(2,1)S(1)}, u32[]{:S(2)}, u32[]{:S(2)}) collective-permute-start(bf16[4,40,3840]{2,1,0:T(8,128)(2,1)S(1)} %collective-permute-done.20.refs_2_), channel_id=1, source_target_pairs={{0,1},{1,0},{2,3},{3,2},{4,5},{5,4},{6,7},{7,6},{8,9},{9,8},{10,11... | collective-permute-start | bytes 3686408 | tf_op jit(solution)/shard_map/ppermute | solution.py:870
  241.8 19.1 %collective-permute-start.28 = (bf16[128,1280]{1,0:T(8,128)(2,1)}, bf16[128,1280]{1,0:T(8,128)(2,1)}, u32[]{:S(2)}, u32[]{:S(2)}) collective-permute-start(bf16[128,1280]{1,0:T(8,128)(2,1)} %dynamic-slice_bitcast_fusion.3), channel_id=1, source_target_pairs={{0,4},{4,0},{1,5},{5,1},{2,6},{6,2},{3,7},{7,3},{8,12},{12,8},{9,1... | collective-permute-start | bytes 983048 | tf_op jit(solution)/shard_map/ppermute | solution.py:870
  252.3 106.6 %reduce-scatter.5.cloned.1.call-start = ((), (), s32[]{:S(2)}) async-start(), calls=%async_computation.12 | async-start | bytes 3276800 | tf_op jit(solution)/shard_map/reduce_scatter | solution.py:920
  306.2 42.5 %collective-permute-start.34 = (bf16[4,40,3840]{2,1,0:T(8,128)(2,1)}, bf16[4,40,3840]{2,1,0:T(8,128)(2,1)}, u32[]{:S(2)}, u32[]{:S(2)}) collective-permute-start(bf16[4,40,3840]{2,1,0:T(8,128)(2,1)} %pad_maximum_fusion), channel_id=1, source_target_pairs={{0,4},{4,0},{1,5},{5,1},{2,6},{6,2},{3,7},{7,3},{8,12},{12,8},{9,1... | collective-permute-start | bytes 3686408 | tf_op jit(solution)/shard_map/ppermute | solution.py:870
  323.2 35.6 %collective-permute-start.35 = (bf16[4,40,3840]{2,1,0:T(8,128)(2,1)}, bf16[4,40,3840]{2,1,0:T(8,128)(2,1)}, u32[]{:S(2)}, u32[]{:S(2)}) collective-permute-start(bf16[4,40,3840]{2,1,0:T(8,128)(2,1)} %pad_maximum_fusion.1), channel_id=1, source_target_pairs={{0,2},{1,3},{2,0},{3,1},{4,6},{5,7},{6,4},{7,5},{8,10},{9,11},{10,... | collective-permute-start | bytes 3686408 | tf_op jit(solution)/shard_map/ppermute | solution.py:870
  335.9 23.0 %all-to-all-start.5 = ((bf16[4,320,256]{2,1,0:T(8,128)(2,1)}), bf16[4,320,256]{2,1,0:T(8,128)(2,1)}, u32[]{:S(2)}, u32[]{:S(2)}) async-start(bf16[4,320,256]{2,1,0:T(8,128)(2,1)} %bitcast.64), calls=%async_computation.5 | async-start | bytes 1310720 | tf_op jit(solution)/shard_map/all_to_all | solution.py:891
  340.1 71.7 %reduce-scatter.7.cloned.1.call-start = ((), (), s32[]{:S(2)}) async-start(), calls=%async_computation.13 | async-start | bytes 1536000 | tf_op jit(solution)/shard_map/reduce_scatter | solution.py:920
  358.9 18.3 %collective-permute-start.36 = (bf16[2,2,4,40,3840]{4,3,2,1,0:T(8,128)(2,1)}, bf16[2,2,4,40,3840]{4,3,2,1,0:T(8,128)(2,1)}, u32[]{:S(2)}, u32[]{:S(2)}) collective-permute-start(bf16[2,2,4,40,3840]{4,3,2,1,0:T(8,128)(2,1)} %get-tuple-element.186), channel_id=1, source_target_pairs={{0,1},{1,0},{2,3},{3,2},{4,5},{5,4},{6,7},{7,6},{8,9},{9,8},{10,11... | collective-permute-start | bytes 14745608 | tf_op jit(solution)/shard_map/ppermute | solution.py:870
  377.2 17.8 %all-to-all-start.6 = ((bf16[4,40,960]{2,1,0:T(8,128)(2,1)}), bf16[4,40,960]{2,1,0:T(8,128)(2,1)S(1)}, u32[]{:S(2)}, u32[]{:S(2)}) async-start(bf16[4,40,960]{2,1,0:T(8,128)(2,1)} %bitcast.72), calls=%async_computation.7 | async-start | bytes 655360 | tf_op jit(solution)/shard_map/all_to_all | solution.py:891
  380.7 70.6 %reduce-scatter.9.cloned.1.call-start = ((), (), s32[]{:S(2)}) async-start(), calls=%async_computation.14 | async-start | bytes 3276800 | tf_op jit(solution)/shard_map/reduce_scatter | solution.py:920
  420.4 29.6 %collective-permute-start.41 = (bf16[4,40,3840]{2,1,0:T(8,128)(2,1)S(1)}, bf16[4,40,3840]{2,1,0:T(8,128)(2,1)}, u32[]{:S(2)}, u32[]{:S(2)}) collective-permute-start(bf16[4,40,3840]{2,1,0:T(8,128)(2,1)S(1)} %pad_maximum_fusion.2), channel_id=1, source_target_pairs={{0,4},{4,0},{1,5},{5,1},{2,6},{6,2},{3,7},{7,3},{8,12},{12,8},{9,1... | collective-permute-start | bytes 3686408 | tf_op jit(solution)/shard_map/ppermute | solution.py:870
  422.0 29.3 %collective-permute-start.42 = (bf16[4,40,3840]{2,1,0:T(8,128)(2,1)S(1)}, bf16[4,40,3840]{2,1,0:T(8,128)(2,1)}, u32[]{:S(2)}, u32[]{:S(2)}) collective-permute-start(bf16[4,40,3840]{2,1,0:T(8,128)(2,1)S(1)} %pad_maximum_fusion.3), channel_id=1, source_target_pairs={{0,2},{1,3},{2,0},{3,1},{4,6},{5,7},{6,4},{7,5},{8,10},{9,11},{10,... | collective-permute-start | bytes 3686408 | tf_op jit(solution)/shard_map/ppermute | solution.py:870
  458.8 21.7 %collective-permute-start.46 = (bf16[2,128,1280]{2,1,0:T(8,128)(2,1)}, bf16[2,128,1280]{2,1,0:T(8,128)(2,1)}, u32[]{:S(2)}, u32[]{:S(2)}) collective-permute-start(bf16[2,128,1280]{2,1,0:T(8,128)(2,1)} %fusion.84), channel_id=1, source_target_pairs={{0,2},{1,3},{2,0},{3,1},{4,6},{5,7},{6,4},{7,5},{8,10},{9,11},{10,... | collective-permute-start | bytes 1966088 | tf_op jit(solution)/shard_map/ppermute | solution.py:870
  467.1 33.7 %reduce-scatter.11.cloned.1.call-start = ((), (), s32[]{:S(2)}) async-start(), calls=%async_computation.15 | async-start | bytes 1536000 | tf_op jit(solution)/shard_map/reduce_scatter | solution.py:920
  (98 other events, 745.3 us)
Sparse Core Ops, SparseCore 0:
  26.0 32.0 all-gather.6
  60.2 30.2 all-gather.8
  92.1 51.1 all-gather.10
  306.3 51.8 reduce-scatter.4
  361.6 31.1 reduce-scatter.6
  395.2 52.3 reduce-scatter.8
  470.7 30.0 reduce-scatter.10

commit v22 on v21

--- a/solution.py
+++ b/solution.py
@@ -1101,7 +1101,7 @@
             others = other_core(others)
             attended_grad, summed = tied(attended_grad, own_sum(own, beside))
             summed = over_batch(summed)
-            z_across = across_sum(z_sum)
+            earlier = across_sum(z_sum)
         else:
             attended_grad = over_head(heads_grad(out_w, out_bar))
             grads, others = dense_grads(attended_t, normed_two, active, out_bar, up_bar, down_bar)
@@ -1111,10 +1111,9 @@
             projected, attended_grad, log_total, scale_vecs[layer], segments, token_rows
         )
         if layer == 0:
-            bars, others, z_across = tied(bars, others, z_across)
-            moved = over_head(z_across.reshape(4, -1, z_across.shape[-1]))
+            bars, earlier = tied(bars, earlier)
             qkv_grad = weight_back(bars, normed_all)
-            bars, qkv_grad, moved = tied(bars, qkv_grad, moved)
+            bars, qkv_grad, others = tied(bars, qkv_grad, others)
             z_sum = over_batch(qkv_grad.reshape(4, 2, -1, qkv_grad.shape[-1]))
             cored = (grads, others)
             bars, rows = tied(bars, diagonal_rows(cored))
@@ -1127,10 +1126,11 @@
             scale_sum = sum_over(jnp.stack(scale_grads), ("head", 1), ("batch", 1), ("batch", 2))
             own = own_quarter(cored)
             halves, sent, z_sum, scale_sum, own = tied(halves, sent, z_sum, scale_sum, own)
-            halves, own = tied(halves, own_sum(own, *sent))
+            halves, own, earlier = tied(halves, own_sum(own, *sent), earlier)
+            moved = over_head(earlier.reshape(4, -1, earlier.shape[-1]))
             dense_first = over_batch(own)
             normed_grad = scatter_row(halves)
-            z_across = across_sum(z_sum)
+            z_across, scale_sum, dense_first = tied(across_sum(z_sum), scale_sum, dense_first)
             z_across = over_head(z_across.reshape(4, -1, z_across.shape[-1]))
             dense_grad = [dense_first, summed]
             qkv_grads = [columns_to_rows(z_across), columns_to_rows(moved)]
@@ -1150,9 +1150,7 @@
             beside = swapped(beside, "head", 2)
         upper = middle_grad + lower_of(normed_grad, stream, factor_one, gains[layer])
     input_grad = swap_halves(upper.astype(BF16).reshape(tokens.shape)).astype(F32)
-    scale_total = sum_over(scale_sum, ("head", 2))
-    scale_total, dense_grad[0] = tied(scale_total, dense_grad[0])
-    scale_total = sum_over(scale_total, ("blk", 1))
+    scale_total = sum_over(scale_sum, ("head", 2), ("blk", 1))
     scale_grad = scale_total * (SCALE_BASE / math.sqrt(head_dim)) * jax.nn.sigmoid(scale_param)
     dense_all = jnp.stack([part.astype(F32) for part in dense_grad])
     qkv_all = jnp.stack(qkv_grads)

time: 521 us -> 516 us (level)
    unnamed x130 -> x136, local copies, waits for them, and re-layouts: 12.2 us -> 11.5 us
  transfers between devices with their start and end apart: 65 -> 65, of which waited for: 33 -> 35; matrix products, arithmetic and copies ran while one was open for 16% -> 14% of each run, Pallas kernels for 21% -> 22%
where the time goes in v22:
time: 516 us; the launch traced here: 508 us
  waiting for transfers between devices  181 us (35%)
  Pallas kernels  113 us (22%)
  starting transfers between devices  73.6 us (14%)
  other arithmetic  50.5 us (10%)
  local copies, waits for them, and re-layouts  35.8 us (7%)
  matrix products  19.7 us (4%)
  blocking collectives  18.7 us (4%)
  between operations  15.7 us (3%)
    ppermute x51, waiting for transfers between devices, swapped(): return lax.ppermute(array, axis, [(i, i ^ mask) for i in range(size)])  132 us
    ppermute x51, starting transfers between devices, swapped(): return lax.ppermute(array, axis, [(i, i ^ mask) for i in range(size)])  47 us
    all_to_all x7, starting transfers between devices, over_head(): lax.all_to_all(parts, 'head', split_axis=0, concat_axis=0, tiled=True)  25.9 us
    pallas_call x2, Pallas kernels, attend_back_rows(): pl.pallas_call(functools.partial(attend_back_kernel, token_rows), grid=(l...  24.7 us
    all_to_all x7, waiting for transfers between devices, over_head(): lax.all_to_all(parts, 'head', split_axis=0, concat_axis=0, tiled=True)  23.1 us
    all_gather x3, waiting for transfers between devices, along_batch(): return lax.all_gather(piece, 'batch', axis=0, tiled=False)  22.4 us
    all_to_all x1, blocking collectives, over_head(): lax.all_to_all(parts, 'head', split_axis=0, concat_axis=0, tiled=True)  18.7 us
    pallas_call x2, Pallas kernels, dense_grads(): pl.pallas_call(dense_grad_kernel, grid_spec=pltpu.PrefetchScalarGridSpec(...  17.1 us
  transfers between devices with their start and end apart: 65, of which 35 were waited for; matrix products, arithmetic and copies ran while one was open for 14% of the time, Pallas kernels for 22%

profile of v22, /device:TPU:0, one launch (start us, length us, event | category | flops | bytes accessed | tf_op | source)
XLA Modules:
  0.0 507.8 jit_solution(9918137853681193033)
XLA Ops:
  19.3 5.8 %all-to-all-done = bf16[4,40,964]{2,1,0:T(8,128)(2,1)S(1)} async-done(((bf16[4,40,964]{2,1,0:T(8,128)(2,1)}), bf16[4,40,964]{2,1,0:T(8,128)(2,1)S(1)}, u32[]{:S(2)}, u32[]{:S(2)}) %all-to-all-start) | async-done | bytes 308512 | tf_op jit(solution)/shard_map/all_to_all | solution.py:891
  28.4 14.4 %collective-permute-done.2.refs_2_ = bf16[256,1280]{1,0:T(8,128)(2,1)S(1)} collective-permute-done((bf16[256,1280]{1,0:T(8,128)(2,1)S(1)}, bf16[256,1280]{1,0:T(8,128)(2,1)S(1)}, u32[]{:S(2)}, u32[]{:S(2)}) %collective-permute-start.2) | collective-permute-done | bytes 655392 | tf_op jit(solution)/shard_map/ppermute | solution.py:870
  45.1 13.0 %all-gather.7.cloned.1.call-done = bf16[640,964]{1,0:T(8,128)(2,1)} async-done(((bf16[160,964]{1,0:T(8,128)(2,1)}), bf16[640,964]{1,0:T(8,128)(2,1)}) %all-gather.7.cloned.1.call-update) | async-done | bytes 1233936 | tf_op jit(solution)/shard_map/all_gather | solution.py:904
  64.9 6.6 %all-to-all-done.1 = bf16[4,40,960]{2,1,0:T(8,128)(2,1)S(1)} async-done(((bf16[4,40,960]{2,1,0:T(8,128)(2,1)}), bf16[4,40,960]{2,1,0:T(8,128)(2,1)S(1)}, u32[]{:S(2)}, u32[]{:S(2)}) %all-to-all-start.1) | async-done | bytes 307232 | tf_op jit(solution)/shard_map/all_to_all | solution.py:891
  71.7 16.5 %collective-permute-done.5.across_ref = bf16[4,160,964]{2,1,0:T(8,128)(2,1)S(1)} collective-permute-done((bf16[4,160,964]{2,1,0:T(8,128)(2,1)}, bf16[4,160,964]{2,1,0:T(8,128)(2,1)S(1)}, u32[]{:S(2)}, u32[]{:S(2)}) %collective-permute-start.5) | collective-permute-done | bytes 1233952 | tf_op jit(solution)/shard_map/ppermute | solution.py:870
  95.0 4.6 shard_map.169
  100.9 7.7 %shard_map.170 = (bf16[1024,1280]{1,0:T(8,128)(2,1)}, f32[960,1024]{1,0:T(8,128)S(1)}) custom-call(s32[3]{0:T(128)S(1)} %pad_add_fusion.place_ref.core_ref, bf16[256,1280]{1,0:T(8,128)(2,1)} %bitcast.227, bf16[256,1280]{1,0:T(8,128)(2,1)} %copy-done.51, bf16[256,1280]{1,0:T(8,128)(2,1)} %copy-done.50, bf16[256,1280]{1,0:T(8,128)(2,1)} %collective-permute-done.3.refs_3_, ...), custom_call_target="tpu_custom_call" | custom-call | flops 1048576 | bytes 1048576 | tf_op jit(solution)/shard_map/pallas_call | solution.py:733
  108.7 6.7 %shard_map.171 = (bf16[4,4,80,256]{3,2,1,0:T(8,128)(2,1)}, f32[4,1,1024]{2,1,0:T(1,128)S(1)}) custom-call(f32[3,4,80,1024]{3,2,1,0:T(8,128)S(1)} %bitcast.197, f32[80,1]{1,0:T(8,128)S(1)} %copy.60.scale_ref, s32[1024,1]{1,0:T(8,128)S(1)} %copy.61.col_ref, s32[1,1024]{1,0:T(1,128)S(1)} %constant_dynamic-slice_fusion.row_ref), custom_call_target="tpu_custom_call" | custom-call | flops 1048576 | bytes 1048576 | tf_op jit(solution)/shard_map/pallas_call | solution.py:435
  115.4 4.5 collective-permute-done.7.refs_2_
  130.8 5.4 %collective-permute-done.9.refs_4_ = bf16[4,40,1920]{2,1,0:T(8,128)(2,1)} collective-permute-done((bf16[4,40,1920]{2,1,0:T(8,128)(2,1)}, bf16[4,40,1920]{2,1,0:T(8,128)(2,1)}, u32[]{:S(2)}, u32[]{:S(2)}) %collective-permute-start.9) | collective-permute-done | bytes 614432 | tf_op jit(solution)/shard_map/ppermute | solution.py:870
  136.2 7.1 %all-gather.11.cloned.1.call-done = bf16[8,40,3840]{2,1,0:T(8,128)(2,1)} async-done(((bf16[2,40,3840]{2,1,0:T(8,128)(2,1)}), bf16[8,40,3840]{2,1,0:T(8,128)(2,1)}) %all-gather.11.cloned.1.call-update) | async-done | bytes 2457616 | tf_op jit(solution)/shard_map/all_gather | solution.py:904
  149.6 4.5 shard_map.172
  161.9 16.6 %collective-permute-done.16.across_ref = bf16[4,40,3840]{2,1,0:T(8,128)(2,1)S(1)} collective-permute-done((bf16[4,40,3840]{2,1,0:T(8,128)(2,1)S(1)}, bf16[4,40,3840]{2,1,0:T(8,128)(2,1)S(1)}, u32[]{:S(2)}, u32[]{:S(2)}) %collective-permute-start.16) | collective-permute-done | bytes 1228832 | tf_op jit(solution)/shard_map/ppermute | solution.py:870
  181.2 4.7 shard_map.173
  185.9 6.6 %shard_map.174 = (bf16[1024,1280]{1,0:T(8,128)(2,1)}, f32[960,1024]{1,0:T(8,128)S(1)}) custom-call(s32[3]{0:T(128)S(1)} %pad_add_fusion.place_ref.core_ref, bf16[256,1280]{1,0:T(8,128)(2,1)} %multiply_convert_fusion.2.refs_0_, bf16[256,1280]{1,0:T(8,128)(2,1)} %collective-permute-done.17.refs_1_, bf16[256,1280]{1,0:T(8,128)(2,1)} %collective-permute-done.15.refs_2_, ...), custom_call_target="tpu_custom_call" | custom-call | flops 1048576 | bytes 1048576 | tf_op jit(solution)/shard_map/pallas_call | solution.py:733
  192.6 6.1 %shard_map.175 = (bf16[4,4,80,256]{3,2,1,0:T(8,128)(2,1)S(1)}, f32[4,1,1024]{2,1,0:T(1,128)S(1)}) custom-call(f32[3,4,80,1024]{3,2,1,0:T(8,128)S(1)} %bitcast.199, f32[80,1]{1,0:T(8,128)S(1)} %copy.64.scale_ref, s32[1024,1]{1,0:T(8,128)S(1)} %copy.61.col_ref, s32[1,1024]{1,0:T(1,128)S(1)} %constant_dynamic-slice_fusion.row_ref), custom_call_target="tpu_custom_call" | custom-call | flops 1048576 | bytes 1048576 | tf_op jit(solution)/shard_map/pallas_call | solution.py:435
  198.7 8.6 %collective-permute-done.20.refs_2_ = bf16[4,40,3840]{2,1,0:T(8,128)(2,1)S(1)} collective-permute-done((bf16[4,40,3840]{2,1,0:T(8,128)(2,1)S(1)}, bf16[4,40,3840]{2,1,0:T(8,128)(2,1)S(1)}, u32[]{:S(2)}, u32[]{:S(2)}) %collective-permute-start.20) | collective-permute-done | bytes 1228832 | tf_op jit(solution)/shard_map/ppermute | solution.py:870
  211.9 18.7 %all_to_all.40 = bf16[4,320,256]{2,1,0:T(8,128)(2,1)S(1)} all-to-all(bf16[4,320,256]{2,1,0:T(8,128)(2,1)S(1)} %bitcast.215), channel_id=1, replica_groups=mesh['batch'=4,'blk'=2,'head'=4] {'head'}, dimensions={0} | all-to-all | bytes 1310720 | tf_op jit(solution)/shard_map/all_to_all | solution.py:891
  247.3 4.2 all-to-all-start.4
  252.0 8.5 %shard_map.177 = (bf16[2,2,4,40,3840]{4,3,2,1,0:T(8,128)(2,1)}, bf16[2,2,4,40,3840]{4,3,2,1,0:T(8,128)(2,1)}) custom-call(s32[3]{0:T(128)S(1)} %pad_add_fusion.place_ref.core_ref, bf16[1280,256]{1,0:T(8,128)(2,1)} %bitcast.239, bf16[256,1280]{1,0:T(8,128)(2,1)} %copy-done.27, bf16[256,1280]{1,0:T(8,128)(2,1)} %copy-done.48, bf16[256,1280]{1,0:T(8,128)(2,1)} %copy-done.28, ...), custom_call_target="tpu_custom_call" | custom-call | flops 1048576 | bytes 1048576 | tf_op jit(solution)/shard_map/pallas_call | solution.py:599
  262.9 12.4 %shard_map.178 = (bf16[3,4,80,1024]{3,2,1,0:T(8,128)(2,1)}, f32[80,128]{1,0:T(8,128)}) custom-call(f32[3,4,80,1024]{3,2,1,0:T(8,128)} %bitcast.200, bf16[4,4,80,256]{3,2,1,0:T(8,128)(2,1)} %bitcast.56.grad_ref, f32[4,1,1024]{2,1,0:T(1,128)S(1)} %get-tuple-element.155.lse_ref, f32[80,1]{1,0:T(8,128)S(1)} %copy.64.scale_ref, s32[1024,1]{1,0:T(8,128)S(1)} %copy.61.col_ref, ...), custom_call_target="tpu_custom_call" | custom-call | flops 1048576 | bytes 1048576 | tf_op jit(solution)/shard_map/pallas_call | solution.py:528
  281.1 11.2 %shard_map.179 = (f32[2,2,128,1280]{3,2,1,0:T(8,128)}, bf16[2,2,128,1280]{3,2,1,0:T(8,128)(2,1)}, bf16[1280,960]{1,0:T(8,128)(2,1)}) custom-call(s32[3]{0:T(128)S(1)} %pad_add_fusion.place_ref.core_ref, bf16[960,1024]{1,0:T(8,128)(2,1)} %bitcast.241, bf16[1280,960]{1,0:T(8,128)(2,1)} %bitcast.217, bf16[1024,1280]{1,0:T(8,128)(2,1)} %get-tuple-element.162.normed_ref), custom_call_target="tpu_custom_call" | custom-call | flops 1048576 | bytes 1048576 | tf_op jit(solution)/shard_map/pallas_call | solution.py:779
  307.2 13.9 %collective-permute-done.33 = bf16[2,128,1280]{2,1,0:T(8,128)(2,1)} collective-permute-done((bf16[2,128,1280]{2,1,0:T(8,128)(2,1)}, bf16[2,128,1280]{2,1,0:T(8,128)(2,1)}, u32[]{:S(2)}, u32[]{:S(2)}) %collective-permute-start.33) | collective-permute-done | bytes 655392 | tf_op jit(solution)/shard_map/ppermute | solution.py:870
  339.7 8.6 %shard_map.180 = (bf16[2,2,4,40,3840]{4,3,2,1,0:T(8,128)(2,1)}, bf16[2,2,4,40,3840]{4,3,2,1,0:T(8,128)(2,1)}) custom-call(s32[3]{0:T(128)S(1)} %pad_add_fusion.place_ref.core_ref, bf16[1280,256]{1,0:T(8,128)(2,1)} %bitcast.236, bf16[256,1280]{1,0:T(8,128)(2,1)} %copy-done.26, bf16[256,1280]{1,0:T(8,128)(2,1)} %copy-done.44, bf16[256,1280]{1,0:T(8,128)(2,1)} %copy-done.32, ...), custom_call_target="tpu_custom_call" | custom-call | flops 1048576 | bytes 1048576 | tf_op jit(solution)/shard_map/pallas_call | solution.py:599
  350.7 7.8 %all-to-all-done.5 = bf16[4,320,256]{2,1,0:T(8,128)(2,1)} async-done(((bf16[4,320,256]{2,1,0:T(8,128)(2,1)}), bf16[4,320,256]{2,1,0:T(8,128)(2,1)}, u32[]{:S(2)}, u32[]{:S(2)}) %all-to-all-start.5) | async-done | bytes 655392 | tf_op jit(solution)/shard_map/all_to_all | solution.py:891
  363.5 12.3 %shard_map.181 = (bf16[3,4,80,1024]{3,2,1,0:T(8,128)(2,1)}, f32[80,128]{1,0:T(8,128)}) custom-call(f32[3,4,80,1024]{3,2,1,0:T(8,128)} %bitcast.198, bf16[4,4,80,256]{3,2,1,0:T(8,128)(2,1)} %bitcast.68.grad_ref, f32[4,1,1024]{2,1,0:T(1,128)S(1)} %get-tuple-element.185.lse_ref, f32[80,1]{1,0:T(8,128)S(1)} %copy.60.scale_ref, s32[1024,1]{1,0:T(8,128)S(1)} %copy.61.col_ref, ...), custom_call_target="tpu_custom_call" | custom-call | flops 1048576 | bytes 1048576 | tf_op jit(solution)/shard_map/pallas_call | solution.py:528
  376.6 7.3 %shard_map.182 = bf16[1280,960]{1,0:T(8,128)(2,1)} custom-call(bf16[960,1024]{1,0:T(8,128)(2,1)} %bitcast.231, bf16[1024,1280]{1,0:T(8,128)(2,1)} %get-tuple-element.189.normed_ref), custom_call_target="tpu_custom_call" | custom-call | flops 1048576 | bytes 1048576 | tf_op jit(solution)/shard_map/pallas_call | solution.py:850
  384.1 4.9 add_bitcast_fusion
  393.6 8.4 %shard_map.183 = (f32[2,2,128,1280]{3,2,1,0:T(8,128)}, bf16[2,2,128,1280]{3,2,1,0:T(8,128)(2,1)}) custom-call(s32[3]{0:T(128)S(1)} %pad_add_fusion.place_ref.core_ref, bf16[960,1024]{1,0:T(8,128)(2,1)} %bitcast.232, bf16[1280,960]{1,0:T(8,128)(2,1)} %bitcast.224), custom_call_target="tpu_custom_call" | custom-call | flops 1048576 | bytes 1048576 | tf_op jit(solution)/shard_map/pallas_call | solution.py:820
  402.0 4.4 collective-permute-done.38
  428.3 14.2 %collective-permute-done.41 = bf16[4,40,3840]{2,1,0:T(8,128)(2,1)S(1)} collective-permute-done((bf16[4,40,3840]{2,1,0:T(8,128)(2,1)S(1)}, bf16[4,40,3840]{2,1,0:T(8,128)(2,1)S(1)}, u32[]{:S(2)}, u32[]{:S(2)}) %collective-permute-start.41) | collective-permute-done | bytes 1228832 | tf_op jit(solution)/shard_map/ppermute | solution.py:870
  459.1 9.8 %collective-permute-done.46 = bf16[2,128,1280]{2,1,0:T(8,128)(2,1)} collective-permute-done((bf16[2,128,1280]{2,1,0:T(8,128)(2,1)}, bf16[2,128,1280]{2,1,0:T(8,128)(2,1)}, u32[]{:S(2)}, u32[]{:S(2)}) %collective-permute-start.46) | collective-permute-done | bytes 655392 | tf_op jit(solution)/shard_map/ppermute | solution.py:870
  (381 shorter events, 205.9 us)
Async XLA Ops:
  18.4 39.7 %all-gather.7.cloned.1.call-start = ((), (), s32[]{:S(2)}) async-start(), calls=%async_computation.16 | async-start | bytes 1638400 | tf_op jit(solution)/shard_map/all_gather | solution.py:904
  25.8 64.7 %all-gather.9.cloned.1.call-start = ((), (), s32[]{:S(2)}) async-start(), calls=%async_computation.17 | async-start | bytes 1536000 | tf_op jit(solution)/shard_map/all_gather | solution.py:904
  58.1 30.1 %collective-permute-start.5 = (bf16[4,160,964]{2,1,0:T(8,128)(2,1)}, bf16[4,160,964]{2,1,0:T(8,128)(2,1)S(1)}, u32[]{:S(2)}, u32[]{:S(2)}) collective-permute-start(bf16[4,160,964]{2,1,0:T(8,128)(2,1)} %bitcast.247), channel_id=1, source_target_pairs={{0,4},{4,0},{1,5},{5,1},{2,6},{6,2},{3,7},{7,3},{8,12},{12,8},{9,1... | collective-permute-start | bytes 3701768 | tf_op jit(solution)/shard_map/ppermute | solution.py:870
  64.8 78.5 %all-gather.11.cloned.1.call-start = ((), (), s32[]{:S(2)}) async-start(), calls=%async_computation.18 | async-start | bytes 3072000 | tf_op jit(solution)/shard_map/all_gather | solution.py:904
  91.5 28.4 %collective-permute-start.7 = (bf16[4,40,3840]{2,1,0:T(8,128)(2,1)}, bf16[4,40,3840]{2,1,0:T(8,128)(2,1)S(1)}, u32[]{:S(2)}, u32[]{:S(2)}) collective-permute-start(bf16[4,40,3840]{2,1,0:T(8,128)(2,1)} %bitcast.19.refs_0_), channel_id=1, source_target_pairs={{0,2},{1,3},{2,0},{3,1},{4,6},{5,7},{6,4},{7,5},{8,10},{9,11},{10,... | collective-permute-start | bytes 3686408 | tf_op jit(solution)/shard_map/ppermute | solution.py:870
  93.0 28.2 %collective-permute-start.6 = (bf16[4,40,3840]{2,1,0:T(8,128)(2,1)}, bf16[4,40,3840]{2,1,0:T(8,128)(2,1)}, u32[]{:S(2)}, u32[]{:S(2)}) collective-permute-start(bf16[4,40,3840]{2,1,0:T(8,128)(2,1)} %bitcast.19.refs_0_), channel_id=1, source_target_pairs={{0,4},{4,0},{1,5},{5,1},{2,6},{6,2},{3,7},{7,3},{8,12},{12,8},{9,1... | collective-permute-start | bytes 3686408 | tf_op jit(solution)/shard_map/ppermute | solution.py:870
  125.5 20.7 %collective-permute-start.8 = (bf16[4,40,1920]{2,1,0:T(8,128)(2,1)}, bf16[4,40,1920]{2,1,0:T(8,128)(2,1)}, u32[]{:S(2)}, u32[]{:S(2)}) collective-permute-start(bf16[4,40,1920]{2,1,0:T(8,128)(2,1)} %slice.153), channel_id=1, source_target_pairs={{0,2},{1,3},{2,0},{3,1},{4,6},{5,7},{6,4},{7,5},{8,10},{9,11},{10,... | collective-permute-start | bytes 1843208 | tf_op jit(solution)/shard_map/ppermute | solution.py:870
  126.0 20.2 %all-to-all-start.2 = ((bf16[4,320,256]{2,1,0:T(8,128)(2,1)}), bf16[4,320,256]{2,1,0:T(8,128)(2,1)S(1)}, u32[]{:S(2)}, u32[]{:S(2)}) async-start(bf16[4,320,256]{2,1,0:T(8,128)(2,1)} %bitcast.31), calls=%async_computation.2 | async-start | bytes 1310720 | tf_op jit(solution)/shard_map/all_to_all | solution.py:891
  129.7 19.2 %collective-permute-start.10 = (bf16[4,40,3840]{2,1,0:T(8,128)(2,1)}, bf16[4,40,3840]{2,1,0:T(8,128)(2,1)}, u32[]{:S(2)}, u32[]{:S(2)}) collective-permute-start(bf16[4,40,3840]{2,1,0:T(8,128)(2,1)} %bitcast.19.refs_0_), channel_id=1, source_target_pairs={{0,1},{1,0},{2,3},{3,2},{4,5},{5,4},{6,7},{7,6},{8,9},{9,8},{10,11... | collective-permute-start | bytes 3686408 | tf_op jit(solution)/shard_map/ppermute | solution.py:870
  130.3 19.3 %collective-permute-start.11 = (bf16[4,40,3840]{2,1,0:T(8,128)(2,1)}, bf16[4,40,3840]{2,1,0:T(8,128)(2,1)}, u32[]{:S(2)}, u32[]{:S(2)}) collective-permute-start(bf16[4,40,3840]{2,1,0:T(8,128)(2,1)} %collective-permute-done.6.refs_1_), channel_id=1, source_target_pairs={{0,1},{1,0},{2,3},{3,2},{4,5},{5,4},{6,7},{7,6},{8,9},{9,8},{10,11... | collective-permute-start | bytes 3686408 | tf_op jit(solution)/shard_map/ppermute | solution.py:870
  130.4 19.2 %collective-permute-start.12 = (bf16[4,40,3840]{2,1,0:T(8,128)(2,1)S(1)}, bf16[4,40,3840]{2,1,0:T(8,128)(2,1)}, u32[]{:S(2)}, u32[]{:S(2)}) collective-permute-start(bf16[4,40,3840]{2,1,0:T(8,128)(2,1)S(1)} %collective-permute-done.7.refs_2_), channel_id=1, source_target_pairs={{0,1},{1,0},{2,3},{3,2},{4,5},{5,4},{6,7},{7,6},{8,9},{9,8},{10,11... | collective-permute-start | bytes 3686408 | tf_op jit(solution)/shard_map/ppermute | solution.py:870
  149.0 29.5 %collective-permute-start.16 = (bf16[4,40,3840]{2,1,0:T(8,128)(2,1)S(1)}, bf16[4,40,3840]{2,1,0:T(8,128)(2,1)S(1)}, u32[]{:S(2)}, u32[]{:S(2)}) collective-permute-start(bf16[4,40,3840]{2,1,0:T(8,128)(2,1)S(1)} %get-tuple-element.247.along_ref), channel_id=1, source_target_pairs={{0,4},{4,0},{1,5},{5,1},{2,6},{6,2},{3,7},{7,3},{8,12},{12,8},{9,1... | collective-permute-start | bytes 3686408 | tf_op jit(solution)/shard_map/ppermute | solution.py:870
  178.5 28.7 %collective-permute-start.20 = (bf16[4,40,3840]{2,1,0:T(8,128)(2,1)S(1)}, bf16[4,40,3840]{2,1,0:T(8,128)(2,1)S(1)}, u32[]{:S(2)}, u32[]{:S(2)}) collective-permute-start(bf16[4,40,3840]{2,1,0:T(8,128)(2,1)S(1)} %get-tuple-element.140.refs_0_), channel_id=1, source_target_pairs={{0,2},{1,3},{2,0},{3,1},{4,6},{5,7},{6,4},{7,5},{8,10},{9,11},{10,... | collective-permute-start | bytes 3686408 | tf_op jit(solution)/shard_map/ppermute | solution.py:870
  179.1 28.5 %collective-permute-start.19 = (bf16[4,40,3840]{2,1,0:T(8,128)(2,1)S(1)}, bf16[4,40,3840]{2,1,0:T(8,128)(2,1)}, u32[]{:S(2)}, u32[]{:S(2)}) collective-permute-start(bf16[4,40,3840]{2,1,0:T(8,128)(2,1)S(1)} %get-tuple-element.140.refs_0_), channel_id=1, source_target_pairs={{0,4},{4,0},{1,5},{5,1},{2,6},{6,2},{3,7},{7,3},{8,12},{12,8},{9,1... | collective-permute-start | bytes 3686408 | tf_op jit(solution)/shard_map/ppermute | solution.py:870
  208.8 21.9 %collective-permute-start.22 = (bf16[4,40,1920]{2,1,0:T(8,128)(2,1)S(1)}, bf16[4,40,1920]{2,1,0:T(8,128)(2,1)S(1)}, u32[]{:S(2)}, u32[]{:S(2)}) collective-permute-start(bf16[4,40,1920]{2,1,0:T(8,128)(2,1)S(1)} %slice.167), channel_id=1, source_target_pairs={{0,4},{4,0},{1,5},{5,1},{2,6},{6,2},{3,7},{7,3},{8,12},{12,8},{9,1... | collective-permute-start | bytes 1843208 | tf_op jit(solution)/shard_map/ppermute | solution.py:870
  209.9 20.7 %collective-permute-start.21 = (bf16[4,40,1920]{2,1,0:T(8,128)(2,1)S(1)}, bf16[4,40,1920]{2,1,0:T(8,128)(2,1)S(1)}, u32[]{:S(2)}, u32[]{:S(2)}) collective-permute-start(bf16[4,40,1920]{2,1,0:T(8,128)(2,1)S(1)} %slice.166), channel_id=1, source_target_pairs={{0,2},{1,3},{2,0},{3,1},{4,6},{5,7},{6,4},{7,5},{8,10},{9,11},{10,... | collective-permute-start | bytes 1843208 | tf_op jit(solution)/shard_map/ppermute | solution.py:870
  211.4 19.9 %collective-permute-start.23 = (bf16[4,40,3840]{2,1,0:T(8,128)(2,1)S(1)}, bf16[4,40,3840]{2,1,0:T(8,128)(2,1)S(1)}, u32[]{:S(2)}, u32[]{:S(2)}) collective-permute-start(bf16[4,40,3840]{2,1,0:T(8,128)(2,1)S(1)} %get-tuple-element.140.refs_0_), channel_id=1, source_target_pairs={{0,1},{1,0},{2,3},{3,2},{4,5},{5,4},{6,7},{7,6},{8,9},{9,8},{10,11... | collective-permute-start | bytes 3686408 | tf_op jit(solution)/shard_map/ppermute | solution.py:870
  211.4 22.3 %collective-permute-start.24 = (bf16[4,40,3840]{2,1,0:T(8,128)(2,1)}, bf16[4,40,3840]{2,1,0:T(8,128)(2,1)S(1)}, u32[]{:S(2)}, u32[]{:S(2)}) collective-permute-start(bf16[4,40,3840]{2,1,0:T(8,128)(2,1)} %collective-permute-done.19.refs_1_), channel_id=1, source_target_pairs={{0,1},{1,0},{2,3},{3,2},{4,5},{5,4},{6,7},{7,6},{8,9},{9,8},{10,11... | collective-permute-start | bytes 3686408 | tf_op jit(solution)/shard_map/ppermute | solution.py:870
  211.9 21.8 %collective-permute-start.25 = (bf16[4,40,3840]{2,1,0:T(8,128)(2,1)S(1)}, bf16[4,40,3840]{2,1,0:T(8,128)(2,1)S(1)}, u32[]{:S(2)}, u32[]{:S(2)}) collective-permute-start(bf16[4,40,3840]{2,1,0:T(8,128)(2,1)S(1)} %collective-permute-done.20.refs_2_), channel_id=1, source_target_pairs={{0,1},{1,0},{2,3},{3,2},{4,5},{5,4},{6,7},{7,6},{8,9},{9,8},{10,11... | collective-permute-start | bytes 3686408 | tf_op jit(solution)/shard_map/ppermute | solution.py:870
  241.1 19.4 %collective-permute-start.28 = (bf16[128,1280]{1,0:T(8,128)(2,1)}, bf16[128,1280]{1,0:T(8,128)(2,1)}, u32[]{:S(2)}, u32[]{:S(2)}) collective-permute-start(bf16[128,1280]{1,0:T(8,128)(2,1)} %dynamic-slice_bitcast_fusion.3), channel_id=1, source_target_pairs={{0,4},{4,0},{1,5},{5,1},{2,6},{6,2},{3,7},{7,3},{8,12},{12,8},{9,1... | collective-permute-start | bytes 983048 | tf_op jit(solution)/shard_map/ppermute | solution.py:870
  251.4 107.0 %reduce-scatter.5.cloned.1.call-start = ((), (), s32[]{:S(2)}) async-start(), calls=%async_computation.12 | async-start | bytes 3276800 | tf_op jit(solution)/shard_map/reduce_scatter | solution.py:920
  305.9 42.4 %collective-permute-start.34 = (bf16[4,40,3840]{2,1,0:T(8,128)(2,1)}, bf16[4,40,3840]{2,1,0:T(8,128)(2,1)}, u32[]{:S(2)}, u32[]{:S(2)}) collective-permute-start(bf16[4,40,3840]{2,1,0:T(8,128)(2,1)} %pad_maximum_fusion), channel_id=1, source_target_pairs={{0,4},{4,0},{1,5},{5,1},{2,6},{6,2},{3,7},{7,3},{8,12},{12,8},{9,1... | collective-permute-start | bytes 3686408 | tf_op jit(solution)/shard_map/ppermute | solution.py:870
  322.8 35.6 %collective-permute-start.35 = (bf16[4,40,3840]{2,1,0:T(8,128)(2,1)}, bf16[4,40,3840]{2,1,0:T(8,128)(2,1)}, u32[]{:S(2)}, u32[]{:S(2)}) collective-permute-start(bf16[4,40,3840]{2,1,0:T(8,128)(2,1)} %pad_maximum_fusion.1), channel_id=1, source_target_pairs={{0,2},{1,3},{2,0},{3,1},{4,6},{5,7},{6,4},{7,5},{8,10},{9,11},{10,... | collective-permute-start | bytes 3686408 | tf_op jit(solution)/shard_map/ppermute | solution.py:870
  335.5 23.0 %all-to-all-start.5 = ((bf16[4,320,256]{2,1,0:T(8,128)(2,1)}), bf16[4,320,256]{2,1,0:T(8,128)(2,1)}, u32[]{:S(2)}, u32[]{:S(2)}) async-start(bf16[4,320,256]{2,1,0:T(8,128)(2,1)} %bitcast.64), calls=%async_computation.5 | async-start | bytes 1310720 | tf_op jit(solution)/shard_map/all_to_all | solution.py:891
  339.7 62.3 %reduce-scatter.7.cloned.1.call-start = ((), (), s32[]{:S(2)}) async-start(), calls=%async_computation.13 | async-start | bytes 1536000 | tf_op jit(solution)/shard_map/reduce_scatter | solution.py:920
  358.5 25.5 %collective-permute-start.37 = (bf16[2,2,4,40,3840]{4,3,2,1,0:T(8,128)(2,1)}, bf16[2,2,4,40,3840]{4,3,2,1,0:T(8,128)(2,1)}, u32[]{:S(2)}, u32[]{:S(2)}) collective-permute-start(bf16[2,2,4,40,3840]{4,3,2,1,0:T(8,128)(2,1)} %get-tuple-element.190), channel_id=1, source_target_pairs={{0,1},{1,0},{2,3},{3,2},{4,5},{5,4},{6,7},{7,6},{8,9},{9,8},{10,11... | collective-permute-start | bytes 14745608 | tf_op jit(solution)/shard_map/ppermute | solution.py:870
  361.1 84.4 %reduce-scatter.9.cloned.1.call-start = ((), (), s32[]{:S(2)}) async-start(), calls=%async_computation.14 | async-start | bytes 3276800 | tf_op jit(solution)/shard_map/reduce_scatter | solution.py:920
  384.0 99.7 %reduce-scatter.11.cloned.1.call-start = ((), (), s32[]{:S(2)}) async-start(), calls=%async_computation.15 | async-start | bytes 1536000 | tf_op jit(solution)/shard_map/reduce_scatter | solution.py:920
  413.1 29.5 %collective-permute-start.41 = (bf16[4,40,3840]{2,1,0:T(8,128)(2,1)S(1)}, bf16[4,40,3840]{2,1,0:T(8,128)(2,1)S(1)}, u32[]{:S(2)}, u32[]{:S(2)}) collective-permute-start(bf16[4,40,3840]{2,1,0:T(8,128)(2,1)S(1)} %pad_maximum_fusion.2), channel_id=1, source_target_pairs={{0,4},{4,0},{1,5},{5,1},{2,6},{6,2},{3,7},{7,3},{8,12},{12,8},{9,1... | collective-permute-start | bytes 3686408 | tf_op jit(solution)/shard_map/ppermute | solution.py:870
  414.4 29.3 %collective-permute-start.42 = (bf16[4,40,3840]{2,1,0:T(8,128)(2,1)S(1)}, bf16[4,40,3840]{2,1,0:T(8,128)(2,1)}, u32[]{:S(2)}, u32[]{:S(2)}) collective-permute-start(bf16[4,40,3840]{2,1,0:T(8,128)(2,1)S(1)} %pad_maximum_fusion.3), channel_id=1, source_target_pairs={{0,2},{1,3},{2,0},{3,1},{4,6},{5,7},{6,4},{7,5},{8,10},{9,11},{10,... | collective-permute-start | bytes 3686408 | tf_op jit(solution)/shard_map/ppermute | solution.py:870
  454.1 20.8 %collective-permute-start.48 = (bf16[160,960]{1,0:T(8,128)(2,1)}, bf16[160,960]{1,0:T(8,128)(2,1)}, u32[]{:S(2)}, u32[]{:S(2)}) collective-permute-start(bf16[160,960]{1,0:T(8,128)(2,1)} %dynamic-slice_bitcast_fusion), channel_id=1, source_target_pairs={{0,4},{4,0},{1,5},{5,1},{2,6},{6,2},{3,7},{7,3},{8,12},{12,8},{9,1... | collective-permute-start | bytes 921608 | tf_op jit(solution)/shard_map/ppermute | solution.py:870
  455.6 18.6 %all-to-all-start.7 = ((bf16[4,40,960]{2,1,0:T(8,128)(2,1)}), bf16[4,40,960]{2,1,0:T(8,128)(2,1)S(1)}, u32[]{:S(2)}, u32[]{:S(2)}) async-start(bf16[4,40,960]{2,1,0:T(8,128)(2,1)} %bitcast.92), calls=%async_computation.11 | async-start | bytes 655360 | tf_op jit(solution)/shard_map/all_to_all | solution.py:891
  (101 other events, 791.3 us)
Sparse Core Ops, SparseCore 0:
  26.0 32.0 all-gather.6
  60.2 30.2 all-gather.8
  92.1 51.1 all-gather.10
  306.0 51.7 reduce-scatter.4
  361.2 31.0 reduce-scatter.6
  394.5 50.9 reduce-scatter.8
  455.8 27.9 reduce-scatter.10

commit v23 on v22

--- a/solution.py
+++ b/solution.py
@@ -361,6 +361,7 @@
 Q_ROWS = 256
 KERNEL = pltpu.CompilerParams(vmem_limit_bytes=32 * 1024 * 1024)
 LIGHT = pl.CostEstimate(flops=1 << 20, bytes_accessed=1 << 20, transcendentals=0)
+HEAVY = pl.CostEstimate(flops=10**11, bytes_accessed=3 * 10**8, transcendentals=0)
 
 
 def in_hbm(*arrays):
@@ -611,6 +612,19 @@
     )(place(), *in_hbm(attended_t, normed, active, out_bar, up_bar, down_bar))
 
 
+def widen_kernel(in_ref, out_ref):
+    out_ref[...] = in_ref[...].astype(F32)
+
+
+def widened(rows):
+    return pl.pallas_call(
+        widen_kernel,
+        out_shape=jax.ShapeDtypeStruct(rows.shape, F32),
+        compiler_params=KERNEL,
+        cost_estimate=HEAVY,
+    )(rows)
+
+
 def place():
     head = lax.axis_index("head")
     return jnp.stack([lax.axis_index("blk"), head // 2, head % 2]).astype(jnp.int32)
@@ -1119,18 +1133,23 @@
             bars, rows = tied(bars, diagonal_rows(cored))
             diagonal = sent_beside_and_across(*rows)
             halves, to_core = rows_back(bars, qkv, token_rows)
-            halves, to_core, diagonal, summed = tied(halves, to_core, diagonal, summed)
-            halves, to_core, rows = tied(halves, to_core, neighbour_rows(cored, *diagonal))
+            scale_sum = sum_over(jnp.stack(scale_grads), ("head", 1))
+            halves, to_core, diagonal, summed, scale_sum = tied(
+                halves, to_core, diagonal, summed, scale_sum
+            )
+            halves, to_core, rows, scale_sum = tied(
+                halves, to_core, neighbour_rows(cored, *diagonal), scale_sum
+            )
             sent = sent_beside_and_across(*rows)
             halves = halves + other_core(to_core).astype(F32)
-            scale_sum = sum_over(jnp.stack(scale_grads), ("head", 1), ("batch", 1), ("batch", 2))
+            scale_sum = sum_over(scale_sum, ("batch", 1), ("batch", 2))
             own = own_quarter(cored)
             halves, sent, z_sum, scale_sum, own = tied(halves, sent, z_sum, scale_sum, own)
             halves, own, earlier = tied(halves, own_sum(own, *sent), earlier)
             moved = over_head(earlier.reshape(4, -1, earlier.shape[-1]))
-            dense_first = over_batch(own)
+            dense_first = widened(over_batch(own))
             normed_grad = scatter_row(halves)
-            z_across, scale_sum, dense_first = tied(across_sum(z_sum), scale_sum, dense_first)
+            z_across = across_sum(z_sum)
             z_across = over_head(z_across.reshape(4, -1, z_across.shape[-1]))
             dense_grad = [dense_first, summed]
             qkv_grads = [columns_to_rows(z_across), columns_to_rows(moved)]

time: 516 us -> 520 us (level)
  local copies, waits for them, and re-layouts: 35.8 us -> 42.7 us
    all_to_all x7, waiting for transfers between devices: 23.1 us -> 34 us  [over_head(): lax.all_to_all(parts, 'head', split_axis=0, concat_axis=0, tiled=True)]
    ppermute x51, waiting for transfers between devices: 132 us -> 123 us  [swapped(): return lax.ppermute(array, axis, [(i, i ^ mask) for i in range(size)])]
    convert_element_type x6, local copies, waits for them, and re-layouts: 1.47 us -> 9.08 us  [columns_to_rows(): moved.reshape(4, rows, 3, -1).transpose(1, 2, 0, 3).reshape(rows, -1)]
    unnamed x136 -> x138, local copies, waits for them, and re-layouts: 11.5 us -> 14 us
  transfers between devices with their start and end apart: 65 -> 65, of which waited for: 35 -> 33; matrix products, arithmetic and copies ran while one was open for 14% -> 16% of each run, Pallas kernels for 22% -> 21%
where the time goes in v23:
time: 520 us; the launch traced here: 512 us
  waiting for transfers between devices  182 us (35%)
  Pallas kernels  113 us (22%)
  starting transfers between devices  72.7 us (14%)
  other arithmetic  47.7 us (9%)
  local copies, waits for them, and re-layouts  42.7 us (8%)
  matrix products  19.7 us (4%)
  blocking collectives  18.7 us (4%)
  between operations  15.9 us (3%)
    ppermute x51, waiting for transfers between devices, swapped(): return lax.ppermute(array, axis, [(i, i ^ mask) for i in range(size)])  123 us
    ppermute x51, starting transfers between devices, swapped(): return lax.ppermute(array, axis, [(i, i ^ mask) for i in range(size)])  45.5 us
    all_to_all x7, waiting for transfers between devices, over_head(): lax.all_to_all(parts, 'head', split_axis=0, concat_axis=0, tiled=True)  34 us
    all_to_all x7, starting transfers between devices, over_head(): lax.all_to_all(parts, 'head', split_axis=0, concat_axis=0, tiled=True)  26.7 us
    pallas_call x2, Pallas kernels, attend_back_rows(): pl.pallas_call(functools.partial(attend_back_kernel, token_rows), grid=(l...  24.9 us
    all_gather x3, waiting for transfers between devices, along_batch(): return lax.all_gather(piece, 'batch', axis=0, tiled=False)  22.1 us
    all_to_all x1, blocking collectives, over_head(): lax.all_to_all(parts, 'head', split_axis=0, concat_axis=0, tiled=True)  18.7 us
    pallas_call x2, Pallas kernels, dense_grads(): pl.pallas_call(dense_grad_kernel, grid_spec=pltpu.PrefetchScalarGridSpec(...  17 us
  transfers between devices with their start and end apart: 65, of which 33 were waited for; matrix products, arithmetic and copies ran while one was open for 16% of the time, Pallas kernels for 21%

profile of v23, /device:TPU:0, one launch (start us, length us, event | category | flops | bytes accessed | tf_op | source)
XLA Modules:
  0.0 512.2 jit_solution(8271142205585982103)
XLA Ops:
  19.1 6.0 %all-to-all-done = bf16[4,40,964]{2,1,0:T(8,128)(2,1)S(1)} async-done(((bf16[4,40,964]{2,1,0:T(8,128)(2,1)}), bf16[4,40,964]{2,1,0:T(8,128)(2,1)S(1)}, u32[]{:S(2)}, u32[]{:S(2)}) %all-to-all-start) | async-done | bytes 308512 | tf_op jit(solution)/shard_map/all_to_all | solution.py:905
  27.2 15.1 %collective-permute-done.2.refs_2_ = bf16[256,1280]{1,0:T(8,128)(2,1)S(1)} collective-permute-done((bf16[256,1280]{1,0:T(8,128)(2,1)S(1)}, bf16[256,1280]{1,0:T(8,128)(2,1)S(1)}, u32[]{:S(2)}, u32[]{:S(2)}) %collective-permute-start.2) | collective-permute-done | bytes 655392 | tf_op jit(solution)/shard_map/ppermute | solution.py:884
  45.3 12.7 %all-gather.7.cloned.1.call-done = bf16[640,964]{1,0:T(8,128)(2,1)} async-done(((bf16[160,964]{1,0:T(8,128)(2,1)}), bf16[640,964]{1,0:T(8,128)(2,1)}) %all-gather.7.cloned.1.call-update) | async-done | bytes 1233936 | tf_op jit(solution)/shard_map/all_gather | solution.py:918
  64.8 6.6 %all-to-all-done.1 = bf16[4,40,960]{2,1,0:T(8,128)(2,1)S(1)} async-done(((bf16[4,40,960]{2,1,0:T(8,128)(2,1)}), bf16[4,40,960]{2,1,0:T(8,128)(2,1)S(1)}, u32[]{:S(2)}, u32[]{:S(2)}) %all-to-all-start.1) | async-done | bytes 307232 | tf_op jit(solution)/shard_map/all_to_all | solution.py:905
  71.7 16.5 %collective-permute-done.5.across_ref = bf16[4,160,964]{2,1,0:T(8,128)(2,1)S(1)} collective-permute-done((bf16[4,160,964]{2,1,0:T(8,128)(2,1)}, bf16[4,160,964]{2,1,0:T(8,128)(2,1)S(1)}, u32[]{:S(2)}, u32[]{:S(2)}) %collective-permute-start.5) | collective-permute-done | bytes 1233952 | tf_op jit(solution)/shard_map/ppermute | solution.py:884
  94.9 4.6 shard_map.169
  101.5 7.7 %shard_map.170 = (bf16[1024,1280]{1,0:T(8,128)(2,1)}, f32[960,1024]{1,0:T(8,128)S(1)}) custom-call(s32[3]{0:T(128)S(1)} %pad_add_fusion.place_ref.core_ref, bf16[256,1280]{1,0:T(8,128)(2,1)} %bitcast.231, bf16[256,1280]{1,0:T(8,128)(2,1)} %copy-done.53, bf16[256,1280]{1,0:T(8,128)(2,1)} %copy-done.52, bf16[256,1280]{1,0:T(8,128)(2,1)} %collective-permute-done.3.refs_3_, ...), custom_call_target="tpu_custom_call" | custom-call | flops 1048576 | bytes 1048576 | tf_op jit(solution)/shard_map/pallas_call | solution.py:747
  109.2 6.7 %shard_map.171 = (bf16[4,4,80,256]{3,2,1,0:T(8,128)(2,1)}, f32[4,1,1024]{2,1,0:T(1,128)S(1)}) custom-call(f32[3,4,80,1024]{3,2,1,0:T(8,128)S(1)} %bitcast.199, f32[80,1]{1,0:T(8,128)S(1)} %copy.60.scale_ref, s32[1024,1]{1,0:T(8,128)S(1)} %copy.61.col_ref, s32[1,1024]{1,0:T(1,128)S(1)} %constant_dynamic-slice_fusion.row_ref), custom_call_target="tpu_custom_call" | custom-call | flops 1048576 | bytes 1048576 | tf_op jit(solution)/shard_map/pallas_call | solution.py:436
  130.9 5.3 %collective-permute-done.9.refs_4_ = bf16[4,40,1920]{2,1,0:T(8,128)(2,1)} collective-permute-done((bf16[4,40,1920]{2,1,0:T(8,128)(2,1)}, bf16[4,40,1920]{2,1,0:T(8,128)(2,1)}, u32[]{:S(2)}, u32[]{:S(2)}) %collective-permute-start.9) | collective-permute-done | bytes 614432 | tf_op jit(solution)/shard_map/ppermute | solution.py:884
  136.2 7.1 %all-gather.11.cloned.1.call-done = bf16[8,40,3840]{2,1,0:T(8,128)(2,1)} async-done(((bf16[2,40,3840]{2,1,0:T(8,128)(2,1)}), bf16[8,40,3840]{2,1,0:T(8,128)(2,1)}) %all-gather.11.cloned.1.call-update) | async-done | bytes 2457616 | tf_op jit(solution)/shard_map/all_gather | solution.py:918
  149.6 4.5 shard_map.172
  161.9 16.6 %collective-permute-done.16.across_ref = bf16[4,40,3840]{2,1,0:T(8,128)(2,1)S(1)} collective-permute-done((bf16[4,40,3840]{2,1,0:T(8,128)(2,1)S(1)}, bf16[4,40,3840]{2,1,0:T(8,128)(2,1)S(1)}, u32[]{:S(2)}, u32[]{:S(2)}) %collective-permute-start.16) | collective-permute-done | bytes 1228832 | tf_op jit(solution)/shard_map/ppermute | solution.py:884
  181.1 4.8 shard_map.173
  185.9 6.6 %shard_map.174 = (bf16[1024,1280]{1,0:T(8,128)(2,1)}, f32[960,1024]{1,0:T(8,128)S(1)}) custom-call(s32[3]{0:T(128)S(1)} %pad_add_fusion.place_ref.core_ref, bf16[256,1280]{1,0:T(8,128)(2,1)} %multiply_convert_fusion.2.refs_0_, bf16[256,1280]{1,0:T(8,128)(2,1)} %collective-permute-done.17.refs_1_, bf16[256,1280]{1,0:T(8,128)(2,1)} %collective-permute-done.15.refs_2_, ...), custom_call_target="tpu_custom_call" | custom-call | flops 1048576 | bytes 1048576 | tf_op jit(solution)/shard_map/pallas_call | solution.py:747
  192.6 6.1 %shard_map.175 = (bf16[4,4,80,256]{3,2,1,0:T(8,128)(2,1)S(1)}, f32[4,1,1024]{2,1,0:T(1,128)S(1)}) custom-call(f32[3,4,80,1024]{3,2,1,0:T(8,128)S(1)} %bitcast.201, f32[80,1]{1,0:T(8,128)S(1)} %copy.64.scale_ref, s32[1024,1]{1,0:T(8,128)S(1)} %copy.61.col_ref, s32[1,1024]{1,0:T(1,128)S(1)} %constant_dynamic-slice_fusion.row_ref), custom_call_target="tpu_custom_call" | custom-call | flops 1048576 | bytes 1048576 | tf_op jit(solution)/shard_map/pallas_call | solution.py:436
  198.7 8.6 %collective-permute-done.20.refs_2_ = bf16[4,40,3840]{2,1,0:T(8,128)(2,1)S(1)} collective-permute-done((bf16[4,40,3840]{2,1,0:T(8,128)(2,1)S(1)}, bf16[4,40,3840]{2,1,0:T(8,128)(2,1)S(1)}, u32[]{:S(2)}, u32[]{:S(2)}) %collective-permute-start.20) | collective-permute-done | bytes 1228832 | tf_op jit(solution)/shard_map/ppermute | solution.py:884
  211.9 18.7 %all_to_all.40 = bf16[4,320,256]{2,1,0:T(8,128)(2,1)S(1)} all-to-all(bf16[4,320,256]{2,1,0:T(8,128)(2,1)S(1)} %bitcast.217), channel_id=1, replica_groups=mesh['batch'=4,'blk'=2,'head'=4] {'head'}, dimensions={0} | all-to-all | bytes 1310720 | tf_op jit(solution)/shard_map/all_to_all | solution.py:905
  248.1 4.2 all-to-all-start.4
  252.5 8.5 %shard_map.177 = (bf16[2,2,4,40,3840]{4,3,2,1,0:T(8,128)(2,1)}, bf16[2,2,4,40,3840]{4,3,2,1,0:T(8,128)(2,1)}) custom-call(s32[3]{0:T(128)S(1)} %pad_add_fusion.place_ref.core_ref, bf16[1280,256]{1,0:T(8,128)(2,1)} %bitcast.243, bf16[256,1280]{1,0:T(8,128)(2,1)} %copy-done.28, bf16[256,1280]{1,0:T(8,128)(2,1)} %copy-done.50, bf16[256,1280]{1,0:T(8,128)(2,1)} %copy-done.29, ...), custom_call_target="tpu_custom_call" | custom-call | flops 1048576 | bytes 1048576 | tf_op jit(solution)/shard_map/pallas_call | solution.py:600
  263.4 12.4 %shard_map.178 = (bf16[3,4,80,1024]{3,2,1,0:T(8,128)(2,1)}, f32[80,128]{1,0:T(8,128)}) custom-call(f32[3,4,80,1024]{3,2,1,0:T(8,128)} %bitcast.202, bf16[4,4,80,256]{3,2,1,0:T(8,128)(2,1)} %bitcast.56.grad_ref, f32[4,1,1024]{2,1,0:T(1,128)S(1)} %get-tuple-element.154.lse_ref, f32[80,1]{1,0:T(8,128)S(1)} %copy.64.scale_ref, s32[1024,1]{1,0:T(8,128)S(1)} %copy.61.col_ref, ...), custom_call_target="tpu_custom_call" | custom-call | flops 1048576 | bytes 1048576 | tf_op jit(solution)/shard_map/pallas_call | solution.py:529
  281.5 11.3 %shard_map.179 = (f32[2,2,128,1280]{3,2,1,0:T(8,128)}, bf16[2,2,128,1280]{3,2,1,0:T(8,128)(2,1)}, bf16[1280,960]{1,0:T(8,128)(2,1)}) custom-call(s32[3]{0:T(128)S(1)} %pad_add_fusion.place_ref.core_ref, bf16[960,1024]{1,0:T(8,128)(2,1)} %bitcast.245, bf16[1280,960]{1,0:T(8,128)(2,1)} %bitcast.221, bf16[1024,1280]{1,0:T(8,128)(2,1)} %get-tuple-element.161.normed_ref), custom_call_target="tpu_custom_call" | custom-call | flops 1048576 | bytes 1048576 | tf_op jit(solution)/shard_map/pallas_call | solution.py:793
  307.8 13.8 %collective-permute-done.33 = bf16[2,128,1280]{2,1,0:T(8,128)(2,1)} collective-permute-done((bf16[2,128,1280]{2,1,0:T(8,128)(2,1)}, bf16[2,128,1280]{2,1,0:T(8,128)(2,1)}, u32[]{:S(2)}, u32[]{:S(2)}) %collective-permute-start.33) | collective-permute-done | bytes 655392 | tf_op jit(solution)/shard_map/ppermute | solution.py:884
  335.9 4.2 all-to-all-start.5
  340.1 8.5 %shard_map.180 = (bf16[2,2,4,40,3840]{4,3,2,1,0:T(8,128)(2,1)}, bf16[2,2,4,40,3840]{4,3,2,1,0:T(8,128)(2,1)}) custom-call(s32[3]{0:T(128)S(1)} %pad_add_fusion.place_ref.core_ref, bf16[1280,256]{1,0:T(8,128)(2,1)} %bitcast.240, bf16[256,1280]{1,0:T(8,128)(2,1)} %copy-done.27, bf16[256,1280]{1,0:T(8,128)(2,1)} %copy-done.46, bf16[256,1280]{1,0:T(8,128)(2,1)} %copy-done.33, ...), custom_call_target="tpu_custom_call" | custom-call | flops 1048576 | bytes 1048576 | tf_op jit(solution)/shard_map/pallas_call | solution.py:600
  351.1 7.8 %all-to-all-done.5 = bf16[4,320,256]{2,1,0:T(8,128)(2,1)} async-done(((bf16[4,320,256]{2,1,0:T(8,128)(2,1)}), bf16[4,320,256]{2,1,0:T(8,128)(2,1)}, u32[]{:S(2)}, u32[]{:S(2)}) %all-to-all-start.5) | async-done | bytes 655392 | tf_op jit(solution)/shard_map/all_to_all | solution.py:905
  364.1 12.5 %shard_map.181 = (bf16[3,4,80,1024]{3,2,1,0:T(8,128)(2,1)}, f32[80,128]{1,0:T(8,128)}) custom-call(f32[3,4,80,1024]{3,2,1,0:T(8,128)} %bitcast.200, bf16[4,4,80,256]{3,2,1,0:T(8,128)(2,1)} %bitcast.68.grad_ref, f32[4,1,1024]{2,1,0:T(1,128)S(1)} %get-tuple-element.184.lse_ref, f32[80,1]{1,0:T(8,128)S(1)} %copy.60.scale_ref, s32[1024,1]{1,0:T(8,128)S(1)} %copy.61.col_ref, ...), custom_call_target="tpu_custom_call" | custom-call | flops 1048576 | bytes 1048576 | tf_op jit(solution)/shard_map/pallas_call | solution.py:529
  377.4 7.3 %shard_map.182 = bf16[1280,960]{1,0:T(8,128)(2,1)} custom-call(bf16[960,1024]{1,0:T(8,128)(2,1)} %bitcast.235, bf16[1024,1280]{1,0:T(8,128)(2,1)} %get-tuple-element.188.normed_ref), custom_call_target="tpu_custom_call" | custom-call | flops 1048576 | bytes 1048576 | tf_op jit(solution)/shard_map/pallas_call | solution.py:864
  384.8 4.9 add_bitcast_fusion
  395.6 8.2 %shard_map.183 = (f32[2,2,128,1280]{3,2,1,0:T(8,128)}, bf16[2,2,128,1280]{3,2,1,0:T(8,128)(2,1)}) custom-call(s32[3]{0:T(128)S(1)} %pad_add_fusion.place_ref.core_ref, bf16[960,1024]{1,0:T(8,128)(2,1)} %bitcast.236, bf16[1280,960]{1,0:T(8,128)(2,1)} %bitcast.228), custom_call_target="tpu_custom_call" | custom-call | flops 1048576 | bytes 1048576 | tf_op jit(solution)/shard_map/pallas_call | solution.py:834
  427.0 15.9 %collective-permute-done.42 = bf16[4,40,3840]{2,1,0:T(8,128)(2,1)} collective-permute-done((bf16[4,40,3840]{2,1,0:T(8,128)(2,1)S(1)}, bf16[4,40,3840]{2,1,0:T(8,128)(2,1)}, u32[]{:S(2)}, u32[]{:S(2)}) %collective-permute-start.42) | collective-permute-done | bytes 1228832 | tf_op jit(solution)/shard_map/ppermute | solution.py:884
  472.0 9.1 %all-to-all-done.6 = bf16[4,40,960]{2,1,0:T(8,128)(2,1)} async-done(((bf16[4,40,960]{2,1,0:T(8,128)(2,1)}), bf16[4,40,960]{2,1,0:T(8,128)(2,1)}, u32[]{:S(2)}, u32[]{:S(2)}) %all-to-all-start.6) | async-done | bytes 307232 | tf_op jit(solution)/shard_map/all_to_all | solution.py:905
  493.1 6.9 %collective-permute-done.47 = bf16[128,1280]{1,0:T(8,128)(2,1)S(1)} collective-permute-done((bf16[128,1280]{1,0:T(8,128)(2,1)S(1)}, bf16[128,1280]{1,0:T(8,128)(2,1)S(1)}, u32[]{:S(2)}, u32[]{:S(2)}) %collective-permute-start.47) | collective-permute-done | bytes 327712 | tf_op jit(solution)/shard_map/ppermute | solution.py:884
  (384 shorter events, 206.5 us)
Async XLA Ops:
  18.4 39.7 %all-gather.7.cloned.1.call-start = ((), (), s32[]{:S(2)}) async-start(), calls=%async_computation.16 | async-start | bytes 1638400 | tf_op jit(solution)/shard_map/all_gather | solution.py:918
  25.8 64.7 %all-gather.9.cloned.1.call-start = ((), (), s32[]{:S(2)}) async-start(), calls=%async_computation.17 | async-start | bytes 1536000 | tf_op jit(solution)/shard_map/all_gather | solution.py:918
  27.2 17.3 %collective-permute-start.1 = (bf16[256,1280]{1,0:T(8,128)(2,1)S(1)}, bf16[256,1280]{1,0:T(8,128)(2,1)S(1)}, u32[]{:S(2)}, u32[]{:S(2)}) collective-permute-start(bf16[256,1280]{1,0:T(8,128)(2,1)S(1)} %bitcast.230), channel_id=1, source_target_pairs={{0,1},{1,0},{2,3},{3,2},{4,5},{5,4},{6,7},{7,6},{8,9},{9,8},{10,11... | collective-permute-start | bytes 1966088 | tf_op jit(solution)/shard_map/ppermute | solution.py:884
  58.1 30.1 %collective-permute-start.5 = (bf16[4,160,964]{2,1,0:T(8,128)(2,1)}, bf16[4,160,964]{2,1,0:T(8,128)(2,1)S(1)}, u32[]{:S(2)}, u32[]{:S(2)}) collective-permute-start(bf16[4,160,964]{2,1,0:T(8,128)(2,1)} %bitcast.251), channel_id=1, source_target_pairs={{0,4},{4,0},{1,5},{5,1},{2,6},{6,2},{3,7},{7,3},{8,12},{12,8},{9,1... | collective-permute-start | bytes 3701768 | tf_op jit(solution)/shard_map/ppermute | solution.py:884
  64.8 78.5 %all-gather.11.cloned.1.call-start = ((), (), s32[]{:S(2)}) async-start(), calls=%async_computation.18 | async-start | bytes 3072000 | tf_op jit(solution)/shard_map/all_gather | solution.py:918
  91.5 28.4 %collective-permute-start.7 = (bf16[4,40,3840]{2,1,0:T(8,128)(2,1)}, bf16[4,40,3840]{2,1,0:T(8,128)(2,1)S(1)}, u32[]{:S(2)}, u32[]{:S(2)}) collective-permute-start(bf16[4,40,3840]{2,1,0:T(8,128)(2,1)} %bitcast.19.refs_0_), channel_id=1, source_target_pairs={{0,2},{1,3},{2,0},{3,1},{4,6},{5,7},{6,4},{7,5},{8,10},{9,11},{10,... | collective-permute-start | bytes 3686408 | tf_op jit(solution)/shard_map/ppermute | solution.py:884
  93.0 28.2 %collective-permute-start.6 = (bf16[4,40,3840]{2,1,0:T(8,128)(2,1)}, bf16[4,40,3840]{2,1,0:T(8,128)(2,1)}, u32[]{:S(2)}, u32[]{:S(2)}) collective-permute-start(bf16[4,40,3840]{2,1,0:T(8,128)(2,1)} %bitcast.19.refs_0_), channel_id=1, source_target_pairs={{0,4},{4,0},{1,5},{5,1},{2,6},{6,2},{3,7},{7,3},{8,12},{12,8},{9,1... | collective-permute-start | bytes 3686408 | tf_op jit(solution)/shard_map/ppermute | solution.py:884
  125.5 20.7 %collective-permute-start.8 = (bf16[4,40,1920]{2,1,0:T(8,128)(2,1)}, bf16[4,40,1920]{2,1,0:T(8,128)(2,1)}, u32[]{:S(2)}, u32[]{:S(2)}) collective-permute-start(bf16[4,40,1920]{2,1,0:T(8,128)(2,1)} %slice.153), channel_id=1, source_target_pairs={{0,2},{1,3},{2,0},{3,1},{4,6},{5,7},{6,4},{7,5},{8,10},{9,11},{10,... | collective-permute-start | bytes 1843208 | tf_op jit(solution)/shard_map/ppermute | solution.py:884
  126.0 20.2 %all-to-all-start.2 = ((bf16[4,320,256]{2,1,0:T(8,128)(2,1)}), bf16[4,320,256]{2,1,0:T(8,128)(2,1)S(1)}, u32[]{:S(2)}, u32[]{:S(2)}) async-start(bf16[4,320,256]{2,1,0:T(8,128)(2,1)} %bitcast.31), calls=%async_computation.2 | async-start | bytes 1310720 | tf_op jit(solution)/shard_map/all_to_all | solution.py:905
  129.9 19.1 %collective-permute-start.10 = (bf16[4,40,3840]{2,1,0:T(8,128)(2,1)}, bf16[4,40,3840]{2,1,0:T(8,128)(2,1)}, u32[]{:S(2)}, u32[]{:S(2)}) collective-permute-start(bf16[4,40,3840]{2,1,0:T(8,128)(2,1)} %bitcast.19.refs_0_), channel_id=1, source_target_pairs={{0,1},{1,0},{2,3},{3,2},{4,5},{5,4},{6,7},{7,6},{8,9},{9,8},{10,11... | collective-permute-start | bytes 3686408 | tf_op jit(solution)/shard_map/ppermute | solution.py:884
  130.4 19.2 %collective-permute-start.11 = (bf16[4,40,3840]{2,1,0:T(8,128)(2,1)}, bf16[4,40,3840]{2,1,0:T(8,128)(2,1)}, u32[]{:S(2)}, u32[]{:S(2)}) collective-permute-start(bf16[4,40,3840]{2,1,0:T(8,128)(2,1)} %collective-permute-done.6.refs_1_), channel_id=1, source_target_pairs={{0,1},{1,0},{2,3},{3,2},{4,5},{5,4},{6,7},{7,6},{8,9},{9,8},{10,11... | collective-permute-start | bytes 3686408 | tf_op jit(solution)/shard_map/ppermute | solution.py:884
  130.5 19.1 %collective-permute-start.12 = (bf16[4,40,3840]{2,1,0:T(8,128)(2,1)S(1)}, bf16[4,40,3840]{2,1,0:T(8,128)(2,1)}, u32[]{:S(2)}, u32[]{:S(2)}) collective-permute-start(bf16[4,40,3840]{2,1,0:T(8,128)(2,1)S(1)} %collective-permute-done.7.refs_2_), channel_id=1, source_target_pairs={{0,1},{1,0},{2,3},{3,2},{4,5},{5,4},{6,7},{7,6},{8,9},{9,8},{10,11... | collective-permute-start | bytes 3686408 | tf_op jit(solution)/shard_map/ppermute | solution.py:884
  149.0 29.5 %collective-permute-start.16 = (bf16[4,40,3840]{2,1,0:T(8,128)(2,1)S(1)}, bf16[4,40,3840]{2,1,0:T(8,128)(2,1)S(1)}, u32[]{:S(2)}, u32[]{:S(2)}) collective-permute-start(bf16[4,40,3840]{2,1,0:T(8,128)(2,1)S(1)} %get-tuple-element.245.along_ref), channel_id=1, source_target_pairs={{0,4},{4,0},{1,5},{5,1},{2,6},{6,2},{3,7},{7,3},{8,12},{12,8},{9,1... | collective-permute-start | bytes 3686408 | tf_op jit(solution)/shard_map/ppermute | solution.py:884
  178.5 28.7 %collective-permute-start.20 = (bf16[4,40,3840]{2,1,0:T(8,128)(2,1)S(1)}, bf16[4,40,3840]{2,1,0:T(8,128)(2,1)S(1)}, u32[]{:S(2)}, u32[]{:S(2)}) collective-permute-start(bf16[4,40,3840]{2,1,0:T(8,128)(2,1)S(1)} %get-tuple-element.139.refs_0_), channel_id=1, source_target_pairs={{0,2},{1,3},{2,0},{3,1},{4,6},{5,7},{6,4},{7,5},{8,10},{9,11},{10,... | collective-permute-start | bytes 3686408 | tf_op jit(solution)/shard_map/ppermute | solution.py:884
  179.1 28.6 %collective-permute-start.19 = (bf16[4,40,3840]{2,1,0:T(8,128)(2,1)S(1)}, bf16[4,40,3840]{2,1,0:T(8,128)(2,1)}, u32[]{:S(2)}, u32[]{:S(2)}) collective-permute-start(bf16[4,40,3840]{2,1,0:T(8,128)(2,1)S(1)} %get-tuple-element.139.refs_0_), channel_id=1, source_target_pairs={{0,4},{4,0},{1,5},{5,1},{2,6},{6,2},{3,7},{7,3},{8,12},{12,8},{9,1... | collective-permute-start | bytes 3686408 | tf_op jit(solution)/shard_map/ppermute | solution.py:884
  208.8 21.8 %collective-permute-start.22 = (bf16[4,40,1920]{2,1,0:T(8,128)(2,1)S(1)}, bf16[4,40,1920]{2,1,0:T(8,128)(2,1)S(1)}, u32[]{:S(2)}, u32[]{:S(2)}) collective-permute-start(bf16[4,40,1920]{2,1,0:T(8,128)(2,1)S(1)} %slice.167), channel_id=1, source_target_pairs={{0,4},{4,0},{1,5},{5,1},{2,6},{6,2},{3,7},{7,3},{8,12},{12,8},{9,1... | collective-permute-start | bytes 1843208 | tf_op jit(solution)/shard_map/ppermute | solution.py:884
  209.9 20.7 %collective-permute-start.21 = (bf16[4,40,1920]{2,1,0:T(8,128)(2,1)S(1)}, bf16[4,40,1920]{2,1,0:T(8,128)(2,1)S(1)}, u32[]{:S(2)}, u32[]{:S(2)}) collective-permute-start(bf16[4,40,1920]{2,1,0:T(8,128)(2,1)S(1)} %slice.166), channel_id=1, source_target_pairs={{0,2},{1,3},{2,0},{3,1},{4,6},{5,7},{6,4},{7,5},{8,10},{9,11},{10,... | collective-permute-start | bytes 1843208 | tf_op jit(solution)/shard_map/ppermute | solution.py:884
  211.4 19.9 %collective-permute-start.23 = (bf16[4,40,3840]{2,1,0:T(8,128)(2,1)S(1)}, bf16[4,40,3840]{2,1,0:T(8,128)(2,1)S(1)}, u32[]{:S(2)}, u32[]{:S(2)}) collective-permute-start(bf16[4,40,3840]{2,1,0:T(8,128)(2,1)S(1)} %get-tuple-element.139.refs_0_), channel_id=1, source_target_pairs={{0,1},{1,0},{2,3},{3,2},{4,5},{5,4},{6,7},{7,6},{8,9},{9,8},{10,11... | collective-permute-start | bytes 3686408 | tf_op jit(solution)/shard_map/ppermute | solution.py:884
  211.4 22.3 %collective-permute-start.24 = (bf16[4,40,3840]{2,1,0:T(8,128)(2,1)}, bf16[4,40,3840]{2,1,0:T(8,128)(2,1)S(1)}, u32[]{:S(2)}, u32[]{:S(2)}) collective-permute-start(bf16[4,40,3840]{2,1,0:T(8,128)(2,1)} %collective-permute-done.19.refs_1_), channel_id=1, source_target_pairs={{0,1},{1,0},{2,3},{3,2},{4,5},{5,4},{6,7},{7,6},{8,9},{9,8},{10,11... | collective-permute-start | bytes 3686408 | tf_op jit(solution)/shard_map/ppermute | solution.py:884
  211.9 21.8 %collective-permute-start.25 = (bf16[4,40,3840]{2,1,0:T(8,128)(2,1)S(1)}, bf16[4,40,3840]{2,1,0:T(8,128)(2,1)S(1)}, u32[]{:S(2)}, u32[]{:S(2)}) collective-permute-start(bf16[4,40,3840]{2,1,0:T(8,128)(2,1)S(1)} %collective-permute-done.20.refs_2_), channel_id=1, source_target_pairs={{0,1},{1,0},{2,3},{3,2},{4,5},{5,4},{6,7},{7,6},{8,9},{9,8},{10,11... | collective-permute-start | bytes 3686408 | tf_op jit(solution)/shard_map/ppermute | solution.py:884
  241.9 19.1 %collective-permute-start.28 = (bf16[128,1280]{1,0:T(8,128)(2,1)}, bf16[128,1280]{1,0:T(8,128)(2,1)}, u32[]{:S(2)}, u32[]{:S(2)}) collective-permute-start(bf16[128,1280]{1,0:T(8,128)(2,1)} %dynamic-slice_bitcast_fusion.3), channel_id=1, source_target_pairs={{0,4},{4,0},{1,5},{5,1},{2,6},{6,2},{3,7},{7,3},{8,12},{12,8},{9,1... | collective-permute-start | bytes 983048 | tf_op jit(solution)/shard_map/ppermute | solution.py:884
  252.3 106.6 %reduce-scatter.5.cloned.1.call-start = ((), (), s32[]{:S(2)}) async-start(), calls=%async_computation.12 | async-start | bytes 3276800 | tf_op jit(solution)/shard_map/reduce_scatter | solution.py:934
  306.3 42.4 %collective-permute-start.34 = (bf16[4,40,3840]{2,1,0:T(8,128)(2,1)}, bf16[4,40,3840]{2,1,0:T(8,128)(2,1)}, u32[]{:S(2)}, u32[]{:S(2)}) collective-permute-start(bf16[4,40,3840]{2,1,0:T(8,128)(2,1)} %pad_maximum_fusion), channel_id=1, source_target_pairs={{0,4},{4,0},{1,5},{5,1},{2,6},{6,2},{3,7},{7,3},{8,12},{12,8},{9,1... | collective-permute-start | bytes 3686408 | tf_op jit(solution)/shard_map/ppermute | solution.py:884
  323.2 35.6 %collective-permute-start.35 = (bf16[4,40,3840]{2,1,0:T(8,128)(2,1)}, bf16[4,40,3840]{2,1,0:T(8,128)(2,1)}, u32[]{:S(2)}, u32[]{:S(2)}) collective-permute-start(bf16[4,40,3840]{2,1,0:T(8,128)(2,1)} %pad_maximum_fusion.1), channel_id=1, source_target_pairs={{0,2},{1,3},{2,0},{3,1},{4,6},{5,7},{6,4},{7,5},{8,10},{9,11},{10,... | collective-permute-start | bytes 3686408 | tf_op jit(solution)/shard_map/ppermute | solution.py:884
  335.9 23.0 %all-to-all-start.5 = ((bf16[4,320,256]{2,1,0:T(8,128)(2,1)}), bf16[4,320,256]{2,1,0:T(8,128)(2,1)}, u32[]{:S(2)}, u32[]{:S(2)}) async-start(bf16[4,320,256]{2,1,0:T(8,128)(2,1)} %bitcast.64), calls=%async_computation.5 | async-start | bytes 1310720 | tf_op jit(solution)/shard_map/all_to_all | solution.py:905
  340.1 63.7 %reduce-scatter.7.cloned.1.call-start = ((), (), s32[]{:S(2)}) async-start(), calls=%async_computation.13 | async-start | bytes 1536000 | tf_op jit(solution)/shard_map/reduce_scatter | solution.py:934
  358.9 25.9 %collective-permute-start.37 = (bf16[2,2,4,40,3840]{4,3,2,1,0:T(8,128)(2,1)}, bf16[2,2,4,40,3840]{4,3,2,1,0:T(8,128)(2,1)}, u32[]{:S(2)}, u32[]{:S(2)}) collective-permute-start(bf16[2,2,4,40,3840]{4,3,2,1,0:T(8,128)(2,1)} %get-tuple-element.189), channel_id=1, source_target_pairs={{0,1},{1,0},{2,3},{3,2},{4,5},{5,4},{6,7},{7,6},{8,9},{9,8},{10,11... | collective-permute-start | bytes 14745608 | tf_op jit(solution)/shard_map/ppermute | solution.py:884
  361.5 84.5 %reduce-scatter.9.cloned.1.call-start = ((), (), s32[]{:S(2)}) async-start(), calls=%async_computation.14 | async-start | bytes 3276800 | tf_op jit(solution)/shard_map/reduce_scatter | solution.py:934
  413.4 29.5 %collective-permute-start.42 = (bf16[4,40,3840]{2,1,0:T(8,128)(2,1)S(1)}, bf16[4,40,3840]{2,1,0:T(8,128)(2,1)}, u32[]{:S(2)}, u32[]{:S(2)}) collective-permute-start(bf16[4,40,3840]{2,1,0:T(8,128)(2,1)S(1)} %pad_maximum_fusion.2), channel_id=1, source_target_pairs={{0,4},{4,0},{1,5},{5,1},{2,6},{6,2},{3,7},{7,3},{8,12},{12,8},{9,1... | collective-permute-start | bytes 3686408 | tf_op jit(solution)/shard_map/ppermute | solution.py:884
  414.8 29.3 %collective-permute-start.43 = (bf16[4,40,3840]{2,1,0:T(8,128)(2,1)S(1)}, bf16[4,40,3840]{2,1,0:T(8,128)(2,1)}, u32[]{:S(2)}, u32[]{:S(2)}) collective-permute-start(bf16[4,40,3840]{2,1,0:T(8,128)(2,1)S(1)} %pad_maximum_fusion.3), channel_id=1, source_target_pairs={{0,2},{1,3},{2,0},{3,1},{4,6},{5,7},{6,4},{7,5},{8,10},{9,11},{10,... | collective-permute-start | bytes 3686408 | tf_op jit(solution)/shard_map/ppermute | solution.py:884
  459.1 28.5 %collective-permute-start.46 = (bf16[2,128,1280]{2,1,0:T(8,128)(2,1)}, bf16[2,128,1280]{2,1,0:T(8,128)(2,1)}, u32[]{:S(2)}, u32[]{:S(2)}) collective-permute-start(bf16[2,128,1280]{2,1,0:T(8,128)(2,1)} %fusion.84), channel_id=1, source_target_pairs={{0,2},{1,3},{2,0},{3,1},{4,6},{5,7},{6,4},{7,5},{8,10},{9,11},{10,... | collective-permute-start | bytes 1966088 | tf_op jit(solution)/shard_map/ppermute | solution.py:884
  468.1 33.2 %reduce-scatter.11.cloned.1.call-start = ((), (), s32[]{:S(2)}) async-start(), calls=%async_computation.15 | async-start | bytes 1536000 | tf_op jit(solution)/shard_map/reduce_scatter | solution.py:934
  (102 other events, 767.9 us)
Sparse Core Ops, SparseCore 0:
  26.0 32.0 all-gather.6
  60.2 30.2 all-gather.8
  92.1 51.1 all-gather.10
  306.4 51.7 reduce-scatter.4
  361.6 31.1 reduce-scatter.6
  395.0 50.8 reduce-scatter.8
  471.3 29.3 reduce-scatter.10

commit v24 on v22

--- a/solution.py
+++ b/solution.py
@@ -1119,18 +1119,24 @@
             bars, rows = tied(bars, diagonal_rows(cored))
             diagonal = sent_beside_and_across(*rows)
             halves, to_core = rows_back(bars, qkv, token_rows)
-            halves, to_core, diagonal, summed = tied(halves, to_core, diagonal, summed)
-            halves, to_core, rows = tied(halves, to_core, neighbour_rows(cored, *diagonal))
+            scale_sum = sum_over(jnp.stack(scale_grads), ("head", 1))
+            halves, to_core, diagonal, summed, scale_sum = tied(
+                halves, to_core, diagonal, summed, scale_sum
+            )
+            scale_sum = sum_over(scale_sum, ("head", 2))
+            halves, to_core, rows, scale_sum = tied(
+                halves, to_core, neighbour_rows(cored, *diagonal), scale_sum
+            )
             sent = sent_beside_and_across(*rows)
             halves = halves + other_core(to_core).astype(F32)
-            scale_sum = sum_over(jnp.stack(scale_grads), ("head", 1), ("batch", 1), ("batch", 2))
+            scale_sum = sum_over(scale_sum, ("batch", 1), ("batch", 2), ("blk", 1))
             own = own_quarter(cored)
             halves, sent, z_sum, scale_sum, own = tied(halves, sent, z_sum, scale_sum, own)
             halves, own, earlier = tied(halves, own_sum(own, *sent), earlier)
             moved = over_head(earlier.reshape(4, -1, earlier.shape[-1]))
             dense_first = over_batch(own)
             normed_grad = scatter_row(halves)
-            z_across, scale_sum, dense_first = tied(across_sum(z_sum), scale_sum, dense_first)
+            z_across, dense_first = tied(across_sum(z_sum), dense_first)
             z_across = over_head(z_across.reshape(4, -1, z_across.shape[-1]))
             dense_grad = [dense_first, summed]
             qkv_grads = [columns_to_rows(z_across), columns_to_rows(moved)]
@@ -1150,8 +1156,7 @@
             beside = swapped(beside, "head", 2)
         upper = middle_grad + lower_of(normed_grad, stream, factor_one, gains[layer])
     input_grad = swap_halves(upper.astype(BF16).reshape(tokens.shape)).astype(F32)
-    scale_total = sum_over(scale_sum, ("head", 2), ("blk", 1))
-    scale_grad = scale_total * (SCALE_BASE / math.sqrt(head_dim)) * jax.nn.sigmoid(scale_param)
+    scale_grad = scale_sum * (SCALE_BASE / math.sqrt(head_dim)) * jax.nn.sigmoid(scale_param)
     dense_all = jnp.stack([part.astype(F32) for part in dense_grad])
     qkv_all = jnp.stack(qkv_grads)
     up_all = dense_all[:, :, width:-width]

time: 516 us -> 514 us (level)
  transfers between devices with their start and end apart: 65 -> 65, of which waited for: 35 -> 32; matrix products, arithmetic and copies ran while one was open for 14% -> 14% of each run, Pallas kernels for 22% -> 22%
where the time goes in v24:
time: 514 us; the launch traced here: 506 us
  waiting for transfers between devices  183 us (36%)
  Pallas kernels  113 us (22%)
  starting transfers between devices  69.8 us (14%)
  other arithmetic  50.1 us (10%)
  local copies, waits for them, and re-layouts  35.8 us (7%)
  matrix products  19.6 us (4%)
  blocking collectives  18.7 us (4%)
  between operations  15.7 us (3%)
    ppermute x51, waiting for transfers between devices, swapped(): return lax.ppermute(array, axis, [(i, i ^ mask) for i in range(size)])  131 us
    ppermute x51, starting transfers between devices, swapped(): return lax.ppermute(array, axis, [(i, i ^ mask) for i in range(size)])  43.2 us
    all_to_all x7, waiting for transfers between devices, over_head(): lax.all_to_all(parts, 'head', split_axis=0, concat_axis=0, tiled=True)  27.1 us
    all_to_all x7, starting transfers between devices, over_head(): lax.all_to_all(parts, 'head', split_axis=0, concat_axis=0, tiled=True)  25.9 us
    pallas_call x2, Pallas kernels, attend_back_rows(): pl.pallas_call(functools.partial(attend_back_kernel, token_rows), grid=(l...  24.8 us
    all_gather x3, waiting for transfers between devices, along_batch(): return lax.all_gather(piece, 'batch', axis=0, tiled=False)  22.4 us
    all_to_all x1, blocking collectives, over_head(): lax.all_to_all(parts, 'head', split_axis=0, concat_axis=0, tiled=True)  18.7 us
    pallas_call x2, Pallas kernels, dense_grads(): pl.pallas_call(dense_grad_kernel, grid_spec=pltpu.PrefetchScalarGridSpec(...  17.1 us
  transfers between devices with their start and end apart: 65, of which 32 were waited for; matrix products, arithmetic and copies ran while one was open for 14% of the time, Pallas kernels for 22%

profile of v24, /device:TPU:0, one launch (start us, length us, event | category | flops | bytes accessed | tf_op | source)
XLA Modules:
  0.0 505.6 jit_solution(9092148739798368610)
XLA Ops:
  19.3 5.8 %all-to-all-done = bf16[4,40,964]{2,1,0:T(8,128)(2,1)S(1)} async-done(((bf16[4,40,964]{2,1,0:T(8,128)(2,1)}), bf16[4,40,964]{2,1,0:T(8,128)(2,1)S(1)}, u32[]{:S(2)}, u32[]{:S(2)}) %all-to-all-start) | async-done | bytes 308512 | tf_op jit(solution)/shard_map/all_to_all | solution.py:891
  28.4 14.4 %collective-permute-done.2.refs_2_ = bf16[256,1280]{1,0:T(8,128)(2,1)S(1)} collective-permute-done((bf16[256,1280]{1,0:T(8,128)(2,1)S(1)}, bf16[256,1280]{1,0:T(8,128)(2,1)S(1)}, u32[]{:S(2)}, u32[]{:S(2)}) %collective-permute-start.2) | collective-permute-done | bytes 655392 | tf_op jit(solution)/shard_map/ppermute | solution.py:870
  45.1 13.0 %all-gather.7.cloned.1.call-done = bf16[640,964]{1,0:T(8,128)(2,1)} async-done(((bf16[160,964]{1,0:T(8,128)(2,1)}), bf16[640,964]{1,0:T(8,128)(2,1)}) %all-gather.7.cloned.1.call-update) | async-done | bytes 1233936 | tf_op jit(solution)/shard_map/all_gather | solution.py:904
  64.9 6.6 %all-to-all-done.1 = bf16[4,40,960]{2,1,0:T(8,128)(2,1)S(1)} async-done(((bf16[4,40,960]{2,1,0:T(8,128)(2,1)}), bf16[4,40,960]{2,1,0:T(8,128)(2,1)S(1)}, u32[]{:S(2)}, u32[]{:S(2)}) %all-to-all-start.1) | async-done | bytes 307232 | tf_op jit(solution)/shard_map/all_to_all | solution.py:891
  71.7 16.5 %collective-permute-done.5.across_ref = bf16[4,160,964]{2,1,0:T(8,128)(2,1)S(1)} collective-permute-done((bf16[4,160,964]{2,1,0:T(8,128)(2,1)}, bf16[4,160,964]{2,1,0:T(8,128)(2,1)S(1)}, u32[]{:S(2)}, u32[]{:S(2)}) %collective-permute-start.5) | collective-permute-done | bytes 1233952 | tf_op jit(solution)/shard_map/ppermute | solution.py:870
  95.0 4.6 shard_map.169
  100.9 7.7 %shard_map.170 = (bf16[1024,1280]{1,0:T(8,128)(2,1)}, f32[960,1024]{1,0:T(8,128)S(1)}) custom-call(s32[3]{0:T(128)S(1)} %pad_add_fusion.place_ref.core_ref, bf16[256,1280]{1,0:T(8,128)(2,1)} %bitcast.227, bf16[256,1280]{1,0:T(8,128)(2,1)} %copy-done.51, bf16[256,1280]{1,0:T(8,128)(2,1)} %copy-done.50, bf16[256,1280]{1,0:T(8,128)(2,1)} %collective-permute-done.3.refs_3_, ...), custom_call_target="tpu_custom_call" | custom-call | flops 1048576 | bytes 1048576 | tf_op jit(solution)/shard_map/pallas_call | solution.py:733
  108.7 6.7 %shard_map.171 = (bf16[4,4,80,256]{3,2,1,0:T(8,128)(2,1)}, f32[4,1,1024]{2,1,0:T(1,128)S(1)}) custom-call(f32[3,4,80,1024]{3,2,1,0:T(8,128)S(1)} %bitcast.197, f32[80,1]{1,0:T(8,128)S(1)} %copy.60.scale_ref, s32[1024,1]{1,0:T(8,128)S(1)} %copy.61.col_ref, s32[1,1024]{1,0:T(1,128)S(1)} %constant_dynamic-slice_fusion.row_ref), custom_call_target="tpu_custom_call" | custom-call | flops 1048576 | bytes 1048576 | tf_op jit(solution)/shard_map/pallas_call | solution.py:435
  115.4 4.5 collective-permute-done.7.refs_2_
  130.8 5.4 %collective-permute-done.9.refs_4_ = bf16[4,40,1920]{2,1,0:T(8,128)(2,1)} collective-permute-done((bf16[4,40,1920]{2,1,0:T(8,128)(2,1)}, bf16[4,40,1920]{2,1,0:T(8,128)(2,1)}, u32[]{:S(2)}, u32[]{:S(2)}) %collective-permute-start.9) | collective-permute-done | bytes 614432 | tf_op jit(solution)/shard_map/ppermute | solution.py:870
  136.2 7.1 %all-gather.11.cloned.1.call-done = bf16[8,40,3840]{2,1,0:T(8,128)(2,1)} async-done(((bf16[2,40,3840]{2,1,0:T(8,128)(2,1)}), bf16[8,40,3840]{2,1,0:T(8,128)(2,1)}) %all-gather.11.cloned.1.call-update) | async-done | bytes 2457616 | tf_op jit(solution)/shard_map/all_gather | solution.py:904
  149.6 4.5 shard_map.172
  161.9 16.6 %collective-permute-done.16.across_ref = bf16[4,40,3840]{2,1,0:T(8,128)(2,1)S(1)} collective-permute-done((bf16[4,40,3840]{2,1,0:T(8,128)(2,1)S(1)}, bf16[4,40,3840]{2,1,0:T(8,128)(2,1)S(1)}, u32[]{:S(2)}, u32[]{:S(2)}) %collective-permute-start.16) | collective-permute-done | bytes 1228832 | tf_op jit(solution)/shard_map/ppermute | solution.py:870
  181.2 4.7 shard_map.173
  185.9 6.6 %shard_map.174 = (bf16[1024,1280]{1,0:T(8,128)(2,1)}, f32[960,1024]{1,0:T(8,128)S(1)}) custom-call(s32[3]{0:T(128)S(1)} %pad_add_fusion.place_ref.core_ref, bf16[256,1280]{1,0:T(8,128)(2,1)} %multiply_convert_fusion.2.refs_0_, bf16[256,1280]{1,0:T(8,128)(2,1)} %collective-permute-done.17.refs_1_, bf16[256,1280]{1,0:T(8,128)(2,1)} %collective-permute-done.15.refs_2_, ...), custom_call_target="tpu_custom_call" | custom-call | flops 1048576 | bytes 1048576 | tf_op jit(solution)/shard_map/pallas_call | solution.py:733
  192.6 6.1 %shard_map.175 = (bf16[4,4,80,256]{3,2,1,0:T(8,128)(2,1)S(1)}, f32[4,1,1024]{2,1,0:T(1,128)S(1)}) custom-call(f32[3,4,80,1024]{3,2,1,0:T(8,128)S(1)} %bitcast.199, f32[80,1]{1,0:T(8,128)S(1)} %copy.64.scale_ref, s32[1024,1]{1,0:T(8,128)S(1)} %copy.61.col_ref, s32[1,1024]{1,0:T(1,128)S(1)} %constant_dynamic-slice_fusion.row_ref), custom_call_target="tpu_custom_call" | custom-call | flops 1048576 | bytes 1048576 | tf_op jit(solution)/shard_map/pallas_call | solution.py:435
  198.6 8.6 %collective-permute-done.20.refs_2_ = bf16[4,40,3840]{2,1,0:T(8,128)(2,1)S(1)} collective-permute-done((bf16[4,40,3840]{2,1,0:T(8,128)(2,1)S(1)}, bf16[4,40,3840]{2,1,0:T(8,128)(2,1)S(1)}, u32[]{:S(2)}, u32[]{:S(2)}) %collective-permute-start.20) | collective-permute-done | bytes 1228832 | tf_op jit(solution)/shard_map/ppermute | solution.py:870
  211.9 18.7 %all_to_all.40 = bf16[4,320,256]{2,1,0:T(8,128)(2,1)S(1)} all-to-all(bf16[4,320,256]{2,1,0:T(8,128)(2,1)S(1)} %bitcast.215), channel_id=1, replica_groups=mesh['batch'=4,'blk'=2,'head'=4] {'head'}, dimensions={0} | all-to-all | bytes 1310720 | tf_op jit(solution)/shard_map/all_to_all | solution.py:891
  247.2 4.2 all-to-all-start.4
  252.0 8.5 %shard_map.177 = (bf16[2,2,4,40,3840]{4,3,2,1,0:T(8,128)(2,1)}, bf16[2,2,4,40,3840]{4,3,2,1,0:T(8,128)(2,1)}) custom-call(s32[3]{0:T(128)S(1)} %pad_add_fusion.place_ref.core_ref, bf16[1280,256]{1,0:T(8,128)(2,1)} %bitcast.239, bf16[256,1280]{1,0:T(8,128)(2,1)} %copy-done.27, bf16[256,1280]{1,0:T(8,128)(2,1)} %copy-done.48, bf16[256,1280]{1,0:T(8,128)(2,1)} %copy-done.28, ...), custom_call_target="tpu_custom_call" | custom-call | flops 1048576 | bytes 1048576 | tf_op jit(solution)/shard_map/pallas_call | solution.py:599
  262.9 12.5 %shard_map.178 = (bf16[3,4,80,1024]{3,2,1,0:T(8,128)(2,1)}, f32[80,128]{1,0:T(8,128)}) custom-call(f32[3,4,80,1024]{3,2,1,0:T(8,128)} %bitcast.200, bf16[4,4,80,256]{3,2,1,0:T(8,128)(2,1)} %bitcast.56.grad_ref, f32[4,1,1024]{2,1,0:T(1,128)S(1)} %get-tuple-element.156.lse_ref, f32[80,1]{1,0:T(8,128)S(1)} %copy.64.scale_ref, s32[1024,1]{1,0:T(8,128)S(1)} %copy.61.col_ref, ...), custom_call_target="tpu_custom_call" | custom-call | flops 1048576 | bytes 1048576 | tf_op jit(solution)/shard_map/pallas_call | solution.py:528
  280.8 11.2 %shard_map.179 = (f32[2,2,128,1280]{3,2,1,0:T(8,128)}, bf16[2,2,128,1280]{3,2,1,0:T(8,128)(2,1)}, bf16[1280,960]{1,0:T(8,128)(2,1)}) custom-call(s32[3]{0:T(128)S(1)} %pad_add_fusion.place_ref.core_ref, bf16[960,1024]{1,0:T(8,128)(2,1)} %bitcast.241, bf16[1280,960]{1,0:T(8,128)(2,1)} %bitcast.217, bf16[1024,1280]{1,0:T(8,128)(2,1)} %get-tuple-element.163.normed_ref), custom_call_target="tpu_custom_call" | custom-call | flops 1048576 | bytes 1048576 | tf_op jit(solution)/shard_map/pallas_call | solution.py:779
  307.0 13.9 %collective-permute-done.33 = bf16[2,128,1280]{2,1,0:T(8,128)(2,1)} collective-permute-done((bf16[2,128,1280]{2,1,0:T(8,128)(2,1)}, bf16[2,128,1280]{2,1,0:T(8,128)(2,1)}, u32[]{:S(2)}, u32[]{:S(2)}) %collective-permute-start.33) | collective-permute-done | bytes 655392 | tf_op jit(solution)/shard_map/ppermute | solution.py:870
  335.2 4.2 all-to-all-start.5
  339.4 8.6 %shard_map.180 = (bf16[2,2,4,40,3840]{4,3,2,1,0:T(8,128)(2,1)}, bf16[2,2,4,40,3840]{4,3,2,1,0:T(8,128)(2,1)}) custom-call(s32[3]{0:T(128)S(1)} %pad_add_fusion.place_ref.core_ref, bf16[1280,256]{1,0:T(8,128)(2,1)} %bitcast.236, bf16[256,1280]{1,0:T(8,128)(2,1)} %copy-done.26, bf16[256,1280]{1,0:T(8,128)(2,1)} %copy-done.44, bf16[256,1280]{1,0:T(8,128)(2,1)} %copy-done.32, ...), custom_call_target="tpu_custom_call" | custom-call | flops 1048576 | bytes 1048576 | tf_op jit(solution)/shard_map/pallas_call | solution.py:599
  350.4 7.8 %all-to-all-done.5 = bf16[4,320,256]{2,1,0:T(8,128)(2,1)} async-done(((bf16[4,320,256]{2,1,0:T(8,128)(2,1)}), bf16[4,320,256]{2,1,0:T(8,128)(2,1)}, u32[]{:S(2)}, u32[]{:S(2)}) %all-to-all-start.5) | async-done | bytes 655392 | tf_op jit(solution)/shard_map/all_to_all | solution.py:891
  363.3 12.3 %shard_map.181 = (bf16[3,4,80,1024]{3,2,1,0:T(8,128)(2,1)}, f32[80,128]{1,0:T(8,128)}) custom-call(f32[3,4,80,1024]{3,2,1,0:T(8,128)} %bitcast.198, bf16[4,4,80,256]{3,2,1,0:T(8,128)(2,1)} %bitcast.68.grad_ref, f32[4,1,1024]{2,1,0:T(1,128)S(1)} %get-tuple-element.186.lse_ref, f32[80,1]{1,0:T(8,128)S(1)} %copy.60.scale_ref, s32[1024,1]{1,0:T(8,128)S(1)} %copy.61.col_ref, ...), custom_call_target="tpu_custom_call" | custom-call | flops 1048576 | bytes 1048576 | tf_op jit(solution)/shard_map/pallas_call | solution.py:528
  376.4 7.3 %shard_map.182 = bf16[1280,960]{1,0:T(8,128)(2,1)} custom-call(bf16[960,1024]{1,0:T(8,128)(2,1)} %bitcast.231, bf16[1024,1280]{1,0:T(8,128)(2,1)} %get-tuple-element.190.normed_ref), custom_call_target="tpu_custom_call" | custom-call | flops 1048576 | bytes 1048576 | tf_op jit(solution)/shard_map/pallas_call | solution.py:850
  383.8 4.9 add_bitcast_fusion
  394.7 8.4 %shard_map.183 = (f32[2,2,128,1280]{3,2,1,0:T(8,128)}, bf16[2,2,128,1280]{3,2,1,0:T(8,128)(2,1)}) custom-call(s32[3]{0:T(128)S(1)} %pad_add_fusion.place_ref.core_ref, bf16[960,1024]{1,0:T(8,128)(2,1)} %bitcast.232, bf16[1280,960]{1,0:T(8,128)(2,1)} %bitcast.224), custom_call_target="tpu_custom_call" | custom-call | flops 1048576 | bytes 1048576 | tf_op jit(solution)/shard_map/pallas_call | solution.py:820
  425.3 18.5 %collective-permute-done.47 = f32[2,80]{1,0:T(2,128)S(1)} collective-permute-done((f32[2,80]{1,0:T(2,128)S(1)}, f32[2,80]{1,0:T(2,128)S(1)}, u32[]{:S(2)}, u32[]{:S(2)}) %collective-permute-start.47) | collective-permute-done | bytes 672 | tf_op jit(solution)/shard_map/ppermute | solution.py:870
  458.8 11.1 %collective-permute-done.48 = bf16[2,128,1280]{2,1,0:T(8,128)(2,1)} collective-permute-done((bf16[2,128,1280]{2,1,0:T(8,128)(2,1)}, bf16[2,128,1280]{2,1,0:T(8,128)(2,1)}, u32[]{:S(2)}, u32[]{:S(2)}) %collective-permute-start.48) | collective-permute-done | bytes 655392 | tf_op jit(solution)/shard_map/ppermute | solution.py:870
  (382 shorter events, 198.4 us)
Async XLA Ops:
  18.4 39.7 %all-gather.7.cloned.1.call-start = ((), (), s32[]{:S(2)}) async-start(), calls=%async_computation.16 | async-start | bytes 1638400 | tf_op jit(solution)/shard_map/all_gather | solution.py:904
  25.8 64.7 %all-gather.9.cloned.1.call-start = ((), (), s32[]{:S(2)}) async-start(), calls=%async_computation.17 | async-start | bytes 1536000 | tf_op jit(solution)/shard_map/all_gather | solution.py:904
  58.1 30.1 %collective-permute-start.5 = (bf16[4,160,964]{2,1,0:T(8,128)(2,1)}, bf16[4,160,964]{2,1,0:T(8,128)(2,1)S(1)}, u32[]{:S(2)}, u32[]{:S(2)}) collective-permute-start(bf16[4,160,964]{2,1,0:T(8,128)(2,1)} %bitcast.247), channel_id=1, source_target_pairs={{0,4},{4,0},{1,5},{5,1},{2,6},{6,2},{3,7},{7,3},{8,12},{12,8},{9,1... | collective-permute-start | bytes 3701768 | tf_op jit(solution)/shard_map/ppermute | solution.py:870
  64.8 78.5 %all-gather.11.cloned.1.call-start = ((), (), s32[]{:S(2)}) async-start(), calls=%async_computation.18 | async-start | bytes 3072000 | tf_op jit(solution)/shard_map/all_gather | solution.py:904
  91.5 28.4 %collective-permute-start.7 = (bf16[4,40,3840]{2,1,0:T(8,128)(2,1)}, bf16[4,40,3840]{2,1,0:T(8,128)(2,1)S(1)}, u32[]{:S(2)}, u32[]{:S(2)}) collective-permute-start(bf16[4,40,3840]{2,1,0:T(8,128)(2,1)} %bitcast.19.refs_0_), channel_id=1, source_target_pairs={{0,2},{1,3},{2,0},{3,1},{4,6},{5,7},{6,4},{7,5},{8,10},{9,11},{10,... | collective-permute-start | bytes 3686408 | tf_op jit(solution)/shard_map/ppermute | solution.py:870
  93.0 28.2 %collective-permute-start.6 = (bf16[4,40,3840]{2,1,0:T(8,128)(2,1)}, bf16[4,40,3840]{2,1,0:T(8,128)(2,1)}, u32[]{:S(2)}, u32[]{:S(2)}) collective-permute-start(bf16[4,40,3840]{2,1,0:T(8,128)(2,1)} %bitcast.19.refs_0_), channel_id=1, source_target_pairs={{0,4},{4,0},{1,5},{5,1},{2,6},{6,2},{3,7},{7,3},{8,12},{12,8},{9,1... | collective-permute-start | bytes 3686408 | tf_op jit(solution)/shard_map/ppermute | solution.py:870
  125.5 20.7 %collective-permute-start.8 = (bf16[4,40,1920]{2,1,0:T(8,128)(2,1)}, bf16[4,40,1920]{2,1,0:T(8,128)(2,1)}, u32[]{:S(2)}, u32[]{:S(2)}) collective-permute-start(bf16[4,40,1920]{2,1,0:T(8,128)(2,1)} %slice.153), channel_id=1, source_target_pairs={{0,2},{1,3},{2,0},{3,1},{4,6},{5,7},{6,4},{7,5},{8,10},{9,11},{10,... | collective-permute-start | bytes 1843208 | tf_op jit(solution)/shard_map/ppermute | solution.py:870
  126.0 20.2 %all-to-all-start.2 = ((bf16[4,320,256]{2,1,0:T(8,128)(2,1)}), bf16[4,320,256]{2,1,0:T(8,128)(2,1)S(1)}, u32[]{:S(2)}, u32[]{:S(2)}) async-start(bf16[4,320,256]{2,1,0:T(8,128)(2,1)} %bitcast.31), calls=%async_computation.2 | async-start | bytes 1310720 | tf_op jit(solution)/shard_map/all_to_all | solution.py:891
  130.3 19.3 %collective-permute-start.11 = (bf16[4,40,3840]{2,1,0:T(8,128)(2,1)}, bf16[4,40,3840]{2,1,0:T(8,128)(2,1)}, u32[]{:S(2)}, u32[]{:S(2)}) collective-permute-start(bf16[4,40,3840]{2,1,0:T(8,128)(2,1)} %collective-permute-done.6.refs_1_), channel_id=1, source_target_pairs={{0,1},{1,0},{2,3},{3,2},{4,5},{5,4},{6,7},{7,6},{8,9},{9,8},{10,11... | collective-permute-start | bytes 3686408 | tf_op jit(solution)/shard_map/ppermute | solution.py:870
  130.4 19.2 %collective-permute-start.12 = (bf16[4,40,3840]{2,1,0:T(8,128)(2,1)S(1)}, bf16[4,40,3840]{2,1,0:T(8,128)(2,1)}, u32[]{:S(2)}, u32[]{:S(2)}) collective-permute-start(bf16[4,40,3840]{2,1,0:T(8,128)(2,1)S(1)} %collective-permute-done.7.refs_2_), channel_id=1, source_target_pairs={{0,1},{1,0},{2,3},{3,2},{4,5},{5,4},{6,7},{7,6},{8,9},{9,8},{10,11... | collective-permute-start | bytes 3686408 | tf_op jit(solution)/shard_map/ppermute | solution.py:870
  149.0 29.5 %collective-permute-start.16 = (bf16[4,40,3840]{2,1,0:T(8,128)(2,1)S(1)}, bf16[4,40,3840]{2,1,0:T(8,128)(2,1)S(1)}, u32[]{:S(2)}, u32[]{:S(2)}) collective-permute-start(bf16[4,40,3840]{2,1,0:T(8,128)(2,1)S(1)} %get-tuple-element.249.along_ref), channel_id=1, source_target_pairs={{0,4},{4,0},{1,5},{5,1},{2,6},{6,2},{3,7},{7,3},{8,12},{12,8},{9,1... | collective-permute-start | bytes 3686408 | tf_op jit(solution)/shard_map/ppermute | solution.py:870
  178.5 28.7 %collective-permute-start.20 = (bf16[4,40,3840]{2,1,0:T(8,128)(2,1)S(1)}, bf16[4,40,3840]{2,1,0:T(8,128)(2,1)S(1)}, u32[]{:S(2)}, u32[]{:S(2)}) collective-permute-start(bf16[4,40,3840]{2,1,0:T(8,128)(2,1)S(1)} %get-tuple-element.141.refs_0_), channel_id=1, source_target_pairs={{0,2},{1,3},{2,0},{3,1},{4,6},{5,7},{6,4},{7,5},{8,10},{9,11},{10,... | collective-permute-start | bytes 3686408 | tf_op jit(solution)/shard_map/ppermute | solution.py:870
  179.1 28.5 %collective-permute-start.19 = (bf16[4,40,3840]{2,1,0:T(8,128)(2,1)S(1)}, bf16[4,40,3840]{2,1,0:T(8,128)(2,1)}, u32[]{:S(2)}, u32[]{:S(2)}) collective-permute-start(bf16[4,40,3840]{2,1,0:T(8,128)(2,1)S(1)} %get-tuple-element.141.refs_0_), channel_id=1, source_target_pairs={{0,4},{4,0},{1,5},{5,1},{2,6},{6,2},{3,7},{7,3},{8,12},{12,8},{9,1... | collective-permute-start | bytes 3686408 | tf_op jit(solution)/shard_map/ppermute | solution.py:870
  208.8 21.9 %collective-permute-start.22 = (bf16[4,40,1920]{2,1,0:T(8,128)(2,1)S(1)}, bf16[4,40,1920]{2,1,0:T(8,128)(2,1)S(1)}, u32[]{:S(2)}, u32[]{:S(2)}) collective-permute-start(bf16[4,40,1920]{2,1,0:T(8,128)(2,1)S(1)} %slice.167), channel_id=1, source_target_pairs={{0,4},{4,0},{1,5},{5,1},{2,6},{6,2},{3,7},{7,3},{8,12},{12,8},{9,1... | collective-permute-start | bytes 1843208 | tf_op jit(solution)/shard_map/ppermute | solution.py:870
  209.9 20.7 %collective-permute-start.21 = (bf16[4,40,1920]{2,1,0:T(8,128)(2,1)S(1)}, bf16[4,40,1920]{2,1,0:T(8,128)(2,1)S(1)}, u32[]{:S(2)}, u32[]{:S(2)}) collective-permute-start(bf16[4,40,1920]{2,1,0:T(8,128)(2,1)S(1)} %slice.166), channel_id=1, source_target_pairs={{0,2},{1,3},{2,0},{3,1},{4,6},{5,7},{6,4},{7,5},{8,10},{9,11},{10,... | collective-permute-start | bytes 1843208 | tf_op jit(solution)/shard_map/ppermute | solution.py:870
  211.4 19.9 %collective-permute-start.23 = (bf16[4,40,3840]{2,1,0:T(8,128)(2,1)S(1)}, bf16[4,40,3840]{2,1,0:T(8,128)(2,1)S(1)}, u32[]{:S(2)}, u32[]{:S(2)}) collective-permute-start(bf16[4,40,3840]{2,1,0:T(8,128)(2,1)S(1)} %get-tuple-element.141.refs_0_), channel_id=1, source_target_pairs={{0,1},{1,0},{2,3},{3,2},{4,5},{5,4},{6,7},{7,6},{8,9},{9,8},{10,11... | collective-permute-start | bytes 3686408 | tf_op jit(solution)/shard_map/ppermute | solution.py:870
  211.4 22.3 %collective-permute-start.24 = (bf16[4,40,3840]{2,1,0:T(8,128)(2,1)}, bf16[4,40,3840]{2,1,0:T(8,128)(2,1)S(1)}, u32[]{:S(2)}, u32[]{:S(2)}) collective-permute-start(bf16[4,40,3840]{2,1,0:T(8,128)(2,1)} %collective-permute-done.19.refs_1_), channel_id=1, source_target_pairs={{0,1},{1,0},{2,3},{3,2},{4,5},{5,4},{6,7},{7,6},{8,9},{9,8},{10,11... | collective-permute-start | bytes 3686408 | tf_op jit(solution)/shard_map/ppermute | solution.py:870
  211.9 21.8 %collective-permute-start.25 = (bf16[4,40,3840]{2,1,0:T(8,128)(2,1)S(1)}, bf16[4,40,3840]{2,1,0:T(8,128)(2,1)S(1)}, u32[]{:S(2)}, u32[]{:S(2)}) collective-permute-start(bf16[4,40,3840]{2,1,0:T(8,128)(2,1)S(1)} %collective-permute-done.20.refs_2_), channel_id=1, source_target_pairs={{0,1},{1,0},{2,3},{3,2},{4,5},{5,4},{6,7},{7,6},{8,9},{9,8},{10,11... | collective-permute-start | bytes 3686408 | tf_op jit(solution)/shard_map/ppermute | solution.py:870
  241.2 19.3 %collective-permute-start.28 = (bf16[128,1280]{1,0:T(8,128)(2,1)}, bf16[128,1280]{1,0:T(8,128)(2,1)}, u32[]{:S(2)}, u32[]{:S(2)}) collective-permute-start(bf16[128,1280]{1,0:T(8,128)(2,1)} %dynamic-slice_bitcast_fusion.3), channel_id=1, source_target_pairs={{0,4},{4,0},{1,5},{5,1},{2,6},{6,2},{3,7},{7,3},{8,12},{12,8},{9,1... | collective-permute-start | bytes 983048 | tf_op jit(solution)/shard_map/ppermute | solution.py:870
  251.4 106.8 %reduce-scatter.5.cloned.1.call-start = ((), (), s32[]{:S(2)}) async-start(), calls=%async_computation.12 | async-start | bytes 3276800 | tf_op jit(solution)/shard_map/reduce_scatter | solution.py:920
  305.6 42.4 %collective-permute-start.34 = (bf16[4,40,3840]{2,1,0:T(8,128)(2,1)}, bf16[4,40,3840]{2,1,0:T(8,128)(2,1)}, u32[]{:S(2)}, u32[]{:S(2)}) collective-permute-start(bf16[4,40,3840]{2,1,0:T(8,128)(2,1)} %pad_maximum_fusion), channel_id=1, source_target_pairs={{0,4},{4,0},{1,5},{5,1},{2,6},{6,2},{3,7},{7,3},{8,12},{12,8},{9,1... | collective-permute-start | bytes 3686408 | tf_op jit(solution)/shard_map/ppermute | solution.py:870
  322.5 35.6 %collective-permute-start.35 = (bf16[4,40,3840]{2,1,0:T(8,128)(2,1)}, bf16[4,40,3840]{2,1,0:T(8,128)(2,1)}, u32[]{:S(2)}, u32[]{:S(2)}) collective-permute-start(bf16[4,40,3840]{2,1,0:T(8,128)(2,1)} %pad_maximum_fusion.1), channel_id=1, source_target_pairs={{0,2},{1,3},{2,0},{3,1},{4,6},{5,7},{6,4},{7,5},{8,10},{9,11},{10,... | collective-permute-start | bytes 3686408 | tf_op jit(solution)/shard_map/ppermute | solution.py:870
  335.2 23.0 %all-to-all-start.5 = ((bf16[4,320,256]{2,1,0:T(8,128)(2,1)}), bf16[4,320,256]{2,1,0:T(8,128)(2,1)}, u32[]{:S(2)}, u32[]{:S(2)}) async-start(bf16[4,320,256]{2,1,0:T(8,128)(2,1)} %bitcast.64), calls=%async_computation.5 | async-start | bytes 1310720 | tf_op jit(solution)/shard_map/all_to_all | solution.py:891
  339.4 63.8 %reduce-scatter.7.cloned.1.call-start = ((), (), s32[]{:S(2)}) async-start(), calls=%async_computation.13 | async-start | bytes 1536000 | tf_op jit(solution)/shard_map/reduce_scatter | solution.py:920
  358.2 25.6 %collective-permute-start.37 = (bf16[2,2,4,40,3840]{4,3,2,1,0:T(8,128)(2,1)}, bf16[2,2,4,40,3840]{4,3,2,1,0:T(8,128)(2,1)}, u32[]{:S(2)}, u32[]{:S(2)}) collective-permute-start(bf16[2,2,4,40,3840]{4,3,2,1,0:T(8,128)(2,1)} %get-tuple-element.191), channel_id=1, source_target_pairs={{0,1},{1,0},{2,3},{3,2},{4,5},{5,4},{6,7},{7,6},{8,9},{9,8},{10,11... | collective-permute-start | bytes 14745608 | tf_op jit(solution)/shard_map/ppermute | solution.py:870
  360.8 85.7 %reduce-scatter.9.cloned.1.call-start = ((), (), s32[]{:S(2)}) async-start(), calls=%async_computation.14 | async-start | bytes 3276800 | tf_op jit(solution)/shard_map/reduce_scatter | solution.py:920
  383.8 102.1 %reduce-scatter.11.cloned.1.call-start = ((), (), s32[]{:S(2)}) async-start(), calls=%async_computation.15 | async-start | bytes 1536000 | tf_op jit(solution)/shard_map/reduce_scatter | solution.py:920
  414.3 29.5 %collective-permute-start.42 = (bf16[2,2,128,1280]{3,2,1,0:T(8,128)(2,1)S(1)}, bf16[2,2,128,1280]{3,2,1,0:T(8,128)(2,1)S(1)}, u32[]{:S(2)}, u32[]{:S(2)}) collective-permute-start(bf16[2,2,128,1280]{3,2,1,0:T(8,128)(2,1)S(1)} %copy-done.62), channel_id=1, source_target_pairs={{0,1},{1,0},{2,3},{3,2},{4,5},{5,4},{6,7},{7,6},{8,9},{9,8},{10,11... | collective-permute-start | bytes 3932168 | tf_op jit(solution)/shard_map/ppermute | solution.py:870
  414.3 31.2 %collective-permute-start.43 = (bf16[4,40,3840]{2,1,0:T(8,128)(2,1)S(1)}, bf16[4,40,3840]{2,1,0:T(8,128)(2,1)S(1)}, u32[]{:S(2)}, u32[]{:S(2)}) collective-permute-start(bf16[4,40,3840]{2,1,0:T(8,128)(2,1)S(1)} %pad_maximum_fusion.2), channel_id=1, source_target_pairs={{0,4},{4,0},{1,5},{5,1},{2,6},{6,2},{3,7},{7,3},{8,12},{12,8},{9,1... | collective-permute-start | bytes 3686408 | tf_op jit(solution)/shard_map/ppermute | solution.py:870
  415.6 31.0 %collective-permute-start.44 = (bf16[4,40,3840]{2,1,0:T(8,128)(2,1)S(1)}, bf16[4,40,3840]{2,1,0:T(8,128)(2,1)}, u32[]{:S(2)}, u32[]{:S(2)}) collective-permute-start(bf16[4,40,3840]{2,1,0:T(8,128)(2,1)S(1)} %pad_maximum_fusion.3), channel_id=1, source_target_pairs={{0,2},{1,3},{2,0},{3,1},{4,6},{5,7},{6,4},{7,5},{8,10},{9,11},{10,... | collective-permute-start | bytes 3686408 | tf_op jit(solution)/shard_map/ppermute | solution.py:870
  454.0 22.4 %collective-permute-start.50 = (bf16[160,960]{1,0:T(8,128)(2,1)}, bf16[160,960]{1,0:T(8,128)(2,1)}, u32[]{:S(2)}, u32[]{:S(2)}) collective-permute-start(bf16[160,960]{1,0:T(8,128)(2,1)} %dynamic-slice_bitcast_fusion), channel_id=1, source_target_pairs={{0,4},{4,0},{1,5},{5,1},{2,6},{6,2},{3,7},{7,3},{8,12},{12,8},{9,1... | collective-permute-start | bytes 921608 | tf_op jit(solution)/shard_map/ppermute | solution.py:870
  455.3 20.3 %all-to-all-start.7 = ((bf16[4,40,960]{2,1,0:T(8,128)(2,1)}), bf16[4,40,960]{2,1,0:T(8,128)(2,1)S(1)}, u32[]{:S(2)}, u32[]{:S(2)}) async-start(bf16[4,40,960]{2,1,0:T(8,128)(2,1)} %bitcast.92), calls=%async_computation.11 | async-start | bytes 655360 | tf_op jit(solution)/shard_map/all_to_all | solution.py:891
  (101 other events, 825.0 us)
Sparse Core Ops, SparseCore 0:
  26.0 32.0 all-gather.6
  60.2 30.2 all-gather.8
  92.1 51.1 all-gather.10
  305.7 51.7 reduce-scatter.4
  360.9 31.0 reduce-scatter.6
  394.3 50.9 reduce-scatter.8
  455.5 30.3 reduce-scatter.10

commit v25 on v24

--- a/solution.py
+++ b/solution.py
@@ -1044,16 +1044,14 @@
         attended, log_total = attend_rows(
             projected, scale_vecs[layer], segments, 4, token_rows
         )
-        attended, across, beside = tied(attended, across, beside)
+        attended_t, across, beside = tied(over_head(attended), across, beside)
         one, two = to_beside(across), to_across(beside)
         if layer == 0:
             two, next_both = tied(two, next_both)
             next_along, dense_next = next_both[:, 0], next_both[:, 1]
             next_across = swapped(next_along, "blk", 1)
-            attended_t, one, two = tied(over_head(attended), one, two)
         else:
             dense_near = dense_next
-            attended_t, one, two = tied(over_head(attended), one, two)
         pieces = (dense_near, across, beside, one, two)
         pieces += tuple(other_core(piece) for piece in pieces)
         attended_t = attended_t.reshape(width, -1)

time: 514 us -> 513 us (level)
  waiting for transfers between devices: 183 us -> 191 us
    ppermute x51, waiting for transfers between devices: 131 us -> 140 us  [swapped(): return lax.ppermute(array, axis, [(i, i ^ mask) for i in range(size)])]
    all_gather x3, waiting for transfers between devices: 22.4 us -> 15.3 us  [along_batch(): return lax.all_gather(piece, 'batch', axis=0, tiled=False)]
    all_to_all x7, waiting for transfers between devices: 27.1 us -> 33.9 us  [over_head(): lax.all_to_all(parts, 'head', split_axis=0, concat_axis=0, tiled=True)]
    all_to_all x1, blocking collectives: 18.7 us -> 13.6 us  [over_head(): lax.all_to_all(parts, 'head', split_axis=0, concat_axis=0, tiled=True)]
    unnamed x136 -> x134, local copies, waits for them, and re-layouts: 11.6 us -> 11.4 us
  transfers between devices with their start and end apart: 65 -> 65, of which waited for: 32 -> 30; matrix products, arithmetic and copies ran while one was open for 14% -> 14% of each run, Pallas kernels for 22% -> 22%
where the time goes in v25:
time: 513 us; the launch traced here: 505 us
  waiting for transfers between devices  191 us (37%)
  Pallas kernels  113 us (22%)
  starting transfers between devices  67.1 us (13%)
  other arithmetic  50.6 us (10%)
  local copies, waits for them, and re-layouts  34 us (7%)
  matrix products  20.8 us (4%)
  between operations  15.7 us (3%)
  blocking collectives  13.6 us (3%)
    ppermute x51, waiting for transfers between devices, swapped(): return lax.ppermute(array, axis, [(i, i ^ mask) for i in range(size)])  140 us
    ppermute x51, starting transfers between devices, swapped(): return lax.ppermute(array, axis, [(i, i ^ mask) for i in range(size)])  39.7 us
    all_to_all x7, waiting for transfers between devices, over_head(): lax.all_to_all(parts, 'head', split_axis=0, concat_axis=0, tiled=True)  33.9 us
    all_to_all x7, starting transfers between devices, over_head(): lax.all_to_all(parts, 'head', split_axis=0, concat_axis=0, tiled=True)  26.6 us
    pallas_call x2, Pallas kernels, attend_back_rows(): pl.pallas_call(functools.partial(attend_back_kernel, token_rows), grid=(l...  24.7 us
    pallas_call x2, Pallas kernels, dense_grads(): pl.pallas_call(dense_grad_kernel, grid_spec=pltpu.PrefetchScalarGridSpec(...  17.1 us
    all_gather x3, waiting for transfers between devices, along_batch(): return lax.all_gather(piece, 'batch', axis=0, tiled=False)  15.3 us
    pallas_call x2, Pallas kernels, project(): pl.pallas_call(functools.partial(project_kernel, with_norm), grid_spec=pl...  14.3 us
  transfers between devices with their start and end apart: 65, of which 30 were waited for; matrix products, arithmetic and copies ran while one was open for 14% of the time, Pallas kernels for 22%

profile of v25, /device:TPU:0, one launch (start us, length us, event | category | flops | bytes accessed | tf_op | source)
XLA Modules:
  0.0 505.2 jit_solution(11427088949763327911)
XLA Ops:
  19.3 5.8 %all-to-all-done = bf16[4,40,964]{2,1,0:T(8,128)(2,1)S(1)} async-done(((bf16[4,40,964]{2,1,0:T(8,128)(2,1)}), bf16[4,40,964]{2,1,0:T(8,128)(2,1)S(1)}, u32[]{:S(2)}, u32[]{:S(2)}) %all-to-all-start) | async-done | bytes 308512 | tf_op jit(solution)/shard_map/all_to_all | solution.py:891
  28.4 14.4 %collective-permute-done.2.refs_2_ = bf16[256,1280]{1,0:T(8,128)(2,1)S(1)} collective-permute-done((bf16[256,1280]{1,0:T(8,128)(2,1)S(1)}, bf16[256,1280]{1,0:T(8,128)(2,1)S(1)}, u32[]{:S(2)}, u32[]{:S(2)}) %collective-permute-start.2) | collective-permute-done | bytes 655392 | tf_op jit(solution)/shard_map/ppermute | solution.py:870
  45.1 13.0 %all-gather.7.cloned.1.call-done = bf16[640,964]{1,0:T(8,128)(2,1)} async-done(((bf16[160,964]{1,0:T(8,128)(2,1)}), bf16[640,964]{1,0:T(8,128)(2,1)}) %all-gather.7.cloned.1.call-update) | async-done | bytes 1233936 | tf_op jit(solution)/shard_map/all_gather | solution.py:904
  64.9 6.6 %all-to-all-done.1 = bf16[4,40,960]{2,1,0:T(8,128)(2,1)S(1)} async-done(((bf16[4,40,960]{2,1,0:T(8,128)(2,1)}), bf16[4,40,960]{2,1,0:T(8,128)(2,1)S(1)}, u32[]{:S(2)}, u32[]{:S(2)}) %all-to-all-start.1) | async-done | bytes 307232 | tf_op jit(solution)/shard_map/all_to_all | solution.py:891
  71.7 16.5 %collective-permute-done.5.across_ref = bf16[4,160,964]{2,1,0:T(8,128)(2,1)S(1)} collective-permute-done((bf16[4,160,964]{2,1,0:T(8,128)(2,1)}, bf16[4,160,964]{2,1,0:T(8,128)(2,1)S(1)}, u32[]{:S(2)}, u32[]{:S(2)}) %collective-permute-start.5) | collective-permute-done | bytes 1233952 | tf_op jit(solution)/shard_map/ppermute | solution.py:870
  94.9 4.6 shard_map.169
  100.9 7.7 %shard_map.170 = (bf16[1024,1280]{1,0:T(8,128)(2,1)}, f32[960,1024]{1,0:T(8,128)S(1)}) custom-call(s32[3]{0:T(128)S(1)} %pad_add_fusion.place_ref.core_ref, bf16[256,1280]{1,0:T(8,128)(2,1)} %bitcast.228, bf16[256,1280]{1,0:T(8,128)(2,1)} %copy-done.50, bf16[256,1280]{1,0:T(8,128)(2,1)} %copy-done.49, bf16[256,1280]{1,0:T(8,128)(2,1)} %collective-permute-done.3.refs_3_, ...), custom_call_target="tpu_custom_call" | custom-call | flops 1048576 | bytes 1048576 | tf_op jit(solution)/shard_map/pallas_call | solution.py:733
  108.7 6.1 %shard_map.171 = (bf16[4,4,80,256]{3,2,1,0:T(8,128)(2,1)S(1)}, f32[4,1,1024]{2,1,0:T(1,128)S(1)}) custom-call(f32[3,4,80,1024]{3,2,1,0:T(8,128)S(1)} %bitcast.197, f32[80,1]{1,0:T(8,128)S(1)} %copy.60.scale_ref, s32[1024,1]{1,0:T(8,128)S(1)} %copy.61.col_ref, s32[1,1024]{1,0:T(1,128)S(1)} %constant_dynamic-slice_fusion.row_ref), custom_call_target="tpu_custom_call" | custom-call | flops 1048576 | bytes 1048576 | tf_op jit(solution)/shard_map/pallas_call | solution.py:435
  114.8 13.6 %all_to_all.40 = bf16[4,320,256]{2,1,0:T(8,128)(2,1)} all-to-all(bf16[4,320,256]{2,1,0:T(8,128)(2,1)S(1)} %bitcast.216), channel_id=1, replica_groups=mesh['batch'=4,'blk'=2,'head'=4] {'head'}, dimensions={0} | all-to-all | bytes 1310720 | tf_op jit(solution)/shard_map/all_to_all | solution.py:891
  131.9 13.3 %collective-permute-done.8.refs_3_ = bf16[4,40,1920]{2,1,0:T(8,128)(2,1)} collective-permute-done((bf16[4,40,1920]{2,1,0:T(8,128)(2,1)S(1)}, bf16[4,40,1920]{2,1,0:T(8,128)(2,1)}, u32[]{:S(2)}, u32[]{:S(2)}) %collective-permute-start.8) | collective-permute-done | bytes 614432 | tf_op jit(solution)/shard_map/ppermute | solution.py:870
  148.7 4.6 shard_map.172
  161.3 15.5 %collective-permute-done.16.across_ref = bf16[4,40,3840]{2,1,0:T(8,128)(2,1)S(1)} collective-permute-done((bf16[4,40,3840]{2,1,0:T(8,128)(2,1)S(1)}, bf16[4,40,3840]{2,1,0:T(8,128)(2,1)S(1)}, u32[]{:S(2)}, u32[]{:S(2)}) %collective-permute-start.16) | collective-permute-done | bytes 1228832 | tf_op jit(solution)/shard_map/ppermute | solution.py:870
  180.7 4.8 shard_map.173
  185.4 6.6 %shard_map.174 = (bf16[1024,1280]{1,0:T(8,128)(2,1)}, f32[960,1024]{1,0:T(8,128)S(1)}) custom-call(s32[3]{0:T(128)S(1)} %pad_add_fusion.place_ref.core_ref, bf16[256,1280]{1,0:T(8,128)(2,1)} %multiply_convert_fusion.2.refs_0_, bf16[256,1280]{1,0:T(8,128)(2,1)} %collective-permute-done.17.refs_1_, bf16[256,1280]{1,0:T(8,128)(2,1)} %collective-permute-done.15.refs_2_, ...), custom_call_target="tpu_custom_call" | custom-call | flops 1048576 | bytes 1048576 | tf_op jit(solution)/shard_map/pallas_call | solution.py:733
  192.1 6.1 %shard_map.175 = (bf16[4,4,80,256]{3,2,1,0:T(8,128)(2,1)S(1)}, f32[4,1,1024]{2,1,0:T(1,128)S(1)}) custom-call(f32[3,4,80,1024]{3,2,1,0:T(8,128)S(1)} %bitcast.199, f32[80,1]{1,0:T(8,128)S(1)} %copy.64.scale_ref, s32[1024,1]{1,0:T(8,128)S(1)} %copy.61.col_ref, s32[1,1024]{1,0:T(1,128)S(1)} %constant_dynamic-slice_fusion.row_ref), custom_call_target="tpu_custom_call" | custom-call | flops 1048576 | bytes 1048576 | tf_op jit(solution)/shard_map/pallas_call | solution.py:435
  199.0 4.4 all-to-all-start.3
  204.0 9.8 %all-to-all-done.3 = bf16[4,320,256]{2,1,0:T(8,128)(2,1)} async-done(((bf16[4,320,256]{2,1,0:T(8,128)(2,1)}), bf16[4,320,256]{2,1,0:T(8,128)(2,1)}, u32[]{:S(2)}, u32[]{:S(2)}) %all-to-all-start.3) | async-done | bytes 655392 | tf_op jit(solution)/shard_map/all_to_all | solution.py:891
  217.3 11.9 %collective-permute-done.22.refs_4_ = bf16[4,40,1920]{2,1,0:T(8,128)(2,1)S(1)} collective-permute-done((bf16[4,40,1920]{2,1,0:T(8,128)(2,1)S(1)}, bf16[4,40,1920]{2,1,0:T(8,128)(2,1)S(1)}, u32[]{:S(2)}, u32[]{:S(2)}) %collective-permute-start.22) | collective-permute-done | bytes 614432 | tf_op jit(solution)/shard_map/ppermute | solution.py:870
  252.6 8.5 %shard_map.177 = (bf16[2,2,4,40,3840]{4,3,2,1,0:T(8,128)(2,1)}, bf16[2,2,4,40,3840]{4,3,2,1,0:T(8,128)(2,1)}) custom-call(s32[3]{0:T(128)S(1)} %pad_add_fusion.place_ref.core_ref, bf16[1280,256]{1,0:T(8,128)(2,1)} %bitcast.49.attended_ref, bf16[256,1280]{1,0:T(8,128)(2,1)} %copy-done.28, bf16[256,1280]{1,0:T(8,128)(2,1)} %copy-done.47, ...), custom_call_target="tpu_custom_call" | custom-call | flops 1048576 | bytes 1048576 | tf_op jit(solution)/shard_map/pallas_call | solution.py:599
  263.5 12.4 %shard_map.178 = (bf16[3,4,80,1024]{3,2,1,0:T(8,128)(2,1)}, f32[80,128]{1,0:T(8,128)}) custom-call(f32[3,4,80,1024]{3,2,1,0:T(8,128)} %bitcast.200, bf16[4,4,80,256]{3,2,1,0:T(8,128)(2,1)} %bitcast.56.grad_ref, f32[4,1,1024]{2,1,0:T(1,128)S(1)} %get-tuple-element.144.lse_ref, f32[80,1]{1,0:T(8,128)S(1)} %copy.64.scale_ref, s32[1024,1]{1,0:T(8,128)S(1)} %copy.61.col_ref, ...), custom_call_target="tpu_custom_call" | custom-call | flops 1048576 | bytes 1048576 | tf_op jit(solution)/shard_map/pallas_call | solution.py:528
  281.5 11.3 %shard_map.179 = (f32[2,2,128,1280]{3,2,1,0:T(8,128)}, bf16[2,2,128,1280]{3,2,1,0:T(8,128)(2,1)}, bf16[1280,960]{1,0:T(8,128)(2,1)}) custom-call(s32[3]{0:T(128)S(1)} %pad_add_fusion.place_ref.core_ref, bf16[960,1024]{1,0:T(8,128)(2,1)} %bitcast.240, bf16[1280,960]{1,0:T(8,128)(2,1)} %bitcast.218, bf16[1024,1280]{1,0:T(8,128)(2,1)} %get-tuple-element.151.normed_ref), custom_call_target="tpu_custom_call" | custom-call | flops 1048576 | bytes 1048576 | tf_op jit(solution)/shard_map/pallas_call | solution.py:779
  307.9 13.7 %collective-permute-done.33 = bf16[2,128,1280]{2,1,0:T(8,128)(2,1)} collective-permute-done((bf16[2,128,1280]{2,1,0:T(8,128)(2,1)}, bf16[2,128,1280]{2,1,0:T(8,128)(2,1)}, u32[]{:S(2)}, u32[]{:S(2)}) %collective-permute-start.33) | collective-permute-done | bytes 655392 | tf_op jit(solution)/shard_map/ppermute | solution.py:870
  340.1 8.5 %shard_map.180 = (bf16[2,2,4,40,3840]{4,3,2,1,0:T(8,128)(2,1)}, bf16[2,2,4,40,3840]{4,3,2,1,0:T(8,128)(2,1)}) custom-call(s32[3]{0:T(128)S(1)} %pad_add_fusion.place_ref.core_ref, bf16[1280,256]{1,0:T(8,128)(2,1)} %bitcast.237, bf16[256,1280]{1,0:T(8,128)(2,1)} %copy-done.27, bf16[256,1280]{1,0:T(8,128)(2,1)} %copy-done.43, bf16[256,1280]{1,0:T(8,128)(2,1)} %copy-done.31, ...), custom_call_target="tpu_custom_call" | custom-call | flops 1048576 | bytes 1048576 | tf_op jit(solution)/shard_map/pallas_call | solution.py:599
  351.1 7.8 %all-to-all-done.5 = bf16[4,320,256]{2,1,0:T(8,128)(2,1)} async-done(((bf16[4,320,256]{2,1,0:T(8,128)(2,1)}), bf16[4,320,256]{2,1,0:T(8,128)(2,1)}, u32[]{:S(2)}, u32[]{:S(2)}) %all-to-all-start.5) | async-done | bytes 655392 | tf_op jit(solution)/shard_map/all_to_all | solution.py:891
  364.2 12.3 %shard_map.181 = (bf16[3,4,80,1024]{3,2,1,0:T(8,128)(2,1)}, f32[80,128]{1,0:T(8,128)}) custom-call(f32[3,4,80,1024]{3,2,1,0:T(8,128)} %bitcast.198, bf16[4,4,80,256]{3,2,1,0:T(8,128)(2,1)} %bitcast.68.grad_ref, f32[4,1,1024]{2,1,0:T(1,128)S(1)} %get-tuple-element.174.lse_ref, f32[80,1]{1,0:T(8,128)S(1)} %copy.60.scale_ref, s32[1024,1]{1,0:T(8,128)S(1)} %copy.61.col_ref, ...), custom_call_target="tpu_custom_call" | custom-call | flops 1048576 | bytes 1048576 | tf_op jit(solution)/shard_map/pallas_call | solution.py:528
  377.3 7.3 %shard_map.182 = bf16[1280,960]{1,0:T(8,128)(2,1)} custom-call(bf16[960,1024]{1,0:T(8,128)(2,1)} %bitcast.232, bf16[1024,1280]{1,0:T(8,128)(2,1)} %get-tuple-element.178.normed_ref), custom_call_target="tpu_custom_call" | custom-call | flops 1048576 | bytes 1048576 | tf_op jit(solution)/shard_map/pallas_call | solution.py:850
  384.7 4.9 add_bitcast_fusion
  395.4 8.4 %shard_map.183 = (f32[2,2,128,1280]{3,2,1,0:T(8,128)}, bf16[2,2,128,1280]{3,2,1,0:T(8,128)(2,1)}) custom-call(s32[3]{0:T(128)S(1)} %pad_add_fusion.place_ref.core_ref, bf16[960,1024]{1,0:T(8,128)(2,1)} %bitcast.233, bf16[1280,960]{1,0:T(8,128)(2,1)} %bitcast.225), custom_call_target="tpu_custom_call" | custom-call | flops 1048576 | bytes 1048576 | tf_op jit(solution)/shard_map/pallas_call | solution.py:820
  417.7 4.3 collective-permute-done.45
  422.0 4.7 collective-permute-done.46
  427.2 17.2 %collective-permute-done.47 = f32[2,80]{1,0:T(2,128)S(1)} collective-permute-done((f32[2,80]{1,0:T(2,128)S(1)}, f32[2,80]{1,0:T(2,128)S(1)}, u32[]{:S(2)}, u32[]{:S(2)}) %collective-permute-start.47) | collective-permute-done | bytes 672 | tf_op jit(solution)/shard_map/ppermute | solution.py:870
  459.7 10.9 %collective-permute-done.48 = bf16[2,128,1280]{2,1,0:T(8,128)(2,1)} collective-permute-done((bf16[2,128,1280]{2,1,0:T(8,128)(2,1)}, bf16[2,128,1280]{2,1,0:T(8,128)(2,1)}, u32[]{:S(2)}, u32[]{:S(2)}) %collective-permute-start.48) | collective-permute-done | bytes 655392 | tf_op jit(solution)/shard_map/ppermute | solution.py:870
  (380 shorter events, 191.8 us)
Async XLA Ops:
  18.4 39.7 %all-gather.7.cloned.1.call-start = ((), (), s32[]{:S(2)}) async-start(), calls=%async_computation.16 | async-start | bytes 1638400 | tf_op jit(solution)/shard_map/all_gather | solution.py:904
  25.8 64.7 %all-gather.9.cloned.1.call-start = ((), (), s32[]{:S(2)}) async-start(), calls=%async_computation.17 | async-start | bytes 1536000 | tf_op jit(solution)/shard_map/all_gather | solution.py:904
  28.4 16.6 %collective-permute-start.1 = (bf16[256,1280]{1,0:T(8,128)(2,1)S(1)}, bf16[256,1280]{1,0:T(8,128)(2,1)S(1)}, u32[]{:S(2)}, u32[]{:S(2)}) collective-permute-start(bf16[256,1280]{1,0:T(8,128)(2,1)S(1)} %bitcast.227), channel_id=1, source_target_pairs={{0,1},{1,0},{2,3},{3,2},{4,5},{5,4},{6,7},{7,6},{8,9},{9,8},{10,11... | collective-permute-start | bytes 1966088 | tf_op jit(solution)/shard_map/ppermute | solution.py:870
  58.1 30.1 %collective-permute-start.5 = (bf16[4,160,964]{2,1,0:T(8,128)(2,1)}, bf16[4,160,964]{2,1,0:T(8,128)(2,1)S(1)}, u32[]{:S(2)}, u32[]{:S(2)}) collective-permute-start(bf16[4,160,964]{2,1,0:T(8,128)(2,1)} %bitcast.246), channel_id=1, source_target_pairs={{0,4},{4,0},{1,5},{5,1},{2,6},{6,2},{3,7},{7,3},{8,12},{12,8},{9,1... | collective-permute-start | bytes 3701768 | tf_op jit(solution)/shard_map/ppermute | solution.py:870
  64.8 80.7 %all-gather.11.cloned.1.call-start = ((), (), s32[]{:S(2)}) async-start(), calls=%async_computation.18 | async-start | bytes 3072000 | tf_op jit(solution)/shard_map/all_gather | solution.py:904
  91.5 36.8 %collective-permute-start.7 = (bf16[4,40,3840]{2,1,0:T(8,128)(2,1)}, bf16[4,40,3840]{2,1,0:T(8,128)(2,1)S(1)}, u32[]{:S(2)}, u32[]{:S(2)}) collective-permute-start(bf16[4,40,3840]{2,1,0:T(8,128)(2,1)} %bitcast.19.refs_0_), channel_id=1, source_target_pairs={{0,2},{1,3},{2,0},{3,1},{4,6},{5,7},{6,4},{7,5},{8,10},{9,11},{10,... | collective-permute-start | bytes 3686408 | tf_op jit(solution)/shard_map/ppermute | solution.py:870
  93.1 35.3 %collective-permute-start.6 = (bf16[4,40,3840]{2,1,0:T(8,128)(2,1)}, bf16[4,40,3840]{2,1,0:T(8,128)(2,1)}, u32[]{:S(2)}, u32[]{:S(2)}) collective-permute-start(bf16[4,40,3840]{2,1,0:T(8,128)(2,1)} %bitcast.19.refs_0_), channel_id=1, source_target_pairs={{0,4},{4,0},{1,5},{5,1},{2,6},{6,2},{3,7},{7,3},{8,12},{12,8},{9,1... | collective-permute-start | bytes 3686408 | tf_op jit(solution)/shard_map/ppermute | solution.py:870
  131.3 17.3 %collective-permute-start.11 = (bf16[4,40,3840]{2,1,0:T(8,128)(2,1)}, bf16[4,40,3840]{2,1,0:T(8,128)(2,1)}, u32[]{:S(2)}, u32[]{:S(2)}) collective-permute-start(bf16[4,40,3840]{2,1,0:T(8,128)(2,1)} %collective-permute-done.6.refs_1_), channel_id=1, source_target_pairs={{0,1},{1,0},{2,3},{3,2},{4,5},{5,4},{6,7},{7,6},{8,9},{9,8},{10,11... | collective-permute-start | bytes 3686408 | tf_op jit(solution)/shard_map/ppermute | solution.py:870
  131.9 16.8 %collective-permute-start.12 = (bf16[4,40,3840]{2,1,0:T(8,128)(2,1)S(1)}, bf16[4,40,3840]{2,1,0:T(8,128)(2,1)}, u32[]{:S(2)}, u32[]{:S(2)}) collective-permute-start(bf16[4,40,3840]{2,1,0:T(8,128)(2,1)S(1)} %collective-permute-done.7.refs_2_), channel_id=1, source_target_pairs={{0,1},{1,0},{2,3},{3,2},{4,5},{5,4},{6,7},{7,6},{8,9},{9,8},{10,11... | collective-permute-start | bytes 3686408 | tf_op jit(solution)/shard_map/ppermute | solution.py:870
  147.6 29.3 %collective-permute-start.16 = (bf16[4,40,3840]{2,1,0:T(8,128)(2,1)S(1)}, bf16[4,40,3840]{2,1,0:T(8,128)(2,1)S(1)}, u32[]{:S(2)}, u32[]{:S(2)}) collective-permute-start(bf16[4,40,3840]{2,1,0:T(8,128)(2,1)S(1)} %get-tuple-element.237.along_ref), channel_id=1, source_target_pairs={{0,4},{4,0},{1,5},{5,1},{2,6},{6,2},{3,7},{7,3},{8,12},{12,8},{9,1... | collective-permute-start | bytes 3686408 | tf_op jit(solution)/shard_map/ppermute | solution.py:870
  160.5 17.2 %collective-permute-start.15 = (bf16[256,1280]{1,0:T(8,128)(2,1)}, bf16[256,1280]{1,0:T(8,128)(2,1)}, u32[]{:S(2)}, u32[]{:S(2)}) collective-permute-start(bf16[256,1280]{1,0:T(8,128)(2,1)} %multiply_convert_fusion.2.refs_0_), channel_id=1, source_target_pairs={{0,2},{1,3},{2,0},{3,1},{4,6},{5,7},{6,4},{7,5},{8,10},{9,11},{10,... | collective-permute-start | bytes 1966088 | tf_op jit(solution)/shard_map/ppermute | solution.py:870
  177.7 36.1 %collective-permute-start.20 = (bf16[4,40,3840]{2,1,0:T(8,128)(2,1)S(1)}, bf16[4,40,3840]{2,1,0:T(8,128)(2,1)S(1)}, u32[]{:S(2)}, u32[]{:S(2)}) collective-permute-start(bf16[4,40,3840]{2,1,0:T(8,128)(2,1)S(1)} %get-tuple-element.132.refs_0_), channel_id=1, source_target_pairs={{0,2},{1,3},{2,0},{3,1},{4,6},{5,7},{6,4},{7,5},{8,10},{9,11},{10,... | collective-permute-start | bytes 3686408 | tf_op jit(solution)/shard_map/ppermute | solution.py:870
  178.5 35.2 %collective-permute-start.19 = (bf16[4,40,3840]{2,1,0:T(8,128)(2,1)S(1)}, bf16[4,40,3840]{2,1,0:T(8,128)(2,1)}, u32[]{:S(2)}, u32[]{:S(2)}) collective-permute-start(bf16[4,40,3840]{2,1,0:T(8,128)(2,1)S(1)} %get-tuple-element.132.refs_0_), channel_id=1, source_target_pairs={{0,4},{4,0},{1,5},{5,1},{2,6},{6,2},{3,7},{7,3},{8,12},{12,8},{9,1... | collective-permute-start | bytes 3686408 | tf_op jit(solution)/shard_map/ppermute | solution.py:870
  203.4 27.2 %collective-permute-start.23 = (bf16[4,40,3840]{2,1,0:T(8,128)(2,1)S(1)}, bf16[4,40,3840]{2,1,0:T(8,128)(2,1)}, u32[]{:S(2)}, u32[]{:S(2)}) collective-permute-start(bf16[4,40,3840]{2,1,0:T(8,128)(2,1)S(1)} %get-tuple-element.132.refs_0_), channel_id=1, source_target_pairs={{0,1},{1,0},{2,3},{3,2},{4,5},{5,4},{6,7},{7,6},{8,9},{9,8},{10,11... | collective-permute-start | bytes 3686408 | tf_op jit(solution)/shard_map/ppermute | solution.py:870
  241.6 19.6 %collective-permute-start.28 = (bf16[128,1280]{1,0:T(8,128)(2,1)}, bf16[128,1280]{1,0:T(8,128)(2,1)}, u32[]{:S(2)}, u32[]{:S(2)}) collective-permute-start(bf16[128,1280]{1,0:T(8,128)(2,1)} %dynamic-slice_bitcast_fusion.3), channel_id=1, source_target_pairs={{0,4},{4,0},{1,5},{5,1},{2,6},{6,2},{3,7},{7,3},{8,12},{12,8},{9,1... | collective-permute-start | bytes 983048 | tf_op jit(solution)/shard_map/ppermute | solution.py:870
  252.1 106.8 %reduce-scatter.5.cloned.1.call-start = ((), (), s32[]{:S(2)}) async-start(), calls=%async_computation.12 | async-start | bytes 3276800 | tf_op jit(solution)/shard_map/reduce_scatter | solution.py:920
  304.5 17.1 %collective-permute-start.33 = (bf16[2,128,1280]{2,1,0:T(8,128)(2,1)}, bf16[2,128,1280]{2,1,0:T(8,128)(2,1)}, u32[]{:S(2)}, u32[]{:S(2)}) collective-permute-start(bf16[2,128,1280]{2,1,0:T(8,128)(2,1)} %fusion.83), channel_id=1, source_target_pairs={{0,2},{1,3},{2,0},{3,1},{4,6},{5,7},{6,4},{7,5},{8,10},{9,11},{10,... | collective-permute-start | bytes 1966088 | tf_op jit(solution)/shard_map/ppermute | solution.py:870
  306.3 42.4 %collective-permute-start.34 = (bf16[4,40,3840]{2,1,0:T(8,128)(2,1)}, bf16[4,40,3840]{2,1,0:T(8,128)(2,1)}, u32[]{:S(2)}, u32[]{:S(2)}) collective-permute-start(bf16[4,40,3840]{2,1,0:T(8,128)(2,1)} %pad_maximum_fusion), channel_id=1, source_target_pairs={{0,4},{4,0},{1,5},{5,1},{2,6},{6,2},{3,7},{7,3},{8,12},{12,8},{9,1... | collective-permute-start | bytes 3686408 | tf_op jit(solution)/shard_map/ppermute | solution.py:870
  323.2 35.7 %collective-permute-start.35 = (bf16[4,40,3840]{2,1,0:T(8,128)(2,1)}, bf16[4,40,3840]{2,1,0:T(8,128)(2,1)}, u32[]{:S(2)}, u32[]{:S(2)}) collective-permute-start(bf16[4,40,3840]{2,1,0:T(8,128)(2,1)} %pad_maximum_fusion.1), channel_id=1, source_target_pairs={{0,2},{1,3},{2,0},{3,1},{4,6},{5,7},{6,4},{7,5},{8,10},{9,11},{10,... | collective-permute-start | bytes 3686408 | tf_op jit(solution)/shard_map/ppermute | solution.py:870
  335.9 23.0 %all-to-all-start.5 = ((bf16[4,320,256]{2,1,0:T(8,128)(2,1)}), bf16[4,320,256]{2,1,0:T(8,128)(2,1)}, u32[]{:S(2)}, u32[]{:S(2)}) async-start(bf16[4,320,256]{2,1,0:T(8,128)(2,1)} %bitcast.64), calls=%async_computation.5 | async-start | bytes 1310720 | tf_op jit(solution)/shard_map/all_to_all | solution.py:891
  340.1 63.7 %reduce-scatter.7.cloned.1.call-start = ((), (), s32[]{:S(2)}) async-start(), calls=%async_computation.13 | async-start | bytes 1536000 | tf_op jit(solution)/shard_map/reduce_scatter | solution.py:920
  358.9 25.7 %collective-permute-start.37 = (bf16[2,2,4,40,3840]{4,3,2,1,0:T(8,128)(2,1)}, bf16[2,2,4,40,3840]{4,3,2,1,0:T(8,128)(2,1)}, u32[]{:S(2)}, u32[]{:S(2)}) collective-permute-start(bf16[2,2,4,40,3840]{4,3,2,1,0:T(8,128)(2,1)} %get-tuple-element.179), channel_id=1, source_target_pairs={{0,1},{1,0},{2,3},{3,2},{4,5},{5,4},{6,7},{7,6},{8,9},{9,8},{10,11... | collective-permute-start | bytes 14745608 | tf_op jit(solution)/shard_map/ppermute | solution.py:870
  361.5 85.7 %reduce-scatter.9.cloned.1.call-start = ((), (), s32[]{:S(2)}) async-start(), calls=%async_computation.14 | async-start | bytes 3276800 | tf_op jit(solution)/shard_map/reduce_scatter | solution.py:920
  384.6 100.8 %reduce-scatter.11.cloned.1.call-start = ((), (), s32[]{:S(2)}) async-start(), calls=%async_computation.15 | async-start | bytes 1536000 | tf_op jit(solution)/shard_map/reduce_scatter | solution.py:920
  390.7 16.3 %collective-permute-start.38 = (bf16[4,40,1920]{2,1,0:T(8,128)(2,1)}, bf16[4,40,1920]{2,1,0:T(8,128)(2,1)}, u32[]{:S(2)}, u32[]{:S(2)}) collective-permute-start(bf16[4,40,1920]{2,1,0:T(8,128)(2,1)} %get-tuple-element.186), channel_id=1, source_target_pairs={{0,4},{4,0},{1,5},{5,1},{2,6},{6,2},{3,7},{7,3},{8,12},{12,8},{9,1... | collective-permute-start | bytes 1843208 | tf_op jit(solution)/shard_map/ppermute | solution.py:870
  414.9 29.5 %collective-permute-start.42 = (bf16[2,2,128,1280]{3,2,1,0:T(8,128)(2,1)S(1)}, bf16[2,2,128,1280]{3,2,1,0:T(8,128)(2,1)S(1)}, u32[]{:S(2)}, u32[]{:S(2)}) collective-permute-start(bf16[2,2,128,1280]{3,2,1,0:T(8,128)(2,1)S(1)} %copy-done.61), channel_id=1, source_target_pairs={{0,1},{1,0},{2,3},{3,2},{4,5},{5,4},{6,7},{7,6},{8,9},{9,8},{10,11... | collective-permute-start | bytes 3932168 | tf_op jit(solution)/shard_map/ppermute | solution.py:870
  414.9 31.2 %collective-permute-start.43 = (bf16[4,40,3840]{2,1,0:T(8,128)(2,1)S(1)}, bf16[4,40,3840]{2,1,0:T(8,128)(2,1)S(1)}, u32[]{:S(2)}, u32[]{:S(2)}) collective-permute-start(bf16[4,40,3840]{2,1,0:T(8,128)(2,1)S(1)} %pad_maximum_fusion.2), channel_id=1, source_target_pairs={{0,4},{4,0},{1,5},{5,1},{2,6},{6,2},{3,7},{7,3},{8,12},{12,8},{9,1... | collective-permute-start | bytes 3686408 | tf_op jit(solution)/shard_map/ppermute | solution.py:870
  416.5 30.7 %collective-permute-start.44 = (bf16[4,40,3840]{2,1,0:T(8,128)(2,1)S(1)}, bf16[4,40,3840]{2,1,0:T(8,128)(2,1)}, u32[]{:S(2)}, u32[]{:S(2)}) collective-permute-start(bf16[4,40,3840]{2,1,0:T(8,128)(2,1)S(1)} %pad_maximum_fusion.3), channel_id=1, source_target_pairs={{0,2},{1,3},{2,0},{3,1},{4,6},{5,7},{6,4},{7,5},{8,10},{9,11},{10,... | collective-permute-start | bytes 3686408 | tf_op jit(solution)/shard_map/ppermute | solution.py:870
  426.7 17.8 %collective-permute-start.47 = (f32[2,80]{1,0:T(2,128)S(1)}, f32[2,80]{1,0:T(2,128)S(1)}, u32[]{:S(2)}, u32[]{:S(2)}) collective-permute-start(f32[2,80]{1,0:T(2,128)S(1)} %add.391), channel_id=1, source_target_pairs={{0,4},{4,0},{1,5},{5,1},{2,6},{6,2},{3,7},{7,3},{8,12},{12,8},{9,1... | collective-permute-start | bytes 1928 | tf_op jit(solution)/shard_map/ppermute | solution.py:870
  452.7 17.9 %collective-permute-start.48 = (bf16[2,128,1280]{2,1,0:T(8,128)(2,1)}, bf16[2,128,1280]{2,1,0:T(8,128)(2,1)}, u32[]{:S(2)}, u32[]{:S(2)}) collective-permute-start(bf16[2,128,1280]{2,1,0:T(8,128)(2,1)} %fusion.84), channel_id=1, source_target_pairs={{0,2},{1,3},{2,0},{3,1},{4,6},{5,7},{6,4},{7,5},{8,10},{9,11},{10,... | collective-permute-start | bytes 1966088 | tf_op jit(solution)/shard_map/ppermute | solution.py:870
  454.7 22.6 %collective-permute-start.50 = (bf16[160,960]{1,0:T(8,128)(2,1)}, bf16[160,960]{1,0:T(8,128)(2,1)}, u32[]{:S(2)}, u32[]{:S(2)}) collective-permute-start(bf16[160,960]{1,0:T(8,128)(2,1)} %dynamic-slice_bitcast_fusion), channel_id=1, source_target_pairs={{0,4},{4,0},{1,5},{5,1},{2,6},{6,2},{3,7},{7,3},{8,12},{12,8},{9,1... | collective-permute-start | bytes 921608 | tf_op jit(solution)/shard_map/ppermute | solution.py:870
  456.3 20.3 %all-to-all-start.7 = ((bf16[4,40,960]{2,1,0:T(8,128)(2,1)}), bf16[4,40,960]{2,1,0:T(8,128)(2,1)S(1)}, u32[]{:S(2)}, u32[]{:S(2)}) async-start(bf16[4,40,960]{2,1,0:T(8,128)(2,1)} %bitcast.92), calls=%async_computation.11 | async-start | bytes 655360 | tf_op jit(solution)/shard_map/all_to_all | solution.py:891
  (100 other events, 819.4 us)
Sparse Core Ops, SparseCore 0:
  26.0 32.0 all-gather.6
  60.2 30.2 all-gather.8
  92.1 51.1 all-gather.10
  306.4 50.4 reduce-scatter.4
  361.6 29.8 reduce-scatter.6
  393.7 50.8 reduce-scatter.8
  456.4 28.9 reduce-scatter.10

commit v26 on v24

--- a/solution.py
+++ b/solution.py
@@ -618,7 +618,7 @@
 
 def assemble_kernel(place_ref, *refs):
     pieces, whole_ref = refs[:10], refs[10]
-    half = whole_ref.shape[-1] // 2
+    split = pieces[3].shape[-1]
     blk, row, core = place_ref[0], place_ref[1], place_ref[2]
     for i in range(2):
         at_core = core if i == 0 else 1 - core
@@ -626,8 +626,8 @@
         whole_ref[0, blk, row, at_core] = own[0]
         whole_ref[0, 1 - blk, row, at_core] = across[0]
         whole_ref[0, blk, 1 - row, at_core] = beside[0]
-        whole_ref[0, 1 - blk, 1 - row, at_core, :, :half] = one[0]
-        whole_ref[0, 1 - blk, 1 - row, at_core, :, half:] = two[0]
+        whole_ref[0, 1 - blk, 1 - row, at_core, :, :split] = one[0]
+        whole_ref[0, 1 - blk, 1 - row, at_core, :, split:] = two[0]
 
 
 def assemble(pieces):
@@ -909,11 +909,11 @@
 
 
 def to_beside(across):
-    return swapped(across[..., : across.shape[-1] // 2], "head", 2)
+    return swapped(across[..., : across.shape[-1] // 3], "head", 2)
 
 
 def to_across(beside):
-    return swapped(beside[..., beside.shape[-1] // 2 :], "blk", 1)
+    return swapped(beside[..., beside.shape[-1] // 3 :], "blk", 1)
 
 
 def over_batch(parts):

time: 514 us -> 518 us (level)
  blocking collectives: 18.7 us -> 0 us
  waiting for transfers between devices: 183 us -> 201 us
    ppermute x51, waiting for transfers between devices: 131 us -> 158 us  [swapped(): return lax.ppermute(array, axis, [(i, i ^ mask) for i in range(size)])]
    all_to_all x1 -> x0, blocking collectives: 18.7 us -> none  [over_head(): lax.all_to_all(parts, 'head', split_axis=0, concat_axis=0, tiled=True)]
    all_to_all x7 -> x8, starting transfers between devices: 25.9 us -> 29.6 us  [over_head(): lax.all_to_all(parts, 'head', split_axis=0, concat_axis=0, tiled=True)]
    all_to_all x7 -> x8, waiting for transfers between devices: 27.1 us -> 24.5 us  [over_head(): lax.all_to_all(parts, 'head', split_axis=0, concat_axis=0, tiled=True)]
    unnamed x136 -> x152, local copies, waits for them, and re-layouts: 11.6 us -> 11.8 us
  transfers between devices with their start and end apart: 65 -> 66, of which waited for: 32 -> 32; matrix products, arithmetic and copies ran while one was open for 14% -> 14% of each run, Pallas kernels for 22% -> 21%
where the time goes in v26:
time: 518 us; the launch traced here: 510 us
  waiting for transfers between devices  201 us (39%)
  Pallas kernels  114 us (22%)
  starting transfers between devices  73.5 us (14%)
  other arithmetic  51.3 us (10%)
  local copies, waits for them, and re-layouts  34.9 us (7%)
  matrix products  20.6 us (4%)
  between operations  15.7 us (3%)
    ppermute x51, waiting for transfers between devices, swapped(): return lax.ppermute(array, axis, [(i, i ^ mask) for i in range(size)])  158 us
    ppermute x51, starting transfers between devices, swapped(): return lax.ppermute(array, axis, [(i, i ^ mask) for i in range(size)])  43 us
    all_to_all x8, starting transfers between devices, over_head(): lax.all_to_all(parts, 'head', split_axis=0, concat_axis=0, tiled=True)  29.6 us
    pallas_call x2, Pallas kernels, attend_back_rows(): pl.pallas_call(functools.partial(attend_back_kernel, token_rows), grid=(l...  24.7 us
    all_to_all x8, waiting for transfers between devices, over_head(): lax.all_to_all(parts, 'head', split_axis=0, concat_axis=0, tiled=True)  24.5 us
    all_gather x3, waiting for transfers between devices, along_batch(): return lax.all_gather(piece, 'batch', axis=0, tiled=False)  17.7 us
    pallas_call x2, Pallas kernels, dense_grads(): pl.pallas_call(dense_grad_kernel, grid_spec=pltpu.PrefetchScalarGridSpec(...  17.1 us
    pallas_call x2, Pallas kernels, project(): pl.pallas_call(functools.partial(project_kernel, with_norm), grid_spec=pl...  14.3 us
  transfers between devices with their start and end apart: 66, of which 32 were waited for; matrix products, arithmetic and copies ran while one was open for 14% of the time, Pallas kernels for 21%

profile of v26, /device:TPU:0, one launch (start us, length us, event | category | flops | bytes accessed | tf_op | source)
XLA Modules:
  0.0 510.3 jit_solution(5360541256636119327)
XLA Ops:
  19.1 6.0 %all-to-all-done = bf16[4,40,964]{2,1,0:T(8,128)(2,1)S(1)} async-done(((bf16[4,40,964]{2,1,0:T(8,128)(2,1)}), bf16[4,40,964]{2,1,0:T(8,128)(2,1)S(1)}, u32[]{:S(2)}, u32[]{:S(2)}) %all-to-all-start) | async-done | bytes 308512 | tf_op jit(solution)/shard_map/all_to_all | solution.py:891
  27.2 15.1 %collective-permute-done.2.refs_2_ = bf16[256,1280]{1,0:T(8,128)(2,1)S(1)} collective-permute-done((bf16[256,1280]{1,0:T(8,128)(2,1)S(1)}, bf16[256,1280]{1,0:T(8,128)(2,1)S(1)}, u32[]{:S(2)}, u32[]{:S(2)}) %collective-permute-start.2) | collective-permute-done | bytes 655392 | tf_op jit(solution)/shard_map/ppermute | solution.py:870
  45.4 12.7 %all-gather.7.cloned.1.call-done = bf16[640,964]{1,0:T(8,128)(2,1)} async-done(((bf16[160,964]{1,0:T(8,128)(2,1)}), bf16[640,964]{1,0:T(8,128)(2,1)}) %all-gather.7.cloned.1.call-update) | async-done | bytes 1233936 | tf_op jit(solution)/shard_map/all_gather | solution.py:904
  64.8 6.6 %all-to-all-done.1 = bf16[4,40,960]{2,1,0:T(8,128)(2,1)S(1)} async-done(((bf16[4,40,960]{2,1,0:T(8,128)(2,1)}), bf16[4,40,960]{2,1,0:T(8,128)(2,1)S(1)}, u32[]{:S(2)}, u32[]{:S(2)}) %all-to-all-start.1) | async-done | bytes 307232 | tf_op jit(solution)/shard_map/all_to_all | solution.py:891
  71.7 16.5 %collective-permute-done.5.across_ref = bf16[4,160,964]{2,1,0:T(8,128)(2,1)S(1)} collective-permute-done((bf16[4,160,964]{2,1,0:T(8,128)(2,1)}, bf16[4,160,964]{2,1,0:T(8,128)(2,1)S(1)}, u32[]{:S(2)}, u32[]{:S(2)}) %collective-permute-start.5) | collective-permute-done | bytes 1233952 | tf_op jit(solution)/shard_map/ppermute | solution.py:870
  94.9 4.6 shard_map.169
  101.5 7.7 %shard_map.170 = (bf16[1024,1280]{1,0:T(8,128)(2,1)}, f32[960,1024]{1,0:T(8,128)S(1)}) custom-call(s32[3]{0:T(128)S(1)} %pad_add_fusion.place_ref.core_ref, bf16[256,1280]{1,0:T(8,128)(2,1)} %bitcast.227, bf16[256,1280]{1,0:T(8,128)(2,1)} %copy-done.55, bf16[256,1280]{1,0:T(8,128)(2,1)} %copy-done.54, bf16[256,1280]{1,0:T(8,128)(2,1)} %collective-permute-done.3.refs_3_, ...), custom_call_target="tpu_custom_call" | custom-call | flops 1048576 | bytes 1048576 | tf_op jit(solution)/shard_map/pallas_call | solution.py:733
  109.2 6.7 %shard_map.171 = (bf16[4,4,80,256]{3,2,1,0:T(8,128)(2,1)}, f32[4,1,1024]{2,1,0:T(1,128)S(1)}) custom-call(f32[3,4,80,1024]{3,2,1,0:T(8,128)S(1)} %bitcast.197, f32[80,1]{1,0:T(8,128)S(1)} %copy.60.scale_ref, s32[1024,1]{1,0:T(8,128)S(1)} %copy.61.col_ref, s32[1,1024]{1,0:T(1,128)S(1)} %constant_dynamic-slice_fusion.row_ref), custom_call_target="tpu_custom_call" | custom-call | flops 1048576 | bytes 1048576 | tf_op jit(solution)/shard_map/pallas_call | solution.py:435
  130.9 9.7 %collective-permute-done.9.refs_4_ = bf16[4,40,2560]{2,1,0:T(8,128)(2,1)} collective-permute-done((bf16[4,40,2560]{2,1,0:T(8,128)(2,1)}, bf16[4,40,2560]{2,1,0:T(8,128)(2,1)}, u32[]{:S(2)}, u32[]{:S(2)}) %collective-permute-start.9) | collective-permute-done | bytes 819232 | tf_op jit(solution)/shard_map/ppermute | solution.py:870
  149.7 4.4 shard_map.172
  161.5 17.0 %collective-permute-done.16.across_ref = bf16[4,40,3840]{2,1,0:T(8,128)(2,1)S(1)} collective-permute-done((bf16[4,40,3840]{2,1,0:T(8,128)(2,1)S(1)}, bf16[4,40,3840]{2,1,0:T(8,128)(2,1)S(1)}, u32[]{:S(2)}, u32[]{:S(2)}) %collective-permute-start.16) | collective-permute-done | bytes 1228832 | tf_op jit(solution)/shard_map/ppermute | solution.py:870
  180.8 4.8 shard_map.173
  185.5 6.6 %shard_map.174 = (bf16[1024,1280]{1,0:T(8,128)(2,1)}, f32[960,1024]{1,0:T(8,128)S(1)}) custom-call(s32[3]{0:T(128)S(1)} %pad_add_fusion.place_ref.core_ref, bf16[256,1280]{1,0:T(8,128)(2,1)} %multiply_convert_fusion.2.refs_0_, bf16[256,1280]{1,0:T(8,128)(2,1)} %collective-permute-done.17.refs_1_, bf16[256,1280]{1,0:T(8,128)(2,1)} %collective-permute-done.15.refs_2_, ...), custom_call_target="tpu_custom_call" | custom-call | flops 1048576 | bytes 1048576 | tf_op jit(solution)/shard_map/pallas_call | solution.py:733
  192.2 6.1 %shard_map.175 = (bf16[4,4,80,256]{3,2,1,0:T(8,128)(2,1)S(1)}, f32[4,1,1024]{2,1,0:T(1,128)S(1)}) custom-call(f32[3,4,80,1024]{3,2,1,0:T(8,128)S(1)} %bitcast.199, f32[80,1]{1,0:T(8,128)S(1)} %copy.64.scale_ref, s32[1024,1]{1,0:T(8,128)S(1)} %copy.61.col_ref, s32[1,1024]{1,0:T(1,128)S(1)} %constant_dynamic-slice_fusion.row_ref), custom_call_target="tpu_custom_call" | custom-call | flops 1048576 | bytes 1048576 | tf_op jit(solution)/shard_map/pallas_call | solution.py:435
  198.3 9.0 %collective-permute-done.20.refs_2_ = bf16[4,40,3840]{2,1,0:T(8,128)(2,1)S(1)} collective-permute-done((bf16[4,40,3840]{2,1,0:T(8,128)(2,1)S(1)}, bf16[4,40,3840]{2,1,0:T(8,128)(2,1)S(1)}, u32[]{:S(2)}, u32[]{:S(2)}) %collective-permute-start.20) | collective-permute-done | bytes 1228832 | tf_op jit(solution)/shard_map/ppermute | solution.py:870
  209.3 4.4 all-to-all-start.3
  217.3 15.4 %collective-permute-done.21.refs_3_ = bf16[4,40,1280]{2,1,0:T(8,128)(2,1)S(1)} collective-permute-done((bf16[4,40,1280]{2,1,0:T(8,128)(2,1)S(1)}, bf16[4,40,1280]{2,1,0:T(8,128)(2,1)S(1)}, u32[]{:S(2)}, u32[]{:S(2)}) %collective-permute-start.21) | collective-permute-done | bytes 409632 | tf_op jit(solution)/shard_map/ppermute | solution.py:870
  235.7 4.1 shard_map.176
  255.9 8.6 %shard_map.177 = (bf16[2,2,4,40,3840]{4,3,2,1,0:T(8,128)(2,1)}, bf16[2,2,4,40,3840]{4,3,2,1,0:T(8,128)(2,1)}) custom-call(s32[3]{0:T(128)S(1)} %pad_add_fusion.place_ref.core_ref, bf16[1280,256]{1,0:T(8,128)(2,1)} %bitcast.49.attended_ref, bf16[256,1280]{1,0:T(8,128)(2,1)} %copy-done.29, bf16[256,1280]{1,0:T(8,128)(2,1)} %copy-done.52, ...), custom_call_target="tpu_custom_call" | custom-call | flops 1048576 | bytes 1048576 | tf_op jit(solution)/shard_map/pallas_call | solution.py:599
  267.3 12.4 %shard_map.178 = (bf16[3,4,80,1024]{3,2,1,0:T(8,128)(2,1)}, f32[80,128]{1,0:T(8,128)}) custom-call(f32[3,4,80,1024]{3,2,1,0:T(8,128)} %bitcast.200, bf16[4,4,80,256]{3,2,1,0:T(8,128)(2,1)} %bitcast.238, f32[4,1,1024]{2,1,0:T(1,128)S(1)} %get-tuple-element.156.lse_ref, f32[80,1]{1,0:T(8,128)S(1)} %copy.64.scale_ref, s32[1024,1]{1,0:T(8,128)S(1)} %copy.61.col_ref, ...), custom_call_target="tpu_custom_call" | custom-call | flops 1048576 | bytes 1048576 | tf_op jit(solution)/shard_map/pallas_call | solution.py:528
  285.9 11.2 %shard_map.179 = (f32[2,2,128,1280]{3,2,1,0:T(8,128)}, bf16[2,2,128,1280]{3,2,1,0:T(8,128)(2,1)}, bf16[1280,960]{1,0:T(8,128)(2,1)}) custom-call(s32[3]{0:T(128)S(1)} %pad_add_fusion.place_ref.core_ref, bf16[960,1024]{1,0:T(8,128)(2,1)} %bitcast.240, bf16[1280,960]{1,0:T(8,128)(2,1)} %bitcast.217, bf16[1024,1280]{1,0:T(8,128)(2,1)} %get-tuple-element.163.normed_ref), custom_call_target="tpu_custom_call" | custom-call | flops 1048576 | bytes 1048576 | tf_op jit(solution)/shard_map/pallas_call | solution.py:779
  313.1 14.1 %collective-permute-done.33 = bf16[2,128,1280]{2,1,0:T(8,128)(2,1)} collective-permute-done((bf16[2,128,1280]{2,1,0:T(8,128)(2,1)}, bf16[2,128,1280]{2,1,0:T(8,128)(2,1)}, u32[]{:S(2)}, u32[]{:S(2)}) %collective-permute-start.33) | collective-permute-done | bytes 655392 | tf_op jit(solution)/shard_map/ppermute | solution.py:870
  341.6 4.2 all-to-all-start.5
  345.8 8.5 %shard_map.180 = (bf16[2,2,4,40,3840]{4,3,2,1,0:T(8,128)(2,1)}, bf16[2,2,4,40,3840]{4,3,2,1,0:T(8,128)(2,1)}) custom-call(s32[3]{0:T(128)S(1)} %pad_add_fusion.place_ref.core_ref, bf16[1280,256]{1,0:T(8,128)(2,1)} %bitcast.236, bf16[256,1280]{1,0:T(8,128)(2,1)} %copy-done.28, bf16[256,1280]{1,0:T(8,128)(2,1)} %copy-done.48, bf16[256,1280]{1,0:T(8,128)(2,1)} %copy-done.34, ...), custom_call_target="tpu_custom_call" | custom-call | flops 1048576 | bytes 1048576 | tf_op jit(solution)/shard_map/pallas_call | solution.py:599
  356.8 7.8 %all-to-all-done.5 = bf16[4,320,256]{2,1,0:T(8,128)(2,1)} async-done(((bf16[4,320,256]{2,1,0:T(8,128)(2,1)}), bf16[4,320,256]{2,1,0:T(8,128)(2,1)}, u32[]{:S(2)}, u32[]{:S(2)}) %all-to-all-start.5) | async-done | bytes 655392 | tf_op jit(solution)/shard_map/all_to_all | solution.py:891
  369.6 12.3 %shard_map.181 = (bf16[3,4,80,1024]{3,2,1,0:T(8,128)(2,1)}, f32[80,128]{1,0:T(8,128)}) custom-call(f32[3,4,80,1024]{3,2,1,0:T(8,128)} %bitcast.198, bf16[4,4,80,256]{3,2,1,0:T(8,128)(2,1)} %bitcast.68.grad_ref, f32[4,1,1024]{2,1,0:T(1,128)S(1)} %get-tuple-element.186.lse_ref, f32[80,1]{1,0:T(8,128)S(1)} %copy.60.scale_ref, s32[1024,1]{1,0:T(8,128)S(1)} %copy.61.col_ref, ...), custom_call_target="tpu_custom_call" | custom-call | flops 1048576 | bytes 1048576 | tf_op jit(solution)/shard_map/pallas_call | solution.py:528
  382.7 7.3 %shard_map.182 = bf16[1280,960]{1,0:T(8,128)(2,1)} custom-call(bf16[960,1024]{1,0:T(8,128)(2,1)} %bitcast.231, bf16[1024,1280]{1,0:T(8,128)(2,1)} %get-tuple-element.190.normed_ref), custom_call_target="tpu_custom_call" | custom-call | flops 1048576 | bytes 1048576 | tf_op jit(solution)/shard_map/pallas_call | solution.py:850
  390.3 4.9 add_bitcast_fusion
  401.2 8.2 %shard_map.183 = (f32[2,2,128,1280]{3,2,1,0:T(8,128)}, bf16[2,2,128,1280]{3,2,1,0:T(8,128)(2,1)}) custom-call(s32[3]{0:T(128)S(1)} %pad_add_fusion.place_ref.core_ref, bf16[960,1024]{1,0:T(8,128)(2,1)} %bitcast.232, bf16[1280,960]{1,0:T(8,128)(2,1)} %bitcast.224), custom_call_target="tpu_custom_call" | custom-call | flops 1048576 | bytes 1048576 | tf_op jit(solution)/shard_map/pallas_call | solution.py:820
  433.1 17.1 %collective-permute-done.47 = f32[2,80]{1,0:T(2,128)S(1)} collective-permute-done((f32[2,80]{1,0:T(2,128)S(1)}, f32[2,80]{1,0:T(2,128)S(1)}, u32[]{:S(2)}, u32[]{:S(2)}) %collective-permute-start.47) | collective-permute-done | bytes 672 | tf_op jit(solution)/shard_map/ppermute | solution.py:870
  464.4 12.0 %collective-permute-done.48 = bf16[2,128,1280]{2,1,0:T(8,128)(2,1)} collective-permute-done((bf16[2,128,1280]{2,1,0:T(8,128)(2,1)}, bf16[2,128,1280]{2,1,0:T(8,128)(2,1)}, u32[]{:S(2)}, u32[]{:S(2)}) %collective-permute-start.48) | collective-permute-done | bytes 655392 | tf_op jit(solution)/shard_map/ppermute | solution.py:870
  483.8 4.2 collective-permute-done.49
  (399 shorter events, 204.2 us)
Async XLA Ops:
  18.4 39.7 %all-gather.7.cloned.1.call-start = ((), (), s32[]{:S(2)}) async-start(), calls=%async_computation.16 | async-start | bytes 1638400 | tf_op jit(solution)/shard_map/all_gather | solution.py:904
  25.8 64.7 %all-gather.9.cloned.1.call-start = ((), (), s32[]{:S(2)}) async-start(), calls=%async_computation.17 | async-start | bytes 1536000 | tf_op jit(solution)/shard_map/all_gather | solution.py:904
  58.1 30.1 %collective-permute-start.5 = (bf16[4,160,964]{2,1,0:T(8,128)(2,1)}, bf16[4,160,964]{2,1,0:T(8,128)(2,1)S(1)}, u32[]{:S(2)}, u32[]{:S(2)}) collective-permute-start(bf16[4,160,964]{2,1,0:T(8,128)(2,1)} %bitcast.246), channel_id=1, source_target_pairs={{0,4},{4,0},{1,5},{5,1},{2,6},{6,2},{3,7},{7,3},{8,12},{12,8},{9,1... | collective-permute-start | bytes 3701768 | tf_op jit(solution)/shard_map/ppermute | solution.py:870
  64.8 78.5 %all-gather.11.cloned.1.call-start = ((), (), s32[]{:S(2)}) async-start(), calls=%async_computation.18 | async-start | bytes 3072000 | tf_op jit(solution)/shard_map/all_gather | solution.py:904
  91.5 28.4 %collective-permute-start.7 = (bf16[4,40,3840]{2,1,0:T(8,128)(2,1)}, bf16[4,40,3840]{2,1,0:T(8,128)(2,1)S(1)}, u32[]{:S(2)}, u32[]{:S(2)}) collective-permute-start(bf16[4,40,3840]{2,1,0:T(8,128)(2,1)} %bitcast.19.refs_0_), channel_id=1, source_target_pairs={{0,2},{1,3},{2,0},{3,1},{4,6},{5,7},{6,4},{7,5},{8,10},{9,11},{10,... | collective-permute-start | bytes 3686408 | tf_op jit(solution)/shard_map/ppermute | solution.py:870
  93.0 28.2 %collective-permute-start.6 = (bf16[4,40,3840]{2,1,0:T(8,128)(2,1)}, bf16[4,40,3840]{2,1,0:T(8,128)(2,1)}, u32[]{:S(2)}, u32[]{:S(2)}) collective-permute-start(bf16[4,40,3840]{2,1,0:T(8,128)(2,1)} %bitcast.19.refs_0_), channel_id=1, source_target_pairs={{0,4},{4,0},{1,5},{5,1},{2,6},{6,2},{3,7},{7,3},{8,12},{12,8},{9,1... | collective-permute-start | bytes 3686408 | tf_op jit(solution)/shard_map/ppermute | solution.py:870
  122.1 18.5 %collective-permute-start.9 = (bf16[4,40,2560]{2,1,0:T(8,128)(2,1)}, bf16[4,40,2560]{2,1,0:T(8,128)(2,1)}, u32[]{:S(2)}, u32[]{:S(2)}) collective-permute-start(bf16[4,40,2560]{2,1,0:T(8,128)(2,1)} %slice.154), channel_id=1, source_target_pairs={{0,4},{4,0},{1,5},{5,1},{2,6},{6,2},{3,7},{7,3},{8,12},{12,8},{9,1... | collective-permute-start | bytes 2457608 | tf_op jit(solution)/shard_map/ppermute | solution.py:870
  123.6 22.7 %all-to-all-start.2 = ((bf16[4,320,256]{2,1,0:T(8,128)(2,1)}), bf16[4,320,256]{2,1,0:T(8,128)(2,1)S(1)}, u32[]{:S(2)}, u32[]{:S(2)}) async-start(bf16[4,320,256]{2,1,0:T(8,128)(2,1)} %bitcast.31), calls=%async_computation.2 | async-start | bytes 1310720 | tf_op jit(solution)/shard_map/all_to_all | solution.py:891
  130.4 18.6 %collective-permute-start.10 = (bf16[4,40,3840]{2,1,0:T(8,128)(2,1)}, bf16[4,40,3840]{2,1,0:T(8,128)(2,1)}, u32[]{:S(2)}, u32[]{:S(2)}) collective-permute-start(bf16[4,40,3840]{2,1,0:T(8,128)(2,1)} %bitcast.19.refs_0_), channel_id=1, source_target_pairs={{0,1},{1,0},{2,3},{3,2},{4,5},{5,4},{6,7},{7,6},{8,9},{9,8},{10,11... | collective-permute-start | bytes 3686408 | tf_op jit(solution)/shard_map/ppermute | solution.py:870
  130.4 19.2 %collective-permute-start.11 = (bf16[4,40,3840]{2,1,0:T(8,128)(2,1)}, bf16[4,40,3840]{2,1,0:T(8,128)(2,1)}, u32[]{:S(2)}, u32[]{:S(2)}) collective-permute-start(bf16[4,40,3840]{2,1,0:T(8,128)(2,1)} %collective-permute-done.6.refs_1_), channel_id=1, source_target_pairs={{0,1},{1,0},{2,3},{3,2},{4,5},{5,4},{6,7},{7,6},{8,9},{9,8},{10,11... | collective-permute-start | bytes 3686408 | tf_op jit(solution)/shard_map/ppermute | solution.py:870
  130.9 18.7 %collective-permute-start.12 = (bf16[4,40,3840]{2,1,0:T(8,128)(2,1)S(1)}, bf16[4,40,3840]{2,1,0:T(8,128)(2,1)}, u32[]{:S(2)}, u32[]{:S(2)}) collective-permute-start(bf16[4,40,3840]{2,1,0:T(8,128)(2,1)S(1)} %collective-permute-done.7.refs_2_), channel_id=1, source_target_pairs={{0,1},{1,0},{2,3},{3,2},{4,5},{5,4},{6,7},{7,6},{8,9},{9,8},{10,11... | collective-permute-start | bytes 3686408 | tf_op jit(solution)/shard_map/ppermute | solution.py:870
  149.0 29.5 %collective-permute-start.16 = (bf16[4,40,3840]{2,1,0:T(8,128)(2,1)S(1)}, bf16[4,40,3840]{2,1,0:T(8,128)(2,1)S(1)}, u32[]{:S(2)}, u32[]{:S(2)}) collective-permute-start(bf16[4,40,3840]{2,1,0:T(8,128)(2,1)S(1)} %get-tuple-element.249.along_ref), channel_id=1, source_target_pairs={{0,4},{4,0},{1,5},{5,1},{2,6},{6,2},{3,7},{7,3},{8,12},{12,8},{9,1... | collective-permute-start | bytes 3686408 | tf_op jit(solution)/shard_map/ppermute | solution.py:870
  178.5 28.8 %collective-permute-start.20 = (bf16[4,40,3840]{2,1,0:T(8,128)(2,1)S(1)}, bf16[4,40,3840]{2,1,0:T(8,128)(2,1)S(1)}, u32[]{:S(2)}, u32[]{:S(2)}) collective-permute-start(bf16[4,40,3840]{2,1,0:T(8,128)(2,1)S(1)} %get-tuple-element.141.refs_0_), channel_id=1, source_target_pairs={{0,2},{1,3},{2,0},{3,1},{4,6},{5,7},{6,4},{7,5},{8,10},{9,11},{10,... | collective-permute-start | bytes 3686408 | tf_op jit(solution)/shard_map/ppermute | solution.py:870
  179.0 28.6 %collective-permute-start.19 = (bf16[4,40,3840]{2,1,0:T(8,128)(2,1)S(1)}, bf16[4,40,3840]{2,1,0:T(8,128)(2,1)}, u32[]{:S(2)}, u32[]{:S(2)}) collective-permute-start(bf16[4,40,3840]{2,1,0:T(8,128)(2,1)S(1)} %get-tuple-element.141.refs_0_), channel_id=1, source_target_pairs={{0,4},{4,0},{1,5},{5,1},{2,6},{6,2},{3,7},{7,3},{8,12},{12,8},{9,1... | collective-permute-start | bytes 3686408 | tf_op jit(solution)/shard_map/ppermute | solution.py:870
  208.5 24.2 %collective-permute-start.22 = (bf16[4,40,2560]{2,1,0:T(8,128)(2,1)}, bf16[4,40,2560]{2,1,0:T(8,128)(2,1)}, u32[]{:S(2)}, u32[]{:S(2)}) collective-permute-start(bf16[4,40,2560]{2,1,0:T(8,128)(2,1)} %slice.167), channel_id=1, source_target_pairs={{0,4},{4,0},{1,5},{5,1},{2,6},{6,2},{3,7},{7,3},{8,12},{12,8},{9,1... | collective-permute-start | bytes 2457608 | tf_op jit(solution)/shard_map/ppermute | solution.py:870
  209.3 23.4 %all-to-all-start.3 = ((bf16[4,320,256]{2,1,0:T(8,128)(2,1)}), bf16[4,320,256]{2,1,0:T(8,128)(2,1)}, u32[]{:S(2)}, u32[]{:S(2)}) async-start(bf16[4,320,256]{2,1,0:T(8,128)(2,1)} %bitcast.215), calls=%async_computation.3 | async-start | bytes 1310720 | tf_op jit(solution)/shard_map/all_to_all | solution.py:891
  216.8 18.9 %collective-permute-start.24 = (bf16[4,40,3840]{2,1,0:T(8,128)(2,1)}, bf16[4,40,3840]{2,1,0:T(8,128)(2,1)}, u32[]{:S(2)}, u32[]{:S(2)}) collective-permute-start(bf16[4,40,3840]{2,1,0:T(8,128)(2,1)} %collective-permute-done.19.refs_1_), channel_id=1, source_target_pairs={{0,1},{1,0},{2,3},{3,2},{4,5},{5,4},{6,7},{7,6},{8,9},{9,8},{10,11... | collective-permute-start | bytes 3686408 | tf_op jit(solution)/shard_map/ppermute | solution.py:870
  245.3 19.2 %collective-permute-start.28 = (bf16[128,1280]{1,0:T(8,128)(2,1)}, bf16[128,1280]{1,0:T(8,128)(2,1)}, u32[]{:S(2)}, u32[]{:S(2)}) collective-permute-start(bf16[128,1280]{1,0:T(8,128)(2,1)} %dynamic-slice_bitcast_fusion.3), channel_id=1, source_target_pairs={{0,4},{4,0},{1,5},{5,1},{2,6},{6,2},{3,7},{7,3},{8,12},{12,8},{9,1... | collective-permute-start | bytes 983048 | tf_op jit(solution)/shard_map/ppermute | solution.py:870
  255.4 109.2 %reduce-scatter.5.cloned.1.call-start = ((), (), s32[]{:S(2)}) async-start(), calls=%async_computation.12 | async-start | bytes 3276800 | tf_op jit(solution)/shard_map/reduce_scatter | solution.py:920
  311.8 42.4 %collective-permute-start.34 = (bf16[4,40,3840]{2,1,0:T(8,128)(2,1)}, bf16[4,40,3840]{2,1,0:T(8,128)(2,1)}, u32[]{:S(2)}, u32[]{:S(2)}) collective-permute-start(bf16[4,40,3840]{2,1,0:T(8,128)(2,1)} %pad_maximum_fusion), channel_id=1, source_target_pairs={{0,4},{4,0},{1,5},{5,1},{2,6},{6,2},{3,7},{7,3},{8,12},{12,8},{9,1... | collective-permute-start | bytes 3686408 | tf_op jit(solution)/shard_map/ppermute | solution.py:870
  328.9 35.7 %collective-permute-start.35 = (bf16[4,40,3840]{2,1,0:T(8,128)(2,1)}, bf16[4,40,3840]{2,1,0:T(8,128)(2,1)}, u32[]{:S(2)}, u32[]{:S(2)}) collective-permute-start(bf16[4,40,3840]{2,1,0:T(8,128)(2,1)} %pad_maximum_fusion.1), channel_id=1, source_target_pairs={{0,2},{1,3},{2,0},{3,1},{4,6},{5,7},{6,4},{7,5},{8,10},{9,11},{10,... | collective-permute-start | bytes 3686408 | tf_op jit(solution)/shard_map/ppermute | solution.py:870
  341.6 23.0 %all-to-all-start.5 = ((bf16[4,320,256]{2,1,0:T(8,128)(2,1)}), bf16[4,320,256]{2,1,0:T(8,128)(2,1)}, u32[]{:S(2)}, u32[]{:S(2)}) async-start(bf16[4,320,256]{2,1,0:T(8,128)(2,1)} %bitcast.64), calls=%async_computation.5 | async-start | bytes 1310720 | tf_op jit(solution)/shard_map/all_to_all | solution.py:891
  345.7 63.6 %reduce-scatter.7.cloned.1.call-start = ((), (), s32[]{:S(2)}) async-start(), calls=%async_computation.13 | async-start | bytes 1536000 | tf_op jit(solution)/shard_map/reduce_scatter | solution.py:920
  364.6 25.4 %collective-permute-start.37 = (bf16[2,2,4,40,3840]{4,3,2,1,0:T(8,128)(2,1)}, bf16[2,2,4,40,3840]{4,3,2,1,0:T(8,128)(2,1)}, u32[]{:S(2)}, u32[]{:S(2)}) collective-permute-start(bf16[2,2,4,40,3840]{4,3,2,1,0:T(8,128)(2,1)} %get-tuple-element.191), channel_id=1, source_target_pairs={{0,1},{1,0},{2,3},{3,2},{4,5},{5,4},{6,7},{7,6},{8,9},{9,8},{10,11... | collective-permute-start | bytes 14745608 | tf_op jit(solution)/shard_map/ppermute | solution.py:870
  367.2 85.8 %reduce-scatter.9.cloned.1.call-start = ((), (), s32[]{:S(2)}) async-start(), calls=%async_computation.14 | async-start | bytes 3276800 | tf_op jit(solution)/shard_map/reduce_scatter | solution.py:920
  390.0 100.5 %reduce-scatter.11.cloned.1.call-start = ((), (), s32[]{:S(2)}) async-start(), calls=%async_computation.15 | async-start | bytes 1536000 | tf_op jit(solution)/shard_map/reduce_scatter | solution.py:920
  420.8 29.5 %collective-permute-start.42 = (bf16[2,2,128,1280]{3,2,1,0:T(8,128)(2,1)S(1)}, bf16[2,2,128,1280]{3,2,1,0:T(8,128)(2,1)S(1)}, u32[]{:S(2)}, u32[]{:S(2)}) collective-permute-start(bf16[2,2,128,1280]{3,2,1,0:T(8,128)(2,1)S(1)} %copy-done.70), channel_id=1, source_target_pairs={{0,1},{1,0},{2,3},{3,2},{4,5},{5,4},{6,7},{7,6},{8,9},{9,8},{10,11... | collective-permute-start | bytes 3932168 | tf_op jit(solution)/shard_map/ppermute | solution.py:870
  420.8 31.2 %collective-permute-start.43 = (bf16[4,40,3840]{2,1,0:T(8,128)(2,1)S(1)}, bf16[4,40,3840]{2,1,0:T(8,128)(2,1)S(1)}, u32[]{:S(2)}, u32[]{:S(2)}) collective-permute-start(bf16[4,40,3840]{2,1,0:T(8,128)(2,1)S(1)} %pad_maximum_fusion.2), channel_id=1, source_target_pairs={{0,4},{4,0},{1,5},{5,1},{2,6},{6,2},{3,7},{7,3},{8,12},{12,8},{9,1... | collective-permute-start | bytes 3686408 | tf_op jit(solution)/shard_map/ppermute | solution.py:870
  422.0 31.0 %collective-permute-start.44 = (bf16[4,40,3840]{2,1,0:T(8,128)(2,1)S(1)}, bf16[4,40,3840]{2,1,0:T(8,128)(2,1)}, u32[]{:S(2)}, u32[]{:S(2)}) collective-permute-start(bf16[4,40,3840]{2,1,0:T(8,128)(2,1)S(1)} %pad_maximum_fusion.3), channel_id=1, source_target_pairs={{0,2},{1,3},{2,0},{3,1},{4,6},{5,7},{6,4},{7,5},{8,10},{9,11},{10,... | collective-permute-start | bytes 3686408 | tf_op jit(solution)/shard_map/ppermute | solution.py:870
  431.6 18.6 %collective-permute-start.47 = (f32[2,80]{1,0:T(2,128)S(1)}, f32[2,80]{1,0:T(2,128)S(1)}, u32[]{:S(2)}, u32[]{:S(2)}) collective-permute-start(f32[2,80]{1,0:T(2,128)S(1)} %add.391), channel_id=1, source_target_pairs={{0,4},{4,0},{1,5},{5,1},{2,6},{6,2},{3,7},{7,3},{8,12},{12,8},{9,1... | collective-permute-start | bytes 1928 | tf_op jit(solution)/shard_map/ppermute | solution.py:870
  459.7 23.2 %collective-permute-start.50 = (bf16[160,960]{1,0:T(8,128)(2,1)}, bf16[160,960]{1,0:T(8,128)(2,1)S(1)}, u32[]{:S(2)}, u32[]{:S(2)}) collective-permute-start(bf16[160,960]{1,0:T(8,128)(2,1)} %dynamic-slice_bitcast_fusion), channel_id=1, source_target_pairs={{0,4},{4,0},{1,5},{5,1},{2,6},{6,2},{3,7},{7,3},{8,12},{12,8},{9,1... | collective-permute-start | bytes 921608 | tf_op jit(solution)/shard_map/ppermute | solution.py:870
  460.9 21.2 %all-to-all-start.7 = ((bf16[4,40,960]{2,1,0:T(8,128)(2,1)}), bf16[4,40,960]{2,1,0:T(8,128)(2,1)S(1)}, u32[]{:S(2)}, u32[]{:S(2)}) async-start(bf16[4,40,960]{2,1,0:T(8,128)(2,1)} %bitcast.92), calls=%async_computation.11 | async-start | bytes 655360 | tf_op jit(solution)/shard_map/all_to_all | solution.py:891
  (110 other events, 873.4 us)
Sparse Core Ops, SparseCore 0:
  26.0 32.0 all-gather.6
  60.2 30.2 all-gather.8
  92.1 51.1 all-gather.10
  312.0 50.8 reduce-scatter.4
  367.3 30.0 reduce-scatter.6
  399.7 50.8 reduce-scatter.8
  461.1 29.3 reduce-scatter.10

commit v27 on v24

--- a/solution.py
+++ b/solution.py
@@ -1006,11 +1006,11 @@
         jnp.concatenate([out_weight[i], up_weight[i], down_weight[i]], axis=1) for i in (0, 1)
     ]
 
+    columns = qkv_columns(qkv_weight[0], own_gains.T)
+    columns, tokens, cotangent = tied(columns.reshape(-1, columns.shape[-1]), tokens, cotangent)
+    along = along_batch(columns)
     first = swap_halves(tokens).reshape(-1, width)
-    columns = qkv_columns(qkv_weight[0], own_gains.T)
-    columns, first, cotangent = tied(columns.reshape(-1, columns.shape[-1]), first, cotangent)
     stream = first.astype(F32)
-    along = along_batch(columns)
     far, near = swapped(first, "head", 2), other_core(first)
     both = other_core(far)
     upper = swap_halves(cotangent)

time: 514 us -> 512 us (level)
    all_gather x3, waiting for transfers between devices: 22.4 us -> 14.6 us  [along_batch(): return lax.all_gather(piece, 'batch', axis=0, tiled=False)]
    unnamed x136 -> x144, local copies, waits for them, and re-layouts: 11.6 us -> 11.6 us
  transfers between devices with their start and end apart: 65 -> 65, of which waited for: 32 -> 32; matrix products, arithmetic and copies ran while one was open for 14% -> 13% of each run, Pallas kernels for 22% -> 22%
where the time goes in v27:
time: 512 us; the launch traced here: 504 us
  waiting for transfers between devices  180 us (35%)
  Pallas kernels  113 us (22%)
  starting transfers between devices  72.6 us (14%)
  other arithmetic  49.2 us (10%)
  local copies, waits for them, and re-layouts  34.6 us (7%)
  matrix products  19.5 us (4%)
  blocking collectives  18.7 us (4%)
  between operations  15.9 us (3%)
    ppermute x51, waiting for transfers between devices, swapped(): return lax.ppermute(array, axis, [(i, i ^ mask) for i in range(size)])  133 us
    ppermute x51, starting transfers between devices, swapped(): return lax.ppermute(array, axis, [(i, i ^ mask) for i in range(size)])  44.8 us
    all_to_all x7, waiting for transfers between devices, over_head(): lax.all_to_all(parts, 'head', split_axis=0, concat_axis=0, tiled=True)  27.5 us
    all_to_all x7, starting transfers between devices, over_head(): lax.all_to_all(parts, 'head', split_axis=0, concat_axis=0, tiled=True)  27.4 us
    pallas_call x2, Pallas kernels, attend_back_rows(): pl.pallas_call(functools.partial(attend_back_kernel, token_rows), grid=(l...  24.8 us
    all_to_all x1, blocking collectives, over_head(): lax.all_to_all(parts, 'head', split_axis=0, concat_axis=0, tiled=True)  18.7 us
    pallas_call x2, Pallas kernels, dense_grads(): pl.pallas_call(dense_grad_kernel, grid_spec=pltpu.PrefetchScalarGridSpec(...  17 us
    all_gather x3, waiting for transfers between devices, along_batch(): return lax.all_gather(piece, 'batch', axis=0, tiled=False)  14.6 us
  transfers between devices with their start and end apart: 65, of which 32 were waited for; matrix products, arithmetic and copies ran while one was open for 13% of the time, Pallas kernels for 22%

profile of v27, /device:TPU:0, one launch (start us, length us, event | category | flops | bytes accessed | tf_op | source)
XLA Modules:
  0.0 504.0 jit_solution(5556435379947664416)
XLA Ops:
  15.8 6.1 %all-to-all-done = bf16[4,40,964]{2,1,0:T(8,128)(2,1)S(1)} async-done(((bf16[4,40,964]{2,1,0:T(8,128)(2,1)}), bf16[4,40,964]{2,1,0:T(8,128)(2,1)S(1)}, u32[]{:S(2)}, u32[]{:S(2)}) %all-to-all-start) | async-done | bytes 308512 | tf_op jit(solution)/shard_map/all_to_all | solution.py:891
  24.9 6.8 %collective-permute-done = bf16[128,1280]{1,0:T(8,128)(2,1)S(1)} collective-permute-done((bf16[128,1280]{1,0:T(8,128)(2,1)S(1)}, bf16[128,1280]{1,0:T(8,128)(2,1)S(1)}, u32[]{:S(2)}, u32[]{:S(2)}) %collective-permute-start) | collective-permute-done | bytes 327712 | tf_op jit(solution)/shard_map/ppermute | solution.py:870
  35.7 12.5 %collective-permute-done.2.refs_2_ = bf16[256,1280]{1,0:T(8,128)(2,1)S(1)} collective-permute-done((bf16[256,1280]{1,0:T(8,128)(2,1)S(1)}, bf16[256,1280]{1,0:T(8,128)(2,1)S(1)}, u32[]{:S(2)}, u32[]{:S(2)}) %collective-permute-start.2) | collective-permute-done | bytes 655392 | tf_op jit(solution)/shard_map/ppermute | solution.py:870
  51.3 5.8 %all-gather.7.cloned.1.call-done = bf16[640,964]{1,0:T(8,128)(2,1)} async-done(((bf16[160,964]{1,0:T(8,128)(2,1)}), bf16[640,964]{1,0:T(8,128)(2,1)}) %all-gather.7.cloned.1.call-update) | async-done | bytes 1233936 | tf_op jit(solution)/shard_map/all_gather | solution.py:904
  63.9 6.6 %all-to-all-done.1 = bf16[4,40,960]{2,1,0:T(8,128)(2,1)S(1)} async-done(((bf16[4,40,960]{2,1,0:T(8,128)(2,1)}), bf16[4,40,960]{2,1,0:T(8,128)(2,1)S(1)}, u32[]{:S(2)}, u32[]{:S(2)}) %all-to-all-start.1) | async-done | bytes 307232 | tf_op jit(solution)/shard_map/all_to_all | solution.py:891
  70.7 16.5 %collective-permute-done.5.across_ref = bf16[4,160,964]{2,1,0:T(8,128)(2,1)S(1)} collective-permute-done((bf16[4,160,964]{2,1,0:T(8,128)(2,1)}, bf16[4,160,964]{2,1,0:T(8,128)(2,1)S(1)}, u32[]{:S(2)}, u32[]{:S(2)}) %collective-permute-start.5) | collective-permute-done | bytes 1233952 | tf_op jit(solution)/shard_map/ppermute | solution.py:870
  93.3 4.6 shard_map.169
  99.3 7.7 %shard_map.170 = (bf16[1024,1280]{1,0:T(8,128)(2,1)}, f32[960,1024]{1,0:T(8,128)S(1)}) custom-call(s32[3]{0:T(128)S(1)} %pad_add_fusion.place_ref.core_ref, bf16[256,1280]{1,0:T(8,128)(2,1)} %bitcast.235, bf16[256,1280]{1,0:T(8,128)(2,1)} %copy-done.55, bf16[256,1280]{1,0:T(8,128)(2,1)} %copy-done.54, bf16[256,1280]{1,0:T(8,128)(2,1)} %collective-permute-done.3.refs_3_, ...), custom_call_target="tpu_custom_call" | custom-call | flops 1048576 | bytes 1048576 | tf_op jit(solution)/shard_map/pallas_call | solution.py:733
  107.0 6.7 %shard_map.171 = (bf16[4,4,80,256]{3,2,1,0:T(8,128)(2,1)}, f32[4,1,1024]{2,1,0:T(1,128)S(1)}) custom-call(f32[3,4,80,1024]{3,2,1,0:T(8,128)S(1)} %bitcast.203, f32[80,1]{1,0:T(8,128)S(1)} %copy.60.scale_ref, s32[1024,1]{1,0:T(8,128)S(1)} %copy.61.col_ref, s32[1,1024]{1,0:T(1,128)S(1)} %constant_dynamic-slice_fusion.row_ref), custom_call_target="tpu_custom_call" | custom-call | flops 1048576 | bytes 1048576 | tf_op jit(solution)/shard_map/pallas_call | solution.py:435
  113.8 4.5 collective-permute-done.7.refs_2_
  129.3 5.3 %collective-permute-done.9.refs_4_ = bf16[4,40,1920]{2,1,0:T(8,128)(2,1)} collective-permute-done((bf16[4,40,1920]{2,1,0:T(8,128)(2,1)}, bf16[4,40,1920]{2,1,0:T(8,128)(2,1)}, u32[]{:S(2)}, u32[]{:S(2)}) %collective-permute-start.9) | collective-permute-done | bytes 614432 | tf_op jit(solution)/shard_map/ppermute | solution.py:870
  134.6 7.1 %all-gather.11.cloned.1.call-done = bf16[8,40,3840]{2,1,0:T(8,128)(2,1)} async-done(((bf16[2,40,3840]{2,1,0:T(8,128)(2,1)}), bf16[8,40,3840]{2,1,0:T(8,128)(2,1)}) %all-gather.11.cloned.1.call-update) | async-done | bytes 2457616 | tf_op jit(solution)/shard_map/all_gather | solution.py:904
  148.0 4.5 shard_map.172
  160.2 16.6 %collective-permute-done.16.across_ref = bf16[4,40,3840]{2,1,0:T(8,128)(2,1)S(1)} collective-permute-done((bf16[4,40,3840]{2,1,0:T(8,128)(2,1)S(1)}, bf16[4,40,3840]{2,1,0:T(8,128)(2,1)S(1)}, u32[]{:S(2)}, u32[]{:S(2)}) %collective-permute-start.16) | collective-permute-done | bytes 1228832 | tf_op jit(solution)/shard_map/ppermute | solution.py:870
  179.5 4.8 shard_map.173
  184.3 6.6 %shard_map.174 = (bf16[1024,1280]{1,0:T(8,128)(2,1)}, f32[960,1024]{1,0:T(8,128)S(1)}) custom-call(s32[3]{0:T(128)S(1)} %pad_add_fusion.place_ref.core_ref, bf16[256,1280]{1,0:T(8,128)(2,1)} %multiply_convert_fusion.2.refs_0_, bf16[256,1280]{1,0:T(8,128)(2,1)} %collective-permute-done.17.refs_1_, bf16[256,1280]{1,0:T(8,128)(2,1)} %collective-permute-done.15.refs_2_, ...), custom_call_target="tpu_custom_call" | custom-call | flops 1048576 | bytes 1048576 | tf_op jit(solution)/shard_map/pallas_call | solution.py:733
  190.9 6.1 %shard_map.175 = (bf16[4,4,80,256]{3,2,1,0:T(8,128)(2,1)S(1)}, f32[4,1,1024]{2,1,0:T(1,128)S(1)}) custom-call(f32[3,4,80,1024]{3,2,1,0:T(8,128)S(1)} %bitcast.205, f32[80,1]{1,0:T(8,128)S(1)} %copy.64.scale_ref, s32[1024,1]{1,0:T(8,128)S(1)} %copy.61.col_ref, s32[1,1024]{1,0:T(1,128)S(1)} %constant_dynamic-slice_fusion.row_ref), custom_call_target="tpu_custom_call" | custom-call | flops 1048576 | bytes 1048576 | tf_op jit(solution)/shard_map/pallas_call | solution.py:435
  197.0 8.6 %collective-permute-done.20.refs_2_ = bf16[4,40,3840]{2,1,0:T(8,128)(2,1)S(1)} collective-permute-done((bf16[4,40,3840]{2,1,0:T(8,128)(2,1)S(1)}, bf16[4,40,3840]{2,1,0:T(8,128)(2,1)S(1)}, u32[]{:S(2)}, u32[]{:S(2)}) %collective-permute-start.20) | collective-permute-done | bytes 1228832 | tf_op jit(solution)/shard_map/ppermute | solution.py:870
  210.2 18.7 %all_to_all.40 = bf16[4,320,256]{2,1,0:T(8,128)(2,1)S(1)} all-to-all(bf16[4,320,256]{2,1,0:T(8,128)(2,1)S(1)} %bitcast.221), channel_id=1, replica_groups=mesh['batch'=4,'blk'=2,'head'=4] {'head'}, dimensions={0} | all-to-all | bytes 1310720 | tf_op jit(solution)/shard_map/all_to_all | solution.py:891
  250.1 8.5 %shard_map.177 = (bf16[2,2,4,40,3840]{4,3,2,1,0:T(8,128)(2,1)}, bf16[2,2,4,40,3840]{4,3,2,1,0:T(8,128)(2,1)}) custom-call(s32[3]{0:T(128)S(1)} %pad_add_fusion.place_ref.core_ref, bf16[1280,256]{1,0:T(8,128)(2,1)} %bitcast.243, bf16[256,1280]{1,0:T(8,128)(2,1)} %copy-done.31, bf16[256,1280]{1,0:T(8,128)(2,1)} %copy-done.52, bf16[256,1280]{1,0:T(8,128)(2,1)} %copy-done.32, ...), custom_call_target="tpu_custom_call" | custom-call | flops 1048576 | bytes 1048576 | tf_op jit(solution)/shard_map/pallas_call | solution.py:599
  261.0 12.5 %shard_map.178 = (bf16[3,4,80,1024]{3,2,1,0:T(8,128)(2,1)}, f32[80,128]{1,0:T(8,128)}) custom-call(f32[3,4,80,1024]{3,2,1,0:T(8,128)} %bitcast.206, bf16[4,4,80,256]{3,2,1,0:T(8,128)(2,1)} %bitcast.56.grad_ref, f32[4,1,1024]{2,1,0:T(1,128)S(1)} %get-tuple-element.156.lse_ref, f32[80,1]{1,0:T(8,128)S(1)} %copy.64.scale_ref, s32[1024,1]{1,0:T(8,128)S(1)} %copy.61.col_ref, ...), custom_call_target="tpu_custom_call" | custom-call | flops 1048576 | bytes 1048576 | tf_op jit(solution)/shard_map/pallas_call | solution.py:528
  278.8 11.3 %shard_map.179 = (f32[2,2,128,1280]{3,2,1,0:T(8,128)}, bf16[2,2,128,1280]{3,2,1,0:T(8,128)(2,1)}, bf16[1280,960]{1,0:T(8,128)(2,1)}) custom-call(s32[3]{0:T(128)S(1)} %pad_add_fusion.place_ref.core_ref, bf16[960,1024]{1,0:T(8,128)(2,1)} %bitcast.245, bf16[1280,960]{1,0:T(8,128)(2,1)} %bitcast.223, bf16[1024,1280]{1,0:T(8,128)(2,1)} %get-tuple-element.163.normed_ref), custom_call_target="tpu_custom_call" | custom-call | flops 1048576 | bytes 1048576 | tf_op jit(solution)/shard_map/pallas_call | solution.py:779
  305.1 13.8 %collective-permute-done.33 = bf16[2,128,1280]{2,1,0:T(8,128)(2,1)} collective-permute-done((bf16[2,128,1280]{2,1,0:T(8,128)(2,1)}, bf16[2,128,1280]{2,1,0:T(8,128)(2,1)}, u32[]{:S(2)}, u32[]{:S(2)}) %collective-permute-start.33) | collective-permute-done | bytes 655392 | tf_op jit(solution)/shard_map/ppermute | solution.py:870
  337.4 8.5 %shard_map.180 = (bf16[2,2,4,40,3840]{4,3,2,1,0:T(8,128)(2,1)}, bf16[2,2,4,40,3840]{4,3,2,1,0:T(8,128)(2,1)}) custom-call(s32[3]{0:T(128)S(1)} %pad_add_fusion.place_ref.core_ref, bf16[1280,256]{1,0:T(8,128)(2,1)} %bitcast.240, bf16[256,1280]{1,0:T(8,128)(2,1)} %copy-done.30, bf16[256,1280]{1,0:T(8,128)(2,1)} %copy-done.48, bf16[256,1280]{1,0:T(8,128)(2,1)} %copy-done.36, ...), custom_call_target="tpu_custom_call" | custom-call | flops 1048576 | bytes 1048576 | tf_op jit(solution)/shard_map/pallas_call | solution.py:599
  348.3 7.9 %all-to-all-done.5 = bf16[4,320,256]{2,1,0:T(8,128)(2,1)} async-done(((bf16[4,320,256]{2,1,0:T(8,128)(2,1)}), bf16[4,320,256]{2,1,0:T(8,128)(2,1)}, u32[]{:S(2)}, u32[]{:S(2)}) %all-to-all-start.5) | async-done | bytes 655392 | tf_op jit(solution)/shard_map/all_to_all | solution.py:891
  361.4 12.4 %shard_map.181 = (bf16[3,4,80,1024]{3,2,1,0:T(8,128)(2,1)}, f32[80,128]{1,0:T(8,128)}) custom-call(f32[3,4,80,1024]{3,2,1,0:T(8,128)} %bitcast.204, bf16[4,4,80,256]{3,2,1,0:T(8,128)(2,1)} %bitcast.69.grad_ref, f32[4,1,1024]{2,1,0:T(1,128)S(1)} %get-tuple-element.186.lse_ref, f32[80,1]{1,0:T(8,128)S(1)} %copy.60.scale_ref, s32[1024,1]{1,0:T(8,128)S(1)} %copy.61.col_ref, ...), custom_call_target="tpu_custom_call" | custom-call | flops 1048576 | bytes 1048576 | tf_op jit(solution)/shard_map/pallas_call | solution.py:528
  374.6 7.4 %shard_map.182 = bf16[1280,960]{1,0:T(8,128)(2,1)} custom-call(bf16[960,1024]{1,0:T(8,128)(2,1)} %bitcast.231, bf16[1024,1280]{1,0:T(8,128)(2,1)} %get-tuple-element.190.normed_ref), custom_call_target="tpu_custom_call" | custom-call | flops 1048576 | bytes 1048576 | tf_op jit(solution)/shard_map/pallas_call | solution.py:850
  382.0 4.9 add_bitcast_fusion
  392.8 8.4 %shard_map.183 = (f32[2,2,128,1280]{3,2,1,0:T(8,128)}, bf16[2,2,128,1280]{3,2,1,0:T(8,128)(2,1)}) custom-call(s32[3]{0:T(128)S(1)} %pad_add_fusion.place_ref.core_ref, bf16[960,1024]{1,0:T(8,128)(2,1)} %bitcast.232, bf16[1280,960]{1,0:T(8,128)(2,1)} %bitcast.230), custom_call_target="tpu_custom_call" | custom-call | flops 1048576 | bytes 1048576 | tf_op jit(solution)/shard_map/pallas_call | solution.py:820
  423.4 18.4 %collective-permute-done.47 = f32[2,80]{1,0:T(2,128)S(1)} collective-permute-done((f32[2,80]{1,0:T(2,128)S(1)}, f32[2,80]{1,0:T(2,128)S(1)}, u32[]{:S(2)}, u32[]{:S(2)}) %collective-permute-start.47) | collective-permute-done | bytes 672 | tf_op jit(solution)/shard_map/ppermute | solution.py:870
  457.7 10.3 %collective-permute-done.48 = bf16[2,128,1280]{2,1,0:T(8,128)(2,1)} collective-permute-done((bf16[2,128,1280]{2,1,0:T(8,128)(2,1)}, bf16[2,128,1280]{2,1,0:T(8,128)(2,1)}, u32[]{:S(2)}, u32[]{:S(2)}) %collective-permute-start.48) | collective-permute-done | bytes 655392 | tf_op jit(solution)/shard_map/ppermute | solution.py:870
  479.0 5.0 reduce-scatter.11.cloned.1.call-done
  (389 shorter events, 202.7 us)
Async XLA Ops:
  15.2 41.9 %all-gather.7.cloned.1.call-start = ((), (), s32[]{:S(2)}) async-start(), calls=%async_computation.16 | async-start | bytes 1638400 | tf_op jit(solution)/shard_map/all_gather | solution.py:904
  24.8 64.1 %all-gather.9.cloned.1.call-start = ((), (), s32[]{:S(2)}) async-start(), calls=%async_computation.17 | async-start | bytes 1536000 | tf_op jit(solution)/shard_map/all_gather | solution.py:904
  57.1 30.1 %collective-permute-start.5 = (bf16[4,160,964]{2,1,0:T(8,128)(2,1)}, bf16[4,160,964]{2,1,0:T(8,128)(2,1)S(1)}, u32[]{:S(2)}, u32[]{:S(2)}) collective-permute-start(bf16[4,160,964]{2,1,0:T(8,128)(2,1)} %bitcast.252), channel_id=1, source_target_pairs={{0,4},{4,0},{1,5},{5,1},{2,6},{6,2},{3,7},{7,3},{8,12},{12,8},{9,1... | collective-permute-start | bytes 3701768 | tf_op jit(solution)/shard_map/ppermute | solution.py:870
  63.8 77.9 %all-gather.11.cloned.1.call-start = ((), (), s32[]{:S(2)}) async-start(), calls=%async_computation.18 | async-start | bytes 3072000 | tf_op jit(solution)/shard_map/all_gather | solution.py:904
  89.9 28.4 %collective-permute-start.7 = (bf16[4,40,3840]{2,1,0:T(8,128)(2,1)}, bf16[4,40,3840]{2,1,0:T(8,128)(2,1)S(1)}, u32[]{:S(2)}, u32[]{:S(2)}) collective-permute-start(bf16[4,40,3840]{2,1,0:T(8,128)(2,1)} %bitcast.19.refs_0_), channel_id=1, source_target_pairs={{0,2},{1,3},{2,0},{3,1},{4,6},{5,7},{6,4},{7,5},{8,10},{9,11},{10,... | collective-permute-start | bytes 3686408 | tf_op jit(solution)/shard_map/ppermute | solution.py:870
  91.4 28.2 %collective-permute-start.6 = (bf16[4,40,3840]{2,1,0:T(8,128)(2,1)}, bf16[4,40,3840]{2,1,0:T(8,128)(2,1)}, u32[]{:S(2)}, u32[]{:S(2)}) collective-permute-start(bf16[4,40,3840]{2,1,0:T(8,128)(2,1)} %bitcast.19.refs_0_), channel_id=1, source_target_pairs={{0,4},{4,0},{1,5},{5,1},{2,6},{6,2},{3,7},{7,3},{8,12},{12,8},{9,1... | collective-permute-start | bytes 3686408 | tf_op jit(solution)/shard_map/ppermute | solution.py:870
  123.9 20.7 %collective-permute-start.8 = (bf16[4,40,1920]{2,1,0:T(8,128)(2,1)}, bf16[4,40,1920]{2,1,0:T(8,128)(2,1)}, u32[]{:S(2)}, u32[]{:S(2)}) collective-permute-start(bf16[4,40,1920]{2,1,0:T(8,128)(2,1)} %slice.153), channel_id=1, source_target_pairs={{0,2},{1,3},{2,0},{3,1},{4,6},{5,7},{6,4},{7,5},{8,10},{9,11},{10,... | collective-permute-start | bytes 1843208 | tf_op jit(solution)/shard_map/ppermute | solution.py:870
  124.4 20.2 %all-to-all-start.2 = ((bf16[4,320,256]{2,1,0:T(8,128)(2,1)}), bf16[4,320,256]{2,1,0:T(8,128)(2,1)S(1)}, u32[]{:S(2)}, u32[]{:S(2)}) async-start(bf16[4,320,256]{2,1,0:T(8,128)(2,1)} %bitcast.31), calls=%async_computation.2 | async-start | bytes 1310720 | tf_op jit(solution)/shard_map/all_to_all | solution.py:891
  128.8 19.2 %collective-permute-start.11 = (bf16[4,40,3840]{2,1,0:T(8,128)(2,1)}, bf16[4,40,3840]{2,1,0:T(8,128)(2,1)}, u32[]{:S(2)}, u32[]{:S(2)}) collective-permute-start(bf16[4,40,3840]{2,1,0:T(8,128)(2,1)} %collective-permute-done.6.refs_1_), channel_id=1, source_target_pairs={{0,1},{1,0},{2,3},{3,2},{4,5},{5,4},{6,7},{7,6},{8,9},{9,8},{10,11... | collective-permute-start | bytes 3686408 | tf_op jit(solution)/shard_map/ppermute | solution.py:870
  128.8 19.2 %collective-permute-start.12 = (bf16[4,40,3840]{2,1,0:T(8,128)(2,1)S(1)}, bf16[4,40,3840]{2,1,0:T(8,128)(2,1)}, u32[]{:S(2)}, u32[]{:S(2)}) collective-permute-start(bf16[4,40,3840]{2,1,0:T(8,128)(2,1)S(1)} %collective-permute-done.7.refs_2_), channel_id=1, source_target_pairs={{0,1},{1,0},{2,3},{3,2},{4,5},{5,4},{6,7},{7,6},{8,9},{9,8},{10,11... | collective-permute-start | bytes 3686408 | tf_op jit(solution)/shard_map/ppermute | solution.py:870
  147.4 29.5 %collective-permute-start.16 = (bf16[4,40,3840]{2,1,0:T(8,128)(2,1)S(1)}, bf16[4,40,3840]{2,1,0:T(8,128)(2,1)S(1)}, u32[]{:S(2)}, u32[]{:S(2)}) collective-permute-start(bf16[4,40,3840]{2,1,0:T(8,128)(2,1)S(1)} %get-tuple-element.250.along_ref), channel_id=1, source_target_pairs={{0,4},{4,0},{1,5},{5,1},{2,6},{6,2},{3,7},{7,3},{8,12},{12,8},{9,1... | collective-permute-start | bytes 3686408 | tf_op jit(solution)/shard_map/ppermute | solution.py:870
  176.9 28.8 %collective-permute-start.20 = (bf16[4,40,3840]{2,1,0:T(8,128)(2,1)S(1)}, bf16[4,40,3840]{2,1,0:T(8,128)(2,1)S(1)}, u32[]{:S(2)}, u32[]{:S(2)}) collective-permute-start(bf16[4,40,3840]{2,1,0:T(8,128)(2,1)S(1)} %get-tuple-element.141.refs_0_), channel_id=1, source_target_pairs={{0,2},{1,3},{2,0},{3,1},{4,6},{5,7},{6,4},{7,5},{8,10},{9,11},{10,... | collective-permute-start | bytes 3686408 | tf_op jit(solution)/shard_map/ppermute | solution.py:870
  177.4 28.6 %collective-permute-start.19 = (bf16[4,40,3840]{2,1,0:T(8,128)(2,1)S(1)}, bf16[4,40,3840]{2,1,0:T(8,128)(2,1)}, u32[]{:S(2)}, u32[]{:S(2)}) collective-permute-start(bf16[4,40,3840]{2,1,0:T(8,128)(2,1)S(1)} %get-tuple-element.141.refs_0_), channel_id=1, source_target_pairs={{0,4},{4,0},{1,5},{5,1},{2,6},{6,2},{3,7},{7,3},{8,12},{12,8},{9,1... | collective-permute-start | bytes 3686408 | tf_op jit(solution)/shard_map/ppermute | solution.py:870
  207.2 21.8 %collective-permute-start.22 = (bf16[4,40,1920]{2,1,0:T(8,128)(2,1)S(1)}, bf16[4,40,1920]{2,1,0:T(8,128)(2,1)S(1)}, u32[]{:S(2)}, u32[]{:S(2)}) collective-permute-start(bf16[4,40,1920]{2,1,0:T(8,128)(2,1)S(1)} %slice.167), channel_id=1, source_target_pairs={{0,4},{4,0},{1,5},{5,1},{2,6},{6,2},{3,7},{7,3},{8,12},{12,8},{9,1... | collective-permute-start | bytes 1843208 | tf_op jit(solution)/shard_map/ppermute | solution.py:870
  208.3 20.7 %collective-permute-start.21 = (bf16[4,40,1920]{2,1,0:T(8,128)(2,1)S(1)}, bf16[4,40,1920]{2,1,0:T(8,128)(2,1)S(1)}, u32[]{:S(2)}, u32[]{:S(2)}) collective-permute-start(bf16[4,40,1920]{2,1,0:T(8,128)(2,1)S(1)} %slice.166), channel_id=1, source_target_pairs={{0,2},{1,3},{2,0},{3,1},{4,6},{5,7},{6,4},{7,5},{8,10},{9,11},{10,... | collective-permute-start | bytes 1843208 | tf_op jit(solution)/shard_map/ppermute | solution.py:870
  209.7 19.8 %collective-permute-start.23 = (bf16[4,40,3840]{2,1,0:T(8,128)(2,1)S(1)}, bf16[4,40,3840]{2,1,0:T(8,128)(2,1)S(1)}, u32[]{:S(2)}, u32[]{:S(2)}) collective-permute-start(bf16[4,40,3840]{2,1,0:T(8,128)(2,1)S(1)} %get-tuple-element.141.refs_0_), channel_id=1, source_target_pairs={{0,1},{1,0},{2,3},{3,2},{4,5},{5,4},{6,7},{7,6},{8,9},{9,8},{10,11... | collective-permute-start | bytes 3686408 | tf_op jit(solution)/shard_map/ppermute | solution.py:870
  209.7 22.2 %collective-permute-start.24 = (bf16[4,40,3840]{2,1,0:T(8,128)(2,1)}, bf16[4,40,3840]{2,1,0:T(8,128)(2,1)S(1)}, u32[]{:S(2)}, u32[]{:S(2)}) collective-permute-start(bf16[4,40,3840]{2,1,0:T(8,128)(2,1)} %collective-permute-done.19.refs_1_), channel_id=1, source_target_pairs={{0,1},{1,0},{2,3},{3,2},{4,5},{5,4},{6,7},{7,6},{8,9},{9,8},{10,11... | collective-permute-start | bytes 3686408 | tf_op jit(solution)/shard_map/ppermute | solution.py:870
  210.2 21.7 %collective-permute-start.25 = (bf16[4,40,3840]{2,1,0:T(8,128)(2,1)S(1)}, bf16[4,40,3840]{2,1,0:T(8,128)(2,1)S(1)}, u32[]{:S(2)}, u32[]{:S(2)}) collective-permute-start(bf16[4,40,3840]{2,1,0:T(8,128)(2,1)S(1)} %collective-permute-done.20.refs_2_), channel_id=1, source_target_pairs={{0,1},{1,0},{2,3},{3,2},{4,5},{5,4},{6,7},{7,6},{8,9},{9,8},{10,11... | collective-permute-start | bytes 3686408 | tf_op jit(solution)/shard_map/ppermute | solution.py:870
  239.5 19.1 %collective-permute-start.28 = (bf16[128,1280]{1,0:T(8,128)(2,1)}, bf16[128,1280]{1,0:T(8,128)(2,1)}, u32[]{:S(2)}, u32[]{:S(2)}) collective-permute-start(bf16[128,1280]{1,0:T(8,128)(2,1)} %dynamic-slice_bitcast_fusion.3), channel_id=1, source_target_pairs={{0,4},{4,0},{1,5},{5,1},{2,6},{6,2},{3,7},{7,3},{8,12},{12,8},{9,1... | collective-permute-start | bytes 983048 | tf_op jit(solution)/shard_map/ppermute | solution.py:870
  249.9 106.3 %reduce-scatter.5.cloned.1.call-start = ((), (), s32[]{:S(2)}) async-start(), calls=%async_computation.12 | async-start | bytes 3276800 | tf_op jit(solution)/shard_map/reduce_scatter | solution.py:920
  303.6 42.3 %collective-permute-start.34 = (bf16[4,40,3840]{2,1,0:T(8,128)(2,1)}, bf16[4,40,3840]{2,1,0:T(8,128)(2,1)}, u32[]{:S(2)}, u32[]{:S(2)}) collective-permute-start(bf16[4,40,3840]{2,1,0:T(8,128)(2,1)} %pad_maximum_fusion), channel_id=1, source_target_pairs={{0,4},{4,0},{1,5},{5,1},{2,6},{6,2},{3,7},{7,3},{8,12},{12,8},{9,1... | collective-permute-start | bytes 3686408 | tf_op jit(solution)/shard_map/ppermute | solution.py:870
  320.6 35.6 %collective-permute-start.35 = (bf16[4,40,3840]{2,1,0:T(8,128)(2,1)}, bf16[4,40,3840]{2,1,0:T(8,128)(2,1)}, u32[]{:S(2)}, u32[]{:S(2)}) collective-permute-start(bf16[4,40,3840]{2,1,0:T(8,128)(2,1)} %pad_maximum_fusion.1), channel_id=1, source_target_pairs={{0,2},{1,3},{2,0},{3,1},{4,6},{5,7},{6,4},{7,5},{8,10},{9,11},{10,... | collective-permute-start | bytes 3686408 | tf_op jit(solution)/shard_map/ppermute | solution.py:870
  333.2 23.0 %all-to-all-start.5 = ((bf16[4,320,256]{2,1,0:T(8,128)(2,1)}), bf16[4,320,256]{2,1,0:T(8,128)(2,1)}, u32[]{:S(2)}, u32[]{:S(2)}) async-start(bf16[4,320,256]{2,1,0:T(8,128)(2,1)} %bitcast.65), calls=%async_computation.5 | async-start | bytes 1310720 | tf_op jit(solution)/shard_map/all_to_all | solution.py:891
  337.4 63.9 %reduce-scatter.7.cloned.1.call-start = ((), (), s32[]{:S(2)}) async-start(), calls=%async_computation.13 | async-start | bytes 1536000 | tf_op jit(solution)/shard_map/reduce_scatter | solution.py:920
  356.2 25.8 %collective-permute-start.37 = (bf16[2,2,4,40,3840]{4,3,2,1,0:T(8,128)(2,1)}, bf16[2,2,4,40,3840]{4,3,2,1,0:T(8,128)(2,1)}, u32[]{:S(2)}, u32[]{:S(2)}) collective-permute-start(bf16[2,2,4,40,3840]{4,3,2,1,0:T(8,128)(2,1)} %get-tuple-element.191), channel_id=1, source_target_pairs={{0,1},{1,0},{2,3},{3,2},{4,5},{5,4},{6,7},{7,6},{8,9},{9,8},{10,11... | collective-permute-start | bytes 14745608 | tf_op jit(solution)/shard_map/ppermute | solution.py:870
  358.8 85.8 %reduce-scatter.9.cloned.1.call-start = ((), (), s32[]{:S(2)}) async-start(), calls=%async_computation.14 | async-start | bytes 3276800 | tf_op jit(solution)/shard_map/reduce_scatter | solution.py:920
  382.0 102.0 %reduce-scatter.11.cloned.1.call-start = ((), (), s32[]{:S(2)}) async-start(), calls=%async_computation.15 | async-start | bytes 1536000 | tf_op jit(solution)/shard_map/reduce_scatter | solution.py:920
  412.3 29.5 %collective-permute-start.42 = (bf16[2,2,128,1280]{3,2,1,0:T(8,128)(2,1)S(1)}, bf16[2,2,128,1280]{3,2,1,0:T(8,128)(2,1)S(1)}, u32[]{:S(2)}, u32[]{:S(2)}) collective-permute-start(bf16[2,2,128,1280]{3,2,1,0:T(8,128)(2,1)S(1)} %copy-done.66), channel_id=1, source_target_pairs={{0,1},{1,0},{2,3},{3,2},{4,5},{5,4},{6,7},{7,6},{8,9},{9,8},{10,11... | collective-permute-start | bytes 3932168 | tf_op jit(solution)/shard_map/ppermute | solution.py:870
  412.3 31.2 %collective-permute-start.43 = (bf16[4,40,3840]{2,1,0:T(8,128)(2,1)S(1)}, bf16[4,40,3840]{2,1,0:T(8,128)(2,1)S(1)}, u32[]{:S(2)}, u32[]{:S(2)}) collective-permute-start(bf16[4,40,3840]{2,1,0:T(8,128)(2,1)S(1)} %pad_maximum_fusion.2), channel_id=1, source_target_pairs={{0,4},{4,0},{1,5},{5,1},{2,6},{6,2},{3,7},{7,3},{8,12},{12,8},{9,1... | collective-permute-start | bytes 3686408 | tf_op jit(solution)/shard_map/ppermute | solution.py:870
  413.8 30.8 %collective-permute-start.44 = (bf16[4,40,3840]{2,1,0:T(8,128)(2,1)S(1)}, bf16[4,40,3840]{2,1,0:T(8,128)(2,1)}, u32[]{:S(2)}, u32[]{:S(2)}) collective-permute-start(bf16[4,40,3840]{2,1,0:T(8,128)(2,1)S(1)} %pad_maximum_fusion.3), channel_id=1, source_target_pairs={{0,2},{1,3},{2,0},{3,1},{4,6},{5,7},{6,4},{7,5},{8,10},{9,11},{10,... | collective-permute-start | bytes 3686408 | tf_op jit(solution)/shard_map/ppermute | solution.py:870
  422.7 19.1 %collective-permute-start.47 = (f32[2,80]{1,0:T(2,128)S(1)}, f32[2,80]{1,0:T(2,128)S(1)}, u32[]{:S(2)}, u32[]{:S(2)}) collective-permute-start(f32[2,80]{1,0:T(2,128)S(1)} %add.392), channel_id=1, source_target_pairs={{0,4},{4,0},{1,5},{5,1},{2,6},{6,2},{3,7},{7,3},{8,12},{12,8},{9,1... | collective-permute-start | bytes 1928 | tf_op jit(solution)/shard_map/ppermute | solution.py:870
  452.1 22.4 %collective-permute-start.50 = (bf16[160,960]{1,0:T(8,128)(2,1)}, bf16[160,960]{1,0:T(8,128)(2,1)}, u32[]{:S(2)}, u32[]{:S(2)}) collective-permute-start(bf16[160,960]{1,0:T(8,128)(2,1)} %dynamic-slice_bitcast_fusion), channel_id=1, source_target_pairs={{0,4},{4,0},{1,5},{5,1},{2,6},{6,2},{3,7},{7,3},{8,12},{12,8},{9,1... | collective-permute-start | bytes 921608 | tf_op jit(solution)/shard_map/ppermute | solution.py:870
  (105 other events, 849.5 us)
Sparse Core Ops, SparseCore 0:
  24.9 32.0 all-gather.6
  58.6 30.2 all-gather.8
  90.5 51.1 all-gather.10
  303.7 51.8 reduce-scatter.4
  358.9 31.1 reduce-scatter.6
  392.4 50.8 reduce-scatter.8
  453.7 30.2 reduce-scatter.10

commit v28 on v27

--- a/solution.py
+++ b/solution.py
@@ -359,7 +359,7 @@
 
 
 Q_ROWS = 256
-KERNEL = pltpu.CompilerParams(vmem_limit_bytes=32 * 1024 * 1024)
+KERNEL = pltpu.CompilerParams(vmem_limit_bytes=24 * 1024 * 1024)
 LIGHT = pl.CostEstimate(flops=1 << 20, bytes_accessed=1 << 20, transcendentals=0)
 
 

time: 512 us -> 512 us (level)
  no operation moved by 1% of the time
where the time goes in v28:
time: 512 us; the launch traced here: 504 us
  waiting for transfers between devices  181 us (35%)
  Pallas kernels  113 us (22%)
  starting transfers between devices  72.5 us (14%)
  other arithmetic  49.2 us (10%)
  local copies, waits for them, and re-layouts  34.6 us (7%)
  matrix products  19.6 us (4%)
  blocking collectives  18.7 us (4%)
  between operations  15.9 us (3%)
    ppermute x51, waiting for transfers between devices, swapped(): return lax.ppermute(array, axis, [(i, i ^ mask) for i in range(size)])  133 us
    ppermute x51, starting transfers between devices, swapped(): return lax.ppermute(array, axis, [(i, i ^ mask) for i in range(size)])  44.7 us
    all_to_all x7, waiting for transfers between devices, over_head(): lax.all_to_all(parts, 'head', split_axis=0, concat_axis=0, tiled=True)  27.5 us
    all_to_all x7, starting transfers between devices, over_head(): lax.all_to_all(parts, 'head', split_axis=0, concat_axis=0, tiled=True)  27.4 us
    pallas_call x2, Pallas kernels, attend_back_rows(): pl.pallas_call(functools.partial(attend_back_kernel, token_rows), grid=(l...  24.8 us
    all_to_all x1, blocking collectives, over_head(): lax.all_to_all(parts, 'head', split_axis=0, concat_axis=0, tiled=True)  18.7 us
    pallas_call x2, Pallas kernels, dense_grads(): pl.pallas_call(dense_grad_kernel, grid_spec=pltpu.PrefetchScalarGridSpec(...  17 us
    all_gather x3, waiting for transfers between devices, along_batch(): return lax.all_gather(piece, 'batch', axis=0, tiled=False)  14.6 us
  transfers between devices with their start and end apart: 65, of which 32 were waited for; matrix products, arithmetic and copies ran while one was open for 13% of the time, Pallas kernels for 22%

profile of v28, /device:TPU:0, one launch (start us, length us, event | category | flops | bytes accessed | tf_op | source)
XLA Modules:
  0.0 504.1 jit_solution(9883565473807071114)
XLA Ops:
  15.8 6.1 %all-to-all-done = bf16[4,40,964]{2,1,0:T(8,128)(2,1)S(1)} async-done(((bf16[4,40,964]{2,1,0:T(8,128)(2,1)}), bf16[4,40,964]{2,1,0:T(8,128)(2,1)S(1)}, u32[]{:S(2)}, u32[]{:S(2)}) %all-to-all-start) | async-done | bytes 308512 | tf_op jit(solution)/shard_map/all_to_all | solution.py:891
  24.9 6.8 %collective-permute-done = bf16[128,1280]{1,0:T(8,128)(2,1)S(1)} collective-permute-done((bf16[128,1280]{1,0:T(8,128)(2,1)S(1)}, bf16[128,1280]{1,0:T(8,128)(2,1)S(1)}, u32[]{:S(2)}, u32[]{:S(2)}) %collective-permute-start) | collective-permute-done | bytes 327712 | tf_op jit(solution)/shard_map/ppermute | solution.py:870
  35.7 12.5 %collective-permute-done.2.refs_2_ = bf16[256,1280]{1,0:T(8,128)(2,1)S(1)} collective-permute-done((bf16[256,1280]{1,0:T(8,128)(2,1)S(1)}, bf16[256,1280]{1,0:T(8,128)(2,1)S(1)}, u32[]{:S(2)}, u32[]{:S(2)}) %collective-permute-start.2) | collective-permute-done | bytes 655392 | tf_op jit(solution)/shard_map/ppermute | solution.py:870
  51.3 5.8 %all-gather.7.cloned.1.call-done = bf16[640,964]{1,0:T(8,128)(2,1)} async-done(((bf16[160,964]{1,0:T(8,128)(2,1)}), bf16[640,964]{1,0:T(8,128)(2,1)}) %all-gather.7.cloned.1.call-update) | async-done | bytes 1233936 | tf_op jit(solution)/shard_map/all_gather | solution.py:904
  63.9 6.6 %all-to-all-done.1 = bf16[4,40,960]{2,1,0:T(8,128)(2,1)S(1)} async-done(((bf16[4,40,960]{2,1,0:T(8,128)(2,1)}), bf16[4,40,960]{2,1,0:T(8,128)(2,1)S(1)}, u32[]{:S(2)}, u32[]{:S(2)}) %all-to-all-start.1) | async-done | bytes 307232 | tf_op jit(solution)/shard_map/all_to_all | solution.py:891
  70.7 16.5 %collective-permute-done.5.across_ref = bf16[4,160,964]{2,1,0:T(8,128)(2,1)S(1)} collective-permute-done((bf16[4,160,964]{2,1,0:T(8,128)(2,1)}, bf16[4,160,964]{2,1,0:T(8,128)(2,1)S(1)}, u32[]{:S(2)}, u32[]{:S(2)}) %collective-permute-start.5) | collective-permute-done | bytes 1233952 | tf_op jit(solution)/shard_map/ppermute | solution.py:870
  93.3 4.6 shard_map.169
  99.3 7.7 %shard_map.170 = (bf16[1024,1280]{1,0:T(8,128)(2,1)}, f32[960,1024]{1,0:T(8,128)S(1)}) custom-call(s32[3]{0:T(128)S(1)} %pad_add_fusion.place_ref.core_ref, bf16[256,1280]{1,0:T(8,128)(2,1)} %bitcast.235, bf16[256,1280]{1,0:T(8,128)(2,1)} %copy-done.55, bf16[256,1280]{1,0:T(8,128)(2,1)} %copy-done.54, bf16[256,1280]{1,0:T(8,128)(2,1)} %collective-permute-done.3.refs_3_, ...), custom_call_target="tpu_custom_call" | custom-call | flops 1048576 | bytes 1048576 | tf_op jit(solution)/shard_map/pallas_call | solution.py:733
  107.0 6.7 %shard_map.171 = (bf16[4,4,80,256]{3,2,1,0:T(8,128)(2,1)}, f32[4,1,1024]{2,1,0:T(1,128)S(1)}) custom-call(f32[3,4,80,1024]{3,2,1,0:T(8,128)S(1)} %bitcast.203, f32[80,1]{1,0:T(8,128)S(1)} %copy.60.scale_ref, s32[1024,1]{1,0:T(8,128)S(1)} %copy.61.col_ref, s32[1,1024]{1,0:T(1,128)S(1)} %constant_dynamic-slice_fusion.row_ref), custom_call_target="tpu_custom_call" | custom-call | flops 1048576 | bytes 1048576 | tf_op jit(solution)/shard_map/pallas_call | solution.py:435
  113.8 4.5 collective-permute-done.7.refs_2_
  129.3 5.3 %collective-permute-done.9.refs_4_ = bf16[4,40,1920]{2,1,0:T(8,128)(2,1)} collective-permute-done((bf16[4,40,1920]{2,1,0:T(8,128)(2,1)}, bf16[4,40,1920]{2,1,0:T(8,128)(2,1)}, u32[]{:S(2)}, u32[]{:S(2)}) %collective-permute-start.9) | collective-permute-done | bytes 614432 | tf_op jit(solution)/shard_map/ppermute | solution.py:870
  134.6 7.1 %all-gather.11.cloned.1.call-done = bf16[8,40,3840]{2,1,0:T(8,128)(2,1)} async-done(((bf16[2,40,3840]{2,1,0:T(8,128)(2,1)}), bf16[8,40,3840]{2,1,0:T(8,128)(2,1)}) %all-gather.11.cloned.1.call-update) | async-done | bytes 2457616 | tf_op jit(solution)/shard_map/all_gather | solution.py:904
  148.0 4.5 shard_map.172
  160.3 16.6 %collective-permute-done.16.across_ref = bf16[4,40,3840]{2,1,0:T(8,128)(2,1)S(1)} collective-permute-done((bf16[4,40,3840]{2,1,0:T(8,128)(2,1)S(1)}, bf16[4,40,3840]{2,1,0:T(8,128)(2,1)S(1)}, u32[]{:S(2)}, u32[]{:S(2)}) %collective-permute-start.16) | collective-permute-done | bytes 1228832 | tf_op jit(solution)/shard_map/ppermute | solution.py:870
  179.5 4.8 shard_map.173
  184.3 6.6 %shard_map.174 = (bf16[1024,1280]{1,0:T(8,128)(2,1)}, f32[960,1024]{1,0:T(8,128)S(1)}) custom-call(s32[3]{0:T(128)S(1)} %pad_add_fusion.place_ref.core_ref, bf16[256,1280]{1,0:T(8,128)(2,1)} %multiply_convert_fusion.2.refs_0_, bf16[256,1280]{1,0:T(8,128)(2,1)} %collective-permute-done.17.refs_1_, bf16[256,1280]{1,0:T(8,128)(2,1)} %collective-permute-done.15.refs_2_, ...), custom_call_target="tpu_custom_call" | custom-call | flops 1048576 | bytes 1048576 | tf_op jit(solution)/shard_map/pallas_call | solution.py:733
  190.9 6.1 %shard_map.175 = (bf16[4,4,80,256]{3,2,1,0:T(8,128)(2,1)S(1)}, f32[4,1,1024]{2,1,0:T(1,128)S(1)}) custom-call(f32[3,4,80,1024]{3,2,1,0:T(8,128)S(1)} %bitcast.205, f32[80,1]{1,0:T(8,128)S(1)} %copy.64.scale_ref, s32[1024,1]{1,0:T(8,128)S(1)} %copy.61.col_ref, s32[1,1024]{1,0:T(1,128)S(1)} %constant_dynamic-slice_fusion.row_ref), custom_call_target="tpu_custom_call" | custom-call | flops 1048576 | bytes 1048576 | tf_op jit(solution)/shard_map/pallas_call | solution.py:435
  197.1 8.6 %collective-permute-done.20.refs_2_ = bf16[4,40,3840]{2,1,0:T(8,128)(2,1)S(1)} collective-permute-done((bf16[4,40,3840]{2,1,0:T(8,128)(2,1)S(1)}, bf16[4,40,3840]{2,1,0:T(8,128)(2,1)S(1)}, u32[]{:S(2)}, u32[]{:S(2)}) %collective-permute-start.20) | collective-permute-done | bytes 1228832 | tf_op jit(solution)/shard_map/ppermute | solution.py:870
  210.3 18.7 %all_to_all.40 = bf16[4,320,256]{2,1,0:T(8,128)(2,1)S(1)} all-to-all(bf16[4,320,256]{2,1,0:T(8,128)(2,1)S(1)} %bitcast.221), channel_id=1, replica_groups=mesh['batch'=4,'blk'=2,'head'=4] {'head'}, dimensions={0} | all-to-all | bytes 1310720 | tf_op jit(solution)/shard_map/all_to_all | solution.py:891
  250.2 8.5 %shard_map.177 = (bf16[2,2,4,40,3840]{4,3,2,1,0:T(8,128)(2,1)}, bf16[2,2,4,40,3840]{4,3,2,1,0:T(8,128)(2,1)}) custom-call(s32[3]{0:T(128)S(1)} %pad_add_fusion.place_ref.core_ref, bf16[1280,256]{1,0:T(8,128)(2,1)} %bitcast.243, bf16[256,1280]{1,0:T(8,128)(2,1)} %copy-done.31, bf16[256,1280]{1,0:T(8,128)(2,1)} %copy-done.52, bf16[256,1280]{1,0:T(8,128)(2,1)} %copy-done.32, ...), custom_call_target="tpu_custom_call" | custom-call | flops 1048576 | bytes 1048576 | tf_op jit(solution)/shard_map/pallas_call | solution.py:599
  261.1 12.5 %shard_map.178 = (bf16[3,4,80,1024]{3,2,1,0:T(8,128)(2,1)}, f32[80,128]{1,0:T(8,128)}) custom-call(f32[3,4,80,1024]{3,2,1,0:T(8,128)} %bitcast.206, bf16[4,4,80,256]{3,2,1,0:T(8,128)(2,1)} %bitcast.56.grad_ref, f32[4,1,1024]{2,1,0:T(1,128)S(1)} %get-tuple-element.156.lse_ref, f32[80,1]{1,0:T(8,128)S(1)} %copy.64.scale_ref, s32[1024,1]{1,0:T(8,128)S(1)} %copy.61.col_ref, ...), custom_call_target="tpu_custom_call" | custom-call | flops 1048576 | bytes 1048576 | tf_op jit(solution)/shard_map/pallas_call | solution.py:528
  278.9 11.3 %shard_map.179 = (f32[2,2,128,1280]{3,2,1,0:T(8,128)}, bf16[2,2,128,1280]{3,2,1,0:T(8,128)(2,1)}, bf16[1280,960]{1,0:T(8,128)(2,1)}) custom-call(s32[3]{0:T(128)S(1)} %pad_add_fusion.place_ref.core_ref, bf16[960,1024]{1,0:T(8,128)(2,1)} %bitcast.245, bf16[1280,960]{1,0:T(8,128)(2,1)} %bitcast.223, bf16[1024,1280]{1,0:T(8,128)(2,1)} %get-tuple-element.163.normed_ref), custom_call_target="tpu_custom_call" | custom-call | flops 1048576 | bytes 1048576 | tf_op jit(solution)/shard_map/pallas_call | solution.py:779
  305.2 13.8 %collective-permute-done.33 = bf16[2,128,1280]{2,1,0:T(8,128)(2,1)} collective-permute-done((bf16[2,128,1280]{2,1,0:T(8,128)(2,1)}, bf16[2,128,1280]{2,1,0:T(8,128)(2,1)}, u32[]{:S(2)}, u32[]{:S(2)}) %collective-permute-start.33) | collective-permute-done | bytes 655392 | tf_op jit(solution)/shard_map/ppermute | solution.py:870
  337.5 8.5 %shard_map.180 = (bf16[2,2,4,40,3840]{4,3,2,1,0:T(8,128)(2,1)}, bf16[2,2,4,40,3840]{4,3,2,1,0:T(8,128)(2,1)}) custom-call(s32[3]{0:T(128)S(1)} %pad_add_fusion.place_ref.core_ref, bf16[1280,256]{1,0:T(8,128)(2,1)} %bitcast.240, bf16[256,1280]{1,0:T(8,128)(2,1)} %copy-done.30, bf16[256,1280]{1,0:T(8,128)(2,1)} %copy-done.48, bf16[256,1280]{1,0:T(8,128)(2,1)} %copy-done.36, ...), custom_call_target="tpu_custom_call" | custom-call | flops 1048576 | bytes 1048576 | tf_op jit(solution)/shard_map/pallas_call | solution.py:599
  348.4 7.9 %all-to-all-done.5 = bf16[4,320,256]{2,1,0:T(8,128)(2,1)} async-done(((bf16[4,320,256]{2,1,0:T(8,128)(2,1)}), bf16[4,320,256]{2,1,0:T(8,128)(2,1)}, u32[]{:S(2)}, u32[]{:S(2)}) %all-to-all-start.5) | async-done | bytes 655392 | tf_op jit(solution)/shard_map/all_to_all | solution.py:891
  361.5 12.3 %shard_map.181 = (bf16[3,4,80,1024]{3,2,1,0:T(8,128)(2,1)}, f32[80,128]{1,0:T(8,128)}) custom-call(f32[3,4,80,1024]{3,2,1,0:T(8,128)} %bitcast.204, bf16[4,4,80,256]{3,2,1,0:T(8,128)(2,1)} %bitcast.69.grad_ref, f32[4,1,1024]{2,1,0:T(1,128)S(1)} %get-tuple-element.186.lse_ref, f32[80,1]{1,0:T(8,128)S(1)} %copy.60.scale_ref, s32[1024,1]{1,0:T(8,128)S(1)} %copy.61.col_ref, ...), custom_call_target="tpu_custom_call" | custom-call | flops 1048576 | bytes 1048576 | tf_op jit(solution)/shard_map/pallas_call | solution.py:528
  374.7 7.4 %shard_map.182 = bf16[1280,960]{1,0:T(8,128)(2,1)} custom-call(bf16[960,1024]{1,0:T(8,128)(2,1)} %bitcast.231, bf16[1024,1280]{1,0:T(8,128)(2,1)} %get-tuple-element.190.normed_ref), custom_call_target="tpu_custom_call" | custom-call | flops 1048576 | bytes 1048576 | tf_op jit(solution)/shard_map/pallas_call | solution.py:850
  382.1 4.9 add_bitcast_fusion
  392.9 8.5 %shard_map.183 = (f32[2,2,128,1280]{3,2,1,0:T(8,128)}, bf16[2,2,128,1280]{3,2,1,0:T(8,128)(2,1)}) custom-call(s32[3]{0:T(128)S(1)} %pad_add_fusion.place_ref.core_ref, bf16[960,1024]{1,0:T(8,128)(2,1)} %bitcast.232, bf16[1280,960]{1,0:T(8,128)(2,1)} %bitcast.230), custom_call_target="tpu_custom_call" | custom-call | flops 1048576 | bytes 1048576 | tf_op jit(solution)/shard_map/pallas_call | solution.py:820
  423.5 18.4 %collective-permute-done.47 = f32[2,80]{1,0:T(2,128)S(1)} collective-permute-done((f32[2,80]{1,0:T(2,128)S(1)}, f32[2,80]{1,0:T(2,128)S(1)}, u32[]{:S(2)}, u32[]{:S(2)}) %collective-permute-start.47) | collective-permute-done | bytes 672 | tf_op jit(solution)/shard_map/ppermute | solution.py:870
  457.7 10.4 %collective-permute-done.48 = bf16[2,128,1280]{2,1,0:T(8,128)(2,1)} collective-permute-done((bf16[2,128,1280]{2,1,0:T(8,128)(2,1)}, bf16[2,128,1280]{2,1,0:T(8,128)(2,1)}, u32[]{:S(2)}, u32[]{:S(2)}) %collective-permute-start.48) | collective-permute-done | bytes 655392 | tf_op jit(solution)/shard_map/ppermute | solution.py:870
  479.0 5.0 reduce-scatter.11.cloned.1.call-done
  (389 shorter events, 202.7 us)
Async XLA Ops:
  15.2 41.9 %all-gather.7.cloned.1.call-start = ((), (), s32[]{:S(2)}) async-start(), calls=%async_computation.16 | async-start | bytes 1638400 | tf_op jit(solution)/shard_map/all_gather | solution.py:904
  24.8 64.1 %all-gather.9.cloned.1.call-start = ((), (), s32[]{:S(2)}) async-start(), calls=%async_computation.17 | async-start | bytes 1536000 | tf_op jit(solution)/shard_map/all_gather | solution.py:904
  57.1 30.1 %collective-permute-start.5 = (bf16[4,160,964]{2,1,0:T(8,128)(2,1)}, bf16[4,160,964]{2,1,0:T(8,128)(2,1)S(1)}, u32[]{:S(2)}, u32[]{:S(2)}) collective-permute-start(bf16[4,160,964]{2,1,0:T(8,128)(2,1)} %bitcast.252), channel_id=1, source_target_pairs={{0,4},{4,0},{1,5},{5,1},{2,6},{6,2},{3,7},{7,3},{8,12},{12,8},{9,1... | collective-permute-start | bytes 3701768 | tf_op jit(solution)/shard_map/ppermute | solution.py:870
  63.8 77.9 %all-gather.11.cloned.1.call-start = ((), (), s32[]{:S(2)}) async-start(), calls=%async_computation.18 | async-start | bytes 3072000 | tf_op jit(solution)/shard_map/all_gather | solution.py:904
  89.9 28.4 %collective-permute-start.7 = (bf16[4,40,3840]{2,1,0:T(8,128)(2,1)}, bf16[4,40,3840]{2,1,0:T(8,128)(2,1)S(1)}, u32[]{:S(2)}, u32[]{:S(2)}) collective-permute-start(bf16[4,40,3840]{2,1,0:T(8,128)(2,1)} %bitcast.19.refs_0_), channel_id=1, source_target_pairs={{0,2},{1,3},{2,0},{3,1},{4,6},{5,7},{6,4},{7,5},{8,10},{9,11},{10,... | collective-permute-start | bytes 3686408 | tf_op jit(solution)/shard_map/ppermute | solution.py:870
  91.4 28.2 %collective-permute-start.6 = (bf16[4,40,3840]{2,1,0:T(8,128)(2,1)}, bf16[4,40,3840]{2,1,0:T(8,128)(2,1)}, u32[]{:S(2)}, u32[]{:S(2)}) collective-permute-start(bf16[4,40,3840]{2,1,0:T(8,128)(2,1)} %bitcast.19.refs_0_), channel_id=1, source_target_pairs={{0,4},{4,0},{1,5},{5,1},{2,6},{6,2},{3,7},{7,3},{8,12},{12,8},{9,1... | collective-permute-start | bytes 3686408 | tf_op jit(solution)/shard_map/ppermute | solution.py:870
  123.9 20.7 %collective-permute-start.8 = (bf16[4,40,1920]{2,1,0:T(8,128)(2,1)}, bf16[4,40,1920]{2,1,0:T(8,128)(2,1)}, u32[]{:S(2)}, u32[]{:S(2)}) collective-permute-start(bf16[4,40,1920]{2,1,0:T(8,128)(2,1)} %slice.153), channel_id=1, source_target_pairs={{0,2},{1,3},{2,0},{3,1},{4,6},{5,7},{6,4},{7,5},{8,10},{9,11},{10,... | collective-permute-start | bytes 1843208 | tf_op jit(solution)/shard_map/ppermute | solution.py:870
  124.4 20.2 %all-to-all-start.2 = ((bf16[4,320,256]{2,1,0:T(8,128)(2,1)}), bf16[4,320,256]{2,1,0:T(8,128)(2,1)S(1)}, u32[]{:S(2)}, u32[]{:S(2)}) async-start(bf16[4,320,256]{2,1,0:T(8,128)(2,1)} %bitcast.31), calls=%async_computation.2 | async-start | bytes 1310720 | tf_op jit(solution)/shard_map/all_to_all | solution.py:891
  128.8 19.2 %collective-permute-start.11 = (bf16[4,40,3840]{2,1,0:T(8,128)(2,1)}, bf16[4,40,3840]{2,1,0:T(8,128)(2,1)}, u32[]{:S(2)}, u32[]{:S(2)}) collective-permute-start(bf16[4,40,3840]{2,1,0:T(8,128)(2,1)} %collective-permute-done.6.refs_1_), channel_id=1, source_target_pairs={{0,1},{1,0},{2,3},{3,2},{4,5},{5,4},{6,7},{7,6},{8,9},{9,8},{10,11... | collective-permute-start | bytes 3686408 | tf_op jit(solution)/shard_map/ppermute | solution.py:870
  128.8 19.2 %collective-permute-start.12 = (bf16[4,40,3840]{2,1,0:T(8,128)(2,1)S(1)}, bf16[4,40,3840]{2,1,0:T(8,128)(2,1)}, u32[]{:S(2)}, u32[]{:S(2)}) collective-permute-start(bf16[4,40,3840]{2,1,0:T(8,128)(2,1)S(1)} %collective-permute-done.7.refs_2_), channel_id=1, source_target_pairs={{0,1},{1,0},{2,3},{3,2},{4,5},{5,4},{6,7},{7,6},{8,9},{9,8},{10,11... | collective-permute-start | bytes 3686408 | tf_op jit(solution)/shard_map/ppermute | solution.py:870
  147.4 29.5 %collective-permute-start.16 = (bf16[4,40,3840]{2,1,0:T(8,128)(2,1)S(1)}, bf16[4,40,3840]{2,1,0:T(8,128)(2,1)S(1)}, u32[]{:S(2)}, u32[]{:S(2)}) collective-permute-start(bf16[4,40,3840]{2,1,0:T(8,128)(2,1)S(1)} %get-tuple-element.250.along_ref), channel_id=1, source_target_pairs={{0,4},{4,0},{1,5},{5,1},{2,6},{6,2},{3,7},{7,3},{8,12},{12,8},{9,1... | collective-permute-start | bytes 3686408 | tf_op jit(solution)/shard_map/ppermute | solution.py:870
  176.9 28.7 %collective-permute-start.20 = (bf16[4,40,3840]{2,1,0:T(8,128)(2,1)S(1)}, bf16[4,40,3840]{2,1,0:T(8,128)(2,1)S(1)}, u32[]{:S(2)}, u32[]{:S(2)}) collective-permute-start(bf16[4,40,3840]{2,1,0:T(8,128)(2,1)S(1)} %get-tuple-element.141.refs_0_), channel_id=1, source_target_pairs={{0,2},{1,3},{2,0},{3,1},{4,6},{5,7},{6,4},{7,5},{8,10},{9,11},{10,... | collective-permute-start | bytes 3686408 | tf_op jit(solution)/shard_map/ppermute | solution.py:870
  177.4 28.6 %collective-permute-start.19 = (bf16[4,40,3840]{2,1,0:T(8,128)(2,1)S(1)}, bf16[4,40,3840]{2,1,0:T(8,128)(2,1)}, u32[]{:S(2)}, u32[]{:S(2)}) collective-permute-start(bf16[4,40,3840]{2,1,0:T(8,128)(2,1)S(1)} %get-tuple-element.141.refs_0_), channel_id=1, source_target_pairs={{0,4},{4,0},{1,5},{5,1},{2,6},{6,2},{3,7},{7,3},{8,12},{12,8},{9,1... | collective-permute-start | bytes 3686408 | tf_op jit(solution)/shard_map/ppermute | solution.py:870
  207.2 21.8 %collective-permute-start.22 = (bf16[4,40,1920]{2,1,0:T(8,128)(2,1)S(1)}, bf16[4,40,1920]{2,1,0:T(8,128)(2,1)S(1)}, u32[]{:S(2)}, u32[]{:S(2)}) collective-permute-start(bf16[4,40,1920]{2,1,0:T(8,128)(2,1)S(1)} %slice.167), channel_id=1, source_target_pairs={{0,4},{4,0},{1,5},{5,1},{2,6},{6,2},{3,7},{7,3},{8,12},{12,8},{9,1... | collective-permute-start | bytes 1843208 | tf_op jit(solution)/shard_map/ppermute | solution.py:870
  208.3 20.7 %collective-permute-start.21 = (bf16[4,40,1920]{2,1,0:T(8,128)(2,1)S(1)}, bf16[4,40,1920]{2,1,0:T(8,128)(2,1)S(1)}, u32[]{:S(2)}, u32[]{:S(2)}) collective-permute-start(bf16[4,40,1920]{2,1,0:T(8,128)(2,1)S(1)} %slice.166), channel_id=1, source_target_pairs={{0,2},{1,3},{2,0},{3,1},{4,6},{5,7},{6,4},{7,5},{8,10},{9,11},{10,... | collective-permute-start | bytes 1843208 | tf_op jit(solution)/shard_map/ppermute | solution.py:870
  209.8 19.8 %collective-permute-start.23 = (bf16[4,40,3840]{2,1,0:T(8,128)(2,1)S(1)}, bf16[4,40,3840]{2,1,0:T(8,128)(2,1)S(1)}, u32[]{:S(2)}, u32[]{:S(2)}) collective-permute-start(bf16[4,40,3840]{2,1,0:T(8,128)(2,1)S(1)} %get-tuple-element.141.refs_0_), channel_id=1, source_target_pairs={{0,1},{1,0},{2,3},{3,2},{4,5},{5,4},{6,7},{7,6},{8,9},{9,8},{10,11... | collective-permute-start | bytes 3686408 | tf_op jit(solution)/shard_map/ppermute | solution.py:870
  209.8 22.2 %collective-permute-start.24 = (bf16[4,40,3840]{2,1,0:T(8,128)(2,1)}, bf16[4,40,3840]{2,1,0:T(8,128)(2,1)S(1)}, u32[]{:S(2)}, u32[]{:S(2)}) collective-permute-start(bf16[4,40,3840]{2,1,0:T(8,128)(2,1)} %collective-permute-done.19.refs_1_), channel_id=1, source_target_pairs={{0,1},{1,0},{2,3},{3,2},{4,5},{5,4},{6,7},{7,6},{8,9},{9,8},{10,11... | collective-permute-start | bytes 3686408 | tf_op jit(solution)/shard_map/ppermute | solution.py:870
  210.3 21.7 %collective-permute-start.25 = (bf16[4,40,3840]{2,1,0:T(8,128)(2,1)S(1)}, bf16[4,40,3840]{2,1,0:T(8,128)(2,1)S(1)}, u32[]{:S(2)}, u32[]{:S(2)}) collective-permute-start(bf16[4,40,3840]{2,1,0:T(8,128)(2,1)S(1)} %collective-permute-done.20.refs_2_), channel_id=1, source_target_pairs={{0,1},{1,0},{2,3},{3,2},{4,5},{5,4},{6,7},{7,6},{8,9},{9,8},{10,11... | collective-permute-start | bytes 3686408 | tf_op jit(solution)/shard_map/ppermute | solution.py:870
  239.5 19.2 %collective-permute-start.28 = (bf16[128,1280]{1,0:T(8,128)(2,1)}, bf16[128,1280]{1,0:T(8,128)(2,1)}, u32[]{:S(2)}, u32[]{:S(2)}) collective-permute-start(bf16[128,1280]{1,0:T(8,128)(2,1)} %dynamic-slice_bitcast_fusion.3), channel_id=1, source_target_pairs={{0,4},{4,0},{1,5},{5,1},{2,6},{6,2},{3,7},{7,3},{8,12},{12,8},{9,1... | collective-permute-start | bytes 983048 | tf_op jit(solution)/shard_map/ppermute | solution.py:870
  249.9 106.4 %reduce-scatter.5.cloned.1.call-start = ((), (), s32[]{:S(2)}) async-start(), calls=%async_computation.12 | async-start | bytes 3276800 | tf_op jit(solution)/shard_map/reduce_scatter | solution.py:920
  303.7 42.3 %collective-permute-start.34 = (bf16[4,40,3840]{2,1,0:T(8,128)(2,1)}, bf16[4,40,3840]{2,1,0:T(8,128)(2,1)}, u32[]{:S(2)}, u32[]{:S(2)}) collective-permute-start(bf16[4,40,3840]{2,1,0:T(8,128)(2,1)} %pad_maximum_fusion), channel_id=1, source_target_pairs={{0,4},{4,0},{1,5},{5,1},{2,6},{6,2},{3,7},{7,3},{8,12},{12,8},{9,1... | collective-permute-start | bytes 3686408 | tf_op jit(solution)/shard_map/ppermute | solution.py:870
  320.6 35.6 %collective-permute-start.35 = (bf16[4,40,3840]{2,1,0:T(8,128)(2,1)}, bf16[4,40,3840]{2,1,0:T(8,128)(2,1)}, u32[]{:S(2)}, u32[]{:S(2)}) collective-permute-start(bf16[4,40,3840]{2,1,0:T(8,128)(2,1)} %pad_maximum_fusion.1), channel_id=1, source_target_pairs={{0,2},{1,3},{2,0},{3,1},{4,6},{5,7},{6,4},{7,5},{8,10},{9,11},{10,... | collective-permute-start | bytes 3686408 | tf_op jit(solution)/shard_map/ppermute | solution.py:870
  333.3 23.0 %all-to-all-start.5 = ((bf16[4,320,256]{2,1,0:T(8,128)(2,1)}), bf16[4,320,256]{2,1,0:T(8,128)(2,1)}, u32[]{:S(2)}, u32[]{:S(2)}) async-start(bf16[4,320,256]{2,1,0:T(8,128)(2,1)} %bitcast.65), calls=%async_computation.5 | async-start | bytes 1310720 | tf_op jit(solution)/shard_map/all_to_all | solution.py:891
  337.5 63.9 %reduce-scatter.7.cloned.1.call-start = ((), (), s32[]{:S(2)}) async-start(), calls=%async_computation.13 | async-start | bytes 1536000 | tf_op jit(solution)/shard_map/reduce_scatter | solution.py:920
  356.3 25.7 %collective-permute-start.37 = (bf16[2,2,4,40,3840]{4,3,2,1,0:T(8,128)(2,1)}, bf16[2,2,4,40,3840]{4,3,2,1,0:T(8,128)(2,1)}, u32[]{:S(2)}, u32[]{:S(2)}) collective-permute-start(bf16[2,2,4,40,3840]{4,3,2,1,0:T(8,128)(2,1)} %get-tuple-element.191), channel_id=1, source_target_pairs={{0,1},{1,0},{2,3},{3,2},{4,5},{5,4},{6,7},{7,6},{8,9},{9,8},{10,11... | collective-permute-start | bytes 14745608 | tf_op jit(solution)/shard_map/ppermute | solution.py:870
  358.9 85.8 %reduce-scatter.9.cloned.1.call-start = ((), (), s32[]{:S(2)}) async-start(), calls=%async_computation.14 | async-start | bytes 3276800 | tf_op jit(solution)/shard_map/reduce_scatter | solution.py:920
  382.0 102.0 %reduce-scatter.11.cloned.1.call-start = ((), (), s32[]{:S(2)}) async-start(), calls=%async_computation.15 | async-start | bytes 1536000 | tf_op jit(solution)/shard_map/reduce_scatter | solution.py:920
  412.4 29.5 %collective-permute-start.42 = (bf16[2,2,128,1280]{3,2,1,0:T(8,128)(2,1)S(1)}, bf16[2,2,128,1280]{3,2,1,0:T(8,128)(2,1)S(1)}, u32[]{:S(2)}, u32[]{:S(2)}) collective-permute-start(bf16[2,2,128,1280]{3,2,1,0:T(8,128)(2,1)S(1)} %copy-done.66), channel_id=1, source_target_pairs={{0,1},{1,0},{2,3},{3,2},{4,5},{5,4},{6,7},{7,6},{8,9},{9,8},{10,11... | collective-permute-start | bytes 3932168 | tf_op jit(solution)/shard_map/ppermute | solution.py:870
  412.4 31.2 %collective-permute-start.43 = (bf16[4,40,3840]{2,1,0:T(8,128)(2,1)S(1)}, bf16[4,40,3840]{2,1,0:T(8,128)(2,1)S(1)}, u32[]{:S(2)}, u32[]{:S(2)}) collective-permute-start(bf16[4,40,3840]{2,1,0:T(8,128)(2,1)S(1)} %pad_maximum_fusion.2), channel_id=1, source_target_pairs={{0,4},{4,0},{1,5},{5,1},{2,6},{6,2},{3,7},{7,3},{8,12},{12,8},{9,1... | collective-permute-start | bytes 3686408 | tf_op jit(solution)/shard_map/ppermute | solution.py:870
  413.8 30.9 %collective-permute-start.44 = (bf16[4,40,3840]{2,1,0:T(8,128)(2,1)S(1)}, bf16[4,40,3840]{2,1,0:T(8,128)(2,1)}, u32[]{:S(2)}, u32[]{:S(2)}) collective-permute-start(bf16[4,40,3840]{2,1,0:T(8,128)(2,1)S(1)} %pad_maximum_fusion.3), channel_id=1, source_target_pairs={{0,2},{1,3},{2,0},{3,1},{4,6},{5,7},{6,4},{7,5},{8,10},{9,11},{10,... | collective-permute-start | bytes 3686408 | tf_op jit(solution)/shard_map/ppermute | solution.py:870
  422.8 19.1 %collective-permute-start.47 = (f32[2,80]{1,0:T(2,128)S(1)}, f32[2,80]{1,0:T(2,128)S(1)}, u32[]{:S(2)}, u32[]{:S(2)}) collective-permute-start(f32[2,80]{1,0:T(2,128)S(1)} %add.392), channel_id=1, source_target_pairs={{0,4},{4,0},{1,5},{5,1},{2,6},{6,2},{3,7},{7,3},{8,12},{12,8},{9,1... | collective-permute-start | bytes 1928 | tf_op jit(solution)/shard_map/ppermute | solution.py:870
  452.2 22.4 %collective-permute-start.50 = (bf16[160,960]{1,0:T(8,128)(2,1)}, bf16[160,960]{1,0:T(8,128)(2,1)}, u32[]{:S(2)}, u32[]{:S(2)}) collective-permute-start(bf16[160,960]{1,0:T(8,128)(2,1)} %dynamic-slice_bitcast_fusion), channel_id=1, source_target_pairs={{0,4},{4,0},{1,5},{5,1},{2,6},{6,2},{3,7},{7,3},{8,12},{12,8},{9,1... | collective-permute-start | bytes 921608 | tf_op jit(solution)/shard_map/ppermute | solution.py:870
  (105 other events, 850.8 us)
Sparse Core Ops, SparseCore 0:
  24.9 32.0 all-gather.6
  58.6 30.2 all-gather.8
  90.5 51.1 all-gather.10
  303.8 51.8 reduce-scatter.4
  359.0 31.1 reduce-scatter.6
  392.5 50.8 reduce-scatter.8
  453.7 30.2 reduce-scatter.10

commit v29 on v27

--- a/solution.py
+++ b/solution.py
@@ -1136,7 +1136,7 @@
             moved = over_head(earlier.reshape(4, -1, earlier.shape[-1]))
             dense_first = over_batch(own)
             normed_grad = scatter_row(halves)
-            z_across, dense_first = tied(across_sum(z_sum), dense_first)
+            z_across = across_sum(z_sum)
             z_across = over_head(z_across.reshape(4, -1, z_across.shape[-1]))
             dense_grad = [dense_first, summed]
             qkv_grads = [columns_to_rows(z_across), columns_to_rows(moved)]
@@ -1155,7 +1155,8 @@
             normed_grad, beside = tied(normed_grad, rows[1])
             beside = swapped(beside, "head", 2)
         upper = middle_grad + lower_of(normed_grad, stream, factor_one, gains[layer])
-    input_grad = swap_halves(upper.astype(BF16).reshape(tokens.shape)).astype(F32)
+    upper, dense_grad[0] = tied(upper.astype(BF16), dense_grad[0])
+    input_grad = swap_halves(upper.reshape(tokens.shape)).astype(F32)
     scale_grad = scale_sum * (SCALE_BASE / math.sqrt(head_dim)) * jax.nn.sigmoid(scale_param)
     dense_all = jnp.stack([part.astype(F32) for part in dense_grad])
     qkv_all = jnp.stack(qkv_grads)

time: 512 us -> 513 us (level)
    unnamed x144 -> x142, local copies, waits for them, and re-layouts: 11.6 us -> 9.67 us
  transfers between devices with their start and end apart: 65 -> 65, of which waited for: 32 -> 33; matrix products, arithmetic and copies ran while one was open for 13% -> 15% of each run, Pallas kernels for 22% -> 22%
where the time goes in v29:
time: 513 us; the launch traced here: 505 us
  waiting for transfers between devices  178 us (35%)
  Pallas kernels  113 us (22%)
  starting transfers between devices  73.4 us (14%)
  other arithmetic  50.3 us (10%)
  local copies, waits for them, and re-layouts  36.2 us (7%)
  matrix products  19.6 us (4%)
  blocking collectives  18.7 us (4%)
  between operations  15.9 us (3%)
    ppermute x51, waiting for transfers between devices, swapped(): return lax.ppermute(array, axis, [(i, i ^ mask) for i in range(size)])  133 us
    ppermute x51, starting transfers between devices, swapped(): return lax.ppermute(array, axis, [(i, i ^ mask) for i in range(size)])  45.5 us
    all_to_all x7, waiting for transfers between devices, over_head(): lax.all_to_all(parts, 'head', split_axis=0, concat_axis=0, tiled=True)  29.9 us
    all_to_all x7, starting transfers between devices, over_head(): lax.all_to_all(parts, 'head', split_axis=0, concat_axis=0, tiled=True)  27.5 us
    pallas_call x2, Pallas kernels, attend_back_rows(): pl.pallas_call(functools.partial(attend_back_kernel, token_rows), grid=(l...  24.8 us
    all_to_all x1, blocking collectives, over_head(): lax.all_to_all(parts, 'head', split_axis=0, concat_axis=0, tiled=True)  18.7 us
    pallas_call x2, Pallas kernels, dense_grads(): pl.pallas_call(dense_grad_kernel, grid_spec=pltpu.PrefetchScalarGridSpec(...  17 us
    all_gather x3, waiting for transfers between devices, along_batch(): return lax.all_gather(piece, 'batch', axis=0, tiled=False)  14.8 us
  transfers between devices with their start and end apart: 65, of which 33 were waited for; matrix products, arithmetic and copies ran while one was open for 15% of the time, Pallas kernels for 22%

profile of v29, /device:TPU:0, one launch (start us, length us, event | category | flops | bytes accessed | tf_op | source)
XLA Modules:
  0.0 504.8 jit_solution(18422674322784466965)
XLA Ops:
  10.9 4.2 all-to-all-start
  15.2 6.7 %all-to-all-done = bf16[4,40,964]{2,1,0:T(8,128)(2,1)S(1)} async-done(((bf16[4,40,964]{2,1,0:T(8,128)(2,1)}), bf16[4,40,964]{2,1,0:T(8,128)(2,1)S(1)}, u32[]{:S(2)}, u32[]{:S(2)}) %all-to-all-start) | async-done | bytes 308512 | tf_op jit(solution)/shard_map/all_to_all | solution.py:891
  24.2 7.4 %collective-permute-done = bf16[128,1280]{1,0:T(8,128)(2,1)S(1)} collective-permute-done((bf16[128,1280]{1,0:T(8,128)(2,1)S(1)}, bf16[128,1280]{1,0:T(8,128)(2,1)S(1)}, u32[]{:S(2)}, u32[]{:S(2)}) %collective-permute-start) | collective-permute-done | bytes 327712 | tf_op jit(solution)/shard_map/ppermute | solution.py:870
  36.4 11.8 %collective-permute-done.2.refs_2_ = bf16[256,1280]{1,0:T(8,128)(2,1)S(1)} collective-permute-done((bf16[256,1280]{1,0:T(8,128)(2,1)S(1)}, bf16[256,1280]{1,0:T(8,128)(2,1)S(1)}, u32[]{:S(2)}, u32[]{:S(2)}) %collective-permute-start.2) | collective-permute-done | bytes 655392 | tf_op jit(solution)/shard_map/ppermute | solution.py:870
  50.4 6.0 %all-gather.7.cloned.1.call-done = bf16[640,964]{1,0:T(8,128)(2,1)} async-done(((bf16[160,964]{1,0:T(8,128)(2,1)}), bf16[640,964]{1,0:T(8,128)(2,1)}) %all-gather.7.cloned.1.call-update) | async-done | bytes 1233936 | tf_op jit(solution)/shard_map/all_gather | solution.py:904
  63.2 6.6 %all-to-all-done.1 = bf16[4,40,960]{2,1,0:T(8,128)(2,1)S(1)} async-done(((bf16[4,40,960]{2,1,0:T(8,128)(2,1)}), bf16[4,40,960]{2,1,0:T(8,128)(2,1)S(1)}, u32[]{:S(2)}, u32[]{:S(2)}) %all-to-all-start.1) | async-done | bytes 307232 | tf_op jit(solution)/shard_map/all_to_all | solution.py:891
  70.1 16.5 %collective-permute-done.5.across_ref = bf16[4,160,964]{2,1,0:T(8,128)(2,1)S(1)} collective-permute-done((bf16[4,160,964]{2,1,0:T(8,128)(2,1)}, bf16[4,160,964]{2,1,0:T(8,128)(2,1)S(1)}, u32[]{:S(2)}, u32[]{:S(2)}) %collective-permute-start.5) | collective-permute-done | bytes 1233952 | tf_op jit(solution)/shard_map/ppermute | solution.py:870
  92.7 4.6 shard_map.169
  99.3 7.7 %shard_map.170 = (bf16[1024,1280]{1,0:T(8,128)(2,1)}, f32[960,1024]{1,0:T(8,128)S(1)}) custom-call(s32[3]{0:T(128)S(1)} %pad_add_fusion.place_ref.core_ref, bf16[256,1280]{1,0:T(8,128)(2,1)} %bitcast.235, bf16[256,1280]{1,0:T(8,128)(2,1)} %copy-done.55, bf16[256,1280]{1,0:T(8,128)(2,1)} %copy-done.54, bf16[256,1280]{1,0:T(8,128)(2,1)} %collective-permute-done.3.refs_3_, ...), custom_call_target="tpu_custom_call" | custom-call | flops 1048576 | bytes 1048576 | tf_op jit(solution)/shard_map/pallas_call | solution.py:733
  107.0 6.7 %shard_map.171 = (bf16[4,4,80,256]{3,2,1,0:T(8,128)(2,1)}, f32[4,1,1024]{2,1,0:T(1,128)S(1)}) custom-call(f32[3,4,80,1024]{3,2,1,0:T(8,128)S(1)} %bitcast.203, f32[80,1]{1,0:T(8,128)S(1)} %copy.60.scale_ref, s32[1024,1]{1,0:T(8,128)S(1)} %copy.61.col_ref, s32[1,1024]{1,0:T(1,128)S(1)} %constant_dynamic-slice_fusion.row_ref), custom_call_target="tpu_custom_call" | custom-call | flops 1048576 | bytes 1048576 | tf_op jit(solution)/shard_map/pallas_call | solution.py:435
  128.7 5.3 %collective-permute-done.9.refs_4_ = bf16[4,40,1920]{2,1,0:T(8,128)(2,1)} collective-permute-done((bf16[4,40,1920]{2,1,0:T(8,128)(2,1)}, bf16[4,40,1920]{2,1,0:T(8,128)(2,1)}, u32[]{:S(2)}, u32[]{:S(2)}) %collective-permute-start.9) | collective-permute-done | bytes 614432 | tf_op jit(solution)/shard_map/ppermute | solution.py:870
  134.0 7.1 %all-gather.11.cloned.1.call-done = bf16[8,40,3840]{2,1,0:T(8,128)(2,1)} async-done(((bf16[2,40,3840]{2,1,0:T(8,128)(2,1)}), bf16[8,40,3840]{2,1,0:T(8,128)(2,1)}) %all-gather.11.cloned.1.call-update) | async-done | bytes 2457616 | tf_op jit(solution)/shard_map/all_gather | solution.py:904
  147.4 4.5 shard_map.172
  159.6 16.6 %collective-permute-done.16.across_ref = bf16[4,40,3840]{2,1,0:T(8,128)(2,1)S(1)} collective-permute-done((bf16[4,40,3840]{2,1,0:T(8,128)(2,1)S(1)}, bf16[4,40,3840]{2,1,0:T(8,128)(2,1)S(1)}, u32[]{:S(2)}, u32[]{:S(2)}) %collective-permute-start.16) | collective-permute-done | bytes 1228832 | tf_op jit(solution)/shard_map/ppermute | solution.py:870
  178.9 4.8 shard_map.173
  183.7 6.6 %shard_map.174 = (bf16[1024,1280]{1,0:T(8,128)(2,1)}, f32[960,1024]{1,0:T(8,128)S(1)}) custom-call(s32[3]{0:T(128)S(1)} %pad_add_fusion.place_ref.core_ref, bf16[256,1280]{1,0:T(8,128)(2,1)} %multiply_convert_fusion.2.refs_0_, bf16[256,1280]{1,0:T(8,128)(2,1)} %collective-permute-done.17.refs_1_, bf16[256,1280]{1,0:T(8,128)(2,1)} %collective-permute-done.15.refs_2_, ...), custom_call_target="tpu_custom_call" | custom-call | flops 1048576 | bytes 1048576 | tf_op jit(solution)/shard_map/pallas_call | solution.py:733
  190.3 6.1 %shard_map.175 = (bf16[4,4,80,256]{3,2,1,0:T(8,128)(2,1)S(1)}, f32[4,1,1024]{2,1,0:T(1,128)S(1)}) custom-call(f32[3,4,80,1024]{3,2,1,0:T(8,128)S(1)} %bitcast.205, f32[80,1]{1,0:T(8,128)S(1)} %copy.64.scale_ref, s32[1024,1]{1,0:T(8,128)S(1)} %copy.61.col_ref, s32[1,1024]{1,0:T(1,128)S(1)} %constant_dynamic-slice_fusion.row_ref), custom_call_target="tpu_custom_call" | custom-call | flops 1048576 | bytes 1048576 | tf_op jit(solution)/shard_map/pallas_call | solution.py:435
  196.4 8.6 %collective-permute-done.20.refs_2_ = bf16[4,40,3840]{2,1,0:T(8,128)(2,1)S(1)} collective-permute-done((bf16[4,40,3840]{2,1,0:T(8,128)(2,1)S(1)}, bf16[4,40,3840]{2,1,0:T(8,128)(2,1)S(1)}, u32[]{:S(2)}, u32[]{:S(2)}) %collective-permute-start.20) | collective-permute-done | bytes 1228832 | tf_op jit(solution)/shard_map/ppermute | solution.py:870
  209.7 18.7 %all_to_all.40 = bf16[4,320,256]{2,1,0:T(8,128)(2,1)S(1)} all-to-all(bf16[4,320,256]{2,1,0:T(8,128)(2,1)S(1)} %bitcast.221), channel_id=1, replica_groups=mesh['batch'=4,'blk'=2,'head'=4] {'head'}, dimensions={0} | all-to-all | bytes 1310720 | tf_op jit(solution)/shard_map/all_to_all | solution.py:891
  249.5 8.5 %shard_map.177 = (bf16[2,2,4,40,3840]{4,3,2,1,0:T(8,128)(2,1)}, bf16[2,2,4,40,3840]{4,3,2,1,0:T(8,128)(2,1)}) custom-call(s32[3]{0:T(128)S(1)} %pad_add_fusion.place_ref.core_ref, bf16[1280,256]{1,0:T(8,128)(2,1)} %bitcast.243, bf16[256,1280]{1,0:T(8,128)(2,1)} %copy-done.31, bf16[256,1280]{1,0:T(8,128)(2,1)} %copy-done.52, bf16[256,1280]{1,0:T(8,128)(2,1)} %copy-done.32, ...), custom_call_target="tpu_custom_call" | custom-call | flops 1048576 | bytes 1048576 | tf_op jit(solution)/shard_map/pallas_call | solution.py:599
  260.4 12.5 %shard_map.178 = (bf16[3,4,80,1024]{3,2,1,0:T(8,128)(2,1)}, f32[80,128]{1,0:T(8,128)}) custom-call(f32[3,4,80,1024]{3,2,1,0:T(8,128)} %bitcast.206, bf16[4,4,80,256]{3,2,1,0:T(8,128)(2,1)} %bitcast.56.grad_ref, f32[4,1,1024]{2,1,0:T(1,128)S(1)} %get-tuple-element.156.lse_ref, f32[80,1]{1,0:T(8,128)S(1)} %copy.64.scale_ref, s32[1024,1]{1,0:T(8,128)S(1)} %copy.61.col_ref, ...), custom_call_target="tpu_custom_call" | custom-call | flops 1048576 | bytes 1048576 | tf_op jit(solution)/shard_map/pallas_call | solution.py:528
  278.2 11.3 %shard_map.179 = (f32[2,2,128,1280]{3,2,1,0:T(8,128)}, bf16[2,2,128,1280]{3,2,1,0:T(8,128)(2,1)}, bf16[1280,960]{1,0:T(8,128)(2,1)}) custom-call(s32[3]{0:T(128)S(1)} %pad_add_fusion.place_ref.core_ref, bf16[960,1024]{1,0:T(8,128)(2,1)} %bitcast.245, bf16[1280,960]{1,0:T(8,128)(2,1)} %bitcast.223, bf16[1024,1280]{1,0:T(8,128)(2,1)} %get-tuple-element.163.normed_ref), custom_call_target="tpu_custom_call" | custom-call | flops 1048576 | bytes 1048576 | tf_op jit(solution)/shard_map/pallas_call | solution.py:779
  304.5 13.8 %collective-permute-done.33 = bf16[2,128,1280]{2,1,0:T(8,128)(2,1)} collective-permute-done((bf16[2,128,1280]{2,1,0:T(8,128)(2,1)}, bf16[2,128,1280]{2,1,0:T(8,128)(2,1)}, u32[]{:S(2)}, u32[]{:S(2)}) %collective-permute-start.33) | collective-permute-done | bytes 655392 | tf_op jit(solution)/shard_map/ppermute | solution.py:870
  336.8 8.5 %shard_map.180 = (bf16[2,2,4,40,3840]{4,3,2,1,0:T(8,128)(2,1)}, bf16[2,2,4,40,3840]{4,3,2,1,0:T(8,128)(2,1)}) custom-call(s32[3]{0:T(128)S(1)} %pad_add_fusion.place_ref.core_ref, bf16[1280,256]{1,0:T(8,128)(2,1)} %bitcast.240, bf16[256,1280]{1,0:T(8,128)(2,1)} %copy-done.30, bf16[256,1280]{1,0:T(8,128)(2,1)} %copy-done.48, bf16[256,1280]{1,0:T(8,128)(2,1)} %copy-done.36, ...), custom_call_target="tpu_custom_call" | custom-call | flops 1048576 | bytes 1048576 | tf_op jit(solution)/shard_map/pallas_call | solution.py:599
  347.8 7.8 %all-to-all-done.5 = bf16[4,320,256]{2,1,0:T(8,128)(2,1)} async-done(((bf16[4,320,256]{2,1,0:T(8,128)(2,1)}), bf16[4,320,256]{2,1,0:T(8,128)(2,1)}, u32[]{:S(2)}, u32[]{:S(2)}) %all-to-all-start.5) | async-done | bytes 655392 | tf_op jit(solution)/shard_map/all_to_all | solution.py:891
  360.8 12.3 %shard_map.181 = (bf16[3,4,80,1024]{3,2,1,0:T(8,128)(2,1)}, f32[80,128]{1,0:T(8,128)}) custom-call(f32[3,4,80,1024]{3,2,1,0:T(8,128)} %bitcast.204, bf16[4,4,80,256]{3,2,1,0:T(8,128)(2,1)} %bitcast.69.grad_ref, f32[4,1,1024]{2,1,0:T(1,128)S(1)} %get-tuple-element.186.lse_ref, f32[80,1]{1,0:T(8,128)S(1)} %copy.60.scale_ref, s32[1024,1]{1,0:T(8,128)S(1)} %copy.61.col_ref, ...), custom_call_target="tpu_custom_call" | custom-call | flops 1048576 | bytes 1048576 | tf_op jit(solution)/shard_map/pallas_call | solution.py:528
  374.0 7.3 %shard_map.182 = bf16[1280,960]{1,0:T(8,128)(2,1)} custom-call(bf16[960,1024]{1,0:T(8,128)(2,1)} %bitcast.231, bf16[1024,1280]{1,0:T(8,128)(2,1)} %get-tuple-element.190.normed_ref), custom_call_target="tpu_custom_call" | custom-call | flops 1048576 | bytes 1048576 | tf_op jit(solution)/shard_map/pallas_call | solution.py:850
  381.4 4.9 add_bitcast_fusion
  392.1 8.5 %shard_map.183 = (f32[2,2,128,1280]{3,2,1,0:T(8,128)}, bf16[2,2,128,1280]{3,2,1,0:T(8,128)(2,1)}) custom-call(s32[3]{0:T(128)S(1)} %pad_add_fusion.place_ref.core_ref, bf16[960,1024]{1,0:T(8,128)(2,1)} %bitcast.232, bf16[1280,960]{1,0:T(8,128)(2,1)} %bitcast.230), custom_call_target="tpu_custom_call" | custom-call | flops 1048576 | bytes 1048576 | tf_op jit(solution)/shard_map/pallas_call | solution.py:820
  422.8 18.4 %collective-permute-done.47 = f32[2,80]{1,0:T(2,128)S(1)} collective-permute-done((f32[2,80]{1,0:T(2,128)S(1)}, f32[2,80]{1,0:T(2,128)S(1)}, u32[]{:S(2)}, u32[]{:S(2)}) %collective-permute-start.47) | collective-permute-done | bytes 672 | tf_op jit(solution)/shard_map/ppermute | solution.py:870
  480.0 4.6 collective-permute-done.48
  490.3 6.0 %collective-permute-done.49 = bf16[128,1280]{1,0:T(8,128)(2,1)S(1)} collective-permute-done((bf16[128,1280]{1,0:T(8,128)(2,1)S(1)}, bf16[128,1280]{1,0:T(8,128)(2,1)S(1)}, u32[]{:S(2)}, u32[]{:S(2)}) %collective-permute-start.49) | collective-permute-done | bytes 327712 | tf_op jit(solution)/shard_map/ppermute | solution.py:870
  (387 shorter events, 207.7 us)
Async XLA Ops:
  15.2 41.3 %all-gather.7.cloned.1.call-start = ((), (), s32[]{:S(2)}) async-start(), calls=%async_computation.16 | async-start | bytes 1638400 | tf_op jit(solution)/shard_map/all_gather | solution.py:904
  24.2 64.1 %all-gather.9.cloned.1.call-start = ((), (), s32[]{:S(2)}) async-start(), calls=%async_computation.17 | async-start | bytes 1536000 | tf_op jit(solution)/shard_map/all_gather | solution.py:904
  56.5 30.1 %collective-permute-start.5 = (bf16[4,160,964]{2,1,0:T(8,128)(2,1)}, bf16[4,160,964]{2,1,0:T(8,128)(2,1)S(1)}, u32[]{:S(2)}, u32[]{:S(2)}) collective-permute-start(bf16[4,160,964]{2,1,0:T(8,128)(2,1)} %bitcast.251), channel_id=1, source_target_pairs={{0,4},{4,0},{1,5},{5,1},{2,6},{6,2},{3,7},{7,3},{8,12},{12,8},{9,1... | collective-permute-start | bytes 3701768 | tf_op jit(solution)/shard_map/ppermute | solution.py:870
  63.1 78.0 %all-gather.11.cloned.1.call-start = ((), (), s32[]{:S(2)}) async-start(), calls=%async_computation.18 | async-start | bytes 3072000 | tf_op jit(solution)/shard_map/all_gather | solution.py:904
  89.3 28.4 %collective-permute-start.7 = (bf16[4,40,3840]{2,1,0:T(8,128)(2,1)}, bf16[4,40,3840]{2,1,0:T(8,128)(2,1)S(1)}, u32[]{:S(2)}, u32[]{:S(2)}) collective-permute-start(bf16[4,40,3840]{2,1,0:T(8,128)(2,1)} %bitcast.19.refs_0_), channel_id=1, source_target_pairs={{0,2},{1,3},{2,0},{3,1},{4,6},{5,7},{6,4},{7,5},{8,10},{9,11},{10,... | collective-permute-start | bytes 3686408 | tf_op jit(solution)/shard_map/ppermute | solution.py:870
  90.8 28.2 %collective-permute-start.6 = (bf16[4,40,3840]{2,1,0:T(8,128)(2,1)}, bf16[4,40,3840]{2,1,0:T(8,128)(2,1)}, u32[]{:S(2)}, u32[]{:S(2)}) collective-permute-start(bf16[4,40,3840]{2,1,0:T(8,128)(2,1)} %bitcast.19.refs_0_), channel_id=1, source_target_pairs={{0,4},{4,0},{1,5},{5,1},{2,6},{6,2},{3,7},{7,3},{8,12},{12,8},{9,1... | collective-permute-start | bytes 3686408 | tf_op jit(solution)/shard_map/ppermute | solution.py:870
  123.3 20.7 %collective-permute-start.8 = (bf16[4,40,1920]{2,1,0:T(8,128)(2,1)}, bf16[4,40,1920]{2,1,0:T(8,128)(2,1)}, u32[]{:S(2)}, u32[]{:S(2)}) collective-permute-start(bf16[4,40,1920]{2,1,0:T(8,128)(2,1)} %slice.153), channel_id=1, source_target_pairs={{0,2},{1,3},{2,0},{3,1},{4,6},{5,7},{6,4},{7,5},{8,10},{9,11},{10,... | collective-permute-start | bytes 1843208 | tf_op jit(solution)/shard_map/ppermute | solution.py:870
  123.8 20.2 %all-to-all-start.2 = ((bf16[4,320,256]{2,1,0:T(8,128)(2,1)}), bf16[4,320,256]{2,1,0:T(8,128)(2,1)S(1)}, u32[]{:S(2)}, u32[]{:S(2)}) async-start(bf16[4,320,256]{2,1,0:T(8,128)(2,1)} %bitcast.31), calls=%async_computation.2 | async-start | bytes 1310720 | tf_op jit(solution)/shard_map/all_to_all | solution.py:891
  127.6 19.1 %collective-permute-start.10 = (bf16[4,40,3840]{2,1,0:T(8,128)(2,1)}, bf16[4,40,3840]{2,1,0:T(8,128)(2,1)}, u32[]{:S(2)}, u32[]{:S(2)}) collective-permute-start(bf16[4,40,3840]{2,1,0:T(8,128)(2,1)} %bitcast.19.refs_0_), channel_id=1, source_target_pairs={{0,1},{1,0},{2,3},{3,2},{4,5},{5,4},{6,7},{7,6},{8,9},{9,8},{10,11... | collective-permute-start | bytes 3686408 | tf_op jit(solution)/shard_map/ppermute | solution.py:870
  128.2 19.2 %collective-permute-start.11 = (bf16[4,40,3840]{2,1,0:T(8,128)(2,1)}, bf16[4,40,3840]{2,1,0:T(8,128)(2,1)}, u32[]{:S(2)}, u32[]{:S(2)}) collective-permute-start(bf16[4,40,3840]{2,1,0:T(8,128)(2,1)} %collective-permute-done.6.refs_1_), channel_id=1, source_target_pairs={{0,1},{1,0},{2,3},{3,2},{4,5},{5,4},{6,7},{7,6},{8,9},{9,8},{10,11... | collective-permute-start | bytes 3686408 | tf_op jit(solution)/shard_map/ppermute | solution.py:870
  128.2 19.2 %collective-permute-start.12 = (bf16[4,40,3840]{2,1,0:T(8,128)(2,1)S(1)}, bf16[4,40,3840]{2,1,0:T(8,128)(2,1)}, u32[]{:S(2)}, u32[]{:S(2)}) collective-permute-start(bf16[4,40,3840]{2,1,0:T(8,128)(2,1)S(1)} %collective-permute-done.7.refs_2_), channel_id=1, source_target_pairs={{0,1},{1,0},{2,3},{3,2},{4,5},{5,4},{6,7},{7,6},{8,9},{9,8},{10,11... | collective-permute-start | bytes 3686408 | tf_op jit(solution)/shard_map/ppermute | solution.py:870
  146.8 29.5 %collective-permute-start.16 = (bf16[4,40,3840]{2,1,0:T(8,128)(2,1)S(1)}, bf16[4,40,3840]{2,1,0:T(8,128)(2,1)S(1)}, u32[]{:S(2)}, u32[]{:S(2)}) collective-permute-start(bf16[4,40,3840]{2,1,0:T(8,128)(2,1)S(1)} %get-tuple-element.250.along_ref), channel_id=1, source_target_pairs={{0,4},{4,0},{1,5},{5,1},{2,6},{6,2},{3,7},{7,3},{8,12},{12,8},{9,1... | collective-permute-start | bytes 3686408 | tf_op jit(solution)/shard_map/ppermute | solution.py:870
  176.3 28.8 %collective-permute-start.20 = (bf16[4,40,3840]{2,1,0:T(8,128)(2,1)S(1)}, bf16[4,40,3840]{2,1,0:T(8,128)(2,1)S(1)}, u32[]{:S(2)}, u32[]{:S(2)}) collective-permute-start(bf16[4,40,3840]{2,1,0:T(8,128)(2,1)S(1)} %get-tuple-element.141.refs_0_), channel_id=1, source_target_pairs={{0,2},{1,3},{2,0},{3,1},{4,6},{5,7},{6,4},{7,5},{8,10},{9,11},{10,... | collective-permute-start | bytes 3686408 | tf_op jit(solution)/shard_map/ppermute | solution.py:870
  176.8 28.6 %collective-permute-start.19 = (bf16[4,40,3840]{2,1,0:T(8,128)(2,1)S(1)}, bf16[4,40,3840]{2,1,0:T(8,128)(2,1)}, u32[]{:S(2)}, u32[]{:S(2)}) collective-permute-start(bf16[4,40,3840]{2,1,0:T(8,128)(2,1)S(1)} %get-tuple-element.141.refs_0_), channel_id=1, source_target_pairs={{0,4},{4,0},{1,5},{5,1},{2,6},{6,2},{3,7},{7,3},{8,12},{12,8},{9,1... | collective-permute-start | bytes 3686408 | tf_op jit(solution)/shard_map/ppermute | solution.py:870
  206.6 21.8 %collective-permute-start.22 = (bf16[4,40,1920]{2,1,0:T(8,128)(2,1)S(1)}, bf16[4,40,1920]{2,1,0:T(8,128)(2,1)S(1)}, u32[]{:S(2)}, u32[]{:S(2)}) collective-permute-start(bf16[4,40,1920]{2,1,0:T(8,128)(2,1)S(1)} %slice.167), channel_id=1, source_target_pairs={{0,4},{4,0},{1,5},{5,1},{2,6},{6,2},{3,7},{7,3},{8,12},{12,8},{9,1... | collective-permute-start | bytes 1843208 | tf_op jit(solution)/shard_map/ppermute | solution.py:870
  207.7 20.7 %collective-permute-start.21 = (bf16[4,40,1920]{2,1,0:T(8,128)(2,1)S(1)}, bf16[4,40,1920]{2,1,0:T(8,128)(2,1)S(1)}, u32[]{:S(2)}, u32[]{:S(2)}) collective-permute-start(bf16[4,40,1920]{2,1,0:T(8,128)(2,1)S(1)} %slice.166), channel_id=1, source_target_pairs={{0,2},{1,3},{2,0},{3,1},{4,6},{5,7},{6,4},{7,5},{8,10},{9,11},{10,... | collective-permute-start | bytes 1843208 | tf_op jit(solution)/shard_map/ppermute | solution.py:870
  209.1 19.9 %collective-permute-start.23 = (bf16[4,40,3840]{2,1,0:T(8,128)(2,1)S(1)}, bf16[4,40,3840]{2,1,0:T(8,128)(2,1)S(1)}, u32[]{:S(2)}, u32[]{:S(2)}) collective-permute-start(bf16[4,40,3840]{2,1,0:T(8,128)(2,1)S(1)} %get-tuple-element.141.refs_0_), channel_id=1, source_target_pairs={{0,1},{1,0},{2,3},{3,2},{4,5},{5,4},{6,7},{7,6},{8,9},{9,8},{10,11... | collective-permute-start | bytes 3686408 | tf_op jit(solution)/shard_map/ppermute | solution.py:870
  209.2 22.3 %collective-permute-start.24 = (bf16[4,40,3840]{2,1,0:T(8,128)(2,1)}, bf16[4,40,3840]{2,1,0:T(8,128)(2,1)S(1)}, u32[]{:S(2)}, u32[]{:S(2)}) collective-permute-start(bf16[4,40,3840]{2,1,0:T(8,128)(2,1)} %collective-permute-done.19.refs_1_), channel_id=1, source_target_pairs={{0,1},{1,0},{2,3},{3,2},{4,5},{5,4},{6,7},{7,6},{8,9},{9,8},{10,11... | collective-permute-start | bytes 3686408 | tf_op jit(solution)/shard_map/ppermute | solution.py:870
  209.7 21.8 %collective-permute-start.25 = (bf16[4,40,3840]{2,1,0:T(8,128)(2,1)S(1)}, bf16[4,40,3840]{2,1,0:T(8,128)(2,1)S(1)}, u32[]{:S(2)}, u32[]{:S(2)}) collective-permute-start(bf16[4,40,3840]{2,1,0:T(8,128)(2,1)S(1)} %collective-permute-done.20.refs_2_), channel_id=1, source_target_pairs={{0,1},{1,0},{2,3},{3,2},{4,5},{5,4},{6,7},{7,6},{8,9},{9,8},{10,11... | collective-permute-start | bytes 3686408 | tf_op jit(solution)/shard_map/ppermute | solution.py:870
  249.3 106.3 %reduce-scatter.5.cloned.1.call-start = ((), (), s32[]{:S(2)}) async-start(), calls=%async_computation.12 | async-start | bytes 3276800 | tf_op jit(solution)/shard_map/reduce_scatter | solution.py:920
  303.0 42.4 %collective-permute-start.34 = (bf16[4,40,3840]{2,1,0:T(8,128)(2,1)}, bf16[4,40,3840]{2,1,0:T(8,128)(2,1)}, u32[]{:S(2)}, u32[]{:S(2)}) collective-permute-start(bf16[4,40,3840]{2,1,0:T(8,128)(2,1)} %pad_maximum_fusion), channel_id=1, source_target_pairs={{0,4},{4,0},{1,5},{5,1},{2,6},{6,2},{3,7},{7,3},{8,12},{12,8},{9,1... | collective-permute-start | bytes 3686408 | tf_op jit(solution)/shard_map/ppermute | solution.py:870
  319.9 35.6 %collective-permute-start.35 = (bf16[4,40,3840]{2,1,0:T(8,128)(2,1)}, bf16[4,40,3840]{2,1,0:T(8,128)(2,1)}, u32[]{:S(2)}, u32[]{:S(2)}) collective-permute-start(bf16[4,40,3840]{2,1,0:T(8,128)(2,1)} %pad_maximum_fusion.1), channel_id=1, source_target_pairs={{0,2},{1,3},{2,0},{3,1},{4,6},{5,7},{6,4},{7,5},{8,10},{9,11},{10,... | collective-permute-start | bytes 3686408 | tf_op jit(solution)/shard_map/ppermute | solution.py:870
  332.6 23.0 %all-to-all-start.5 = ((bf16[4,320,256]{2,1,0:T(8,128)(2,1)}), bf16[4,320,256]{2,1,0:T(8,128)(2,1)}, u32[]{:S(2)}, u32[]{:S(2)}) async-start(bf16[4,320,256]{2,1,0:T(8,128)(2,1)} %bitcast.65), calls=%async_computation.5 | async-start | bytes 1310720 | tf_op jit(solution)/shard_map/all_to_all | solution.py:891
  336.8 63.9 %reduce-scatter.7.cloned.1.call-start = ((), (), s32[]{:S(2)}) async-start(), calls=%async_computation.13 | async-start | bytes 1536000 | tf_op jit(solution)/shard_map/reduce_scatter | solution.py:920
  355.6 25.7 %collective-permute-start.37 = (bf16[2,2,4,40,3840]{4,3,2,1,0:T(8,128)(2,1)}, bf16[2,2,4,40,3840]{4,3,2,1,0:T(8,128)(2,1)}, u32[]{:S(2)}, u32[]{:S(2)}) collective-permute-start(bf16[2,2,4,40,3840]{4,3,2,1,0:T(8,128)(2,1)} %get-tuple-element.191), channel_id=1, source_target_pairs={{0,1},{1,0},{2,3},{3,2},{4,5},{5,4},{6,7},{7,6},{8,9},{9,8},{10,11... | collective-permute-start | bytes 14745608 | tf_op jit(solution)/shard_map/ppermute | solution.py:870
  358.2 84.8 %reduce-scatter.9.cloned.1.call-start = ((), (), s32[]{:S(2)}) async-start(), calls=%async_computation.14 | async-start | bytes 3276800 | tf_op jit(solution)/shard_map/reduce_scatter | solution.py:920
  381.3 105.6 %reduce-scatter.11.cloned.1.call-start = ((), (), s32[]{:S(2)}) async-start(), calls=%async_computation.15 | async-start | bytes 1536000 | tf_op jit(solution)/shard_map/reduce_scatter | solution.py:920
  411.7 29.6 %collective-permute-start.42 = (bf16[2,2,128,1280]{3,2,1,0:T(8,128)(2,1)S(1)}, bf16[2,2,128,1280]{3,2,1,0:T(8,128)(2,1)S(1)}, u32[]{:S(2)}, u32[]{:S(2)}) collective-permute-start(bf16[2,2,128,1280]{3,2,1,0:T(8,128)(2,1)S(1)} %copy-done.65), channel_id=1, source_target_pairs={{0,1},{1,0},{2,3},{3,2},{4,5},{5,4},{6,7},{7,6},{8,9},{9,8},{10,11... | collective-permute-start | bytes 3932168 | tf_op jit(solution)/shard_map/ppermute | solution.py:870
  411.7 31.3 %collective-permute-start.43 = (bf16[4,40,3840]{2,1,0:T(8,128)(2,1)S(1)}, bf16[4,40,3840]{2,1,0:T(8,128)(2,1)}, u32[]{:S(2)}, u32[]{:S(2)}) collective-permute-start(bf16[4,40,3840]{2,1,0:T(8,128)(2,1)S(1)} %pad_maximum_fusion.2), channel_id=1, source_target_pairs={{0,4},{4,0},{1,5},{5,1},{2,6},{6,2},{3,7},{7,3},{8,12},{12,8},{9,1... | collective-permute-start | bytes 3686408 | tf_op jit(solution)/shard_map/ppermute | solution.py:870
  413.1 29.9 %collective-permute-start.44 = (bf16[4,40,3840]{2,1,0:T(8,128)(2,1)S(1)}, bf16[4,40,3840]{2,1,0:T(8,128)(2,1)}, u32[]{:S(2)}, u32[]{:S(2)}) collective-permute-start(bf16[4,40,3840]{2,1,0:T(8,128)(2,1)S(1)} %pad_maximum_fusion.3), channel_id=1, source_target_pairs={{0,2},{1,3},{2,0},{3,1},{4,6},{5,7},{6,4},{7,5},{8,10},{9,11},{10,... | collective-permute-start | bytes 3686408 | tf_op jit(solution)/shard_map/ppermute | solution.py:870
  422.1 19.2 %collective-permute-start.47 = (f32[2,80]{1,0:T(2,128)S(1)}, f32[2,80]{1,0:T(2,128)S(1)}, u32[]{:S(2)}, u32[]{:S(2)}) collective-permute-start(f32[2,80]{1,0:T(2,128)S(1)} %add.392), channel_id=1, source_target_pairs={{0,4},{4,0},{1,5},{5,1},{2,6},{6,2},{3,7},{7,3},{8,12},{12,8},{9,1... | collective-permute-start | bytes 1928 | tf_op jit(solution)/shard_map/ppermute | solution.py:870
  464.7 19.9 %collective-permute-start.48 = (bf16[2,128,1280]{2,1,0:T(8,128)(2,1)}, bf16[2,128,1280]{2,1,0:T(8,128)(2,1)}, u32[]{:S(2)}, u32[]{:S(2)}) collective-permute-start(bf16[2,128,1280]{2,1,0:T(8,128)(2,1)} %fusion.85), channel_id=1, source_target_pairs={{0,2},{1,3},{2,0},{3,1},{4,6},{5,7},{6,4},{7,5},{8,10},{9,11},{10,... | collective-permute-start | bytes 1966088 | tf_op jit(solution)/shard_map/ppermute | solution.py:870
  (104 other events, 808.8 us)
Sparse Core Ops, SparseCore 0:
  24.3 32.0 all-gather.6
  58.0 30.2 all-gather.8
  89.9 51.1 all-gather.10
  303.1 51.7 reduce-scatter.4
  358.3 31.1 reduce-scatter.6
  391.7 50.8 reduce-scatter.8
  449.5 29.0 reduce-scatter.10

commit v30 on v27

--- a/solution.py
+++ b/solution.py
@@ -1011,17 +1011,17 @@
     along = along_batch(columns)
     first = swap_halves(tokens).reshape(-1, width)
     stream = first.astype(F32)
+    upper = swap_halves(cotangent)
+    along, first, dense_near, upper = tied(along, first, dense_own[0], upper)
     far, near = swapped(first, "head", 2), other_core(first)
     both = other_core(far)
-    upper = swap_halves(cotangent)
-    along, near, far, both, dense_near, upper = tied(
-        along, near, far, both, dense_own[0], upper
-    )
-    token_pieces = (first, near, far, both)
     dense_near = along_batch(dense_near)
     qkv_across = swapped(along, "blk", 1)
     next_columns = jnp.concatenate(list(qkv_columns(qkv_weight[1], None)), axis=1)
-    qkv_across, dense_near, next_columns = tied(qkv_across, dense_near, next_columns)
+    qkv_across, dense_near, next_columns, near, far, both = tied(
+        qkv_across, dense_near, next_columns, near, far, both
+    )
+    token_pieces = (first, near, far, both)
     across, beside = swapped(dense_near, "blk", 1), swapped(dense_near, "head", 2)
     next_both = along_batch(jnp.stack([next_columns, dense_own[1]]))
     weight, gains = assemble_columns(along, qkv_across, part3)

time: 512 us -> 512 us (level)
    all_gather x3, waiting for transfers between devices: 14.6 us -> 24.2 us  [along_batch(): return lax.all_gather(piece, 'batch', axis=0, tiled=False)]
    all_to_all x7, waiting for transfers between devices: 27.5 us -> 21.7 us  [over_head(): lax.all_to_all(parts, 'head', split_axis=0, concat_axis=0, tiled=True)]
    unnamed x144 -> x142, local copies, waits for them, and re-layouts: 11.6 us -> 11.5 us
  transfers between devices with their start and end apart: 65 -> 65, of which waited for: 32 -> 33; matrix products, arithmetic and copies ran while one was open for 13% -> 13% of each run, Pallas kernels for 22% -> 22%
where the time goes in v30:
time: 512 us; the launch traced here: 504 us
  waiting for transfers between devices  182 us (36%)
  Pallas kernels  113 us (22%)
  starting transfers between devices  72.2 us (14%)
  other arithmetic  48 us (9%)
  local copies, waits for them, and re-layouts  34.6 us (7%)
  matrix products  19.6 us (4%)
  blocking collectives  18.8 us (4%)
  between operations  15.9 us (3%)
    ppermute x51, waiting for transfers between devices, swapped(): return lax.ppermute(array, axis, [(i, i ^ mask) for i in range(size)])  131 us
    ppermute x51, starting transfers between devices, swapped(): return lax.ppermute(array, axis, [(i, i ^ mask) for i in range(size)])  44.4 us
    all_to_all x7, starting transfers between devices, over_head(): lax.all_to_all(parts, 'head', split_axis=0, concat_axis=0, tiled=True)  27.4 us
    pallas_call x2, Pallas kernels, attend_back_rows(): pl.pallas_call(functools.partial(attend_back_kernel, token_rows), grid=(l...  24.8 us
    all_gather x3, waiting for transfers between devices, along_batch(): return lax.all_gather(piece, 'batch', axis=0, tiled=False)  24.2 us
    all_to_all x7, waiting for transfers between devices, over_head(): lax.all_to_all(parts, 'head', split_axis=0, concat_axis=0, tiled=True)  21.7 us
    all_to_all x1, blocking collectives, over_head(): lax.all_to_all(parts, 'head', split_axis=0, concat_axis=0, tiled=True)  18.8 us
    pallas_call x2, Pallas kernels, dense_grads(): pl.pallas_call(dense_grad_kernel, grid_spec=pltpu.PrefetchScalarGridSpec(...  17 us
  transfers between devices with their start and end apart: 65, of which 33 were waited for; matrix products, arithmetic and copies ran while one was open for 13% of the time, Pallas kernels for 22%

profile of v30, /device:TPU:0, one launch (start us, length us, event | category | flops | bytes accessed | tf_op | source)
XLA Modules:
  0.0 503.9 jit_solution(2740852514325940122)
XLA Ops:
  16.5 5.4 %all-to-all-done = bf16[4,40,964]{2,1,0:T(8,128)(2,1)S(1)} async-done(((bf16[4,40,964]{2,1,0:T(8,128)(2,1)}), bf16[4,40,964]{2,1,0:T(8,128)(2,1)S(1)}, u32[]{:S(2)}, u32[]{:S(2)}) %all-to-all-start) | async-done | bytes 308512 | tf_op jit(solution)/shard_map/all_to_all | solution.py:891
  25.8 7.7 %collective-permute-done.1 = bf16[128,1280]{1,0:T(8,128)(2,1)S(1)} collective-permute-done((bf16[128,1280]{1,0:T(8,128)(2,1)S(1)}, bf16[128,1280]{1,0:T(8,128)(2,1)S(1)}, u32[]{:S(2)}, u32[]{:S(2)}) %collective-permute-start.1) | collective-permute-done | bytes 327712 | tf_op jit(solution)/shard_map/ppermute | solution.py:870
  34.5 5.0 collective-permute-done
  40.4 16.0 %all-gather.7.cloned.1.call-done = bf16[640,964]{1,0:T(8,128)(2,1)} async-done(((bf16[160,964]{1,0:T(8,128)(2,1)}), bf16[640,964]{1,0:T(8,128)(2,1)}) %all-gather.7.cloned.1.call-update) | async-done | bytes 1233936 | tf_op jit(solution)/shard_map/all_gather | solution.py:904
  65.1 9.1 %collective-permute-done.4.refs_2_ = bf16[256,1280]{1,0:T(8,128)(2,1)} collective-permute-done((bf16[256,1280]{1,0:T(8,128)(2,1)S(1)}, bf16[256,1280]{1,0:T(8,128)(2,1)}, u32[]{:S(2)}, u32[]{:S(2)}) %collective-permute-start.4) | collective-permute-done | bytes 655392 | tf_op jit(solution)/shard_map/ppermute | solution.py:870
  76.1 11.7 %collective-permute-done.2.across_ref = bf16[4,160,964]{2,1,0:T(8,128)(2,1)S(1)} collective-permute-done((bf16[4,160,964]{2,1,0:T(8,128)(2,1)}, bf16[4,160,964]{2,1,0:T(8,128)(2,1)S(1)}, u32[]{:S(2)}, u32[]{:S(2)}) %collective-permute-start.2) | collective-permute-done | bytes 1233952 | tf_op jit(solution)/shard_map/ppermute | solution.py:870
  93.4 4.6 shard_map.169
  99.3 7.7 %shard_map.170 = (bf16[1024,1280]{1,0:T(8,128)(2,1)}, f32[960,1024]{1,0:T(8,128)S(1)}) custom-call(s32[3]{0:T(128)S(1)} %pad_add_fusion.place_ref.core_ref, bf16[256,1280]{1,0:T(8,128)(2,1)} %bitcast.235, bf16[256,1280]{1,0:T(8,128)(2,1)} %collective-permute-done.3.refs_1_, bf16[256,1280]{1,0:T(8,128)(2,1)} %collective-permute-done.4.refs_2_, ...), custom_call_target="tpu_custom_call" | custom-call | flops 1048576 | bytes 1048576 | tf_op jit(solution)/shard_map/pallas_call | solution.py:733
  107.1 6.7 %shard_map.171 = (bf16[4,4,80,256]{3,2,1,0:T(8,128)(2,1)}, f32[4,1,1024]{2,1,0:T(1,128)S(1)}) custom-call(f32[3,4,80,1024]{3,2,1,0:T(8,128)S(1)} %bitcast.203, f32[80,1]{1,0:T(8,128)S(1)} %copy.60.scale_ref, s32[1024,1]{1,0:T(8,128)S(1)} %copy.61.col_ref, s32[1,1024]{1,0:T(1,128)S(1)} %constant_dynamic-slice_fusion.row_ref), custom_call_target="tpu_custom_call" | custom-call | flops 1048576 | bytes 1048576 | tf_op jit(solution)/shard_map/pallas_call | solution.py:435
  113.8 4.5 collective-permute-done.7.refs_2_
  129.3 5.3 %collective-permute-done.9.refs_4_ = bf16[4,40,1920]{2,1,0:T(8,128)(2,1)} collective-permute-done((bf16[4,40,1920]{2,1,0:T(8,128)(2,1)}, bf16[4,40,1920]{2,1,0:T(8,128)(2,1)}, u32[]{:S(2)}, u32[]{:S(2)}) %collective-permute-start.9) | collective-permute-done | bytes 614432 | tf_op jit(solution)/shard_map/ppermute | solution.py:870
  134.6 7.1 %all-gather.11.cloned.1.call-done = bf16[8,40,3840]{2,1,0:T(8,128)(2,1)} async-done(((bf16[2,40,3840]{2,1,0:T(8,128)(2,1)}), bf16[8,40,3840]{2,1,0:T(8,128)(2,1)}) %all-gather.11.cloned.1.call-update) | async-done | bytes 2457616 | tf_op jit(solution)/shard_map/all_gather | solution.py:904
  148.0 4.5 shard_map.172
  160.2 16.6 %collective-permute-done.16.across_ref = bf16[4,40,3840]{2,1,0:T(8,128)(2,1)S(1)} collective-permute-done((bf16[4,40,3840]{2,1,0:T(8,128)(2,1)S(1)}, bf16[4,40,3840]{2,1,0:T(8,128)(2,1)S(1)}, u32[]{:S(2)}, u32[]{:S(2)}) %collective-permute-start.16) | collective-permute-done | bytes 1228832 | tf_op jit(solution)/shard_map/ppermute | solution.py:870
  179.5 4.8 shard_map.173
  184.3 6.6 %shard_map.174 = (bf16[1024,1280]{1,0:T(8,128)(2,1)}, f32[960,1024]{1,0:T(8,128)S(1)}) custom-call(s32[3]{0:T(128)S(1)} %pad_add_fusion.place_ref.core_ref, bf16[256,1280]{1,0:T(8,128)(2,1)} %multiply_convert_fusion.2.refs_0_, bf16[256,1280]{1,0:T(8,128)(2,1)} %collective-permute-done.17.refs_1_, bf16[256,1280]{1,0:T(8,128)(2,1)} %collective-permute-done.15.refs_2_, ...), custom_call_target="tpu_custom_call" | custom-call | flops 1048576 | bytes 1048576 | tf_op jit(solution)/shard_map/pallas_call | solution.py:733
  190.9 6.1 %shard_map.175 = (bf16[4,4,80,256]{3,2,1,0:T(8,128)(2,1)S(1)}, f32[4,1,1024]{2,1,0:T(1,128)S(1)}) custom-call(f32[3,4,80,1024]{3,2,1,0:T(8,128)S(1)} %bitcast.205, f32[80,1]{1,0:T(8,128)S(1)} %copy.64.scale_ref, s32[1024,1]{1,0:T(8,128)S(1)} %copy.61.col_ref, s32[1,1024]{1,0:T(1,128)S(1)} %constant_dynamic-slice_fusion.row_ref), custom_call_target="tpu_custom_call" | custom-call | flops 1048576 | bytes 1048576 | tf_op jit(solution)/shard_map/pallas_call | solution.py:435
  197.0 8.6 %collective-permute-done.20.refs_2_ = bf16[4,40,3840]{2,1,0:T(8,128)(2,1)S(1)} collective-permute-done((bf16[4,40,3840]{2,1,0:T(8,128)(2,1)S(1)}, bf16[4,40,3840]{2,1,0:T(8,128)(2,1)S(1)}, u32[]{:S(2)}, u32[]{:S(2)}) %collective-permute-start.20) | collective-permute-done | bytes 1228832 | tf_op jit(solution)/shard_map/ppermute | solution.py:870
  210.3 18.8 %all_to_all.40 = bf16[4,320,256]{2,1,0:T(8,128)(2,1)S(1)} all-to-all(bf16[4,320,256]{2,1,0:T(8,128)(2,1)S(1)} %bitcast.221), channel_id=1, replica_groups=mesh['batch'=4,'blk'=2,'head'=4] {'head'}, dimensions={0} | all-to-all | bytes 1310720 | tf_op jit(solution)/shard_map/all_to_all | solution.py:891
  250.2 8.5 %shard_map.177 = (bf16[2,2,4,40,3840]{4,3,2,1,0:T(8,128)(2,1)}, bf16[2,2,4,40,3840]{4,3,2,1,0:T(8,128)(2,1)}) custom-call(s32[3]{0:T(128)S(1)} %pad_add_fusion.place_ref.core_ref, bf16[1280,256]{1,0:T(8,128)(2,1)} %bitcast.243, bf16[256,1280]{1,0:T(8,128)(2,1)} %copy-done.31, bf16[256,1280]{1,0:T(8,128)(2,1)} %copy-done.52, bf16[256,1280]{1,0:T(8,128)(2,1)} %copy-done.32, ...), custom_call_target="tpu_custom_call" | custom-call | flops 1048576 | bytes 1048576 | tf_op jit(solution)/shard_map/pallas_call | solution.py:599
  261.1 12.5 %shard_map.178 = (bf16[3,4,80,1024]{3,2,1,0:T(8,128)(2,1)}, f32[80,128]{1,0:T(8,128)}) custom-call(f32[3,4,80,1024]{3,2,1,0:T(8,128)} %bitcast.206, bf16[4,4,80,256]{3,2,1,0:T(8,128)(2,1)} %bitcast.56.grad_ref, f32[4,1,1024]{2,1,0:T(1,128)S(1)} %get-tuple-element.158.lse_ref, f32[80,1]{1,0:T(8,128)S(1)} %copy.64.scale_ref, s32[1024,1]{1,0:T(8,128)S(1)} %copy.61.col_ref, ...), custom_call_target="tpu_custom_call" | custom-call | flops 1048576 | bytes 1048576 | tf_op jit(solution)/shard_map/pallas_call | solution.py:528
  278.9 11.3 %shard_map.179 = (f32[2,2,128,1280]{3,2,1,0:T(8,128)}, bf16[2,2,128,1280]{3,2,1,0:T(8,128)(2,1)}, bf16[1280,960]{1,0:T(8,128)(2,1)}) custom-call(s32[3]{0:T(128)S(1)} %pad_add_fusion.place_ref.core_ref, bf16[960,1024]{1,0:T(8,128)(2,1)} %bitcast.245, bf16[1280,960]{1,0:T(8,128)(2,1)} %bitcast.223, bf16[1024,1280]{1,0:T(8,128)(2,1)} %get-tuple-element.165.normed_ref), custom_call_target="tpu_custom_call" | custom-call | flops 1048576 | bytes 1048576 | tf_op jit(solution)/shard_map/pallas_call | solution.py:779
  305.2 13.7 %collective-permute-done.33 = bf16[2,128,1280]{2,1,0:T(8,128)(2,1)} collective-permute-done((bf16[2,128,1280]{2,1,0:T(8,128)(2,1)}, bf16[2,128,1280]{2,1,0:T(8,128)(2,1)}, u32[]{:S(2)}, u32[]{:S(2)}) %collective-permute-start.33) | collective-permute-done | bytes 655392 | tf_op jit(solution)/shard_map/ppermute | solution.py:870
  337.5 8.5 %shard_map.180 = (bf16[2,2,4,40,3840]{4,3,2,1,0:T(8,128)(2,1)}, bf16[2,2,4,40,3840]{4,3,2,1,0:T(8,128)(2,1)}) custom-call(s32[3]{0:T(128)S(1)} %pad_add_fusion.place_ref.core_ref, bf16[1280,256]{1,0:T(8,128)(2,1)} %bitcast.240, bf16[256,1280]{1,0:T(8,128)(2,1)} %copy-done.30, bf16[256,1280]{1,0:T(8,128)(2,1)} %copy-done.48, bf16[256,1280]{1,0:T(8,128)(2,1)} %copy-done.36, ...), custom_call_target="tpu_custom_call" | custom-call | flops 1048576 | bytes 1048576 | tf_op jit(solution)/shard_map/pallas_call | solution.py:599
  348.4 7.8 %all-to-all-done.5 = bf16[4,320,256]{2,1,0:T(8,128)(2,1)} async-done(((bf16[4,320,256]{2,1,0:T(8,128)(2,1)}), bf16[4,320,256]{2,1,0:T(8,128)(2,1)}, u32[]{:S(2)}, u32[]{:S(2)}) %all-to-all-start.5) | async-done | bytes 655392 | tf_op jit(solution)/shard_map/all_to_all | solution.py:891
  361.5 12.3 %shard_map.181 = (bf16[3,4,80,1024]{3,2,1,0:T(8,128)(2,1)}, f32[80,128]{1,0:T(8,128)}) custom-call(f32[3,4,80,1024]{3,2,1,0:T(8,128)} %bitcast.204, bf16[4,4,80,256]{3,2,1,0:T(8,128)(2,1)} %bitcast.69.grad_ref, f32[4,1,1024]{2,1,0:T(1,128)S(1)} %get-tuple-element.188.lse_ref, f32[80,1]{1,0:T(8,128)S(1)} %copy.60.scale_ref, s32[1024,1]{1,0:T(8,128)S(1)} %copy.61.col_ref, ...), custom_call_target="tpu_custom_call" | custom-call | flops 1048576 | bytes 1048576 | tf_op jit(solution)/shard_map/pallas_call | solution.py:528
  374.7 7.3 %shard_map.182 = bf16[1280,960]{1,0:T(8,128)(2,1)} custom-call(bf16[960,1024]{1,0:T(8,128)(2,1)} %bitcast.231, bf16[1024,1280]{1,0:T(8,128)(2,1)} %get-tuple-element.192.normed_ref), custom_call_target="tpu_custom_call" | custom-call | flops 1048576 | bytes 1048576 | tf_op jit(solution)/shard_map/pallas_call | solution.py:850
  382.1 4.9 add_bitcast_fusion
  392.8 8.5 %shard_map.183 = (f32[2,2,128,1280]{3,2,1,0:T(8,128)}, bf16[2,2,128,1280]{3,2,1,0:T(8,128)(2,1)}) custom-call(s32[3]{0:T(128)S(1)} %pad_add_fusion.place_ref.core_ref, bf16[960,1024]{1,0:T(8,128)(2,1)} %bitcast.232, bf16[1280,960]{1,0:T(8,128)(2,1)} %bitcast.230), custom_call_target="tpu_custom_call" | custom-call | flops 1048576 | bytes 1048576 | tf_op jit(solution)/shard_map/pallas_call | solution.py:820
  423.5 18.4 %collective-permute-done.47 = f32[2,80]{1,0:T(2,128)S(1)} collective-permute-done((f32[2,80]{1,0:T(2,128)S(1)}, f32[2,80]{1,0:T(2,128)S(1)}, u32[]{:S(2)}, u32[]{:S(2)}) %collective-permute-start.47) | collective-permute-done | bytes 672 | tf_op jit(solution)/shard_map/ppermute | solution.py:870
  457.8 10.3 %collective-permute-done.48 = bf16[2,128,1280]{2,1,0:T(8,128)(2,1)} collective-permute-done((bf16[2,128,1280]{2,1,0:T(8,128)(2,1)}, bf16[2,128,1280]{2,1,0:T(8,128)(2,1)}, u32[]{:S(2)}, u32[]{:S(2)}) %collective-permute-start.48) | collective-permute-done | bytes 655392 | tf_op jit(solution)/shard_map/ppermute | solution.py:870
  479.0 5.0 reduce-scatter.11.cloned.1.call-done
  (387 shorter events, 202.1 us)
Async XLA Ops:
  15.2 41.3 %all-gather.7.cloned.1.call-start = ((), (), s32[]{:S(2)}) async-start(), calls=%async_computation.16 | async-start | bytes 1638400 | tf_op jit(solution)/shard_map/all_gather | solution.py:904
  22.6 66.2 %all-gather.9.cloned.1.call-start = ((), (), s32[]{:S(2)}) async-start(), calls=%async_computation.17 | async-start | bytes 1536000 | tf_op jit(solution)/shard_map/all_gather | solution.py:904
  58.0 29.8 %collective-permute-start.2 = (bf16[4,160,964]{2,1,0:T(8,128)(2,1)}, bf16[4,160,964]{2,1,0:T(8,128)(2,1)S(1)}, u32[]{:S(2)}, u32[]{:S(2)}) collective-permute-start(bf16[4,160,964]{2,1,0:T(8,128)(2,1)} %bitcast.252), channel_id=1, source_target_pairs={{0,4},{4,0},{1,5},{5,1},{2,6},{6,2},{3,7},{7,3},{8,12},{12,8},{9,1... | collective-permute-start | bytes 3701768 | tf_op jit(solution)/shard_map/ppermute | solution.py:870
  64.7 77.0 %all-gather.11.cloned.1.call-start = ((), (), s32[]{:S(2)}) async-start(), calls=%async_computation.18 | async-start | bytes 3072000 | tf_op jit(solution)/shard_map/all_gather | solution.py:904
  89.9 28.4 %collective-permute-start.7 = (bf16[4,40,3840]{2,1,0:T(8,128)(2,1)}, bf16[4,40,3840]{2,1,0:T(8,128)(2,1)S(1)}, u32[]{:S(2)}, u32[]{:S(2)}) collective-permute-start(bf16[4,40,3840]{2,1,0:T(8,128)(2,1)} %bitcast.19.refs_0_), channel_id=1, source_target_pairs={{0,2},{1,3},{2,0},{3,1},{4,6},{5,7},{6,4},{7,5},{8,10},{9,11},{10,... | collective-permute-start | bytes 3686408 | tf_op jit(solution)/shard_map/ppermute | solution.py:870
  91.4 28.2 %collective-permute-start.6 = (bf16[4,40,3840]{2,1,0:T(8,128)(2,1)}, bf16[4,40,3840]{2,1,0:T(8,128)(2,1)}, u32[]{:S(2)}, u32[]{:S(2)}) collective-permute-start(bf16[4,40,3840]{2,1,0:T(8,128)(2,1)} %bitcast.19.refs_0_), channel_id=1, source_target_pairs={{0,4},{4,0},{1,5},{5,1},{2,6},{6,2},{3,7},{7,3},{8,12},{12,8},{9,1... | collective-permute-start | bytes 3686408 | tf_op jit(solution)/shard_map/ppermute | solution.py:870
  123.9 20.7 %collective-permute-start.8 = (bf16[4,40,1920]{2,1,0:T(8,128)(2,1)}, bf16[4,40,1920]{2,1,0:T(8,128)(2,1)}, u32[]{:S(2)}, u32[]{:S(2)}) collective-permute-start(bf16[4,40,1920]{2,1,0:T(8,128)(2,1)} %slice.153), channel_id=1, source_target_pairs={{0,2},{1,3},{2,0},{3,1},{4,6},{5,7},{6,4},{7,5},{8,10},{9,11},{10,... | collective-permute-start | bytes 1843208 | tf_op jit(solution)/shard_map/ppermute | solution.py:870
  124.4 20.2 %all-to-all-start.2 = ((bf16[4,320,256]{2,1,0:T(8,128)(2,1)}), bf16[4,320,256]{2,1,0:T(8,128)(2,1)S(1)}, u32[]{:S(2)}, u32[]{:S(2)}) async-start(bf16[4,320,256]{2,1,0:T(8,128)(2,1)} %bitcast.31), calls=%async_computation.2 | async-start | bytes 1310720 | tf_op jit(solution)/shard_map/all_to_all | solution.py:891
  128.2 19.1 %collective-permute-start.10 = (bf16[4,40,3840]{2,1,0:T(8,128)(2,1)}, bf16[4,40,3840]{2,1,0:T(8,128)(2,1)}, u32[]{:S(2)}, u32[]{:S(2)}) collective-permute-start(bf16[4,40,3840]{2,1,0:T(8,128)(2,1)} %bitcast.19.refs_0_), channel_id=1, source_target_pairs={{0,1},{1,0},{2,3},{3,2},{4,5},{5,4},{6,7},{7,6},{8,9},{9,8},{10,11... | collective-permute-start | bytes 3686408 | tf_op jit(solution)/shard_map/ppermute | solution.py:870
  128.8 19.2 %collective-permute-start.11 = (bf16[4,40,3840]{2,1,0:T(8,128)(2,1)}, bf16[4,40,3840]{2,1,0:T(8,128)(2,1)}, u32[]{:S(2)}, u32[]{:S(2)}) collective-permute-start(bf16[4,40,3840]{2,1,0:T(8,128)(2,1)} %collective-permute-done.6.refs_1_), channel_id=1, source_target_pairs={{0,1},{1,0},{2,3},{3,2},{4,5},{5,4},{6,7},{7,6},{8,9},{9,8},{10,11... | collective-permute-start | bytes 3686408 | tf_op jit(solution)/shard_map/ppermute | solution.py:870
  128.8 19.2 %collective-permute-start.12 = (bf16[4,40,3840]{2,1,0:T(8,128)(2,1)S(1)}, bf16[4,40,3840]{2,1,0:T(8,128)(2,1)}, u32[]{:S(2)}, u32[]{:S(2)}) collective-permute-start(bf16[4,40,3840]{2,1,0:T(8,128)(2,1)S(1)} %collective-permute-done.7.refs_2_), channel_id=1, source_target_pairs={{0,1},{1,0},{2,3},{3,2},{4,5},{5,4},{6,7},{7,6},{8,9},{9,8},{10,11... | collective-permute-start | bytes 3686408 | tf_op jit(solution)/shard_map/ppermute | solution.py:870
  147.4 29.5 %collective-permute-start.16 = (bf16[4,40,3840]{2,1,0:T(8,128)(2,1)S(1)}, bf16[4,40,3840]{2,1,0:T(8,128)(2,1)S(1)}, u32[]{:S(2)}, u32[]{:S(2)}) collective-permute-start(bf16[4,40,3840]{2,1,0:T(8,128)(2,1)S(1)} %get-tuple-element.252.along_ref), channel_id=1, source_target_pairs={{0,4},{4,0},{1,5},{5,1},{2,6},{6,2},{3,7},{7,3},{8,12},{12,8},{9,1... | collective-permute-start | bytes 3686408 | tf_op jit(solution)/shard_map/ppermute | solution.py:870
  176.9 28.8 %collective-permute-start.20 = (bf16[4,40,3840]{2,1,0:T(8,128)(2,1)S(1)}, bf16[4,40,3840]{2,1,0:T(8,128)(2,1)S(1)}, u32[]{:S(2)}, u32[]{:S(2)}) collective-permute-start(bf16[4,40,3840]{2,1,0:T(8,128)(2,1)S(1)} %get-tuple-element.143.refs_0_), channel_id=1, source_target_pairs={{0,2},{1,3},{2,0},{3,1},{4,6},{5,7},{6,4},{7,5},{8,10},{9,11},{10,... | collective-permute-start | bytes 3686408 | tf_op jit(solution)/shard_map/ppermute | solution.py:870
  177.5 28.6 %collective-permute-start.19 = (bf16[4,40,3840]{2,1,0:T(8,128)(2,1)S(1)}, bf16[4,40,3840]{2,1,0:T(8,128)(2,1)}, u32[]{:S(2)}, u32[]{:S(2)}) collective-permute-start(bf16[4,40,3840]{2,1,0:T(8,128)(2,1)S(1)} %get-tuple-element.143.refs_0_), channel_id=1, source_target_pairs={{0,4},{4,0},{1,5},{5,1},{2,6},{6,2},{3,7},{7,3},{8,12},{12,8},{9,1... | collective-permute-start | bytes 3686408 | tf_op jit(solution)/shard_map/ppermute | solution.py:870
  207.2 21.8 %collective-permute-start.22 = (bf16[4,40,1920]{2,1,0:T(8,128)(2,1)S(1)}, bf16[4,40,1920]{2,1,0:T(8,128)(2,1)S(1)}, u32[]{:S(2)}, u32[]{:S(2)}) collective-permute-start(bf16[4,40,1920]{2,1,0:T(8,128)(2,1)S(1)} %slice.167), channel_id=1, source_target_pairs={{0,4},{4,0},{1,5},{5,1},{2,6},{6,2},{3,7},{7,3},{8,12},{12,8},{9,1... | collective-permute-start | bytes 1843208 | tf_op jit(solution)/shard_map/ppermute | solution.py:870
  208.3 20.7 %collective-permute-start.21 = (bf16[4,40,1920]{2,1,0:T(8,128)(2,1)S(1)}, bf16[4,40,1920]{2,1,0:T(8,128)(2,1)S(1)}, u32[]{:S(2)}, u32[]{:S(2)}) collective-permute-start(bf16[4,40,1920]{2,1,0:T(8,128)(2,1)S(1)} %slice.166), channel_id=1, source_target_pairs={{0,2},{1,3},{2,0},{3,1},{4,6},{5,7},{6,4},{7,5},{8,10},{9,11},{10,... | collective-permute-start | bytes 1843208 | tf_op jit(solution)/shard_map/ppermute | solution.py:870
  209.7 19.9 %collective-permute-start.23 = (bf16[4,40,3840]{2,1,0:T(8,128)(2,1)S(1)}, bf16[4,40,3840]{2,1,0:T(8,128)(2,1)S(1)}, u32[]{:S(2)}, u32[]{:S(2)}) collective-permute-start(bf16[4,40,3840]{2,1,0:T(8,128)(2,1)S(1)} %get-tuple-element.143.refs_0_), channel_id=1, source_target_pairs={{0,1},{1,0},{2,3},{3,2},{4,5},{5,4},{6,7},{7,6},{8,9},{9,8},{10,11... | collective-permute-start | bytes 3686408 | tf_op jit(solution)/shard_map/ppermute | solution.py:870
  209.7 22.3 %collective-permute-start.24 = (bf16[4,40,3840]{2,1,0:T(8,128)(2,1)}, bf16[4,40,3840]{2,1,0:T(8,128)(2,1)S(1)}, u32[]{:S(2)}, u32[]{:S(2)}) collective-permute-start(bf16[4,40,3840]{2,1,0:T(8,128)(2,1)} %collective-permute-done.19.refs_1_), channel_id=1, source_target_pairs={{0,1},{1,0},{2,3},{3,2},{4,5},{5,4},{6,7},{7,6},{8,9},{9,8},{10,11... | collective-permute-start | bytes 3686408 | tf_op jit(solution)/shard_map/ppermute | solution.py:870
  210.2 21.8 %collective-permute-start.25 = (bf16[4,40,3840]{2,1,0:T(8,128)(2,1)S(1)}, bf16[4,40,3840]{2,1,0:T(8,128)(2,1)S(1)}, u32[]{:S(2)}, u32[]{:S(2)}) collective-permute-start(bf16[4,40,3840]{2,1,0:T(8,128)(2,1)S(1)} %collective-permute-done.20.refs_2_), channel_id=1, source_target_pairs={{0,1},{1,0},{2,3},{3,2},{4,5},{5,4},{6,7},{7,6},{8,9},{9,8},{10,11... | collective-permute-start | bytes 3686408 | tf_op jit(solution)/shard_map/ppermute | solution.py:870
  239.5 19.2 %collective-permute-start.28 = (bf16[128,1280]{1,0:T(8,128)(2,1)}, bf16[128,1280]{1,0:T(8,128)(2,1)}, u32[]{:S(2)}, u32[]{:S(2)}) collective-permute-start(bf16[128,1280]{1,0:T(8,128)(2,1)} %dynamic-slice_bitcast_fusion.3), channel_id=1, source_target_pairs={{0,4},{4,0},{1,5},{5,1},{2,6},{6,2},{3,7},{7,3},{8,12},{12,8},{9,1... | collective-permute-start | bytes 983048 | tf_op jit(solution)/shard_map/ppermute | solution.py:870
  249.9 106.3 %reduce-scatter.5.cloned.1.call-start = ((), (), s32[]{:S(2)}) async-start(), calls=%async_computation.12 | async-start | bytes 3276800 | tf_op jit(solution)/shard_map/reduce_scatter | solution.py:920
  303.6 42.4 %collective-permute-start.34 = (bf16[4,40,3840]{2,1,0:T(8,128)(2,1)}, bf16[4,40,3840]{2,1,0:T(8,128)(2,1)}, u32[]{:S(2)}, u32[]{:S(2)}) collective-permute-start(bf16[4,40,3840]{2,1,0:T(8,128)(2,1)} %pad_maximum_fusion), channel_id=1, source_target_pairs={{0,4},{4,0},{1,5},{5,1},{2,6},{6,2},{3,7},{7,3},{8,12},{12,8},{9,1... | collective-permute-start | bytes 3686408 | tf_op jit(solution)/shard_map/ppermute | solution.py:870
  320.6 35.6 %collective-permute-start.35 = (bf16[4,40,3840]{2,1,0:T(8,128)(2,1)}, bf16[4,40,3840]{2,1,0:T(8,128)(2,1)}, u32[]{:S(2)}, u32[]{:S(2)}) collective-permute-start(bf16[4,40,3840]{2,1,0:T(8,128)(2,1)} %pad_maximum_fusion.1), channel_id=1, source_target_pairs={{0,2},{1,3},{2,0},{3,1},{4,6},{5,7},{6,4},{7,5},{8,10},{9,11},{10,... | collective-permute-start | bytes 3686408 | tf_op jit(solution)/shard_map/ppermute | solution.py:870
  333.2 23.0 %all-to-all-start.5 = ((bf16[4,320,256]{2,1,0:T(8,128)(2,1)}), bf16[4,320,256]{2,1,0:T(8,128)(2,1)}, u32[]{:S(2)}, u32[]{:S(2)}) async-start(bf16[4,320,256]{2,1,0:T(8,128)(2,1)} %bitcast.65), calls=%async_computation.5 | async-start | bytes 1310720 | tf_op jit(solution)/shard_map/all_to_all | solution.py:891
  337.4 63.9 %reduce-scatter.7.cloned.1.call-start = ((), (), s32[]{:S(2)}) async-start(), calls=%async_computation.13 | async-start | bytes 1536000 | tf_op jit(solution)/shard_map/reduce_scatter | solution.py:920
  356.2 25.8 %collective-permute-start.37 = (bf16[2,2,4,40,3840]{4,3,2,1,0:T(8,128)(2,1)}, bf16[2,2,4,40,3840]{4,3,2,1,0:T(8,128)(2,1)}, u32[]{:S(2)}, u32[]{:S(2)}) collective-permute-start(bf16[2,2,4,40,3840]{4,3,2,1,0:T(8,128)(2,1)} %get-tuple-element.193), channel_id=1, source_target_pairs={{0,1},{1,0},{2,3},{3,2},{4,5},{5,4},{6,7},{7,6},{8,9},{9,8},{10,11... | collective-permute-start | bytes 14745608 | tf_op jit(solution)/shard_map/ppermute | solution.py:870
  358.8 85.8 %reduce-scatter.9.cloned.1.call-start = ((), (), s32[]{:S(2)}) async-start(), calls=%async_computation.14 | async-start | bytes 3276800 | tf_op jit(solution)/shard_map/reduce_scatter | solution.py:920
  382.1 101.9 %reduce-scatter.11.cloned.1.call-start = ((), (), s32[]{:S(2)}) async-start(), calls=%async_computation.15 | async-start | bytes 1536000 | tf_op jit(solution)/shard_map/reduce_scatter | solution.py:920
  412.3 29.5 %collective-permute-start.42 = (bf16[2,2,128,1280]{3,2,1,0:T(8,128)(2,1)S(1)}, bf16[2,2,128,1280]{3,2,1,0:T(8,128)(2,1)S(1)}, u32[]{:S(2)}, u32[]{:S(2)}) collective-permute-start(bf16[2,2,128,1280]{3,2,1,0:T(8,128)(2,1)S(1)} %copy-done.65), channel_id=1, source_target_pairs={{0,1},{1,0},{2,3},{3,2},{4,5},{5,4},{6,7},{7,6},{8,9},{9,8},{10,11... | collective-permute-start | bytes 3932168 | tf_op jit(solution)/shard_map/ppermute | solution.py:870
  412.3 31.2 %collective-permute-start.43 = (bf16[4,40,3840]{2,1,0:T(8,128)(2,1)S(1)}, bf16[4,40,3840]{2,1,0:T(8,128)(2,1)S(1)}, u32[]{:S(2)}, u32[]{:S(2)}) collective-permute-start(bf16[4,40,3840]{2,1,0:T(8,128)(2,1)S(1)} %pad_maximum_fusion.2), channel_id=1, source_target_pairs={{0,4},{4,0},{1,5},{5,1},{2,6},{6,2},{3,7},{7,3},{8,12},{12,8},{9,1... | collective-permute-start | bytes 3686408 | tf_op jit(solution)/shard_map/ppermute | solution.py:870
  413.9 30.8 %collective-permute-start.44 = (bf16[4,40,3840]{2,1,0:T(8,128)(2,1)S(1)}, bf16[4,40,3840]{2,1,0:T(8,128)(2,1)}, u32[]{:S(2)}, u32[]{:S(2)}) collective-permute-start(bf16[4,40,3840]{2,1,0:T(8,128)(2,1)S(1)} %pad_maximum_fusion.3), channel_id=1, source_target_pairs={{0,2},{1,3},{2,0},{3,1},{4,6},{5,7},{6,4},{7,5},{8,10},{9,11},{10,... | collective-permute-start | bytes 3686408 | tf_op jit(solution)/shard_map/ppermute | solution.py:870
  452.1 22.5 %collective-permute-start.50 = (bf16[160,960]{1,0:T(8,128)(2,1)}, bf16[160,960]{1,0:T(8,128)(2,1)}, u32[]{:S(2)}, u32[]{:S(2)}) collective-permute-start(bf16[160,960]{1,0:T(8,128)(2,1)} %dynamic-slice_bitcast_fusion), channel_id=1, source_target_pairs={{0,4},{4,0},{1,5},{5,1},{2,6},{6,2},{3,7},{7,3},{8,12},{12,8},{9,1... | collective-permute-start | bytes 921608 | tf_op jit(solution)/shard_map/ppermute | solution.py:870
  (104 other events, 885.9 us)
Sparse Core Ops, SparseCore 0:
  22.8 33.6 all-gather.6
  58.6 30.2 all-gather.8
  90.5 51.1 all-gather.10
  303.7 51.8 reduce-scatter.4
  359.0 31.1 reduce-scatter.6
  392.4 50.8 reduce-scatter.8
  453.8 30.0 reduce-scatter.10
